TPU v7x, 32 devices: a whole 2x2x4 slice. The times are simulated.
32 devices in a mesh: ctx: 8 (over y, x, core), kv: 4 (over z).
Axes of the slice: x: 2, y: 2, z: 4, core: 2. Of those that a mesh axis runs over, the one named last changes fastest.
Arguments:
- new_tokens: float32 [2, 16384], P(None, 'ctx'), may hold values from -3 to 3
- ctx_hidden: bfloat16 [1, 2560, 16384], P(None, 'ctx'), may hold values from -200 to 200
- norm_gain: float32 [1, 16384], replicated, may hold values from 0.1 to 1.9
- query_weight: bfloat16 [1, 16384, 4096], P(None, 'ctx', 'kv'), may hold values from -9 to 9
- key_weight: bfloat16 [1, 16384, 512], P(None, 'ctx', 'kv'), may hold values from -9 to 9
- value_weight: bfloat16 [1, 16384, 512], P(None, 'ctx', 'kv'), may hold values from -0.046875 to 0.046875
- out_weight: bfloat16 [1, 4096, 16384], P(None, 'kv', 'ctx'), may hold values from -0.09375 to 0.09375
- lengths: int32 [2], replicated, may hold values from 320 to 1280, as said below
- positions: int32 [2], replicated, may hold values from 320 to 2559, as said below
Outputs:
- hidden_out: float32 [2, 16384], P(None, 'ctx')
Inputs may be any that keep to these rules, and one draw needn't show every extreme that they name: `lengths`: one request's length equals 1280. lengths[r] <= positions[r] < lengths[r] + 1280 for every request.
All inputs are finite; a program needn't handle non-finite values.
Results may differ from a plain program's by a relative error of at most 0.0045.
The roundings to bfloat16 on the way count: a program that leaves them out, or rounds other values in their place, can miss the bound.
Values may be sent and summed in bfloat16 or wider, within the bound.
No kernel may reach another device: no remote copies, remote signals or barrier semaphores. Data moves between devices by JAX's collectives and lax.ppermute only.
A program may use at most 128 MiB of HBM per device.

v0:
```python
import math

import jax
import jax.numpy as jnp
from jax import lax
from jax.sharding import PartitionSpec as P

ROPE_BASE = 500000.0
EPSILON = 1e-05
FLOOR = -1e30


def rms_scaled(row_block, gain_row):
    values = row_block.astype(jnp.float32)
    factor = lax.rsqrt(jnp.mean(values * values, axis=-1, keepdims=True) + EPSILON)
    return (values * factor * gain_row).astype(jnp.bfloat16)


def rotary(values, placed):
    half_size = values.shape[-1] // 2
    frequency = jnp.exp(
        jnp.arange(half_size, dtype=jnp.float32) * (-2.0 * math.log(ROPE_BASE) / values.shape[-1])
    )
    angles = placed[..., None] * frequency
    cosine = jnp.cos(angles)
    sine_part = jnp.sin(angles)
    leading = values[..., :half_size]
    trailing = values[..., half_size:]
    return jnp.concatenate(
        (leading * cosine - trailing * sine_part, trailing * cosine + leading * sine_part), axis=-1
    )


def add_columns(pieces_in, normed_rows):
    return (
        jnp.dot(normed_rows, pieces_in[0], preferred_element_type=jnp.float32),
        jnp.dot(normed_rows, pieces_in[1], preferred_element_type=jnp.float32),
    )


def shards(
    new_tokens,
    ctx_hidden,
    norm_gain,
    query_weight,
    key_weight,
    value_weight,
    out_weight,
    lengths,
    positions,
):
    ctx_count = lax.axis_size("ctx")
    ctx_place = lax.axis_index("ctx")
    row_count = ctx_hidden.shape[1]
    head_size = key_weight.shape[2]
    group_heads = query_weight.shape[2] // head_size
    requests = new_tokens.shape[0]
    slice_width = new_tokens.shape[1]
    slot_count = row_count * ctx_count // requests
    global_rows = ctx_place * row_count + jnp.arange(row_count, dtype=jnp.int32)
    owners = global_rows // slot_count
    within = global_rows % slot_count
    request_ids = jnp.arange(requests, dtype=jnp.int32)
    valid = (owners[None, :] == request_ids[:, None]) & (within[None, :] < lengths[:, None])
    key_places = within.astype(jnp.float32)
    new_places = positions.astype(jnp.float32)
    scale = 1.0 / math.sqrt(head_size)
    state = new_tokens
    gain_row = norm_gain[0]
    full_state = lax.all_gather(state, "ctx", axis=1, tiled=True)
    normed = rms_scaled(full_state, gain_row)
    own_columns = lax.dynamic_slice_in_dim(normed, ctx_place * slice_width, slice_width, 1)
    query_part = jnp.dot(own_columns, query_weight[0], preferred_element_type=jnp.float32)
    key_part = jnp.dot(own_columns, key_weight[0], preferred_element_type=jnp.float32)
    value_part = jnp.dot(own_columns, value_weight[0], preferred_element_type=jnp.float32)
    query_sum, key_sum, value_sum = lax.psum((query_part, key_part, value_part), "ctx")
    queries = rotary(
        query_sum.reshape(requests, group_heads, head_size), new_places[:, None]
    ).astype(jnp.bfloat16)
    self_key = rotary(key_sum, new_places).astype(jnp.bfloat16)
    self_value = value_sum.astype(jnp.bfloat16)
    ctx_normed = rms_scaled(ctx_hidden[0], gain_row)
    keys_raw, values_raw = add_columns(
        (
            lax.all_gather(key_weight[0], "ctx", axis=0, tiled=True),
            lax.all_gather(value_weight[0], "ctx", axis=0, tiled=True),
        ),
        normed_rows=ctx_normed,
    )
    ctx_keys = rotary(keys_raw, key_places).astype(jnp.bfloat16)
    ctx_values = values_raw.astype(jnp.bfloat16)
    scores = (
        jnp.einsum("rgh,nh->rgn", queries, ctx_keys, preferred_element_type=jnp.float32) * scale
    )
    masked = jnp.where(valid[:, None, :], scores, FLOOR)
    self_scores = (
        jnp.einsum("rgh,rh->rg", queries, self_key, preferred_element_type=jnp.float32) * scale
    )
    local_top = jnp.maximum(jnp.max(masked, axis=-1), self_scores)
    highest = lax.pmax(local_top, "ctx")
    weights = jnp.where(valid[:, None, :], jnp.exp(masked - highest[..., None]), 0.0).astype(
        jnp.bfloat16
    )
    mass_part = jnp.sum(weights.astype(jnp.float32), axis=-1)
    accum_part = jnp.einsum("rgn,nh->rgh", weights, ctx_values, preferred_element_type=jnp.float32)
    mass, accum = lax.psum((mass_part, accum_part), "ctx")
    self_weight = jnp.exp(self_scores - highest).astype(jnp.bfloat16).astype(jnp.float32)
    total_mass = mass + self_weight
    accum = accum + self_weight[..., None] * self_value.astype(jnp.float32)[:, None, :]
    attended = (
        (accum / total_mass[..., None])
        .reshape(requests, group_heads * head_size)
        .astype(jnp.bfloat16)
    )
    update = jnp.dot(attended, out_weight[0], preferred_element_type=jnp.float32)
    state = state + lax.psum(update, "kv")
    return state


def solution(mesh):
    in_specs = (
        P(None, "ctx"),
        P(None, "ctx", None),
        P(),
        P(None, "ctx", "kv"),
        P(None, "ctx", "kv"),
        P(None, "ctx", "kv"),
        P(None, "kv", "ctx"),
        P(),
        P(),
    )
    out_specs = P(None, "ctx")
    return jax.shard_map(shards, mesh=mesh, in_specs=in_specs, out_specs=out_specs, check_vma=False)
```

profile of v0, /device:TPU:0, one launch (start us, length us, event | category | flops | bytes accessed | tf_op | source)
XLA Modules:
  0.0 148.6 jit_solution(5164165735427725781)
XLA Ops:
  6.5 0.0 copy-start.2
  6.5 0.0 copy-start.3
  6.5 0.0 all-gather.5.cloned.1.call-start
  6.5 0.7 all-gather.5.cloned.1.call-update
  7.3 0.0 all-gather.7.cloned.1.call-start
  7.3 0.7 all-gather.7.cloned.1.call-update
  8.0 0.7 dynamic-slice
  8.7 10.8 %all_gather.9 = f32[2,16384]{1,0:T(2,128)S(1)} all-gather(f32[2,2048]{1,0:T(2,128)} %param.9), channel_id=1, replica_groups=mesh['ctx'=8,'kv'=4] {'ctx'}, dimensions={1}, use_global_device_ids=true | all-gather | bytes 147456 | tf_op jit(solution)/shard_map/all_gather | solution.py:70
  19.5 0.2 multiply_reduce_fusion
  19.8 3.0 %fusion.24 = f32[1,2,8,128]{3,1,2,0:T(2,128)S(1)} fusion(bf16[1,2048,1024]{2,1,0:T(8,128)(2,1)} %param.12, f32[2,16384]{1,0:T(2,128)S(1)} %all_gather.9, s32[]{:T(128)S(6)} %select_n.36, f32[2]{0:T(128)S(1)} %add_rsqrt_fusion.1, f32[2048]{0:T(1024)S(1)} %dynamic-slice), kind=kOutput, calls=%fused_computation.17 | convolution fusion | flops 8400896 | bytes 4227588 | tf_op jit(solution)/shard_map/dot_general | solution.py:73
  22.8 0.7 convert_element_type.53
  23.5 1.3 fusion.34
  24.8 14.1 %all-reduce.1 = (f32[2,8,128]{2,1,0:T(8,128)S(1)}, f32[2,128]{1,0:T(2,128)S(1)}) all-reduce(f32[2,8,128]{2,1,0:T(8,128)S(1)} %bitcast.62, f32[2,128]{1,0:T(2,128)S(1)} %fusion.34), channel_id=1, replica_groups=mesh['ctx'=8,'kv'=4] {'ctx'}, use_global_device_ids=true, to_apply=%region_1.2 | all-reduce | flops 2304 | bytes 18432 | tf_op jit(solution)/shard_map/psum | solution.py:76
  38.9 0.1 subtract_convert_fusion.1
  39.0 0.1 maximum_bitcast_fusion.2
  39.1 0.1 subtract_convert_fusion
  39.2 0.2 fusion.56
  39.4 6.3 %fusion = f32[320]{0:T(512)S(1)} fusion(bf16[1,320,16384]{2,1,0:T(8,128)(2,1)} %param.10), kind=kLoop, calls=%fused_computation.2 | loop fusion | flops 15728320 | bytes 10487040 | tf_op jit(solution)/shard_map/reduce_sum | solution.py:15
  45.7 0.0 copy-done.3
  45.7 0.1 compare_and_fusion
  45.8 0.0 copy-start
  45.8 3.1 %all-gather.5.cloned.1.call-done = bf16[1,16384,128]{2,1,0:T(8,128)(2,1)} async-done(((bf16[1,2048,128]{2,1,0:T(8,128)(2,1)}), bf16[1,16384,128]{2,1,0:T(8,128)(2,1)}) %all-gather.5.cloned.1.call-update) | async-done | bytes 4194320 | tf_op jit(solution)/shard_map/all_gather | solution.py:85
  48.8 0.0 copy-done.2
  48.8 7.4 %fusion.7 = f32[320,128]{1,0:T(8,128)S(1)} fusion(bf16[1,16384,128]{2,1,0:T(8,128)(2,1)} %all-gather.5.cloned.1.call-done, bf16[1,320,16384]{2,1,0:T(8,128)(2,1)} %param.10, f32[16384]{0:T(1024)S(1)} %bitcast.66, f32[320]{0:T(512)S(1)} %add_rsqrt_fusion), kind=kOutput, calls=%fused_computation.9 | convolution fusion | flops 1363148800 | bytes 14910720 | tf_op jit(solution)/shard_map/dot_general | solution.py:36
  56.3 0.7 fusion.41
  57.0 0.3 fusion.68
  57.3 0.0 copy-done
  57.3 0.2 fusion.32
  57.5 13.3 %pmax.7 = f32[2,8]{1,0:T(2,128)S(1)} all-reduce(f32[2,8]{1,0:T(2,128)S(1)} %multiply_maximum_fusion), channel_id=1, replica_groups=mesh['ctx'=8,'kv'=4] {'ctx'}, use_global_device_ids=true, to_apply=%region_5.6 | all-reduce | flops 16 | bytes 128 | tf_op jit(solution)/shard_map/pmax | solution.py:100
  70.8 16.7 %all-gather.7.cloned.1.call-done = bf16[1,16384,128]{2,1,0:T(8,128)(2,1)} async-done(((bf16[1,2048,128]{2,1,0:T(8,128)(2,1)}), bf16[1,16384,128]{2,1,0:T(8,128)(2,1)}) %all-gather.7.cloned.1.call-update) | async-done | bytes 4194320 | tf_op jit(solution)/shard_map/all_gather | solution.py:86
  87.6 0.0 copy-start.1
  87.6 8.2 %fusion.29 = f32[2,8,128]{2,1,0:T(8,128)S(1)} fusion(bf16[1,16384,128]{2,1,0:T(8,128)(2,1)} %all-gather.7.cloned.1.call-done, bf16[1,320,16384]{2,1,0:T(8,128)(2,1)} %param.10, f32[16384]{0:T(1024)S(1)} %bitcast.67, f32[320]{0:T(512)S(1)} %add_rsqrt_fusion, f32[2,8,320]{2,1,0:T(8,128)S(1)} %get-tuple-element.21, f32[2,8]{1,0:T(2,128)S(1)} %pmax.7, ...), kind=kOutput, calls=%fused_computation.18 | convolution fusion | flops 1364515840 | bytes 14776256 | tf_op jit(solution)/shard_map/rgn,nh->rgh/dot_general | solution.py:105
  95.8 0.2 convert_reduce_fusion
  96.0 23.5 %all-reduce = (f32[2,8]{1,0:T(2,128)S(1)}, f32[2,8,128]{2,1,0:T(8,128)S(1)}, bf16[2,128]{1,0:T(2,128)(2,1)S(1)}) all-reduce(f32[2,8]{1,0:T(2,128)S(1)} %convert_reduce_fusion, f32[2,8,128]{2,1,0:T(8,128)S(1)} %fusion.29, f32[2,128]{1,0:T(2,128)S(1)} %fusion.32), channel_id=1, replica_groups=mesh['ctx'=8,'kv'=4] {'ctx'}, use_global_device_ids=true, to_apply=%region_9.10 | all-reduce | flops 2320 | bytes 18048 | tf_op jit(solution)/shard_map/psum | solution.py:106
  119.5 0.1 fusion.50
  119.5 2.8 %fusion.3 = f32[2,2048]{1,0:T(2,128)S(1)} fusion(bf16[1,1024,2048]{2,1,0:T(8,128)(2,1)} %param.15, bf16[1,2,8,128]{3,2,1,0:T(8,128)(2,1)S(1)} %fusion.50), kind=kOutput, calls=%fused_computation.5 | convolution fusion | flops 8388608 | bytes 4214784 | tf_op jit(solution)/shard_map/dot_general | solution.py:115
  122.4 18.7 %psum.47 = f32[2,2048]{1,0:T(2,128)S(1)} all-reduce(f32[2,2048]{1,0:T(2,128)S(1)} %fusion.3), channel_id=1, replica_groups=mesh['ctx'=8,'kv'=4] {'kv'}, use_global_device_ids=true, to_apply=%region_10.11 | all-reduce | flops 4096 | bytes 32768 | tf_op jit(solution)/shard_map/psum | solution.py:116
  141.1 0.0 copy-done.1
  141.1 0.6 add.100
  (9 shorter events, 0.1 us)
Async XLA Ops:
  6.5 42.3 %copy-start.2 = (f32[1,16384]{1,0:T(1,128)S(1)}, f32[1,16384]{1,0:T(1,128)}, u32[]{:S(2)}) copy-start(f32[1,16384]{1,0:T(1,128)} %param.11) | copy-start | bytes 196612
  6.5 39.1 %copy-start.3 = (s32[2]{0:T(128)S(1)}, s32[2]{0:T(128)}, u32[]{:S(2)}) copy-start(s32[2]{0:T(128)} %param.16) | copy-start | bytes 28
  6.5 42.3 %all-gather.5.cloned.1.call-start = ((), (), s32[]{:S(2)}) async-start(), calls=%async_computation | async-start | bytes 4718592 | tf_op jit(solution)/shard_map/all_gather | solution.py:85
  7.3 80.3 %all-gather.7.cloned.1.call-start = ((), (), s32[]{:S(2)}) async-start(), calls=%async_computation.1 | async-start | bytes 4718592 | tf_op jit(solution)/shard_map/all_gather | solution.py:86
  45.8 11.5 %copy-start = (bf16[1,2048,128]{2,1,0:T(8,128)(2,1)S(1)}, bf16[1,2048,128]{2,1,0:T(8,128)(2,1)}, u32[]{:S(2)}) copy-start(bf16[1,2048,128]{2,1,0:T(8,128)(2,1)} %param.14) | copy-start | bytes 1572868
  87.6 53.6 %copy-start.1 = (f32[2,2048]{1,0:T(2,128)S(1)}, f32[2,2048]{1,0:T(2,128)}, u32[]{:S(2)}) copy-start(f32[2,2048]{1,0:T(2,128)} %param.9) | copy-start | bytes 49156
Sparse Core Ops, SparseCore 0:
  9.2 39.5 all-gather.4
  50.7 36.7 all-gather.6
where the time goes:
time: 149 us
  blocking collectives  80.5 us (54%)
  matrix products  23.5 us (16%)
  waiting for transfers between devices  21.2 us (14%)
  between operations  13.5 us (9%)
  other arithmetic  9.16 us (6%)
    psum x1, blocking collectives, shards(): mass, accum = lax.psum((mass_part, accum_part), 'ctx')  23.5 us
    psum x1, blocking collectives, shards(): state = state + lax.psum(update, 'kv')  18.7 us
    all_gather x1, waiting for transfers between devices, shards(): lax.all_gather(value_weight[0], 'ctx', axis=0, tiled=True)  16.7 us
    psum x1, blocking collectives, shards(): lax.psum((query_part, key_part, value_part), 'ctx')  14.1 us
    pmax x1, blocking collectives, shards(): highest = lax.pmax(local_top, 'ctx')  13.3 us
    all_gather x1, blocking collectives, shards(): full_state = lax.all_gather(state, 'ctx', axis=1, tiled=True)  10.8 us
    dot_general x1, matrix products, shards(): jnp.einsum('rgn,nh->rgh', weights, ctx_values, preferred_element_type=jnp...  8.23 us
    dot_general x1, matrix products, add_columns(): jnp.dot(normed_rows, pieces_in[0], preferred_element_type=jnp.float32)  7.42 us
  transfers between devices with their start and end apart: 2, of which 2 were waited for; matrix products, arithmetic and copies ran while one was open for 14% of the time, Pallas kernels for 0%

commit v1 on v0

v1 whole, which is shorter than its diff:
```python
import math

import jax
import jax.numpy as jnp
from jax import lax
from jax.sharding import PartitionSpec as P

ROPE_BASE = 500000.0
EPSILON = 1e-05
FLOOR = -1e30


def swap(value, axis, distance):
    count = lax.axis_size(axis)
    return lax.ppermute(value, axis, [(i, i ^ distance) for i in range(count)])


def tree(parts, join):
    while len(parts) > 1:
        parts = [join(parts[i], parts[i + 1]) for i in range(0, len(parts), 2)]
    return parts[0]


def pick(values, index):
    return lax.dynamic_index_in_dim(values, index, 0, keepdims=False)


def exchange_all(value, axis, count):
    return [value] + [swap(value, axis, d) for d in range(1, count)]


def rotary(values, placed):
    half_size = values.shape[-1] // 2
    frequency = jnp.exp(
        jnp.arange(half_size, dtype=jnp.float32) * (-2.0 * math.log(ROPE_BASE) / values.shape[-1])
    )
    angles = placed[..., None] * frequency
    cosine = jnp.cos(angles)
    sine_part = jnp.sin(angles)
    leading = values[..., :half_size]
    trailing = values[..., half_size:]
    return jnp.concatenate(
        (leading * cosine - trailing * sine_part, trailing * cosine + leading * sine_part), axis=-1
    )


def gather_blocks(own):
    count = lax.axis_size("ctx")
    rows = own.shape[0]
    held = [[(0, 0, own[: rows // 2])], [(0, rows // 2, own[rows // 2 :])]]
    bits = [1 << b for b in range(1, count.bit_length() - 1)]
    orders = [bits, bits[::-1]]
    for step in range(len(bits)):
        for part in range(2):
            bit = orders[part][step]
            held[part] = held[part] + [
                (d ^ bit, first, swap(block, "ctx", bit)) for d, first, block in held[part]
            ]
    blocks = held[0] + held[1]
    return blocks + [(d ^ 1, first, swap(block, "ctx", 1)) for d, first, block in blocks]


def project(rows_in, blocks, place, width):
    total = None
    for distance, first, block in blocks:
        columns = lax.dynamic_slice_in_dim(
            rows_in, (place ^ distance) * width + first, block.shape[0], 1
        )
        part = jnp.dot(columns, block, preferred_element_type=jnp.float32)
        total = part if total is None else total + part
    return total


def shards(
    new_tokens,
    ctx_hidden,
    norm_gain,
    query_weight,
    key_weight,
    value_weight,
    out_weight,
    lengths,
    positions,
):
    ctx_count = lax.axis_size("ctx")
    kv_count = lax.axis_size("kv")
    place = lax.axis_index("ctx")
    row_count, features = ctx_hidden.shape[1:]
    head_size = key_weight.shape[2]
    heads = query_weight.shape[2] // head_size
    requests, width = new_tokens.shape
    slot_count = row_count * ctx_count // requests
    team = slot_count // row_count
    request = place // team
    scale = 1.0 / math.sqrt(head_size)
    gain_row = norm_gain[0]

    key_blocks = gather_blocks(key_weight[0])
    value_blocks = gather_blocks(value_weight[0])

    squares = jnp.sum(new_tokens * new_tokens, axis=-1)
    squares = tree(exchange_all(squares, "ctx", ctx_count), jnp.add)
    factor = lax.rsqrt(squares / features + EPSILON)[:, None]
    own_gain = lax.dynamic_slice_in_dim(gain_row, place * width, width, 0)
    normed = (new_tokens * factor * own_gain).astype(jnp.bfloat16)
    parts = jnp.concatenate(
        [
            jnp.dot(normed, weight[0], preferred_element_type=jnp.float32)
            for weight in (query_weight, key_weight, value_weight)
        ],
        axis=1,
    ).reshape(requests, heads + 2, head_size)
    summed = tree(
        [pick(parts, request)]
        + [swap(pick(parts, (place ^ d) // team), "ctx", d) for d in range(1, ctx_count)],
        jnp.add,
    )
    new_place = pick(positions, request).astype(jnp.float32)
    turned = rotary(summed[: heads + 1], new_place[None]).astype(jnp.bfloat16)
    queries = turned[:heads]
    self_key = turned[heads]
    self_value = summed[heads + 1].astype(jnp.bfloat16).astype(jnp.float32)
    self_scores = (
        jnp.sum(queries.astype(jnp.float32) * self_key.astype(jnp.float32), axis=-1) * scale
    )

    hidden = ctx_hidden[0].astype(jnp.float32)
    row_factor = lax.rsqrt(jnp.mean(hidden * hidden, axis=-1, keepdims=True) + EPSILON)
    ctx_normed = (hidden * row_factor * gain_row).astype(jnp.bfloat16)
    within = (place % team) * row_count + jnp.arange(row_count, dtype=jnp.int32)
    live = within < pick(lengths, request)
    ctx_keys = rotary(
        project(ctx_normed, key_blocks, place, width), within.astype(jnp.float32)
    ).astype(jnp.bfloat16)
    scores = jnp.einsum("gh,nh->gn", queries, ctx_keys, preferred_element_type=jnp.float32) * scale
    masked = jnp.where(live[None, :], scores, FLOOR)
    top = jnp.maximum(jnp.max(masked, axis=-1), self_scores)
    top = tree(exchange_all(top, "ctx", team), jnp.maximum)
    weights = jnp.where(live[None, :], jnp.exp(masked - top[:, None]), 0.0).astype(jnp.bfloat16)
    self_weight = jnp.exp(self_scores - top).astype(jnp.bfloat16).astype(jnp.float32)
    self_weight = jnp.where(place % team == 0, self_weight, 0.0)
    mass = jnp.sum(weights.astype(jnp.float32), axis=-1) + self_weight
    ctx_values = project(ctx_normed, value_blocks, place, width).astype(jnp.bfloat16)
    accum = jnp.dot(weights, ctx_values, preferred_element_type=jnp.float32)
    accum = accum + self_weight[:, None] * self_value

    packed = jnp.concatenate((accum, jnp.broadcast_to(mass[:, None], accum.shape)), axis=1)
    packed = exchange_all(packed, "ctx", ctx_count)
    sums = jnp.stack(
        [tree(packed[j * team : (j + 1) * team], jnp.add) for j in range(requests)]
    )
    sums = sums[jnp.arange(requests) ^ request]
    attended = (sums[..., :head_size] / sums[..., head_size:]).astype(jnp.bfloat16)
    update = jnp.dot(
        attended.reshape(requests, heads * head_size),
        out_weight[0],
        preferred_element_type=jnp.float32,
    )
    return new_tokens + tree(exchange_all(update, "kv", kv_count), jnp.add)


def solution(mesh):
    in_specs = (
        P(None, "ctx"),
        P(None, "ctx", None),
        P(),
        P(None, "ctx", "kv"),
        P(None, "ctx", "kv"),
        P(None, "ctx", "kv"),
        P(None, "kv", "ctx"),
        P(),
        P(),
    )
    out_specs = P(None, "ctx")
    return jax.shard_map(shards, mesh=mesh, in_specs=in_specs, out_specs=out_specs, check_vma=False)
```

time: 149 us -> 145 us (0.973)
  blocking collectives: 80.5 us -> 0 us
  starting transfers between devices: 0.04 us -> 43.7 us
  waiting for transfers between devices: 21.2 us -> 35.5 us
  matrix products: 23.5 us -> 37.7 us
  between operations: 13.5 us -> 1.47 us
  local copies, waits for them, and re-layouts: 0.72 us -> 8.62 us
  other arithmetic: 9.16 us -> 16.8 us
    psum x3 -> x0, blocking collectives: 56.3 us -> none  [the longest x1 23.5 us: shards(): mass, accum = lax.psum((mass_part, accum_part), 'ctx')]
    ppermute x0 -> x55, starting transfers between devices: none -> 43.7 us  [swap(): return lax.ppermute(value, axis, [(i, i ^ distance) for i in range(count)])]
    ppermute x0 -> x55, waiting for transfers between devices: none -> 35.5 us  [swap(): return lax.ppermute(value, axis, [(i, i ^ distance) for i in range(count)])]
    all_gather x2 -> x0, waiting for transfers between devices: 19.8 us -> none  [the longest x1 16.7 us: shards(): lax.all_gather(value_weight[0], 'ctx', axis=0, tiled=True)]
    dot_general x8 -> x37, matrix products: 23.5 us -> 37.7 us  [the longest x31 29.6 us: project(): part = jnp.dot(columns, block, preferred_element_type=jnp.float32)]
    pmax x1 -> x0, blocking collectives: 13.3 us -> none  [shards(): highest = lax.pmax(local_top, 'ctx')]
    all_gather x1 -> x0, blocking collectives: 10.8 us -> none  [shards(): full_state = lax.all_gather(state, 'ctx', axis=1, tiled=True)]
    convert_element_type x3 -> x2, other arithmetic: 0.68 us -> 6.85 us  [the longest x1 6.85 us: shards(): ctx_normed = (hidden * row_factor * gain_row).astype(jnp.bfloat16)]
  transfers between devices with their start and end apart: 2 -> 55, of which waited for: 2 -> 15; matrix products, arithmetic and copies ran while one was open for 14% -> 34% of each run, Pallas kernels for 0% -> 0%
where the time goes in v1:
time: 145 us; the launch traced here: 144 us
  starting transfers between devices  43.7 us (30%)
  matrix products  37.7 us (26%)
  waiting for transfers between devices  35.5 us (24%)
  other arithmetic  16.8 us (12%)
  local copies, waits for them, and re-layouts  8.62 us (6%)
  between operations  1.47 us (1%)
    ppermute x55, starting transfers between devices, swap(): return lax.ppermute(value, axis, [(i, i ^ distance) for i in range(count)])  43.7 us
    ppermute x55, waiting for transfers between devices, swap(): return lax.ppermute(value, axis, [(i, i ^ distance) for i in range(count)])  35.5 us
    dot_general x31, matrix products, project(): part = jnp.dot(columns, block, preferred_element_type=jnp.float32)  29.6 us
    convert_element_type x1, other arithmetic, shards(): ctx_normed = (hidden * row_factor * gain_row).astype(jnp.bfloat16)  6.85 us
    reduce_sum x1, other arithmetic, shards(): jnp.mean(hidden * hidden, axis=-1, keepdims=True) + EPSILON  6.15 us
    unnamed x22, local copies, waits for them, and re-layouts  4.09 us
    dot_general x3, matrix products, shards(): jnp.dot(normed, weight[0], preferred_element_type=jnp.float32)  3.39 us
  transfers between devices with their start and end apart: 55, of which 15 were waited for; matrix products, arithmetic and copies ran while one was open for 34% of the time, Pallas kernels for 0%

profile of v1, /device:TPU:0, one launch (start us, length us, event | category | flops | bytes accessed | tf_op | source)
XLA Modules:
  0.0 143.9 jit_solution(10363281274310074208)
XLA Ops:
  0.0 0.9 multiply_reduce_fusion
  0.9 4.0 %collective-permute-start.5 = (f32[2]{0:T(128)S(1)}, f32[2]{0:T(128)S(1)}, u32[]{:S(2)}, u32[]{:S(2)}) collective-permute-start(f32[2]{0:T(128)S(1)} %multiply_reduce_fusion), channel_id=1, source_target_pairs={{0,24},{4,28},{8,16},{12,20},{16,8},{20,12},{24,0},{28,4},{1,25},{... | collective-permute-start | bytes 32 | tf_op jit(solution)/shard_map/ppermute | solution.py:15
  4.8 1.2 collective-permute-start.3
  6.0 0.6 collective-permute-start.4
  6.6 1.7 %collective-permute-start.1 = (f32[2]{0:T(128)S(1)}, f32[2]{0:T(128)S(1)}, u32[]{:S(2)}, u32[]{:S(2)}) collective-permute-start(f32[2]{0:T(128)S(1)} %multiply_reduce_fusion), channel_id=1, source_target_pairs={{0,8},{4,12},{8,0},{12,4},{16,24},{20,28},{24,16},{28,20},{1,9},{5... | collective-permute-start | bytes 32 | tf_op jit(solution)/shard_map/ppermute | solution.py:15
  8.3 1.9 %slice_bitcast_fusion.3 = (bf16[1024,128]{1,0:T(8,128)(2,1)}, bf16[1024,128]{1,0:T(8,128)(2,1)}) fusion(bf16[1,2048,128]{2,1,0:T(8,128)(2,1)} %param.13), kind=kLoop, calls=%fused_computation.98 | loop fusion | bytes 1048576 | tf_op jit(solution)/shard_map/slice | solution.py:50
  10.1 6.2 %fusion = f32[320]{0:T(512)S(1)} fusion(bf16[1,320,16384]{2,1,0:T(8,128)(2,1)} %param.10), kind=kLoop, calls=%fused_computation.3 | loop fusion | flops 15728320 | bytes 10487040 | tf_op jit(solution)/shard_map/reduce_sum | solution.py:128
  16.4 6.8 %fusion.2 = bf16[320,16384]{1,0:T(8,128)(2,1)S(1)} fusion(bf16[1,320,16384]{2,1,0:T(8,128)(2,1)} %param.10, f32[16384]{0:T(1024)S(1)} %bitcast.103, f32[320]{0:T(512)S(1)} %add_rsqrt_fusion), kind=kLoop, calls=%fused_computation.5 | loop fusion | flops 20971520 | bytes 21038336 | tf_op jit(solution)/shard_map/convert_element_type | solution.py:129
  23.2 4.0 %copy-done = bf16[320,16384]{1,0:T(8,128)(2,1)} copy-done((bf16[320,16384]{1,0:T(8,128)(2,1)}, bf16[320,16384]{1,0:T(8,128)(2,1)S(1)}, u32[]{:S(2)}) %copy-start) | copy-done | bytes 10485784
  27.3 1.0 fusion.68
  28.3 1.4 fusion.58
  29.7 0.8 slice_bitcast_fusion.1
  30.6 1.4 fusion.56
  32.0 2.2 %fusion.66 = f32[320,128]{1,0:T(8,128)} fusion(bf16[320,16384]{1,0:T(8,128)(2,1)} %copy-done, s32[]{:T(128)S(6)} %select_n.155, bf16[1,2048,128]{2,1,0:T(8,128)(2,1)S(1)} %copy-done.1), kind=kOutput, calls=%fused_computation.87 | convolution fusion | flops 83886080 | bytes 1081348 | tf_op jit(solution)/shard_map/dot_general | solution.py:69
  36.2 2.5 %collective-permute-done.2 = f32[2]{0:T(128)S(1)} collective-permute-done((f32[2]{0:T(128)S(1)}, f32[2]{0:T(128)S(1)}, u32[]{:S(2)}, u32[]{:S(2)}) %collective-permute-start.2) | collective-permute-done | bytes 40 | tf_op jit(solution)/shard_map/ppermute | solution.py:15
  39.1 2.9 %fusion.5 = f32[2,1024]{1,0:T(2,128)S(1)} fusion(bf16[1,2048,1024]{2,1,0:T(8,128)(2,1)} %param.12, f32[2,2048]{1,0:T(2,128)S(1)} %copy-done.4, f32[2]{0:T(128)S(1)} %add_rsqrt_fusion.1, f32[2048]{0:T(1024)S(1)} %bitcast.106), kind=kOutput, calls=%fused_computation.8 | convolution fusion | flops 8400896 | bytes 4227080 | tf_op jit(solution)/shard_map/dot_general | solution.py:108
  42.2 1.5 %collective-permute-start.12 = (f32[10,128]{1,0:T(8,128)S(1)}, f32[10,128]{1,0:T(8,128)S(1)}, u32[]{:S(2)}, u32[]{:S(2)}) collective-permute-start(f32[10,128]{1,0:T(8,128)S(1)} %get-tuple-element.15), channel_id=1, source_target_pairs={{0,24},{4,28},{8,16},{12,20},{16,8},{20,12},{24,0},{28,4},{1,25},{... | collective-permute-start | bytes 15368 | tf_op jit(solution)/shard_map/ppermute | solution.py:15
  44.4 1.2 collective-permute-start.13
  45.6 1.5 %collective-permute-start.10 = (f32[10,128]{1,0:T(8,128)S(1)}, f32[10,128]{1,0:T(8,128)S(1)}, u32[]{:S(2)}, u32[]{:S(2)}) collective-permute-start(f32[10,128]{1,0:T(8,128)S(1)} %get-tuple-element.17), channel_id=1, source_target_pairs={{0,16},{4,20},{8,24},{12,28},{16,0},{20,4},{24,8},{28,12},{1,17},{... | collective-permute-start | bytes 15368 | tf_op jit(solution)/shard_map/ppermute | solution.py:15
  47.7 1.4 collective-permute-start.9
  49.1 0.7 fusion.126
  50.4 1.7 %collective-permute-start.15 = (bf16[1024,128]{1,0:T(8,128)(2,1)}, bf16[1024,128]{1,0:T(8,128)(2,1)S(1)}, u32[]{:S(2)}, u32[]{:S(2)}) collective-permute-start(bf16[1024,128]{1,0:T(8,128)(2,1)} %get-tuple-element.9), channel_id=1, source_target_pairs={{0,16},{4,20},{8,24},{12,28},{16,0},{20,4},{24,8},{28,12},{1,17},{... | collective-permute-start | bytes 786440 | tf_op jit(solution)/shard_map/ppermute | solution.py:15
  52.0 1.5 %collective-permute-start.14 = (bf16[1024,128]{1,0:T(8,128)(2,1)}, bf16[1024,128]{1,0:T(8,128)(2,1)S(1)}, u32[]{:S(2)}, u32[]{:S(2)}) collective-permute-start(bf16[1024,128]{1,0:T(8,128)(2,1)} %get-tuple-element.9), channel_id=1, source_target_pairs={{0,8},{4,12},{8,0},{12,4},{16,24},{20,28},{24,16},{28,20},{1,9},{5... | collective-permute-start | bytes 786440 | tf_op jit(solution)/shard_map/ppermute | solution.py:15
  54.4 10.4 %collective-permute-done.14 = bf16[1024,128]{1,0:T(8,128)(2,1)S(1)} collective-permute-done((bf16[1024,128]{1,0:T(8,128)(2,1)}, bf16[1024,128]{1,0:T(8,128)(2,1)S(1)}, u32[]{:S(2)}, u32[]{:S(2)}) %collective-permute-start.14) | collective-permute-done | bytes 262176 | tf_op jit(solution)/shard_map/ppermute | solution.py:15
  64.8 1.5 %convolution_add_fusion.17 = f32[320,128]{1,0:T(8,128)S(1)} fusion(f32[320,128]{1,0:T(8,128)} %fusion.68, bf16[1024,128]{1,0:T(8,128)(2,1)S(1)} %collective-permute-done.14, bf16[320,16384]{1,0:T(8,128)(2,1)} %copy-done, s32[]{:T(128)S(6)} %select_n.170), kind=kOutput, calls=%fused_computation.27 | convolution fusion | flops 83927040 | bytes 1245188 | tf_op jit(solution)/shard_map/dot_general | solution.py:69
  66.3 3.6 %collective-permute-done.31 = bf16[1024,128]{1,0:T(8,128)(2,1)S(1)} collective-permute-done((bf16[1024,128]{1,0:T(8,128)(2,1)}, bf16[1024,128]{1,0:T(8,128)(2,1)S(1)}, u32[]{:S(2)}, u32[]{:S(2)}) %collective-permute-start.31) | collective-permute-done | bytes 262176 | tf_op jit(solution)/shard_map/ppermute | solution.py:15
  69.9 1.5 %collective-permute-start.17 = (bf16[1024,128]{1,0:T(8,128)(2,1)}, bf16[1024,128]{1,0:T(8,128)(2,1)S(1)}, u32[]{:S(2)}, u32[]{:S(2)}) collective-permute-start(bf16[1024,128]{1,0:T(8,128)(2,1)} %get-tuple-element.10), channel_id=1, source_target_pairs={{0,16},{4,20},{8,24},{12,28},{16,0},{20,4},{24,8},{28,12},{1,17},{... | collective-permute-start | bytes 786440 | tf_op jit(solution)/shard_map/ppermute | solution.py:15
  71.4 1.5 %convolution_add_fusion.8 = f32[320,128]{1,0:T(8,128)S(1)} fusion(f32[320,128]{1,0:T(8,128)} %fusion.66, bf16[1024,128]{1,0:T(8,128)(2,1)S(1)} %collective-permute-done.31, bf16[320,16384]{1,0:T(8,128)(2,1)} %copy-done, s32[]{:T(128)S(6)} %select_n.170), kind=kOutput, calls=%fused_computation.18 | convolution fusion | flops 83927040 | bytes 1245188 | tf_op jit(solution)/shard_map/dot_general | solution.py:69
  73.0 1.4 convolution_add_fusion.16
  74.4 0.6 collective-permute-start.35
  75.0 1.4 fusion.34
  76.9 1.4 fusion.32
  78.4 1.4 fusion.46
  79.9 1.7 %collective-permute-start.34 = (bf16[1024,128]{1,0:T(8,128)(2,1)}, bf16[1024,128]{1,0:T(8,128)(2,1)S(1)}, u32[]{:S(2)}, u32[]{:S(2)}) collective-permute-start(bf16[1024,128]{1,0:T(8,128)(2,1)} %get-tuple-element.8), channel_id=1, source_target_pairs={{0,16},{4,20},{8,24},{12,28},{16,0},{20,4},{24,8},{28,12},{1,17},{... | collective-permute-start | bytes 786440 | tf_op jit(solution)/shard_map/ppermute | solution.py:15
  81.6 1.4 fusion.52
  83.3 1.6 %fusion.44 = f32[320,128]{1,0:T(8,128)S(1)} fusion(bf16[1024,128]{1,0:T(8,128)(2,1)S(1)} %collective-permute-done.37, bf16[320,16384]{1,0:T(8,128)(2,1)} %copy-done, s32[]{:T(128)S(6)} %select_n.177), kind=kOutput, calls=%fused_computation.65 | convolution fusion | flops 83886080 | bytes 1081348 | tf_op jit(solution)/shard_map/dot_general | solution.py:69
  85.3 1.4 fusion.50
  86.9 1.4 convolution_add_fusion.7
  88.3 1.7 %collective-permute-start.33 = (bf16[1024,128]{1,0:T(8,128)(2,1)S(1)}, bf16[1024,128]{1,0:T(8,128)(2,1)S(1)}, u32[]{:S(2)}, u32[]{:S(2)}) collective-permute-start(bf16[1024,128]{1,0:T(8,128)(2,1)S(1)} %collective-permute-done.31), channel_id=1, source_target_pairs={{0,16},{4,20},{8,24},{12,28},{16,0},{20,4},{24,8},{28,12},{1,17},{... | collective-permute-start | bytes 786440 | tf_op jit(solution)/shard_map/ppermute | solution.py:15
  90.0 7.1 %collective-permute-done.16 = bf16[1024,128]{1,0:T(8,128)(2,1)S(1)} collective-permute-done((bf16[1024,128]{1,0:T(8,128)(2,1)S(1)}, bf16[1024,128]{1,0:T(8,128)(2,1)S(1)}, u32[]{:S(2)}, u32[]{:S(2)}) %collective-permute-start.16) | collective-permute-done | bytes 262176 | tf_op jit(solution)/shard_map/ppermute | solution.py:15
  97.1 1.5 %collective-permute-start.19 = (bf16[1024,128]{1,0:T(8,128)(2,1)S(1)}, bf16[1024,128]{1,0:T(8,128)(2,1)S(1)}, u32[]{:S(2)}, u32[]{:S(2)}) collective-permute-start(bf16[1024,128]{1,0:T(8,128)(2,1)S(1)} %collective-permute-done.17), channel_id=1, source_target_pairs={{0,8},{4,12},{8,0},{12,4},{16,24},{20,28},{24,16},{28,20},{1,9},{5... | collective-permute-start | bytes 786440 | tf_op jit(solution)/shard_map/ppermute | solution.py:15
  98.6 1.4 fusion.7
  100.0 1.4 %fusion.8 = f32[320,128]{1,0:T(8,128)S(1)} fusion(f32[320,128]{1,0:T(8,128)S(1)} %fusion.52, f32[320,128]{1,0:T(8,128)S(1)} %fusion.7, bf16[1024,128]{1,0:T(8,128)(2,1)S(1)} %collective-permute-done.17, bf16[320,16384]{1,0:T(8,128)(2,1)} %copy-done, s32[]{:T(128)S(6)} %select_n.174), kind=kOutput, calls=%fused_computation.29 | convolution fusion | flops 83968000 | bytes 1409028 | tf_op jit(solution)/shard_map/dot_general | solution.py:69
  102.0 1.5 %collective-permute-start.36 = (bf16[1024,128]{1,0:T(8,128)(2,1)S(1)}, bf16[1024,128]{1,0:T(8,128)(2,1)S(1)}, u32[]{:S(2)}, u32[]{:S(2)}) collective-permute-start(bf16[1024,128]{1,0:T(8,128)(2,1)S(1)} %collective-permute-done.34), channel_id=1, source_target_pairs={{0,8},{4,12},{8,0},{12,4},{16,24},{20,28},{24,16},{28,20},{1,9},{5... | collective-permute-start | bytes 786440 | tf_op jit(solution)/shard_map/ppermute | solution.py:15
  103.5 1.4 fusion.13
  105.8 4.5 %collective-permute-done.36 = bf16[1024,128]{1,0:T(8,128)(2,1)S(1)} collective-permute-done((bf16[1024,128]{1,0:T(8,128)(2,1)S(1)}, bf16[1024,128]{1,0:T(8,128)(2,1)S(1)}, u32[]{:S(2)}, u32[]{:S(2)}) %collective-permute-start.36) | collective-permute-done | bytes 262176 | tf_op jit(solution)/shard_map/ppermute | solution.py:15
  116.5 0.9 fusion.79
  117.8 0.9 collective-permute-start.29
  118.7 0.6 collective-permute-start.30
  119.3 0.7 collective-permute-start.28
  120.7 0.7 collective-permute-done.29
  121.9 1.5 %fusion.22 = f32[8,128]{1,0:T(8,128)S(1)} fusion(f32[320,128]{1,0:T(8,128)S(1)} %fusion.18, bf16[1024,128]{1,0:T(8,128)(2,1)S(1)} %collective-permute-done.44, bf16[320,16384]{1,0:T(8,128)(2,1)} %copy-done, s32[]{:T(128)S(6)} %select_n.184, f32[128]{0:T(128)S(1)} %fusion.129, f32[8]{0:T(128)S(1)} %get-tuple-element.6, f32[8,320]{1,0:T(8,128)S(1)} %get-tuple-element.23, ...), kind=kOutput, calls=%fused_computation.44 | convolution fusion | flops 84633088 | bytes 1096580 | tf_op jit(solution)/shard_map/dot_general | solution.py:144
  123.5 1.2 collective-permute-start.46
  124.7 0.9 collective-permute-start.45
  125.7 1.1 collective-permute-start.50
  126.8 1.2 collective-permute-start.51
  128.5 1.6 %collective-permute-start.49 = (f32[8,256]{1,0:T(8,128)S(1)}, f32[8,256]{1,0:T(8,128)S(1)}, u32[]{:S(2)}, u32[]{:S(2)}) collective-permute-start(f32[8,256]{1,0:T(8,128)S(1)} %pad_maximum_fusion.2), channel_id=1, source_target_pairs={{0,20},{4,16},{8,28},{12,24},{16,4},{20,0},{24,12},{28,8},{1,21},{... | collective-permute-start | bytes 24584 | tf_op jit(solution)/shard_map/ppermute | solution.py:15
  130.2 0.6 collective-permute-done.51
  130.8 0.8 collective-permute-done.48
  132.3 2.8 %fusion.3 = f32[2,2048]{1,0:T(2,128)S(1)} fusion(bf16[1,1024,2048]{2,1,0:T(8,128)(2,1)} %param.15, bf16[1,2,8,128]{3,2,1,0:T(8,128)(2,1)S(1)} %fusion.123), kind=kOutput, calls=%fused_computation.6 | convolution fusion | flops 8388608 | bytes 4214784 | tf_op jit(solution)/shard_map/dot_general | solution.py:154
  135.1 2.6 %collective-permute-start.53 = (f32[2,2048]{1,0:T(2,128)S(1)}, f32[2,2048]{1,0:T(2,128)S(1)}, u32[]{:S(2)}, u32[]{:S(2)}) collective-permute-start(f32[2,2048]{1,0:T(2,128)S(1)} %fusion.3), channel_id=1, source_target_pairs={{0,2},{1,3},{2,0},{3,1},{4,6},{5,7},{6,4},{7,5},{8,10},{9,11},{10,... | collective-permute-start | bytes 49160 | tf_op jit(solution)/shard_map/ppermute | solution.py:15
  137.7 1.3 collective-permute-start.54
  139.7 3.5 %collective-permute-done.54 = f32[2,2048]{1,0:T(2,128)S(1)} collective-permute-done((f32[2,2048]{1,0:T(2,128)S(1)}, f32[2,2048]{1,0:T(2,128)S(1)}, u32[]{:S(2)}, u32[]{:S(2)}) %collective-permute-start.54) | collective-permute-done | bytes 16416 | tf_op jit(solution)/shard_map/ppermute | solution.py:15
  143.2 0.6 add_add_fusion
  (143 shorter events, 16.9 us)
Async XLA Ops:
  0.0 16.3 %copy-start.5 = (f32[1,16384]{1,0:T(1,128)S(1)}, f32[1,16384]{1,0:T(1,128)}, u32[]{:S(2)}) copy-start(f32[1,16384]{1,0:T(1,128)} %param.11) | copy-start | bytes 196612
  0.9 34.7 %collective-permute-start.5 = (f32[2]{0:T(128)S(1)}, f32[2]{0:T(128)S(1)}, u32[]{:S(2)}, u32[]{:S(2)}) collective-permute-start(f32[2]{0:T(128)S(1)} %multiply_reduce_fusion), channel_id=1, source_target_pairs={{0,24},{4,28},{8,16},{12,20},{16,8},{20,12},{24,0},{28,4},{1,25},{... | collective-permute-start | bytes 32 | tf_op jit(solution)/shard_map/ppermute | solution.py:15
  4.8 30.9 %collective-permute-start.6 = (f32[2]{0:T(128)S(1)}, f32[2]{0:T(128)S(1)}, u32[]{:S(2)}, u32[]{:S(2)}) collective-permute-start(f32[2]{0:T(128)S(1)} %multiply_reduce_fusion), channel_id=1, source_target_pairs={{0,28},{4,24},{8,20},{12,16},{16,12},{20,8},{24,4},{28,0},{1,29},{... | collective-permute-start | bytes 32 | tf_op jit(solution)/shard_map/ppermute | solution.py:15
  4.8 31.3 %collective-permute-start.3 = (f32[2]{0:T(128)S(1)}, f32[2]{0:T(128)S(1)}, u32[]{:S(2)}, u32[]{:S(2)}) collective-permute-start(f32[2]{0:T(128)S(1)} %multiply_reduce_fusion), channel_id=1, source_target_pairs={{0,16},{4,20},{8,24},{12,28},{16,0},{20,4},{24,8},{28,12},{1,17},{... | collective-permute-start | bytes 32 | tf_op jit(solution)/shard_map/ppermute | solution.py:15
  6.0 30.2 %collective-permute-start.4 = (f32[2]{0:T(128)S(1)}, f32[2]{0:T(128)S(1)}, u32[]{:S(2)}, u32[]{:S(2)}) collective-permute-start(f32[2]{0:T(128)S(1)} %multiply_reduce_fusion), channel_id=1, source_target_pairs={{0,20},{4,16},{8,28},{12,24},{16,4},{20,0},{24,12},{28,8},{1,21},{... | collective-permute-start | bytes 32 | tf_op jit(solution)/shard_map/ppermute | solution.py:15
  6.6 29.6 %collective-permute-start.1 = (f32[2]{0:T(128)S(1)}, f32[2]{0:T(128)S(1)}, u32[]{:S(2)}, u32[]{:S(2)}) collective-permute-start(f32[2]{0:T(128)S(1)} %multiply_reduce_fusion), channel_id=1, source_target_pairs={{0,8},{4,12},{8,0},{12,4},{16,24},{20,28},{24,16},{28,20},{1,9},{5... | collective-permute-start | bytes 32 | tf_op jit(solution)/shard_map/ppermute | solution.py:15
  16.3 13.4 %copy-start.1 = (bf16[1,2048,128]{2,1,0:T(8,128)(2,1)S(1)}, bf16[1,2048,128]{2,1,0:T(8,128)(2,1)}, u32[]{:S(2)}) copy-start(bf16[1,2048,128]{2,1,0:T(8,128)(2,1)} %param.14) | copy-start | bytes 1572868
  16.4 17.9 %copy-start.6 = (s32[2]{0:T(128)S(1)}, s32[2]{0:T(128)}, u32[]{:S(2)}) copy-start(s32[2]{0:T(128)} %param.17) | copy-start | bytes 28
  16.4 22.3 %copy-start.4 = (f32[2,2048]{1,0:T(2,128)S(1)}, f32[2,2048]{1,0:T(2,128)}, u32[]{:S(2)}) copy-start(f32[2,2048]{1,0:T(2,128)} %param.9) | copy-start | bytes 49156
  27.3 16.5 %copy-start.7 = (s32[2]{0:T(128)S(1)}, s32[2]{0:T(128)}, u32[]{:S(2)}) copy-start(s32[2]{0:T(128)} %param.16) | copy-start | bytes 28
  32.0 72.9 %slice-start = ((s8[10485760]{0:T(1024)(128)(4,1)}), s8[2097152]{0:T(1024)(128)(4,1)S(1)}, s32[]{:S(2)}) async-start(s8[10485760]{0:T(1024)(128)(4,1)} %bitcast.101), calls=%async_computation | async-start | bytes 4194304
  35.6 3.0 %collective-permute-start.2 = (f32[2]{0:T(128)S(1)}, f32[2]{0:T(128)S(1)}, u32[]{:S(2)}, u32[]{:S(2)}) collective-permute-start(f32[2]{0:T(128)S(1)} %multiply_reduce_fusion), channel_id=1, source_target_pairs={{0,12},{4,8},{8,4},{12,0},{16,28},{20,24},{24,20},{28,16},{1,13},{... | collective-permute-start | bytes 32 | tf_op jit(solution)/shard_map/ppermute | solution.py:15
  35.8 2.9 %collective-permute-start = (f32[2]{0:T(128)S(1)}, f32[2]{0:T(128)S(1)}, u32[]{:S(2)}, u32[]{:S(2)}) collective-permute-start(f32[2]{0:T(128)S(1)} %multiply_reduce_fusion), channel_id=1, source_target_pairs={{0,4},{4,0},{8,12},{12,8},{16,20},{20,16},{24,28},{28,24},{1,5},{5... | collective-permute-start | bytes 32 | tf_op jit(solution)/shard_map/ppermute | solution.py:15
  39.1 39.2 %copy-start.3 = (bf16[1024,128]{1,0:T(8,128)(2,1)S(1)}, bf16[1024,128]{1,0:T(8,128)(2,1)}, u32[]{:S(2)}) copy-start(bf16[1024,128]{1,0:T(8,128)(2,1)} %get-tuple-element.7) | copy-start | bytes 786436
  42.1 5.1 %collective-permute-start.7 = (f32[10,128]{1,0:T(8,128)S(1)}, f32[10,128]{1,0:T(8,128)S(1)}, u32[]{:S(2)}, u32[]{:S(2)}) collective-permute-start(f32[10,128]{1,0:T(8,128)S(1)} %get-tuple-element.19), channel_id=1, source_target_pairs={{0,4},{4,0},{8,12},{12,8},{16,20},{20,16},{24,28},{28,24},{1,5},{5... | collective-permute-start | bytes 15368 | tf_op jit(solution)/shard_map/ppermute | solution.py:15
  42.2 5.5 %collective-permute-start.12 = (f32[10,128]{1,0:T(8,128)S(1)}, f32[10,128]{1,0:T(8,128)S(1)}, u32[]{:S(2)}, u32[]{:S(2)}) collective-permute-start(f32[10,128]{1,0:T(8,128)S(1)} %get-tuple-element.15), channel_id=1, source_target_pairs={{0,24},{4,28},{8,16},{12,20},{16,8},{20,12},{24,0},{28,4},{1,25},{... | collective-permute-start | bytes 15368 | tf_op jit(solution)/shard_map/ppermute | solution.py:15
  44.4 5.5 %collective-permute-start.13 = (f32[10,128]{1,0:T(8,128)S(1)}, f32[10,128]{1,0:T(8,128)S(1)}, u32[]{:S(2)}, u32[]{:S(2)}) collective-permute-start(f32[10,128]{1,0:T(8,128)S(1)} %get-tuple-element.14), channel_id=1, source_target_pairs={{0,28},{4,24},{8,20},{12,16},{16,12},{20,8},{24,4},{28,0},{1,29},{... | collective-permute-start | bytes 15368 | tf_op jit(solution)/shard_map/ppermute | solution.py:15
  45.6 4.7 %collective-permute-start.10 = (f32[10,128]{1,0:T(8,128)S(1)}, f32[10,128]{1,0:T(8,128)S(1)}, u32[]{:S(2)}, u32[]{:S(2)}) collective-permute-start(f32[10,128]{1,0:T(8,128)S(1)} %get-tuple-element.17), channel_id=1, source_target_pairs={{0,16},{4,20},{8,24},{12,28},{16,0},{20,4},{24,8},{28,12},{1,17},{... | collective-permute-start | bytes 15368 | tf_op jit(solution)/shard_map/ppermute | solution.py:15
  47.1 3.3 %collective-permute-start.11 = (f32[10,128]{1,0:T(8,128)S(1)}, f32[10,128]{1,0:T(8,128)S(1)}, u32[]{:S(2)}, u32[]{:S(2)}) collective-permute-start(f32[10,128]{1,0:T(8,128)S(1)} %get-tuple-element.16), channel_id=1, source_target_pairs={{0,20},{4,16},{8,28},{12,24},{16,4},{20,0},{24,12},{28,8},{1,21},{... | collective-permute-start | bytes 15368 | tf_op jit(solution)/shard_map/ppermute | solution.py:15
  47.3 4.8 %collective-permute-start.8 = (f32[10,128]{1,0:T(8,128)S(1)}, f32[10,128]{1,0:T(8,128)S(1)}, u32[]{:S(2)}, u32[]{:S(2)}) collective-permute-start(f32[10,128]{1,0:T(8,128)S(1)} %get-tuple-element.18), channel_id=1, source_target_pairs={{0,8},{4,12},{8,0},{12,4},{16,24},{20,28},{24,16},{28,20},{1,9},{5... | collective-permute-start | bytes 15368 | tf_op jit(solution)/shard_map/ppermute | solution.py:15
  47.7 5.9 %collective-permute-start.9 = (f32[10,128]{1,0:T(8,128)S(1)}, f32[10,128]{1,0:T(8,128)S(1)}, u32[]{:S(2)}, u32[]{:S(2)}) collective-permute-start(f32[10,128]{1,0:T(8,128)S(1)} %get-tuple-element.13), channel_id=1, source_target_pairs={{0,12},{4,8},{8,4},{12,0},{16,28},{20,24},{24,20},{28,16},{1,13},{... | collective-permute-start | bytes 15368 | tf_op jit(solution)/shard_map/ppermute | solution.py:15
  49.8 30.0 %collective-permute-start.18 = (bf16[1024,128]{1,0:T(8,128)(2,1)}, bf16[1024,128]{1,0:T(8,128)(2,1)S(1)}, u32[]{:S(2)}, u32[]{:S(2)}) collective-permute-start(bf16[1024,128]{1,0:T(8,128)(2,1)} %get-tuple-element.10), channel_id=1, source_target_pairs={{0,8},{4,12},{8,0},{12,4},{16,24},{20,28},{24,16},{28,20},{1,9},{5... | collective-permute-start | bytes 786440 | tf_op jit(solution)/shard_map/ppermute | solution.py:15
  50.3 24.1 %collective-permute-start.24 = (bf16[1024,128]{1,0:T(8,128)(2,1)}, bf16[1024,128]{1,0:T(8,128)(2,1)S(1)}, u32[]{:S(2)}, u32[]{:S(2)}) collective-permute-start(bf16[1024,128]{1,0:T(8,128)(2,1)} %get-tuple-element.10), channel_id=1, source_target_pairs={{0,4},{4,0},{8,12},{12,8},{16,20},{20,16},{24,28},{28,24},{1,5},{5... | collective-permute-start | bytes 786440 | tf_op jit(solution)/shard_map/ppermute | solution.py:15
  50.4 22.5 %collective-permute-start.15 = (bf16[1024,128]{1,0:T(8,128)(2,1)}, bf16[1024,128]{1,0:T(8,128)(2,1)S(1)}, u32[]{:S(2)}, u32[]{:S(2)}) collective-permute-start(bf16[1024,128]{1,0:T(8,128)(2,1)} %get-tuple-element.9), channel_id=1, source_target_pairs={{0,16},{4,20},{8,24},{12,28},{16,0},{20,4},{24,8},{28,12},{1,17},{... | collective-permute-start | bytes 786440 | tf_op jit(solution)/shard_map/ppermute | solution.py:15
  52.0 12.8 %collective-permute-start.14 = (bf16[1024,128]{1,0:T(8,128)(2,1)}, bf16[1024,128]{1,0:T(8,128)(2,1)S(1)}, u32[]{:S(2)}, u32[]{:S(2)}) collective-permute-start(bf16[1024,128]{1,0:T(8,128)(2,1)} %get-tuple-element.9), channel_id=1, source_target_pairs={{0,8},{4,12},{8,0},{12,4},{16,24},{20,28},{24,16},{28,20},{1,9},{5... | collective-permute-start | bytes 786440 | tf_op jit(solution)/shard_map/ppermute | solution.py:15
  53.5 16.4 %collective-permute-start.31 = (bf16[1024,128]{1,0:T(8,128)(2,1)}, bf16[1024,128]{1,0:T(8,128)(2,1)S(1)}, u32[]{:S(2)}, u32[]{:S(2)}) collective-permute-start(bf16[1024,128]{1,0:T(8,128)(2,1)} %get-tuple-element.7), channel_id=1, source_target_pairs={{0,8},{4,12},{8,0},{12,4},{16,24},{20,28},{24,16},{28,20},{1,9},{5... | collective-permute-start | bytes 786440 | tf_op jit(solution)/shard_map/ppermute | solution.py:15
  54.4 50.5 %slice-start.1 = ((s8[10485760]{0:T(1024)(128)(4,1)}), s8[4194304]{0:T(1024)(128)(4,1)S(1)}, s32[]{:S(2)}) async-start(s8[10485760]{0:T(1024)(128)(4,1)} %bitcast.101), calls=%async_computation.1 | async-start | bytes 8388608
  64.8 13.5 %collective-permute-start.20 = (bf16[1024,128]{1,0:T(8,128)(2,1)}, bf16[1024,128]{1,0:T(8,128)(2,1)S(1)}, u32[]{:S(2)}, u32[]{:S(2)}) collective-permute-start(bf16[1024,128]{1,0:T(8,128)(2,1)} %get-tuple-element.9), channel_id=1, source_target_pairs={{0,4},{4,0},{8,12},{12,8},{16,20},{20,16},{24,28},{28,24},{1,5},{5... | collective-permute-start | bytes 786440 | tf_op jit(solution)/shard_map/ppermute | solution.py:15
  69.9 18.4 %collective-permute-start.17 = (bf16[1024,128]{1,0:T(8,128)(2,1)}, bf16[1024,128]{1,0:T(8,128)(2,1)S(1)}, u32[]{:S(2)}, u32[]{:S(2)}) collective-permute-start(bf16[1024,128]{1,0:T(8,128)(2,1)} %get-tuple-element.10), channel_id=1, source_target_pairs={{0,16},{4,20},{8,24},{12,28},{16,0},{20,4},{24,8},{28,12},{1,17},{... | collective-permute-start | bytes 786440 | tf_op jit(solution)/shard_map/ppermute | solution.py:15
  72.9 3.6 %collective-permute-start.41 = (bf16[1024,128]{1,0:T(8,128)(2,1)}, bf16[1024,128]{1,0:T(8,128)(2,1)S(1)}, u32[]{:S(2)}, u32[]{:S(2)}) collective-permute-start(bf16[1024,128]{1,0:T(8,128)(2,1)} %get-tuple-element.8), channel_id=1, source_target_pairs={{0,4},{4,0},{8,12},{12,8},{16,20},{20,16},{24,28},{28,24},{1,5},{5... | collective-permute-start | bytes 786440 | tf_op jit(solution)/shard_map/ppermute | solution.py:15
  74.4 10.5 %collective-permute-start.35 = (bf16[1024,128]{1,0:T(8,128)(2,1)}, bf16[1024,128]{1,0:T(8,128)(2,1)S(1)}, u32[]{:S(2)}, u32[]{:S(2)}) collective-permute-start(bf16[1024,128]{1,0:T(8,128)(2,1)} %get-tuple-element.8), channel_id=1, source_target_pairs={{0,8},{4,12},{8,0},{12,4},{16,24},{20,28},{24,16},{28,20},{1,9},{5... | collective-permute-start | bytes 786440 | tf_op jit(solution)/shard_map/ppermute | solution.py:15
  76.4 10.3 %collective-permute-start.32 = (bf16[1024,128]{1,0:T(8,128)(2,1)}, bf16[1024,128]{1,0:T(8,128)(2,1)S(1)}, u32[]{:S(2)}, u32[]{:S(2)}) collective-permute-start(bf16[1024,128]{1,0:T(8,128)(2,1)} %get-tuple-element.7), channel_id=1, source_target_pairs={{0,16},{4,20},{8,24},{12,28},{16,0},{20,4},{24,8},{28,12},{1,17},{... | collective-permute-start | bytes 786440 | tf_op jit(solution)/shard_map/ppermute | solution.py:15
  78.3 4.7 %collective-permute-start.37 = (bf16[1024,128]{1,0:T(8,128)(2,1)S(1)}, bf16[1024,128]{1,0:T(8,128)(2,1)S(1)}, u32[]{:S(2)}, u32[]{:S(2)}) collective-permute-start(bf16[1024,128]{1,0:T(8,128)(2,1)S(1)} %copy-done.3), channel_id=1, source_target_pairs={{0,4},{4,0},{8,12},{12,8},{16,20},{20,16},{24,28},{28,24},{1,5},{5... | collective-permute-start | bytes 786440 | tf_op jit(solution)/shard_map/ppermute | solution.py:15
  79.9 21.6 %collective-permute-start.34 = (bf16[1024,128]{1,0:T(8,128)(2,1)}, bf16[1024,128]{1,0:T(8,128)(2,1)S(1)}, u32[]{:S(2)}, u32[]{:S(2)}) collective-permute-start(bf16[1024,128]{1,0:T(8,128)(2,1)} %get-tuple-element.8), channel_id=1, source_target_pairs={{0,16},{4,20},{8,24},{12,28},{16,0},{20,4},{24,8},{28,12},{1,17},{... | collective-permute-start | bytes 786440 | tf_op jit(solution)/shard_map/ppermute | solution.py:15
  83.0 22.0 %slice-start.2 = ((s8[10485760]{0:T(1024)(128)(4,1)}), s8[4194304]{0:T(1024)(128)(4,1)S(1)}, s32[]{:S(2)}) async-start(s8[10485760]{0:T(1024)(128)(4,1)} %bitcast.101), calls=%async_computation.2 | async-start | bytes 8388608
  83.0 30.6 %collective-permute-start.26 = (bf16[1024,128]{1,0:T(8,128)(2,1)S(1)}, bf16[1024,128]{1,0:T(8,128)(2,1)S(1)}, u32[]{:S(2)}, u32[]{:S(2)}) collective-permute-start(bf16[1024,128]{1,0:T(8,128)(2,1)S(1)} %collective-permute-done.18), channel_id=1, source_target_pairs={{0,4},{4,0},{8,12},{12,8},{16,20},{20,16},{24,28},{28,24},{1,5},{5... | collective-permute-start | bytes 786440 | tf_op jit(solution)/shard_map/ppermute | solution.py:15
  84.9 12.2 %collective-permute-start.16 = (bf16[1024,128]{1,0:T(8,128)(2,1)S(1)}, bf16[1024,128]{1,0:T(8,128)(2,1)S(1)}, u32[]{:S(2)}, u32[]{:S(2)}) collective-permute-start(bf16[1024,128]{1,0:T(8,128)(2,1)S(1)} %collective-permute-done.14), channel_id=1, source_target_pairs={{0,16},{4,20},{8,24},{12,28},{16,0},{20,4},{24,8},{28,12},{1,17},{... | collective-permute-start | bytes 786440 | tf_op jit(solution)/shard_map/ppermute | solution.py:15
  86.8 23.9 %collective-permute-start.22 = (bf16[1024,128]{1,0:T(8,128)(2,1)S(1)}, bf16[1024,128]{1,0:T(8,128)(2,1)S(1)}, u32[]{:S(2)}, u32[]{:S(2)}) collective-permute-start(bf16[1024,128]{1,0:T(8,128)(2,1)S(1)} %collective-permute-done.15), channel_id=1, source_target_pairs={{0,4},{4,0},{8,12},{12,8},{16,20},{20,16},{24,28},{28,24},{1,5},{5... | collective-permute-start | bytes 786440 | tf_op jit(solution)/shard_map/ppermute | solution.py:15
  88.3 13.7 %collective-permute-start.33 = (bf16[1024,128]{1,0:T(8,128)(2,1)S(1)}, bf16[1024,128]{1,0:T(8,128)(2,1)S(1)}, u32[]{:S(2)}, u32[]{:S(2)}) collective-permute-start(bf16[1024,128]{1,0:T(8,128)(2,1)S(1)} %collective-permute-done.31), channel_id=1, source_target_pairs={{0,16},{4,20},{8,24},{12,28},{16,0},{20,4},{24,8},{28,12},{1,17},{... | collective-permute-start | bytes 786440 | tf_op jit(solution)/shard_map/ppermute | solution.py:15
  97.1 8.2 %collective-permute-start.19 = (bf16[1024,128]{1,0:T(8,128)(2,1)S(1)}, bf16[1024,128]{1,0:T(8,128)(2,1)S(1)}, u32[]{:S(2)}, u32[]{:S(2)}) collective-permute-start(bf16[1024,128]{1,0:T(8,128)(2,1)S(1)} %collective-permute-done.17), channel_id=1, source_target_pairs={{0,8},{4,12},{8,0},{12,4},{16,24},{20,28},{24,16},{28,20},{1,9},{5... | collective-permute-start | bytes 786440 | tf_op jit(solution)/shard_map/ppermute | solution.py:15
  101.5 10.1 %collective-permute-start.21 = (bf16[1024,128]{1,0:T(8,128)(2,1)S(1)}, bf16[1024,128]{1,0:T(8,128)(2,1)S(1)}, u32[]{:S(2)}, u32[]{:S(2)}) collective-permute-start(bf16[1024,128]{1,0:T(8,128)(2,1)S(1)} %collective-permute-done.14), channel_id=1, source_target_pairs={{0,4},{4,0},{8,12},{12,8},{16,20},{20,16},{24,28},{28,24},{1,5},{5... | collective-permute-start | bytes 786440 | tf_op jit(solution)/shard_map/ppermute | solution.py:15
  102.0 8.3 %collective-permute-start.36 = (bf16[1024,128]{1,0:T(8,128)(2,1)S(1)}, bf16[1024,128]{1,0:T(8,128)(2,1)S(1)}, u32[]{:S(2)}, u32[]{:S(2)}) collective-permute-start(bf16[1024,128]{1,0:T(8,128)(2,1)S(1)} %collective-permute-done.34), channel_id=1, source_target_pairs={{0,8},{4,12},{8,0},{12,4},{16,24},{20,28},{24,16},{28,20},{1,9},{5... | collective-permute-start | bytes 786440 | tf_op jit(solution)/shard_map/ppermute | solution.py:15
  105.3 10.5 %collective-permute-start.25 = (bf16[1024,128]{1,0:T(8,128)(2,1)S(1)}, bf16[1024,128]{1,0:T(8,128)(2,1)S(1)}, u32[]{:S(2)}, u32[]{:S(2)}) collective-permute-start(bf16[1024,128]{1,0:T(8,128)(2,1)S(1)} %collective-permute-done.17), channel_id=1, source_target_pairs={{0,4},{4,0},{8,12},{12,8},{16,20},{20,16},{24,28},{28,24},{1,5},{5... | collective-permute-start | bytes 786440 | tf_op jit(solution)/shard_map/ppermute | solution.py:15
  110.3 4.2 %collective-permute-start.43 = (bf16[1024,128]{1,0:T(8,128)(2,1)S(1)}, bf16[1024,128]{1,0:T(8,128)(2,1)S(1)}, u32[]{:S(2)}, u32[]{:S(2)}) collective-permute-start(bf16[1024,128]{1,0:T(8,128)(2,1)S(1)} %collective-permute-done.35), channel_id=1, source_target_pairs={{0,4},{4,0},{8,12},{12,8},{16,20},{20,16},{24,28},{28,24},{1,5},{5... | collective-permute-start | bytes 786440 | tf_op jit(solution)/shard_map/ppermute | solution.py:15
  110.6 1.7 %collective-permute-start.39 = (bf16[1024,128]{1,0:T(8,128)(2,1)S(1)}, bf16[1024,128]{1,0:T(8,128)(2,1)S(1)}, u32[]{:S(2)}, u32[]{:S(2)}) collective-permute-start(bf16[1024,128]{1,0:T(8,128)(2,1)S(1)} %collective-permute-done.32), channel_id=1, source_target_pairs={{0,4},{4,0},{8,12},{12,8},{16,20},{20,16},{24,28},{28,24},{1,5},{5... | collective-permute-start | bytes 786440 | tf_op jit(solution)/shard_map/ppermute | solution.py:15
  111.6 1.6 %collective-permute-start.38 = (bf16[1024,128]{1,0:T(8,128)(2,1)S(1)}, bf16[1024,128]{1,0:T(8,128)(2,1)S(1)}, u32[]{:S(2)}, u32[]{:S(2)}) collective-permute-start(bf16[1024,128]{1,0:T(8,128)(2,1)S(1)} %collective-permute-done.31), channel_id=1, source_target_pairs={{0,4},{4,0},{8,12},{12,8},{16,20},{20,16},{24,28},{28,24},{1,5},{5... | collective-permute-start | bytes 786440 | tf_op jit(solution)/shard_map/ppermute | solution.py:15
  112.4 8.0 %collective-permute-start.42 = (bf16[1024,128]{1,0:T(8,128)(2,1)S(1)}, bf16[1024,128]{1,0:T(8,128)(2,1)S(1)}, u32[]{:S(2)}, u32[]{:S(2)}) collective-permute-start(bf16[1024,128]{1,0:T(8,128)(2,1)S(1)} %collective-permute-done.34), channel_id=1, source_target_pairs={{0,4},{4,0},{8,12},{12,8},{16,20},{20,16},{24,28},{28,24},{1,5},{5... | collective-permute-start | bytes 786440 | tf_op jit(solution)/shard_map/ppermute | solution.py:15
  113.2 1.8 %collective-permute-start.23 = (bf16[1024,128]{1,0:T(8,128)(2,1)S(1)}, bf16[1024,128]{1,0:T(8,128)(2,1)S(1)}, u32[]{:S(2)}, u32[]{:S(2)}) collective-permute-start(bf16[1024,128]{1,0:T(8,128)(2,1)S(1)} %collective-permute-done.16), channel_id=1, source_target_pairs={{0,4},{4,0},{8,12},{12,8},{16,20},{20,16},{24,28},{28,24},{1,5},{5... | collective-permute-start | bytes 786440 | tf_op jit(solution)/shard_map/ppermute | solution.py:15
  113.6 2.5 %collective-permute-start.27 = (bf16[1024,128]{1,0:T(8,128)(2,1)S(1)}, bf16[1024,128]{1,0:T(8,128)(2,1)S(1)}, u32[]{:S(2)}, u32[]{:S(2)}) collective-permute-start(bf16[1024,128]{1,0:T(8,128)(2,1)S(1)} %collective-permute-done.19), channel_id=1, source_target_pairs={{0,4},{4,0},{8,12},{12,8},{16,20},{20,16},{24,28},{28,24},{1,5},{5... | collective-permute-start | bytes 786440 | tf_op jit(solution)/shard_map/ppermute | solution.py:15
  114.4 4.9 %collective-permute-start.40 = (bf16[1024,128]{1,0:T(8,128)(2,1)S(1)}, bf16[1024,128]{1,0:T(8,128)(2,1)S(1)}, u32[]{:S(2)}, u32[]{:S(2)}) collective-permute-start(bf16[1024,128]{1,0:T(8,128)(2,1)S(1)} %collective-permute-done.33), channel_id=1, source_target_pairs={{0,4},{4,0},{8,12},{12,8},{16,20},{20,16},{24,28},{28,24},{1,5},{5... | collective-permute-start | bytes 786440 | tf_op jit(solution)/shard_map/ppermute | solution.py:15
  115.0 6.9 %collective-permute-start.44 = (bf16[1024,128]{1,0:T(8,128)(2,1)S(1)}, bf16[1024,128]{1,0:T(8,128)(2,1)S(1)}, u32[]{:S(2)}, u32[]{:S(2)}) collective-permute-start(bf16[1024,128]{1,0:T(8,128)(2,1)S(1)} %collective-permute-done.36), channel_id=1, source_target_pairs={{0,4},{4,0},{8,12},{12,8},{16,20},{20,16},{24,28},{28,24},{1,5},{5... | collective-permute-start | bytes 786440 | tf_op jit(solution)/shard_map/ppermute | solution.py:15
  117.8 3.6 %collective-permute-start.29 = (f32[8]{0:T(128)S(1)}, f32[8]{0:T(128)S(1)}, u32[]{:S(2)}, u32[]{:S(2)}) collective-permute-start(f32[8]{0:T(128)S(1)} %multiply_maximum_fusion), channel_id=1, source_target_pairs={{0,8},{4,12},{8,0},{12,4},{16,24},{20,28},{24,16},{28,20},{1,9},{5... | collective-permute-start | bytes 104 | tf_op jit(solution)/shard_map/ppermute | solution.py:15
  118.7 3.0 %collective-permute-start.30 = (f32[8]{0:T(128)S(1)}, f32[8]{0:T(128)S(1)}, u32[]{:S(2)}, u32[]{:S(2)}) collective-permute-start(f32[8]{0:T(128)S(1)} %multiply_maximum_fusion), channel_id=1, source_target_pairs={{0,12},{4,8},{8,4},{12,0},{16,28},{20,24},{24,20},{28,16},{1,13},{... | collective-permute-start | bytes 104 | tf_op jit(solution)/shard_map/ppermute | solution.py:15
  119.3 2.3 %collective-permute-start.28 = (f32[8]{0:T(128)S(1)}, f32[8]{0:T(128)S(1)}, u32[]{:S(2)}, u32[]{:S(2)}) collective-permute-start(f32[8]{0:T(128)S(1)} %multiply_maximum_fusion), channel_id=1, source_target_pairs={{0,4},{4,0},{8,12},{12,8},{16,20},{20,16},{24,28},{28,24},{1,5},{5... | collective-permute-start | bytes 104 | tf_op jit(solution)/shard_map/ppermute | solution.py:15
  123.5 4.5 %collective-permute-start.46 = (f32[8,256]{1,0:T(8,128)S(1)}, f32[8,256]{1,0:T(8,128)S(1)}, u32[]{:S(2)}, u32[]{:S(2)}) collective-permute-start(f32[8,256]{1,0:T(8,128)S(1)} %pad_maximum_fusion.2), channel_id=1, source_target_pairs={{0,8},{4,12},{8,0},{12,4},{16,24},{20,28},{24,16},{28,20},{1,9},{5... | collective-permute-start | bytes 24584 | tf_op jit(solution)/shard_map/ppermute | solution.py:15
  124.7 3.8 %collective-permute-start.47 = (f32[8,256]{1,0:T(8,128)S(1)}, f32[8,256]{1,0:T(8,128)S(1)}, u32[]{:S(2)}, u32[]{:S(2)}) collective-permute-start(f32[8,256]{1,0:T(8,128)S(1)} %pad_maximum_fusion.2), channel_id=1, source_target_pairs={{0,12},{4,8},{8,4},{12,0},{16,28},{20,24},{24,20},{28,16},{1,13},{... | collective-permute-start | bytes 24584 | tf_op jit(solution)/shard_map/ppermute | solution.py:15
  124.7 5.3 %collective-permute-start.45 = (f32[8,256]{1,0:T(8,128)S(1)}, f32[8,256]{1,0:T(8,128)S(1)}, u32[]{:S(2)}, u32[]{:S(2)}) collective-permute-start(f32[8,256]{1,0:T(8,128)S(1)} %pad_maximum_fusion.2), channel_id=1, source_target_pairs={{0,4},{4,0},{8,12},{12,8},{16,20},{20,16},{24,28},{28,24},{1,5},{5... | collective-permute-start | bytes 24584 | tf_op jit(solution)/shard_map/ppermute | solution.py:15
  125.7 4.5 %collective-permute-start.50 = (f32[8,256]{1,0:T(8,128)S(1)}, f32[8,256]{1,0:T(8,128)S(1)}, u32[]{:S(2)}, u32[]{:S(2)}) collective-permute-start(f32[8,256]{1,0:T(8,128)S(1)} %pad_maximum_fusion.2), channel_id=1, source_target_pairs={{0,24},{4,28},{8,16},{12,20},{16,8},{20,12},{24,0},{28,4},{1,25},{... | collective-permute-start | bytes 24584 | tf_op jit(solution)/shard_map/ppermute | solution.py:15
  126.8 4.0 %collective-permute-start.51 = (f32[8,256]{1,0:T(8,128)S(1)}, f32[8,256]{1,0:T(8,128)S(1)}, u32[]{:S(2)}, u32[]{:S(2)}) collective-permute-start(f32[8,256]{1,0:T(8,128)S(1)} %pad_maximum_fusion.2), channel_id=1, source_target_pairs={{0,28},{4,24},{8,20},{12,16},{16,12},{20,8},{24,4},{28,0},{1,29},{... | collective-permute-start | bytes 24584 | tf_op jit(solution)/shard_map/ppermute | solution.py:15
  128.0 3.7 %collective-permute-start.48 = (f32[8,256]{1,0:T(8,128)S(1)}, f32[8,256]{1,0:T(8,128)S(1)}, u32[]{:S(2)}, u32[]{:S(2)}) collective-permute-start(f32[8,256]{1,0:T(8,128)S(1)} %pad_maximum_fusion.2), channel_id=1, source_target_pairs={{0,16},{4,20},{8,24},{12,28},{16,0},{20,4},{24,8},{28,12},{1,17},{... | collective-permute-start | bytes 24584 | tf_op jit(solution)/shard_map/ppermute | solution.py:15
  128.5 3.2 %collective-permute-start.49 = (f32[8,256]{1,0:T(8,128)S(1)}, f32[8,256]{1,0:T(8,128)S(1)}, u32[]{:S(2)}, u32[]{:S(2)}) collective-permute-start(f32[8,256]{1,0:T(8,128)S(1)} %pad_maximum_fusion.2), channel_id=1, source_target_pairs={{0,20},{4,16},{8,28},{12,24},{16,4},{20,0},{24,12},{28,8},{1,21},{... | collective-permute-start | bytes 24584 | tf_op jit(solution)/shard_map/ppermute | solution.py:15
  135.1 4.6 %collective-permute-start.53 = (f32[2,2048]{1,0:T(2,128)S(1)}, f32[2,2048]{1,0:T(2,128)S(1)}, u32[]{:S(2)}, u32[]{:S(2)}) collective-permute-start(f32[2,2048]{1,0:T(2,128)S(1)} %fusion.3), channel_id=1, source_target_pairs={{0,2},{1,3},{2,0},{3,1},{4,6},{5,7},{6,4},{7,5},{8,10},{9,11},{10,... | collective-permute-start | bytes 49160 | tf_op jit(solution)/shard_map/ppermute | solution.py:15
  137.7 5.5 %collective-permute-start.54 = (f32[2,2048]{1,0:T(2,128)S(1)}, f32[2,2048]{1,0:T(2,128)S(1)}, u32[]{:S(2)}, u32[]{:S(2)}) collective-permute-start(f32[2,2048]{1,0:T(2,128)S(1)} %fusion.3), channel_id=1, source_target_pairs={{0,3},{1,2},{2,1},{3,0},{4,7},{5,6},{6,5},{7,4},{8,11},{9,10},{10,... | collective-permute-start | bytes 49160 | tf_op jit(solution)/shard_map/ppermute | solution.py:15
  139.0 4.2 %collective-permute-start.52 = (f32[2,2048]{1,0:T(2,128)S(1)}, f32[2,2048]{1,0:T(2,128)S(1)}, u32[]{:S(2)}, u32[]{:S(2)}) collective-permute-start(f32[2,2048]{1,0:T(2,128)S(1)} %fusion.3), channel_id=1, source_target_pairs={{0,1},{1,0},{2,3},{3,2},{4,5},{5,4},{6,7},{7,6},{8,9},{9,8},{10,11... | collective-permute-start | bytes 49160 | tf_op jit(solution)/shard_map/ppermute | solution.py:15
  (2 other events, 15.0 us)

commit v2 on v1

v2 whole, which is shorter than its diff:
```python
import functools
import math

import jax
import jax.numpy as jnp
from jax import lax
from jax.experimental import pallas as pl
from jax.experimental.pallas import tpu as pltpu
from jax.sharding import PartitionSpec as P

ROPE_BASE = 500000.0
EPSILON = 1e-05
FLOOR = -1e30
VMEM_BYTES = 16 * 1024 * 1024
CHEAP = pl.CostEstimate(flops=1000, bytes_accessed=1000, transcendentals=0)
IN_VMEM = pl.BlockSpec(memory_space=pltpu.VMEM)
IN_SMEM = pl.BlockSpec(memory_space=pltpu.SMEM)
IN_HBM = pl.BlockSpec(memory_space=pltpu.HBM)


def params():
    return pltpu.CompilerParams(vmem_limit_bytes=VMEM_BYTES)


def swap(value, axis, distance):
    count = lax.axis_size(axis)
    return lax.ppermute(value, axis, [(i, i ^ distance) for i in range(count)])


def pick(values, index):
    return lax.dynamic_index_in_dim(values, index, 0, keepdims=False)


def spread(value, axis):
    count = lax.axis_size(axis)
    return lax.all_to_all(jnp.broadcast_to(value[None], (count,) + value.shape), axis, 0, 0)


def rotary(values, placed):
    half_size = values.shape[-1] // 2
    frequency = jnp.exp(
        jnp.arange(half_size, dtype=jnp.float32) * (-2.0 * math.log(ROPE_BASE) / values.shape[-1])
    )
    angles = placed[..., None] * frequency
    cosine = jnp.cos(angles)
    sine_part = jnp.sin(angles)
    leading = values[..., :half_size]
    trailing = values[..., half_size:]
    return jnp.concatenate(
        (leading * cosine - trailing * sine_part, trailing * cosine + leading * sine_part), axis=-1
    )


def norm_kernel(chunk, x_ref, gain_ref, out_ref, sems):
    blocks, rows, width = out_ref.shape
    copies = []
    for c in range(rows // chunk):
        part = pl.ds(c * chunk, chunk)
        copies.append(
            [
                pltpu.make_async_copy(
                    x_ref.at[part, pl.ds(b * width, width)], out_ref.at[b, part, :], sems.at[c, b]
                )
                for b in range(blocks)
            ]
        )
        for copy in copies[-1]:
            copy.start()
    for c in range(rows // chunk):
        part = pl.ds(c * chunk, chunk)
        for copy in copies[c]:
            copy.wait()

        def add_squares(b, total):
            values = out_ref[b, part, :].astype(jnp.float32)
            squares = values * values
            for j in range(width // 128):
                total = total + squares[:, j * 128 : (j + 1) * 128]
            return total

        total = lax.fori_loop(0, blocks, add_squares, jnp.zeros((chunk, 128), jnp.float32))
        mean = jnp.sum(total, axis=-1, keepdims=True) / (blocks * width)
        factor = lax.rsqrt(mean + EPSILON)

        def scale(b, _):
            values = out_ref[b, part, :].astype(jnp.float32)
            out_ref[b, part, :] = (values * factor * gain_ref[b]).astype(jnp.bfloat16)
            return 0

        lax.fori_loop(0, blocks, scale, 0)


def normalise(hidden, gain_row, blocks):
    rows, features = hidden.shape
    width = features // blocks
    chunk = 32
    return pl.pallas_call(
        functools.partial(norm_kernel, chunk),
        in_specs=[IN_HBM, IN_VMEM],
        out_specs=IN_VMEM,
        out_shape=jax.ShapeDtypeStruct((blocks, rows, width), jnp.bfloat16),
        scratch_shapes=[pltpu.SemaphoreType.DMA((rows // chunk, blocks))],
        compiler_params=params(),
        cost_estimate=CHEAP,
        name="normalise",
    )(hidden, gain_row.reshape(blocks, 1, width))


def project_kernel(pieces, has_total, place_ref, rows_ref, *refs):
    place = place_ref[0]
    out_ref = refs[-1]
    total = refs[len(pieces)][...] if has_total else None
    for (distance, first), block_ref in zip(pieces, refs):
        depth = block_ref.shape[0]
        part = jnp.dot(
            rows_ref[place ^ distance, :, first : first + depth],
            block_ref[...],
            preferred_element_type=jnp.float32,
        )
        total = part if total is None else total + part
    out_ref[...] = total


def project(place, rows_in, blocks, total):
    extra = [] if total is None else [total]
    pieces = [(distance, first) for distance, first, _ in blocks]
    return pl.pallas_call(
        functools.partial(project_kernel, pieces, total is not None),
        in_specs=[IN_SMEM] + [IN_VMEM] * (1 + len(blocks) + len(extra)),
        out_specs=IN_VMEM,
        out_shape=jax.ShapeDtypeStruct((rows_in.shape[1], blocks[0][2].shape[1]), jnp.float32),
        compiler_params=params(),
        cost_estimate=CHEAP,
        name="project",
    )(place, rows_in, *[block for _, _, block in blocks], *extra)


def gather_rounds(own):
    count = lax.axis_size("ctx")
    rows = own.shape[0]
    bits = [1 << b for b in range(1, count.bit_length() - 1)]
    rounds = [[(0, 0, own)]] + [[] for _ in bits]
    halves = {}
    for bit in bits:
        block = swap(own, "ctx", bit)
        rounds[1].append((bit, 0, block))
        halves[bit] = (block[: rows // 2], block[rows // 2 :])
    for distance in sorted(range(2, count, 2), key=lambda d: bin(d).count("1")):
        hops = bin(distance).count("1")
        if hops < 2:
            continue
        low = distance & -distance
        high = 1 << (distance.bit_length() - 1)
        halves[distance] = (
            swap(halves[distance ^ high][0], "ctx", high),
            swap(halves[distance ^ low][1], "ctx", low),
        )
        rounds[hops].append((distance, 0, halves[distance][0]))
        rounds[hops].append((distance, rows // 2, halves[distance][1]))
    return [r + [(d ^ 1, first, swap(block, "ctx", 1)) for d, first, block in r] for r in rounds]


def project_all(place, rows_in, rounds):
    total = None
    for blocks in rounds:
        total = project(place, rows_in, blocks, total)
    return total


def shards(
    new_tokens,
    ctx_hidden,
    norm_gain,
    query_weight,
    key_weight,
    value_weight,
    out_weight,
    lengths,
    positions,
):
    ctx_count = lax.axis_size("ctx")
    place = lax.axis_index("ctx")
    places = place.astype(jnp.int32).reshape(1)
    row_count, features = ctx_hidden.shape[1:]
    head_size = key_weight.shape[2]
    heads = query_weight.shape[2] // head_size
    requests, width = new_tokens.shape
    slot_count = row_count * ctx_count // requests
    team = slot_count // row_count
    request = place // team
    scale = 1.0 / math.sqrt(head_size)
    gain_row = norm_gain[0]

    key_rounds = gather_rounds(key_weight[0])
    first_hop = [block for distance, _, block in key_rounds[1] if distance % 2 == 0]
    own_values = lax.optimization_barrier((value_weight[0], *first_hop))[0]
    value_rounds = gather_rounds(own_values)

    squares = jnp.sum(new_tokens * new_tokens, axis=-1)
    squares = spread(jnp.broadcast_to(squares[:, None], (requests, 128)), "ctx")
    factor = lax.rsqrt(jnp.sum(squares, axis=0)[:, :1] / features + EPSILON)
    own_gain = lax.dynamic_slice_in_dim(gain_row, place * width, width, 0)
    normed = (new_tokens * factor * own_gain).astype(jnp.bfloat16)
    parts = jnp.concatenate(
        [
            jnp.dot(normed, weight[0], preferred_element_type=jnp.float32)
            for weight in (query_weight, key_weight, value_weight)
        ],
        axis=1,
    ).reshape(requests, heads + 2, head_size)
    summed = jnp.sum(
        lax.all_to_all(jnp.repeat(parts, team, axis=0), "ctx", 0, 0), axis=0
    )
    new_place = pick(positions, request).astype(jnp.float32)
    turned = rotary(summed[: heads + 1], new_place[None]).astype(jnp.bfloat16)
    queries = turned[:heads]
    self_key = turned[heads]
    self_value = summed[heads + 1].astype(jnp.bfloat16).astype(jnp.float32)
    self_scores = (
        jnp.sum(queries.astype(jnp.float32) * self_key.astype(jnp.float32), axis=-1) * scale
    )

    ctx_normed = normalise(ctx_hidden[0], gain_row, ctx_count)
    within = (place % team) * row_count + jnp.arange(row_count, dtype=jnp.int32)
    live = within < pick(lengths, request)
    keys_raw = project_all(places, ctx_normed, key_rounds)
    ctx_keys = rotary(keys_raw, within.astype(jnp.float32)).astype(jnp.bfloat16)
    scores = jnp.einsum("gh,nh->gn", queries, ctx_keys, preferred_element_type=jnp.float32) * scale
    masked = jnp.where(live[None, :], scores, FLOOR)
    top = jnp.maximum(jnp.max(masked, axis=-1), self_scores)
    tops = spread(jnp.broadcast_to(top[:, None], (heads, 128)), "ctx")
    tops = tops.reshape(requests, team, heads, 128)[:, :, :, 0]
    top = jnp.max(pick(tops, request), axis=0)
    weights = jnp.where(live[None, :], jnp.exp(masked - top[:, None]), 0.0).astype(jnp.bfloat16)
    self_weight = jnp.exp(self_scores - top).astype(jnp.bfloat16).astype(jnp.float32)
    self_weight = jnp.where(place % team == 0, self_weight, 0.0)
    mass = jnp.sum(weights.astype(jnp.float32), axis=-1) + self_weight
    ctx_values = project_all(places, ctx_normed, value_rounds).astype(jnp.bfloat16)
    accum = jnp.dot(weights, ctx_values, preferred_element_type=jnp.float32)
    accum = accum + self_weight[:, None] * self_value

    packed = jnp.concatenate((accum, jnp.broadcast_to(mass[:, None], accum.shape)), axis=1)
    packed = spread(packed, "ctx")
    sums = jnp.sum(packed.reshape((requests, team) + packed.shape[1:]), axis=1)
    attended = (sums[..., :head_size] / sums[..., head_size:]).astype(jnp.bfloat16)
    update = jnp.dot(
        attended.reshape(requests, heads * head_size),
        out_weight[0],
        preferred_element_type=jnp.float32,
    )
    return new_tokens + jnp.sum(spread(update, "kv"), axis=0)


def solution(mesh):
    in_specs = (
        P(None, "ctx"),
        P(None, "ctx", None),
        P(),
        P(None, "ctx", "kv"),
        P(None, "ctx", "kv"),
        P(None, "ctx", "kv"),
        P(None, "kv", "ctx"),
        P(),
        P(),
    )
    out_specs = P(None, "ctx")
    return jax.shard_map(shards, mesh=mesh, in_specs=in_specs, out_specs=out_specs, check_vma=False)
```

time: 145 us -> 109 us (0.75)
  waiting for transfers between devices: 35.5 us -> 1.73 us
  matrix products: 37.7 us -> 4.53 us
  Pallas kernels: 0 us -> 21.9 us
  local copies, waits for them, and re-layouts: 8.62 us -> 28.2 us
  starting transfers between devices: 43.7 us -> 24.4 us
  blocking collectives: 0 us -> 19.3 us
  other arithmetic: 16.8 us -> 6.56 us
    ppermute x55 -> x18, waiting for transfers between devices: 35.5 us -> 0.05 us  [swap(): return lax.ppermute(value, axis, [(i, i ^ distance) for i in range(count)])]
    dot_general x31 -> x0, matrix products: 29.6 us -> none  [project(): part = jnp.dot(columns, block, preferred_element_type=jnp.float32)]
    ppermute x55 -> x18, starting transfers between devices: 43.7 us -> 14.4 us  [swap(): return lax.ppermute(value, axis, [(i, i ^ distance) for i in range(count)])]
    pallas_call x0 -> x7, Pallas kernels: none -> 21.9 us  [the longest x6 11.8 us: project(): pl.pallas_call(functools.partial(project_kernel, pieces, total is not Non...]
    all_to_all x0 -> x2, blocking collectives: none -> 19.3 us  [spread(): lax.all_to_all(jnp.broadcast_to(value[None], (count,) + value.shape), axi...]
    unnamed x22 -> x26, local copies, waits for them, and re-layouts: 4.09 us -> 19.9 us
    all_to_all x0 -> x3, starting transfers between devices: none -> 10 us  [the longest x2 6.66 us: spread(): lax.all_to_all(jnp.broadcast_to(value[None], (count,) + value.shape), axi...]
    convert_element_type x2 -> x1, other arithmetic: 6.85 us -> 0.57 us  [shards(): ctx_keys = rotary(keys_raw, within.astype(jnp.float32)).astype(jnp.bfloat16)]
  transfers between devices with their start and end apart: 55 -> 21, of which waited for: 15 -> 1; matrix products, arithmetic and copies ran while one was open for 34% -> 17% of each run, Pallas kernels for 0% -> 19%
where the time goes in v2:
time: 109 us; the launch traced here: 108 us
  local copies, waits for them, and re-layouts  28.2 us (26%)
  starting transfers between devices  24.4 us (22%)
  Pallas kernels  21.9 us (20%)
  blocking collectives  19.3 us (18%)
  other arithmetic  6.56 us (6%)
  matrix products  4.53 us (4%)
  waiting for transfers between devices  1.73 us (2%)
    unnamed x26, local copies, waits for them, and re-layouts  19.9 us
    all_to_all x2, blocking collectives, spread(): lax.all_to_all(jnp.broadcast_to(value[None], (count,) + value.shape), axi...  19.3 us
    ppermute x18, starting transfers between devices, swap(): return lax.ppermute(value, axis, [(i, i ^ distance) for i in range(count)])  14.4 us
    pallas_call x6, Pallas kernels, project(): pl.pallas_call(functools.partial(project_kernel, pieces, total is not Non...  11.8 us
    pallas_call x1, Pallas kernels, normalise(): pl.pallas_call(functools.partial(norm_kernel, chunk), in_specs=[IN_HBM, I...  10.2 us
    all_to_all x2, starting transfers between devices, spread(): lax.all_to_all(jnp.broadcast_to(value[None], (count,) + value.shape), axi...  6.66 us
    dot_general x3, matrix products, shards(): jnp.dot(normed, weight[0], preferred_element_type=jnp.float32)  3.36 us
    all_to_all x1, starting transfers between devices, shards(): lax.all_to_all(jnp.repeat(parts, team, axis=0), 'ctx', 0, 0)  3.35 us
  transfers between devices with their start and end apart: 21, of which 1 were waited for; matrix products, arithmetic and copies ran while one was open for 17% of the time, Pallas kernels for 19%

profile of v2, /device:TPU:0, one launch (start us, length us, event | category | flops | bytes accessed | tf_op | source)
XLA Modules:
  0.0 107.7 jit_solution(7197121446382123445)
XLA Ops:
  0.0 3.0 %collective-permute-start = (bf16[2048,128]{1,0:T(8,128)(2,1)}, bf16[2048,128]{1,0:T(8,128)(2,1)S(1)}, u32[]{:S(2)}, u32[]{:S(2)}) collective-permute-start(bf16[2048,128]{1,0:T(8,128)(2,1)} %bitcast.39), channel_id=1, source_target_pairs={{0,8},{4,12},{8,0},{12,4},{16,24},{20,28},{24,16},{28,20},{1,9},{5... | collective-permute-start | bytes 1572872 | tf_op jit(solution)/shard_map/ppermute | solution.py:27
  3.0 1.5 %collective-permute-start.2 = (bf16[2048,128]{1,0:T(8,128)(2,1)}, bf16[2048,128]{1,0:T(8,128)(2,1)S(1)}, u32[]{:S(2)}, u32[]{:S(2)}) collective-permute-start(bf16[2048,128]{1,0:T(8,128)(2,1)} %bitcast.40), channel_id=1, source_target_pairs={{0,16},{4,20},{8,24},{12,28},{16,0},{20,4},{24,8},{28,12},{1,17},{... | collective-permute-start | bytes 1572872 | tf_op jit(solution)/shard_map/ppermute | solution.py:27
  4.5 0.8 multiply_reduce_fusion
  5.4 0.7 broadcast_in_dim_broadcast_in_dim_broadcast_in_dim.4
  6.1 3.3 %all-to-all-start = ((f32[8,2,128]{2,1,0:T(2,128)}), f32[8,2,128]{2,1,0:T(2,128)S(1)}, u32[]{:S(2)}, u32[]{:S(2)}) async-start(f32[8,2,128]{2,1,0:T(2,128)} %broadcast_in_dim_broadcast_in_dim_broadcast_in_dim.4), calls=%async_computation | async-start | bytes 16384 | tf_op jit(solution)/shard_map/all_to_all | solution.py:36
  9.4 0.6 fusion.22
  10.0 1.3 %dynamic_slice.16 = s32[1]{0:T(128)} dynamic-slice(s32[2]{0:T(128)} %param.17, s32[]{:T(128)S(6)} %select_n.47), dynamic_slice_sizes={1} | dynamic-slice | bytes 12 | tf_op jit(solution)/shard_map/jit(dynamic_index_in_dim)/dynamic_slice | solution.py:31
  11.9 0.6 multiply_sine_fusion.1
  12.6 0.7 constant_dynamic-slice_fusion
  13.3 0.5 multiply_exponential_fusion
  13.8 1.3 %dynamic_slice.14 = s32[1]{0:T(128)} dynamic-slice(s32[2]{0:T(128)} %param.16, s32[]{:T(128)S(6)} %select_n.47), dynamic_slice_sizes={1} | dynamic-slice | bytes 12 | tf_op jit(solution)/shard_map/jit(dynamic_index_in_dim)/dynamic_slice | solution.py:31
  15.1 1.7 %all-to-all-done = f32[8,2,128]{2,1,0:T(2,128)S(1)} async-done(((f32[8,2,128]{2,1,0:T(2,128)}), f32[8,2,128]{2,1,0:T(2,128)S(1)}, u32[]{:S(2)}, u32[]{:S(2)}) %all-to-all-start) | async-done | bytes 8224 | tf_op jit(solution)/shard_map/all_to_all | solution.py:36
  16.8 0.1 rsqrt_reduce_fusion
  16.9 2.9 %fusion.2 = f32[2,1024]{1,0:T(2,128)S(1)} fusion(bf16[1,2048,1024]{2,1,0:T(8,128)(2,1)} %param.12, f32[2,2048]{1,0:T(2,128)} %param.9, f32[2]{0:T(128)S(1)} %rsqrt_reduce_fusion, f32[2048]{0:T(1024)S(1)} %bitcast.49), kind=kOutput, calls=%fused_computation.2 | convolution fusion | flops 8400896 | bytes 4227080 | tf_op jit(solution)/shard_map/dot_general | solution.py:206
  19.8 0.2 fusion.29
  20.0 1.2 %collective-permute-start.9 = (bf16[2048,128]{1,0:T(8,128)(2,1)S(1)}, bf16[2048,128]{1,0:T(8,128)(2,1)S(1)}, u32[]{:S(2)}, u32[]{:S(2)}) collective-permute-start(bf16[2048,128]{1,0:T(8,128)(2,1)S(1)} %bitcast.43), channel_id=1, source_target_pairs={{0,8},{4,12},{8,0},{12,4},{16,24},{20,28},{24,16},{28,20},{1,9},{5... | collective-permute-start | bytes 1572872 | tf_op jit(solution)/shard_map/ppermute | solution.py:27
  21.3 0.7 slice.68
  22.0 0.9 collective-permute-start.1
  22.9 0.2 fusion.31
  23.1 0.7 slice.69
  23.8 1.5 %collective-permute-start.3 = (bf16[1024,128]{1,0:T(8,128)(2,1)}, bf16[1024,128]{1,0:T(8,128)(2,1)}, u32[]{:S(2)}, u32[]{:S(2)}) collective-permute-start(bf16[1024,128]{1,0:T(8,128)(2,1)} %slice.69), channel_id=1, source_target_pairs={{0,8},{4,12},{8,0},{12,4},{16,24},{20,28},{24,16},{28,20},{1,9},{5... | collective-permute-start | bytes 786440 | tf_op jit(solution)/shard_map/ppermute | solution.py:27
  25.4 0.6 broadcast_in_dim.31
  26.0 3.3 %all-to-all-start.1 = ((f32[8,10,128]{2,1,0:T(8,128)}), f32[8,10,128]{2,1,0:T(8,128)S(1)}, u32[]{:S(2)}, u32[]{:S(2)}) async-start(f32[8,10,128]{2,1,0:T(8,128)} %bitcast.5), calls=%async_computation.1 | async-start | bytes 131072 | tf_op jit(solution)/shard_map/all_to_all | solution.py:212
  29.3 1.9 %collective-permute-start.11 = (bf16[2048,128]{1,0:T(8,128)(2,1)S(1)}, bf16[2048,128]{1,0:T(8,128)(2,1)S(1)}, u32[]{:S(2)}, u32[]{:S(2)}) collective-permute-start(bf16[2048,128]{1,0:T(8,128)(2,1)S(1)} %bitcast.44), channel_id=1, source_target_pairs={{0,16},{4,20},{8,24},{12,28},{16,0},{20,4},{24,8},{28,12},{1,17},{... | collective-permute-start | bytes 1572872 | tf_op jit(solution)/shard_map/ppermute | solution.py:27
  31.3 0.5 collective-permute-start.7
  31.8 1.1 %fusion.23 = pred[320]{0:T(512)(128)(4,1)} fusion(s32[]{:T(128)} %bitcast, s32[]{:T(128)S(6)} %mul.161), kind=kLoop, calls=%fused_computation.42 | loop fusion | flops 640 | bytes 328 | tf_op jit(solution)/shard_map/lt | solution.py:225
  33.0 4.0 %copy-done.4 = bf16[1,320,16384]{2,1,0:T(8,128)(2,1)S(1)} copy-done((bf16[1,320,16384]{2,1,0:T(8,128)(2,1)S(1)}, bf16[1,320,16384]{2,1,0:T(8,128)(2,1)}, u32[]{:S(2)}) %copy-start.4) | copy-done | bytes 10485784
  36.9 10.2 %normalise.1.rows_ref = bf16[8,320,2048]{2,1,0:T(8,128)(2,1)S(1)} custom-call(bf16[320,16384]{1,0:T(8,128)(2,1)S(1)} %bitcast.38, f32[8,1,2048]{2,1,0:T(1,128)S(1)} %bitcast.47), custom_call_target="tpu_custom_call" | custom-call | flops 1000 | bytes 1000 | tf_op jit(solution)/shard_map/normalise/pallas_call | solution.py:97
  47.1 4.0 %copy-done = bf16[8,320,2048]{2,1,0:T(8,128)(2,1)} copy-done((bf16[8,320,2048]{2,1,0:T(8,128)(2,1)}, bf16[8,320,2048]{2,1,0:T(8,128)(2,1)S(1)}, u32[]{:S(2)}) %copy-start) | copy-done | bytes 10485784
  51.2 0.1 collective-permute-start.4
  51.3 0.4 collective-permute-start.5
  51.7 0.7 add_convert_fusion
  52.5 0.1 fusion.27
  52.6 0.2 multiply_reduce_fusion.1
  52.7 4.0 %copy-done.1 = bf16[8,320,2048]{2,1,0:T(8,128)(2,1)S(1)} copy-done((bf16[8,320,2048]{2,1,0:T(8,128)(2,1)S(1)}, bf16[8,320,2048]{2,1,0:T(8,128)(2,1)}, u32[]{:S(2)}) %copy-start.1) | copy-done | bytes 10485784
  56.7 1.9 %project.6.refs_4_ = f32[320,128]{1,0:T(8,128)S(1)} custom-call(s32[1]{0:T(128)} %bitcast.7.place_ref, bf16[8,320,2048]{2,1,0:T(8,128)(2,1)S(1)} %copy-done.1, bf16[2048,128]{1,0:T(8,128)(2,1)S(1)} %bitcast.42, bf16[2048,128]{1,0:T(8,128)(2,1)} %collective-permute-done.8.refs_1_), custom_call_target="tpu_custom_call" | custom-call | flops 1000 | bytes 1000 | tf_op jit(solution)/shard_map/project/pallas_call | solution.py:127
  58.6 0.7 slice.73
  59.3 0.1 collective-permute-start.17
  59.4 0.7 slice.74
  60.2 0.2 collective-permute-start.10
  60.3 1.9 %collective-permute-start.12 = (bf16[1024,128]{1,0:T(8,128)(2,1)}, bf16[1024,128]{1,0:T(8,128)(2,1)}, u32[]{:S(2)}, u32[]{:S(2)}) collective-permute-start(bf16[1024,128]{1,0:T(8,128)(2,1)} %slice.74), channel_id=1, source_target_pairs={{0,8},{4,12},{8,0},{12,4},{16,24},{20,28},{24,16},{28,20},{1,9},{5... | collective-permute-start | bytes 786440 | tf_op jit(solution)/shard_map/ppermute | solution.py:27
  62.2 2.7 %project.7.refs_4_ = f32[320,128]{1,0:T(8,128)S(1)} custom-call(s32[1]{0:T(128)} %bitcast.7.place_ref, bf16[8,320,2048]{2,1,0:T(8,128)(2,1)S(1)} %copy-done.1, bf16[2048,128]{1,0:T(8,128)(2,1)S(1)} %collective-permute-done.refs_0_, bf16[2048,128]{1,0:T(8,128)(2,1)S(1)} %collective-permute-done.2.refs_1_, bf16[2048,128]{1,0:T(8,128)(2,1)} %collective-permute-done.6.refs_2_, ...), custom_call_target="tpu_custom_call" | custom-call | flops 1000 | bytes 1000 | tf_op jit(solution)/shard_map/project/pallas_call | solution.py:127
  64.9 1.8 %project.8 = f32[320,128]{1,0:T(8,128)S(1)} custom-call(s32[1]{0:T(128)} %bitcast.7.place_ref, bf16[8,320,2048]{2,1,0:T(8,128)(2,1)S(1)} %copy-done.1, bf16[1024,128]{1,0:T(8,128)(2,1)S(1)} %collective-permute-done.1.refs_0_, bf16[1024,128]{1,0:T(8,128)(2,1)} %collective-permute-done.3.refs_1_, bf16[1024,128]{1,0:T(8,128)(2,1)S(1)} %collective-permute-done.4.refs_2_, ...), custom_call_target="tpu_custom_call" | custom-call | flops 1000 | bytes 1000 | tf_op jit(solution)/shard_map/project/pallas_call | solution.py:127
  66.8 0.7 fusion.10
  67.5 0.3 fusion.35
  67.8 0.7 broadcast_in_dim_broadcast_in_dim_broadcast_in_dim.5
  68.5 3.3 %all-to-all-start.2 = ((f32[8,8,128]{2,1,0:T(8,128)}), f32[8,8,128]{2,1,0:T(8,128)S(1)}, u32[]{:S(2)}, u32[]{:S(2)}) async-start(f32[8,8,128]{2,1,0:T(8,128)} %broadcast_in_dim_broadcast_in_dim_broadcast_in_dim.5), calls=%async_computation.2 | async-start | bytes 65536 | tf_op jit(solution)/shard_map/all_to_all | solution.py:36
  71.8 0.4 collective-permute-start.15
  72.2 0.2 collective-permute-start.16
  72.4 4.0 %copy-done.2 = bf16[8,320,2048]{2,1,0:T(8,128)(2,1)S(1)} copy-done((bf16[8,320,2048]{2,1,0:T(8,128)(2,1)S(1)}, bf16[8,320,2048]{2,1,0:T(8,128)(2,1)}, u32[]{:S(2)}) %copy-start.2) | copy-done | bytes 10485784
  76.4 0.8 project.9.refs_4_
  77.3 0.1 dynamic-slice_reduce_fusion
  77.4 0.4 collective-permute-start.13
  77.8 0.2 collective-permute-start.14
  78.0 0.2 convert_reduce_fusion
  78.2 4.0 %copy-done.3 = bf16[8,320,2048]{2,1,0:T(8,128)(2,1)S(1)} copy-done((bf16[8,320,2048]{2,1,0:T(8,128)(2,1)S(1)}, bf16[8,320,2048]{2,1,0:T(8,128)(2,1)}, u32[]{:S(2)}) %copy-start.3) | copy-done | bytes 10485784
  82.2 2.5 %project.10.refs_4_ = f32[320,128]{1,0:T(8,128)S(1)} custom-call(s32[1]{0:T(128)} %bitcast.7.place_ref, bf16[8,320,2048]{2,1,0:T(8,128)(2,1)S(1)} %copy-done.3, bf16[2048,128]{1,0:T(8,128)(2,1)S(1)} %collective-permute-done.9.refs_0_, bf16[2048,128]{1,0:T(8,128)(2,1)S(1)} %collective-permute-done.11.refs_1_, ...), custom_call_target="tpu_custom_call" | custom-call | flops 1000 | bytes 1000 | tf_op jit(solution)/shard_map/project/pallas_call | solution.py:127
  84.8 2.0 %project.11 = f32[320,128]{1,0:T(8,128)S(1)} custom-call(s32[1]{0:T(128)} %bitcast.7.place_ref, bf16[8,320,2048]{2,1,0:T(8,128)(2,1)S(1)} %copy-done.3, bf16[1024,128]{1,0:T(8,128)(2,1)} %collective-permute-done.10.refs_0_, bf16[1024,128]{1,0:T(8,128)(2,1)} %collective-permute-done.12.refs_1_, bf16[1024,128]{1,0:T(8,128)(2,1)S(1)} %collective-permute-done.13.refs_2_, ...), custom_call_target="tpu_custom_call" | custom-call | flops 1000 | bytes 1000 | tf_op jit(solution)/shard_map/project/pallas_call | solution.py:127
  86.8 0.2 convolution_add_fusion
  87.0 0.1 broadcast_in_dim.60
  87.1 8.9 %all_to_all.25 = f32[8,8,256]{2,1,0:T(8,128)S(1)} all-to-all(f32[8,8,256]{2,1,0:T(8,128)S(1)} %broadcast_in_dim.61), channel_id=1, replica_groups=mesh['ctx'=8,'kv'=4] {'ctx'}, dimensions={0} | all-to-all | bytes 131072 | tf_op jit(solution)/shard_map/all_to_all | solution.py:36
  96.0 0.7 fusion
  96.6 10.4 %all_to_all.26 = f32[4,2,2048]{2,1,0:T(2,128)S(1)} all-to-all(f32[4,2,2048]{2,1,0:T(2,128)S(1)} %broadcast_in_dim.62), channel_id=1, replica_groups=mesh['ctx'=8,'kv'=4] {'kv'}, dimensions={0} | all-to-all | bytes 131072 | tf_op jit(solution)/shard_map/all_to_all | solution.py:36
  107.1 0.6 add.62
  (56 shorter events, 0.3 us)
Async XLA Ops:
  0.0 22.9 %copy-start.5 = (bf16[1,2048,128]{2,1,0:T(8,128)(2,1)S(1)}, bf16[1,2048,128]{2,1,0:T(8,128)(2,1)}, u32[]{:S(2)}) copy-start(bf16[1,2048,128]{2,1,0:T(8,128)(2,1)} %param.13) | copy-start | bytes 1572868
  0.0 19.8 %copy-start.9 = (f32[2,2048]{1,0:T(2,128)S(1)}, f32[2,2048]{1,0:T(2,128)}, u32[]{:S(2)}) copy-start(f32[2,2048]{1,0:T(2,128)} %param.9) | copy-start | bytes 49156
  0.0 32.9 %copy-start.7 = (f32[1,16384]{1,0:T(1,128)S(1)}, f32[1,16384]{1,0:T(1,128)}, u32[]{:S(2)}) copy-start(f32[1,16384]{1,0:T(1,128)} %param.11) | copy-start | bytes 196612
  0.0 19.8 %copy-start.6 = (bf16[1,2048,128]{2,1,0:T(8,128)(2,1)S(1)}, bf16[1,2048,128]{2,1,0:T(8,128)(2,1)}, u32[]{:S(2)}) copy-start(bf16[1,2048,128]{2,1,0:T(8,128)(2,1)} %param.14) | copy-start | bytes 1572868
  0.0 20.0 %collective-permute-start = (bf16[2048,128]{1,0:T(8,128)(2,1)}, bf16[2048,128]{1,0:T(8,128)(2,1)S(1)}, u32[]{:S(2)}, u32[]{:S(2)}) collective-permute-start(bf16[2048,128]{1,0:T(8,128)(2,1)} %bitcast.39), channel_id=1, source_target_pairs={{0,8},{4,12},{8,0},{12,4},{16,24},{20,28},{24,16},{28,20},{1,9},{5... | collective-permute-start | bytes 1572872 | tf_op jit(solution)/shard_map/ppermute | solution.py:27
  3.0 17.0 %collective-permute-start.2 = (bf16[2048,128]{1,0:T(8,128)(2,1)}, bf16[2048,128]{1,0:T(8,128)(2,1)S(1)}, u32[]{:S(2)}, u32[]{:S(2)}) collective-permute-start(bf16[2048,128]{1,0:T(8,128)(2,1)} %bitcast.40), channel_id=1, source_target_pairs={{0,16},{4,20},{8,24},{12,28},{16,0},{20,4},{24,8},{28,12},{1,17},{... | collective-permute-start | bytes 1572872 | tf_op jit(solution)/shard_map/ppermute | solution.py:27
  4.5 26.7 %collective-permute-start.8 = (bf16[2048,128]{1,0:T(8,128)(2,1)}, bf16[2048,128]{1,0:T(8,128)(2,1)}, u32[]{:S(2)}, u32[]{:S(2)}) collective-permute-start(bf16[2048,128]{1,0:T(8,128)(2,1)} %bitcast.41), channel_id=1, source_target_pairs={{0,4},{4,0},{8,12},{12,8},{16,20},{20,16},{24,28},{28,24},{1,5},{5... | collective-permute-start | bytes 1572872 | tf_op jit(solution)/shard_map/ppermute | solution.py:27
  6.1 10.7 %all-to-all-start = ((f32[8,2,128]{2,1,0:T(2,128)}), f32[8,2,128]{2,1,0:T(2,128)S(1)}, u32[]{:S(2)}, u32[]{:S(2)}) async-start(f32[8,2,128]{2,1,0:T(2,128)} %broadcast_in_dim_broadcast_in_dim_broadcast_in_dim.4), calls=%async_computation | async-start | bytes 16384 | tf_op jit(solution)/shard_map/all_to_all | solution.py:36
  20.0 31.3 %collective-permute-start.9 = (bf16[2048,128]{1,0:T(8,128)(2,1)S(1)}, bf16[2048,128]{1,0:T(8,128)(2,1)S(1)}, u32[]{:S(2)}, u32[]{:S(2)}) collective-permute-start(bf16[2048,128]{1,0:T(8,128)(2,1)S(1)} %bitcast.43), channel_id=1, source_target_pairs={{0,8},{4,12},{8,0},{12,4},{16,24},{20,28},{24,16},{28,20},{1,9},{5... | collective-permute-start | bytes 1572872 | tf_op jit(solution)/shard_map/ppermute | solution.py:27
  22.0 9.3 %collective-permute-start.1 = (bf16[1024,128]{1,0:T(8,128)(2,1)}, bf16[1024,128]{1,0:T(8,128)(2,1)S(1)}, u32[]{:S(2)}, u32[]{:S(2)}) collective-permute-start(bf16[1024,128]{1,0:T(8,128)(2,1)} %slice.68), channel_id=1, source_target_pairs={{0,16},{4,20},{8,24},{12,28},{16,0},{20,4},{24,8},{28,12},{1,17},{... | collective-permute-start | bytes 786440 | tf_op jit(solution)/shard_map/ppermute | solution.py:27
  23.8 27.3 %collective-permute-start.3 = (bf16[1024,128]{1,0:T(8,128)(2,1)}, bf16[1024,128]{1,0:T(8,128)(2,1)}, u32[]{:S(2)}, u32[]{:S(2)}) collective-permute-start(bf16[1024,128]{1,0:T(8,128)(2,1)} %slice.69), channel_id=1, source_target_pairs={{0,8},{4,12},{8,0},{12,4},{16,24},{20,28},{24,16},{28,20},{1,9},{5... | collective-permute-start | bytes 786440 | tf_op jit(solution)/shard_map/ppermute | solution.py:27
  26.0 25.1 %all-to-all-start.1 = ((f32[8,10,128]{2,1,0:T(8,128)}), f32[8,10,128]{2,1,0:T(8,128)S(1)}, u32[]{:S(2)}, u32[]{:S(2)}) async-start(f32[8,10,128]{2,1,0:T(8,128)} %bitcast.5), calls=%async_computation.1 | async-start | bytes 131072 | tf_op jit(solution)/shard_map/all_to_all | solution.py:212
  29.3 30.0 %collective-permute-start.11 = (bf16[2048,128]{1,0:T(8,128)(2,1)S(1)}, bf16[2048,128]{1,0:T(8,128)(2,1)S(1)}, u32[]{:S(2)}, u32[]{:S(2)}) collective-permute-start(bf16[2048,128]{1,0:T(8,128)(2,1)S(1)} %bitcast.44), channel_id=1, source_target_pairs={{0,16},{4,20},{8,24},{12,28},{16,0},{20,4},{24,8},{28,12},{1,17},{... | collective-permute-start | bytes 1572872 | tf_op jit(solution)/shard_map/ppermute | solution.py:27
  31.3 28.9 %collective-permute-start.6 = (bf16[2048,128]{1,0:T(8,128)(2,1)S(1)}, bf16[2048,128]{1,0:T(8,128)(2,1)}, u32[]{:S(2)}, u32[]{:S(2)}) collective-permute-start(bf16[2048,128]{1,0:T(8,128)(2,1)S(1)} %collective-permute-done.refs_0_), channel_id=1, source_target_pairs={{0,4},{4,0},{8,12},{12,8},{16,20},{20,16},{24,28},{28,24},{1,5},{5... | collective-permute-start | bytes 1572872 | tf_op jit(solution)/shard_map/ppermute | solution.py:27
  31.3 29.0 %collective-permute-start.7 = (bf16[2048,128]{1,0:T(8,128)(2,1)S(1)}, bf16[2048,128]{1,0:T(8,128)(2,1)}, u32[]{:S(2)}, u32[]{:S(2)}) collective-permute-start(bf16[2048,128]{1,0:T(8,128)(2,1)S(1)} %collective-permute-done.2.refs_1_), channel_id=1, source_target_pairs={{0,4},{4,0},{8,12},{12,8},{16,20},{20,16},{24,28},{28,24},{1,5},{5... | collective-permute-start | bytes 1572872 | tf_op jit(solution)/shard_map/ppermute | solution.py:27
  33.0 4.0 %copy-start.4 = (bf16[1,320,16384]{2,1,0:T(8,128)(2,1)S(1)}, bf16[1,320,16384]{2,1,0:T(8,128)(2,1)}, u32[]{:S(2)}) copy-start(bf16[1,320,16384]{2,1,0:T(8,128)(2,1)} %param.10) | copy-start | bytes 31457284
  47.1 4.0 %copy-start = (bf16[8,320,2048]{2,1,0:T(8,128)(2,1)}, bf16[8,320,2048]{2,1,0:T(8,128)(2,1)S(1)}, u32[]{:S(2)}) copy-start(bf16[8,320,2048]{2,1,0:T(8,128)(2,1)S(1)} %normalise.1.rows_ref) | copy-start | bytes 31457284
  51.2 13.8 %collective-permute-start.4 = (bf16[1024,128]{1,0:T(8,128)(2,1)S(1)}, bf16[1024,128]{1,0:T(8,128)(2,1)S(1)}, u32[]{:S(2)}, u32[]{:S(2)}) collective-permute-start(bf16[1024,128]{1,0:T(8,128)(2,1)S(1)} %collective-permute-done.1.refs_0_), channel_id=1, source_target_pairs={{0,4},{4,0},{8,12},{12,8},{16,20},{20,16},{24,28},{28,24},{1,5},{5... | collective-permute-start | bytes 786440 | tf_op jit(solution)/shard_map/ppermute | solution.py:27
  51.3 13.6 %collective-permute-start.5 = (bf16[1024,128]{1,0:T(8,128)(2,1)}, bf16[1024,128]{1,0:T(8,128)(2,1)S(1)}, u32[]{:S(2)}, u32[]{:S(2)}) collective-permute-start(bf16[1024,128]{1,0:T(8,128)(2,1)} %collective-permute-done.3.refs_1_), channel_id=1, source_target_pairs={{0,4},{4,0},{8,12},{12,8},{16,20},{20,16},{24,28},{28,24},{1,5},{5... | collective-permute-start | bytes 786440 | tf_op jit(solution)/shard_map/ppermute | solution.py:27
  52.7 4.0 %copy-start.1 = (bf16[8,320,2048]{2,1,0:T(8,128)(2,1)S(1)}, bf16[8,320,2048]{2,1,0:T(8,128)(2,1)}, u32[]{:S(2)}) copy-start(bf16[8,320,2048]{2,1,0:T(8,128)(2,1)} %copy-done) | copy-start | bytes 31457284
  59.3 13.1 %collective-permute-start.17 = (bf16[2048,128]{1,0:T(8,128)(2,1)S(1)}, bf16[2048,128]{1,0:T(8,128)(2,1)S(1)}, u32[]{:S(2)}, u32[]{:S(2)}) collective-permute-start(bf16[2048,128]{1,0:T(8,128)(2,1)S(1)} %bitcast.45), channel_id=1, source_target_pairs={{0,4},{4,0},{8,12},{12,8},{16,20},{20,16},{24,28},{28,24},{1,5},{5... | collective-permute-start | bytes 1572872 | tf_op jit(solution)/shard_map/ppermute | solution.py:27
  60.2 17.2 %collective-permute-start.10 = (bf16[1024,128]{1,0:T(8,128)(2,1)}, bf16[1024,128]{1,0:T(8,128)(2,1)}, u32[]{:S(2)}, u32[]{:S(2)}) collective-permute-start(bf16[1024,128]{1,0:T(8,128)(2,1)} %slice.73), channel_id=1, source_target_pairs={{0,16},{4,20},{8,24},{12,28},{16,0},{20,4},{24,8},{28,12},{1,17},{... | collective-permute-start | bytes 786440 | tf_op jit(solution)/shard_map/ppermute | solution.py:27
  60.3 17.5 %collective-permute-start.12 = (bf16[1024,128]{1,0:T(8,128)(2,1)}, bf16[1024,128]{1,0:T(8,128)(2,1)}, u32[]{:S(2)}, u32[]{:S(2)}) collective-permute-start(bf16[1024,128]{1,0:T(8,128)(2,1)} %slice.74), channel_id=1, source_target_pairs={{0,8},{4,12},{8,0},{12,4},{16,24},{20,28},{24,16},{28,20},{1,9},{5... | collective-permute-start | bytes 786440 | tf_op jit(solution)/shard_map/ppermute | solution.py:27
  64.9 1.9 %copy-start.10 = (f32[320]{0:T(512)S(1)}, f32[320]{0:T(512)}, u32[]{:S(2)}) copy-start(f32[320]{0:T(512)} %fusion.22) | copy-start | bytes 3844
  64.9 1.9 %copy-start.12 = (f32[64]{0:T(128)S(1)}, f32[64]{0:T(128)}, u32[]{:S(2)}) copy-start(f32[64]{0:T(128)} %multiply_exponential_fusion) | copy-start | bytes 772
  64.9 2.6 %copy-start.11 = (pred[320]{0:T(512)(128)(4,1)S(1)}, pred[320]{0:T(512)(128)(4,1)}, u32[]{:S(2)}) copy-start(pred[320]{0:T(512)(128)(4,1)} %fusion.23) | copy-start | bytes 964
  68.5 8.7 %all-to-all-start.2 = ((f32[8,8,128]{2,1,0:T(8,128)}), f32[8,8,128]{2,1,0:T(8,128)S(1)}, u32[]{:S(2)}, u32[]{:S(2)}) async-start(f32[8,8,128]{2,1,0:T(8,128)} %broadcast_in_dim_broadcast_in_dim_broadcast_in_dim.5), calls=%async_computation.2 | async-start | bytes 65536 | tf_op jit(solution)/shard_map/all_to_all | solution.py:36
  71.8 6.3 %collective-permute-start.15 = (bf16[2048,128]{1,0:T(8,128)(2,1)S(1)}, bf16[2048,128]{1,0:T(8,128)(2,1)S(1)}, u32[]{:S(2)}, u32[]{:S(2)}) collective-permute-start(bf16[2048,128]{1,0:T(8,128)(2,1)S(1)} %collective-permute-done.9.refs_0_), channel_id=1, source_target_pairs={{0,4},{4,0},{8,12},{12,8},{16,20},{20,16},{24,28},{28,24},{1,5},{5... | collective-permute-start | bytes 1572872 | tf_op jit(solution)/shard_map/ppermute | solution.py:27
  72.2 5.9 %collective-permute-start.16 = (bf16[2048,128]{1,0:T(8,128)(2,1)S(1)}, bf16[2048,128]{1,0:T(8,128)(2,1)}, u32[]{:S(2)}, u32[]{:S(2)}) collective-permute-start(bf16[2048,128]{1,0:T(8,128)(2,1)S(1)} %collective-permute-done.11.refs_1_), channel_id=1, source_target_pairs={{0,4},{4,0},{8,12},{12,8},{16,20},{20,16},{24,28},{28,24},{1,5},{5... | collective-permute-start | bytes 1572872 | tf_op jit(solution)/shard_map/ppermute | solution.py:27
  72.4 4.0 %copy-start.2 = (bf16[8,320,2048]{2,1,0:T(8,128)(2,1)S(1)}, bf16[8,320,2048]{2,1,0:T(8,128)(2,1)}, u32[]{:S(2)}) copy-start(bf16[8,320,2048]{2,1,0:T(8,128)(2,1)} %copy-done) | copy-start | bytes 31457284
  77.4 7.4 %collective-permute-start.13 = (bf16[1024,128]{1,0:T(8,128)(2,1)}, bf16[1024,128]{1,0:T(8,128)(2,1)S(1)}, u32[]{:S(2)}, u32[]{:S(2)}) collective-permute-start(bf16[1024,128]{1,0:T(8,128)(2,1)} %collective-permute-done.10.refs_0_), channel_id=1, source_target_pairs={{0,4},{4,0},{8,12},{12,8},{16,20},{20,16},{24,28},{28,24},{1,5},{5... | collective-permute-start | bytes 786440 | tf_op jit(solution)/shard_map/ppermute | solution.py:27
  77.8 7.0 %collective-permute-start.14 = (bf16[1024,128]{1,0:T(8,128)(2,1)}, bf16[1024,128]{1,0:T(8,128)(2,1)S(1)}, u32[]{:S(2)}, u32[]{:S(2)}) collective-permute-start(bf16[1024,128]{1,0:T(8,128)(2,1)} %collective-permute-done.12.refs_1_), channel_id=1, source_target_pairs={{0,4},{4,0},{8,12},{12,8},{16,20},{20,16},{24,28},{28,24},{1,5},{5... | collective-permute-start | bytes 786440 | tf_op jit(solution)/shard_map/ppermute | solution.py:27
  78.2 4.0 %copy-start.3 = (bf16[8,320,2048]{2,1,0:T(8,128)(2,1)S(1)}, bf16[8,320,2048]{2,1,0:T(8,128)(2,1)}, u32[]{:S(2)}) copy-start(bf16[8,320,2048]{2,1,0:T(8,128)(2,1)} %copy-done) | copy-start | bytes 31457284
  84.7 11.2 %copy-start.8 = (bf16[1,1024,2048]{2,1,0:T(8,128)(2,1)S(1)}, bf16[1,1024,2048]{2,1,0:T(8,128)(2,1)}, u32[]{:S(2)}) copy-start(bf16[1,1024,2048]{2,1,0:T(8,128)(2,1)} %param.15) | copy-start | bytes 12582916

commit v3 on v2

v3 whole, which is shorter than its diff:
```python
import functools
import math

import jax
import jax.numpy as jnp
from jax import lax
from jax.experimental import pallas as pl
from jax.experimental.pallas import tpu as pltpu
from jax.sharding import PartitionSpec as P

ROPE_BASE = 500000.0
EPSILON = 1e-05
FLOOR = -1e30
LANES = 128
NORM_ROWS = 64
VMEM_BYTES = 16 * 1024 * 1024
CHEAP = pl.CostEstimate(flops=1000, bytes_accessed=1000, transcendentals=0)
IN_VMEM = pl.BlockSpec(memory_space=pltpu.VMEM)
IN_SMEM = pl.BlockSpec(memory_space=pltpu.SMEM)
IN_HBM = pl.BlockSpec(memory_space=pltpu.HBM)


def call(kernel, name, in_specs, out_shape, scratch_shapes=()):
    return pl.pallas_call(
        kernel,
        in_specs=in_specs,
        out_specs=jax.tree.map(lambda _: IN_VMEM, out_shape),
        out_shape=out_shape,
        scratch_shapes=scratch_shapes,
        compiler_params=pltpu.CompilerParams(vmem_limit_bytes=VMEM_BYTES),
        cost_estimate=CHEAP,
        name=name,
    )


def shape(dims, dtype=jnp.float32):
    return jax.ShapeDtypeStruct(dims, dtype)


def swap(value, axis, distance):
    count = lax.axis_size(axis)
    return lax.ppermute(value, axis, [(i, i ^ distance) for i in range(count)])


def after(value, *others):
    return lax.optimization_barrier((value, *others))[0]


def bits_below(count):
    return [1 << b for b in range(count.bit_length() - 1)]


def tables(placed, head_size):
    half_size = head_size // 2
    frequency = jnp.exp(
        jnp.arange(half_size, dtype=jnp.float32) * (-2.0 * math.log(ROPE_BASE) / head_size)
    )
    angles = placed[..., None] * frequency
    cosine = jnp.cos(angles)
    sine_part = jnp.sin(angles)
    return (
        jnp.concatenate((cosine, cosine), axis=-1),
        jnp.concatenate((-sine_part, sine_part), axis=-1),
    )


def turn(values, cosine, signed_sine):
    half_size = values.shape[-1] // 2
    swapped = jnp.concatenate((values[:, half_size:], values[:, :half_size]), axis=-1)
    return values * cosine + swapped * signed_sine


def squares_kernel(tokens_ref, out_ref):
    values = tokens_ref[...]
    total = jnp.sum(values * values, axis=-1, keepdims=True)
    out_ref[...] = jnp.broadcast_to(total, out_ref.shape)


def norm_kernel(first, x_ref, gain_ref, out_ref, sems):
    blocks, rows, width = out_ref.shape
    step = 16
    copies = []
    for c in range(rows // step):
        copies.append(
            [
                pltpu.make_async_copy(
                    x_ref.at[pl.ds(first + c * step, step), pl.ds(b * width, width)],
                    out_ref.at[b, pl.ds(c * step, step), :],
                    sems.at[c, b],
                )
                for b in range(blocks)
            ]
        )
        for copy in copies[-1]:
            copy.start()
    for c in range(rows // step):
        part = pl.ds(c * step, step)
        for copy in copies[c]:
            copy.wait()

        def add_squares(b, totals):
            totals = list(totals)
            for j in range(width // LANES):
                values = out_ref[b, part, j * LANES : (j + 1) * LANES].astype(jnp.float32)
                totals[j % 4] = totals[j % 4] + values * values
            return tuple(totals)

        zero = jnp.zeros((step, LANES), jnp.float32)
        totals = lax.fori_loop(0, blocks, add_squares, (zero,) * 4)
        total = (totals[0] + totals[1]) + (totals[2] + totals[3])
        mean = jnp.sum(total, axis=-1, keepdims=True) / (blocks * width)
        factor = jnp.broadcast_to(lax.rsqrt(mean + EPSILON), (step, LANES))

        def scale(b, _):
            for j in range(width // LANES):
                lanes = slice(j * LANES, (j + 1) * LANES)
                values = out_ref[b, part, lanes].astype(jnp.float32)
                out_ref[b, part, lanes] = (values * factor * gain_ref[b, :, lanes]).astype(
                    jnp.bfloat16
                )
            return 0

        lax.fori_loop(0, blocks, scale, 0)


def normalise(hidden, gains, first):
    blocks, _, width = gains.shape
    return call(
        functools.partial(norm_kernel, first),
        "normalise",
        [IN_HBM, IN_VMEM],
        shape((blocks, NORM_ROWS, width), jnp.bfloat16),
        [pltpu.SemaphoreType.DMA((NORM_ROWS // 16, blocks))],
    )(pltpu.with_memory_space_constraint(hidden, pltpu.HBM), gains)


def query_kernel(
    features, place_ref, squares_ref, tokens_ref, gains_ref, query_ref, key_ref, value_ref, out_ref
):
    requests = tokens_ref.shape[0]
    factor = lax.rsqrt(squares_ref[:, :1] / features + EPSILON)
    normed = (tokens_ref[...] * factor * gains_ref[place_ref[0]]).astype(jnp.bfloat16)
    row = 0
    for weight_ref in (query_ref, key_ref, value_ref):
        part = jnp.dot(normed, weight_ref[...], preferred_element_type=jnp.float32)
        for h in range(weight_ref.shape[1] // LANES):
            for r in range(requests):
                out_ref[r, row : row + 1, :] = part[r : r + 1, h * LANES : (h + 1) * LANES]
            row += 1


def blocks_dot(pieces, place, row_refs, block_refs, total):
    for (distance, first), block_ref in zip(pieces, block_refs):
        depth = block_ref.shape[0]
        rows = jnp.concatenate(
            [ref[place ^ distance, :, first : first + depth] for ref in row_refs], axis=0
        )
        part = jnp.dot(rows, block_ref[...], preferred_element_type=jnp.float32)
        total = part if total is None else total + part
    return total


def project_kernel(pieces, row_count, has_total, place_ref, *refs):
    rows, refs = refs[:row_count], refs[row_count:]
    total = refs[len(pieces)][...] if has_total else None
    refs[-1][...] = blocks_dot(pieces, place_ref[0], rows, refs, total)


def project(place, rows, blocks, total):
    extra = [] if total is None else [total]
    pieces = [(distance, first) for distance, first, _ in blocks]
    row_count = sum(r.shape[1] for r in rows)
    return call(
        functools.partial(project_kernel, pieces, len(rows), total is not None),
        "project",
        [IN_SMEM] + [IN_VMEM] * (len(rows) + len(blocks) + len(extra)),
        shape((row_count, blocks[0][2].shape[1])),
    )(place, *rows, *[block for _, _, block in blocks], *extra)


def live_rows(dims, team, place, lengths_ref):
    rows = dims[1]
    within = lax.rem(place, team) * rows + lax.broadcasted_iota(jnp.int32, dims, 1)
    return within < lengths_ref[lax.div(place, team)]


def score_kernel(pieces, row_count, team, place_ref, lengths_ref, *refs):
    rows, refs = refs[:row_count], refs[row_count:]
    blocks, refs = refs[: len(pieces)], refs[len(pieces) :]
    total_ref, cos_ref, sin_ref, new_cos_ref, new_sin_ref, summed_ref = refs[:6]
    masked_ref, top_ref, self_ref = refs[6:]
    place = place_ref[0]
    request = lax.div(place, team)
    heads = masked_ref.shape[0]
    scale = 1.0 / math.sqrt(LANES)
    turned = turn(
        summed_ref[...], new_cos_ref[pl.ds(request, 1), :], new_sin_ref[pl.ds(request, 1), :]
    ).astype(jnp.bfloat16)
    queries = turned[:heads]
    self_key = turned[heads : heads + 1].astype(jnp.float32)
    self_scores = (
        jnp.sum(queries.astype(jnp.float32) * self_key, axis=-1, keepdims=True) * scale
    )
    keys = blocks_dot(pieces, place, rows, blocks, total_ref[...])
    keys = turn(keys, cos_ref[...], sin_ref[...]).astype(jnp.bfloat16)
    scores = (
        lax.dot_general(
            queries, keys, (((1,), (1,)), ((), ())), preferred_element_type=jnp.float32
        )
        * scale
    )
    masked = jnp.where(live_rows(scores.shape, team, place, lengths_ref), scores, FLOOR)
    masked_ref[...] = masked
    top = jnp.maximum(jnp.max(masked, axis=-1, keepdims=True), self_scores)
    top_ref[...] = jnp.broadcast_to(top, top_ref.shape)
    self_ref[...] = jnp.broadcast_to(self_scores, self_ref.shape)


def weigh_kernel(pieces, row_count, team, place_ref, lengths_ref, *refs):
    rows, refs = refs[:row_count], refs[row_count:]
    blocks, refs = refs[: len(pieces)], refs[len(pieces) :]
    total_ref, masked_ref, top_ref, self_ref, summed_ref, out_ref = refs
    place = place_ref[0]
    heads = masked_ref.shape[0]
    masked = masked_ref[...]
    top = top_ref[:, :1]
    live = live_rows(masked.shape, team, place, lengths_ref)
    weights = jnp.where(live, jnp.exp(masked - top), 0.0).astype(jnp.bfloat16)
    self_weight = jnp.exp(self_ref[...] - top_ref[...]).astype(jnp.bfloat16).astype(jnp.float32)
    self_weight = jnp.where(lax.rem(place, team) == 0, self_weight, 0.0)
    self_value = summed_ref[heads + 1 : heads + 2, :].astype(jnp.bfloat16).astype(jnp.float32)
    mass = jnp.sum(weights.astype(jnp.float32), axis=-1, keepdims=True) + self_weight
    values = blocks_dot(pieces, place, rows, blocks, total_ref[...]).astype(jnp.bfloat16)
    accum = jnp.dot(weights, values, preferred_element_type=jnp.float32)
    out_ref[:, :LANES] = accum + self_weight * self_value
    out_ref[:, LANES:] = mass


def output_kernel(team, place_ref, mine_ref, other_ref, weight_ref, out_ref):
    request = lax.div(place_ref[0], team)
    heads = mine_ref.shape[0]
    attended = []
    for ref in (mine_ref, other_ref):
        attended.append(ref[:, :LANES] / ref[:, LANES:])
    first = jnp.where(request == 0, attended[0], attended[1]).astype(jnp.bfloat16)
    second = jnp.where(request == 0, attended[1], attended[0]).astype(jnp.bfloat16)
    both = jnp.concatenate(
        [
            jnp.concatenate((first[h : h + 1], second[h : h + 1]), axis=0)
            for h in range(heads)
        ],
        axis=1,
    )
    out_ref[...] = jnp.dot(both, weight_ref[...], preferred_element_type=jnp.float32)


def gather_rounds(own):
    count = lax.axis_size("ctx")
    rows = own.shape[0]
    bits = [1 << b for b in range(1, count.bit_length() - 1)]
    rounds = [[(0, 0, own)]] + [[] for _ in bits]
    halves = {}
    for bit in bits:
        block = swap(own, "ctx", bit)
        rounds[1].append((bit, 0, block))
        halves[bit] = (block[: rows // 2], block[rows // 2 :])
    for distance in sorted(range(2, count, 2), key=lambda d: bin(d).count("1")):
        hops = bin(distance).count("1")
        if hops < 2:
            continue
        low = distance & -distance
        high = 1 << (distance.bit_length() - 1)
        halves[distance] = (
            swap(halves[distance ^ high][0], "ctx", high),
            swap(halves[distance ^ low][1], "ctx", low),
        )
        rounds[hops].append((distance, 0, halves[distance][0]))
        rounds[hops].append((distance, rows // 2, halves[distance][1]))
    return [r + [(d ^ 1, first, swap(block, "ctx", 1)) for d, first, block in r] for r in rounds]


def shards(
    new_tokens,
    ctx_hidden,
    norm_gain,
    query_weight,
    key_weight,
    value_weight,
    out_weight,
    lengths,
    positions,
):
    ctx_count = lax.axis_size("ctx")
    kv_count = lax.axis_size("kv")
    place = lax.axis_index("ctx").astype(jnp.int32)
    places = place.reshape(1)
    row_count, features = ctx_hidden.shape[1:]
    head_size = key_weight.shape[2]
    heads = query_weight.shape[2] // head_size
    requests, width = new_tokens.shape
    slot_count = row_count * ctx_count // requests
    team = slot_count // row_count
    assert requests == 2 and slot_count % row_count == 0 and row_count % NORM_ROWS == 0
    assert head_size == LANES
    gains = norm_gain.reshape(ctx_count, 1, width)
    steps = row_count // NORM_ROWS

    key_rounds = gather_rounds(key_weight[0])

    rows = []

    def normalise_beside(sent, received):
        if len(rows) == steps:
            return received
        rows.append(normalise(after(ctx_hidden[0], sent), gains, len(rows) * NORM_ROWS))
        return after(received, rows[-1])

    squares = call(squares_kernel, "squares", [IN_VMEM], shape((requests, LANES)))(new_tokens)
    for distance in bits_below(ctx_count):
        received = normalise_beside(squares, swap(squares, "ctx", distance))
        squares = squares + received
    parts = call(
        functools.partial(query_kernel, features),
        "query_products",
        [IN_SMEM] + [IN_VMEM] * 6,
        shape((requests, heads + 2, head_size)),
    )(places, squares, new_tokens, gains, query_weight[0], key_weight[0], value_weight[0])
    request = place // team
    own_part = jnp.where(request == 0, parts[0], parts[1])
    sent = jnp.where(request == 0, parts[1], parts[0])
    summed = own_part + normalise_beside(sent, swap(sent, "ctx", team))
    for distance in bits_below(team):
        received = normalise_beside(summed, swap(summed, "ctx", distance))
        summed = summed + received
    while len(rows) < steps:
        normalise_beside(summed, summed)

    within = (place % team) * row_count + jnp.arange(row_count, dtype=jnp.int32)
    cosine, sine_part = tables(within.astype(jnp.float32), head_size)
    new_cosine, new_sine = tables(positions.astype(jnp.float32), head_size)
    key_total = None
    for blocks in key_rounds[:-1]:
        key_total = project(places, rows, blocks, key_total)
    blocks = key_rounds[-1]
    masked, top, self_scores = call(
        functools.partial(
            score_kernel, [(d, first) for d, first, _ in blocks], len(rows), team
        ),
        "scores",
        [IN_SMEM] * 2 + [IN_VMEM] * (len(rows) + len(blocks) + 6),
        (shape((heads, row_count)), shape((heads, LANES)), shape((heads, LANES))),
    )(
        places,
        lengths,
        *rows,
        *[block for _, _, block in blocks],
        key_total,
        cosine,
        sine_part,
        new_cosine,
        new_sine,
        summed,
    )
    for distance in bits_below(team):
        top = jnp.maximum(top, swap(top, "ctx", distance))

    value_rounds = gather_rounds(after(value_weight[0], key_total))
    value_total = None
    for blocks in value_rounds[:-1]:
        value_total = project(places, rows, blocks, value_total)
    blocks = value_rounds[-1]
    packed = call(
        functools.partial(
            weigh_kernel, [(d, first) for d, first, _ in blocks], len(rows), team
        ),
        "weighted_values",
        [IN_SMEM] * 2 + [IN_VMEM] * (len(rows) + len(blocks) + 5),
        shape((heads, 2 * head_size)),
    )(
        places,
        lengths,
        *rows,
        *[block for _, _, block in blocks],
        value_total,
        masked,
        top,
        self_scores,
        summed,
    )
    for distance in bits_below(team):
        packed = packed + swap(packed, "ctx", distance)
    other = swap(packed, "ctx", team)
    update = call(
        functools.partial(output_kernel, team),
        "output_products",
        [IN_SMEM] + [IN_VMEM] * 3,
        shape((requests, out_weight.shape[2])),
    )(places, packed, other, out_weight[0])
    for distance in bits_below(kv_count):
        update = update + swap(update, "kv", distance)
    return new_tokens + update


def solution(mesh):
    in_specs = (
        P(None, "ctx"),
        P(None, "ctx", None),
        P(),
        P(None, "ctx", "kv"),
        P(None, "ctx", "kv"),
        P(None, "ctx", "kv"),
        P(None, "kv", "ctx"),
        P(),
        P(),
    )
    out_specs = P(None, "ctx")
    return jax.shard_map(shards, mesh=mesh, in_specs=in_specs, out_specs=out_specs, check_vma=False)
```

time: 109 us -> 84.5 us (0.78)
  waiting for transfers between devices: 1.73 us -> 30.5 us
  local copies, waits for them, and re-layouts: 28.2 us -> 3.12 us
  blocking collectives: 19.3 us -> 0 us
  other arithmetic: 6.56 us -> 1.67 us
  matrix products: 4.53 us -> 0 us
  Pallas kernels: 21.9 us -> 25.1 us
  starting transfers between devices: 24.4 us -> 23.3 us
    ppermute x18 -> x31, waiting for transfers between devices: 0.05 us -> 30.5 us  [swap(): return lax.ppermute(value, axis, [(i, i ^ distance) for i in range(count)])]
    all_to_all x2 -> x0, blocking collectives: 19.3 us -> none  [spread(): lax.all_to_all(jnp.broadcast_to(value[None], (count,) + value.shape), axi...]
    unnamed x26 -> x24, local copies, waits for them, and re-layouts: 19.9 us -> 3.05 us
    all_to_all x3 -> x0, starting transfers between devices: 10 us -> none  [the longest x2 6.66 us: spread(): lax.all_to_all(jnp.broadcast_to(value[None], (count,) + value.shape), axi...]
    ppermute x18 -> x31, starting transfers between devices: 14.4 us -> 23.3 us  [swap(): return lax.ppermute(value, axis, [(i, i ^ distance) for i in range(count)])]
    dot_general x6 -> x0, matrix products: 4.53 us -> none  [the longest x3 3.36 us: shards(): jnp.dot(normed, weight[0], preferred_element_type=jnp.float32)]
    dynamic_slice x3 -> x0, local copies, waits for them, and re-layouts: 3.3 us -> none  [the longest x2 2.6 us: pick(): return lax.dynamic_index_in_dim(values, index, 0, keepdims=False)]
    pallas_call x7 -> x14, Pallas kernels: 21.9 us -> 25.1 us  [the longest x5 14.5 us: normalise(): call(functools.partial(norm_kernel, first), 'normalise', [IN_HBM, IN_VMEM...]
  transfers between devices with their start and end apart: 21 -> 31, of which waited for: 1 -> 13; matrix products, arithmetic and copies ran while one was open for 17% -> 1% of each run, Pallas kernels for 19% -> 27%
where the time goes in v3:
time: 84.5 us; the launch traced here: 84.1 us
  waiting for transfers between devices  30.5 us (36%)
  Pallas kernels  25.1 us (30%)
  starting transfers between devices  23.3 us (28%)
  local copies, waits for them, and re-layouts  3.12 us (4%)
  other arithmetic  1.67 us (2%)
    ppermute x31, waiting for transfers between devices, swap(): return lax.ppermute(value, axis, [(i, i ^ distance) for i in range(count)])  30.5 us
    ppermute x31, starting transfers between devices, swap(): return lax.ppermute(value, axis, [(i, i ^ distance) for i in range(count)])  23.3 us
    pallas_call x5, Pallas kernels, normalise(): call(functools.partial(norm_kernel, first), 'normalise', [IN_HBM, IN_VMEM...  14.5 us
    pallas_call x4, Pallas kernels, project(): call(functools.partial(project_kernel, pieces, len(rows), total is not No...  5.79 us
    unnamed x24, local copies, waits for them, and re-layouts  3.05 us
    pallas_call x1, Pallas kernels, shards(): call(functools.partial(score_kernel, [(d, first) for d, first, _ in block...  1.71 us
  transfers between devices with their start and end apart: 31, of which 13 were waited for; matrix products, arithmetic and copies ran while one was open for 1% of the time, Pallas kernels for 27%

profile of v3, /device:TPU:0, one launch (start us, length us, event | category | flops | bytes accessed | tf_op | source)
XLA Modules:
  0.0 84.1 jit_solution(17560704314418473513)
XLA Ops:
  0.0 2.9 %collective-permute-start.4 = (bf16[2048,128]{1,0:T(8,128)(2,1)}, bf16[2048,128]{1,0:T(8,128)(2,1)S(1)}, u32[]{:S(2)}, u32[]{:S(2)}) collective-permute-start(bf16[2048,128]{1,0:T(8,128)(2,1)} %bitcast.19), channel_id=1, source_target_pairs={{0,8},{4,12},{8,0},{12,4},{16,24},{20,28},{24,16},{28,20},{1,9},{5... | collective-permute-start | bytes 1572872 | tf_op jit(solution)/shard_map/ppermute | solution.py:42
  2.9 1.5 %collective-permute-start.5 = (bf16[2048,128]{1,0:T(8,128)(2,1)}, bf16[2048,128]{1,0:T(8,128)(2,1)S(1)}, u32[]{:S(2)}, u32[]{:S(2)}) collective-permute-start(bf16[2048,128]{1,0:T(8,128)(2,1)} %bitcast.20), channel_id=1, source_target_pairs={{0,16},{4,20},{8,24},{12,28},{16,0},{20,4},{24,8},{28,12},{1,17},{... | collective-permute-start | bytes 1572872 | tf_op jit(solution)/shard_map/ppermute | solution.py:42
  4.5 0.7 copy-done.8
  5.2 0.1 squares.1
  5.3 0.5 collective-permute-start.8
  5.8 0.8 copy-done.4
  6.6 2.9 %normalise.5.refs_0_ = bf16[8,64,2048]{2,1,0:T(8,128)(2,1)S(1)} custom-call(bf16[320,16384]{1,0:T(8,128)(2,1)} %bitcast.29, f32[8,1,2048]{2,1,0:T(1,128)S(1)} %bitcast.13), custom_call_target="tpu_custom_call" | custom-call | flops 1000 | bytes 1000 | tf_op jit(solution)/shard_map/normalise/pallas_call | solution.py:128
  9.5 0.6 collective-permute-start.1
  10.1 2.8 %normalise.6.refs_1_ = bf16[8,64,2048]{2,1,0:T(8,128)(2,1)S(1)} custom-call(bf16[320,16384]{1,0:T(8,128)(2,1)} %bitcast.30, f32[8,1,2048]{2,1,0:T(1,128)S(1)} %bitcast.14), custom_call_target="tpu_custom_call" | custom-call | flops 1000 | bytes 1000 | tf_op jit(solution)/shard_map/normalise/pallas_call | solution.py:128
  13.0 1.3 %copy-done = bf16[8,64,2048]{2,1,0:T(8,128)(2,1)} copy-done((bf16[8,64,2048]{2,1,0:T(8,128)(2,1)}, bf16[8,64,2048]{2,1,0:T(8,128)(2,1)S(1)}, u32[]{:S(2)}) %copy-start) | copy-done | bytes 2097176
  14.3 0.8 collective-permute-done.1
  15.1 1.8 %collective-permute-start.2 = (f32[2,128]{1,0:T(2,128)S(1)}, f32[2,128]{1,0:T(2,128)S(1)}, u32[]{:S(2)}, u32[]{:S(2)}) collective-permute-start(f32[2,128]{1,0:T(2,128)S(1)} %add.49), channel_id=1, source_target_pairs={{0,16},{4,20},{8,24},{12,28},{16,0},{20,4},{24,8},{28,12},{1,17},{... | collective-permute-start | bytes 3080 | tf_op jit(solution)/shard_map/ppermute | solution.py:42
  16.9 0.0 copy-start.9
  16.9 3.0 %normalise.7.refs_2_ = bf16[8,64,2048]{2,1,0:T(8,128)(2,1)S(1)} custom-call(bf16[320,16384]{1,0:T(8,128)(2,1)} %bitcast.31, f32[8,1,2048]{2,1,0:T(1,128)S(1)} %bitcast.15), custom_call_target="tpu_custom_call" | custom-call | flops 1000 | bytes 1000 | tf_op jit(solution)/shard_map/normalise/pallas_call | solution.py:128
  20.0 0.1 copy-done.7
  20.1 0.8 query_products.1
  20.9 0.1 collective-permute-start.6
  21.0 0.5 collective-permute-start.7
  21.5 0.4 collective-permute-start.3
  21.9 2.8 %normalise.8.refs_3_ = bf16[8,64,2048]{2,1,0:T(8,128)(2,1)S(1)} custom-call(bf16[320,16384]{1,0:T(8,128)(2,1)} %bitcast.32, f32[8,1,2048]{2,1,0:T(1,128)S(1)} %bitcast.17), custom_call_target="tpu_custom_call" | custom-call | flops 1000 | bytes 1000 | tf_op jit(solution)/shard_map/normalise/pallas_call | solution.py:128
  24.8 0.4 collective-permute-done.3
  25.2 1.3 %collective-permute-start.18 = (bf16[1024,128]{1,0:T(8,128)(2,1)S(1)}, bf16[1024,128]{1,0:T(8,128)(2,1)S(1)}, u32[]{:S(2)}, u32[]{:S(2)}) collective-permute-start(bf16[1024,128]{1,0:T(8,128)(2,1)S(1)} %slice.30), channel_id=1, source_target_pairs={{0,16},{4,20},{8,24},{12,28},{16,0},{20,4},{24,8},{28,12},{1,17},{... | collective-permute-start | bytes 786440 | tf_op jit(solution)/shard_map/ppermute | solution.py:42
  26.5 1.6 %collective-permute-start.19 = (bf16[1024,128]{1,0:T(8,128)(2,1)S(1)}, bf16[1024,128]{1,0:T(8,128)(2,1)S(1)}, u32[]{:S(2)}, u32[]{:S(2)}) collective-permute-start(bf16[1024,128]{1,0:T(8,128)(2,1)S(1)} %slice.31), channel_id=1, source_target_pairs={{0,8},{4,12},{8,0},{12,4},{16,24},{20,28},{24,16},{28,20},{1,9},{5... | collective-permute-start | bytes 786440 | tf_op jit(solution)/shard_map/ppermute | solution.py:42
  28.1 3.0 %normalise.9.refs_4_ = bf16[8,64,2048]{2,1,0:T(8,128)(2,1)S(1)} custom-call(bf16[320,16384]{1,0:T(8,128)(2,1)} %bitcast.33, f32[8,1,2048]{2,1,0:T(1,128)S(1)} %bitcast.18), custom_call_target="tpu_custom_call" | custom-call | flops 1000 | bytes 1000 | tf_op jit(solution)/shard_map/normalise/pallas_call | solution.py:128
  31.1 1.9 %project.4.refs_9_ = f32[320,128]{1,0:T(8,128)S(1)} custom-call(s32[1]{0:T(128)} %bitcast.place_ref, bf16[8,64,2048]{2,1,0:T(8,128)(2,1)S(1)} %normalise.5.refs_0_, bf16[8,64,2048]{2,1,0:T(8,128)(2,1)S(1)} %copy-done.1, bf16[8,64,2048]{2,1,0:T(8,128)(2,1)S(1)} %normalise.7.refs_2_, bf16[8,64,2048]{2,1,0:T(8,128)(2,1)S(1)} %normalise.8.refs_3_, ...), custom_call_target="tpu_custom_call" | custom-call | flops 1000 | bytes 1000 | tf_op jit(solution)/shard_map/project/pallas_call | solution.py:173
  33.0 0.0 copy-start.11
  33.1 1.5 %project.5.refs_9_ = f32[320,128]{1,0:T(8,128)S(1)} custom-call(s32[1]{0:T(128)} %bitcast.place_ref, bf16[8,64,2048]{2,1,0:T(8,128)(2,1)S(1)} %normalise.5.refs_0_, bf16[8,64,2048]{2,1,0:T(8,128)(2,1)S(1)} %copy-done.1, bf16[8,64,2048]{2,1,0:T(8,128)(2,1)S(1)} %normalise.7.refs_2_, bf16[8,64,2048]{2,1,0:T(8,128)(2,1)S(1)} %normalise.8.refs_3_, ...), custom_call_target="tpu_custom_call" | custom-call | flops 1000 | bytes 1000 | tf_op jit(solution)/shard_map/project/pallas_call | solution.py:173
  34.6 0.6 collective-permute-start.9
  35.2 0.8 collective-permute-start.11
  36.0 0.6 fusion
  36.7 0.1 collective-permute-start.20
  36.7 0.5 collective-permute-start.21
  37.2 0.1 fusion.1
  37.3 0.1 collective-permute-start.22
  37.5 0.2 pad_maximum_fusion
  37.7 1.0 %collective-permute-done.22 = f32[10,128]{1,0:T(8,128)S(1)} collective-permute-done((f32[10,128]{1,0:T(8,128)S(1)}, f32[10,128]{1,0:T(8,128)S(1)}, u32[]{:S(2)}, u32[]{:S(2)}) %collective-permute-start.22) | collective-permute-done | bytes 5152 | tf_op jit(solution)/shard_map/ppermute | solution.py:42
  38.6 1.5 %collective-permute-start.23 = (f32[10,128]{1,0:T(8,128)S(1)}, f32[10,128]{1,0:T(8,128)S(1)}, u32[]{:S(2)}, u32[]{:S(2)}) collective-permute-start(f32[10,128]{1,0:T(8,128)S(1)} %add.55), channel_id=1, source_target_pairs={{0,8},{4,12},{8,0},{12,4},{16,24},{20,28},{24,16},{28,20},{1,9},{5... | collective-permute-start | bytes 15368 | tf_op jit(solution)/shard_map/ppermute | solution.py:42
  40.1 0.1 pad_maximum_fusion.2
  40.2 7.7 %collective-permute-done.23 = f32[10,128]{1,0:T(8,128)S(1)} collective-permute-done((f32[10,128]{1,0:T(8,128)S(1)}, f32[10,128]{1,0:T(8,128)S(1)}, u32[]{:S(2)}, u32[]{:S(2)}) %collective-permute-start.23) | collective-permute-done | bytes 5152 | tf_op jit(solution)/shard_map/ppermute | solution.py:42
  47.9 1.7 %scores.1 = (f32[8,320]{1,0:T(8,128)S(1)}, f32[8,128]{1,0:T(8,128)S(1)}, f32[8,128]{1,0:T(8,128)S(1)}) custom-call(s32[1]{0:T(128)} %bitcast.place_ref, s32[2]{0:T(128)S(1)} %copy-done.10, bf16[8,64,2048]{2,1,0:T(8,128)(2,1)S(1)} %normalise.5.refs_0_, bf16[8,64,2048]{2,1,0:T(8,128)(2,1)S(1)} %copy-done.1, bf16[8,64,2048]{2,1,0:T(8,128)(2,1)S(1)} %normalise.7.refs_2_, ...), custom_call_target="tpu_custom_call" | custom-call | flops 1000 | bytes 1000 | tf_op jit(solution)/shard_map/scores/pallas_call | solution.py:345
  49.6 1.2 %collective-permute-done.24 = f32[8,128]{1,0:T(8,128)S(1)} collective-permute-done((f32[8,128]{1,0:T(8,128)S(1)}, f32[8,128]{1,0:T(8,128)S(1)}, u32[]{:S(2)}, u32[]{:S(2)}) %collective-permute-start.24) | collective-permute-done | bytes 4128 | tf_op jit(solution)/shard_map/ppermute | solution.py:42
  50.8 0.5 collective-permute-start.25
  51.4 0.5 collective-permute-start.10
  51.9 0.2 collective-permute-start.15
  52.1 0.3 collective-permute-start.16
  52.4 2.0 %collective-permute-done.25 = f32[8,128]{1,0:T(8,128)S(1)} collective-permute-done((f32[8,128]{1,0:T(8,128)S(1)}, f32[8,128]{1,0:T(8,128)S(1)}, u32[]{:S(2)}, u32[]{:S(2)}) %collective-permute-start.25) | collective-permute-done | bytes 4128 | tf_op jit(solution)/shard_map/ppermute | solution.py:42
  54.4 0.5 collective-permute-start.12
  55.0 5.2 %collective-permute-done.10.refs_5_ = bf16[1024,128]{1,0:T(8,128)(2,1)S(1)} collective-permute-done((bf16[1024,128]{1,0:T(8,128)(2,1)S(1)}, bf16[1024,128]{1,0:T(8,128)(2,1)S(1)}, u32[]{:S(2)}, u32[]{:S(2)}) %collective-permute-start.10) | collective-permute-done | bytes 262176 | tf_op jit(solution)/shard_map/ppermute | solution.py:42
  60.2 1.5 %collective-permute-done.12.refs_6_ = bf16[1024,128]{1,0:T(8,128)(2,1)S(1)} collective-permute-done((bf16[1024,128]{1,0:T(8,128)(2,1)S(1)}, bf16[1024,128]{1,0:T(8,128)(2,1)S(1)}, u32[]{:S(2)}, u32[]{:S(2)}) %collective-permute-start.12) | collective-permute-done | bytes 262176 | tf_op jit(solution)/shard_map/ppermute | solution.py:42
  61.7 0.9 %project.6.refs_9_ = f32[320,128]{1,0:T(8,128)S(1)} custom-call(s32[1]{0:T(128)} %bitcast.place_ref, bf16[8,64,2048]{2,1,0:T(8,128)(2,1)S(1)} %normalise.5.refs_0_, bf16[8,64,2048]{2,1,0:T(8,128)(2,1)S(1)} %copy-done.1, bf16[8,64,2048]{2,1,0:T(8,128)(2,1)S(1)} %normalise.7.refs_2_, bf16[8,64,2048]{2,1,0:T(8,128)(2,1)S(1)} %normalise.8.refs_3_, ...), custom_call_target="tpu_custom_call" | custom-call | flops 1000 | bytes 1000 | tf_op jit(solution)/shard_map/project/pallas_call | solution.py:173
  62.6 1.5 %project.7.refs_9_ = f32[320,128]{1,0:T(8,128)S(1)} custom-call(s32[1]{0:T(128)} %bitcast.place_ref, bf16[8,64,2048]{2,1,0:T(8,128)(2,1)S(1)} %normalise.5.refs_0_, bf16[8,64,2048]{2,1,0:T(8,128)(2,1)S(1)} %copy-done.1, bf16[8,64,2048]{2,1,0:T(8,128)(2,1)S(1)} %normalise.7.refs_2_, bf16[8,64,2048]{2,1,0:T(8,128)(2,1)S(1)} %normalise.8.refs_3_, ...), custom_call_target="tpu_custom_call" | custom-call | flops 1000 | bytes 1000 | tf_op jit(solution)/shard_map/project/pallas_call | solution.py:173
  64.1 1.5 %weighted_values.1 = f32[8,256]{1,0:T(8,128)S(1)} custom-call(s32[1]{0:T(128)} %bitcast.place_ref, s32[2]{0:T(128)S(1)} %copy-done.10, bf16[8,64,2048]{2,1,0:T(8,128)(2,1)S(1)} %normalise.5.refs_0_, bf16[8,64,2048]{2,1,0:T(8,128)(2,1)S(1)} %copy-done.1, bf16[8,64,2048]{2,1,0:T(8,128)(2,1)S(1)} %normalise.7.refs_2_, ...), custom_call_target="tpu_custom_call" | custom-call | flops 1000 | bytes 1000 | tf_op jit(solution)/shard_map/weighted_values/pallas_call | solution.py:372
  65.6 0.5 collective-permute-start.26
  66.2 0.8 collective-permute-done.26
  67.0 0.8 collective-permute-start.27
  67.8 2.8 %collective-permute-done.27 = f32[8,256]{1,0:T(8,128)S(1)} collective-permute-done((f32[8,256]{1,0:T(8,128)S(1)}, f32[8,256]{1,0:T(8,128)S(1)}, u32[]{:S(2)}, u32[]{:S(2)}) %collective-permute-start.27) | collective-permute-done | bytes 8224 | tf_op jit(solution)/shard_map/ppermute | solution.py:42
  70.7 0.9 %collective-permute-start.28 = (f32[8,256]{1,0:T(8,128)S(1)}, f32[8,256]{1,0:T(8,128)S(1)}, u32[]{:S(2)}, u32[]{:S(2)}) collective-permute-start(f32[8,256]{1,0:T(8,128)S(1)} %add.58.mine_ref), channel_id=1, source_target_pairs={{0,16},{4,20},{8,24},{12,28},{16,0},{20,4},{24,8},{28,12},{1,17},{... | collective-permute-start | bytes 24584 | tf_op jit(solution)/shard_map/ppermute | solution.py:42
  71.5 2.8 %collective-permute-done.28.other_ref = f32[8,256]{1,0:T(8,128)S(1)} collective-permute-done((f32[8,256]{1,0:T(8,128)S(1)}, f32[8,256]{1,0:T(8,128)S(1)}, u32[]{:S(2)}, u32[]{:S(2)}) %collective-permute-start.28) | collective-permute-done | bytes 8224 | tf_op jit(solution)/shard_map/ppermute | solution.py:42
  74.3 0.7 output_products.1
  75.0 1.6 %collective-permute-start.29 = (f32[2,2048]{1,0:T(2,128)S(1)}, f32[2,2048]{1,0:T(2,128)S(1)}, u32[]{:S(2)}, u32[]{:S(2)}) collective-permute-start(f32[2,2048]{1,0:T(2,128)S(1)} %output_products.1), channel_id=1, source_target_pairs={{0,1},{1,0},{2,3},{3,2},{4,5},{5,4},{6,7},{7,6},{8,9},{9,8},{10,11... | collective-permute-start | bytes 49160 | tf_op jit(solution)/shard_map/ppermute | solution.py:42
  76.6 2.2 %collective-permute-done.29 = f32[2,2048]{1,0:T(2,128)S(1)} collective-permute-done((f32[2,2048]{1,0:T(2,128)S(1)}, f32[2,2048]{1,0:T(2,128)S(1)}, u32[]{:S(2)}, u32[]{:S(2)}) %collective-permute-start.29) | collective-permute-done | bytes 16416 | tf_op jit(solution)/shard_map/ppermute | solution.py:42
  78.7 2.7 %collective-permute-start.30 = (f32[2,2048]{1,0:T(2,128)S(1)}, f32[2,2048]{1,0:T(2,128)S(1)}, u32[]{:S(2)}, u32[]{:S(2)}) collective-permute-start(f32[2,2048]{1,0:T(2,128)S(1)} %add.59), channel_id=1, source_target_pairs={{0,2},{1,3},{2,0},{3,1},{4,6},{5,7},{6,4},{7,5},{8,10},{9,11},{10,... | collective-permute-start | bytes 49160 | tf_op jit(solution)/shard_map/ppermute | solution.py:42
  81.4 2.1 %collective-permute-done.30 = f32[2,2048]{1,0:T(2,128)S(1)} collective-permute-done((f32[2,2048]{1,0:T(2,128)S(1)}, f32[2,2048]{1,0:T(2,128)S(1)}, u32[]{:S(2)}, u32[]{:S(2)}) %collective-permute-start.30) | collective-permute-done | bytes 16416 | tf_op jit(solution)/shard_map/ppermute | solution.py:42
  83.4 0.6 add_add_fusion
  (60 shorter events, 0.2 us)
Async XLA Ops:
  0.0 20.9 %collective-permute-start.4 = (bf16[2048,128]{1,0:T(8,128)(2,1)}, bf16[2048,128]{1,0:T(8,128)(2,1)S(1)}, u32[]{:S(2)}, u32[]{:S(2)}) collective-permute-start(bf16[2048,128]{1,0:T(8,128)(2,1)} %bitcast.19), channel_id=1, source_target_pairs={{0,8},{4,12},{8,0},{12,4},{16,24},{20,28},{24,16},{28,20},{1,9},{5... | collective-permute-start | bytes 1572872 | tf_op jit(solution)/shard_map/ppermute | solution.py:42
  2.9 18.1 %collective-permute-start.5 = (bf16[2048,128]{1,0:T(8,128)(2,1)}, bf16[2048,128]{1,0:T(8,128)(2,1)S(1)}, u32[]{:S(2)}, u32[]{:S(2)}) collective-permute-start(bf16[2048,128]{1,0:T(8,128)(2,1)} %bitcast.20), channel_id=1, source_target_pairs={{0,16},{4,20},{8,24},{12,28},{16,0},{20,4},{24,8},{28,12},{1,17},{... | collective-permute-start | bytes 1572872 | tf_op jit(solution)/shard_map/ppermute | solution.py:42
  4.5 0.7 copy-start.8
  5.3 4.2 %collective-permute-start = (f32[2,128]{1,0:T(2,128)S(1)}, f32[2,128]{1,0:T(2,128)S(1)}, u32[]{:S(2)}, u32[]{:S(2)}) collective-permute-start(f32[2,128]{1,0:T(2,128)S(1)} %squares.1), channel_id=1, source_target_pairs={{0,4},{4,0},{8,12},{12,8},{16,20},{20,16},{24,28},{28,24},{1,5},{5... | collective-permute-start | bytes 3080 | tf_op jit(solution)/shard_map/ppermute | solution.py:42
  5.3 25.8 %collective-permute-start.8 = (bf16[2048,128]{1,0:T(8,128)(2,1)}, bf16[2048,128]{1,0:T(8,128)(2,1)}, u32[]{:S(2)}, u32[]{:S(2)}) collective-permute-start(bf16[2048,128]{1,0:T(8,128)(2,1)} %bitcast.21), channel_id=1, source_target_pairs={{0,4},{4,0},{8,12},{12,8},{16,20},{20,16},{24,28},{28,24},{1,5},{5... | collective-permute-start | bytes 1572872 | tf_op jit(solution)/shard_map/ppermute | solution.py:42
  5.8 0.8 copy-start.4
  6.6 3.5 %copy-start.5 = (f32[1,16384]{1,0:T(1,128)S(1)}, f32[1,16384]{1,0:T(1,128)}, u32[]{:S(2)}) copy-start(f32[1,16384]{1,0:T(1,128)} %param.11) | copy-start | bytes 196612
  9.5 5.6 %collective-permute-start.1 = (f32[2,128]{1,0:T(2,128)S(1)}, f32[2,128]{1,0:T(2,128)S(1)}, u32[]{:S(2)}, u32[]{:S(2)}) collective-permute-start(f32[2,128]{1,0:T(2,128)S(1)} %add.48), channel_id=1, source_target_pairs={{0,8},{4,12},{8,0},{12,4},{16,24},{20,28},{24,16},{28,20},{1,9},{5... | collective-permute-start | bytes 3080 | tf_op jit(solution)/shard_map/ppermute | solution.py:42
  13.0 1.3 %copy-start = (bf16[8,64,2048]{2,1,0:T(8,128)(2,1)}, bf16[8,64,2048]{2,1,0:T(8,128)(2,1)S(1)}, u32[]{:S(2)}) copy-start(bf16[8,64,2048]{2,1,0:T(8,128)(2,1)S(1)} %normalise.6.refs_1_) | copy-start | bytes 6291460
  15.1 4.8 %collective-permute-start.2 = (f32[2,128]{1,0:T(2,128)S(1)}, f32[2,128]{1,0:T(2,128)S(1)}, u32[]{:S(2)}, u32[]{:S(2)}) collective-permute-start(f32[2,128]{1,0:T(2,128)S(1)} %add.49), channel_id=1, source_target_pairs={{0,16},{4,20},{8,24},{12,28},{16,0},{20,4},{24,8},{28,12},{1,17},{... | collective-permute-start | bytes 3080 | tf_op jit(solution)/shard_map/ppermute | solution.py:42
  16.9 3.1 %copy-start.2 = (bf16[1,2048,1024]{2,1,0:T(8,128)(2,1)S(1)}, bf16[1,2048,1024]{2,1,0:T(8,128)(2,1)}, u32[]{:S(2)}) copy-start(bf16[1,2048,1024]{2,1,0:T(8,128)(2,1)} %param.12) | copy-start | bytes 12582916
  16.9 3.1 %copy-start.6 = (bf16[1,2048,128]{2,1,0:T(8,128)(2,1)S(1)}, bf16[1,2048,128]{2,1,0:T(8,128)(2,1)}, u32[]{:S(2)}) copy-start(bf16[1,2048,128]{2,1,0:T(8,128)(2,1)} %param.13) | copy-start | bytes 1572868
  16.9 3.2 %copy-start.7 = (bf16[1,2048,128]{2,1,0:T(8,128)(2,1)S(1)}, bf16[1,2048,128]{2,1,0:T(8,128)(2,1)}, u32[]{:S(2)}) copy-start(bf16[1,2048,128]{2,1,0:T(8,128)(2,1)} %param.14) | copy-start | bytes 1572868
  16.9 3.2 %copy-start.9 = (f32[2,2048]{1,0:T(2,128)S(1)}, f32[2,2048]{1,0:T(2,128)}, u32[]{:S(2)}) copy-start(f32[2,2048]{1,0:T(2,128)} %tokens_ref.3) | copy-start | bytes 49156
  20.9 12.1 %collective-permute-start.6 = (bf16[2048,128]{1,0:T(8,128)(2,1)S(1)}, bf16[2048,128]{1,0:T(8,128)(2,1)S(1)}, u32[]{:S(2)}, u32[]{:S(2)}) collective-permute-start(bf16[2048,128]{1,0:T(8,128)(2,1)S(1)} %collective-permute-done.4.refs_5_), channel_id=1, source_target_pairs={{0,4},{4,0},{8,12},{12,8},{16,20},{20,16},{24,28},{28,24},{1,5},{5... | collective-permute-start | bytes 1572872 | tf_op jit(solution)/shard_map/ppermute | solution.py:42
  21.0 12.0 %collective-permute-start.7 = (bf16[2048,128]{1,0:T(8,128)(2,1)S(1)}, bf16[2048,128]{1,0:T(8,128)(2,1)S(1)}, u32[]{:S(2)}, u32[]{:S(2)}) collective-permute-start(bf16[2048,128]{1,0:T(8,128)(2,1)S(1)} %collective-permute-done.5.refs_6_), channel_id=1, source_target_pairs={{0,4},{4,0},{8,12},{12,8},{16,20},{20,16},{24,28},{28,24},{1,5},{5... | collective-permute-start | bytes 1572872 | tf_op jit(solution)/shard_map/ppermute | solution.py:42
  21.5 3.7 %collective-permute-start.3 = (f32[10,128]{1,0:T(8,128)S(1)}, f32[10,128]{1,0:T(8,128)S(1)}, u32[]{:S(2)}, u32[]{:S(2)}) collective-permute-start(f32[10,128]{1,0:T(8,128)S(1)} %select_bitcast_fusion), channel_id=1, source_target_pairs={{0,16},{4,20},{8,24},{12,28},{16,0},{20,4},{24,8},{28,12},{1,17},{... | collective-permute-start | bytes 15368 | tf_op jit(solution)/shard_map/ppermute | solution.py:42
  25.2 11.5 %collective-permute-start.18 = (bf16[1024,128]{1,0:T(8,128)(2,1)S(1)}, bf16[1024,128]{1,0:T(8,128)(2,1)S(1)}, u32[]{:S(2)}, u32[]{:S(2)}) collective-permute-start(bf16[1024,128]{1,0:T(8,128)(2,1)S(1)} %slice.30), channel_id=1, source_target_pairs={{0,16},{4,20},{8,24},{12,28},{16,0},{20,4},{24,8},{28,12},{1,17},{... | collective-permute-start | bytes 786440 | tf_op jit(solution)/shard_map/ppermute | solution.py:42
  26.5 10.2 %collective-permute-start.19 = (bf16[1024,128]{1,0:T(8,128)(2,1)S(1)}, bf16[1024,128]{1,0:T(8,128)(2,1)S(1)}, u32[]{:S(2)}, u32[]{:S(2)}) collective-permute-start(bf16[1024,128]{1,0:T(8,128)(2,1)S(1)} %slice.31), channel_id=1, source_target_pairs={{0,8},{4,12},{8,0},{12,4},{16,24},{20,28},{24,16},{28,20},{1,9},{5... | collective-permute-start | bytes 786440 | tf_op jit(solution)/shard_map/ppermute | solution.py:42
  28.1 3.0 %copy-start.1 = (bf16[8,64,2048]{2,1,0:T(8,128)(2,1)S(1)}, bf16[8,64,2048]{2,1,0:T(8,128)(2,1)}, u32[]{:S(2)}) copy-start(bf16[8,64,2048]{2,1,0:T(8,128)(2,1)} %copy-done) | copy-start | bytes 6291460
  33.0 3.6 %copy-start.11 = (s32[2]{0:T(128)S(1)}, s32[2]{0:T(128)}, u32[]{:S(2)}) copy-start(s32[2]{0:T(128)} %param.17) | copy-start | bytes 28
  33.0 14.9 %copy-start.10 = (s32[2]{0:T(128)S(1)}, s32[2]{0:T(128)}, u32[]{:S(2)}) copy-start(s32[2]{0:T(128)} %lengths_ref.3) | copy-start | bytes 28
  34.6 16.8 %collective-permute-start.9 = (bf16[2048,128]{1,0:T(8,128)(2,1)S(1)}, bf16[2048,128]{1,0:T(8,128)(2,1)S(1)}, u32[]{:S(2)}, u32[]{:S(2)}) collective-permute-start(bf16[2048,128]{1,0:T(8,128)(2,1)S(1)} %bitcast.25), channel_id=1, source_target_pairs={{0,8},{4,12},{8,0},{12,4},{16,24},{20,28},{24,16},{28,20},{1,9},{5... | collective-permute-start | bytes 1572872 | tf_op jit(solution)/shard_map/ppermute | solution.py:42
  35.2 16.9 %collective-permute-start.11 = (bf16[2048,128]{1,0:T(8,128)(2,1)S(1)}, bf16[2048,128]{1,0:T(8,128)(2,1)S(1)}, u32[]{:S(2)}, u32[]{:S(2)}) collective-permute-start(bf16[2048,128]{1,0:T(8,128)(2,1)S(1)} %bitcast.26), channel_id=1, source_target_pairs={{0,16},{4,20},{8,24},{12,28},{16,0},{20,4},{24,8},{28,12},{1,17},{... | collective-permute-start | bytes 1572872 | tf_op jit(solution)/shard_map/ppermute | solution.py:42
  36.7 11.3 %collective-permute-start.20 = (bf16[1024,128]{1,0:T(8,128)(2,1)S(1)}, bf16[1024,128]{1,0:T(8,128)(2,1)S(1)}, u32[]{:S(2)}, u32[]{:S(2)}) collective-permute-start(bf16[1024,128]{1,0:T(8,128)(2,1)S(1)} %collective-permute-done.18.refs_5_), channel_id=1, source_target_pairs={{0,4},{4,0},{8,12},{12,8},{16,20},{20,16},{24,28},{28,24},{1,5},{5... | collective-permute-start | bytes 786440 | tf_op jit(solution)/shard_map/ppermute | solution.py:42
  36.7 11.2 %collective-permute-start.21 = (bf16[1024,128]{1,0:T(8,128)(2,1)S(1)}, bf16[1024,128]{1,0:T(8,128)(2,1)S(1)}, u32[]{:S(2)}, u32[]{:S(2)}) collective-permute-start(bf16[1024,128]{1,0:T(8,128)(2,1)S(1)} %collective-permute-done.19.refs_6_), channel_id=1, source_target_pairs={{0,4},{4,0},{8,12},{12,8},{16,20},{20,16},{24,28},{28,24},{1,5},{5... | collective-permute-start | bytes 786440 | tf_op jit(solution)/shard_map/ppermute | solution.py:42
  37.3 1.3 %collective-permute-start.22 = (f32[10,128]{1,0:T(8,128)S(1)}, f32[10,128]{1,0:T(8,128)S(1)}, u32[]{:S(2)}, u32[]{:S(2)}) collective-permute-start(f32[10,128]{1,0:T(8,128)S(1)} %bitcast_add_fusion), channel_id=1, source_target_pairs={{0,4},{4,0},{8,12},{12,8},{16,20},{20,16},{24,28},{28,24},{1,5},{5... | collective-permute-start | bytes 15368 | tf_op jit(solution)/shard_map/ppermute | solution.py:42
  38.6 9.3 %collective-permute-start.23 = (f32[10,128]{1,0:T(8,128)S(1)}, f32[10,128]{1,0:T(8,128)S(1)}, u32[]{:S(2)}, u32[]{:S(2)}) collective-permute-start(f32[10,128]{1,0:T(8,128)S(1)} %add.55), channel_id=1, source_target_pairs={{0,8},{4,12},{8,0},{12,4},{16,24},{20,28},{24,16},{28,20},{1,9},{5... | collective-permute-start | bytes 15368 | tf_op jit(solution)/shard_map/ppermute | solution.py:42
  49.6 1.2 %collective-permute-start.24 = (f32[8,128]{1,0:T(8,128)S(1)}, f32[8,128]{1,0:T(8,128)S(1)}, u32[]{:S(2)}, u32[]{:S(2)}) collective-permute-start(f32[8,128]{1,0:T(8,128)S(1)} %get-tuple-element.31), channel_id=1, source_target_pairs={{0,4},{4,0},{8,12},{12,8},{16,20},{20,16},{24,28},{28,24},{1,5},{5... | collective-permute-start | bytes 12296 | tf_op jit(solution)/shard_map/ppermute | solution.py:42
  50.8 3.6 %collective-permute-start.25 = (f32[8,128]{1,0:T(8,128)S(1)}, f32[8,128]{1,0:T(8,128)S(1)}, u32[]{:S(2)}, u32[]{:S(2)}) collective-permute-start(f32[8,128]{1,0:T(8,128)S(1)} %max.6), channel_id=1, source_target_pairs={{0,8},{4,12},{8,0},{12,4},{16,24},{20,28},{24,16},{28,20},{1,9},{5... | collective-permute-start | bytes 12296 | tf_op jit(solution)/shard_map/ppermute | solution.py:42
  51.4 10.3 %collective-permute-start.17 = (bf16[2048,128]{1,0:T(8,128)(2,1)S(1)}, bf16[2048,128]{1,0:T(8,128)(2,1)S(1)}, u32[]{:S(2)}, u32[]{:S(2)}) collective-permute-start(bf16[2048,128]{1,0:T(8,128)(2,1)S(1)} %bitcast.27), channel_id=1, source_target_pairs={{0,4},{4,0},{8,12},{12,8},{16,20},{20,16},{24,28},{28,24},{1,5},{5... | collective-permute-start | bytes 1572872 | tf_op jit(solution)/shard_map/ppermute | solution.py:42
  51.4 8.8 %collective-permute-start.10 = (bf16[1024,128]{1,0:T(8,128)(2,1)S(1)}, bf16[1024,128]{1,0:T(8,128)(2,1)S(1)}, u32[]{:S(2)}, u32[]{:S(2)}) collective-permute-start(bf16[1024,128]{1,0:T(8,128)(2,1)S(1)} %slice.28), channel_id=1, source_target_pairs={{0,16},{4,20},{8,24},{12,28},{16,0},{20,4},{24,8},{28,12},{1,17},{... | collective-permute-start | bytes 786440 | tf_op jit(solution)/shard_map/ppermute | solution.py:42
  51.9 10.7 %collective-permute-start.15 = (bf16[2048,128]{1,0:T(8,128)(2,1)S(1)}, bf16[2048,128]{1,0:T(8,128)(2,1)S(1)}, u32[]{:S(2)}, u32[]{:S(2)}) collective-permute-start(bf16[2048,128]{1,0:T(8,128)(2,1)S(1)} %collective-permute-done.9.refs_5_), channel_id=1, source_target_pairs={{0,4},{4,0},{8,12},{12,8},{16,20},{20,16},{24,28},{28,24},{1,5},{5... | collective-permute-start | bytes 1572872 | tf_op jit(solution)/shard_map/ppermute | solution.py:42
  52.1 10.5 %collective-permute-start.16 = (bf16[2048,128]{1,0:T(8,128)(2,1)S(1)}, bf16[2048,128]{1,0:T(8,128)(2,1)S(1)}, u32[]{:S(2)}, u32[]{:S(2)}) collective-permute-start(bf16[2048,128]{1,0:T(8,128)(2,1)S(1)} %collective-permute-done.11.refs_6_), channel_id=1, source_target_pairs={{0,4},{4,0},{8,12},{12,8},{16,20},{20,16},{24,28},{28,24},{1,5},{5... | collective-permute-start | bytes 1572872 | tf_op jit(solution)/shard_map/ppermute | solution.py:42
  54.4 7.2 %collective-permute-start.12 = (bf16[1024,128]{1,0:T(8,128)(2,1)S(1)}, bf16[1024,128]{1,0:T(8,128)(2,1)S(1)}, u32[]{:S(2)}, u32[]{:S(2)}) collective-permute-start(bf16[1024,128]{1,0:T(8,128)(2,1)S(1)} %slice.29), channel_id=1, source_target_pairs={{0,8},{4,12},{8,0},{12,4},{16,24},{20,28},{24,16},{28,20},{1,9},{5... | collective-permute-start | bytes 786440 | tf_op jit(solution)/shard_map/ppermute | solution.py:42
  60.2 3.9 %collective-permute-start.13 = (bf16[1024,128]{1,0:T(8,128)(2,1)S(1)}, bf16[1024,128]{1,0:T(8,128)(2,1)S(1)}, u32[]{:S(2)}, u32[]{:S(2)}) collective-permute-start(bf16[1024,128]{1,0:T(8,128)(2,1)S(1)} %collective-permute-done.10.refs_5_), channel_id=1, source_target_pairs={{0,4},{4,0},{8,12},{12,8},{16,20},{20,16},{24,28},{28,24},{1,5},{5... | collective-permute-start | bytes 786440 | tf_op jit(solution)/shard_map/ppermute | solution.py:42
  61.7 2.4 %collective-permute-start.14 = (bf16[1024,128]{1,0:T(8,128)(2,1)S(1)}, bf16[1024,128]{1,0:T(8,128)(2,1)S(1)}, u32[]{:S(2)}, u32[]{:S(2)}) collective-permute-start(bf16[1024,128]{1,0:T(8,128)(2,1)S(1)} %collective-permute-done.12.refs_6_), channel_id=1, source_target_pairs={{0,4},{4,0},{8,12},{12,8},{16,20},{20,16},{24,28},{28,24},{1,5},{5... | collective-permute-start | bytes 786440 | tf_op jit(solution)/shard_map/ppermute | solution.py:42
  64.1 10.2 %copy-start.3 = (bf16[1,1024,2048]{2,1,0:T(8,128)(2,1)S(1)}, bf16[1,1024,2048]{2,1,0:T(8,128)(2,1)}, u32[]{:S(2)}) copy-start(bf16[1,1024,2048]{2,1,0:T(8,128)(2,1)} %param.15) | copy-start | bytes 12582916
  65.6 1.3 %collective-permute-start.26 = (f32[8,256]{1,0:T(8,128)S(1)}, f32[8,256]{1,0:T(8,128)S(1)}, u32[]{:S(2)}, u32[]{:S(2)}) collective-permute-start(f32[8,256]{1,0:T(8,128)S(1)} %weighted_values.1), channel_id=1, source_target_pairs={{0,4},{4,0},{8,12},{12,8},{16,20},{20,16},{24,28},{28,24},{1,5},{5... | collective-permute-start | bytes 24584 | tf_op jit(solution)/shard_map/ppermute | solution.py:42
  67.0 3.7 %collective-permute-start.27 = (f32[8,256]{1,0:T(8,128)S(1)}, f32[8,256]{1,0:T(8,128)S(1)}, u32[]{:S(2)}, u32[]{:S(2)}) collective-permute-start(f32[8,256]{1,0:T(8,128)S(1)} %add.57), channel_id=1, source_target_pairs={{0,8},{4,12},{8,0},{12,4},{16,24},{20,28},{24,16},{28,20},{1,9},{5... | collective-permute-start | bytes 24584 | tf_op jit(solution)/shard_map/ppermute | solution.py:42
  70.7 3.7 %collective-permute-start.28 = (f32[8,256]{1,0:T(8,128)S(1)}, f32[8,256]{1,0:T(8,128)S(1)}, u32[]{:S(2)}, u32[]{:S(2)}) collective-permute-start(f32[8,256]{1,0:T(8,128)S(1)} %add.58.mine_ref), channel_id=1, source_target_pairs={{0,16},{4,20},{8,24},{12,28},{16,0},{20,4},{24,8},{28,12},{1,17},{... | collective-permute-start | bytes 24584 | tf_op jit(solution)/shard_map/ppermute | solution.py:42
  75.0 3.8 %collective-permute-start.29 = (f32[2,2048]{1,0:T(2,128)S(1)}, f32[2,2048]{1,0:T(2,128)S(1)}, u32[]{:S(2)}, u32[]{:S(2)}) collective-permute-start(f32[2,2048]{1,0:T(2,128)S(1)} %output_products.1), channel_id=1, source_target_pairs={{0,1},{1,0},{2,3},{3,2},{4,5},{5,4},{6,7},{7,6},{8,9},{9,8},{10,11... | collective-permute-start | bytes 49160 | tf_op jit(solution)/shard_map/ppermute | solution.py:42
  78.7 4.7 %collective-permute-start.30 = (f32[2,2048]{1,0:T(2,128)S(1)}, f32[2,2048]{1,0:T(2,128)S(1)}, u32[]{:S(2)}, u32[]{:S(2)}) collective-permute-start(f32[2,2048]{1,0:T(2,128)S(1)} %add.59), channel_id=1, source_target_pairs={{0,2},{1,3},{2,0},{3,1},{4,6},{5,7},{6,4},{7,5},{8,10},{9,11},{10,... | collective-permute-start | bytes 49160 | tf_op jit(solution)/shard_map/ppermute | solution.py:42

commit v4 on v3

--- a/solution.py
+++ b/solution.py
@@ -12,7 +12,8 @@
 EPSILON = 1e-05
 FLOOR = -1e30
 LANES = 128
-NORM_ROWS = 64
+NORM_ROWS = 160
+GROUP_ROWS = 16
 VMEM_BYTES = 16 * 1024 * 1024
 CHEAP = pl.CostEstimate(flops=1000, bytes_accessed=1000, transcendentals=0)
 IN_VMEM = pl.BlockSpec(memory_space=pltpu.VMEM)
@@ -50,6 +51,23 @@
     return [1 << b for b in range(count.bit_length() - 1)]
 
 
+def others(bits):
+    found = [0]
+    for bit in bits:
+        found += [d | bit for d in found]
+    return sorted(found[1:], key=lambda d: (-bin(d).count("1"), -d))
+
+
+def combine(value, axis, bits, join):
+    if len(bits) > 2:
+        return combine(join(value, swap(value, axis, bits[0])), axis, bits[1:], join)
+    parts = {d: swap(value, axis, d) for d in others(bits)}
+    parts[0] = value
+    for bit in bits:
+        parts = {d: join(parts[d], parts[d | bit]) for d in sorted(parts) if not d & bit}
+    return parts[0]
+
+
 def tables(placed, head_size):
     half_size = head_size // 2
     frequency = jnp.exp(
@@ -76,61 +94,62 @@
     out_ref[...] = jnp.broadcast_to(total, out_ref.shape)
 
 
-def norm_kernel(first, x_ref, gain_ref, out_ref, sems):
+def norm_kernel(first, x_ref, gain_ref, out_ref, held_ref, sems):
     blocks, rows, width = out_ref.shape
-    step = 16
-    copies = []
-    for c in range(rows // step):
-        copies.append(
-            [
-                pltpu.make_async_copy(
-                    x_ref.at[pl.ds(first + c * step, step), pl.ds(b * width, width)],
-                    out_ref.at[b, pl.ds(c * step, step), :],
-                    sems.at[c, b],
-                )
-                for b in range(blocks)
-            ]
+    features = blocks * width
+    groups = rows // GROUP_ROWS
+    tiles = width // LANES
+
+    def copy(g):
+        return pltpu.make_async_copy(
+            x_ref.at[pl.ds(first + g * GROUP_ROWS, GROUP_ROWS), :], held_ref.at[g], sems.at[g]
         )
-        for copy in copies[-1]:
-            copy.start()
-    for c in range(rows // step):
-        part = pl.ds(c * step, step)
-        for copy in copies[c]:
-            copy.wait()
-
-        def add_squares(b, totals):
-            totals = list(totals)
-            for j in range(width // LANES):
-                values = out_ref[b, part, j * LANES : (j + 1) * LANES].astype(jnp.float32)
-                totals[j % 4] = totals[j % 4] + values * values
-            return tuple(totals)
-
-        zero = jnp.zeros((step, LANES), jnp.float32)
-        totals = lax.fori_loop(0, blocks, add_squares, (zero,) * 4)
+
+    def factor_of(g):
+        totals = [jnp.zeros((GROUP_ROWS, LANES), jnp.float32) for _ in range(4)]
+        for j in range(blocks * tiles):
+            values = held_ref[g, :, j * LANES : (j + 1) * LANES].astype(jnp.float32)
+            totals[j % 4] = totals[j % 4] + values * values
         total = (totals[0] + totals[1]) + (totals[2] + totals[3])
-        mean = jnp.sum(total, axis=-1, keepdims=True) / (blocks * width)
-        factor = jnp.broadcast_to(lax.rsqrt(mean + EPSILON), (step, LANES))
-
-        def scale(b, _):
-            for j in range(width // LANES):
+        mean = jnp.sum(total, axis=-1, keepdims=True) / features
+        return jnp.broadcast_to(lax.rsqrt(mean + EPSILON), (GROUP_ROWS, LANES))
+
+    def scale(g, factor):
+        part = pl.ds(pl.multiple_of(g * GROUP_ROWS, GROUP_ROWS), GROUP_ROWS)
+        for b in range(blocks):
+            for j in range(tiles):
                 lanes = slice(j * LANES, (j + 1) * LANES)
-                values = out_ref[b, part, lanes].astype(jnp.float32)
+                from_lane = b * width + j * LANES
+                values = held_ref[g, :, from_lane : from_lane + LANES].astype(jnp.float32)
                 out_ref[b, part, lanes] = (values * factor * gain_ref[b, :, lanes]).astype(
                     jnp.bfloat16
                 )
-            return 0
-
-        lax.fori_loop(0, blocks, scale, 0)
+
+    for g in range(groups):
+        copy(g).start()
+    copy(0).wait()
+
+    def step(g, factor):
+        copy(g + 1).wait()
+        following = factor_of(g + 1)
+        scale(g, factor)
+        return following
+
+    scale(groups - 1, lax.fori_loop(0, groups - 1, step, factor_of(0)))
 
 
 def normalise(hidden, gains, first):
     blocks, _, width = gains.shape
+    groups = NORM_ROWS // GROUP_ROWS
     return call(
         functools.partial(norm_kernel, first),
         "normalise",
         [IN_HBM, IN_VMEM],
         shape((blocks, NORM_ROWS, width), jnp.bfloat16),
-        [pltpu.SemaphoreType.DMA((NORM_ROWS // 16, blocks))],
+        [
+            pltpu.VMEM((groups, GROUP_ROWS, blocks * width), jnp.bfloat16),
+            pltpu.SemaphoreType.DMA((groups,)),
+        ],
     )(pltpu.with_memory_space_constraint(hidden, pltpu.HBM), gains)
 
 
@@ -254,14 +273,14 @@
     out_ref[...] = jnp.dot(both, weight_ref[...], preferred_element_type=jnp.float32)
 
 
-def gather_rounds(own):
+def gather_rounds(own, far):
     count = lax.axis_size("ctx")
     rows = own.shape[0]
-    bits = [1 << b for b in range(1, count.bit_length() - 1)]
+    bits = bits_below(count)[1:]
     rounds = [[(0, 0, own)]] + [[] for _ in bits]
     halves = {}
     for bit in bits:
-        block = swap(own, "ctx", bit)
+        block = swap(far, "ctx", bit)
         rounds[1].append((bit, 0, block))
         halves[bit] = (block[: rows // 2], block[rows // 2 :])
     for distance in sorted(range(2, count, 2), key=lambda d: bin(d).count("1")):
@@ -276,7 +295,22 @@
         )
         rounds[hops].append((distance, 0, halves[distance][0]))
         rounds[hops].append((distance, rows // 2, halves[distance][1]))
-    return [r + [(d ^ 1, first, swap(block, "ctx", 1)) for d, first, block in r] for r in rounds]
+    return rounds
+
+
+def shared(blocks, *before):
+    passed = [
+        (d ^ 1, first, swap(after(block, *before) if before else block, "ctx", 1))
+        for d, first, block in blocks
+    ]
+    return blocks + passed
+
+
+def project_all(place, rows, rounds):
+    total = None
+    for blocks in rounds[:-1]:
+        total = project(place, rows, shared(blocks), total)
+    return total, shared(rounds[-1], total)
 
 
 def shards(
@@ -303,45 +337,46 @@
     assert requests == 2 and slot_count % row_count == 0 and row_count % NORM_ROWS == 0
     assert head_size == LANES
     gains = norm_gain.reshape(ctx_count, 1, width)
-    steps = row_count // NORM_ROWS
-
-    key_rounds = gather_rounds(key_weight[0])
-
-    rows = []
-
-    def normalise_beside(sent, received):
-        if len(rows) == steps:
-            return received
-        rows.append(normalise(after(ctx_hidden[0], sent), gains, len(rows) * NORM_ROWS))
-        return after(received, rows[-1])
-
+
+    key_rounds = gather_rounds(key_weight[0], key_weight[0])
+
+    chip_bits = bits_below(ctx_count)[1:]
+    first_hop = [block for _, _, block in key_rounds[1]]
     squares = call(squares_kernel, "squares", [IN_VMEM], shape((requests, LANES)))(new_tokens)
-    for distance in bits_below(ctx_count):
-        received = normalise_beside(squares, swap(squares, "ctx", distance))
-        squares = squares + received
+    squares = combine(squares, "ctx", [1], jnp.add)
+    rows = [
+        normalise(after(ctx_hidden[0], squares), gains, first)
+        for first in range(0, row_count, NORM_ROWS)
+    ]
+    squares = combine(squares, "ctx", chip_bits, jnp.add)
+    squares = after(squares, *rows, *first_hop)
     parts = call(
         functools.partial(query_kernel, features),
         "query_products",
         [IN_SMEM] + [IN_VMEM] * 6,
         shape((requests, heads + 2, head_size)),
     )(places, squares, new_tokens, gains, query_weight[0], key_weight[0], value_weight[0])
+    parts = combine(parts, "ctx", [1], jnp.add)
     request = place // team
     own_part = jnp.where(request == 0, parts[0], parts[1])
-    sent = jnp.where(request == 0, parts[1], parts[0])
-    summed = own_part + normalise_beside(sent, swap(sent, "ctx", team))
-    for distance in bits_below(team):
-        received = normalise_beside(summed, swap(summed, "ctx", distance))
-        summed = summed + received
-    while len(rows) < steps:
-        normalise_beside(summed, summed)
+    other_part = jnp.where(request == 0, parts[1], parts[0])
+    if len(chip_bits) > 2:
+        summed = combine(own_part + swap(other_part, "ctx", team), "ctx", chip_bits[:-1], jnp.add)
+    else:
+        received = {
+            d: swap(other_part if d & team else own_part, "ctx", d) for d in others(chip_bits)
+        }
+        received[0] = own_part
+        for bit in chip_bits:
+            received = {
+                d: received[d] + received[d | bit] for d in sorted(received) if not d & bit
+            }
+        summed = received[0]
 
     within = (place % team) * row_count + jnp.arange(row_count, dtype=jnp.int32)
     cosine, sine_part = tables(within.astype(jnp.float32), head_size)
     new_cosine, new_sine = tables(positions.astype(jnp.float32), head_size)
-    key_total = None
-    for blocks in key_rounds[:-1]:
-        key_total = project(places, rows, blocks, key_total)
-    blocks = key_rounds[-1]
+    key_total, blocks = project_all(places, rows, key_rounds)
     masked, top, self_scores = call(
         functools.partial(
             score_kernel, [(d, first) for d, first, _ in blocks], len(rows), team
@@ -361,14 +396,11 @@
         new_sine,
         summed,
     )
-    for distance in bits_below(team):
-        top = jnp.maximum(top, swap(top, "ctx", distance))
-
-    value_rounds = gather_rounds(after(value_weight[0], key_total))
-    value_total = None
-    for blocks in value_rounds[:-1]:
-        value_total = project(places, rows, blocks, value_total)
-    blocks = value_rounds[-1]
+    top = combine(top, "ctx", [1], jnp.maximum)
+    top = combine(top, "ctx", bits_below(team)[1:], jnp.maximum)
+
+    value_rounds = gather_rounds(value_weight[0], after(value_weight[0], parts))
+    value_total, blocks = project_all(places, rows, value_rounds)
     packed = call(
         functools.partial(
             weigh_kernel, [(d, first) for d, first, _ in blocks], len(rows), team
@@ -387,18 +419,25 @@
         self_scores,
         summed,
     )
-    for distance in bits_below(team):
-        packed = packed + swap(packed, "ctx", distance)
-    other = swap(packed, "ctx", team)
+    packed = combine(packed, "ctx", [1], jnp.add)
+    if len(chip_bits) > 2:
+        packed = combine(packed, "ctx", chip_bits[:-1], jnp.add)
+        other = swap(packed, "ctx", team)
+    else:
+        received = {d: swap(packed, "ctx", d) for d in others(chip_bits)}
+        received[0] = packed
+        for bit in chip_bits[:-1]:
+            received = {
+                d: received[d] + received[d | bit] for d in sorted(received) if not d & bit
+            }
+        packed, other = received[0], received[team]
     update = call(
         functools.partial(output_kernel, team),
         "output_products",
         [IN_SMEM] + [IN_VMEM] * 3,
         shape((requests, out_weight.shape[2])),
     )(places, packed, other, out_weight[0])
-    for distance in bits_below(kv_count):
-        update = update + swap(update, "kv", distance)
-    return new_tokens + update
+    return new_tokens + combine(update, "kv", bits_below(kv_count), jnp.add)
 
 
 def solution(mesh):

time: 84.5 us -> 97.2 us (1.15)
  local copies, waits for them, and re-layouts: 3.12 us -> 12.8 us
  starting transfers between devices: 23.3 us -> 28.5 us
  Pallas kernels: 25.1 us -> 21.8 us
    unnamed x24 -> x32, local copies, waits for them, and re-layouts: 3.05 us -> 11.3 us
    pallas_call x5 -> x2, Pallas kernels: 14.5 us -> 7.4 us  [normalise(): call(functools.partial(norm_kernel, first), 'normalise', [IN_HBM, IN_VMEM...]
    ppermute x31 -> x35, starting transfers between devices: 23.3 us -> 28.5 us  [swap(): return lax.ppermute(value, axis, [(i, i ^ distance) for i in range(count)])]
    pallas_call x4, Pallas kernels: 5.79 us -> 9.22 us  [project(): call(functools.partial(project_kernel, pieces, len(rows), total is not No...]
    slice x4, local copies, waits for them, and re-layouts: 0.07 us -> 1.51 us  [gather_rounds(): halves[bit] = (block[:rows // 2], block[rows // 2:])]
    ppermute x31 -> x35, waiting for transfers between devices: 30.5 us -> 30.9 us  [swap(): return lax.ppermute(value, axis, [(i, i ^ distance) for i in range(count)])]
  transfers between devices with their start and end apart: 31 -> 35, of which waited for: 13 -> 13; matrix products, arithmetic and copies ran while one was open for 1% -> 3% of each run, Pallas kernels for 27% -> 20%
where the time goes in v4:
time: 97.2 us; the launch traced here: 96.8 us
  waiting for transfers between devices  30.9 us (32%)
  starting transfers between devices  28.5 us (29%)
  Pallas kernels  21.8 us (22%)
  local copies, waits for them, and re-layouts  12.8 us (13%)
  other arithmetic  2.47 us (3%)
    ppermute x35, waiting for transfers between devices, swap(): return lax.ppermute(value, axis, [(i, i ^ distance) for i in range(count)])  30.9 us
    ppermute x35, starting transfers between devices, swap(): return lax.ppermute(value, axis, [(i, i ^ distance) for i in range(count)])  28.5 us
    unnamed x32, local copies, waits for them, and re-layouts  11.3 us
    pallas_call x4, Pallas kernels, project(): call(functools.partial(project_kernel, pieces, len(rows), total is not No...  9.22 us
    pallas_call x2, Pallas kernels, normalise(): call(functools.partial(norm_kernel, first), 'normalise', [IN_HBM, IN_VMEM...  7.4 us
    pallas_call x1, Pallas kernels, shards(): call(functools.partial(score_kernel, [(d, first) for d, first, _ in block...  2.11 us
  transfers between devices with their start and end apart: 35, of which 13 were waited for; matrix products, arithmetic and copies ran while one was open for 3% of the time, Pallas kernels for 20%

profile of v4, /device:TPU:0, one launch (start us, length us, event | category | flops | bytes accessed | tf_op | source)
XLA Modules:
  0.0 96.8 jit_solution(17612933174073839450)
XLA Ops:
  0.0 2.9 %collective-permute-start.4 = (bf16[2048,128]{1,0:T(8,128)(2,1)}, bf16[2048,128]{1,0:T(8,128)(2,1)S(1)}, u32[]{:S(2)}, u32[]{:S(2)}) collective-permute-start(bf16[2048,128]{1,0:T(8,128)(2,1)} %bitcast.13), channel_id=1, source_target_pairs={{0,8},{4,12},{8,0},{12,4},{16,24},{20,28},{24,16},{28,20},{1,9},{5... | collective-permute-start | bytes 1572872 | tf_op jit(solution)/shard_map/ppermute | solution.py:43
  2.9 1.5 %collective-permute-start.5 = (bf16[2048,128]{1,0:T(8,128)(2,1)}, bf16[2048,128]{1,0:T(8,128)(2,1)S(1)}, u32[]{:S(2)}, u32[]{:S(2)}) collective-permute-start(bf16[2048,128]{1,0:T(8,128)(2,1)} %bitcast.14), channel_id=1, source_target_pairs={{0,16},{4,20},{8,24},{12,28},{16,0},{20,4},{24,8},{28,12},{1,17},{... | collective-permute-start | bytes 1572872 | tf_op jit(solution)/shard_map/ppermute | solution.py:43
  4.5 0.7 copy-done.9
  5.2 0.1 squares.1
  5.3 1.1 %collective-permute-done = f32[2,128]{1,0:T(2,128)S(1)} collective-permute-done((f32[2,128]{1,0:T(2,128)S(1)}, f32[2,128]{1,0:T(2,128)S(1)}, u32[]{:S(2)}, u32[]{:S(2)}) %collective-permute-start) | collective-permute-done | bytes 1056 | tf_op jit(solution)/shard_map/ppermute | solution.py:43
  6.4 0.5 collective-permute-start.1
  7.0 3.0 %collective-permute-start.3 = (f32[2,128]{1,0:T(2,128)S(1)}, f32[2,128]{1,0:T(2,128)S(1)}, u32[]{:S(2)}, u32[]{:S(2)}) collective-permute-start(f32[2,128]{1,0:T(2,128)S(1)} %add.60), channel_id=1, source_target_pairs={{0,24},{4,28},{8,16},{12,20},{16,8},{20,12},{24,0},{28,4},{1,25},{... | collective-permute-start | bytes 3080 | tf_op jit(solution)/shard_map/ppermute | solution.py:43
  9.9 0.8 copy-done.8
  10.7 3.6 %normalise.2.refs_0_ = bf16[8,160,2048]{2,1,0:T(8,128)(2,1)S(1)} custom-call(bf16[320,16384]{1,0:T(8,128)(2,1)} %bitcast.26, f32[8,1,2048]{2,1,0:T(1,128)S(1)} %bitcast.23), custom_call_target="tpu_custom_call" | custom-call | flops 1000 | bytes 1000 | tf_op jit(solution)/shard_map/normalise/pallas_call | solution.py:144
  14.4 2.3 %copy-done = bf16[8,160,2048]{2,1,0:T(8,128)(2,1)} copy-done((bf16[8,160,2048]{2,1,0:T(8,128)(2,1)}, bf16[8,160,2048]{2,1,0:T(8,128)(2,1)S(1)}, u32[]{:S(2)}) %copy-start) | copy-done | bytes 5242904
  16.7 3.8 %normalise.3.refs_1_ = bf16[8,160,2048]{2,1,0:T(8,128)(2,1)S(1)} custom-call(bf16[320,16384]{1,0:T(8,128)(2,1)} %bitcast.27, f32[8,1,2048]{2,1,0:T(1,128)S(1)} %bitcast.24), custom_call_target="tpu_custom_call" | custom-call | flops 1000 | bytes 1000 | tf_op jit(solution)/shard_map/normalise/pallas_call | solution.py:144
  20.5 2.4 %copy-done.2 = bf16[8,160,2048]{2,1,0:T(8,128)(2,1)} copy-done((bf16[8,160,2048]{2,1,0:T(8,128)(2,1)}, bf16[8,160,2048]{2,1,0:T(8,128)(2,1)S(1)}, u32[]{:S(2)}) %copy-start.2) | copy-done | bytes 5242904
  23.1 0.8 query_products.1
  23.9 0.5 collective-permute-start.6
  24.4 0.1 collective-permute-start.13
  24.5 0.8 collective-permute-done.6
  25.3 0.5 collective-permute-start.7
  25.8 0.7 slice.29
  26.6 2.0 %collective-permute-start.17 = (bf16[1024,128]{1,0:T(8,128)(2,1)}, bf16[1024,128]{1,0:T(8,128)(2,1)S(1)}, u32[]{:S(2)}, u32[]{:S(2)}) collective-permute-start(bf16[1024,128]{1,0:T(8,128)(2,1)} %slice.29), channel_id=1, source_target_pairs={{0,8},{4,12},{8,0},{12,4},{16,24},{20,28},{24,16},{28,20},{1,9},{5... | collective-permute-start | bytes 786440 | tf_op jit(solution)/shard_map/ppermute | solution.py:43
  28.6 0.7 slice.28
  29.3 1.5 %collective-permute-start.16 = (bf16[1024,128]{1,0:T(8,128)(2,1)}, bf16[1024,128]{1,0:T(8,128)(2,1)}, u32[]{:S(2)}, u32[]{:S(2)}) collective-permute-start(bf16[1024,128]{1,0:T(8,128)(2,1)} %slice.28), channel_id=1, source_target_pairs={{0,16},{4,20},{8,24},{12,28},{16,0},{20,4},{24,8},{28,12},{1,17},{... | collective-permute-start | bytes 786440 | tf_op jit(solution)/shard_map/ppermute | solution.py:43
  30.8 14.2 %collective-permute-done.17.refs_3_ = bf16[1024,128]{1,0:T(8,128)(2,1)S(1)} collective-permute-done((bf16[1024,128]{1,0:T(8,128)(2,1)}, bf16[1024,128]{1,0:T(8,128)(2,1)S(1)}, u32[]{:S(2)}, u32[]{:S(2)}) %collective-permute-start.17) | collective-permute-done | bytes 262176 | tf_op jit(solution)/shard_map/ppermute | solution.py:43
  45.1 0.5 collective-permute-start.11
  45.6 1.4 %fusion = (f32[320,64]{1,0:T(8,128)}, f32[320,64]{1,0:T(8,128)}, f32[320,64]{1,0:T(8,128)}) fusion(f32[64]{0:T(128)S(1)} %multiply_exponential_fusion, f32[320]{0:T(512)S(1)} %add_convert_fusion), kind=kLoop, calls=%fused_computation.4 | loop fusion | flops 40960 | bytes 247296 | tf_op jit(solution)/shard_map/neg | solution.py:81
  47.0 0.1 collective-permute-start.12
  47.1 0.1 fusion.1
  47.2 2.5 %copy-done.1 = bf16[8,160,2048]{2,1,0:T(8,128)(2,1)S(1)} copy-done((bf16[8,160,2048]{2,1,0:T(8,128)(2,1)S(1)}, bf16[8,160,2048]{2,1,0:T(8,128)(2,1)}, u32[]{:S(2)}) %copy-start.1) | copy-done | bytes 5242904
  49.7 2.5 %copy-done.3 = bf16[8,160,2048]{2,1,0:T(8,128)(2,1)S(1)} copy-done((bf16[8,160,2048]{2,1,0:T(8,128)(2,1)S(1)}, bf16[8,160,2048]{2,1,0:T(8,128)(2,1)}, u32[]{:S(2)}) %copy-start.3) | copy-done | bytes 5242904
  52.2 1.9 %project.6.refs_6_ = f32[320,128]{1,0:T(8,128)S(1)} custom-call(s32[1]{0:T(128)} %bitcast.place_ref, bf16[8,160,2048]{2,1,0:T(8,128)(2,1)S(1)} %copy-done.1, bf16[8,160,2048]{2,1,0:T(8,128)(2,1)S(1)} %copy-done.3, bf16[2048,128]{1,0:T(8,128)(2,1)S(1)} %bitcast.17, bf16[2048,128]{1,0:T(8,128)(2,1)} %collective-permute-done.20.refs_3_), custom_call_target="tpu_custom_call" | custom-call | flops 1000 | bytes 1000 | tf_op jit(solution)/shard_map/project/pallas_call | solution.py:192
  54.2 0.6 collective-permute-start.10
  54.8 0.3 collective-permute-start.8
  55.1 1.7 %collective-permute-start.23 = (f32[10,128]{1,0:T(8,128)S(1)}, f32[10,128]{1,0:T(8,128)S(1)}, u32[]{:S(2)}, u32[]{:S(2)}) collective-permute-start(f32[10,128]{1,0:T(8,128)S(1)} %get-tuple-element.25), channel_id=1, source_target_pairs={{0,8},{4,12},{8,0},{12,4},{16,24},{20,28},{24,16},{28,20},{1,9},{5... | collective-permute-start | bytes 15368 | tf_op jit(solution)/shard_map/ppermute | solution.py:43
  56.8 1.5 %collective-permute-start.24 = (f32[10,128]{1,0:T(8,128)S(1)}, f32[10,128]{1,0:T(8,128)S(1)}, u32[]{:S(2)}, u32[]{:S(2)}) collective-permute-start(f32[10,128]{1,0:T(8,128)S(1)} %get-tuple-element.26), channel_id=1, source_target_pairs={{0,16},{4,20},{8,24},{12,28},{16,0},{20,4},{24,8},{28,12},{1,17},{... | collective-permute-start | bytes 15368 | tf_op jit(solution)/shard_map/ppermute | solution.py:43
  58.4 0.2 pad_maximum_fusion
  58.5 1.9 %project.4.refs_6_ = f32[320,128]{1,0:T(8,128)S(1)} custom-call(s32[1]{0:T(128)} %bitcast.place_ref, bf16[8,160,2048]{2,1,0:T(8,128)(2,1)S(1)} %copy-done.1, bf16[8,160,2048]{2,1,0:T(8,128)(2,1)S(1)} %copy-done.3, bf16[2048,128]{1,0:T(8,128)(2,1)S(1)} %bitcast.22, bf16[2048,128]{1,0:T(8,128)(2,1)} %collective-permute-done.13.refs_3_), custom_call_target="tpu_custom_call" | custom-call | flops 1000 | bytes 1000 | tf_op jit(solution)/shard_map/project/pallas_call | solution.py:192
  60.4 2.7 %project.7.refs_6_ = f32[320,128]{1,0:T(8,128)S(1)} custom-call(s32[1]{0:T(128)} %bitcast.place_ref, bf16[8,160,2048]{2,1,0:T(8,128)(2,1)S(1)} %copy-done.1, bf16[8,160,2048]{2,1,0:T(8,128)(2,1)S(1)} %copy-done.3, bf16[2048,128]{1,0:T(8,128)(2,1)S(1)} %collective-permute-done.4.refs_2_, bf16[2048,128]{1,0:T(8,128)(2,1)S(1)} %collective-permute-done.5.refs_3_, ...), custom_call_target="tpu_custom_call" | custom-call | flops 1000 | bytes 1000 | tf_op jit(solution)/shard_map/project/pallas_call | solution.py:192
  63.1 0.3 collective-permute-start.25
  63.4 2.7 %project.5.refs_6_ = f32[320,128]{1,0:T(8,128)S(1)} custom-call(s32[1]{0:T(128)} %bitcast.place_ref, bf16[8,160,2048]{2,1,0:T(8,128)(2,1)S(1)} %copy-done.1, bf16[8,160,2048]{2,1,0:T(8,128)(2,1)S(1)} %copy-done.3, bf16[2048,128]{1,0:T(8,128)(2,1)S(1)} %collective-permute-done.7.refs_2_, bf16[2048,128]{1,0:T(8,128)(2,1)S(1)} %collective-permute-done.9.refs_3_, ...), custom_call_target="tpu_custom_call" | custom-call | flops 1000 | bytes 1000 | tf_op jit(solution)/shard_map/project/pallas_call | solution.py:192
  66.2 0.5 collective-permute-start.21
  66.7 0.1 collective-permute-start.15
  66.8 0.4 collective-permute-start.14
  67.3 0.1 pad_maximum_fusion.2
  67.3 0.4 collective-permute-done.25
  67.8 0.6 collective-permute-done.21.refs_4_
  68.3 2.1 %scores.1 = (f32[8,320]{1,0:T(8,128)S(1)}, f32[8,128]{1,0:T(8,128)S(1)}, f32[8,128]{1,0:T(8,128)S(1)}) custom-call(s32[1]{0:T(128)} %bitcast.place_ref, s32[2]{0:T(128)S(1)} %copy-done.11, bf16[8,160,2048]{2,1,0:T(8,128)(2,1)S(1)} %copy-done.1, bf16[8,160,2048]{2,1,0:T(8,128)(2,1)S(1)} %copy-done.3, bf16[1024,128]{1,0:T(8,128)(2,1)} %collective-permute-done.16.refs_2_, ...), custom_call_target="tpu_custom_call" | custom-call | flops 1000 | bytes 1000 | tf_op jit(solution)/shard_map/scores/pallas_call | solution.py:380
  70.5 0.2 collective-permute-start.26
  70.6 1.0 %collective-permute-done.26 = f32[8,128]{1,0:T(8,128)S(1)} collective-permute-done((f32[8,128]{1,0:T(8,128)S(1)}, f32[8,128]{1,0:T(8,128)S(1)}, u32[]{:S(2)}, u32[]{:S(2)}) %collective-permute-start.26) | collective-permute-done | bytes 4128 | tf_op jit(solution)/shard_map/ppermute | solution.py:43
  71.6 1.7 %collective-permute-start.27 = (f32[8,128]{1,0:T(8,128)S(1)}, f32[8,128]{1,0:T(8,128)S(1)}, u32[]{:S(2)}, u32[]{:S(2)}) collective-permute-start(f32[8,128]{1,0:T(8,128)S(1)} %max.6), channel_id=1, source_target_pairs={{0,8},{4,12},{8,0},{12,4},{16,24},{20,28},{24,16},{28,20},{1,9},{5... | collective-permute-start | bytes 12296 | tf_op jit(solution)/shard_map/ppermute | solution.py:43
  73.4 1.9 %collective-permute-done.27 = f32[8,128]{1,0:T(8,128)S(1)} collective-permute-done((f32[8,128]{1,0:T(8,128)S(1)}, f32[8,128]{1,0:T(8,128)S(1)}, u32[]{:S(2)}, u32[]{:S(2)}) %collective-permute-start.27) | collective-permute-done | bytes 4128 | tf_op jit(solution)/shard_map/ppermute | solution.py:43
  75.3 1.5 %weighted_values.1 = f32[8,256]{1,0:T(8,128)S(1)} custom-call(s32[1]{0:T(128)} %bitcast.place_ref, s32[2]{0:T(128)S(1)} %copy-done.11, bf16[8,160,2048]{2,1,0:T(8,128)(2,1)S(1)} %copy-done.1, bf16[8,160,2048]{2,1,0:T(8,128)(2,1)S(1)} %copy-done.3, bf16[1024,128]{1,0:T(8,128)(2,1)S(1)} %collective-permute-done.8.refs_2_, ...), custom_call_target="tpu_custom_call" | custom-call | flops 1000 | bytes 1000 | tf_op jit(solution)/shard_map/weighted_values/pallas_call | solution.py:404
  76.8 1.2 %collective-permute-done.28 = f32[8,256]{1,0:T(8,128)S(1)} collective-permute-done((f32[8,256]{1,0:T(8,128)S(1)}, f32[8,256]{1,0:T(8,128)S(1)}, u32[]{:S(2)}, u32[]{:S(2)}) %collective-permute-start.28) | collective-permute-done | bytes 8224 | tf_op jit(solution)/shard_map/ppermute | solution.py:43
  78.0 1.7 %collective-permute-start.29 = (f32[8,256]{1,0:T(8,128)S(1)}, f32[8,256]{1,0:T(8,128)S(1)}, u32[]{:S(2)}, u32[]{:S(2)}) collective-permute-start(f32[8,256]{1,0:T(8,128)S(1)} %add.71), channel_id=1, source_target_pairs={{0,8},{4,12},{8,0},{12,4},{16,24},{20,28},{24,16},{28,20},{1,9},{5... | collective-permute-start | bytes 24584 | tf_op jit(solution)/shard_map/ppermute | solution.py:43
  79.7 1.5 %collective-permute-start.30 = (f32[8,256]{1,0:T(8,128)S(1)}, f32[8,256]{1,0:T(8,128)S(1)}, u32[]{:S(2)}, u32[]{:S(2)}) collective-permute-start(f32[8,256]{1,0:T(8,128)S(1)} %add.71), channel_id=1, source_target_pairs={{0,16},{4,20},{8,24},{12,28},{16,0},{20,4},{24,8},{28,12},{1,17},{... | collective-permute-start | bytes 24584 | tf_op jit(solution)/shard_map/ppermute | solution.py:43
  81.3 0.2 collective-permute-start.31
  81.5 0.2 collective-permute-done.29
  81.7 1.7 %collective-permute-done.30 = f32[8,256]{1,0:T(8,128)S(1)} collective-permute-done((f32[8,256]{1,0:T(8,128)S(1)}, f32[8,256]{1,0:T(8,128)S(1)}, u32[]{:S(2)}, u32[]{:S(2)}) %collective-permute-start.30) | collective-permute-done | bytes 8224 | tf_op jit(solution)/shard_map/ppermute | solution.py:43
  83.4 2.4 %collective-permute-done.31 = f32[8,256]{1,0:T(8,128)S(1)} collective-permute-done((f32[8,256]{1,0:T(8,128)S(1)}, f32[8,256]{1,0:T(8,128)S(1)}, u32[]{:S(2)}, u32[]{:S(2)}) %collective-permute-start.31) | collective-permute-done | bytes 8224 | tf_op jit(solution)/shard_map/ppermute | solution.py:43
  85.8 0.6 output_products.1
  86.5 1.6 %collective-permute-start.32 = (f32[2,2048]{1,0:T(2,128)S(1)}, f32[2,2048]{1,0:T(2,128)S(1)}, u32[]{:S(2)}, u32[]{:S(2)}) collective-permute-start(f32[2,2048]{1,0:T(2,128)S(1)} %output_products.1), channel_id=1, source_target_pairs={{0,1},{1,0},{2,3},{3,2},{4,5},{5,4},{6,7},{7,6},{8,9},{9,8},{10,11... | collective-permute-start | bytes 49160 | tf_op jit(solution)/shard_map/ppermute | solution.py:43
  88.1 2.6 %collective-permute-start.33 = (f32[2,2048]{1,0:T(2,128)S(1)}, f32[2,2048]{1,0:T(2,128)S(1)}, u32[]{:S(2)}, u32[]{:S(2)}) collective-permute-start(f32[2,2048]{1,0:T(2,128)S(1)} %output_products.1), channel_id=1, source_target_pairs={{0,2},{1,3},{2,0},{3,1},{4,6},{5,7},{6,4},{7,5},{8,10},{9,11},{10,... | collective-permute-start | bytes 49160 | tf_op jit(solution)/shard_map/ppermute | solution.py:43
  90.6 0.2 collective-permute-start.34
  90.9 1.9 %collective-permute-done.33 = f32[2,2048]{1,0:T(2,128)S(1)} collective-permute-done((f32[2,2048]{1,0:T(2,128)S(1)}, f32[2,2048]{1,0:T(2,128)S(1)}, u32[]{:S(2)}, u32[]{:S(2)}) %collective-permute-start.33) | collective-permute-done | bytes 16416 | tf_op jit(solution)/shard_map/ppermute | solution.py:43
  92.8 3.4 %collective-permute-done.34 = f32[2,2048]{1,0:T(2,128)S(1)} collective-permute-done((f32[2,2048]{1,0:T(2,128)S(1)}, f32[2,2048]{1,0:T(2,128)S(1)}, u32[]{:S(2)}, u32[]{:S(2)}) %collective-permute-start.34) | collective-permute-done | bytes 16416 | tf_op jit(solution)/shard_map/ppermute | solution.py:43
  96.2 0.6 add_add_fusion
  (71 shorter events, 0.4 us)
Async XLA Ops:
  0.0 23.0 %collective-permute-start.4 = (bf16[2048,128]{1,0:T(8,128)(2,1)}, bf16[2048,128]{1,0:T(8,128)(2,1)S(1)}, u32[]{:S(2)}, u32[]{:S(2)}) collective-permute-start(bf16[2048,128]{1,0:T(8,128)(2,1)} %bitcast.13), channel_id=1, source_target_pairs={{0,8},{4,12},{8,0},{12,4},{16,24},{20,28},{24,16},{28,20},{1,9},{5... | collective-permute-start | bytes 1572872 | tf_op jit(solution)/shard_map/ppermute | solution.py:43
  2.9 20.1 %collective-permute-start.5 = (bf16[2048,128]{1,0:T(8,128)(2,1)}, bf16[2048,128]{1,0:T(8,128)(2,1)S(1)}, u32[]{:S(2)}, u32[]{:S(2)}) collective-permute-start(bf16[2048,128]{1,0:T(8,128)(2,1)} %bitcast.14), channel_id=1, source_target_pairs={{0,16},{4,20},{8,24},{12,28},{16,0},{20,4},{24,8},{28,12},{1,17},{... | collective-permute-start | bytes 1572872 | tf_op jit(solution)/shard_map/ppermute | solution.py:43
  4.5 0.7 copy-start.9
  5.3 1.1 %collective-permute-start = (f32[2,128]{1,0:T(2,128)S(1)}, f32[2,128]{1,0:T(2,128)S(1)}, u32[]{:S(2)}, u32[]{:S(2)}) collective-permute-start(f32[2,128]{1,0:T(2,128)S(1)} %squares.1), channel_id=1, source_target_pairs={{0,4},{4,0},{8,12},{12,8},{16,20},{20,16},{24,28},{28,24},{1,5},{5... | collective-permute-start | bytes 3080 | tf_op jit(solution)/shard_map/ppermute | solution.py:43
  6.4 16.5 %collective-permute-start.1 = (f32[2,128]{1,0:T(2,128)S(1)}, f32[2,128]{1,0:T(2,128)S(1)}, u32[]{:S(2)}, u32[]{:S(2)}) collective-permute-start(f32[2,128]{1,0:T(2,128)S(1)} %add.60), channel_id=1, source_target_pairs={{0,8},{4,12},{8,0},{12,4},{16,24},{20,28},{24,16},{28,20},{1,9},{5... | collective-permute-start | bytes 3080 | tf_op jit(solution)/shard_map/ppermute | solution.py:43
  7.0 16.0 %collective-permute-start.2 = (f32[2,128]{1,0:T(2,128)S(1)}, f32[2,128]{1,0:T(2,128)S(1)}, u32[]{:S(2)}, u32[]{:S(2)}) collective-permute-start(f32[2,128]{1,0:T(2,128)S(1)} %add.60), channel_id=1, source_target_pairs={{0,16},{4,20},{8,24},{12,28},{16,0},{20,4},{24,8},{28,12},{1,17},{... | collective-permute-start | bytes 3080 | tf_op jit(solution)/shard_map/ppermute | solution.py:43
  7.0 16.0 %collective-permute-start.3 = (f32[2,128]{1,0:T(2,128)S(1)}, f32[2,128]{1,0:T(2,128)S(1)}, u32[]{:S(2)}, u32[]{:S(2)}) collective-permute-start(f32[2,128]{1,0:T(2,128)S(1)} %add.60), channel_id=1, source_target_pairs={{0,24},{4,28},{8,16},{12,20},{16,8},{20,12},{24,0},{28,4},{1,25},{... | collective-permute-start | bytes 3080 | tf_op jit(solution)/shard_map/ppermute | solution.py:43
  9.9 0.8 copy-start.8
  14.4 2.3 %copy-start = (bf16[8,160,2048]{2,1,0:T(8,128)(2,1)}, bf16[8,160,2048]{2,1,0:T(8,128)(2,1)S(1)}, u32[]{:S(2)}) copy-start(bf16[8,160,2048]{2,1,0:T(8,128)(2,1)S(1)} %normalise.2.refs_0_) | copy-start | bytes 15728644
  16.7 6.2 %copy-start.6 = (bf16[1,2048,128]{2,1,0:T(8,128)(2,1)S(1)}, bf16[1,2048,128]{2,1,0:T(8,128)(2,1)}, u32[]{:S(2)}) copy-start(bf16[1,2048,128]{2,1,0:T(8,128)(2,1)} %param.13) | copy-start | bytes 1572868
  16.7 6.3 %copy-start.4 = (bf16[1,2048,1024]{2,1,0:T(8,128)(2,1)S(1)}, bf16[1,2048,1024]{2,1,0:T(8,128)(2,1)}, u32[]{:S(2)}) copy-start(bf16[1,2048,1024]{2,1,0:T(8,128)(2,1)} %param.12) | copy-start | bytes 12582916
  16.7 6.3 %copy-start.7 = (bf16[1,2048,128]{2,1,0:T(8,128)(2,1)S(1)}, bf16[1,2048,128]{2,1,0:T(8,128)(2,1)}, u32[]{:S(2)}) copy-start(bf16[1,2048,128]{2,1,0:T(8,128)(2,1)} %param.14) | copy-start | bytes 1572868
  16.7 6.3 %copy-start.10 = (f32[2,2048]{1,0:T(2,128)S(1)}, f32[2,2048]{1,0:T(2,128)}, u32[]{:S(2)}) copy-start(f32[2,2048]{1,0:T(2,128)} %tokens_ref.3) | copy-start | bytes 49156
  20.5 2.4 %copy-start.2 = (bf16[8,160,2048]{2,1,0:T(8,128)(2,1)}, bf16[8,160,2048]{2,1,0:T(8,128)(2,1)S(1)}, u32[]{:S(2)}) copy-start(bf16[8,160,2048]{2,1,0:T(8,128)(2,1)S(1)} %normalise.3.refs_1_) | copy-start | bytes 15728644
  22.9 24.1 %copy-start.15 = (s32[2]{0:T(128)S(1)}, s32[2]{0:T(128)}, u32[]{:S(2)}) copy-start(s32[2]{0:T(128)} %param.17) | copy-start | bytes 28
  22.9 5.6 %collective-permute-start.20 = (bf16[2048,128]{1,0:T(8,128)(2,1)S(1)}, bf16[2048,128]{1,0:T(8,128)(2,1)}, u32[]{:S(2)}, u32[]{:S(2)}) collective-permute-start(bf16[2048,128]{1,0:T(8,128)(2,1)S(1)} %bitcast.15), channel_id=1, source_target_pairs={{0,4},{4,0},{8,12},{12,8},{16,20},{20,16},{24,28},{28,24},{1,5},{5... | collective-permute-start | bytes 1572872 | tf_op jit(solution)/shard_map/ppermute | solution.py:43
  23.9 1.4 %collective-permute-start.6 = (f32[2,10,128]{2,1,0:T(8,128)S(1)}, f32[2,10,128]{2,1,0:T(8,128)S(1)}, u32[]{:S(2)}, u32[]{:S(2)}) collective-permute-start(f32[2,10,128]{2,1,0:T(8,128)S(1)} %query_products.1), channel_id=1, source_target_pairs={{0,4},{4,0},{8,12},{12,8},{16,20},{20,16},{24,28},{28,24},{1,5},{5... | collective-permute-start | bytes 30728 | tf_op jit(solution)/shard_map/ppermute | solution.py:43
  24.4 4.9 %collective-permute-start.13 = (bf16[2048,128]{1,0:T(8,128)(2,1)S(1)}, bf16[2048,128]{1,0:T(8,128)(2,1)}, u32[]{:S(2)}, u32[]{:S(2)}) collective-permute-start(bf16[2048,128]{1,0:T(8,128)(2,1)S(1)} %bitcast.19), channel_id=1, source_target_pairs={{0,4},{4,0},{8,12},{12,8},{16,20},{20,16},{24,28},{28,24},{1,5},{5... | collective-permute-start | bytes 1572872 | tf_op jit(solution)/shard_map/ppermute | solution.py:43
  25.3 19.8 %collective-permute-start.7 = (bf16[2048,128]{1,0:T(8,128)(2,1)S(1)}, bf16[2048,128]{1,0:T(8,128)(2,1)S(1)}, u32[]{:S(2)}, u32[]{:S(2)}) collective-permute-start(bf16[2048,128]{1,0:T(8,128)(2,1)S(1)} %bitcast.20), channel_id=1, source_target_pairs={{0,8},{4,12},{8,0},{12,4},{16,24},{20,28},{24,16},{28,20},{1,9},{5... | collective-permute-start | bytes 1572872 | tf_op jit(solution)/shard_map/ppermute | solution.py:43
  25.8 21.2 %collective-permute-start.9 = (bf16[2048,128]{1,0:T(8,128)(2,1)S(1)}, bf16[2048,128]{1,0:T(8,128)(2,1)S(1)}, u32[]{:S(2)}, u32[]{:S(2)}) collective-permute-start(bf16[2048,128]{1,0:T(8,128)(2,1)S(1)} %bitcast.21), channel_id=1, source_target_pairs={{0,16},{4,20},{8,24},{12,28},{16,0},{20,4},{24,8},{28,12},{1,17},{... | collective-permute-start | bytes 1572872 | tf_op jit(solution)/shard_map/ppermute | solution.py:43
  26.6 18.5 %collective-permute-start.17 = (bf16[1024,128]{1,0:T(8,128)(2,1)}, bf16[1024,128]{1,0:T(8,128)(2,1)S(1)}, u32[]{:S(2)}, u32[]{:S(2)}) collective-permute-start(bf16[1024,128]{1,0:T(8,128)(2,1)} %slice.29), channel_id=1, source_target_pairs={{0,8},{4,12},{8,0},{12,4},{16,24},{20,28},{24,16},{28,20},{1,9},{5... | collective-permute-start | bytes 786440 | tf_op jit(solution)/shard_map/ppermute | solution.py:43
  28.5 26.3 %collective-permute-start.18 = (bf16[2048,128]{1,0:T(8,128)(2,1)S(1)}, bf16[2048,128]{1,0:T(8,128)(2,1)}, u32[]{:S(2)}, u32[]{:S(2)}) collective-permute-start(bf16[2048,128]{1,0:T(8,128)(2,1)S(1)} %collective-permute-done.4.refs_2_), channel_id=1, source_target_pairs={{0,4},{4,0},{8,12},{12,8},{16,20},{20,16},{24,28},{28,24},{1,5},{5... | collective-permute-start | bytes 1572872 | tf_op jit(solution)/shard_map/ppermute | solution.py:43
  29.3 24.9 %collective-permute-start.16 = (bf16[1024,128]{1,0:T(8,128)(2,1)}, bf16[1024,128]{1,0:T(8,128)(2,1)}, u32[]{:S(2)}, u32[]{:S(2)}) collective-permute-start(bf16[1024,128]{1,0:T(8,128)(2,1)} %slice.28), channel_id=1, source_target_pairs={{0,16},{4,20},{8,24},{12,28},{16,0},{20,4},{24,8},{28,12},{1,17},{... | collective-permute-start | bytes 786440 | tf_op jit(solution)/shard_map/ppermute | solution.py:43
  45.1 10.0 %collective-permute-start.19 = (bf16[2048,128]{1,0:T(8,128)(2,1)S(1)}, bf16[2048,128]{1,0:T(8,128)(2,1)}, u32[]{:S(2)}, u32[]{:S(2)}) collective-permute-start(bf16[2048,128]{1,0:T(8,128)(2,1)S(1)} %collective-permute-done.5.refs_3_), channel_id=1, source_target_pairs={{0,4},{4,0},{8,12},{12,8},{16,20},{20,16},{24,28},{28,24},{1,5},{5... | collective-permute-start | bytes 1572872 | tf_op jit(solution)/shard_map/ppermute | solution.py:43
  45.1 11.8 %collective-permute-start.11 = (bf16[2048,128]{1,0:T(8,128)(2,1)S(1)}, bf16[2048,128]{1,0:T(8,128)(2,1)}, u32[]{:S(2)}, u32[]{:S(2)}) collective-permute-start(bf16[2048,128]{1,0:T(8,128)(2,1)S(1)} %collective-permute-done.7.refs_2_), channel_id=1, source_target_pairs={{0,4},{4,0},{8,12},{12,8},{16,20},{20,16},{24,28},{28,24},{1,5},{5... | collective-permute-start | bytes 1572872 | tf_op jit(solution)/shard_map/ppermute | solution.py:43
  47.0 16.1 %collective-permute-start.12 = (bf16[2048,128]{1,0:T(8,128)(2,1)S(1)}, bf16[2048,128]{1,0:T(8,128)(2,1)}, u32[]{:S(2)}, u32[]{:S(2)}) collective-permute-start(bf16[2048,128]{1,0:T(8,128)(2,1)S(1)} %collective-permute-done.9.refs_3_), channel_id=1, source_target_pairs={{0,4},{4,0},{8,12},{12,8},{16,20},{20,16},{24,28},{28,24},{1,5},{5... | collective-permute-start | bytes 1572872 | tf_op jit(solution)/shard_map/ppermute | solution.py:43
  47.2 2.5 %copy-start.1 = (bf16[8,160,2048]{2,1,0:T(8,128)(2,1)S(1)}, bf16[8,160,2048]{2,1,0:T(8,128)(2,1)}, u32[]{:S(2)}) copy-start(bf16[8,160,2048]{2,1,0:T(8,128)(2,1)} %copy-done) | copy-start | bytes 15728644
  49.7 2.5 %copy-start.3 = (bf16[8,160,2048]{2,1,0:T(8,128)(2,1)S(1)}, bf16[8,160,2048]{2,1,0:T(8,128)(2,1)}, u32[]{:S(2)}) copy-start(bf16[8,160,2048]{2,1,0:T(8,128)(2,1)} %copy-done.2) | copy-start | bytes 15728644
  52.2 6.1 %copy-start.12 = (f32[320,64]{1,0:T(8,128)S(1)}, f32[320,64]{1,0:T(8,128)}, u32[]{:S(2)}) copy-start(f32[320,64]{1,0:T(8,128)} %get-tuple-element.27) | copy-start | bytes 245764
  52.2 6.1 %copy-start.13 = (f32[320,64]{1,0:T(8,128)S(1)}, f32[320,64]{1,0:T(8,128)}, u32[]{:S(2)}) copy-start(f32[320,64]{1,0:T(8,128)} %get-tuple-element.28) | copy-start | bytes 245764
  52.2 6.1 %copy-start.14 = (f32[320,64]{1,0:T(8,128)S(1)}, f32[320,64]{1,0:T(8,128)}, u32[]{:S(2)}) copy-start(f32[320,64]{1,0:T(8,128)} %get-tuple-element.29) | copy-start | bytes 245764
  54.2 11.9 %collective-permute-start.10 = (bf16[1024,128]{1,0:T(8,128)(2,1)S(1)}, bf16[1024,128]{1,0:T(8,128)(2,1)S(1)}, u32[]{:S(2)}, u32[]{:S(2)}) collective-permute-start(bf16[1024,128]{1,0:T(8,128)(2,1)S(1)} %slice.27), channel_id=1, source_target_pairs={{0,8},{4,12},{8,0},{12,4},{16,24},{20,28},{24,16},{28,20},{1,9},{5... | collective-permute-start | bytes 786440 | tf_op jit(solution)/shard_map/ppermute | solution.py:43
  54.8 11.4 %collective-permute-start.8 = (bf16[1024,128]{1,0:T(8,128)(2,1)S(1)}, bf16[1024,128]{1,0:T(8,128)(2,1)S(1)}, u32[]{:S(2)}, u32[]{:S(2)}) collective-permute-start(bf16[1024,128]{1,0:T(8,128)(2,1)S(1)} %slice.26), channel_id=1, source_target_pairs={{0,16},{4,20},{8,24},{12,28},{16,0},{20,4},{24,8},{28,12},{1,17},{... | collective-permute-start | bytes 786440 | tf_op jit(solution)/shard_map/ppermute | solution.py:43
  55.1 11.7 %collective-permute-start.23 = (f32[10,128]{1,0:T(8,128)S(1)}, f32[10,128]{1,0:T(8,128)S(1)}, u32[]{:S(2)}, u32[]{:S(2)}) collective-permute-start(f32[10,128]{1,0:T(8,128)S(1)} %get-tuple-element.25), channel_id=1, source_target_pairs={{0,8},{4,12},{8,0},{12,4},{16,24},{20,28},{24,16},{28,20},{1,9},{5... | collective-permute-start | bytes 15368 | tf_op jit(solution)/shard_map/ppermute | solution.py:43
  56.8 10.0 %collective-permute-start.24 = (f32[10,128]{1,0:T(8,128)S(1)}, f32[10,128]{1,0:T(8,128)S(1)}, u32[]{:S(2)}, u32[]{:S(2)}) collective-permute-start(f32[10,128]{1,0:T(8,128)S(1)} %get-tuple-element.26), channel_id=1, source_target_pairs={{0,16},{4,20},{8,24},{12,28},{16,0},{20,4},{24,8},{28,12},{1,17},{... | collective-permute-start | bytes 15368 | tf_op jit(solution)/shard_map/ppermute | solution.py:43
  63.1 5.2 %copy-start.11 = (s32[2]{0:T(128)S(1)}, s32[2]{0:T(128)}, u32[]{:S(2)}) copy-start(s32[2]{0:T(128)} %lengths_ref.3) | copy-start | bytes 28
  63.1 4.6 %collective-permute-start.25 = (f32[10,128]{1,0:T(8,128)S(1)}, f32[10,128]{1,0:T(8,128)S(1)}, u32[]{:S(2)}, u32[]{:S(2)}) collective-permute-start(f32[10,128]{1,0:T(8,128)S(1)} %get-tuple-element.26), channel_id=1, source_target_pairs={{0,24},{4,28},{8,16},{12,20},{16,8},{20,12},{24,0},{28,4},{1,25},{... | collective-permute-start | bytes 15368 | tf_op jit(solution)/shard_map/ppermute | solution.py:43
  66.2 1.6 %collective-permute-start.22 = (bf16[1024,128]{1,0:T(8,128)(2,1)S(1)}, bf16[1024,128]{1,0:T(8,128)(2,1)S(1)}, u32[]{:S(2)}, u32[]{:S(2)}) collective-permute-start(bf16[1024,128]{1,0:T(8,128)(2,1)S(1)} %collective-permute-done.17.refs_3_), channel_id=1, source_target_pairs={{0,4},{4,0},{8,12},{12,8},{16,20},{20,16},{24,28},{28,24},{1,5},{5... | collective-permute-start | bytes 786440 | tf_op jit(solution)/shard_map/ppermute | solution.py:43
  66.2 2.1 %collective-permute-start.21 = (bf16[1024,128]{1,0:T(8,128)(2,1)}, bf16[1024,128]{1,0:T(8,128)(2,1)S(1)}, u32[]{:S(2)}, u32[]{:S(2)}) collective-permute-start(bf16[1024,128]{1,0:T(8,128)(2,1)} %collective-permute-done.16.refs_2_), channel_id=1, source_target_pairs={{0,4},{4,0},{8,12},{12,8},{16,20},{20,16},{24,28},{28,24},{1,5},{5... | collective-permute-start | bytes 786440 | tf_op jit(solution)/shard_map/ppermute | solution.py:43
  66.7 8.5 %collective-permute-start.15 = (bf16[1024,128]{1,0:T(8,128)(2,1)S(1)}, bf16[1024,128]{1,0:T(8,128)(2,1)S(1)}, u32[]{:S(2)}, u32[]{:S(2)}) collective-permute-start(bf16[1024,128]{1,0:T(8,128)(2,1)S(1)} %collective-permute-done.10.refs_3_), channel_id=1, source_target_pairs={{0,4},{4,0},{8,12},{12,8},{16,20},{20,16},{24,28},{28,24},{1,5},{5... | collective-permute-start | bytes 786440 | tf_op jit(solution)/shard_map/ppermute | solution.py:43
  66.8 8.4 %collective-permute-start.14 = (bf16[1024,128]{1,0:T(8,128)(2,1)S(1)}, bf16[1024,128]{1,0:T(8,128)(2,1)S(1)}, u32[]{:S(2)}, u32[]{:S(2)}) collective-permute-start(bf16[1024,128]{1,0:T(8,128)(2,1)S(1)} %collective-permute-done.8.refs_2_), channel_id=1, source_target_pairs={{0,4},{4,0},{8,12},{12,8},{16,20},{20,16},{24,28},{28,24},{1,5},{5... | collective-permute-start | bytes 786440 | tf_op jit(solution)/shard_map/ppermute | solution.py:43
  70.5 1.2 %collective-permute-start.26 = (f32[8,128]{1,0:T(8,128)S(1)}, f32[8,128]{1,0:T(8,128)S(1)}, u32[]{:S(2)}, u32[]{:S(2)}) collective-permute-start(f32[8,128]{1,0:T(8,128)S(1)} %get-tuple-element.23), channel_id=1, source_target_pairs={{0,4},{4,0},{8,12},{12,8},{16,20},{20,16},{24,28},{28,24},{1,5},{5... | collective-permute-start | bytes 12296 | tf_op jit(solution)/shard_map/ppermute | solution.py:43
  71.6 3.6 %collective-permute-start.27 = (f32[8,128]{1,0:T(8,128)S(1)}, f32[8,128]{1,0:T(8,128)S(1)}, u32[]{:S(2)}, u32[]{:S(2)}) collective-permute-start(f32[8,128]{1,0:T(8,128)S(1)} %max.6), channel_id=1, source_target_pairs={{0,8},{4,12},{8,0},{12,4},{16,24},{20,28},{24,16},{28,20},{1,9},{5... | collective-permute-start | bytes 12296 | tf_op jit(solution)/shard_map/ppermute | solution.py:43
  75.3 10.6 %copy-start.5 = (bf16[1,1024,2048]{2,1,0:T(8,128)(2,1)S(1)}, bf16[1,1024,2048]{2,1,0:T(8,128)(2,1)}, u32[]{:S(2)}) copy-start(bf16[1,1024,2048]{2,1,0:T(8,128)(2,1)} %param.15) | copy-start | bytes 12582916
  76.8 1.2 %collective-permute-start.28 = (f32[8,256]{1,0:T(8,128)S(1)}, f32[8,256]{1,0:T(8,128)S(1)}, u32[]{:S(2)}, u32[]{:S(2)}) collective-permute-start(f32[8,256]{1,0:T(8,128)S(1)} %weighted_values.1), channel_id=1, source_target_pairs={{0,4},{4,0},{8,12},{12,8},{16,20},{20,16},{24,28},{28,24},{1,5},{5... | collective-permute-start | bytes 24584 | tf_op jit(solution)/shard_map/ppermute | solution.py:43
  78.0 3.7 %collective-permute-start.29 = (f32[8,256]{1,0:T(8,128)S(1)}, f32[8,256]{1,0:T(8,128)S(1)}, u32[]{:S(2)}, u32[]{:S(2)}) collective-permute-start(f32[8,256]{1,0:T(8,128)S(1)} %add.71), channel_id=1, source_target_pairs={{0,8},{4,12},{8,0},{12,4},{16,24},{20,28},{24,16},{28,20},{1,9},{5... | collective-permute-start | bytes 24584 | tf_op jit(solution)/shard_map/ppermute | solution.py:43
  79.7 3.7 %collective-permute-start.30 = (f32[8,256]{1,0:T(8,128)S(1)}, f32[8,256]{1,0:T(8,128)S(1)}, u32[]{:S(2)}, u32[]{:S(2)}) collective-permute-start(f32[8,256]{1,0:T(8,128)S(1)} %add.71), channel_id=1, source_target_pairs={{0,16},{4,20},{8,24},{12,28},{16,0},{20,4},{24,8},{28,12},{1,17},{... | collective-permute-start | bytes 24584 | tf_op jit(solution)/shard_map/ppermute | solution.py:43
  81.3 4.5 %collective-permute-start.31 = (f32[8,256]{1,0:T(8,128)S(1)}, f32[8,256]{1,0:T(8,128)S(1)}, u32[]{:S(2)}, u32[]{:S(2)}) collective-permute-start(f32[8,256]{1,0:T(8,128)S(1)} %add.71), channel_id=1, source_target_pairs={{0,24},{4,28},{8,16},{12,20},{16,8},{20,12},{24,0},{28,4},{1,25},{... | collective-permute-start | bytes 24584 | tf_op jit(solution)/shard_map/ppermute | solution.py:43
  86.5 4.4 %collective-permute-start.32 = (f32[2,2048]{1,0:T(2,128)S(1)}, f32[2,2048]{1,0:T(2,128)S(1)}, u32[]{:S(2)}, u32[]{:S(2)}) collective-permute-start(f32[2,2048]{1,0:T(2,128)S(1)} %output_products.1), channel_id=1, source_target_pairs={{0,1},{1,0},{2,3},{3,2},{4,5},{5,4},{6,7},{7,6},{8,9},{9,8},{10,11... | collective-permute-start | bytes 49160 | tf_op jit(solution)/shard_map/ppermute | solution.py:43
  88.1 4.7 %collective-permute-start.33 = (f32[2,2048]{1,0:T(2,128)S(1)}, f32[2,2048]{1,0:T(2,128)S(1)}, u32[]{:S(2)}, u32[]{:S(2)}) collective-permute-start(f32[2,2048]{1,0:T(2,128)S(1)} %output_products.1), channel_id=1, source_target_pairs={{0,2},{1,3},{2,0},{3,1},{4,6},{5,7},{6,4},{7,5},{8,10},{9,11},{10,... | collective-permute-start | bytes 49160 | tf_op jit(solution)/shard_map/ppermute | solution.py:43
  90.6 5.5 %collective-permute-start.34 = (f32[2,2048]{1,0:T(2,128)S(1)}, f32[2,2048]{1,0:T(2,128)S(1)}, u32[]{:S(2)}, u32[]{:S(2)}) collective-permute-start(f32[2,2048]{1,0:T(2,128)S(1)} %output_products.1), channel_id=1, source_target_pairs={{0,3},{1,2},{2,1},{3,0},{4,7},{5,6},{6,5},{7,4},{8,11},{9,10},{10,... | collective-permute-start | bytes 49160 | tf_op jit(solution)/shard_map/ppermute | solution.py:43

commit v5 on v4

v5 whole, which is shorter than its diff:
```python
import functools
import math

import jax
import jax.numpy as jnp
from jax import lax
from jax.experimental import pallas as pl
from jax.experimental.pallas import tpu as pltpu
from jax.sharding import PartitionSpec as P

ROPE_BASE = 500000.0
EPSILON = 1e-05
FLOOR = -1e30
LANES = 128
NORM_ROWS = 64
GROUP_ROWS = 16
VMEM_BYTES = 16 * 1024 * 1024
CHEAP = pl.CostEstimate(flops=1000, bytes_accessed=1000, transcendentals=0)
IN_VMEM = pl.BlockSpec(memory_space=pltpu.VMEM)
IN_SMEM = pl.BlockSpec(memory_space=pltpu.SMEM)
IN_HBM = pl.BlockSpec(memory_space=pltpu.HBM)


def call(kernel, name, in_specs, out_shape, scratch_shapes=()):
    return pl.pallas_call(
        kernel,
        in_specs=in_specs,
        out_specs=jax.tree.map(lambda _: IN_VMEM, out_shape),
        out_shape=out_shape,
        scratch_shapes=scratch_shapes,
        compiler_params=pltpu.CompilerParams(vmem_limit_bytes=VMEM_BYTES),
        cost_estimate=CHEAP,
        name=name,
    )


def shape(dims, dtype=jnp.float32):
    return jax.ShapeDtypeStruct(dims, dtype)


def swap(value, axis, distance):
    count = lax.axis_size(axis)
    return lax.ppermute(value, axis, [(i, i ^ distance) for i in range(count)])


def after(value, *others):
    return lax.optimization_barrier((value, *others))[0]


def bits_below(count):
    return [1 << b for b in range(count.bit_length() - 1)]


def butterfly(value, axis, bits, join):
    for bit in bits:
        value = join(value, swap(value, axis, bit))
    return value


def by_core(value, bit_0, bit_1):
    count = lax.axis_size("ctx")
    bits = (bit_0, bit_1)
    pairs = [(i, i ^ bits[i % 2]) for i in range(count) if bits[i % 2]]
    return lax.ppermute(value, "ctx", pairs)


def on_core(core):
    return lax.axis_index("ctx") % 2 == core


def send_first(own, partner):
    count = lax.axis_size("ctx")
    if count != 8:
        return [((d, d), swap(own, "ctx", d)) for d in range(2, count // 2)]
    return [((2, 4), by_core(own, 2, 4)), ((3, 5), by_core(partner, 2, 4))]


def share(blocks, *before):
    count = lax.axis_size("ctx")
    if count != 8:
        return []
    return [
        ((odd ^ 1, even ^ 1), swap(after(block, *before) if before else block, "ctx", 1))
        for (even, odd), block in blocks
    ]


def send_last(own, received):
    count = lax.axis_size("ctx")
    if count != 8:
        return [((d, d), swap(own, "ctx", d)) for d in range(count // 2, count)]
    return [((7, 7), by_core(received[0][1], 2, 4))]


def tables(placed, head_size):
    half_size = head_size // 2
    frequency = jnp.exp(
        jnp.arange(half_size, dtype=jnp.float32) * (-2.0 * math.log(ROPE_BASE) / head_size)
    )
    angles = placed[..., None] * frequency
    cosine = jnp.cos(angles)
    sine_part = jnp.sin(angles)
    return (
        jnp.concatenate((cosine, cosine), axis=-1),
        jnp.concatenate((-sine_part, sine_part), axis=-1),
    )


def turn(values, cosine, signed_sine):
    half_size = values.shape[-1] // 2
    swapped = jnp.concatenate((values[:, half_size:], values[:, :half_size]), axis=-1)
    return values * cosine + swapped * signed_sine


def squares_kernel(tokens_ref, out_ref):
    values = tokens_ref[...]
    total = jnp.sum(values * values, axis=-1, keepdims=True)
    out_ref[...] = jnp.broadcast_to(total, out_ref.shape)


def norm_kernel(first, x_ref, gain_ref, *refs):
    out_refs, (held_ref, sems) = refs[:-2], refs[-2:]
    blocks, rows, width = out_refs[0].shape
    features = blocks * width
    groups = len(out_refs) * rows // GROUP_ROWS
    tiles = width // LANES

    def copy(g):
        return pltpu.make_async_copy(
            x_ref.at[pl.ds(first + g * GROUP_ROWS, GROUP_ROWS), :], held_ref.at[g], sems.at[g]
        )

    def factor_of(g):
        totals = [jnp.zeros((GROUP_ROWS, LANES), jnp.float32) for _ in range(4)]
        for j in range(blocks * tiles):
            values = held_ref[g, :, j * LANES : (j + 1) * LANES].astype(jnp.float32)
            totals[j % 4] = totals[j % 4] + values * values
        total = (totals[0] + totals[1]) + (totals[2] + totals[3])
        mean = jnp.sum(total, axis=-1, keepdims=True) / features
        return jnp.broadcast_to(lax.rsqrt(mean + EPSILON), (GROUP_ROWS, LANES))

    def scale(g, factor, out_ref, row):
        part = pl.ds(pl.multiple_of(row, GROUP_ROWS), GROUP_ROWS)
        for b in range(blocks):
            for j in range(tiles):
                lanes = slice(j * LANES, (j + 1) * LANES)
                from_lane = b * width + j * LANES
                values = held_ref[g, :, from_lane : from_lane + LANES].astype(jnp.float32)
                out_ref[b, part, lanes] = (values * factor * gain_ref[b, :, lanes]).astype(
                    jnp.bfloat16
                )

    for g in range(groups):
        copy(g).start()
    copy(0).wait()

    factor = factor_of(0)
    for i, out_ref in enumerate(out_refs):
        start = i * rows // GROUP_ROWS
        stop = min(start + rows // GROUP_ROWS, groups - 1)

        def step(g, factor, out_ref=out_ref, start=start):
            copy(g + 1).wait()
            following = factor_of(g + 1)
            scale(g, factor, out_ref, (g - start) * GROUP_ROWS)
            return following

        factor = lax.fori_loop(start, stop, step, factor)
    scale(groups - 1, factor, out_refs[-1], rows - GROUP_ROWS)


def normalise(hidden, gains, first, parts):
    blocks, _, width = gains.shape
    groups = parts * NORM_ROWS // GROUP_ROWS
    return call(
        functools.partial(norm_kernel, first),
        "normalise",
        [IN_HBM, IN_VMEM],
        (shape((blocks, NORM_ROWS, width), jnp.bfloat16),) * parts,
        [
            pltpu.VMEM((groups, GROUP_ROWS, blocks * width), jnp.bfloat16),
            pltpu.SemaphoreType.DMA((groups,)),
        ],
    )(pltpu.with_memory_space_constraint(hidden, pltpu.HBM), gains)


def query_kernel(
    features, place_ref, squares_ref, tokens_ref, gains_ref, query_ref, key_ref, value_ref, out_ref
):
    requests = tokens_ref.shape[0]
    factor = lax.rsqrt(squares_ref[:, :1] / features + EPSILON)
    normed = (tokens_ref[...] * factor * gains_ref[place_ref[0]]).astype(jnp.bfloat16)
    row = 0
    for weight_ref in (query_ref, key_ref, value_ref):
        part = jnp.dot(normed, weight_ref[...], preferred_element_type=jnp.float32)
        for h in range(weight_ref.shape[1] // LANES):
            for r in range(requests):
                out_ref[r, row : row + 1, :] = part[r : r + 1, h * LANES : (h + 1) * LANES]
            row += 1


def blocks_dot(distances, place, row_refs, block_refs, total):
    for (even, odd), block_ref in zip(distances, block_refs):
        distance = jnp.where(lax.rem(place, 2) == 0, even, odd)
        rows = jnp.concatenate([ref[place ^ distance] for ref in row_refs], axis=0)
        part = jnp.dot(rows, block_ref[...], preferred_element_type=jnp.float32)
        total = part if total is None else total + part
    return total


def project_kernel(distances, row_count, has_total, place_ref, *refs):
    rows, refs = refs[:row_count], refs[row_count:]
    total = refs[len(distances)][...] if has_total else None
    refs[-1][...] = blocks_dot(distances, place_ref[0], rows, refs, total)


def project(place, rows, blocks, total=None):
    extra = [] if total is None else [total]
    row_count = sum(r.shape[1] for r in rows)
    return call(
        functools.partial(project_kernel, [d for d, _ in blocks], len(rows), total is not None),
        "project",
        [IN_SMEM] + [IN_VMEM] * (len(rows) + len(blocks) + len(extra)),
        shape((row_count, LANES)),
    )(place, *rows, *[block for _, block in blocks], *extra)


def live_rows(dims, team, place, lengths_ref):
    rows = dims[1]
    within = lax.rem(place, team) * rows + lax.broadcasted_iota(jnp.int32, dims, 1)
    return within < lengths_ref[lax.div(place, team)]


def score_kernel(team, place_ref, lengths_ref, *refs):
    keys_ref, cos_ref, sin_ref, new_cos_ref, new_sin_ref, summed_ref = refs[:6]
    masked_ref, top_ref, self_ref = refs[6:]
    place = place_ref[0]
    request = lax.div(place, team)
    heads = masked_ref.shape[0]
    scale = 1.0 / math.sqrt(LANES)
    turned = turn(
        summed_ref[...], new_cos_ref[pl.ds(request, 1), :], new_sin_ref[pl.ds(request, 1), :]
    ).astype(jnp.bfloat16)
    queries = turned[:heads]
    self_key = turned[heads : heads + 1].astype(jnp.float32)
    self_scores = (
        jnp.sum(queries.astype(jnp.float32) * self_key, axis=-1, keepdims=True) * scale
    )
    keys = turn(keys_ref[...], cos_ref[...], sin_ref[...]).astype(jnp.bfloat16)
    scores = (
        lax.dot_general(
            queries, keys, (((1,), (1,)), ((), ())), preferred_element_type=jnp.float32
        )
        * scale
    )
    masked = jnp.where(live_rows(scores.shape, team, place, lengths_ref), scores, FLOOR)
    masked_ref[...] = masked
    top = jnp.maximum(jnp.max(masked, axis=-1, keepdims=True), self_scores)
    top_ref[...] = jnp.broadcast_to(top, top_ref.shape)
    self_ref[...] = jnp.broadcast_to(self_scores, self_ref.shape)


def weigh_kernel(distances, row_count, team, place_ref, lengths_ref, *refs):
    rows, refs = refs[:row_count], refs[row_count:]
    blocks, refs = refs[: len(distances)], refs[len(distances) :]
    total_ref, masked_ref, top_ref, self_ref, summed_ref, out_ref = refs
    place = place_ref[0]
    heads = masked_ref.shape[0]
    masked = masked_ref[...]
    top = top_ref[:, :1]
    live = live_rows(masked.shape, team, place, lengths_ref)
    weights = jnp.where(live, jnp.exp(masked - top), 0.0).astype(jnp.bfloat16)
    self_weight = jnp.exp(self_ref[...] - top_ref[...]).astype(jnp.bfloat16).astype(jnp.float32)
    self_weight = jnp.where(lax.rem(place, team) == 0, self_weight, 0.0)
    self_value = summed_ref[heads + 1 : heads + 2, :].astype(jnp.bfloat16).astype(jnp.float32)
    mass = jnp.sum(weights.astype(jnp.float32), axis=-1, keepdims=True) + self_weight
    values = blocks_dot(distances, place, rows, blocks, total_ref[...]).astype(jnp.bfloat16)
    accum = jnp.dot(weights, values, preferred_element_type=jnp.float32)
    out_ref[:, :LANES] = accum + self_weight * self_value
    out_ref[:, LANES:] = mass


def output_kernel(team, place_ref, mine_ref, other_ref, weight_ref, out_ref):
    request = lax.div(place_ref[0], team)
    heads = mine_ref.shape[0]
    attended = []
    for ref in (mine_ref, other_ref):
        attended.append(ref[:, :LANES] / ref[:, LANES:])
    first = jnp.where(request == 0, attended[0], attended[1]).astype(jnp.bfloat16)
    second = jnp.where(request == 0, attended[1], attended[0]).astype(jnp.bfloat16)
    both = jnp.concatenate(
        [
            jnp.concatenate((first[h : h + 1], second[h : h + 1]), axis=0)
            for h in range(heads)
        ],
        axis=1,
    )
    out_ref[...] = jnp.dot(both, weight_ref[...], preferred_element_type=jnp.float32)


def shards(
    new_tokens,
    ctx_hidden,
    norm_gain,
    query_weight,
    key_weight,
    value_weight,
    out_weight,
    lengths,
    positions,
):
    ctx_count = lax.axis_size("ctx")
    kv_count = lax.axis_size("kv")
    place = lax.axis_index("ctx").astype(jnp.int32)
    places = place.reshape(1)
    row_count, features = ctx_hidden.shape[1:]
    head_size = key_weight.shape[2]
    heads = query_weight.shape[2] // head_size
    requests, width = new_tokens.shape
    slot_count = row_count * ctx_count // requests
    team = slot_count // row_count
    assert requests == 2 and slot_count % row_count == 0 and row_count % NORM_ROWS == 0
    assert head_size == LANES
    gains = norm_gain.reshape(ctx_count, 1, width)

    split = ctx_count == 8
    chip_bits = bits_below(ctx_count)[1:]
    rows = []

    def beside(received, sent):
        if len(rows) * NORM_ROWS == row_count:
            return received
        rows.extend(
            normalise(after(ctx_hidden[0], sent), gains, len(rows) * NORM_ROWS, 1)
        )
        return after(received, rows[-1])

    def over_x(value, join):
        value = join(value, beside(by_core(value, 0, 2), value))
        return jnp.where(on_core(0), beside(swap(value, "ctx", 1), value), value)

    def over_y(sent, value, join):
        value = join(value, beside(by_core(sent, 4, 0), sent))
        return jnp.where(on_core(1), beside(swap(value, "ctx", 1), value), value)

    key_partner = swap(key_weight[0], "ctx", 1)
    value_partner = swap(value_weight[0], "ctx", 1)
    key_near = [((0, 0), key_weight[0]), ((1, 1), key_partner)]
    value_near = [((0, 0), value_weight[0]), ((1, 1), value_partner)]
    key_far = send_first(key_weight[0], key_partner)

    squares = call(squares_kernel, "squares", [IN_VMEM], shape((requests, LANES)))(new_tokens)
    squares = squares + swap(squares, "ctx", 1)
    squares = after(squares, key_partner, value_partner)
    if split:
        squares = over_x(squares, jnp.add)
        key_shared = share(key_far, squares)
        squares = over_y(squares, squares, jnp.add)
        squares = after(squares, key_far[1][1])
    else:
        key_shared = share(key_far)
        squares = butterfly(squares, "ctx", chip_bits, jnp.add)
    key_last = send_last(key_weight[0], key_shared)
    own_values = after(value_weight[0], *[block for _, block in key_shared[:1]])
    value_far = send_first(own_values, value_partner)

    parts = call(
        functools.partial(query_kernel, features),
        "query_products",
        [IN_SMEM] + [IN_VMEM] * 6,
        shape((requests, heads + 2, head_size)),
    )(places, squares, new_tokens, gains, query_weight[0], key_weight[0], value_weight[0])
    parts = parts + beside(swap(parts, "ctx", 1), parts)
    request = place // team
    if split:
        parts = over_x(parts, jnp.add)
    own_part = jnp.where(request == 0, parts[0], parts[1])
    other_part = jnp.where(request == 0, parts[1], parts[0])
    if split:
        summed = over_y(other_part, own_part, jnp.add)
    else:
        summed = own_part + swap(other_part, "ctx", team)
        summed = butterfly(summed, "ctx", chip_bits[:-1], jnp.add)
    while len(rows) * NORM_ROWS < row_count:
        summed = beside(summed, summed)

    key_total = project(places, rows, key_near)
    key_total = project(places, rows, key_far + key_shared, key_total)
    key_total = project(places, rows, key_last + share(key_last), key_total)
    value_total = project(places, rows, value_near)
    value_shared = share(value_far)
    value_last = send_last(own_values, value_shared)
    value_total = project(places, rows, value_far + value_shared, value_total)

    within = (place % team) * row_count + jnp.arange(row_count, dtype=jnp.int32)
    cosine, sine_part = tables(within.astype(jnp.float32), head_size)
    new_cosine, new_sine = tables(positions.astype(jnp.float32), head_size)
    masked, top, self_scores = call(
        functools.partial(score_kernel, team),
        "scores",
        [IN_SMEM] * 2 + [IN_VMEM] * 6,
        (shape((heads, row_count)), shape((heads, LANES)), shape((heads, LANES))),
    )(places, lengths, key_total, cosine, sine_part, new_cosine, new_sine, summed)
    if split:
        top = over_x(jnp.maximum(top, swap(top, "ctx", 1)), jnp.maximum)
    else:
        top = butterfly(top, "ctx", bits_below(team), jnp.maximum)

    blocks = value_last + share(value_last, value_total)
    packed = call(
        functools.partial(weigh_kernel, [d for d, _ in blocks], len(rows), team),
        "weighted_values",
        [IN_SMEM] * 2 + [IN_VMEM] * (len(rows) + len(blocks) + 5),
        shape((heads, 2 * head_size)),
    )(
        places,
        lengths,
        *rows,
        *[block for _, block in blocks],
        value_total,
        masked,
        top,
        self_scores,
        summed,
    )
    packed = butterfly(packed, "ctx", bits_below(team), jnp.add)
    other = swap(packed, "ctx", team)
    update = call(
        functools.partial(output_kernel, team),
        "output_products",
        [IN_SMEM] + [IN_VMEM] * 3,
        shape((requests, out_weight.shape[2])),
    )(places, packed, other, out_weight[0])
    return new_tokens + butterfly(update, "kv", bits_below(kv_count), jnp.add)


def solution(mesh):
    in_specs = (
        P(None, "ctx"),
        P(None, "ctx", None),
        P(),
        P(None, "ctx", "kv"),
        P(None, "ctx", "kv"),
        P(None, "ctx", "kv"),
        P(None, "kv", "ctx"),
        P(),
        P(),
    )
    out_specs = P(None, "ctx")
    return jax.shard_map(shards, mesh=mesh, in_specs=in_specs, out_specs=out_specs, check_vma=False)
```

time: 97.2 us -> 92 us (0.947)
  waiting for transfers between devices: 30.9 us -> 13.8 us
  starting transfers between devices: 28.5 us -> 34.4 us
  Pallas kernels: 21.8 us -> 25.1 us
  local copies, waits for them, and re-layouts: 12.8 us -> 14.2 us
    ppermute x35 -> x21, waiting for transfers between devices: 30.9 us -> 13.8 us  [swap(): return lax.ppermute(value, axis, [(i, i ^ distance) for i in range(count)])]
    ppermute x0 -> x11, starting transfers between devices: none -> 15.5 us  [by_core(): return lax.ppermute(value, 'ctx', pairs)]
    ppermute x35 -> x21, starting transfers between devices: 28.5 us -> 18.9 us  [swap(): return lax.ppermute(value, axis, [(i, i ^ distance) for i in range(count)])]
    pallas_call x2 -> x5, Pallas kernels: 7.4 us -> 10.9 us  [normalise(): call(functools.partial(norm_kernel, first), 'normalise', [IN_HBM, IN_VMEM...]
    unnamed x32 -> x48, local copies, waits for them, and re-layouts: 11.3 us -> 14.2 us
    slice x4 -> x0, local copies, waits for them, and re-layouts: 1.51 us -> none  [gather_rounds(): halves[bit] = (block[:rows // 2], block[rows // 2:])]
    concatenate x2, other arithmetic: 0.23 us -> 1.22 us  [tables(): jnp.concatenate((cosine, cosine), axis=-1)]
    pallas_call x6 -> x7, Pallas kernels: 12.9 us -> 12.6 us  [the longest x5 10.3 us: project(): call(functools.partial(project_kernel, [d for d, _ in blocks], len(rows),...]
  transfers between devices with their start and end apart: 35 -> 32, of which waited for: 13 -> 9; matrix products, arithmetic and copies ran while one was open for 3% -> 3% of each run, Pallas kernels for 20% -> 25%
where the time goes in v5:
time: 92 us; the launch traced here: 91.3 us
  starting transfers between devices  34.4 us (37%)
  Pallas kernels  25.1 us (27%)
  local copies, waits for them, and re-layouts  14.2 us (15%)
  waiting for transfers between devices  13.8 us (15%)
  other arithmetic  3.36 us (4%)
    ppermute x21, starting transfers between devices, swap(): return lax.ppermute(value, axis, [(i, i ^ distance) for i in range(count)])  18.9 us
    ppermute x11, starting transfers between devices, by_core(): return lax.ppermute(value, 'ctx', pairs)  15.5 us
    unnamed x48, local copies, waits for them, and re-layouts  14.2 us
    ppermute x21, waiting for transfers between devices, swap(): return lax.ppermute(value, axis, [(i, i ^ distance) for i in range(count)])  13.8 us
    pallas_call x5, Pallas kernels, normalise(): call(functools.partial(norm_kernel, first), 'normalise', [IN_HBM, IN_VMEM...  10.9 us
    pallas_call x5, Pallas kernels, project(): call(functools.partial(project_kernel, [d for d, _ in blocks], len(rows),...  10.3 us
  transfers between devices with their start and end apart: 32, of which 9 were waited for; matrix products, arithmetic and copies ran while one was open for 3% of the time, Pallas kernels for 25%

profile of v5, /device:TPU:0, one launch (start us, length us, event | category | flops | bytes accessed | tf_op | source)
XLA Modules:
  0.0 91.3 jit_solution(14691687974580148423)
XLA Ops:
  0.0 0.5 collective-permute-start.1
  0.5 2.9 %collective-permute-start.8 = (bf16[2048,128]{1,0:T(8,128)(2,1)}, bf16[2048,128]{1,0:T(8,128)(2,1)S(1)}, u32[]{:S(2)}, u32[]{:S(2)}) collective-permute-start(bf16[2048,128]{1,0:T(8,128)(2,1)} %bitcast.24), channel_id=1, source_target_pairs={{0,8},{4,20},{8,0},{12,28},{16,24},{20,4},{24,16},{28,12},{1,9},{5... | collective-permute-start | bytes 1572872 | tf_op jit(solution)/shard_map/ppermute | solution.py:64
  3.5 0.7 copy-done.20
  4.2 0.1 squares.1
  4.3 1.1 %collective-permute-done = f32[2,128]{1,0:T(2,128)S(1)} collective-permute-done((f32[2,128]{1,0:T(2,128)S(1)}, f32[2,128]{1,0:T(2,128)S(1)}, u32[]{:S(2)}, u32[]{:S(2)}) %collective-permute-start) | collective-permute-done | bytes 1056 | tf_op jit(solution)/shard_map/ppermute | solution.py:43
  5.4 0.7 collective-permute-start.3
  6.1 0.8 copy-done.12
  6.9 2.2 %normalise.5.refs_0_ = bf16[8,64,2048]{2,1,0:T(8,128)(2,1)S(1)} custom-call(bf16[320,16384]{1,0:T(8,128)(2,1)} %bitcast.27, f32[8,1,2048]{2,1,0:T(1,128)S(1)} %bitcast.13), custom_call_target="tpu_custom_call" | custom-call | flops 1000 | bytes 1000 | tf_op jit(solution)/shard_map/normalise/pallas_call | solution.py:175
  9.1 2.3 %collective-permute-start.4 = (f32[2,128]{1,0:T(2,128)S(1)}, f32[2,128]{1,0:T(2,128)S(1)}, u32[]{:S(2)}, u32[]{:S(2)}) collective-permute-start(f32[2,128]{1,0:T(2,128)S(1)} %add.56), channel_id=1, source_target_pairs={{0,4},{4,0},{8,12},{12,8},{16,20},{20,16},{24,28},{28,24},{1,5},{5... | collective-permute-start | bytes 3080 | tf_op jit(solution)/shard_map/ppermute | solution.py:43
  11.4 2.2 %normalise.6.refs_1_ = bf16[8,64,2048]{2,1,0:T(8,128)(2,1)S(1)} custom-call(bf16[320,16384]{1,0:T(8,128)(2,1)} %bitcast.28, f32[8,1,2048]{2,1,0:T(1,128)S(1)} %bitcast.14), custom_call_target="tpu_custom_call" | custom-call | flops 1000 | bytes 1000 | tf_op jit(solution)/shard_map/normalise/pallas_call | solution.py:175
  13.6 1.3 %copy-done = bf16[8,64,2048]{2,1,0:T(8,128)(2,1)} copy-done((bf16[8,64,2048]{2,1,0:T(8,128)(2,1)}, bf16[8,64,2048]{2,1,0:T(8,128)(2,1)S(1)}, u32[]{:S(2)}) %copy-start) | copy-done | bytes 2097176
  15.0 0.1 collective-permute-start.9
  15.1 1.0 %collective-permute-start.7 = (bf16[2048,128]{1,0:T(8,128)(2,1)}, bf16[2048,128]{1,0:T(8,128)(2,1)}, u32[]{:S(2)}, u32[]{:S(2)}) collective-permute-start(bf16[2048,128]{1,0:T(8,128)(2,1)} %collective-permute-done.1.refs_6_), channel_id=1, source_target_pairs={{0,8},{4,20},{8,0},{12,28},{16,24},{20,4},{24,16},{28,12},{1,9},{5... | collective-permute-start | bytes 1572872 | tf_op jit(solution)/shard_map/ppermute | solution.py:64
  16.1 0.9 collective-permute-done.9.refs_7_
  16.9 0.8 copy-done.18
  17.7 1.0 %collective-permute-start.10 = (bf16[2048,128]{1,0:T(8,128)(2,1)S(1)}, bf16[2048,128]{1,0:T(8,128)(2,1)}, u32[]{:S(2)}, u32[]{:S(2)}) collective-permute-start(bf16[2048,128]{1,0:T(8,128)(2,1)S(1)} %bitcast.20), channel_id=1, source_target_pairs={{0,8},{4,20},{8,0},{12,28},{16,24},{20,4},{24,16},{28,12},{1,9},{5... | collective-permute-start | bytes 1572872 | tf_op jit(solution)/shard_map/ppermute | solution.py:64
  18.7 3.4 %collective-permute-start.5 = (f32[2,128]{1,0:T(2,128)S(1)}, f32[2,128]{1,0:T(2,128)S(1)}, u32[]{:S(2)}, u32[]{:S(2)}) collective-permute-start(f32[2,128]{1,0:T(2,128)S(1)} %broadcast_select_fusion.4), channel_id=1, source_target_pairs={{0,16},{8,24},{16,0},{24,8},{1,17},{9,25},{17,1},{25,9},{2,18},{10... | collective-permute-start | bytes 3080 | tf_op jit(solution)/shard_map/ppermute | solution.py:64
  22.2 2.1 %normalise.7.refs_2_ = bf16[8,64,2048]{2,1,0:T(8,128)(2,1)S(1)} custom-call(bf16[320,16384]{1,0:T(8,128)(2,1)} %bitcast.29, f32[8,1,2048]{2,1,0:T(1,128)S(1)} %bitcast.15), custom_call_target="tpu_custom_call" | custom-call | flops 1000 | bytes 1000 | tf_op jit(solution)/shard_map/normalise/pallas_call | solution.py:175
  24.3 1.4 %copy-done.3 = bf16[8,64,2048]{2,1,0:T(8,128)(2,1)} copy-done((bf16[8,64,2048]{2,1,0:T(8,128)(2,1)}, bf16[8,64,2048]{2,1,0:T(8,128)(2,1)S(1)}, u32[]{:S(2)}) %copy-start.3) | copy-done | bytes 2097176
  25.7 0.6 collective-permute-start.13
  26.3 2.3 %normalise.8.refs_3_ = bf16[8,64,2048]{2,1,0:T(8,128)(2,1)S(1)} custom-call(bf16[320,16384]{1,0:T(8,128)(2,1)} %bitcast.30, f32[8,1,2048]{2,1,0:T(1,128)S(1)} %bitcast.16), custom_call_target="tpu_custom_call" | custom-call | flops 1000 | bytes 1000 | tf_op jit(solution)/shard_map/normalise/pallas_call | solution.py:175
  28.6 1.4 %copy-done.6 = bf16[8,64,2048]{2,1,0:T(8,128)(2,1)} copy-done((bf16[8,64,2048]{2,1,0:T(8,128)(2,1)}, bf16[8,64,2048]{2,1,0:T(8,128)(2,1)S(1)}, u32[]{:S(2)}) %copy-start.6) | copy-done | bytes 2097176
  30.0 0.8 query_products.1
  30.9 0.2 collective-permute-start.19
  31.1 2.1 %normalise.9.refs_4_ = bf16[8,64,2048]{2,1,0:T(8,128)(2,1)S(1)} custom-call(bf16[320,16384]{1,0:T(8,128)(2,1)} %bitcast.31, f32[8,1,2048]{2,1,0:T(1,128)S(1)} %bitcast.18), custom_call_target="tpu_custom_call" | custom-call | flops 1000 | bytes 1000 | tf_op jit(solution)/shard_map/normalise/pallas_call | solution.py:175
  33.2 1.4 %copy-done.8 = bf16[8,64,2048]{2,1,0:T(8,128)(2,1)} copy-done((bf16[8,64,2048]{2,1,0:T(8,128)(2,1)}, bf16[8,64,2048]{2,1,0:T(8,128)(2,1)S(1)}, u32[]{:S(2)}) %copy-start.8) | copy-done | bytes 2097176
  34.6 0.7 collective-permute-start.20
  35.3 2.9 %collective-permute-start.11 = (bf16[2048,128]{1,0:T(8,128)(2,1)}, bf16[2048,128]{1,0:T(8,128)(2,1)}, u32[]{:S(2)}, u32[]{:S(2)}) collective-permute-start(bf16[2048,128]{1,0:T(8,128)(2,1)} %collective-permute-done.10.refs_5_), channel_id=1, source_target_pairs={{0,4},{4,0},{8,12},{12,8},{16,20},{20,16},{24,28},{28,24},{1,5},{5... | collective-permute-start | bytes 1572872 | tf_op jit(solution)/shard_map/ppermute | solution.py:43
  38.1 1.3 %fusion = (f32[320,64]{1,0:T(8,128)S(1)}, f32[320,64]{1,0:T(8,128)S(1)}, f32[320,64]{1,0:T(8,128)}) fusion(f32[64]{0:T(128)S(1)} %multiply_exponential_fusion, f32[320]{0:T(512)S(1)} %add_convert_fusion), kind=kLoop, calls=%fused_computation.4 | loop fusion | flops 40960 | bytes 247296 | tf_op jit(solution)/shard_map/neg | solution.py:105
  39.6 0.1 fusion.1
  39.7 0.6 collective-permute-start.14
  40.3 0.9 %collective-permute-start.16 = (bf16[2048,128]{1,0:T(8,128)(2,1)}, bf16[2048,128]{1,0:T(8,128)(2,1)S(1)}, u32[]{:S(2)}, u32[]{:S(2)}) collective-permute-start(bf16[2048,128]{1,0:T(8,128)(2,1)} %copy-done.18), channel_id=1, source_target_pairs={{0,8},{4,20},{8,0},{12,28},{16,24},{20,4},{24,16},{28,12},{1,9},{5... | collective-permute-start | bytes 1572872 | tf_op jit(solution)/shard_map/ppermute | solution.py:64
  41.2 1.1 %collective-permute-start.12 = (bf16[2048,128]{1,0:T(8,128)(2,1)}, bf16[2048,128]{1,0:T(8,128)(2,1)S(1)}, u32[]{:S(2)}, u32[]{:S(2)}) collective-permute-start(bf16[2048,128]{1,0:T(8,128)(2,1)} %collective-permute-done.11.refs_7_), channel_id=1, source_target_pairs={{0,8},{4,20},{8,0},{12,28},{16,24},{20,4},{24,16},{28,12},{1,9},{5... | collective-permute-start | bytes 1572872 | tf_op jit(solution)/shard_map/ppermute | solution.py:64
  42.4 2.5 %collective-permute-start.22 = (f32[10,128]{1,0:T(8,128)S(1)}, f32[10,128]{1,0:T(8,128)S(1)}, u32[]{:S(2)}, u32[]{:S(2)}) collective-permute-start(f32[10,128]{1,0:T(8,128)S(1)} %select_bitcast_fusion), channel_id=1, source_target_pairs={{0,16},{8,24},{16,0},{24,8},{1,17},{9,25},{17,1},{25,9},{2,18},{10... | collective-permute-start | bytes 15368 | tf_op jit(solution)/shard_map/ppermute | solution.py:64
  44.9 1.1 %pad_maximum_fusion = (f32[320,128]{1,0:T(8,128)S(1)}, f32[320,128]{1,0:T(8,128)S(1)}) fusion(f32[320,64]{1,0:T(8,128)} %get-tuple-element.45, f32[320,64]{1,0:T(8,128)S(1)} %get-tuple-element.44, f32[320,64]{1,0:T(8,128)S(1)} %get-tuple-element.43), kind=kLoop, calls=%fused_computation.2 | loop fusion | flops 81920 | bytes 573440 | tf_op jit(solution)/shard_map/concatenate | solution.py:104
  46.1 1.6 %copy-done.1 = bf16[8,64,2048]{2,1,0:T(8,128)(2,1)S(1)} copy-done((bf16[8,64,2048]{2,1,0:T(8,128)(2,1)S(1)}, bf16[8,64,2048]{2,1,0:T(8,128)(2,1)}, u32[]{:S(2)}) %copy-start.1) | copy-done | bytes 2097176
  47.7 1.6 %copy-done.4 = bf16[8,64,2048]{2,1,0:T(8,128)(2,1)S(1)} copy-done((bf16[8,64,2048]{2,1,0:T(8,128)(2,1)S(1)}, bf16[8,64,2048]{2,1,0:T(8,128)(2,1)}, u32[]{:S(2)}) %copy-start.4) | copy-done | bytes 2097176
  49.3 1.6 %copy-done.7 = bf16[8,64,2048]{2,1,0:T(8,128)(2,1)S(1)} copy-done((bf16[8,64,2048]{2,1,0:T(8,128)(2,1)S(1)}, bf16[8,64,2048]{2,1,0:T(8,128)(2,1)}, u32[]{:S(2)}) %copy-start.7) | copy-done | bytes 2097176
  50.9 1.6 %copy-done.9 = bf16[8,64,2048]{2,1,0:T(8,128)(2,1)S(1)} copy-done((bf16[8,64,2048]{2,1,0:T(8,128)(2,1)S(1)}, bf16[8,64,2048]{2,1,0:T(8,128)(2,1)}, u32[]{:S(2)}) %copy-start.9) | copy-done | bytes 2097176
  52.5 1.9 %project.5.refs_9_ = f32[320,128]{1,0:T(8,128)S(1)} custom-call(s32[1]{0:T(128)} %bitcast.place_ref, bf16[8,64,2048]{2,1,0:T(8,128)(2,1)S(1)} %normalise.5.refs_0_, bf16[8,64,2048]{2,1,0:T(8,128)(2,1)S(1)} %copy-done.1, bf16[8,64,2048]{2,1,0:T(8,128)(2,1)S(1)} %copy-done.4, bf16[8,64,2048]{2,1,0:T(8,128)(2,1)S(1)} %copy-done.7, ...), custom_call_target="tpu_custom_call" | custom-call | flops 1000 | bytes 1000 | tf_op jit(solution)/shard_map/project/pallas_call | solution.py:220
  54.4 0.6 collective-permute-start.17
  55.1 2.9 %project.6.refs_7_ = f32[320,128]{1,0:T(8,128)S(1)} custom-call(s32[1]{0:T(128)} %bitcast.place_ref, bf16[8,64,2048]{2,1,0:T(8,128)(2,1)S(1)} %normalise.5.refs_0_, bf16[8,64,2048]{2,1,0:T(8,128)(2,1)S(1)} %copy-done.1, bf16[8,64,2048]{2,1,0:T(8,128)(2,1)S(1)} %copy-done.4, bf16[8,64,2048]{2,1,0:T(8,128)(2,1)S(1)} %copy-done.7, ...), custom_call_target="tpu_custom_call" | custom-call | flops 1000 | bytes 1000 | tf_op jit(solution)/shard_map/project/pallas_call | solution.py:220
  58.0 0.5 collective-permute-start.15
  58.5 2.0 %project.7.refs_9_ = f32[320,128]{1,0:T(8,128)S(1)} custom-call(s32[1]{0:T(128)} %bitcast.place_ref, bf16[8,64,2048]{2,1,0:T(8,128)(2,1)S(1)} %normalise.5.refs_0_, bf16[8,64,2048]{2,1,0:T(8,128)(2,1)S(1)} %copy-done.1, bf16[8,64,2048]{2,1,0:T(8,128)(2,1)S(1)} %copy-done.4, bf16[8,64,2048]{2,1,0:T(8,128)(2,1)S(1)} %copy-done.7, ...), custom_call_target="tpu_custom_call" | custom-call | flops 1000 | bytes 1000 | tf_op jit(solution)/shard_map/project/pallas_call | solution.py:220
  60.5 2.7 %project.8.refs_7_ = f32[320,128]{1,0:T(8,128)S(1)} custom-call(s32[1]{0:T(128)} %bitcast.place_ref, bf16[8,64,2048]{2,1,0:T(8,128)(2,1)S(1)} %normalise.5.refs_0_, bf16[8,64,2048]{2,1,0:T(8,128)(2,1)S(1)} %copy-done.1, bf16[8,64,2048]{2,1,0:T(8,128)(2,1)S(1)} %copy-done.4, bf16[8,64,2048]{2,1,0:T(8,128)(2,1)S(1)} %copy-done.7, ...), custom_call_target="tpu_custom_call" | custom-call | flops 1000 | bytes 1000 | tf_op jit(solution)/shard_map/project/pallas_call | solution.py:220
  63.3 0.8 project.9.refs_0_
  64.2 0.8 scores.1
  65.1 1.1 %collective-permute-done.24 = f32[8,128]{1,0:T(8,128)S(1)} collective-permute-done((f32[8,128]{1,0:T(8,128)S(1)}, f32[8,128]{1,0:T(8,128)S(1)}, u32[]{:S(2)}, u32[]{:S(2)}) %collective-permute-start.24) | collective-permute-done | bytes 4128 | tf_op jit(solution)/shard_map/ppermute | solution.py:43
  66.2 0.7 collective-permute-start.25
  66.9 3.8 %collective-permute-start.26 = (f32[8,128]{1,0:T(8,128)S(1)}, f32[8,128]{1,0:T(8,128)S(1)}, u32[]{:S(2)}, u32[]{:S(2)}) collective-permute-start(f32[8,128]{1,0:T(8,128)S(1)} %max.7), channel_id=1, source_target_pairs={{0,4},{4,0},{8,12},{12,8},{16,20},{20,16},{24,28},{28,24},{1,5},{5... | collective-permute-start | bytes 12296 | tf_op jit(solution)/shard_map/ppermute | solution.py:43
  70.7 0.8 collective-permute-done.26
  71.5 1.5 %weighted_values.1 = f32[8,256]{1,0:T(8,128)S(1)} custom-call(s32[1]{0:T(128)} %bitcast.place_ref, s32[2]{0:T(128)S(1)} %copy-done.22, bf16[8,64,2048]{2,1,0:T(8,128)(2,1)S(1)} %normalise.5.refs_0_, bf16[8,64,2048]{2,1,0:T(8,128)(2,1)S(1)} %copy-done.2, bf16[8,64,2048]{2,1,0:T(8,128)(2,1)S(1)} %copy-done.5, bf16[8,64,2048]{2,1,0:T(8,128)(2,1)S(1)} %copy-done.7, ...), custom_call_target="tpu_custom_call" | custom-call | flops 1000 | bytes 1000 | tf_op jit(solution)/shard_map/weighted_values/pallas_call | solution.py:410
  73.1 0.4 collective-permute-start.27
  73.4 0.8 collective-permute-done.27
  74.3 1.1 %collective-permute-start.28 = (f32[8,256]{1,0:T(8,128)S(1)}, f32[8,256]{1,0:T(8,128)S(1)}, u32[]{:S(2)}, u32[]{:S(2)}) collective-permute-start(f32[8,256]{1,0:T(8,128)S(1)} %add.65), channel_id=1, source_target_pairs={{0,8},{4,12},{8,0},{12,4},{16,24},{20,28},{24,16},{28,20},{1,9},{5... | collective-permute-start | bytes 24584 | tf_op jit(solution)/shard_map/ppermute | solution.py:43
  75.3 2.6 %collective-permute-done.28 = f32[8,256]{1,0:T(8,128)S(1)} collective-permute-done((f32[8,256]{1,0:T(8,128)S(1)}, f32[8,256]{1,0:T(8,128)S(1)}, u32[]{:S(2)}, u32[]{:S(2)}) %collective-permute-start.28) | collective-permute-done | bytes 8224 | tf_op jit(solution)/shard_map/ppermute | solution.py:43
  77.9 1.4 %collective-permute-start.29 = (f32[8,256]{1,0:T(8,128)S(1)}, f32[8,256]{1,0:T(8,128)S(1)}, u32[]{:S(2)}, u32[]{:S(2)}) collective-permute-start(f32[8,256]{1,0:T(8,128)S(1)} %add.66.mine_ref), channel_id=1, source_target_pairs={{0,16},{4,20},{8,24},{12,28},{16,0},{20,4},{24,8},{28,12},{1,17},{... | collective-permute-start | bytes 24584 | tf_op jit(solution)/shard_map/ppermute | solution.py:43
  79.3 2.3 %collective-permute-done.29.other_ref = f32[8,256]{1,0:T(8,128)S(1)} collective-permute-done((f32[8,256]{1,0:T(8,128)S(1)}, f32[8,256]{1,0:T(8,128)S(1)}, u32[]{:S(2)}, u32[]{:S(2)}) %collective-permute-start.29) | collective-permute-done | bytes 8224 | tf_op jit(solution)/shard_map/ppermute | solution.py:43
  81.6 0.7 output_products.1
  82.2 1.6 %collective-permute-start.30 = (f32[2,2048]{1,0:T(2,128)S(1)}, f32[2,2048]{1,0:T(2,128)S(1)}, u32[]{:S(2)}, u32[]{:S(2)}) collective-permute-start(f32[2,2048]{1,0:T(2,128)S(1)} %output_products.1), channel_id=1, source_target_pairs={{0,1},{1,0},{2,3},{3,2},{4,5},{5,4},{6,7},{7,6},{8,9},{9,8},{10,11... | collective-permute-start | bytes 49160 | tf_op jit(solution)/shard_map/ppermute | solution.py:43
  83.8 2.2 %collective-permute-done.30 = f32[2,2048]{1,0:T(2,128)S(1)} collective-permute-done((f32[2,2048]{1,0:T(2,128)S(1)}, f32[2,2048]{1,0:T(2,128)S(1)}, u32[]{:S(2)}, u32[]{:S(2)}) %collective-permute-start.30) | collective-permute-done | bytes 16416 | tf_op jit(solution)/shard_map/ppermute | solution.py:43
  86.0 2.7 %collective-permute-start.31 = (f32[2,2048]{1,0:T(2,128)S(1)}, f32[2,2048]{1,0:T(2,128)S(1)}, u32[]{:S(2)}, u32[]{:S(2)}) collective-permute-start(f32[2,2048]{1,0:T(2,128)S(1)} %add.67), channel_id=1, source_target_pairs={{0,2},{1,3},{2,0},{3,1},{4,6},{5,7},{6,4},{7,5},{8,10},{9,11},{10,... | collective-permute-start | bytes 49160 | tf_op jit(solution)/shard_map/ppermute | solution.py:43
  88.6 2.0 %collective-permute-done.31 = f32[2,2048]{1,0:T(2,128)S(1)} collective-permute-done((f32[2,2048]{1,0:T(2,128)S(1)}, f32[2,2048]{1,0:T(2,128)S(1)}, u32[]{:S(2)}, u32[]{:S(2)}) %collective-permute-start.31) | collective-permute-done | bytes 16416 | tf_op jit(solution)/shard_map/ppermute | solution.py:43
  90.7 0.6 add_add_fusion
  (88 shorter events, 0.7 us)
Async XLA Ops:
  0.0 5.4 %collective-permute-start.1 = (bf16[2048,128]{1,0:T(8,128)(2,1)}, bf16[2048,128]{1,0:T(8,128)(2,1)}, u32[]{:S(2)}, u32[]{:S(2)}) collective-permute-start(bf16[2048,128]{1,0:T(8,128)(2,1)} %bitcast.23), channel_id=1, source_target_pairs={{0,4},{4,0},{8,12},{12,8},{16,20},{20,16},{24,28},{28,24},{1,5},{5... | collective-permute-start | bytes 1572872 | tf_op jit(solution)/shard_map/ppermute | solution.py:43
  0.5 5.0 %collective-permute-start.2 = (bf16[2048,128]{1,0:T(8,128)(2,1)}, bf16[2048,128]{1,0:T(8,128)(2,1)}, u32[]{:S(2)}, u32[]{:S(2)}) collective-permute-start(bf16[2048,128]{1,0:T(8,128)(2,1)} %bitcast.19), channel_id=1, source_target_pairs={{0,4},{4,0},{8,12},{12,8},{16,20},{20,16},{24,28},{28,24},{1,5},{5... | collective-permute-start | bytes 1572872 | tf_op jit(solution)/shard_map/ppermute | solution.py:43
  0.5 14.4 %collective-permute-start.8 = (bf16[2048,128]{1,0:T(8,128)(2,1)}, bf16[2048,128]{1,0:T(8,128)(2,1)S(1)}, u32[]{:S(2)}, u32[]{:S(2)}) collective-permute-start(bf16[2048,128]{1,0:T(8,128)(2,1)} %bitcast.24), channel_id=1, source_target_pairs={{0,8},{4,20},{8,0},{12,28},{16,24},{20,4},{24,16},{28,12},{1,9},{5... | collective-permute-start | bytes 1572872 | tf_op jit(solution)/shard_map/ppermute | solution.py:64
  3.5 0.7 copy-start.20
  4.3 1.1 %collective-permute-start = (f32[2,128]{1,0:T(2,128)S(1)}, f32[2,128]{1,0:T(2,128)S(1)}, u32[]{:S(2)}, u32[]{:S(2)}) collective-permute-start(f32[2,128]{1,0:T(2,128)S(1)} %squares.1), channel_id=1, source_target_pairs={{0,4},{4,0},{8,12},{12,8},{16,20},{20,16},{24,28},{28,24},{1,5},{5... | collective-permute-start | bytes 3080 | tf_op jit(solution)/shard_map/ppermute | solution.py:43
  5.4 3.7 %collective-permute-start.3 = (f32[2,128]{1,0:T(2,128)S(1)}, f32[2,128]{1,0:T(2,128)S(1)}, u32[]{:S(2)}, u32[]{:S(2)}) collective-permute-start(f32[2,128]{1,0:T(2,128)S(1)} %add.55), channel_id=1, source_target_pairs={{4,12},{12,4},{20,28},{28,20},{5,13},{13,5},{21,29},{29,21},{6,14}... | collective-permute-start | bytes 3080 | tf_op jit(solution)/shard_map/ppermute | solution.py:64
  6.1 0.8 copy-start.12
  6.9 4.5 %copy-start.13 = (f32[1,16384]{1,0:T(1,128)S(1)}, f32[1,16384]{1,0:T(1,128)}, u32[]{:S(2)}) copy-start(f32[1,16384]{1,0:T(1,128)} %param.11) | copy-start | bytes 196612
  9.1 5.8 %collective-permute-start.4 = (f32[2,128]{1,0:T(2,128)S(1)}, f32[2,128]{1,0:T(2,128)S(1)}, u32[]{:S(2)}, u32[]{:S(2)}) collective-permute-start(f32[2,128]{1,0:T(2,128)S(1)} %add.56), channel_id=1, source_target_pairs={{0,4},{4,0},{8,12},{12,8},{16,20},{20,16},{24,28},{28,24},{1,5},{5... | collective-permute-start | bytes 3080 | tf_op jit(solution)/shard_map/ppermute | solution.py:43
  11.4 6.3 %copy-start.14 = (bf16[1,2048,128]{2,1,0:T(8,128)(2,1)S(1)}, bf16[1,2048,128]{2,1,0:T(8,128)(2,1)}, u32[]{:S(2)}) copy-start(bf16[1,2048,128]{2,1,0:T(8,128)(2,1)} %param.14) | copy-start | bytes 1572868
  13.6 1.4 %copy-start = (bf16[8,64,2048]{2,1,0:T(8,128)(2,1)}, bf16[8,64,2048]{2,1,0:T(8,128)(2,1)S(1)}, u32[]{:S(2)}) copy-start(bf16[8,64,2048]{2,1,0:T(8,128)(2,1)S(1)} %normalise.6.refs_1_) | copy-start | bytes 6291460
  15.0 9.3 %copy-start.16 = (bf16[2048,128]{1,0:T(8,128)(2,1)}, bf16[2048,128]{1,0:T(8,128)(2,1)S(1)}, u32[]{:S(2)}) copy-start(bf16[2048,128]{1,0:T(8,128)(2,1)S(1)} %collective-permute-done.8.refs_5_) | copy-start | bytes 1572868
  15.0 2.0 %collective-permute-start.9 = (bf16[2048,128]{1,0:T(8,128)(2,1)S(1)}, bf16[2048,128]{1,0:T(8,128)(2,1)S(1)}, u32[]{:S(2)}, u32[]{:S(2)}) collective-permute-start(bf16[2048,128]{1,0:T(8,128)(2,1)S(1)} %collective-permute-done.8.refs_5_), channel_id=1, source_target_pairs={{0,4},{4,0},{8,12},{12,8},{16,20},{20,16},{24,28},{28,24},{1,5},{5... | collective-permute-start | bytes 1572872 | tf_op jit(solution)/shard_map/ppermute | solution.py:43
  15.1 14.9 %collective-permute-start.7 = (bf16[2048,128]{1,0:T(8,128)(2,1)}, bf16[2048,128]{1,0:T(8,128)(2,1)}, u32[]{:S(2)}, u32[]{:S(2)}) collective-permute-start(bf16[2048,128]{1,0:T(8,128)(2,1)} %collective-permute-done.1.refs_6_), channel_id=1, source_target_pairs={{0,8},{4,20},{8,0},{12,28},{16,24},{20,4},{24,16},{28,12},{1,9},{5... | collective-permute-start | bytes 1572872 | tf_op jit(solution)/shard_map/ppermute | solution.py:64
  16.9 0.8 copy-start.18
  17.7 17.5 %collective-permute-start.10 = (bf16[2048,128]{1,0:T(8,128)(2,1)S(1)}, bf16[2048,128]{1,0:T(8,128)(2,1)}, u32[]{:S(2)}, u32[]{:S(2)}) collective-permute-start(bf16[2048,128]{1,0:T(8,128)(2,1)S(1)} %bitcast.20), channel_id=1, source_target_pairs={{0,8},{4,20},{8,0},{12,28},{16,24},{20,4},{24,16},{28,12},{1,9},{5... | collective-permute-start | bytes 1572872 | tf_op jit(solution)/shard_map/ppermute | solution.py:64
  18.7 7.0 %collective-permute-start.5 = (f32[2,128]{1,0:T(2,128)S(1)}, f32[2,128]{1,0:T(2,128)S(1)}, u32[]{:S(2)}, u32[]{:S(2)}) collective-permute-start(f32[2,128]{1,0:T(2,128)S(1)} %broadcast_select_fusion.4), channel_id=1, source_target_pairs={{0,16},{8,24},{16,0},{24,8},{1,17},{9,25},{17,1},{25,9},{2,18},{10... | collective-permute-start | bytes 3080 | tf_op jit(solution)/shard_map/ppermute | solution.py:64
  24.3 1.4 %copy-start.3 = (bf16[8,64,2048]{2,1,0:T(8,128)(2,1)}, bf16[8,64,2048]{2,1,0:T(8,128)(2,1)S(1)}, u32[]{:S(2)}) copy-start(bf16[8,64,2048]{2,1,0:T(8,128)(2,1)S(1)} %normalise.7.refs_2_) | copy-start | bytes 6291460
  25.7 4.3 %collective-permute-start.6 = (f32[2,128]{1,0:T(2,128)S(1)}, f32[2,128]{1,0:T(2,128)S(1)}, u32[]{:S(2)}, u32[]{:S(2)}) collective-permute-start(f32[2,128]{1,0:T(2,128)S(1)} %add.58), channel_id=1, source_target_pairs={{0,4},{4,0},{8,12},{12,8},{16,20},{20,16},{24,28},{28,24},{1,5},{5... | collective-permute-start | bytes 3080 | tf_op jit(solution)/shard_map/ppermute | solution.py:43
  25.7 4.3 %copy-start.15 = (bf16[1,2048,128]{2,1,0:T(8,128)(2,1)S(1)}, bf16[1,2048,128]{2,1,0:T(8,128)(2,1)}, u32[]{:S(2)}) copy-start(bf16[1,2048,128]{2,1,0:T(8,128)(2,1)} %param.13) | copy-start | bytes 1572868
  25.7 4.3 %copy-start.21 = (f32[2,2048]{1,0:T(2,128)S(1)}, f32[2,2048]{1,0:T(2,128)}, u32[]{:S(2)}) copy-start(f32[2,2048]{1,0:T(2,128)} %tokens_ref.3) | copy-start | bytes 49156
  25.7 14.0 %collective-permute-start.13 = (bf16[2048,128]{1,0:T(8,128)(2,1)}, bf16[2048,128]{1,0:T(8,128)(2,1)}, u32[]{:S(2)}, u32[]{:S(2)}) collective-permute-start(bf16[2048,128]{1,0:T(8,128)(2,1)} %collective-permute-done.2.refs_6_), channel_id=1, source_target_pairs={{0,8},{4,20},{8,0},{12,28},{16,24},{20,4},{24,16},{28,12},{1,9},{5... | collective-permute-start | bytes 1572872 | tf_op jit(solution)/shard_map/ppermute | solution.py:64
  26.3 3.7 %copy-start.10 = (bf16[1,2048,1024]{2,1,0:T(8,128)(2,1)S(1)}, bf16[1,2048,1024]{2,1,0:T(8,128)(2,1)}, u32[]{:S(2)}) copy-start(bf16[1,2048,1024]{2,1,0:T(8,128)(2,1)} %param.12) | copy-start | bytes 12582916
  28.6 1.4 %copy-start.6 = (bf16[8,64,2048]{2,1,0:T(8,128)(2,1)}, bf16[8,64,2048]{2,1,0:T(8,128)(2,1)S(1)}, u32[]{:S(2)}) copy-start(bf16[8,64,2048]{2,1,0:T(8,128)(2,1)S(1)} %normalise.8.refs_3_) | copy-start | bytes 6291460
  30.9 3.7 %collective-permute-start.19 = (f32[2,10,128]{2,1,0:T(8,128)S(1)}, f32[2,10,128]{2,1,0:T(8,128)S(1)}, u32[]{:S(2)}, u32[]{:S(2)}) collective-permute-start(f32[2,10,128]{2,1,0:T(8,128)S(1)} %query_products.1), channel_id=1, source_target_pairs={{0,4},{4,0},{8,12},{12,8},{16,20},{20,16},{24,28},{28,24},{1,5},{5... | collective-permute-start | bytes 30728 | tf_op jit(solution)/shard_map/ppermute | solution.py:43
  31.1 8.4 %copy-start.23 = (s32[2]{0:T(128)S(1)}, s32[2]{0:T(128)}, u32[]{:S(2)}) copy-start(s32[2]{0:T(128)} %param.17) | copy-start | bytes 28
  33.2 1.4 %copy-start.8 = (bf16[8,64,2048]{2,1,0:T(8,128)(2,1)}, bf16[8,64,2048]{2,1,0:T(8,128)(2,1)S(1)}, u32[]{:S(2)}) copy-start(bf16[8,64,2048]{2,1,0:T(8,128)(2,1)S(1)} %normalise.9.refs_4_) | copy-start | bytes 6291460
  34.6 4.9 %collective-permute-start.20 = (f32[2,10,128]{2,1,0:T(8,128)S(1)}, f32[2,10,128]{2,1,0:T(8,128)S(1)}, u32[]{:S(2)}, u32[]{:S(2)}) collective-permute-start(f32[2,10,128]{2,1,0:T(8,128)S(1)} %add.62), channel_id=1, source_target_pairs={{4,12},{12,4},{20,28},{28,20},{5,13},{13,5},{21,29},{29,21},{6,14}... | collective-permute-start | bytes 30728 | tf_op jit(solution)/shard_map/ppermute | solution.py:64
  35.3 5.9 %collective-permute-start.11 = (bf16[2048,128]{1,0:T(8,128)(2,1)}, bf16[2048,128]{1,0:T(8,128)(2,1)}, u32[]{:S(2)}, u32[]{:S(2)}) collective-permute-start(bf16[2048,128]{1,0:T(8,128)(2,1)} %collective-permute-done.10.refs_5_), channel_id=1, source_target_pairs={{0,4},{4,0},{8,12},{12,8},{16,20},{20,16},{24,28},{28,24},{1,5},{5... | collective-permute-start | bytes 1572872 | tf_op jit(solution)/shard_map/ppermute | solution.py:43
  39.5 1.7 %collective-permute-start.21 = (f32[2,10,128]{2,1,0:T(8,128)S(1)}, f32[2,10,128]{2,1,0:T(8,128)S(1)}, u32[]{:S(2)}, u32[]{:S(2)}) collective-permute-start(f32[2,10,128]{2,1,0:T(8,128)S(1)} %add.63), channel_id=1, source_target_pairs={{0,4},{4,0},{8,12},{12,8},{16,20},{20,16},{24,28},{28,24},{1,5},{5... | collective-permute-start | bytes 30728 | tf_op jit(solution)/shard_map/ppermute | solution.py:43
  39.7 15.4 %collective-permute-start.14 = (bf16[2048,128]{1,0:T(8,128)(2,1)}, bf16[2048,128]{1,0:T(8,128)(2,1)S(1)}, u32[]{:S(2)}, u32[]{:S(2)}) collective-permute-start(bf16[2048,128]{1,0:T(8,128)(2,1)} %collective-permute-done.13.refs_6_), channel_id=1, source_target_pairs={{0,4},{4,0},{8,12},{12,8},{16,20},{20,16},{24,28},{28,24},{1,5},{5... | collective-permute-start | bytes 1572872 | tf_op jit(solution)/shard_map/ppermute | solution.py:43
  40.3 14.1 %collective-permute-start.16 = (bf16[2048,128]{1,0:T(8,128)(2,1)}, bf16[2048,128]{1,0:T(8,128)(2,1)S(1)}, u32[]{:S(2)}, u32[]{:S(2)}) collective-permute-start(bf16[2048,128]{1,0:T(8,128)(2,1)} %copy-done.18), channel_id=1, source_target_pairs={{0,8},{4,20},{8,0},{12,28},{16,24},{20,4},{24,16},{28,12},{1,9},{5... | collective-permute-start | bytes 1572872 | tf_op jit(solution)/shard_map/ppermute | solution.py:64
  41.2 16.7 %collective-permute-start.12 = (bf16[2048,128]{1,0:T(8,128)(2,1)}, bf16[2048,128]{1,0:T(8,128)(2,1)S(1)}, u32[]{:S(2)}, u32[]{:S(2)}) collective-permute-start(bf16[2048,128]{1,0:T(8,128)(2,1)} %collective-permute-done.11.refs_7_), channel_id=1, source_target_pairs={{0,8},{4,20},{8,0},{12,28},{16,24},{20,4},{24,16},{28,12},{1,9},{5... | collective-permute-start | bytes 1572872 | tf_op jit(solution)/shard_map/ppermute | solution.py:64
  42.4 12.6 %collective-permute-start.22 = (f32[10,128]{1,0:T(8,128)S(1)}, f32[10,128]{1,0:T(8,128)S(1)}, u32[]{:S(2)}, u32[]{:S(2)}) collective-permute-start(f32[10,128]{1,0:T(8,128)S(1)} %select_bitcast_fusion), channel_id=1, source_target_pairs={{0,16},{8,24},{16,0},{24,8},{1,17},{9,25},{17,1},{25,9},{2,18},{10... | collective-permute-start | bytes 15368 | tf_op jit(solution)/shard_map/ppermute | solution.py:64
  46.1 14.5 %collective-permute-start.18 = (bf16[2048,128]{1,0:T(8,128)(2,1)}, bf16[2048,128]{1,0:T(8,128)(2,1)S(1)}, u32[]{:S(2)}, u32[]{:S(2)}) collective-permute-start(bf16[2048,128]{1,0:T(8,128)(2,1)} %collective-permute-done.7.refs_6_), channel_id=1, source_target_pairs={{0,4},{4,0},{8,12},{12,8},{16,20},{20,16},{24,28},{28,24},{1,5},{5... | collective-permute-start | bytes 1572872 | tf_op jit(solution)/shard_map/ppermute | solution.py:43
  46.1 1.6 %copy-start.1 = (bf16[8,64,2048]{2,1,0:T(8,128)(2,1)S(1)}, bf16[8,64,2048]{2,1,0:T(8,128)(2,1)}, u32[]{:S(2)}) copy-start(bf16[8,64,2048]{2,1,0:T(8,128)(2,1)} %copy-done) | copy-start | bytes 6291460
  47.7 1.6 %copy-start.4 = (bf16[8,64,2048]{2,1,0:T(8,128)(2,1)S(1)}, bf16[8,64,2048]{2,1,0:T(8,128)(2,1)}, u32[]{:S(2)}) copy-start(bf16[8,64,2048]{2,1,0:T(8,128)(2,1)} %copy-done.3) | copy-start | bytes 6291460
  49.3 1.6 %copy-start.7 = (bf16[8,64,2048]{2,1,0:T(8,128)(2,1)S(1)}, bf16[8,64,2048]{2,1,0:T(8,128)(2,1)}, u32[]{:S(2)}) copy-start(bf16[8,64,2048]{2,1,0:T(8,128)(2,1)} %copy-done.6) | copy-start | bytes 6291460
  50.9 1.6 %copy-start.9 = (bf16[8,64,2048]{2,1,0:T(8,128)(2,1)S(1)}, bf16[8,64,2048]{2,1,0:T(8,128)(2,1)}, u32[]{:S(2)}) copy-start(bf16[8,64,2048]{2,1,0:T(8,128)(2,1)} %copy-done.8) | copy-start | bytes 6291460
  54.4 8.9 %collective-permute-start.17 = (bf16[2048,128]{1,0:T(8,128)(2,1)S(1)}, bf16[2048,128]{1,0:T(8,128)(2,1)S(1)}, u32[]{:S(2)}, u32[]{:S(2)}) collective-permute-start(bf16[2048,128]{1,0:T(8,128)(2,1)S(1)} %collective-permute-done.16.refs_5_), channel_id=1, source_target_pairs={{0,4},{4,0},{8,12},{12,8},{16,20},{20,16},{24,28},{28,24},{1,5},{5... | collective-permute-start | bytes 1572872 | tf_op jit(solution)/shard_map/ppermute | solution.py:43
  55.0 5.5 %collective-permute-start.23 = (f32[10,128]{1,0:T(8,128)S(1)}, f32[10,128]{1,0:T(8,128)S(1)}, u32[]{:S(2)}, u32[]{:S(2)}) collective-permute-start(f32[10,128]{1,0:T(8,128)S(1)} %bitcast_add_fusion), channel_id=1, source_target_pairs={{0,4},{4,0},{8,12},{12,8},{16,20},{20,16},{24,28},{28,24},{1,5},{5... | collective-permute-start | bytes 15368 | tf_op jit(solution)/shard_map/ppermute | solution.py:43
  58.0 13.6 %collective-permute-start.15 = (bf16[2048,128]{1,0:T(8,128)(2,1)S(1)}, bf16[2048,128]{1,0:T(8,128)(2,1)S(1)}, u32[]{:S(2)}, u32[]{:S(2)}) collective-permute-start(bf16[2048,128]{1,0:T(8,128)(2,1)S(1)} %collective-permute-done.12.refs_5_), channel_id=1, source_target_pairs={{0,4},{4,0},{8,12},{12,8},{16,20},{20,16},{24,28},{28,24},{1,5},{5... | collective-permute-start | bytes 1572872 | tf_op jit(solution)/shard_map/ppermute | solution.py:43
  58.5 2.0 %copy-start.17 = (bf16[2048,128]{1,0:T(8,128)(2,1)S(1)}, bf16[2048,128]{1,0:T(8,128)(2,1)}, u32[]{:S(2)}) copy-start(bf16[2048,128]{1,0:T(8,128)(2,1)} %copy-done.16) | copy-start | bytes 1572868
  58.5 2.0 %copy-start.19 = (bf16[2048,128]{1,0:T(8,128)(2,1)S(1)}, bf16[2048,128]{1,0:T(8,128)(2,1)}, u32[]{:S(2)}) copy-start(bf16[2048,128]{1,0:T(8,128)(2,1)} %copy-done.18) | copy-start | bytes 1572868
  60.5 2.8 %copy-start.5 = (bf16[8,64,2048]{2,1,0:T(8,128)(2,1)S(1)}, bf16[8,64,2048]{2,1,0:T(8,128)(2,1)}, u32[]{:S(2)}) copy-start(bf16[8,64,2048]{2,1,0:T(8,128)(2,1)} %copy-done.3) | copy-start | bytes 6291460
  63.3 0.9 copy-start.22
  63.3 8.3 %copy-start.2 = (bf16[8,64,2048]{2,1,0:T(8,128)(2,1)S(1)}, bf16[8,64,2048]{2,1,0:T(8,128)(2,1)}, u32[]{:S(2)}) copy-start(bf16[8,64,2048]{2,1,0:T(8,128)(2,1)} %copy-done) | copy-start | bytes 6291460
  65.0 1.2 %collective-permute-start.24 = (f32[8,128]{1,0:T(8,128)S(1)}, f32[8,128]{1,0:T(8,128)S(1)}, u32[]{:S(2)}, u32[]{:S(2)}) collective-permute-start(f32[8,128]{1,0:T(8,128)S(1)} %get-tuple-element.41), channel_id=1, source_target_pairs={{0,4},{4,0},{8,12},{12,8},{16,20},{20,16},{24,28},{28,24},{1,5},{5... | collective-permute-start | bytes 12296 | tf_op jit(solution)/shard_map/ppermute | solution.py:43
  66.2 0.7 collective-permute-start.25
  66.9 4.7 %collective-permute-start.26 = (f32[8,128]{1,0:T(8,128)S(1)}, f32[8,128]{1,0:T(8,128)S(1)}, u32[]{:S(2)}, u32[]{:S(2)}) collective-permute-start(f32[8,128]{1,0:T(8,128)S(1)} %max.7), channel_id=1, source_target_pairs={{0,4},{4,0},{8,12},{12,8},{16,20},{20,16},{24,28},{28,24},{1,5},{5... | collective-permute-start | bytes 12296 | tf_op jit(solution)/shard_map/ppermute | solution.py:43
  71.5 10.0 %copy-start.11 = (bf16[1,1024,2048]{2,1,0:T(8,128)(2,1)S(1)}, bf16[1,1024,2048]{2,1,0:T(8,128)(2,1)}, u32[]{:S(2)}) copy-start(bf16[1,1024,2048]{2,1,0:T(8,128)(2,1)} %param.15) | copy-start | bytes 12582916
  73.1 1.2 %collective-permute-start.27 = (f32[8,256]{1,0:T(8,128)S(1)}, f32[8,256]{1,0:T(8,128)S(1)}, u32[]{:S(2)}, u32[]{:S(2)}) collective-permute-start(f32[8,256]{1,0:T(8,128)S(1)} %weighted_values.1), channel_id=1, source_target_pairs={{0,4},{4,0},{8,12},{12,8},{16,20},{20,16},{24,28},{28,24},{1,5},{5... | collective-permute-start | bytes 24584 | tf_op jit(solution)/shard_map/ppermute | solution.py:43
  74.3 3.7 %collective-permute-start.28 = (f32[8,256]{1,0:T(8,128)S(1)}, f32[8,256]{1,0:T(8,128)S(1)}, u32[]{:S(2)}, u32[]{:S(2)}) collective-permute-start(f32[8,256]{1,0:T(8,128)S(1)} %add.65), channel_id=1, source_target_pairs={{0,8},{4,12},{8,0},{12,4},{16,24},{20,28},{24,16},{28,20},{1,9},{5... | collective-permute-start | bytes 24584 | tf_op jit(solution)/shard_map/ppermute | solution.py:43
  77.9 3.7 %collective-permute-start.29 = (f32[8,256]{1,0:T(8,128)S(1)}, f32[8,256]{1,0:T(8,128)S(1)}, u32[]{:S(2)}, u32[]{:S(2)}) collective-permute-start(f32[8,256]{1,0:T(8,128)S(1)} %add.66.mine_ref), channel_id=1, source_target_pairs={{0,16},{4,20},{8,24},{12,28},{16,0},{20,4},{24,8},{28,12},{1,17},{... | collective-permute-start | bytes 24584 | tf_op jit(solution)/shard_map/ppermute | solution.py:43
  82.2 3.8 %collective-permute-start.30 = (f32[2,2048]{1,0:T(2,128)S(1)}, f32[2,2048]{1,0:T(2,128)S(1)}, u32[]{:S(2)}, u32[]{:S(2)}) collective-permute-start(f32[2,2048]{1,0:T(2,128)S(1)} %output_products.1), channel_id=1, source_target_pairs={{0,1},{1,0},{2,3},{3,2},{4,5},{5,4},{6,7},{7,6},{8,9},{9,8},{10,11... | collective-permute-start | bytes 49160 | tf_op jit(solution)/shard_map/ppermute | solution.py:43
  86.0 4.7 %collective-permute-start.31 = (f32[2,2048]{1,0:T(2,128)S(1)}, f32[2,2048]{1,0:T(2,128)S(1)}, u32[]{:S(2)}, u32[]{:S(2)}) collective-permute-start(f32[2,2048]{1,0:T(2,128)S(1)} %add.67), channel_id=1, source_target_pairs={{0,2},{1,3},{2,0},{3,1},{4,6},{5,7},{6,4},{7,5},{8,10},{9,11},{10,... | collective-permute-start | bytes 49160 | tf_op jit(solution)/shard_map/ppermute | solution.py:43

commit v6 on v5

--- a/solution.py
+++ b/solution.py
@@ -64,10 +64,6 @@
     return lax.ppermute(value, "ctx", pairs)
 
 
-def on_core(core):
-    return lax.axis_index("ctx") % 2 == core
-
-
 def send_first(own, partner):
     count = lax.axis_size("ctx")
     if count != 8:
@@ -98,24 +94,26 @@
         jnp.arange(half_size, dtype=jnp.float32) * (-2.0 * math.log(ROPE_BASE) / head_size)
     )
     angles = placed[..., None] * frequency
-    cosine = jnp.cos(angles)
-    sine_part = jnp.sin(angles)
-    return (
-        jnp.concatenate((cosine, cosine), axis=-1),
-        jnp.concatenate((-sine_part, sine_part), axis=-1),
-    )
-
-
-def turn(values, cosine, signed_sine):
+    return jnp.cos(angles), jnp.sin(angles)
+
+
+def turn(values, cosine, sine_part):
     half_size = values.shape[-1] // 2
-    swapped = jnp.concatenate((values[:, half_size:], values[:, :half_size]), axis=-1)
-    return values * cosine + swapped * signed_sine
-
-
-def squares_kernel(tokens_ref, out_ref):
+    leading = values[:, :half_size]
+    trailing = values[:, half_size:]
+    return jnp.concatenate(
+        (leading * cosine - trailing * sine_part, trailing * cosine + leading * sine_part), axis=-1
+    )
+
+
+def squares_kernel(team, row_count, place_ref, tokens_ref, out_ref, core_ref, request_ref, row_ref):
     values = tokens_ref[...]
     total = jnp.sum(values * values, axis=-1, keepdims=True)
     out_ref[...] = jnp.broadcast_to(total, out_ref.shape)
+    place = place_ref[0]
+    core_ref[...] = jnp.full(core_ref.shape, lax.rem(place, 2))
+    request_ref[...] = jnp.full(request_ref.shape, lax.div(place, team))
+    row_ref[...] = jnp.full(row_ref.shape, lax.rem(place, team) * row_count)
 
 
 def norm_kernel(first, x_ref, gain_ref, *refs):
@@ -326,22 +324,29 @@
     split = ctx_count == 8
     chip_bits = bits_below(ctx_count)[1:]
     rows = []
-
-    def beside(received, sent):
-        if len(rows) * NORM_ROWS == row_count:
-            return received
-        rows.extend(
-            normalise(after(ctx_hidden[0], sent), gains, len(rows) * NORM_ROWS, 1)
-        )
+    squares, core, own_request, first_row = call(
+        functools.partial(squares_kernel, team, row_count),
+        "squares",
+        [IN_SMEM, IN_VMEM],
+        (shape((requests, LANES)),) + (shape((1, LANES), jnp.int32),) * 3,
+    )(places, new_tokens)
+
+    def beside(received, sent, parts):
+        first = len(rows) * NORM_ROWS
+        rows.extend(normalise(after(ctx_hidden[0], sent), gains, first, parts))
         return after(received, rows[-1])
 
-    def over_x(value, join):
-        value = join(value, beside(by_core(value, 0, 2), value))
-        return jnp.where(on_core(0), beside(swap(value, "ctx", 1), value), value)
-
-    def over_y(sent, value, join):
-        value = join(value, beside(by_core(sent, 4, 0), sent))
-        return jnp.where(on_core(1), beside(swap(value, "ctx", 1), value), value)
+    def sum_chips(value, norm_parts=0):
+        received = by_core(value, 4, 2)
+        if norm_parts:
+            received = beside(received, value, norm_parts)
+        told = swap(received, "ctx", 1)
+        opposite = by_core(told, 4, 2)
+        if norm_parts:
+            opposite = beside(opposite, told, row_count // NORM_ROWS - norm_parts)
+        over_x = jnp.where(core == 0, told, received)
+        over_y = jnp.where(core == 0, received, told)
+        return (value + over_x) + (over_y + opposite), told
 
     key_partner = swap(key_weight[0], "ctx", 1)
     value_partner = swap(value_weight[0], "ctx", 1)
@@ -349,16 +354,15 @@
     value_near = [((0, 0), value_weight[0]), ((1, 1), value_partner)]
     key_far = send_first(key_weight[0], key_partner)
 
-    squares = call(squares_kernel, "squares", [IN_VMEM], shape((requests, LANES)))(new_tokens)
     squares = squares + swap(squares, "ctx", 1)
     squares = after(squares, key_partner, value_partner)
     if split:
-        squares = over_x(squares, jnp.add)
-        key_shared = share(key_far, squares)
-        squares = over_y(squares, squares, jnp.add)
+        squares, told = sum_chips(squares, row_count // NORM_ROWS // 2)
+        key_shared = share(key_far, told)
         squares = after(squares, key_far[1][1])
     else:
         key_shared = share(key_far)
+        squares = beside(squares, squares, row_count // NORM_ROWS)
         squares = butterfly(squares, "ctx", chip_bits, jnp.add)
     key_last = send_last(key_weight[0], key_shared)
     own_values = after(value_weight[0], *[block for _, block in key_shared[:1]])
@@ -370,29 +374,26 @@
         [IN_SMEM] + [IN_VMEM] * 6,
         shape((requests, heads + 2, head_size)),
     )(places, squares, new_tokens, gains, query_weight[0], key_weight[0], value_weight[0])
-    parts = parts + beside(swap(parts, "ctx", 1), parts)
-    request = place // team
+    parts = parts + swap(parts, "ctx", 1)
+    parts_sent = parts
     if split:
-        parts = over_x(parts, jnp.add)
-    own_part = jnp.where(request == 0, parts[0], parts[1])
-    other_part = jnp.where(request == 0, parts[1], parts[0])
-    if split:
-        summed = over_y(other_part, own_part, jnp.add)
+        parts, _ = sum_chips(parts)
+        summed = jnp.where(own_request == 0, parts[0], parts[1])
     else:
+        own_part = jnp.where(own_request == 0, parts[0], parts[1])
+        other_part = jnp.where(own_request == 0, parts[1], parts[0])
         summed = own_part + swap(other_part, "ctx", team)
         summed = butterfly(summed, "ctx", chip_bits[:-1], jnp.add)
-    while len(rows) * NORM_ROWS < row_count:
-        summed = beside(summed, summed)
 
     key_total = project(places, rows, key_near)
     key_total = project(places, rows, key_far + key_shared, key_total)
     key_total = project(places, rows, key_last + share(key_last), key_total)
     value_total = project(places, rows, value_near)
-    value_shared = share(value_far)
+    value_shared = share(value_far, parts_sent)
     value_last = send_last(own_values, value_shared)
     value_total = project(places, rows, value_far + value_shared, value_total)
 
-    within = (place % team) * row_count + jnp.arange(row_count, dtype=jnp.int32)
+    within = first_row[0, :1] + jnp.arange(row_count, dtype=jnp.int32)
     cosine, sine_part = tables(within.astype(jnp.float32), head_size)
     new_cosine, new_sine = tables(positions.astype(jnp.float32), head_size)
     masked, top, self_scores = call(
@@ -402,7 +403,9 @@
         (shape((heads, row_count)), shape((heads, LANES)), shape((heads, LANES))),
     )(places, lengths, key_total, cosine, sine_part, new_cosine, new_sine, summed)
     if split:
-        top = over_x(jnp.maximum(top, swap(top, "ctx", 1)), jnp.maximum)
+        top = jnp.maximum(top, swap(top, "ctx", 1))
+        top = jnp.maximum(top, by_core(top, 0, 2))
+        top = jnp.where(core == 0, swap(top, "ctx", 1), top)
     else:
         top = butterfly(top, "ctx", bits_below(team), jnp.maximum)
 

time: 92 us -> 74.8 us (0.81)
  waiting for transfers between devices: 13.8 us -> 30 us
  local copies, waits for them, and re-layouts: 14.2 us -> 1.58 us
  starting transfers between devices: 34.4 us -> 24 us
  Pallas kernels: 25.1 us -> 17.2 us
  other arithmetic: 3.36 us -> 1.49 us
    unnamed x48 -> x18, local copies, waits for them, and re-layouts: 14.2 us -> 1.58 us
    ppermute x11, waiting for transfers between devices: 0.03 us -> 12.5 us  [by_core(): return lax.ppermute(value, 'ctx', pairs)]
    ppermute x21 -> x19, starting transfers between devices: 18.9 us -> 11.7 us  [swap(): return lax.ppermute(value, axis, [(i, i ^ distance) for i in range(count)])]
    pallas_call x5, Pallas kernels: 10.3 us -> 5.67 us  [project(): call(functools.partial(project_kernel, [d for d, _ in blocks], len(rows),...]
    ppermute x21 -> x19, waiting for transfers between devices: 13.8 us -> 17.5 us  [swap(): return lax.ppermute(value, axis, [(i, i ^ distance) for i in range(count)])]
    pallas_call x5 -> x2, Pallas kernels: 10.9 us -> 7.48 us  [normalise(): call(functools.partial(norm_kernel, first), 'normalise', [IN_HBM, IN_VMEM...]
    ppermute x11, starting transfers between devices: 15.5 us -> 12.4 us  [by_core(): return lax.ppermute(value, 'ctx', pairs)]
    neg x2 -> x0, other arithmetic: 1.42 us -> none  [tables(): -sine_part]
  transfers between devices with their start and end apart: 32 -> 30, of which waited for: 9 -> 17; matrix products, arithmetic and copies ran while one was open for 3% -> 1% of each run, Pallas kernels for 25% -> 20%
where the time goes in v6:
time: 74.8 us; the launch traced here: 74.6 us
  waiting for transfers between devices  30 us (40%)
  starting transfers between devices  24 us (32%)
  Pallas kernels  17.2 us (23%)
  local copies, waits for them, and re-layouts  1.58 us (2%)
  other arithmetic  1.49 us (2%)
    ppermute x19, waiting for transfers between devices, swap(): return lax.ppermute(value, axis, [(i, i ^ distance) for i in range(count)])  17.5 us
    ppermute x11, waiting for transfers between devices, by_core(): return lax.ppermute(value, 'ctx', pairs)  12.5 us
    ppermute x11, starting transfers between devices, by_core(): return lax.ppermute(value, 'ctx', pairs)  12.4 us
    ppermute x19, starting transfers between devices, swap(): return lax.ppermute(value, axis, [(i, i ^ distance) for i in range(count)])  11.7 us
    pallas_call x2, Pallas kernels, normalise(): call(functools.partial(norm_kernel, first), 'normalise', [IN_HBM, IN_VMEM...  7.48 us
    pallas_call x5, Pallas kernels, project(): call(functools.partial(project_kernel, [d for d, _ in blocks], len(rows),...  5.67 us
    unnamed x18, local copies, waits for them, and re-layouts  1.58 us
    pallas_call x1, Pallas kernels, shards(): call(functools.partial(weigh_kernel, [d for d, _ in blocks], len(rows), t...  1.52 us
  transfers between devices with their start and end apart: 30, of which 17 were waited for; matrix products, arithmetic and copies ran while one was open for 1% of the time, Pallas kernels for 20%

profile of v6, /device:TPU:0, one launch (start us, length us, event | category | flops | bytes accessed | tf_op | source)
XLA Modules:
  0.0 74.6 jit_solution(14158621953331918248)
XLA Ops:
  0.0 0.5 collective-permute-start.1
  0.5 0.1 collective-permute-start.2
  0.5 2.9 %collective-permute-start.5 = (bf16[2048,128]{1,0:T(8,128)(2,1)}, bf16[2048,128]{1,0:T(8,128)(2,1)S(1)}, u32[]{:S(2)}, u32[]{:S(2)}) collective-permute-start(bf16[2048,128]{1,0:T(8,128)(2,1)} %bitcast.24), channel_id=1, source_target_pairs={{0,8},{4,20},{8,0},{12,28},{16,24},{20,4},{24,16},{28,12},{1,9},{5... | collective-permute-start | bytes 1572872 | tf_op jit(solution)/shard_map/ppermute | solution.py:64
  3.5 0.7 copy-done.5
  4.2 0.1 squares.1
  4.3 1.1 %collective-permute-done = f32[2,128]{1,0:T(2,128)S(1)} collective-permute-done((f32[2,128]{1,0:T(2,128)S(1)}, f32[2,128]{1,0:T(2,128)S(1)}, u32[]{:S(2)}, u32[]{:S(2)}) %collective-permute-start) | collective-permute-done | bytes 1056 | tf_op jit(solution)/shard_map/ppermute | solution.py:43
  5.4 1.6 %collective-permute-start.3 = (f32[2,128]{1,0:T(2,128)S(1)}, f32[2,128]{1,0:T(2,128)S(1)}, u32[]{:S(2)}, u32[]{:S(2)}) collective-permute-start(f32[2,128]{1,0:T(2,128)S(1)} %add.53), channel_id=1, source_target_pairs={{0,16},{4,12},{8,24},{12,4},{16,0},{20,28},{24,8},{28,20},{1,17},{... | collective-permute-start | bytes 3080 | tf_op jit(solution)/shard_map/ppermute | solution.py:64
  7.0 0.8 %copy-done.4 = f32[1,16384]{1,0:T(1,128)S(1)} copy-done((f32[1,16384]{1,0:T(1,128)S(1)}, f32[1,16384]{1,0:T(1,128)}, u32[]{:S(2)}) %copy-start.4) | copy-done | bytes 65560
  7.8 3.2 %normalise.2 = (bf16[8,64,2048]{2,1,0:T(8,128)(2,1)S(1)}, bf16[8,64,2048]{2,1,0:T(8,128)(2,1)S(1)}) custom-call(bf16[320,16384]{1,0:T(8,128)(2,1)} %bitcast.35, f32[8,1,2048]{2,1,0:T(1,128)S(1)} %bitcast.31), custom_call_target="tpu_custom_call" | custom-call | flops 1000 | bytes 1000 | tf_op jit(solution)/shard_map/normalise/pallas_call | solution.py:173
  11.0 0.0 collective-permute-done.3
  11.1 0.1 collective-permute-start.4
  11.1 1.1 %collective-permute-done.4 = f32[2,128]{1,0:T(2,128)S(1)} collective-permute-done((f32[2,128]{1,0:T(2,128)S(1)}, f32[2,128]{1,0:T(2,128)S(1)}, u32[]{:S(2)}, u32[]{:S(2)}) %collective-permute-start.4) | collective-permute-done | bytes 1056 | tf_op jit(solution)/shard_map/ppermute | solution.py:43
  12.3 0.2 collective-permute-start.6
  12.5 0.5 collective-permute-start.9
  13.0 1.2 %collective-permute-done.6.refs_7_ = bf16[2048,128]{1,0:T(8,128)(2,1)S(1)} collective-permute-done((bf16[2048,128]{1,0:T(8,128)(2,1)S(1)}, bf16[2048,128]{1,0:T(8,128)(2,1)S(1)}, u32[]{:S(2)}, u32[]{:S(2)}) %collective-permute-start.6) | collective-permute-done | bytes 524320 | tf_op jit(solution)/shard_map/ppermute | solution.py:43
  14.2 0.6 collective-permute-start.7
  14.8 1.5 %collective-permute-start.8 = (f32[2,128]{1,0:T(2,128)S(1)}, f32[2,128]{1,0:T(2,128)S(1)}, u32[]{:S(2)}, u32[]{:S(2)}) collective-permute-start(f32[2,128]{1,0:T(2,128)S(1)} %collective-permute-done.4), channel_id=1, source_target_pairs={{0,16},{4,12},{8,24},{12,4},{16,0},{20,28},{24,8},{28,20},{1,17},{... | collective-permute-start | bytes 3080 | tf_op jit(solution)/shard_map/ppermute | solution.py:64
  16.3 4.3 %normalise.3 = (bf16[8,64,2048]{2,1,0:T(8,128)(2,1)S(1)}, bf16[8,64,2048]{2,1,0:T(8,128)(2,1)S(1)}, bf16[8,64,2048]{2,1,0:T(8,128)(2,1)S(1)}) custom-call(bf16[320,16384]{1,0:T(8,128)(2,1)} %bitcast.36, f32[8,1,2048]{2,1,0:T(1,128)S(1)} %bitcast.32), custom_call_target="tpu_custom_call" | custom-call | flops 1000 | bytes 1000 | tf_op jit(solution)/shard_map/normalise/pallas_call | solution.py:173
  20.6 0.0 collective-permute-done.8
  20.6 1.0 %collective-permute-done.9.refs_6_ = bf16[2048,128]{1,0:T(8,128)(2,1)S(1)} collective-permute-done((bf16[2048,128]{1,0:T(8,128)(2,1)S(1)}, bf16[2048,128]{1,0:T(8,128)(2,1)S(1)}, u32[]{:S(2)}, u32[]{:S(2)}) %collective-permute-start.9) | collective-permute-done | bytes 524320 | tf_op jit(solution)/shard_map/ppermute | solution.py:64
  21.7 0.8 %query_products.1 = f32[2,10,128]{2,1,0:T(8,128)S(1)} custom-call(s32[1]{0:T(128)} %bitcast.place_ref, f32[2,128]{1,0:T(2,128)S(1)} %add_add_fusion.2.squares_ref, f32[2,2048]{1,0:T(2,128)S(1)} %copy-done.5, f32[8,1,2048]{2,1,0:T(1,128)S(1)} %bitcast.33, bf16[2048,1024]{1,0:T(8,128)(2,1)S(1)} %bitcast.21, bf16[2048,128]{1,0:T(8,128)(2,1)S(1)} %bitcast.25, ...), custom_call_target="tpu_custom_call" | custom-call | flops 1000 | bytes 1000 | tf_op jit(solution)/shard_map/query_products/pallas_call | solution.py:371
  22.5 0.1 collective-permute-start.10
  22.5 0.6 collective-permute-start.13
  23.1 0.6 collective-permute-done.10
  23.7 3.5 %collective-permute-done.7.refs_5_ = bf16[2048,128]{1,0:T(8,128)(2,1)S(1)} collective-permute-done((bf16[2048,128]{1,0:T(8,128)(2,1)S(1)}, bf16[2048,128]{1,0:T(8,128)(2,1)S(1)}, u32[]{:S(2)}, u32[]{:S(2)}) %collective-permute-start.7) | collective-permute-done | bytes 524320 | tf_op jit(solution)/shard_map/ppermute | solution.py:64
  27.3 0.0 collective-permute-start.11
  27.3 0.6 collective-permute-start.16
  27.9 1.4 %collective-permute-start.19 = (f32[2,10,128]{2,1,0:T(8,128)S(1)}, f32[2,10,128]{2,1,0:T(8,128)S(1)}, u32[]{:S(2)}, u32[]{:S(2)}) collective-permute-start(f32[2,10,128]{2,1,0:T(8,128)S(1)} %add.57), channel_id=1, source_target_pairs={{0,16},{4,12},{8,24},{12,4},{16,0},{20,28},{24,8},{28,20},{1,17},{... | collective-permute-start | bytes 30728 | tf_op jit(solution)/shard_map/ppermute | solution.py:64
  29.3 3.7 %collective-permute-done.13.refs_6_ = bf16[2048,128]{1,0:T(8,128)(2,1)S(1)} collective-permute-done((bf16[2048,128]{1,0:T(8,128)(2,1)S(1)}, bf16[2048,128]{1,0:T(8,128)(2,1)S(1)}, u32[]{:S(2)}, u32[]{:S(2)}) %collective-permute-start.13) | collective-permute-done | bytes 524320 | tf_op jit(solution)/shard_map/ppermute | solution.py:64
  33.1 0.0 collective-permute-start.14
  33.1 0.5 collective-permute-start.12
  33.6 0.6 multiply_sine_fusion
  34.3 0.3 collective-permute-start.20
  34.5 0.1 multiply_sine_fusion.1
  34.6 0.4 collective-permute-start.18
  35.0 0.5 collective-permute-done.20
  35.5 1.4 %collective-permute-start.21 = (f32[2,10,128]{2,1,0:T(8,128)S(1)}, f32[2,10,128]{2,1,0:T(8,128)S(1)}, u32[]{:S(2)}, u32[]{:S(2)}) collective-permute-start(f32[2,10,128]{2,1,0:T(8,128)S(1)} %collective-permute-done.20), channel_id=1, source_target_pairs={{0,16},{4,12},{8,24},{12,4},{16,0},{20,28},{24,8},{28,20},{1,17},{... | collective-permute-start | bytes 30728 | tf_op jit(solution)/shard_map/ppermute | solution.py:64
  36.9 1.9 %collective-permute-done.16.refs_5_ = bf16[2048,128]{1,0:T(8,128)(2,1)S(1)} collective-permute-done((bf16[2048,128]{1,0:T(8,128)(2,1)S(1)}, bf16[2048,128]{1,0:T(8,128)(2,1)S(1)}, u32[]{:S(2)}, u32[]{:S(2)}) %collective-permute-start.16) | collective-permute-done | bytes 524320 | tf_op jit(solution)/shard_map/ppermute | solution.py:64
  38.9 0.9 %project.7.refs_9_ = f32[320,128]{1,0:T(8,128)S(1)} custom-call(s32[1]{0:T(128)} %bitcast.place_ref, bf16[8,64,2048]{2,1,0:T(8,128)(2,1)S(1)} %get-tuple-element.32.refs_0_, bf16[8,64,2048]{2,1,0:T(8,128)(2,1)S(1)} %get-tuple-element.33.refs_1_, bf16[8,64,2048]{2,1,0:T(8,128)(2,1)S(1)} %get-tuple-element.36.refs_2_, ...), custom_call_target="tpu_custom_call" | custom-call | flops 1000 | bytes 1000 | tf_op jit(solution)/shard_map/project/pallas_call | solution.py:218
  39.7 0.9 %project.5.refs_9_ = f32[320,128]{1,0:T(8,128)S(1)} custom-call(s32[1]{0:T(128)} %bitcast.place_ref, bf16[8,64,2048]{2,1,0:T(8,128)(2,1)S(1)} %get-tuple-element.32.refs_0_, bf16[8,64,2048]{2,1,0:T(8,128)(2,1)S(1)} %get-tuple-element.33.refs_1_, bf16[8,64,2048]{2,1,0:T(8,128)(2,1)S(1)} %get-tuple-element.36.refs_2_, ...), custom_call_target="tpu_custom_call" | custom-call | flops 1000 | bytes 1000 | tf_op jit(solution)/shard_map/project/pallas_call | solution.py:218
  40.6 1.5 %project.6.refs_7_ = f32[320,128]{1,0:T(8,128)S(1)} custom-call(s32[1]{0:T(128)} %bitcast.place_ref, bf16[8,64,2048]{2,1,0:T(8,128)(2,1)S(1)} %get-tuple-element.32.refs_0_, bf16[8,64,2048]{2,1,0:T(8,128)(2,1)S(1)} %get-tuple-element.33.refs_1_, bf16[8,64,2048]{2,1,0:T(8,128)(2,1)S(1)} %get-tuple-element.36.refs_2_, ...), custom_call_target="tpu_custom_call" | custom-call | flops 1000 | bytes 1000 | tf_op jit(solution)/shard_map/project/pallas_call | solution.py:218
  42.2 2.3 %collective-permute-done.12.refs_5_ = bf16[2048,128]{1,0:T(8,128)(2,1)S(1)} collective-permute-done((bf16[2048,128]{1,0:T(8,128)(2,1)S(1)}, bf16[2048,128]{1,0:T(8,128)(2,1)S(1)}, u32[]{:S(2)}, u32[]{:S(2)}) %collective-permute-start.12) | collective-permute-done | bytes 524320 | tf_op jit(solution)/shard_map/ppermute | solution.py:64
  44.5 1.5 %project.8.refs_7_ = f32[320,128]{1,0:T(8,128)S(1)} custom-call(s32[1]{0:T(128)} %bitcast.place_ref, bf16[8,64,2048]{2,1,0:T(8,128)(2,1)S(1)} %get-tuple-element.32.refs_0_, bf16[8,64,2048]{2,1,0:T(8,128)(2,1)S(1)} %get-tuple-element.33.refs_1_, bf16[8,64,2048]{2,1,0:T(8,128)(2,1)S(1)} %get-tuple-element.36.refs_2_, ...), custom_call_target="tpu_custom_call" | custom-call | flops 1000 | bytes 1000 | tf_op jit(solution)/shard_map/project/pallas_call | solution.py:218
  46.1 0.0 copy-start.7
  46.1 0.9 %project.9.refs_0_ = f32[320,128]{1,0:T(8,128)S(1)} custom-call(s32[1]{0:T(128)} %bitcast.place_ref, bf16[8,64,2048]{2,1,0:T(8,128)(2,1)S(1)} %get-tuple-element.32.refs_0_, bf16[8,64,2048]{2,1,0:T(8,128)(2,1)S(1)} %get-tuple-element.33.refs_1_, bf16[8,64,2048]{2,1,0:T(8,128)(2,1)S(1)} %get-tuple-element.36.refs_2_, ...), custom_call_target="tpu_custom_call" | custom-call | flops 1000 | bytes 1000 | tf_op jit(solution)/shard_map/project/pallas_call | solution.py:218
  47.0 1.0 %scores.1 = (f32[8,320]{1,0:T(8,128)S(1)}, f32[8,128]{1,0:T(8,128)S(1)}, f32[8,128]{1,0:T(8,128)S(1)}) custom-call(s32[1]{0:T(128)} %bitcast.place_ref, s32[2]{0:T(128)S(1)} %copy-done.7, f32[320,128]{1,0:T(8,128)S(1)} %project.9.refs_0_, f32[320,64]{1,0:T(8,128)S(1)} %get-tuple-element.54.refs_1_, f32[320,64]{1,0:T(8,128)S(1)} %get-tuple-element.53.refs_2_, ...), custom_call_target="tpu_custom_call" | custom-call | flops 1000 | bytes 1000 | tf_op jit(solution)/shard_map/scores/pallas_call | solution.py:399
  48.0 0.5 collective-permute-start.22
  48.5 0.8 %collective-permute-done.22 = f32[8,128]{1,0:T(8,128)S(1)} collective-permute-done((f32[8,128]{1,0:T(8,128)S(1)}, f32[8,128]{1,0:T(8,128)S(1)}, u32[]{:S(2)}, u32[]{:S(2)}) %collective-permute-start.22) | collective-permute-done | bytes 4128 | tf_op jit(solution)/shard_map/ppermute | solution.py:43
  49.3 0.6 collective-permute-start.23
  50.0 4.0 %collective-permute-start.24 = (f32[8,128]{1,0:T(8,128)S(1)}, f32[8,128]{1,0:T(8,128)S(1)}, u32[]{:S(2)}, u32[]{:S(2)}) collective-permute-start(f32[8,128]{1,0:T(8,128)S(1)} %max.7), channel_id=1, source_target_pairs={{0,4},{4,0},{8,12},{12,8},{16,20},{20,16},{24,28},{28,24},{1,5},{5... | collective-permute-start | bytes 12296 | tf_op jit(solution)/shard_map/ppermute | solution.py:43
  54.0 0.8 %collective-permute-done.24 = f32[8,128]{1,0:T(8,128)S(1)} collective-permute-done((f32[8,128]{1,0:T(8,128)S(1)}, f32[8,128]{1,0:T(8,128)S(1)}, u32[]{:S(2)}, u32[]{:S(2)}) %collective-permute-start.24) | collective-permute-done | bytes 4128 | tf_op jit(solution)/shard_map/ppermute | solution.py:43
  54.8 1.5 %weighted_values.1 = f32[8,256]{1,0:T(8,128)S(1)} custom-call(s32[1]{0:T(128)} %bitcast.place_ref, s32[2]{0:T(128)S(1)} %copy-done.7, bf16[8,64,2048]{2,1,0:T(8,128)(2,1)S(1)} %get-tuple-element.32.refs_0_, bf16[8,64,2048]{2,1,0:T(8,128)(2,1)S(1)} %get-tuple-element.33.refs_1_, bf16[8,64,2048]{2,1,0:T(8,128)(2,1)S(1)} %get-tuple-element.36.refs_2_, ...), custom_call_target="tpu_custom_call" | custom-call | flops 1000 | bytes 1000 | tf_op jit(solution)/shard_map/weighted_values/pallas_call | solution.py:413
  56.3 0.4 collective-permute-start.25
  56.7 0.8 %collective-permute-done.25 = f32[8,256]{1,0:T(8,128)S(1)} collective-permute-done((f32[8,256]{1,0:T(8,128)S(1)}, f32[8,256]{1,0:T(8,128)S(1)}, u32[]{:S(2)}, u32[]{:S(2)}) %collective-permute-start.25) | collective-permute-done | bytes 8224 | tf_op jit(solution)/shard_map/ppermute | solution.py:43
  57.5 0.5 collective-permute-start.26
  58.1 3.1 %collective-permute-done.26 = f32[8,256]{1,0:T(8,128)S(1)} collective-permute-done((f32[8,256]{1,0:T(8,128)S(1)}, f32[8,256]{1,0:T(8,128)S(1)}, u32[]{:S(2)}, u32[]{:S(2)}) %collective-permute-start.26) | collective-permute-done | bytes 8224 | tf_op jit(solution)/shard_map/ppermute | solution.py:43
  61.2 0.5 collective-permute-start.27
  61.7 3.1 %collective-permute-done.27.other_ref = f32[8,256]{1,0:T(8,128)S(1)} collective-permute-done((f32[8,256]{1,0:T(8,128)S(1)}, f32[8,256]{1,0:T(8,128)S(1)}, u32[]{:S(2)}, u32[]{:S(2)}) %collective-permute-start.27) | collective-permute-done | bytes 8224 | tf_op jit(solution)/shard_map/ppermute | solution.py:43
  64.8 0.6 output_products.1
  65.5 1.6 %collective-permute-start.28 = (f32[2,2048]{1,0:T(2,128)S(1)}, f32[2,2048]{1,0:T(2,128)S(1)}, u32[]{:S(2)}, u32[]{:S(2)}) collective-permute-start(f32[2,2048]{1,0:T(2,128)S(1)} %output_products.1), channel_id=1, source_target_pairs={{0,1},{1,0},{2,3},{3,2},{4,5},{5,4},{6,7},{7,6},{8,9},{9,8},{10,11... | collective-permute-start | bytes 49160 | tf_op jit(solution)/shard_map/ppermute | solution.py:43
  67.1 2.2 %collective-permute-done.28 = f32[2,2048]{1,0:T(2,128)S(1)} collective-permute-done((f32[2,2048]{1,0:T(2,128)S(1)}, f32[2,2048]{1,0:T(2,128)S(1)}, u32[]{:S(2)}, u32[]{:S(2)}) %collective-permute-start.28) | collective-permute-done | bytes 16416 | tf_op jit(solution)/shard_map/ppermute | solution.py:43
  69.3 2.7 %collective-permute-start.29 = (f32[2,2048]{1,0:T(2,128)S(1)}, f32[2,2048]{1,0:T(2,128)S(1)}, u32[]{:S(2)}, u32[]{:S(2)}) collective-permute-start(f32[2,2048]{1,0:T(2,128)S(1)} %add.66), channel_id=1, source_target_pairs={{0,2},{1,3},{2,0},{3,1},{4,6},{5,7},{6,4},{7,5},{8,10},{9,11},{10,... | collective-permute-start | bytes 49160 | tf_op jit(solution)/shard_map/ppermute | solution.py:43
  71.9 2.0 %collective-permute-done.29 = f32[2,2048]{1,0:T(2,128)S(1)} collective-permute-done((f32[2,2048]{1,0:T(2,128)S(1)}, f32[2,2048]{1,0:T(2,128)S(1)}, u32[]{:S(2)}, u32[]{:S(2)}) %collective-permute-start.29) | collective-permute-done | bytes 16416 | tf_op jit(solution)/shard_map/ppermute | solution.py:43
  74.0 0.6 add_add_fusion
  (45 shorter events, 0.2 us)
Async XLA Ops:
  0.0 5.4 %collective-permute-start.1 = (bf16[2048,128]{1,0:T(8,128)(2,1)}, bf16[2048,128]{1,0:T(8,128)(2,1)S(1)}, u32[]{:S(2)}, u32[]{:S(2)}) collective-permute-start(bf16[2048,128]{1,0:T(8,128)(2,1)} %bitcast.23), channel_id=1, source_target_pairs={{0,4},{4,0},{8,12},{12,8},{16,20},{20,16},{24,28},{28,24},{1,5},{5... | collective-permute-start | bytes 1572872 | tf_op jit(solution)/shard_map/ppermute | solution.py:43
  0.5 5.0 %collective-permute-start.2 = (bf16[2048,128]{1,0:T(8,128)(2,1)}, bf16[2048,128]{1,0:T(8,128)(2,1)S(1)}, u32[]{:S(2)}, u32[]{:S(2)}) collective-permute-start(bf16[2048,128]{1,0:T(8,128)(2,1)} %bitcast.27), channel_id=1, source_target_pairs={{0,4},{4,0},{8,12},{12,8},{16,20},{20,16},{24,28},{28,24},{1,5},{5... | collective-permute-start | bytes 1572872 | tf_op jit(solution)/shard_map/ppermute | solution.py:43
  0.5 10.6 %collective-permute-start.5 = (bf16[2048,128]{1,0:T(8,128)(2,1)}, bf16[2048,128]{1,0:T(8,128)(2,1)S(1)}, u32[]{:S(2)}, u32[]{:S(2)}) collective-permute-start(bf16[2048,128]{1,0:T(8,128)(2,1)} %bitcast.24), channel_id=1, source_target_pairs={{0,8},{4,20},{8,0},{12,28},{16,24},{20,4},{24,16},{28,12},{1,9},{5... | collective-permute-start | bytes 1572872 | tf_op jit(solution)/shard_map/ppermute | solution.py:64
  3.5 0.7 copy-start.5
  4.3 1.1 %collective-permute-start = (f32[2,128]{1,0:T(2,128)S(1)}, f32[2,128]{1,0:T(2,128)S(1)}, u32[]{:S(2)}, u32[]{:S(2)}) collective-permute-start(f32[2,128]{1,0:T(2,128)S(1)} %get-tuple-element.29), channel_id=1, source_target_pairs={{0,4},{4,0},{8,12},{12,8},{16,20},{20,16},{24,28},{28,24},{1,5},{5... | collective-permute-start | bytes 3080 | tf_op jit(solution)/shard_map/ppermute | solution.py:43
  5.4 5.6 %collective-permute-start.3 = (f32[2,128]{1,0:T(2,128)S(1)}, f32[2,128]{1,0:T(2,128)S(1)}, u32[]{:S(2)}, u32[]{:S(2)}) collective-permute-start(f32[2,128]{1,0:T(2,128)S(1)} %add.53), channel_id=1, source_target_pairs={{0,16},{4,12},{8,24},{12,4},{16,0},{20,28},{24,8},{28,20},{1,17},{... | collective-permute-start | bytes 3080 | tf_op jit(solution)/shard_map/ppermute | solution.py:64
  7.0 0.8 %copy-start.4 = (f32[1,16384]{1,0:T(1,128)S(1)}, f32[1,16384]{1,0:T(1,128)}, u32[]{:S(2)}) copy-start(f32[1,16384]{1,0:T(1,128)} %param.11) | copy-start | bytes 196612
  7.8 6.3 %copy-start.3 = (bf16[1,2048,128]{2,1,0:T(8,128)(2,1)S(1)}, bf16[1,2048,128]{2,1,0:T(8,128)(2,1)}, u32[]{:S(2)}) copy-start(bf16[1,2048,128]{2,1,0:T(8,128)(2,1)} %param.14) | copy-start | bytes 1572868
  11.1 1.2 %collective-permute-start.4 = (f32[2,128]{1,0:T(2,128)S(1)}, f32[2,128]{1,0:T(2,128)S(1)}, u32[]{:S(2)}, u32[]{:S(2)}) collective-permute-start(f32[2,128]{1,0:T(2,128)S(1)} %collective-permute-done.3), channel_id=1, source_target_pairs={{0,4},{4,0},{8,12},{12,8},{16,20},{20,16},{24,28},{28,24},{1,5},{5... | collective-permute-start | bytes 3080 | tf_op jit(solution)/shard_map/ppermute | solution.py:43
  12.3 1.9 %collective-permute-start.6 = (bf16[2048,128]{1,0:T(8,128)(2,1)S(1)}, bf16[2048,128]{1,0:T(8,128)(2,1)S(1)}, u32[]{:S(2)}, u32[]{:S(2)}) collective-permute-start(bf16[2048,128]{1,0:T(8,128)(2,1)S(1)} %collective-permute-done.5.refs_5_), channel_id=1, source_target_pairs={{0,4},{4,0},{8,12},{12,8},{16,20},{20,16},{24,28},{28,24},{1,5},{5... | collective-permute-start | bytes 1572872 | tf_op jit(solution)/shard_map/ppermute | solution.py:43
  12.5 9.2 %collective-permute-start.9 = (bf16[2048,128]{1,0:T(8,128)(2,1)S(1)}, bf16[2048,128]{1,0:T(8,128)(2,1)S(1)}, u32[]{:S(2)}, u32[]{:S(2)}) collective-permute-start(bf16[2048,128]{1,0:T(8,128)(2,1)S(1)} %collective-permute-done.1.refs_6_), channel_id=1, source_target_pairs={{0,8},{4,20},{8,0},{12,28},{16,24},{20,4},{24,16},{28,12},{1,9},{5... | collective-permute-start | bytes 1572872 | tf_op jit(solution)/shard_map/ppermute | solution.py:64
  14.2 13.1 %collective-permute-start.7 = (bf16[2048,128]{1,0:T(8,128)(2,1)S(1)}, bf16[2048,128]{1,0:T(8,128)(2,1)S(1)}, u32[]{:S(2)}, u32[]{:S(2)}) collective-permute-start(bf16[2048,128]{1,0:T(8,128)(2,1)S(1)} %bitcast.28), channel_id=1, source_target_pairs={{0,8},{4,20},{8,0},{12,28},{16,24},{20,4},{24,16},{28,12},{1,9},{5... | collective-permute-start | bytes 1572872 | tf_op jit(solution)/shard_map/ppermute | solution.py:64
  14.8 5.8 %collective-permute-start.8 = (f32[2,128]{1,0:T(2,128)S(1)}, f32[2,128]{1,0:T(2,128)S(1)}, u32[]{:S(2)}, u32[]{:S(2)}) collective-permute-start(f32[2,128]{1,0:T(2,128)S(1)} %collective-permute-done.4), channel_id=1, source_target_pairs={{0,16},{4,12},{8,24},{12,4},{16,0},{20,28},{24,8},{28,20},{1,17},{... | collective-permute-start | bytes 3080 | tf_op jit(solution)/shard_map/ppermute | solution.py:64
  16.3 5.3 %copy-start = (bf16[1,2048,1024]{2,1,0:T(8,128)(2,1)S(1)}, bf16[1,2048,1024]{2,1,0:T(8,128)(2,1)}, u32[]{:S(2)}) copy-start(bf16[1,2048,1024]{2,1,0:T(8,128)(2,1)} %param.12) | copy-start | bytes 12582916
  16.3 5.3 %copy-start.2 = (bf16[1,2048,128]{2,1,0:T(8,128)(2,1)S(1)}, bf16[1,2048,128]{2,1,0:T(8,128)(2,1)}, u32[]{:S(2)}) copy-start(bf16[1,2048,128]{2,1,0:T(8,128)(2,1)} %param.13) | copy-start | bytes 1572868
  21.6 12.6 %copy-start.8 = (s32[2]{0:T(128)S(1)}, s32[2]{0:T(128)}, u32[]{:S(2)}) copy-start(s32[2]{0:T(128)} %param.17) | copy-start | bytes 28
  22.5 1.2 %collective-permute-start.10 = (f32[2,10,128]{2,1,0:T(8,128)S(1)}, f32[2,10,128]{2,1,0:T(8,128)S(1)}, u32[]{:S(2)}, u32[]{:S(2)}) collective-permute-start(f32[2,10,128]{2,1,0:T(8,128)S(1)} %query_products.1), channel_id=1, source_target_pairs={{0,4},{4,0},{8,12},{12,8},{16,20},{20,16},{24,28},{28,24},{1,5},{5... | collective-permute-start | bytes 30728 | tf_op jit(solution)/shard_map/ppermute | solution.py:43
  22.5 10.5 %collective-permute-start.13 = (bf16[2048,128]{1,0:T(8,128)(2,1)S(1)}, bf16[2048,128]{1,0:T(8,128)(2,1)S(1)}, u32[]{:S(2)}, u32[]{:S(2)}) collective-permute-start(bf16[2048,128]{1,0:T(8,128)(2,1)S(1)} %collective-permute-done.2.refs_6_), channel_id=1, source_target_pairs={{0,8},{4,20},{8,0},{12,28},{16,24},{20,4},{24,16},{28,12},{1,9},{5... | collective-permute-start | bytes 1572872 | tf_op jit(solution)/shard_map/ppermute | solution.py:64
  27.3 5.8 %collective-permute-start.11 = (bf16[2048,128]{1,0:T(8,128)(2,1)S(1)}, bf16[2048,128]{1,0:T(8,128)(2,1)S(1)}, u32[]{:S(2)}, u32[]{:S(2)}) collective-permute-start(bf16[2048,128]{1,0:T(8,128)(2,1)S(1)} %collective-permute-done.7.refs_5_), channel_id=1, source_target_pairs={{0,4},{4,0},{8,12},{12,8},{16,20},{20,16},{24,28},{28,24},{1,5},{5... | collective-permute-start | bytes 1572872 | tf_op jit(solution)/shard_map/ppermute | solution.py:43
  27.3 11.5 %collective-permute-start.16 = (bf16[2048,128]{1,0:T(8,128)(2,1)S(1)}, bf16[2048,128]{1,0:T(8,128)(2,1)S(1)}, u32[]{:S(2)}, u32[]{:S(2)}) collective-permute-start(bf16[2048,128]{1,0:T(8,128)(2,1)S(1)} %collective-permute-done.6.refs_7_), channel_id=1, source_target_pairs={{0,8},{4,20},{8,0},{12,28},{16,24},{20,4},{24,16},{28,12},{1,9},{5... | collective-permute-start | bytes 1572872 | tf_op jit(solution)/shard_map/ppermute | solution.py:64
  27.9 6.3 %collective-permute-start.19 = (f32[2,10,128]{2,1,0:T(8,128)S(1)}, f32[2,10,128]{2,1,0:T(8,128)S(1)}, u32[]{:S(2)}, u32[]{:S(2)}) collective-permute-start(f32[2,10,128]{2,1,0:T(8,128)S(1)} %add.57), channel_id=1, source_target_pairs={{0,16},{4,12},{8,24},{12,4},{16,0},{20,28},{24,8},{28,20},{1,17},{... | collective-permute-start | bytes 30728 | tf_op jit(solution)/shard_map/ppermute | solution.py:64
  33.1 7.5 %collective-permute-start.14 = (bf16[2048,128]{1,0:T(8,128)(2,1)S(1)}, bf16[2048,128]{1,0:T(8,128)(2,1)S(1)}, u32[]{:S(2)}, u32[]{:S(2)}) collective-permute-start(bf16[2048,128]{1,0:T(8,128)(2,1)S(1)} %collective-permute-done.13.refs_6_), channel_id=1, source_target_pairs={{0,4},{4,0},{8,12},{12,8},{16,20},{20,16},{24,28},{28,24},{1,5},{5... | collective-permute-start | bytes 1572872 | tf_op jit(solution)/shard_map/ppermute | solution.py:43
  33.1 11.4 %collective-permute-start.12 = (bf16[2048,128]{1,0:T(8,128)(2,1)S(1)}, bf16[2048,128]{1,0:T(8,128)(2,1)S(1)}, u32[]{:S(2)}, u32[]{:S(2)}) collective-permute-start(bf16[2048,128]{1,0:T(8,128)(2,1)S(1)} %collective-permute-done.11.refs_7_), channel_id=1, source_target_pairs={{0,8},{4,20},{8,0},{12,28},{16,24},{20,4},{24,16},{28,12},{1,9},{5... | collective-permute-start | bytes 1572872 | tf_op jit(solution)/shard_map/ppermute | solution.py:64
  34.3 1.2 %collective-permute-start.20 = (f32[2,10,128]{2,1,0:T(8,128)S(1)}, f32[2,10,128]{2,1,0:T(8,128)S(1)}, u32[]{:S(2)}, u32[]{:S(2)}) collective-permute-start(f32[2,10,128]{2,1,0:T(8,128)S(1)} %collective-permute-done.19), channel_id=1, source_target_pairs={{0,4},{4,0},{8,12},{12,8},{16,20},{20,16},{24,28},{28,24},{1,5},{5... | collective-permute-start | bytes 30728 | tf_op jit(solution)/shard_map/ppermute | solution.py:43
  34.6 9.9 %collective-permute-start.18 = (bf16[2048,128]{1,0:T(8,128)(2,1)S(1)}, bf16[2048,128]{1,0:T(8,128)(2,1)S(1)}, u32[]{:S(2)}, u32[]{:S(2)}) collective-permute-start(bf16[2048,128]{1,0:T(8,128)(2,1)S(1)} %collective-permute-done.9.refs_6_), channel_id=1, source_target_pairs={{0,4},{4,0},{8,12},{12,8},{16,20},{20,16},{24,28},{28,24},{1,5},{5... | collective-permute-start | bytes 1572872 | tf_op jit(solution)/shard_map/ppermute | solution.py:43
  35.5 8.9 %collective-permute-start.21 = (f32[2,10,128]{2,1,0:T(8,128)S(1)}, f32[2,10,128]{2,1,0:T(8,128)S(1)}, u32[]{:S(2)}, u32[]{:S(2)}) collective-permute-start(f32[2,10,128]{2,1,0:T(8,128)S(1)} %collective-permute-done.20), channel_id=1, source_target_pairs={{0,16},{4,12},{8,24},{12,4},{16,0},{20,28},{24,8},{28,20},{1,17},{... | collective-permute-start | bytes 30728 | tf_op jit(solution)/shard_map/ppermute | solution.py:64
  38.8 7.2 %collective-permute-start.17 = (bf16[2048,128]{1,0:T(8,128)(2,1)S(1)}, bf16[2048,128]{1,0:T(8,128)(2,1)S(1)}, u32[]{:S(2)}, u32[]{:S(2)}) collective-permute-start(bf16[2048,128]{1,0:T(8,128)(2,1)S(1)} %collective-permute-done.16.refs_5_), channel_id=1, source_target_pairs={{0,4},{4,0},{8,12},{12,8},{16,20},{20,16},{24,28},{28,24},{1,5},{5... | collective-permute-start | bytes 1572872 | tf_op jit(solution)/shard_map/ppermute | solution.py:43
  44.5 10.3 %collective-permute-start.15 = (bf16[2048,128]{1,0:T(8,128)(2,1)S(1)}, bf16[2048,128]{1,0:T(8,128)(2,1)S(1)}, u32[]{:S(2)}, u32[]{:S(2)}) collective-permute-start(bf16[2048,128]{1,0:T(8,128)(2,1)S(1)} %collective-permute-done.12.refs_5_), channel_id=1, source_target_pairs={{0,4},{4,0},{8,12},{12,8},{16,20},{20,16},{24,28},{28,24},{1,5},{5... | collective-permute-start | bytes 1572872 | tf_op jit(solution)/shard_map/ppermute | solution.py:43
  46.1 0.9 %copy-start.7 = (s32[2]{0:T(128)S(1)}, s32[2]{0:T(128)}, u32[]{:S(2)}) copy-start(s32[2]{0:T(128)} %lengths_ref.3) | copy-start | bytes 28
  48.0 1.3 %collective-permute-start.22 = (f32[8,128]{1,0:T(8,128)S(1)}, f32[8,128]{1,0:T(8,128)S(1)}, u32[]{:S(2)}, u32[]{:S(2)}) collective-permute-start(f32[8,128]{1,0:T(8,128)S(1)} %get-tuple-element.51), channel_id=1, source_target_pairs={{0,4},{4,0},{8,12},{12,8},{16,20},{20,16},{24,28},{28,24},{1,5},{5... | collective-permute-start | bytes 12296 | tf_op jit(solution)/shard_map/ppermute | solution.py:43
  49.3 0.7 collective-permute-start.23
  50.0 4.8 %collective-permute-start.24 = (f32[8,128]{1,0:T(8,128)S(1)}, f32[8,128]{1,0:T(8,128)S(1)}, u32[]{:S(2)}, u32[]{:S(2)}) collective-permute-start(f32[8,128]{1,0:T(8,128)S(1)} %max.7), channel_id=1, source_target_pairs={{0,4},{4,0},{8,12},{12,8},{16,20},{20,16},{24,28},{28,24},{1,5},{5... | collective-permute-start | bytes 12296 | tf_op jit(solution)/shard_map/ppermute | solution.py:43
  54.8 10.0 %copy-start.1 = (bf16[1,1024,2048]{2,1,0:T(8,128)(2,1)S(1)}, bf16[1,1024,2048]{2,1,0:T(8,128)(2,1)}, u32[]{:S(2)}) copy-start(bf16[1,1024,2048]{2,1,0:T(8,128)(2,1)} %param.15) | copy-start | bytes 12582916
  56.3 1.2 %collective-permute-start.25 = (f32[8,256]{1,0:T(8,128)S(1)}, f32[8,256]{1,0:T(8,128)S(1)}, u32[]{:S(2)}, u32[]{:S(2)}) collective-permute-start(f32[8,256]{1,0:T(8,128)S(1)} %weighted_values.1), channel_id=1, source_target_pairs={{0,4},{4,0},{8,12},{12,8},{16,20},{20,16},{24,28},{28,24},{1,5},{5... | collective-permute-start | bytes 24584 | tf_op jit(solution)/shard_map/ppermute | solution.py:43
  57.5 3.7 %collective-permute-start.26 = (f32[8,256]{1,0:T(8,128)S(1)}, f32[8,256]{1,0:T(8,128)S(1)}, u32[]{:S(2)}, u32[]{:S(2)}) collective-permute-start(f32[8,256]{1,0:T(8,128)S(1)} %add.64), channel_id=1, source_target_pairs={{0,8},{4,12},{8,0},{12,4},{16,24},{20,28},{24,16},{28,20},{1,9},{5... | collective-permute-start | bytes 24584 | tf_op jit(solution)/shard_map/ppermute | solution.py:43
  61.2 3.7 %collective-permute-start.27 = (f32[8,256]{1,0:T(8,128)S(1)}, f32[8,256]{1,0:T(8,128)S(1)}, u32[]{:S(2)}, u32[]{:S(2)}) collective-permute-start(f32[8,256]{1,0:T(8,128)S(1)} %add.65.mine_ref), channel_id=1, source_target_pairs={{0,16},{4,20},{8,24},{12,28},{16,0},{20,4},{24,8},{28,12},{1,17},{... | collective-permute-start | bytes 24584 | tf_op jit(solution)/shard_map/ppermute | solution.py:43
  64.8 9.1 %copy-start.6 = (f32[2,2048]{1,0:T(2,128)S(1)}, f32[2,2048]{1,0:T(2,128)}, u32[]{:S(2)}) copy-start(f32[2,2048]{1,0:T(2,128)} %tokens_ref.3) | copy-start | bytes 49156
  65.5 3.8 %collective-permute-start.28 = (f32[2,2048]{1,0:T(2,128)S(1)}, f32[2,2048]{1,0:T(2,128)S(1)}, u32[]{:S(2)}, u32[]{:S(2)}) collective-permute-start(f32[2,2048]{1,0:T(2,128)S(1)} %output_products.1), channel_id=1, source_target_pairs={{0,1},{1,0},{2,3},{3,2},{4,5},{5,4},{6,7},{7,6},{8,9},{9,8},{10,11... | collective-permute-start | bytes 49160 | tf_op jit(solution)/shard_map/ppermute | solution.py:43
  69.3 4.7 %collective-permute-start.29 = (f32[2,2048]{1,0:T(2,128)S(1)}, f32[2,2048]{1,0:T(2,128)S(1)}, u32[]{:S(2)}, u32[]{:S(2)}) collective-permute-start(f32[2,2048]{1,0:T(2,128)S(1)} %add.66), channel_id=1, source_target_pairs={{0,2},{1,3},{2,0},{3,1},{4,6},{5,7},{6,4},{7,5},{8,10},{9,11},{10,... | collective-permute-start | bytes 49160 | tf_op jit(solution)/shard_map/ppermute | solution.py:43

commit v7 on v6

--- a/solution.py
+++ b/solution.py
@@ -359,14 +359,12 @@
     if split:
         squares, told = sum_chips(squares, row_count // NORM_ROWS // 2)
         key_shared = share(key_far, told)
-        squares = after(squares, key_far[1][1])
+        squares = after(squares, key_far[1][1], key_shared[0][1])
     else:
         key_shared = share(key_far)
         squares = beside(squares, squares, row_count // NORM_ROWS)
         squares = butterfly(squares, "ctx", chip_bits, jnp.add)
     key_last = send_last(key_weight[0], key_shared)
-    own_values = after(value_weight[0], *[block for _, block in key_shared[:1]])
-    value_far = send_first(own_values, value_partner)
 
     parts = call(
         functools.partial(query_kernel, features),
@@ -376,6 +374,7 @@
     )(places, squares, new_tokens, gains, query_weight[0], key_weight[0], value_weight[0])
     parts = parts + swap(parts, "ctx", 1)
     parts_sent = parts
+    value_far = send_first(value_weight[0], after(value_partner, parts))
     if split:
         parts, _ = sum_chips(parts)
         summed = jnp.where(own_request == 0, parts[0], parts[1])
@@ -388,10 +387,6 @@
     key_total = project(places, rows, key_near)
     key_total = project(places, rows, key_far + key_shared, key_total)
     key_total = project(places, rows, key_last + share(key_last), key_total)
-    value_total = project(places, rows, value_near)
-    value_shared = share(value_far, parts_sent)
-    value_last = send_last(own_values, value_shared)
-    value_total = project(places, rows, value_far + value_shared, value_total)
 
     within = first_row[0, :1] + jnp.arange(row_count, dtype=jnp.int32)
     cosine, sine_part = tables(within.astype(jnp.float32), head_size)
@@ -402,12 +397,14 @@
         [IN_SMEM] * 2 + [IN_VMEM] * 6,
         (shape((heads, row_count)), shape((heads, LANES)), shape((heads, LANES))),
     )(places, lengths, key_total, cosine, sine_part, new_cosine, new_sine, summed)
-    if split:
-        top = jnp.maximum(top, swap(top, "ctx", 1))
-        top = jnp.maximum(top, by_core(top, 0, 2))
-        top = jnp.where(core == 0, swap(top, "ctx", 1), top)
-    else:
-        top = butterfly(top, "ctx", bits_below(team), jnp.maximum)
+    top = butterfly(top, "ctx", [1], jnp.maximum)
+    near_top = top
+    top = butterfly(top, "ctx", bits_below(team)[1:], jnp.maximum)
+
+    value_shared = share(value_far, parts_sent)
+    value_last = send_last(value_weight[0], value_shared)
+    value_total = project(after(places, near_top), rows, value_near)
+    value_total = project(after(places, top), rows, value_far + value_shared, value_total)
 
     blocks = value_last + share(value_last, value_total)
     packed = call(

time: 74.8 us -> 70.8 us (0.947)
  starting transfers between devices: 24 us -> 20.8 us
    ppermute x11 -> x10, starting transfers between devices: 12.4 us -> 10.4 us  [by_core(): return lax.ppermute(value, 'ctx', pairs)]
    ppermute x19, starting transfers between devices: 11.7 us -> 10.4 us  [swap(): return lax.ppermute(value, axis, [(i, i ^ distance) for i in range(count)])]
    ppermute x19, waiting for transfers between devices: 17.5 us -> 16.5 us  [swap(): return lax.ppermute(value, axis, [(i, i ^ distance) for i in range(count)])]
    ppermute x11 -> x10, waiting for transfers between devices: 12.5 us -> 12.7 us  [by_core(): return lax.ppermute(value, 'ctx', pairs)]
  transfers between devices with their start and end apart: 30 -> 29, of which waited for: 17 -> 16; matrix products, arithmetic and copies ran while one was open for 1% -> 1% of each run, Pallas kernels for 20% -> 21%
where the time goes in v7:
time: 70.8 us; the launch traced here: 70.6 us
  waiting for transfers between devices  29.3 us (41%)
  starting transfers between devices  20.8 us (29%)
  Pallas kernels  17.2 us (24%)
  local copies, waits for them, and re-layouts  1.59 us (2%)
  other arithmetic  1.48 us (2%)
    ppermute x19, waiting for transfers between devices, swap(): return lax.ppermute(value, axis, [(i, i ^ distance) for i in range(count)])  16.5 us
    ppermute x10, waiting for transfers between devices, by_core(): return lax.ppermute(value, 'ctx', pairs)  12.7 us
    ppermute x19, starting transfers between devices, swap(): return lax.ppermute(value, axis, [(i, i ^ distance) for i in range(count)])  10.4 us
    ppermute x10, starting transfers between devices, by_core(): return lax.ppermute(value, 'ctx', pairs)  10.4 us
    pallas_call x2, Pallas kernels, normalise(): call(functools.partial(norm_kernel, first), 'normalise', [IN_HBM, IN_VMEM...  7.47 us
    pallas_call x5, Pallas kernels, project(): call(functools.partial(project_kernel, [d for d, _ in blocks], len(rows),...  5.66 us
    unnamed x18, local copies, waits for them, and re-layouts  1.59 us
    pallas_call x1, Pallas kernels, shards(): call(functools.partial(weigh_kernel, [d for d, _ in blocks], len(rows), t...  1.52 us
  transfers between devices with their start and end apart: 29, of which 16 were waited for; matrix products, arithmetic and copies ran while one was open for 1% of the time, Pallas kernels for 21%

profile of v7, /device:TPU:0, one launch (start us, length us, event | category | flops | bytes accessed | tf_op | source)
XLA Modules:
  0.0 70.6 jit_solution(11360269887226854615)
XLA Ops:
  0.0 0.5 collective-permute-start.1
  0.5 0.1 collective-permute-start.2
  0.5 2.9 %collective-permute-start.8 = (bf16[2048,128]{1,0:T(8,128)(2,1)}, bf16[2048,128]{1,0:T(8,128)(2,1)S(1)}, u32[]{:S(2)}, u32[]{:S(2)}) collective-permute-start(bf16[2048,128]{1,0:T(8,128)(2,1)} %bitcast.24), channel_id=1, source_target_pairs={{0,8},{4,20},{8,0},{12,28},{16,24},{20,4},{24,16},{28,12},{1,9},{5... | collective-permute-start | bytes 1572872 | tf_op jit(solution)/shard_map/ppermute | solution.py:64
  3.5 0.7 %copy-done.5 = f32[2,2048]{1,0:T(2,128)S(1)} copy-done((f32[2,2048]{1,0:T(2,128)S(1)}, f32[2,2048]{1,0:T(2,128)}, u32[]{:S(2)}) %copy-start.5) | copy-done | bytes 16408
  4.2 0.1 squares.1
  4.3 0.0 collective-permute-start
  4.3 1.1 %collective-permute-done = f32[2,128]{1,0:T(2,128)S(1)} collective-permute-done((f32[2,128]{1,0:T(2,128)S(1)}, f32[2,128]{1,0:T(2,128)S(1)}, u32[]{:S(2)}, u32[]{:S(2)}) %collective-permute-start) | collective-permute-done | bytes 1056 | tf_op jit(solution)/shard_map/ppermute | solution.py:43
  5.4 0.0 collective-permute-done.1.refs_6_
  5.4 0.0 collective-permute-done.2.refs_6_
  5.4 1.6 %collective-permute-start.3 = (f32[2,128]{1,0:T(2,128)S(1)}, f32[2,128]{1,0:T(2,128)S(1)}, u32[]{:S(2)}, u32[]{:S(2)}) collective-permute-start(f32[2,128]{1,0:T(2,128)S(1)} %add.53), channel_id=1, source_target_pairs={{0,16},{4,12},{8,24},{12,4},{16,0},{20,28},{24,8},{28,20},{1,17},{... | collective-permute-start | bytes 3080 | tf_op jit(solution)/shard_map/ppermute | solution.py:64
  7.0 0.8 %copy-done.4 = f32[1,16384]{1,0:T(1,128)S(1)} copy-done((f32[1,16384]{1,0:T(1,128)S(1)}, f32[1,16384]{1,0:T(1,128)}, u32[]{:S(2)}) %copy-start.4) | copy-done | bytes 65560
  7.8 3.2 %normalise.2 = (bf16[8,64,2048]{2,1,0:T(8,128)(2,1)S(1)}, bf16[8,64,2048]{2,1,0:T(8,128)(2,1)S(1)}) custom-call(bf16[320,16384]{1,0:T(8,128)(2,1)} %bitcast.35, f32[8,1,2048]{2,1,0:T(1,128)S(1)} %bitcast.31), custom_call_target="tpu_custom_call" | custom-call | flops 1000 | bytes 1000 | tf_op jit(solution)/shard_map/normalise/pallas_call | solution.py:173
  11.0 0.0 collective-permute-done.3
  11.0 0.1 collective-permute-start.4
  11.1 0.6 collective-permute-start.7
  11.7 0.5 collective-permute-done.4
  12.3 0.2 collective-permute-start.9
  12.4 0.9 %collective-permute-start.5 = (bf16[2048,128]{1,0:T(8,128)(2,1)S(1)}, bf16[2048,128]{1,0:T(8,128)(2,1)S(1)}, u32[]{:S(2)}, u32[]{:S(2)}) collective-permute-start(bf16[2048,128]{1,0:T(8,128)(2,1)S(1)} %bitcast.28), channel_id=1, source_target_pairs={{0,8},{4,20},{8,0},{12,28},{16,24},{20,4},{24,16},{28,12},{1,9},{5... | collective-permute-start | bytes 1572872 | tf_op jit(solution)/shard_map/ppermute | solution.py:64
  13.3 1.1 %collective-permute-start.6 = (f32[2,128]{1,0:T(2,128)S(1)}, f32[2,128]{1,0:T(2,128)S(1)}, u32[]{:S(2)}, u32[]{:S(2)}) collective-permute-start(f32[2,128]{1,0:T(2,128)S(1)} %collective-permute-done.4), channel_id=1, source_target_pairs={{0,16},{4,12},{8,24},{12,4},{16,0},{20,28},{24,8},{28,20},{1,17},{... | collective-permute-start | bytes 3080 | tf_op jit(solution)/shard_map/ppermute | solution.py:64
  14.5 4.3 %normalise.3 = (bf16[8,64,2048]{2,1,0:T(8,128)(2,1)S(1)}, bf16[8,64,2048]{2,1,0:T(8,128)(2,1)S(1)}, bf16[8,64,2048]{2,1,0:T(8,128)(2,1)S(1)}) custom-call(bf16[320,16384]{1,0:T(8,128)(2,1)} %bitcast.36, f32[8,1,2048]{2,1,0:T(1,128)S(1)} %bitcast.32), custom_call_target="tpu_custom_call" | custom-call | flops 1000 | bytes 1000 | tf_op jit(solution)/shard_map/normalise/pallas_call | solution.py:173
  18.8 1.6 %collective-permute-done.7.refs_6_ = bf16[2048,128]{1,0:T(8,128)(2,1)S(1)} collective-permute-done((bf16[2048,128]{1,0:T(8,128)(2,1)S(1)}, bf16[2048,128]{1,0:T(8,128)(2,1)S(1)}, u32[]{:S(2)}, u32[]{:S(2)}) %collective-permute-start.7) | collective-permute-done | bytes 524320 | tf_op jit(solution)/shard_map/ppermute | solution.py:64
  20.4 0.0 copy-start.8
  20.4 0.8 %query_products.1 = f32[2,10,128]{2,1,0:T(8,128)S(1)} custom-call(s32[1]{0:T(128)} %bitcast.place_ref, f32[2,128]{1,0:T(2,128)S(1)} %add_add_fusion.2.squares_ref, f32[2,2048]{1,0:T(2,128)S(1)} %copy-done.5, f32[8,1,2048]{2,1,0:T(1,128)S(1)} %bitcast.33, bf16[2048,1024]{1,0:T(8,128)(2,1)S(1)} %bitcast.21, bf16[2048,128]{1,0:T(8,128)(2,1)S(1)} %bitcast.25, ...), custom_call_target="tpu_custom_call" | custom-call | flops 1000 | bytes 1000 | tf_op jit(solution)/shard_map/query_products/pallas_call | solution.py:369
  21.2 0.1 collective-permute-start.10
  21.4 0.6 collective-permute-start.13
  22.0 0.5 collective-permute-done.10
  22.5 1.0 %collective-permute-start.21 = (bf16[2048,128]{1,0:T(8,128)(2,1)S(1)}, bf16[2048,128]{1,0:T(8,128)(2,1)S(1)}, u32[]{:S(2)}, u32[]{:S(2)}) collective-permute-start(bf16[2048,128]{1,0:T(8,128)(2,1)S(1)} %collective-permute-done.2.refs_6_), channel_id=1, source_target_pairs={{0,8},{4,20},{8,0},{12,28},{16,24},{20,4},{24,16},{28,12},{1,9},{5... | collective-permute-start | bytes 1572872 | tf_op jit(solution)/shard_map/ppermute | solution.py:64
  23.5 2.5 %collective-permute-done.5.refs_5_ = bf16[2048,128]{1,0:T(8,128)(2,1)S(1)} collective-permute-done((bf16[2048,128]{1,0:T(8,128)(2,1)S(1)}, bf16[2048,128]{1,0:T(8,128)(2,1)S(1)}, u32[]{:S(2)}, u32[]{:S(2)}) %collective-permute-start.5) | collective-permute-done | bytes 524320 | tf_op jit(solution)/shard_map/ppermute | solution.py:64
  26.0 0.6 collective-permute-start.16
  26.6 0.6 multiply_sine_fusion
  27.3 2.8 %collective-permute-done.16 = f32[2,10,128]{2,1,0:T(8,128)S(1)} collective-permute-done((f32[2,10,128]{2,1,0:T(8,128)S(1)}, f32[2,10,128]{2,1,0:T(8,128)S(1)}, u32[]{:S(2)}, u32[]{:S(2)}) %collective-permute-start.16) | collective-permute-done | bytes 10272 | tf_op jit(solution)/shard_map/ppermute | solution.py:64
  30.1 0.1 multiply_sine_fusion.1
  30.2 0.6 collective-permute-start.15
  30.7 0.5 collective-permute-done.17
  31.2 0.5 collective-permute-start.18
  31.8 0.0 collective-permute-done.13.refs_5_
  31.8 5.8 %collective-permute-done.21.refs_6_ = bf16[2048,128]{1,0:T(8,128)(2,1)S(1)} collective-permute-done((bf16[2048,128]{1,0:T(8,128)(2,1)S(1)}, bf16[2048,128]{1,0:T(8,128)(2,1)S(1)}, u32[]{:S(2)}, u32[]{:S(2)}) %collective-permute-start.21) | collective-permute-done | bytes 524320 | tf_op jit(solution)/shard_map/ppermute | solution.py:64
  37.6 0.5 collective-permute-start.12
  38.1 0.9 %project.5.refs_9_ = f32[320,128]{1,0:T(8,128)S(1)} custom-call(s32[1]{0:T(128)} %bitcast.place_ref, bf16[8,64,2048]{2,1,0:T(8,128)(2,1)S(1)} %get-tuple-element.34.refs_0_, bf16[8,64,2048]{2,1,0:T(8,128)(2,1)S(1)} %get-tuple-element.35.refs_1_, bf16[8,64,2048]{2,1,0:T(8,128)(2,1)S(1)} %get-tuple-element.38.refs_2_, ...), custom_call_target="tpu_custom_call" | custom-call | flops 1000 | bytes 1000 | tf_op jit(solution)/shard_map/project/pallas_call | solution.py:218
  39.1 1.5 %project.6.refs_7_ = f32[320,128]{1,0:T(8,128)S(1)} custom-call(s32[1]{0:T(128)} %bitcast.place_ref, bf16[8,64,2048]{2,1,0:T(8,128)(2,1)S(1)} %get-tuple-element.34.refs_0_, bf16[8,64,2048]{2,1,0:T(8,128)(2,1)S(1)} %get-tuple-element.35.refs_1_, bf16[8,64,2048]{2,1,0:T(8,128)(2,1)S(1)} %get-tuple-element.38.refs_2_, ...), custom_call_target="tpu_custom_call" | custom-call | flops 1000 | bytes 1000 | tf_op jit(solution)/shard_map/project/pallas_call | solution.py:218
  40.6 0.0 copy-start.7
  40.6 0.9 %project.7.refs_0_ = f32[320,128]{1,0:T(8,128)S(1)} custom-call(s32[1]{0:T(128)} %bitcast.place_ref, bf16[8,64,2048]{2,1,0:T(8,128)(2,1)S(1)} %get-tuple-element.34.refs_0_, bf16[8,64,2048]{2,1,0:T(8,128)(2,1)S(1)} %get-tuple-element.35.refs_1_, bf16[8,64,2048]{2,1,0:T(8,128)(2,1)S(1)} %get-tuple-element.38.refs_2_, ...), custom_call_target="tpu_custom_call" | custom-call | flops 1000 | bytes 1000 | tf_op jit(solution)/shard_map/project/pallas_call | solution.py:218
  41.5 1.0 %scores.1 = (f32[8,320]{1,0:T(8,128)S(1)}, f32[8,128]{1,0:T(8,128)S(1)}, f32[8,128]{1,0:T(8,128)S(1)}) custom-call(s32[1]{0:T(128)} %bitcast.place_ref, s32[2]{0:T(128)S(1)} %copy-done.7, f32[320,128]{1,0:T(8,128)S(1)} %project.7.refs_0_, f32[320,64]{1,0:T(8,128)S(1)} %get-tuple-element.58.refs_1_, f32[320,64]{1,0:T(8,128)S(1)} %get-tuple-element.57.refs_2_, ...), custom_call_target="tpu_custom_call" | custom-call | flops 1000 | bytes 1000 | tf_op jit(solution)/shard_map/scores/pallas_call | solution.py:394
  42.5 0.2 collective-permute-start.19
  42.7 1.0 %collective-permute-done.19 = f32[8,128]{1,0:T(8,128)S(1)} collective-permute-done((f32[8,128]{1,0:T(8,128)S(1)}, f32[8,128]{1,0:T(8,128)S(1)}, u32[]{:S(2)}, u32[]{:S(2)}) %collective-permute-start.19) | collective-permute-done | bytes 4128 | tf_op jit(solution)/shard_map/ppermute | solution.py:43
  43.7 1.5 %collective-permute-start.20 = (f32[8,128]{1,0:T(8,128)S(1)}, f32[8,128]{1,0:T(8,128)S(1)}, u32[]{:S(2)}, u32[]{:S(2)}) collective-permute-start(f32[8,128]{1,0:T(8,128)S(1)} %max.6), channel_id=1, source_target_pairs={{0,8},{4,12},{8,0},{12,4},{16,24},{20,28},{24,16},{28,20},{1,9},{5... | collective-permute-start | bytes 12296 | tf_op jit(solution)/shard_map/ppermute | solution.py:43
  45.2 0.9 %project.8.refs_9_ = f32[320,128]{1,0:T(8,128)S(1)} custom-call(s32[1]{0:T(128)} %bitcast.place_ref, bf16[8,64,2048]{2,1,0:T(8,128)(2,1)S(1)} %get-tuple-element.34.refs_0_, bf16[8,64,2048]{2,1,0:T(8,128)(2,1)S(1)} %get-tuple-element.35.refs_1_, bf16[8,64,2048]{2,1,0:T(8,128)(2,1)S(1)} %get-tuple-element.38.refs_2_, ...), custom_call_target="tpu_custom_call" | custom-call | flops 1000 | bytes 1000 | tf_op jit(solution)/shard_map/project/pallas_call | solution.py:218
  46.0 1.2 %collective-permute-done.20 = f32[8,128]{1,0:T(8,128)S(1)} collective-permute-done((f32[8,128]{1,0:T(8,128)S(1)}, f32[8,128]{1,0:T(8,128)S(1)}, u32[]{:S(2)}, u32[]{:S(2)}) %collective-permute-start.20) | collective-permute-done | bytes 4128 | tf_op jit(solution)/shard_map/ppermute | solution.py:43
  47.3 1.5 %project.9.refs_7_ = f32[320,128]{1,0:T(8,128)S(1)} custom-call(s32[1]{0:T(128)} %bitcast.place_ref, bf16[8,64,2048]{2,1,0:T(8,128)(2,1)S(1)} %get-tuple-element.34.refs_0_, bf16[8,64,2048]{2,1,0:T(8,128)(2,1)S(1)} %get-tuple-element.35.refs_1_, bf16[8,64,2048]{2,1,0:T(8,128)(2,1)S(1)} %get-tuple-element.38.refs_2_, ...), custom_call_target="tpu_custom_call" | custom-call | flops 1000 | bytes 1000 | tf_op jit(solution)/shard_map/project/pallas_call | solution.py:218
  48.8 0.1 collective-permute-start.23
  48.9 1.9 %collective-permute-done.23.refs_6_ = bf16[2048,128]{1,0:T(8,128)(2,1)S(1)} collective-permute-done((bf16[2048,128]{1,0:T(8,128)(2,1)S(1)}, bf16[2048,128]{1,0:T(8,128)(2,1)S(1)}, u32[]{:S(2)}, u32[]{:S(2)}) %collective-permute-start.23) | collective-permute-done | bytes 524320 | tf_op jit(solution)/shard_map/ppermute | solution.py:43
  50.8 1.5 %weighted_values.1 = f32[8,256]{1,0:T(8,128)S(1)} custom-call(s32[1]{0:T(128)} %bitcast.place_ref, s32[2]{0:T(128)S(1)} %copy-done.7, bf16[8,64,2048]{2,1,0:T(8,128)(2,1)S(1)} %get-tuple-element.34.refs_0_, bf16[8,64,2048]{2,1,0:T(8,128)(2,1)S(1)} %get-tuple-element.35.refs_1_, bf16[8,64,2048]{2,1,0:T(8,128)(2,1)S(1)} %get-tuple-element.38.refs_2_, ...), custom_call_target="tpu_custom_call" | custom-call | flops 1000 | bytes 1000 | tf_op jit(solution)/shard_map/weighted_values/pallas_call | solution.py:410
  52.3 0.2 collective-permute-start.24
  52.5 1.0 %collective-permute-done.24 = f32[8,256]{1,0:T(8,128)S(1)} collective-permute-done((f32[8,256]{1,0:T(8,128)S(1)}, f32[8,256]{1,0:T(8,128)S(1)}, u32[]{:S(2)}, u32[]{:S(2)}) %collective-permute-start.24) | collective-permute-done | bytes 8224 | tf_op jit(solution)/shard_map/ppermute | solution.py:43
  53.5 1.5 %collective-permute-start.25 = (f32[8,256]{1,0:T(8,128)S(1)}, f32[8,256]{1,0:T(8,128)S(1)}, u32[]{:S(2)}, u32[]{:S(2)}) collective-permute-start(f32[8,256]{1,0:T(8,128)S(1)} %add.64), channel_id=1, source_target_pairs={{0,8},{4,12},{8,0},{12,4},{16,24},{20,28},{24,16},{28,20},{1,9},{5... | collective-permute-start | bytes 24584 | tf_op jit(solution)/shard_map/ppermute | solution.py:43
  55.0 2.2 %collective-permute-done.25 = f32[8,256]{1,0:T(8,128)S(1)} collective-permute-done((f32[8,256]{1,0:T(8,128)S(1)}, f32[8,256]{1,0:T(8,128)S(1)}, u32[]{:S(2)}, u32[]{:S(2)}) %collective-permute-start.25) | collective-permute-done | bytes 8224 | tf_op jit(solution)/shard_map/ppermute | solution.py:43
  57.2 1.4 %collective-permute-start.26 = (f32[8,256]{1,0:T(8,128)S(1)}, f32[8,256]{1,0:T(8,128)S(1)}, u32[]{:S(2)}, u32[]{:S(2)}) collective-permute-start(f32[8,256]{1,0:T(8,128)S(1)} %add.65.mine_ref), channel_id=1, source_target_pairs={{0,16},{4,20},{8,24},{12,28},{16,0},{20,4},{24,8},{28,12},{1,17},{... | collective-permute-start | bytes 24584 | tf_op jit(solution)/shard_map/ppermute | solution.py:43
  58.6 2.3 %collective-permute-done.26.other_ref = f32[8,256]{1,0:T(8,128)S(1)} collective-permute-done((f32[8,256]{1,0:T(8,128)S(1)}, f32[8,256]{1,0:T(8,128)S(1)}, u32[]{:S(2)}, u32[]{:S(2)}) %collective-permute-start.26) | collective-permute-done | bytes 8224 | tf_op jit(solution)/shard_map/ppermute | solution.py:43
  60.9 0.6 output_products.1
  61.5 1.6 %collective-permute-start.27 = (f32[2,2048]{1,0:T(2,128)S(1)}, f32[2,2048]{1,0:T(2,128)S(1)}, u32[]{:S(2)}, u32[]{:S(2)}) collective-permute-start(f32[2,2048]{1,0:T(2,128)S(1)} %output_products.1), channel_id=1, source_target_pairs={{0,1},{1,0},{2,3},{3,2},{4,5},{5,4},{6,7},{7,6},{8,9},{9,8},{10,11... | collective-permute-start | bytes 49160 | tf_op jit(solution)/shard_map/ppermute | solution.py:43
  63.1 2.2 %collective-permute-done.27 = f32[2,2048]{1,0:T(2,128)S(1)} collective-permute-done((f32[2,2048]{1,0:T(2,128)S(1)}, f32[2,2048]{1,0:T(2,128)S(1)}, u32[]{:S(2)}, u32[]{:S(2)}) %collective-permute-start.27) | collective-permute-done | bytes 16416 | tf_op jit(solution)/shard_map/ppermute | solution.py:43
  65.3 2.6 %collective-permute-start.28 = (f32[2,2048]{1,0:T(2,128)S(1)}, f32[2,2048]{1,0:T(2,128)S(1)}, u32[]{:S(2)}, u32[]{:S(2)}) collective-permute-start(f32[2,2048]{1,0:T(2,128)S(1)} %add.66), channel_id=1, source_target_pairs={{0,2},{1,3},{2,0},{3,1},{4,6},{5,7},{6,4},{7,5},{8,10},{9,11},{10,... | collective-permute-start | bytes 49160 | tf_op jit(solution)/shard_map/ppermute | solution.py:43
  67.9 2.1 %collective-permute-done.28 = f32[2,2048]{1,0:T(2,128)S(1)} collective-permute-done((f32[2,2048]{1,0:T(2,128)S(1)}, f32[2,2048]{1,0:T(2,128)S(1)}, u32[]{:S(2)}, u32[]{:S(2)}) %collective-permute-start.28) | collective-permute-done | bytes 16416 | tf_op jit(solution)/shard_map/ppermute | solution.py:43
  70.0 0.6 add_add_fusion
  (42 shorter events, 0.2 us)
Async XLA Ops:
  0.0 5.4 %collective-permute-start.1 = (bf16[2048,128]{1,0:T(8,128)(2,1)}, bf16[2048,128]{1,0:T(8,128)(2,1)S(1)}, u32[]{:S(2)}, u32[]{:S(2)}) collective-permute-start(bf16[2048,128]{1,0:T(8,128)(2,1)} %bitcast.23), channel_id=1, source_target_pairs={{0,4},{4,0},{8,12},{12,8},{16,20},{20,16},{24,28},{28,24},{1,5},{5... | collective-permute-start | bytes 1572872 | tf_op jit(solution)/shard_map/ppermute | solution.py:43
  0.5 5.0 %collective-permute-start.2 = (bf16[2048,128]{1,0:T(8,128)(2,1)}, bf16[2048,128]{1,0:T(8,128)(2,1)S(1)}, u32[]{:S(2)}, u32[]{:S(2)}) collective-permute-start(bf16[2048,128]{1,0:T(8,128)(2,1)} %bitcast.27), channel_id=1, source_target_pairs={{0,4},{4,0},{8,12},{12,8},{16,20},{20,16},{24,28},{28,24},{1,5},{5... | collective-permute-start | bytes 1572872 | tf_op jit(solution)/shard_map/ppermute | solution.py:43
  0.5 11.2 %collective-permute-start.8 = (bf16[2048,128]{1,0:T(8,128)(2,1)}, bf16[2048,128]{1,0:T(8,128)(2,1)S(1)}, u32[]{:S(2)}, u32[]{:S(2)}) collective-permute-start(bf16[2048,128]{1,0:T(8,128)(2,1)} %bitcast.24), channel_id=1, source_target_pairs={{0,8},{4,20},{8,0},{12,28},{16,24},{20,4},{24,16},{28,12},{1,9},{5... | collective-permute-start | bytes 1572872 | tf_op jit(solution)/shard_map/ppermute | solution.py:64
  3.5 0.7 %copy-start.5 = (f32[2,2048]{1,0:T(2,128)S(1)}, f32[2,2048]{1,0:T(2,128)}, u32[]{:S(2)}) copy-start(f32[2,2048]{1,0:T(2,128)} %tokens_ref.3) | copy-start | bytes 49156
  4.3 1.1 %collective-permute-start = (f32[2,128]{1,0:T(2,128)S(1)}, f32[2,128]{1,0:T(2,128)S(1)}, u32[]{:S(2)}, u32[]{:S(2)}) collective-permute-start(f32[2,128]{1,0:T(2,128)S(1)} %get-tuple-element.31), channel_id=1, source_target_pairs={{0,4},{4,0},{8,12},{12,8},{16,20},{20,16},{24,28},{28,24},{1,5},{5... | collective-permute-start | bytes 3080 | tf_op jit(solution)/shard_map/ppermute | solution.py:43
  5.4 5.6 %collective-permute-start.3 = (f32[2,128]{1,0:T(2,128)S(1)}, f32[2,128]{1,0:T(2,128)S(1)}, u32[]{:S(2)}, u32[]{:S(2)}) collective-permute-start(f32[2,128]{1,0:T(2,128)S(1)} %add.53), channel_id=1, source_target_pairs={{0,16},{4,12},{8,24},{12,4},{16,0},{20,28},{24,8},{28,20},{1,17},{... | collective-permute-start | bytes 3080 | tf_op jit(solution)/shard_map/ppermute | solution.py:64
  7.0 0.8 %copy-start.4 = (f32[1,16384]{1,0:T(1,128)S(1)}, f32[1,16384]{1,0:T(1,128)}, u32[]{:S(2)}) copy-start(f32[1,16384]{1,0:T(1,128)} %param.11) | copy-start | bytes 196612
  7.8 4.6 %copy-start.3 = (bf16[1,2048,128]{2,1,0:T(8,128)(2,1)S(1)}, bf16[1,2048,128]{2,1,0:T(8,128)(2,1)}, u32[]{:S(2)}) copy-start(bf16[1,2048,128]{2,1,0:T(8,128)(2,1)} %param.14) | copy-start | bytes 1572868
  11.0 1.2 %collective-permute-start.4 = (f32[2,128]{1,0:T(2,128)S(1)}, f32[2,128]{1,0:T(2,128)S(1)}, u32[]{:S(2)}, u32[]{:S(2)}) collective-permute-start(f32[2,128]{1,0:T(2,128)S(1)} %collective-permute-done.3), channel_id=1, source_target_pairs={{0,4},{4,0},{8,12},{12,8},{16,20},{20,16},{24,28},{28,24},{1,5},{5... | collective-permute-start | bytes 3080 | tf_op jit(solution)/shard_map/ppermute | solution.py:43
  11.1 9.3 %collective-permute-start.7 = (bf16[2048,128]{1,0:T(8,128)(2,1)S(1)}, bf16[2048,128]{1,0:T(8,128)(2,1)S(1)}, u32[]{:S(2)}, u32[]{:S(2)}) collective-permute-start(bf16[2048,128]{1,0:T(8,128)(2,1)S(1)} %collective-permute-done.1.refs_6_), channel_id=1, source_target_pairs={{0,8},{4,20},{8,0},{12,28},{16,24},{20,4},{24,16},{28,12},{1,9},{5... | collective-permute-start | bytes 1572872 | tf_op jit(solution)/shard_map/ppermute | solution.py:64
  12.3 8.1 %collective-permute-start.9 = (bf16[2048,128]{1,0:T(8,128)(2,1)S(1)}, bf16[2048,128]{1,0:T(8,128)(2,1)S(1)}, u32[]{:S(2)}, u32[]{:S(2)}) collective-permute-start(bf16[2048,128]{1,0:T(8,128)(2,1)S(1)} %collective-permute-done.8.refs_5_), channel_id=1, source_target_pairs={{0,4},{4,0},{8,12},{12,8},{16,20},{20,16},{24,28},{28,24},{1,5},{5... | collective-permute-start | bytes 1572872 | tf_op jit(solution)/shard_map/ppermute | solution.py:43
  12.4 13.6 %collective-permute-start.5 = (bf16[2048,128]{1,0:T(8,128)(2,1)S(1)}, bf16[2048,128]{1,0:T(8,128)(2,1)S(1)}, u32[]{:S(2)}, u32[]{:S(2)}) collective-permute-start(bf16[2048,128]{1,0:T(8,128)(2,1)S(1)} %bitcast.28), channel_id=1, source_target_pairs={{0,8},{4,20},{8,0},{12,28},{16,24},{20,4},{24,16},{28,12},{1,9},{5... | collective-permute-start | bytes 1572872 | tf_op jit(solution)/shard_map/ppermute | solution.py:64
  13.3 5.4 %collective-permute-start.6 = (f32[2,128]{1,0:T(2,128)S(1)}, f32[2,128]{1,0:T(2,128)S(1)}, u32[]{:S(2)}, u32[]{:S(2)}) collective-permute-start(f32[2,128]{1,0:T(2,128)S(1)} %collective-permute-done.4), channel_id=1, source_target_pairs={{0,16},{4,12},{8,24},{12,4},{16,0},{20,28},{24,8},{28,20},{1,17},{... | collective-permute-start | bytes 3080 | tf_op jit(solution)/shard_map/ppermute | solution.py:64
  14.5 5.9 %copy-start = (bf16[1,2048,1024]{2,1,0:T(8,128)(2,1)S(1)}, bf16[1,2048,1024]{2,1,0:T(8,128)(2,1)}, u32[]{:S(2)}) copy-start(bf16[1,2048,1024]{2,1,0:T(8,128)(2,1)} %param.12) | copy-start | bytes 12582916
  14.5 5.9 %copy-start.2 = (bf16[1,2048,128]{2,1,0:T(8,128)(2,1)S(1)}, bf16[1,2048,128]{2,1,0:T(8,128)(2,1)}, u32[]{:S(2)}) copy-start(bf16[1,2048,128]{2,1,0:T(8,128)(2,1)} %param.13) | copy-start | bytes 1572868
  20.4 6.8 %copy-start.8 = (s32[2]{0:T(128)S(1)}, s32[2]{0:T(128)}, u32[]{:S(2)}) copy-start(s32[2]{0:T(128)} %param.17) | copy-start | bytes 28
  21.2 1.2 %collective-permute-start.10 = (f32[2,10,128]{2,1,0:T(8,128)S(1)}, f32[2,10,128]{2,1,0:T(8,128)S(1)}, u32[]{:S(2)}, u32[]{:S(2)}) collective-permute-start(f32[2,10,128]{2,1,0:T(8,128)S(1)} %query_products.1), channel_id=1, source_target_pairs={{0,4},{4,0},{8,12},{12,8},{16,20},{20,16},{24,28},{28,24},{1,5},{5... | collective-permute-start | bytes 30728 | tf_op jit(solution)/shard_map/ppermute | solution.py:43
  21.4 10.4 %collective-permute-start.13 = (bf16[2048,128]{1,0:T(8,128)(2,1)S(1)}, bf16[2048,128]{1,0:T(8,128)(2,1)S(1)}, u32[]{:S(2)}, u32[]{:S(2)}) collective-permute-start(bf16[2048,128]{1,0:T(8,128)(2,1)S(1)} %collective-permute-done.9.refs_7_), channel_id=1, source_target_pairs={{0,8},{4,20},{8,0},{12,28},{16,24},{20,4},{24,16},{28,12},{1,9},{5... | collective-permute-start | bytes 1572872 | tf_op jit(solution)/shard_map/ppermute | solution.py:64
  22.5 15.1 %collective-permute-start.21 = (bf16[2048,128]{1,0:T(8,128)(2,1)S(1)}, bf16[2048,128]{1,0:T(8,128)(2,1)S(1)}, u32[]{:S(2)}, u32[]{:S(2)}) collective-permute-start(bf16[2048,128]{1,0:T(8,128)(2,1)S(1)} %collective-permute-done.2.refs_6_), channel_id=1, source_target_pairs={{0,8},{4,20},{8,0},{12,28},{16,24},{20,4},{24,16},{28,12},{1,9},{5... | collective-permute-start | bytes 1572872 | tf_op jit(solution)/shard_map/ppermute | solution.py:64
  26.0 11.6 %collective-permute-start.11 = (bf16[2048,128]{1,0:T(8,128)(2,1)S(1)}, bf16[2048,128]{1,0:T(8,128)(2,1)S(1)}, u32[]{:S(2)}, u32[]{:S(2)}) collective-permute-start(bf16[2048,128]{1,0:T(8,128)(2,1)S(1)} %collective-permute-done.5.refs_5_), channel_id=1, source_target_pairs={{0,4},{4,0},{8,12},{12,8},{16,20},{20,16},{24,28},{28,24},{1,5},{5... | collective-permute-start | bytes 1572872 | tf_op jit(solution)/shard_map/ppermute | solution.py:43
  26.0 4.0 %collective-permute-start.16 = (f32[2,10,128]{2,1,0:T(8,128)S(1)}, f32[2,10,128]{2,1,0:T(8,128)S(1)}, u32[]{:S(2)}, u32[]{:S(2)}) collective-permute-start(f32[2,10,128]{2,1,0:T(8,128)S(1)} %add.57), channel_id=1, source_target_pairs={{0,16},{4,12},{8,24},{12,4},{16,0},{20,28},{24,8},{28,20},{1,17},{... | collective-permute-start | bytes 30728 | tf_op jit(solution)/shard_map/ppermute | solution.py:64
  30.1 1.2 %collective-permute-start.17 = (f32[2,10,128]{2,1,0:T(8,128)S(1)}, f32[2,10,128]{2,1,0:T(8,128)S(1)}, u32[]{:S(2)}, u32[]{:S(2)}) collective-permute-start(f32[2,10,128]{2,1,0:T(8,128)S(1)} %collective-permute-done.16), channel_id=1, source_target_pairs={{0,4},{4,0},{8,12},{12,8},{16,20},{20,16},{24,28},{28,24},{1,5},{5... | collective-permute-start | bytes 30728 | tf_op jit(solution)/shard_map/ppermute | solution.py:43
  30.2 8.9 %collective-permute-start.15 = (bf16[2048,128]{1,0:T(8,128)(2,1)S(1)}, bf16[2048,128]{1,0:T(8,128)(2,1)S(1)}, u32[]{:S(2)}, u32[]{:S(2)}) collective-permute-start(bf16[2048,128]{1,0:T(8,128)(2,1)S(1)} %collective-permute-done.7.refs_6_), channel_id=1, source_target_pairs={{0,4},{4,0},{8,12},{12,8},{16,20},{20,16},{24,28},{28,24},{1,5},{5... | collective-permute-start | bytes 1572872 | tf_op jit(solution)/shard_map/ppermute | solution.py:43
  31.2 7.8 %collective-permute-start.18 = (f32[2,10,128]{2,1,0:T(8,128)S(1)}, f32[2,10,128]{2,1,0:T(8,128)S(1)}, u32[]{:S(2)}, u32[]{:S(2)}) collective-permute-start(f32[2,10,128]{2,1,0:T(8,128)S(1)} %collective-permute-done.17), channel_id=1, source_target_pairs={{0,16},{4,12},{8,24},{12,4},{16,0},{20,28},{24,8},{28,20},{1,17},{... | collective-permute-start | bytes 30728 | tf_op jit(solution)/shard_map/ppermute | solution.py:64
  31.8 8.8 %collective-permute-start.14 = (bf16[2048,128]{1,0:T(8,128)(2,1)S(1)}, bf16[2048,128]{1,0:T(8,128)(2,1)S(1)}, u32[]{:S(2)}, u32[]{:S(2)}) collective-permute-start(bf16[2048,128]{1,0:T(8,128)(2,1)S(1)} %collective-permute-done.13.refs_5_), channel_id=1, source_target_pairs={{0,4},{4,0},{8,12},{12,8},{16,20},{20,16},{24,28},{28,24},{1,5},{5... | collective-permute-start | bytes 1572872 | tf_op jit(solution)/shard_map/ppermute | solution.py:43
  37.6 9.7 %collective-permute-start.22 = (bf16[2048,128]{1,0:T(8,128)(2,1)S(1)}, bf16[2048,128]{1,0:T(8,128)(2,1)S(1)}, u32[]{:S(2)}, u32[]{:S(2)}) collective-permute-start(bf16[2048,128]{1,0:T(8,128)(2,1)S(1)} %collective-permute-done.21.refs_6_), channel_id=1, source_target_pairs={{0,4},{4,0},{8,12},{12,8},{16,20},{20,16},{24,28},{28,24},{1,5},{5... | collective-permute-start | bytes 1572872 | tf_op jit(solution)/shard_map/ppermute | solution.py:43
  37.6 11.2 %collective-permute-start.12 = (bf16[2048,128]{1,0:T(8,128)(2,1)S(1)}, bf16[2048,128]{1,0:T(8,128)(2,1)S(1)}, u32[]{:S(2)}, u32[]{:S(2)}) collective-permute-start(bf16[2048,128]{1,0:T(8,128)(2,1)S(1)} %collective-permute-done.11.refs_7_), channel_id=1, source_target_pairs={{0,8},{4,20},{8,0},{12,28},{16,24},{20,4},{24,16},{28,12},{1,9},{5... | collective-permute-start | bytes 1572872 | tf_op jit(solution)/shard_map/ppermute | solution.py:64
  40.6 0.9 %copy-start.7 = (s32[2]{0:T(128)S(1)}, s32[2]{0:T(128)}, u32[]{:S(2)}) copy-start(s32[2]{0:T(128)} %lengths_ref.3) | copy-start | bytes 28
  42.5 1.2 %collective-permute-start.19 = (f32[8,128]{1,0:T(8,128)S(1)}, f32[8,128]{1,0:T(8,128)S(1)}, u32[]{:S(2)}, u32[]{:S(2)}) collective-permute-start(f32[8,128]{1,0:T(8,128)S(1)} %get-tuple-element.49), channel_id=1, source_target_pairs={{0,4},{4,0},{8,12},{12,8},{16,20},{20,16},{24,28},{28,24},{1,5},{5... | collective-permute-start | bytes 12296 | tf_op jit(solution)/shard_map/ppermute | solution.py:43
  43.7 3.6 %collective-permute-start.20 = (f32[8,128]{1,0:T(8,128)S(1)}, f32[8,128]{1,0:T(8,128)S(1)}, u32[]{:S(2)}, u32[]{:S(2)}) collective-permute-start(f32[8,128]{1,0:T(8,128)S(1)} %max.6), channel_id=1, source_target_pairs={{0,8},{4,12},{8,0},{12,4},{16,24},{20,28},{24,16},{28,20},{1,9},{5... | collective-permute-start | bytes 12296 | tf_op jit(solution)/shard_map/ppermute | solution.py:43
  48.8 2.0 %collective-permute-start.23 = (bf16[2048,128]{1,0:T(8,128)(2,1)S(1)}, bf16[2048,128]{1,0:T(8,128)(2,1)S(1)}, u32[]{:S(2)}, u32[]{:S(2)}) collective-permute-start(bf16[2048,128]{1,0:T(8,128)(2,1)S(1)} %collective-permute-done.12.refs_5_), channel_id=1, source_target_pairs={{0,4},{4,0},{8,12},{12,8},{16,20},{20,16},{24,28},{28,24},{1,5},{5... | collective-permute-start | bytes 1572872 | tf_op jit(solution)/shard_map/ppermute | solution.py:43
  50.8 10.0 %copy-start.1 = (bf16[1,1024,2048]{2,1,0:T(8,128)(2,1)S(1)}, bf16[1,1024,2048]{2,1,0:T(8,128)(2,1)}, u32[]{:S(2)}) copy-start(bf16[1,1024,2048]{2,1,0:T(8,128)(2,1)} %param.15) | copy-start | bytes 12582916
  52.3 1.2 %collective-permute-start.24 = (f32[8,256]{1,0:T(8,128)S(1)}, f32[8,256]{1,0:T(8,128)S(1)}, u32[]{:S(2)}, u32[]{:S(2)}) collective-permute-start(f32[8,256]{1,0:T(8,128)S(1)} %weighted_values.1), channel_id=1, source_target_pairs={{0,4},{4,0},{8,12},{12,8},{16,20},{20,16},{24,28},{28,24},{1,5},{5... | collective-permute-start | bytes 24584 | tf_op jit(solution)/shard_map/ppermute | solution.py:43
  53.5 3.7 %collective-permute-start.25 = (f32[8,256]{1,0:T(8,128)S(1)}, f32[8,256]{1,0:T(8,128)S(1)}, u32[]{:S(2)}, u32[]{:S(2)}) collective-permute-start(f32[8,256]{1,0:T(8,128)S(1)} %add.64), channel_id=1, source_target_pairs={{0,8},{4,12},{8,0},{12,4},{16,24},{20,28},{24,16},{28,20},{1,9},{5... | collective-permute-start | bytes 24584 | tf_op jit(solution)/shard_map/ppermute | solution.py:43
  57.2 3.7 %collective-permute-start.26 = (f32[8,256]{1,0:T(8,128)S(1)}, f32[8,256]{1,0:T(8,128)S(1)}, u32[]{:S(2)}, u32[]{:S(2)}) collective-permute-start(f32[8,256]{1,0:T(8,128)S(1)} %add.65.mine_ref), channel_id=1, source_target_pairs={{0,16},{4,20},{8,24},{12,28},{16,0},{20,4},{24,8},{28,12},{1,17},{... | collective-permute-start | bytes 24584 | tf_op jit(solution)/shard_map/ppermute | solution.py:43
  60.8 9.1 %copy-start.6 = (f32[2,2048]{1,0:T(2,128)S(1)}, f32[2,2048]{1,0:T(2,128)}, u32[]{:S(2)}) copy-start(f32[2,2048]{1,0:T(2,128)} %tokens_ref.3) | copy-start | bytes 49156
  61.5 3.8 %collective-permute-start.27 = (f32[2,2048]{1,0:T(2,128)S(1)}, f32[2,2048]{1,0:T(2,128)S(1)}, u32[]{:S(2)}, u32[]{:S(2)}) collective-permute-start(f32[2,2048]{1,0:T(2,128)S(1)} %output_products.1), channel_id=1, source_target_pairs={{0,1},{1,0},{2,3},{3,2},{4,5},{5,4},{6,7},{7,6},{8,9},{9,8},{10,11... | collective-permute-start | bytes 49160 | tf_op jit(solution)/shard_map/ppermute | solution.py:43
  65.3 4.7 %collective-permute-start.28 = (f32[2,2048]{1,0:T(2,128)S(1)}, f32[2,2048]{1,0:T(2,128)S(1)}, u32[]{:S(2)}, u32[]{:S(2)}) collective-permute-start(f32[2,2048]{1,0:T(2,128)S(1)} %add.66), channel_id=1, source_target_pairs={{0,2},{1,3},{2,0},{3,1},{4,6},{5,7},{6,4},{7,5},{8,10},{9,11},{10,... | collective-permute-start | bytes 49160 | tf_op jit(solution)/shard_map/ppermute | solution.py:43

commit v8 on v7

--- a/solution.py
+++ b/solution.py
@@ -18,6 +18,7 @@
 CHEAP = pl.CostEstimate(flops=1000, bytes_accessed=1000, transcendentals=0)
 IN_VMEM = pl.BlockSpec(memory_space=pltpu.VMEM)
 IN_SMEM = pl.BlockSpec(memory_space=pltpu.SMEM)
+IN_ANY = pl.BlockSpec(memory_space=pl.ANY)
 IN_HBM = pl.BlockSpec(memory_space=pltpu.HBM)
 
 
@@ -62,30 +63,6 @@
     bits = (bit_0, bit_1)
     pairs = [(i, i ^ bits[i % 2]) for i in range(count) if bits[i % 2]]
     return lax.ppermute(value, "ctx", pairs)
-
-
-def send_first(own, partner):
-    count = lax.axis_size("ctx")
-    if count != 8:
-        return [((d, d), swap(own, "ctx", d)) for d in range(2, count // 2)]
-    return [((2, 4), by_core(own, 2, 4)), ((3, 5), by_core(partner, 2, 4))]
-
-
-def share(blocks, *before):
-    count = lax.axis_size("ctx")
-    if count != 8:
-        return []
-    return [
-        ((odd ^ 1, even ^ 1), swap(after(block, *before) if before else block, "ctx", 1))
-        for (even, odd), block in blocks
-    ]
-
-
-def send_last(own, received):
-    count = lax.axis_size("ctx")
-    if count != 8:
-        return [((d, d), swap(own, "ctx", d)) for d in range(count // 2, count)]
-    return [((7, 7), by_core(received[0][1], 2, 4))]
 
 
 def tables(placed, head_size):
@@ -182,6 +159,30 @@
     )(pltpu.with_memory_space_constraint(hidden, pltpu.HBM), gains)
 
 
+def join_kernel(*refs):
+    ins, (out_ref, sems) = refs[:-2], refs[-2:]
+    rows = ins[0].shape[0]
+    copies = [
+        pltpu.make_async_copy(ref, out_ref.at[pl.ds(i * rows, rows), :], sems.at[i])
+        for i, ref in enumerate(ins)
+    ]
+    for copy in copies:
+        copy.start()
+    for copy in copies:
+        copy.wait()
+
+
+def join(*arrays):
+    rows, columns = arrays[0].shape
+    return call(
+        join_kernel,
+        "join",
+        [IN_ANY] * len(arrays),
+        shape((len(arrays) * rows, columns), arrays[0].dtype),
+        [pltpu.SemaphoreType.DMA((len(arrays),))],
+    )(*arrays)
+
+
 def query_kernel(
     features, place_ref, squares_ref, tokens_ref, gains_ref, query_ref, key_ref, value_ref, out_ref
 ):
@@ -197,30 +198,31 @@
             row += 1
 
 
-def blocks_dot(distances, place, row_refs, block_refs, total):
-    for (even, odd), block_ref in zip(distances, block_refs):
+def blocks_dot(pieces, place, row_refs, block_refs, total):
+    for ((even, odd), first), block_ref in zip(pieces, block_refs):
         distance = jnp.where(lax.rem(place, 2) == 0, even, odd)
         rows = jnp.concatenate([ref[place ^ distance] for ref in row_refs], axis=0)
-        part = jnp.dot(rows, block_ref[...], preferred_element_type=jnp.float32)
+        block = block_ref[first : first + rows.shape[1], :]
+        part = jnp.dot(rows, block, preferred_element_type=jnp.float32)
         total = part if total is None else total + part
     return total
 
 
-def project_kernel(distances, row_count, has_total, place_ref, *refs):
+def project_kernel(pieces, row_count, has_total, place_ref, *refs):
     rows, refs = refs[:row_count], refs[row_count:]
-    total = refs[len(distances)][...] if has_total else None
-    refs[-1][...] = blocks_dot(distances, place_ref[0], rows, refs, total)
+    total = refs[len(pieces)][...] if has_total else None
+    refs[-1][...] = blocks_dot(pieces, place_ref[0], rows, refs, total)
 
 
 def project(place, rows, blocks, total=None):
     extra = [] if total is None else [total]
     row_count = sum(r.shape[1] for r in rows)
     return call(
-        functools.partial(project_kernel, [d for d, _ in blocks], len(rows), total is not None),
+        functools.partial(project_kernel, [b[1:] for b in blocks], len(rows), total is not None),
         "project",
         [IN_SMEM] + [IN_VMEM] * (len(rows) + len(blocks) + len(extra)),
         shape((row_count, LANES)),
-    )(place, *rows, *[block for _, block in blocks], *extra)
+    )(place, *rows, *[b[0] for b in blocks], *extra)
 
 
 def live_rows(dims, team, place, lengths_ref):
@@ -258,9 +260,9 @@
     self_ref[...] = jnp.broadcast_to(self_scores, self_ref.shape)
 
 
-def weigh_kernel(distances, row_count, team, place_ref, lengths_ref, *refs):
+def weigh_kernel(pieces, row_count, team, place_ref, lengths_ref, *refs):
     rows, refs = refs[:row_count], refs[row_count:]
-    blocks, refs = refs[: len(distances)], refs[len(distances) :]
+    blocks, refs = refs[: len(pieces)], refs[len(pieces) :]
     total_ref, masked_ref, top_ref, self_ref, summed_ref, out_ref = refs
     place = place_ref[0]
     heads = masked_ref.shape[0]
@@ -272,18 +274,18 @@
     self_weight = jnp.where(lax.rem(place, team) == 0, self_weight, 0.0)
     self_value = summed_ref[heads + 1 : heads + 2, :].astype(jnp.bfloat16).astype(jnp.float32)
     mass = jnp.sum(weights.astype(jnp.float32), axis=-1, keepdims=True) + self_weight
-    values = blocks_dot(distances, place, rows, blocks, total_ref[...]).astype(jnp.bfloat16)
+    values = blocks_dot(pieces, place, rows, blocks, total_ref[...]).astype(jnp.bfloat16)
     accum = jnp.dot(weights, values, preferred_element_type=jnp.float32)
     out_ref[:, :LANES] = accum + self_weight * self_value
     out_ref[:, LANES:] = mass
 
 
-def output_kernel(team, place_ref, mine_ref, other_ref, weight_ref, out_ref):
+def output_kernel(team, place_ref, sums_ref, weight_ref, out_ref):
     request = lax.div(place_ref[0], team)
-    heads = mine_ref.shape[0]
+    heads = sums_ref.shape[0] // 2
     attended = []
-    for ref in (mine_ref, other_ref):
-        attended.append(ref[:, :LANES] / ref[:, LANES:])
+    for own in (slice(0, heads), slice(heads, 2 * heads)):
+        attended.append(sums_ref[own, :LANES] / sums_ref[own, LANES:])
     first = jnp.where(request == 0, attended[0], attended[1]).astype(jnp.bfloat16)
     second = jnp.where(request == 0, attended[1], attended[0]).astype(jnp.bfloat16)
     both = jnp.concatenate(
@@ -331,40 +333,39 @@
         (shape((requests, LANES)),) + (shape((1, LANES), jnp.int32),) * 3,
     )(places, new_tokens)
 
-    def beside(received, sent, parts):
+    def normalise_next(parts, sent):
         first = len(rows) * NORM_ROWS
         rows.extend(normalise(after(ctx_hidden[0], sent), gains, first, parts))
-        return after(received, rows[-1])
-
-    def sum_chips(value, norm_parts=0):
+
+    def sum_chips(value, norm_parts=(0, 0)):
         received = by_core(value, 4, 2)
-        if norm_parts:
-            received = beside(received, value, norm_parts)
+        if norm_parts[0]:
+            normalise_next(norm_parts[0], value)
+            received = after(received, rows[-1])
         told = swap(received, "ctx", 1)
         opposite = by_core(told, 4, 2)
-        if norm_parts:
-            opposite = beside(opposite, told, row_count // NORM_ROWS - norm_parts)
+        if norm_parts[1]:
+            normalise_next(norm_parts[1], told)
+            opposite = after(opposite, rows[-1])
         over_x = jnp.where(core == 0, told, received)
         over_y = jnp.where(core == 0, received, told)
         return (value + over_x) + (over_y + opposite), told
 
-    key_partner = swap(key_weight[0], "ctx", 1)
-    value_partner = swap(value_weight[0], "ctx", 1)
-    key_near = [((0, 0), key_weight[0]), ((1, 1), key_partner)]
-    value_near = [((0, 0), value_weight[0]), ((1, 1), value_partner)]
-    key_far = send_first(key_weight[0], key_partner)
-
+    own_key, own_value = key_weight[0], value_weight[0]
+    key_partner = swap(own_key, "ctx", 1)
+    value_partner = swap(own_value, "ctx", 1)
     squares = squares + swap(squares, "ctx", 1)
     squares = after(squares, key_partner, value_partner)
+    norm_calls = row_count // NORM_ROWS
     if split:
-        squares, told = sum_chips(squares, row_count // NORM_ROWS // 2)
-        key_shared = share(key_far, told)
-        squares = after(squares, key_far[1][1], key_shared[0][1])
+        key_far = by_core(join(own_key, key_partner), 2, 4)
+        squares, _ = sum_chips(squares, (2, norm_calls - 2))
+        key_told = swap(after(key_far, squares), "ctx", 1)
+        value_far = by_core(join(own_value, value_partner), 2, 4)
+        key_last = by_core(key_told[:width], 2, 4)
     else:
-        key_shared = share(key_far)
-        squares = beside(squares, squares, row_count // NORM_ROWS)
+        normalise_next(norm_calls, squares)
         squares = butterfly(squares, "ctx", chip_bits, jnp.add)
-    key_last = send_last(key_weight[0], key_shared)
 
     parts = call(
         functools.partial(query_kernel, features),
@@ -373,10 +374,8 @@
         shape((requests, heads + 2, head_size)),
     )(places, squares, new_tokens, gains, query_weight[0], key_weight[0], value_weight[0])
     parts = parts + swap(parts, "ctx", 1)
-    parts_sent = parts
-    value_far = send_first(value_weight[0], after(value_partner, parts))
     if split:
-        parts, _ = sum_chips(parts)
+        parts, told = sum_chips(parts)
         summed = jnp.where(own_request == 0, parts[0], parts[1])
     else:
         own_part = jnp.where(own_request == 0, parts[0], parts[1])
@@ -384,9 +383,25 @@
         summed = own_part + swap(other_part, "ctx", team)
         summed = butterfly(summed, "ctx", chip_bits[:-1], jnp.add)
 
-    key_total = project(places, rows, key_near)
-    key_total = project(places, rows, key_far + key_shared, key_total)
-    key_total = project(places, rows, key_last + share(key_last), key_total)
+    key_total = project(
+        places, rows, [(own_key, (0, 0), 0), (key_partner, (1, 1), 0)]
+    )
+    if split:
+        blocks = [
+            (key_far, (2, 4), 0),
+            (key_far, (3, 5), width),
+            (key_told, (5, 3), 0),
+            (key_told, (4, 2), width),
+        ]
+        key_total = project(places, rows, blocks, key_total)
+        value_told = swap(after(value_far, told), "ctx", 1)
+        value_last = by_core(value_told[:width], 2, 4)
+        shared = swap(after(key_last, key_total), "ctx", 1)
+        blocks = [(key_last, (7, 7), 0), (shared, (6, 6), 0)]
+        key_total = project(places, rows, blocks, key_total)
+    else:
+        blocks = [(swap(own_key, "ctx", d), (d, d), 0) for d in range(2, ctx_count)]
+        key_total = project(places, rows, blocks, key_total)
 
     within = first_row[0, :1] + jnp.arange(row_count, dtype=jnp.int32)
     cosine, sine_part = tables(within.astype(jnp.float32), head_size)
@@ -401,14 +416,23 @@
     near_top = top
     top = butterfly(top, "ctx", bits_below(team)[1:], jnp.maximum)
 
-    value_shared = share(value_far, parts_sent)
-    value_last = send_last(value_weight[0], value_shared)
-    value_total = project(after(places, near_top), rows, value_near)
-    value_total = project(after(places, top), rows, value_far + value_shared, value_total)
-
-    blocks = value_last + share(value_last, value_total)
+    value_total = project(
+        after(places, near_top), rows, [(own_value, (0, 0), 0), (value_partner, (1, 1), 0)]
+    )
+    if split:
+        blocks = [
+            (value_far, (2, 4), 0),
+            (value_far, (3, 5), width),
+            (value_told, (5, 3), 0),
+            (value_told, (4, 2), width),
+        ]
+        value_total = project(after(places, top), rows, blocks, value_total)
+        blocks = [(swap(after(value_last, value_total), "ctx", 1), (6, 6), 0)]
+        value_total = project(places, rows, [(value_last, (7, 7), 0)], value_total)
+    else:
+        blocks = [(swap(own_value, "ctx", d), (d, d), 0) for d in range(2, ctx_count)]
     packed = call(
-        functools.partial(weigh_kernel, [d for d, _ in blocks], len(rows), team),
+        functools.partial(weigh_kernel, [b[1:] for b in blocks], len(rows), team),
         "weighted_values",
         [IN_SMEM] * 2 + [IN_VMEM] * (len(rows) + len(blocks) + 5),
         shape((heads, 2 * head_size)),
@@ -416,21 +440,28 @@
         places,
         lengths,
         *rows,
-        *[block for _, block in blocks],
+        *[b[0] for b in blocks],
         value_total,
         masked,
         top,
         self_scores,
         summed,
     )
-    packed = butterfly(packed, "ctx", bits_below(team), jnp.add)
-    other = swap(packed, "ctx", team)
+    if split:
+        packed = packed + swap(packed, "ctx", 1)
+        packed = packed + by_core(packed, 0, 2)
+        sums = jnp.concatenate((packed, by_core(packed, 0, 4)), axis=0)
+        told = lax.ppermute(sums, "ctx", [(i, i ^ 1) for i in range(1, ctx_count, 2)])
+        sums = jnp.where(core[:, :1] == 0, told, sums)
+    else:
+        packed = butterfly(packed, "ctx", bits_below(team), jnp.add)
+        sums = jnp.concatenate((packed, swap(packed, "ctx", team)), axis=0)
     update = call(
         functools.partial(output_kernel, team),
         "output_products",
-        [IN_SMEM] + [IN_VMEM] * 3,
+        [IN_SMEM] + [IN_VMEM] * 2,
         shape((requests, out_weight.shape[2])),
-    )(places, packed, other, out_weight[0])
+    )(places, sums, out_weight[0])
     return new_tokens + butterfly(update, "kv", bits_below(kv_count), jnp.add)
 
 

time: 70.8 us -> 76.8 us (1.085)
  waiting for transfers between devices: 29.3 us -> 31.7 us
  Pallas kernels: 17.2 us -> 19.5 us
  starting transfers between devices: 20.8 us -> 22.5 us
    ppermute x0 -> x1, waiting for transfers between devices: none -> 8.49 us  [shards(): lax.ppermute(sums, 'ctx', [(i, i ^ 1) for i in range(1, ctx_count, 2)])]
    ppermute x10, waiting for transfers between devices: 12.7 us -> 5.31 us  [by_core(): return lax.ppermute(value, 'ctx', pairs)]
    pallas_call x6 -> x9, Pallas kernels: 7.18 us -> 9.49 us  [the longest x6 6.18 us: project(): call(functools.partial(project_kernel, [b[1:] for b in blocks], len(rows)...]
    ppermute x10, starting transfers between devices: 10.4 us -> 12.6 us  [by_core(): return lax.ppermute(value, 'ctx', pairs)]
    ppermute x19 -> x15, starting transfers between devices: 10.4 us -> 8.59 us  [swap(): return lax.ppermute(value, axis, [(i, i ^ distance) for i in range(count)])]
    ppermute x19 -> x15, waiting for transfers between devices: 16.5 us -> 17.9 us  [swap(): return lax.ppermute(value, axis, [(i, i ^ distance) for i in range(count)])]
    ppermute x0 -> x1, starting transfers between devices: none -> 1.29 us  [shards(): lax.ppermute(sums, 'ctx', [(i, i ^ 1) for i in range(1, ctx_count, 2)])]
    unnamed x18 -> x22, local copies, waits for them, and re-layouts: 1.59 us -> 1.08 us
  transfers between devices with their start and end apart: 29 -> 26, of which waited for: 16 -> 17; matrix products, arithmetic and copies ran while one was open for 1% -> 1% of each run, Pallas kernels for 21% -> 22%
where the time goes in v8:
time: 76.8 us; the launch traced here: 76.6 us
  waiting for transfers between devices  31.7 us (41%)
  starting transfers between devices  22.5 us (29%)
  Pallas kernels  19.5 us (25%)
  other arithmetic  1.5 us (2%)
  local copies, waits for them, and re-layouts  1.15 us (1%)
    ppermute x15, waiting for transfers between devices, swap(): return lax.ppermute(value, axis, [(i, i ^ distance) for i in range(count)])  17.9 us
    ppermute x10, starting transfers between devices, by_core(): return lax.ppermute(value, 'ctx', pairs)  12.6 us
    ppermute x15, starting transfers between devices, swap(): return lax.ppermute(value, axis, [(i, i ^ distance) for i in range(count)])  8.59 us
    ppermute x1, waiting for transfers between devices, shards(): lax.ppermute(sums, 'ctx', [(i, i ^ 1) for i in range(1, ctx_count, 2)])  8.49 us
    pallas_call x2, Pallas kernels, normalise(): call(functools.partial(norm_kernel, first), 'normalise', [IN_HBM, IN_VMEM...  7.4 us
    pallas_call x6, Pallas kernels, project(): call(functools.partial(project_kernel, [b[1:] for b in blocks], len(rows)...  6.18 us
    ppermute x10, waiting for transfers between devices, by_core(): return lax.ppermute(value, 'ctx', pairs)  5.31 us
    pallas_call x2, Pallas kernels, join(): call(join_kernel, 'join', [IN_ANY] * len(arrays), shape((len(arrays) * ro...  2.16 us
  transfers between devices with their start and end apart: 26, of which 17 were waited for; matrix products, arithmetic and copies ran while one was open for 1% of the time, Pallas kernels for 22%

profile of v8, /device:TPU:0, one launch (start us, length us, event | category | flops | bytes accessed | tf_op | source)
XLA Modules:
  0.0 76.6 jit_solution(5338160117613756198)
XLA Ops:
  0.0 0.5 collective-permute-start.1
  0.5 1.7 %collective-permute-done.1.refs_1_.refs_6_ = bf16[2048,128]{1,0:T(8,128)(2,1)S(1)} collective-permute-done((bf16[2048,128]{1,0:T(8,128)(2,1)}, bf16[2048,128]{1,0:T(8,128)(2,1)S(1)}, u32[]{:S(2)}, u32[]{:S(2)}) %collective-permute-start.1) | collective-permute-done | bytes 524320 | tf_op jit(solution)/shard_map/ppermute | solution.py:44
  2.2 1.0 %copy-done = bf16[1,2048,128]{2,1,0:T(8,128)(2,1)S(1)} copy-done((bf16[1,2048,128]{2,1,0:T(8,128)(2,1)S(1)}, bf16[1,2048,128]{2,1,0:T(8,128)(2,1)}, u32[]{:S(2)}) %copy-start) | copy-done | bytes 524312
  3.3 1.1 %join.3 = bf16[4096,128]{1,0:T(8,128)(2,1)} custom-call(bf16[2048,128]{1,0:T(8,128)(2,1)S(1)} %bitcast.24, bf16[2048,128]{1,0:T(8,128)(2,1)S(1)} %collective-permute-done.1.refs_1_.refs_6_), custom_call_target="tpu_custom_call" | custom-call | flops 1000 | bytes 1000 | tf_op jit(solution)/shard_map/join/pallas_call | solution.py:177
  4.3 2.9 %collective-permute-start.12 = (bf16[4096,128]{1,0:T(8,128)(2,1)}, bf16[4096,128]{1,0:T(8,128)(2,1)S(1)}, u32[]{:S(2)}, u32[]{:S(2)}) collective-permute-start(bf16[4096,128]{1,0:T(8,128)(2,1)} %join.3), channel_id=1, source_target_pairs={{0,8},{4,20},{8,0},{12,28},{16,24},{20,4},{24,16},{28,12},{1,9},{5... | collective-permute-start | bytes 3145736 | tf_op jit(solution)/shard_map/ppermute | solution.py:65
  7.3 1.9 %collective-permute-done.2.refs_1_.refs_6_ = bf16[2048,128]{1,0:T(8,128)(2,1)S(1)} collective-permute-done((bf16[2048,128]{1,0:T(8,128)(2,1)S(1)}, bf16[2048,128]{1,0:T(8,128)(2,1)S(1)}, u32[]{:S(2)}, u32[]{:S(2)}) %collective-permute-start.2) | collective-permute-done | bytes 524320 | tf_op jit(solution)/shard_map/ppermute | solution.py:44
  9.2 1.1 %join.2 = bf16[4096,128]{1,0:T(8,128)(2,1)} custom-call(bf16[2048,128]{1,0:T(8,128)(2,1)S(1)} %bitcast.28, bf16[2048,128]{1,0:T(8,128)(2,1)S(1)} %collective-permute-done.2.refs_1_.refs_6_), custom_call_target="tpu_custom_call" | custom-call | flops 1000 | bytes 1000 | tf_op jit(solution)/shard_map/join/pallas_call | solution.py:177
  10.3 1.1 %collective-permute-start.5 = (bf16[4096,128]{1,0:T(8,128)(2,1)}, bf16[4096,128]{1,0:T(8,128)(2,1)S(1)}, u32[]{:S(2)}, u32[]{:S(2)}) collective-permute-start(bf16[4096,128]{1,0:T(8,128)(2,1)} %join.2), channel_id=1, source_target_pairs={{0,8},{4,20},{8,0},{12,28},{16,24},{20,4},{24,16},{28,12},{1,9},{5... | collective-permute-start | bytes 3145736 | tf_op jit(solution)/shard_map/ppermute | solution.py:65
  11.3 0.1 squares.1
  11.4 0.4 collective-permute-start
  11.8 0.8 %collective-permute-done = f32[2,128]{1,0:T(2,128)S(1)} collective-permute-done((f32[2,128]{1,0:T(2,128)S(1)}, f32[2,128]{1,0:T(2,128)S(1)}, u32[]{:S(2)}, u32[]{:S(2)}) %collective-permute-start) | collective-permute-done | bytes 1056 | tf_op jit(solution)/shard_map/ppermute | solution.py:44
  12.6 1.0 %collective-permute-start.3 = (f32[2,128]{1,0:T(2,128)S(1)}, f32[2,128]{1,0:T(2,128)S(1)}, u32[]{:S(2)}, u32[]{:S(2)}) collective-permute-start(f32[2,128]{1,0:T(2,128)S(1)} %add.53), channel_id=1, source_target_pairs={{0,16},{4,12},{8,24},{12,4},{16,0},{20,28},{24,8},{28,20},{1,17},{... | collective-permute-start | bytes 3080 | tf_op jit(solution)/shard_map/ppermute | solution.py:65
  13.6 3.1 %normalise.2 = (bf16[8,64,2048]{2,1,0:T(8,128)(2,1)S(1)}, bf16[8,64,2048]{2,1,0:T(8,128)(2,1)S(1)}) custom-call(bf16[320,16384]{1,0:T(8,128)(2,1)} %bitcast.38, f32[8,1,2048]{2,1,0:T(1,128)S(1)} %bitcast.33), custom_call_target="tpu_custom_call" | custom-call | flops 1000 | bytes 1000 | tf_op jit(solution)/shard_map/normalise/pallas_call | solution.py:150
  16.8 0.1 collective-permute-start.4
  16.9 1.1 %collective-permute-done.4 = f32[2,128]{1,0:T(2,128)S(1)} collective-permute-done((f32[2,128]{1,0:T(2,128)S(1)}, f32[2,128]{1,0:T(2,128)S(1)}, u32[]{:S(2)}, u32[]{:S(2)}) %collective-permute-start.4) | collective-permute-done | bytes 1056 | tf_op jit(solution)/shard_map/ppermute | solution.py:44
  18.0 1.1 %collective-permute-start.6 = (f32[2,128]{1,0:T(2,128)S(1)}, f32[2,128]{1,0:T(2,128)S(1)}, u32[]{:S(2)}, u32[]{:S(2)}) collective-permute-start(f32[2,128]{1,0:T(2,128)S(1)} %collective-permute-done.4), channel_id=1, source_target_pairs={{0,16},{4,12},{8,24},{12,4},{16,0},{20,28},{24,8},{28,20},{1,17},{... | collective-permute-start | bytes 3080 | tf_op jit(solution)/shard_map/ppermute | solution.py:65
  19.1 4.3 %normalise.3 = (bf16[8,64,2048]{2,1,0:T(8,128)(2,1)S(1)}, bf16[8,64,2048]{2,1,0:T(8,128)(2,1)S(1)}, bf16[8,64,2048]{2,1,0:T(8,128)(2,1)S(1)}) custom-call(bf16[320,16384]{1,0:T(8,128)(2,1)} %bitcast.39, f32[8,1,2048]{2,1,0:T(1,128)S(1)} %bitcast.34), custom_call_target="tpu_custom_call" | custom-call | flops 1000 | bytes 1000 | tf_op jit(solution)/shard_map/normalise/pallas_call | solution.py:150
  23.4 0.4 collective-permute-start.13
  23.8 0.8 %query_products.1 = f32[2,10,128]{2,1,0:T(8,128)S(1)} custom-call(s32[1]{0:T(128)} %bitcast.place_ref, f32[2,128]{1,0:T(2,128)S(1)} %add_add_fusion.2.squares_ref, f32[2,2048]{1,0:T(2,128)S(1)} %copy-done.8, f32[8,1,2048]{2,1,0:T(1,128)S(1)} %bitcast.35, bf16[2048,1024]{1,0:T(8,128)(2,1)S(1)} %bitcast.31, bf16[2048,128]{1,0:T(8,128)(2,1)S(1)} %bitcast.25, ...), custom_call_target="tpu_custom_call" | custom-call | flops 1000 | bytes 1000 | tf_op jit(solution)/shard_map/query_products/pallas_call | solution.py:370
  24.6 0.2 collective-permute-start.7
  24.9 1.3 %collective-permute-done.7 = f32[2,10,128]{2,1,0:T(8,128)S(1)} collective-permute-done((f32[2,10,128]{2,1,0:T(8,128)S(1)}, f32[2,10,128]{2,1,0:T(8,128)S(1)}, u32[]{:S(2)}, u32[]{:S(2)}) %collective-permute-start.7) | collective-permute-done | bytes 10272 | tf_op jit(solution)/shard_map/ppermute | solution.py:44
  26.2 0.9 %collective-permute-start.8 = (f32[2,10,128]{2,1,0:T(8,128)S(1)}, f32[2,10,128]{2,1,0:T(8,128)S(1)}, u32[]{:S(2)}, u32[]{:S(2)}) collective-permute-start(f32[2,10,128]{2,1,0:T(8,128)S(1)} %add.57), channel_id=1, source_target_pairs={{0,16},{4,12},{8,24},{12,4},{16,0},{20,28},{24,8},{28,20},{1,17},{... | collective-permute-start | bytes 30728 | tf_op jit(solution)/shard_map/ppermute | solution.py:65
  27.1 3.0 %collective-permute-done.8 = f32[2,10,128]{2,1,0:T(8,128)S(1)} collective-permute-done((f32[2,10,128]{2,1,0:T(8,128)S(1)}, f32[2,10,128]{2,1,0:T(8,128)S(1)}, u32[]{:S(2)}, u32[]{:S(2)}) %collective-permute-start.8) | collective-permute-done | bytes 10272 | tf_op jit(solution)/shard_map/ppermute | solution.py:65
  30.1 1.2 %collective-permute-done.9 = f32[2,10,128]{2,1,0:T(8,128)S(1)} collective-permute-done((f32[2,10,128]{2,1,0:T(8,128)S(1)}, f32[2,10,128]{2,1,0:T(8,128)S(1)}, u32[]{:S(2)}, u32[]{:S(2)}) %collective-permute-start.9) | collective-permute-done | bytes 10272 | tf_op jit(solution)/shard_map/ppermute | solution.py:44
  31.3 0.4 collective-permute-done.5.refs_5_.refs_6_
  31.7 0.0 collective-permute-start.10
  31.8 2.1 %collective-permute-start.14 = (bf16[2048,128]{1,0:T(8,128)(2,1)S(1)}, bf16[2048,128]{1,0:T(8,128)(2,1)S(1)}, u32[]{:S(2)}, u32[]{:S(2)}) collective-permute-start(bf16[2048,128]{1,0:T(8,128)(2,1)S(1)} %slice.25), channel_id=1, source_target_pairs={{0,8},{4,20},{8,0},{12,28},{16,24},{20,4},{24,16},{28,12},{1,9},{5... | collective-permute-start | bytes 1572872 | tf_op jit(solution)/shard_map/ppermute | solution.py:65
  33.9 0.1 multiply_sine_fusion.1
  34.0 0.6 multiply_sine_fusion
  34.7 0.9 %project.6.refs_9_ = f32[320,128]{1,0:T(8,128)S(1)} custom-call(s32[1]{0:T(128)} %bitcast.place_ref, bf16[8,64,2048]{2,1,0:T(8,128)(2,1)S(1)} %get-tuple-element.32.refs_0_, bf16[8,64,2048]{2,1,0:T(8,128)(2,1)S(1)} %get-tuple-element.33.refs_1_, bf16[8,64,2048]{2,1,0:T(8,128)(2,1)S(1)} %get-tuple-element.36.refs_2_, ...), custom_call_target="tpu_custom_call" | custom-call | flops 1000 | bytes 1000 | tf_op jit(solution)/shard_map/project/pallas_call | solution.py:220
  35.5 1.6 %collective-permute-start.16 = (f32[2,10,128]{2,1,0:T(8,128)S(1)}, f32[2,10,128]{2,1,0:T(8,128)S(1)}, u32[]{:S(2)}, u32[]{:S(2)}) collective-permute-start(f32[2,10,128]{2,1,0:T(8,128)S(1)} %collective-permute-done.9), channel_id=1, source_target_pairs={{0,16},{4,12},{8,24},{12,4},{16,0},{20,28},{24,8},{28,20},{1,17},{... | collective-permute-start | bytes 30728 | tf_op jit(solution)/shard_map/ppermute | solution.py:65
  37.2 0.6 collective-permute-start.11
  37.8 1.5 %project.7.refs_7_ = f32[320,128]{1,0:T(8,128)S(1)} custom-call(s32[1]{0:T(128)} %bitcast.place_ref, bf16[8,64,2048]{2,1,0:T(8,128)(2,1)S(1)} %get-tuple-element.32.refs_0_, bf16[8,64,2048]{2,1,0:T(8,128)(2,1)S(1)} %get-tuple-element.33.refs_1_, bf16[8,64,2048]{2,1,0:T(8,128)(2,1)S(1)} %get-tuple-element.36.refs_2_, ...), custom_call_target="tpu_custom_call" | custom-call | flops 1000 | bytes 1000 | tf_op jit(solution)/shard_map/project/pallas_call | solution.py:220
  39.3 1.9 %collective-permute-done.14.refs_5_ = bf16[2048,128]{1,0:T(8,128)(2,1)S(1)} collective-permute-done((bf16[2048,128]{1,0:T(8,128)(2,1)S(1)}, bf16[2048,128]{1,0:T(8,128)(2,1)S(1)}, u32[]{:S(2)}, u32[]{:S(2)}) %collective-permute-start.14) | collective-permute-done | bytes 524320 | tf_op jit(solution)/shard_map/ppermute | solution.py:65
  41.2 0.0 collective-permute-start.15
  41.2 0.0 collective-permute-done.16
  41.3 0.0 copy-start.9
  41.3 1.8 %collective-permute-done.15.refs_6_ = bf16[2048,128]{1,0:T(8,128)(2,1)S(1)} collective-permute-done((bf16[2048,128]{1,0:T(8,128)(2,1)S(1)}, bf16[2048,128]{1,0:T(8,128)(2,1)S(1)}, u32[]{:S(2)}, u32[]{:S(2)}) %collective-permute-start.15) | collective-permute-done | bytes 524320 | tf_op jit(solution)/shard_map/ppermute | solution.py:44
  43.1 0.9 %project.8.refs_0_ = f32[320,128]{1,0:T(8,128)S(1)} custom-call(s32[1]{0:T(128)} %bitcast.place_ref, bf16[8,64,2048]{2,1,0:T(8,128)(2,1)S(1)} %get-tuple-element.32.refs_0_, bf16[8,64,2048]{2,1,0:T(8,128)(2,1)S(1)} %get-tuple-element.33.refs_1_, bf16[8,64,2048]{2,1,0:T(8,128)(2,1)S(1)} %get-tuple-element.36.refs_2_, ...), custom_call_target="tpu_custom_call" | custom-call | flops 1000 | bytes 1000 | tf_op jit(solution)/shard_map/project/pallas_call | solution.py:220
  44.0 1.0 %scores.1 = (f32[8,320]{1,0:T(8,128)S(1)}, f32[8,128]{1,0:T(8,128)S(1)}, f32[8,128]{1,0:T(8,128)S(1)}) custom-call(s32[1]{0:T(128)} %bitcast.place_ref, s32[2]{0:T(128)S(1)} %copy-done.9, f32[320,128]{1,0:T(8,128)S(1)} %project.8.refs_0_, f32[320,64]{1,0:T(8,128)S(1)} %get-tuple-element.52.refs_1_, f32[320,64]{1,0:T(8,128)S(1)} %get-tuple-element.51.refs_2_, ...), custom_call_target="tpu_custom_call" | custom-call | flops 1000 | bytes 1000 | tf_op jit(solution)/shard_map/scores/pallas_call | solution.py:409
  45.0 0.1 collective-permute-start.17
  45.1 1.0 %collective-permute-done.17 = f32[8,128]{1,0:T(8,128)S(1)} collective-permute-done((f32[8,128]{1,0:T(8,128)S(1)}, f32[8,128]{1,0:T(8,128)S(1)}, u32[]{:S(2)}, u32[]{:S(2)}) %collective-permute-start.17) | collective-permute-done | bytes 4128 | tf_op jit(solution)/shard_map/ppermute | solution.py:44
  46.2 2.0 %collective-permute-start.18 = (f32[8,128]{1,0:T(8,128)S(1)}, f32[8,128]{1,0:T(8,128)S(1)}, u32[]{:S(2)}, u32[]{:S(2)}) collective-permute-start(f32[8,128]{1,0:T(8,128)S(1)} %max.6), channel_id=1, source_target_pairs={{0,8},{4,12},{8,0},{12,4},{16,24},{20,28},{24,16},{28,20},{1,9},{5... | collective-permute-start | bytes 12296 | tf_op jit(solution)/shard_map/ppermute | solution.py:44
  48.2 0.9 %project.9.refs_9_ = f32[320,128]{1,0:T(8,128)S(1)} custom-call(s32[1]{0:T(128)} %bitcast.place_ref, bf16[8,64,2048]{2,1,0:T(8,128)(2,1)S(1)} %get-tuple-element.32.refs_0_, bf16[8,64,2048]{2,1,0:T(8,128)(2,1)S(1)} %get-tuple-element.33.refs_1_, bf16[8,64,2048]{2,1,0:T(8,128)(2,1)S(1)} %get-tuple-element.36.refs_2_, ...), custom_call_target="tpu_custom_call" | custom-call | flops 1000 | bytes 1000 | tf_op jit(solution)/shard_map/project/pallas_call | solution.py:220
  49.1 0.7 collective-permute-done.18
  49.8 1.5 %project.10.refs_6_ = f32[320,128]{1,0:T(8,128)S(1)} custom-call(s32[1]{0:T(128)} %bitcast.place_ref, bf16[8,64,2048]{2,1,0:T(8,128)(2,1)S(1)} %get-tuple-element.32.refs_0_, bf16[8,64,2048]{2,1,0:T(8,128)(2,1)S(1)} %get-tuple-element.33.refs_1_, bf16[8,64,2048]{2,1,0:T(8,128)(2,1)S(1)} %get-tuple-element.36.refs_2_, ...), custom_call_target="tpu_custom_call" | custom-call | flops 1000 | bytes 1000 | tf_op jit(solution)/shard_map/project/pallas_call | solution.py:220
  51.3 0.1 collective-permute-start.19
  51.4 0.5 project.11.refs_6_
  51.9 1.4 %collective-permute-done.19.refs_5_ = bf16[2048,128]{1,0:T(8,128)(2,1)S(1)} collective-permute-done((bf16[2048,128]{1,0:T(8,128)(2,1)S(1)}, bf16[2048,128]{1,0:T(8,128)(2,1)S(1)}, u32[]{:S(2)}, u32[]{:S(2)}) %collective-permute-start.19) | collective-permute-done | bytes 524320 | tf_op jit(solution)/shard_map/ppermute | solution.py:44
  53.3 1.2 %weighted_values.1 = f32[8,256]{1,0:T(8,128)S(1)} custom-call(s32[1]{0:T(128)} %bitcast.place_ref, s32[2]{0:T(128)S(1)} %copy-done.9, bf16[8,64,2048]{2,1,0:T(8,128)(2,1)S(1)} %get-tuple-element.32.refs_0_, bf16[8,64,2048]{2,1,0:T(8,128)(2,1)S(1)} %get-tuple-element.33.refs_1_, bf16[8,64,2048]{2,1,0:T(8,128)(2,1)S(1)} %get-tuple-element.36.refs_2_, ...), custom_call_target="tpu_custom_call" | custom-call | flops 1000 | bytes 1000 | tf_op jit(solution)/shard_map/weighted_values/pallas_call | solution.py:434
  54.5 0.1 collective-permute-start.20
  54.6 1.0 %collective-permute-done.20 = f32[8,256]{1,0:T(8,128)S(1)} collective-permute-done((f32[8,256]{1,0:T(8,128)S(1)}, f32[8,256]{1,0:T(8,128)S(1)}, u32[]{:S(2)}, u32[]{:S(2)}) %collective-permute-start.20) | collective-permute-done | bytes 8224 | tf_op jit(solution)/shard_map/ppermute | solution.py:44
  55.7 0.7 collective-permute-start.21
  56.3 0.0 collective-permute-done.21
  56.3 0.7 collective-permute-start.22
  57.0 0.0 collective-permute-done.22
  57.0 1.3 %collective-permute-start.23 = (f32[16,256]{1,0:T(8,128)S(1)}, f32[16,256]{1,0:T(8,128)S(1)}, u32[]{:S(2)}, u32[]{:S(2)}) collective-permute-start(f32[16,256]{1,0:T(8,128)S(1)} %pad_maximum_fusion), channel_id=1, source_target_pairs={{4,0},{12,8},{20,16},{28,24},{5,1},{13,9},{21,17},{29,25},{6,2},{1... | collective-permute-start | bytes 49160 | tf_op jit(solution)/shard_map/ppermute | solution.py:454
  58.4 8.5 %collective-permute-done.23 = f32[16,256]{1,0:T(8,128)S(1)} collective-permute-done((f32[16,256]{1,0:T(8,128)S(1)}, f32[16,256]{1,0:T(8,128)S(1)}, u32[]{:S(2)}, u32[]{:S(2)}) %collective-permute-start.23) | collective-permute-done | bytes 16416 | tf_op jit(solution)/shard_map/ppermute | solution.py:454
  66.9 0.6 output_products.1
  67.5 1.8 %collective-permute-start.24 = (f32[2,2048]{1,0:T(2,128)S(1)}, f32[2,2048]{1,0:T(2,128)S(1)}, u32[]{:S(2)}, u32[]{:S(2)}) collective-permute-start(f32[2,2048]{1,0:T(2,128)S(1)} %output_products.1), channel_id=1, source_target_pairs={{0,1},{1,0},{2,3},{3,2},{4,5},{5,4},{6,7},{7,6},{8,9},{9,8},{10,11... | collective-permute-start | bytes 49160 | tf_op jit(solution)/shard_map/ppermute | solution.py:44
  69.3 1.9 %collective-permute-done.24 = f32[2,2048]{1,0:T(2,128)S(1)} collective-permute-done((f32[2,2048]{1,0:T(2,128)S(1)}, f32[2,2048]{1,0:T(2,128)S(1)}, u32[]{:S(2)}, u32[]{:S(2)}) %collective-permute-start.24) | collective-permute-done | bytes 16416 | tf_op jit(solution)/shard_map/ppermute | solution.py:44
  71.3 2.9 %collective-permute-start.25 = (f32[2,2048]{1,0:T(2,128)S(1)}, f32[2,2048]{1,0:T(2,128)S(1)}, u32[]{:S(2)}, u32[]{:S(2)}) collective-permute-start(f32[2,2048]{1,0:T(2,128)S(1)} %add.66), channel_id=1, source_target_pairs={{0,2},{1,3},{2,0},{3,1},{4,6},{5,7},{6,4},{7,5},{8,10},{9,11},{10,... | collective-permute-start | bytes 49160 | tf_op jit(solution)/shard_map/ppermute | solution.py:44
  74.1 1.8 %collective-permute-done.25 = f32[2,2048]{1,0:T(2,128)S(1)} collective-permute-done((f32[2,2048]{1,0:T(2,128)S(1)}, f32[2,2048]{1,0:T(2,128)S(1)}, u32[]{:S(2)}, u32[]{:S(2)}) %collective-permute-start.25) | collective-permute-done | bytes 16416 | tf_op jit(solution)/shard_map/ppermute | solution.py:44
  76.0 0.6 add_add_fusion
  (47 shorter events, 0.3 us)
Async XLA Ops:
  0.0 2.2 %collective-permute-start.1 = (bf16[2048,128]{1,0:T(8,128)(2,1)}, bf16[2048,128]{1,0:T(8,128)(2,1)S(1)}, u32[]{:S(2)}, u32[]{:S(2)}) collective-permute-start(bf16[2048,128]{1,0:T(8,128)(2,1)} %bitcast.23), channel_id=1, source_target_pairs={{0,4},{4,0},{8,12},{12,8},{16,20},{20,16},{24,28},{28,24},{1,5},{5... | collective-permute-start | bytes 1572872 | tf_op jit(solution)/shard_map/ppermute | solution.py:44
  2.2 1.0 %copy-start = (bf16[1,2048,128]{2,1,0:T(8,128)(2,1)S(1)}, bf16[1,2048,128]{2,1,0:T(8,128)(2,1)}, u32[]{:S(2)}) copy-start(bf16[1,2048,128]{2,1,0:T(8,128)(2,1)} %param.13) | copy-start | bytes 1572868
  3.2 7.0 %copy-start.5 = (bf16[2048,128]{1,0:T(8,128)(2,1)}, bf16[2048,128]{1,0:T(8,128)(2,1)S(1)}, u32[]{:S(2)}) copy-start(bf16[2048,128]{1,0:T(8,128)(2,1)S(1)} %collective-permute-done.1.refs_1_.refs_6_) | copy-start | bytes 1572868
  3.2 4.0 %copy-start.2 = (bf16[1,2048,128]{2,1,0:T(8,128)(2,1)S(1)}, bf16[1,2048,128]{2,1,0:T(8,128)(2,1)}, u32[]{:S(2)}) copy-start(bf16[1,2048,128]{2,1,0:T(8,128)(2,1)} %param.14) | copy-start | bytes 1572868
  3.2 8.1 %copy-start.8 = (f32[2,2048]{1,0:T(2,128)S(1)}, f32[2,2048]{1,0:T(2,128)}, u32[]{:S(2)}) copy-start(f32[2,2048]{1,0:T(2,128)} %tokens_ref.3) | copy-start | bytes 49156
  3.2 10.4 %copy-start.7 = (f32[1,16384]{1,0:T(1,128)S(1)}, f32[1,16384]{1,0:T(1,128)}, u32[]{:S(2)}) copy-start(f32[1,16384]{1,0:T(1,128)} %param.11) | copy-start | bytes 196612
  4.3 19.1 %collective-permute-start.12 = (bf16[4096,128]{1,0:T(8,128)(2,1)}, bf16[4096,128]{1,0:T(8,128)(2,1)S(1)}, u32[]{:S(2)}, u32[]{:S(2)}) collective-permute-start(bf16[4096,128]{1,0:T(8,128)(2,1)} %join.3), channel_id=1, source_target_pairs={{0,8},{4,20},{8,0},{12,28},{16,24},{20,4},{24,16},{28,12},{1,9},{5... | collective-permute-start | bytes 3145736 | tf_op jit(solution)/shard_map/ppermute | solution.py:65
  7.3 1.9 %collective-permute-start.2 = (bf16[2048,128]{1,0:T(8,128)(2,1)S(1)}, bf16[2048,128]{1,0:T(8,128)(2,1)S(1)}, u32[]{:S(2)}, u32[]{:S(2)}) collective-permute-start(bf16[2048,128]{1,0:T(8,128)(2,1)S(1)} %bitcast.27), channel_id=1, source_target_pairs={{0,4},{4,0},{8,12},{12,8},{16,20},{20,16},{24,28},{28,24},{1,5},{5... | collective-permute-start | bytes 1572872 | tf_op jit(solution)/shard_map/ppermute | solution.py:44
  10.3 21.4 %collective-permute-start.5 = (bf16[4096,128]{1,0:T(8,128)(2,1)}, bf16[4096,128]{1,0:T(8,128)(2,1)S(1)}, u32[]{:S(2)}, u32[]{:S(2)}) collective-permute-start(bf16[4096,128]{1,0:T(8,128)(2,1)} %join.2), channel_id=1, source_target_pairs={{0,8},{4,20},{8,0},{12,28},{16,24},{20,4},{24,16},{28,12},{1,9},{5... | collective-permute-start | bytes 3145736 | tf_op jit(solution)/shard_map/ppermute | solution.py:65
  11.4 1.2 %collective-permute-start = (f32[2,128]{1,0:T(2,128)S(1)}, f32[2,128]{1,0:T(2,128)S(1)}, u32[]{:S(2)}, u32[]{:S(2)}) collective-permute-start(f32[2,128]{1,0:T(2,128)S(1)} %get-tuple-element.29), channel_id=1, source_target_pairs={{0,4},{4,0},{8,12},{12,8},{16,20},{20,16},{24,28},{28,24},{1,5},{5... | collective-permute-start | bytes 3080 | tf_op jit(solution)/shard_map/ppermute | solution.py:44
  12.6 4.1 %collective-permute-start.3 = (f32[2,128]{1,0:T(2,128)S(1)}, f32[2,128]{1,0:T(2,128)S(1)}, u32[]{:S(2)}, u32[]{:S(2)}) collective-permute-start(f32[2,128]{1,0:T(2,128)S(1)} %add.53), channel_id=1, source_target_pairs={{0,16},{4,12},{8,24},{12,4},{16,0},{20,28},{24,8},{28,20},{1,17},{... | collective-permute-start | bytes 3080 | tf_op jit(solution)/shard_map/ppermute | solution.py:65
  16.8 1.2 %collective-permute-start.4 = (f32[2,128]{1,0:T(2,128)S(1)}, f32[2,128]{1,0:T(2,128)S(1)}, u32[]{:S(2)}, u32[]{:S(2)}) collective-permute-start(f32[2,128]{1,0:T(2,128)S(1)} %collective-permute-done.3), channel_id=1, source_target_pairs={{0,4},{4,0},{8,12},{12,8},{16,20},{20,16},{24,28},{28,24},{1,5},{5... | collective-permute-start | bytes 3080 | tf_op jit(solution)/shard_map/ppermute | solution.py:44
  18.0 5.4 %collective-permute-start.6 = (f32[2,128]{1,0:T(2,128)S(1)}, f32[2,128]{1,0:T(2,128)S(1)}, u32[]{:S(2)}, u32[]{:S(2)}) collective-permute-start(f32[2,128]{1,0:T(2,128)S(1)} %collective-permute-done.4), channel_id=1, source_target_pairs={{0,16},{4,12},{8,24},{12,4},{16,0},{20,28},{24,8},{28,20},{1,17},{... | collective-permute-start | bytes 3080 | tf_op jit(solution)/shard_map/ppermute | solution.py:65
  19.1 4.7 %copy-start.1 = (bf16[1,2048,128]{2,1,0:T(8,128)(2,1)S(1)}, bf16[1,2048,128]{2,1,0:T(8,128)(2,1)}, u32[]{:S(2)}) copy-start(bf16[1,2048,128]{2,1,0:T(8,128)(2,1)} %param.13) | copy-start | bytes 1572868
  19.1 4.7 %copy-start.3 = (bf16[1,2048,1024]{2,1,0:T(8,128)(2,1)S(1)}, bf16[1,2048,1024]{2,1,0:T(8,128)(2,1)}, u32[]{:S(2)}) copy-start(bf16[1,2048,1024]{2,1,0:T(8,128)(2,1)} %param.12) | copy-start | bytes 12582916
  23.4 8.3 %collective-permute-start.13 = (bf16[4096,128]{1,0:T(8,128)(2,1)S(1)}, bf16[4096,128]{1,0:T(8,128)(2,1)S(1)}, u32[]{:S(2)}, u32[]{:S(2)}) collective-permute-start(bf16[4096,128]{1,0:T(8,128)(2,1)S(1)} %collective-permute-done.12.refs_5_.refs_6_), channel_id=1, source_target_pairs={{0,4},{4,0},{8,12},{12,8},{16,20},{20,16},{24,28},{28,24},{1,5},{5... | collective-permute-start | bytes 3145736 | tf_op jit(solution)/shard_map/ppermute | solution.py:44
  23.8 7.9 %copy-start.10 = (s32[2]{0:T(128)S(1)}, s32[2]{0:T(128)}, u32[]{:S(2)}) copy-start(s32[2]{0:T(128)} %param.17) | copy-start | bytes 28
  23.8 10.9 %copy-start.6 = (bf16[2048,128]{1,0:T(8,128)(2,1)S(1)}, bf16[2048,128]{1,0:T(8,128)(2,1)}, u32[]{:S(2)}) copy-start(bf16[2048,128]{1,0:T(8,128)(2,1)} %copy-done.5) | copy-start | bytes 1572868
  24.6 1.5 %collective-permute-start.7 = (f32[2,10,128]{2,1,0:T(8,128)S(1)}, f32[2,10,128]{2,1,0:T(8,128)S(1)}, u32[]{:S(2)}, u32[]{:S(2)}) collective-permute-start(f32[2,10,128]{2,1,0:T(8,128)S(1)} %query_products.1), channel_id=1, source_target_pairs={{0,4},{4,0},{8,12},{12,8},{16,20},{20,16},{24,28},{28,24},{1,5},{5... | collective-permute-start | bytes 30728 | tf_op jit(solution)/shard_map/ppermute | solution.py:44
  26.2 4.0 %collective-permute-start.8 = (f32[2,10,128]{2,1,0:T(8,128)S(1)}, f32[2,10,128]{2,1,0:T(8,128)S(1)}, u32[]{:S(2)}, u32[]{:S(2)}) collective-permute-start(f32[2,10,128]{2,1,0:T(8,128)S(1)} %add.57), channel_id=1, source_target_pairs={{0,16},{4,12},{8,24},{12,4},{16,0},{20,28},{24,8},{28,20},{1,17},{... | collective-permute-start | bytes 30728 | tf_op jit(solution)/shard_map/ppermute | solution.py:65
  30.1 1.2 %collective-permute-start.9 = (f32[2,10,128]{2,1,0:T(8,128)S(1)}, f32[2,10,128]{2,1,0:T(8,128)S(1)}, u32[]{:S(2)}, u32[]{:S(2)}) collective-permute-start(f32[2,10,128]{2,1,0:T(8,128)S(1)} %collective-permute-done.8), channel_id=1, source_target_pairs={{0,4},{4,0},{8,12},{12,8},{16,20},{20,16},{24,28},{28,24},{1,5},{5... | collective-permute-start | bytes 30728 | tf_op jit(solution)/shard_map/ppermute | solution.py:44
  31.7 5.4 %collective-permute-start.10 = (bf16[4096,128]{1,0:T(8,128)(2,1)S(1)}, bf16[4096,128]{1,0:T(8,128)(2,1)S(1)}, u32[]{:S(2)}, u32[]{:S(2)}) collective-permute-start(bf16[4096,128]{1,0:T(8,128)(2,1)S(1)} %collective-permute-done.5.refs_5_.refs_6_), channel_id=1, source_target_pairs={{0,4},{4,0},{8,12},{12,8},{16,20},{20,16},{24,28},{28,24},{1,5},{5... | collective-permute-start | bytes 3145736 | tf_op jit(solution)/shard_map/ppermute | solution.py:44
  31.8 9.4 %collective-permute-start.14 = (bf16[2048,128]{1,0:T(8,128)(2,1)S(1)}, bf16[2048,128]{1,0:T(8,128)(2,1)S(1)}, u32[]{:S(2)}, u32[]{:S(2)}) collective-permute-start(bf16[2048,128]{1,0:T(8,128)(2,1)S(1)} %slice.25), channel_id=1, source_target_pairs={{0,8},{4,20},{8,0},{12,28},{16,24},{20,4},{24,16},{28,12},{1,9},{5... | collective-permute-start | bytes 1572872 | tf_op jit(solution)/shard_map/ppermute | solution.py:65
  35.5 5.7 %collective-permute-start.16 = (f32[2,10,128]{2,1,0:T(8,128)S(1)}, f32[2,10,128]{2,1,0:T(8,128)S(1)}, u32[]{:S(2)}, u32[]{:S(2)}) collective-permute-start(f32[2,10,128]{2,1,0:T(8,128)S(1)} %collective-permute-done.9), channel_id=1, source_target_pairs={{0,16},{4,12},{8,24},{12,4},{16,0},{20,28},{24,8},{28,20},{1,17},{... | collective-permute-start | bytes 30728 | tf_op jit(solution)/shard_map/ppermute | solution.py:65
  37.2 14.2 %collective-permute-start.11 = (bf16[2048,128]{1,0:T(8,128)(2,1)S(1)}, bf16[2048,128]{1,0:T(8,128)(2,1)S(1)}, u32[]{:S(2)}, u32[]{:S(2)}) collective-permute-start(bf16[2048,128]{1,0:T(8,128)(2,1)S(1)} %slice.24), channel_id=1, source_target_pairs={{0,8},{4,20},{8,0},{12,28},{16,24},{20,4},{24,16},{28,12},{1,9},{5... | collective-permute-start | bytes 1572872 | tf_op jit(solution)/shard_map/ppermute | solution.py:65
  41.2 1.9 %collective-permute-start.15 = (bf16[2048,128]{1,0:T(8,128)(2,1)S(1)}, bf16[2048,128]{1,0:T(8,128)(2,1)S(1)}, u32[]{:S(2)}, u32[]{:S(2)}) collective-permute-start(bf16[2048,128]{1,0:T(8,128)(2,1)S(1)} %collective-permute-done.14.refs_5_), channel_id=1, source_target_pairs={{0,4},{4,0},{8,12},{12,8},{16,20},{20,16},{24,28},{28,24},{1,5},{5... | collective-permute-start | bytes 1572872 | tf_op jit(solution)/shard_map/ppermute | solution.py:44
  41.3 2.7 %copy-start.9 = (s32[2]{0:T(128)S(1)}, s32[2]{0:T(128)}, u32[]{:S(2)}) copy-start(s32[2]{0:T(128)} %lengths_ref.3) | copy-start | bytes 28
  45.0 1.2 %collective-permute-start.17 = (f32[8,128]{1,0:T(8,128)S(1)}, f32[8,128]{1,0:T(8,128)S(1)}, u32[]{:S(2)}, u32[]{:S(2)}) collective-permute-start(f32[8,128]{1,0:T(8,128)S(1)} %get-tuple-element.45), channel_id=1, source_target_pairs={{0,4},{4,0},{8,12},{12,8},{16,20},{20,16},{24,28},{28,24},{1,5},{5... | collective-permute-start | bytes 12296 | tf_op jit(solution)/shard_map/ppermute | solution.py:44
  46.2 3.6 %collective-permute-start.18 = (f32[8,128]{1,0:T(8,128)S(1)}, f32[8,128]{1,0:T(8,128)S(1)}, u32[]{:S(2)}, u32[]{:S(2)}) collective-permute-start(f32[8,128]{1,0:T(8,128)S(1)} %max.6), channel_id=1, source_target_pairs={{0,8},{4,12},{8,0},{12,4},{16,24},{20,28},{24,16},{28,20},{1,9},{5... | collective-permute-start | bytes 12296 | tf_op jit(solution)/shard_map/ppermute | solution.py:44
  51.3 2.0 %collective-permute-start.19 = (bf16[2048,128]{1,0:T(8,128)(2,1)S(1)}, bf16[2048,128]{1,0:T(8,128)(2,1)S(1)}, u32[]{:S(2)}, u32[]{:S(2)}) collective-permute-start(bf16[2048,128]{1,0:T(8,128)(2,1)S(1)} %collective-permute-done.11.refs_5_), channel_id=1, source_target_pairs={{0,4},{4,0},{8,12},{12,8},{16,20},{20,16},{24,28},{28,24},{1,5},{5... | collective-permute-start | bytes 1572872 | tf_op jit(solution)/shard_map/ppermute | solution.py:44
  53.3 13.5 %copy-start.4 = (bf16[1,1024,2048]{2,1,0:T(8,128)(2,1)S(1)}, bf16[1,1024,2048]{2,1,0:T(8,128)(2,1)}, u32[]{:S(2)}) copy-start(bf16[1,1024,2048]{2,1,0:T(8,128)(2,1)} %param.15) | copy-start | bytes 12582916
  54.5 1.2 %collective-permute-start.20 = (f32[8,256]{1,0:T(8,128)S(1)}, f32[8,256]{1,0:T(8,128)S(1)}, u32[]{:S(2)}, u32[]{:S(2)}) collective-permute-start(f32[8,256]{1,0:T(8,128)S(1)} %weighted_values.1), channel_id=1, source_target_pairs={{0,4},{4,0},{8,12},{12,8},{16,20},{20,16},{24,28},{28,24},{1,5},{5... | collective-permute-start | bytes 24584 | tf_op jit(solution)/shard_map/ppermute | solution.py:44
  55.7 0.7 collective-permute-start.21
  56.3 0.7 collective-permute-start.22
  57.0 9.8 %collective-permute-start.23 = (f32[16,256]{1,0:T(8,128)S(1)}, f32[16,256]{1,0:T(8,128)S(1)}, u32[]{:S(2)}, u32[]{:S(2)}) collective-permute-start(f32[16,256]{1,0:T(8,128)S(1)} %pad_maximum_fusion), channel_id=1, source_target_pairs={{4,0},{12,8},{20,16},{28,24},{5,1},{13,9},{21,17},{29,25},{6,2},{1... | collective-permute-start | bytes 49160 | tf_op jit(solution)/shard_map/ppermute | solution.py:454
  67.5 3.8 %collective-permute-start.24 = (f32[2,2048]{1,0:T(2,128)S(1)}, f32[2,2048]{1,0:T(2,128)S(1)}, u32[]{:S(2)}, u32[]{:S(2)}) collective-permute-start(f32[2,2048]{1,0:T(2,128)S(1)} %output_products.1), channel_id=1, source_target_pairs={{0,1},{1,0},{2,3},{3,2},{4,5},{5,4},{6,7},{7,6},{8,9},{9,8},{10,11... | collective-permute-start | bytes 49160 | tf_op jit(solution)/shard_map/ppermute | solution.py:44
  71.3 4.7 %collective-permute-start.25 = (f32[2,2048]{1,0:T(2,128)S(1)}, f32[2,2048]{1,0:T(2,128)S(1)}, u32[]{:S(2)}, u32[]{:S(2)}) collective-permute-start(f32[2,2048]{1,0:T(2,128)S(1)} %add.66), channel_id=1, source_target_pairs={{0,2},{1,3},{2,0},{3,1},{4,6},{5,7},{6,4},{7,5},{8,10},{9,11},{10,... | collective-permute-start | bytes 49160 | tf_op jit(solution)/shard_map/ppermute | solution.py:44

commit v9 on v7

--- a/solution.py
+++ b/solution.py
@@ -346,7 +346,7 @@
             opposite = beside(opposite, told, row_count // NORM_ROWS - norm_parts)
         over_x = jnp.where(core == 0, told, received)
         over_y = jnp.where(core == 0, received, told)
-        return (value + over_x) + (over_y + opposite), told
+        return (value + over_x) + (over_y + opposite), told, received
 
     key_partner = swap(key_weight[0], "ctx", 1)
     value_partner = swap(value_weight[0], "ctx", 1)
@@ -357,7 +357,7 @@
     squares = squares + swap(squares, "ctx", 1)
     squares = after(squares, key_partner, value_partner)
     if split:
-        squares, told = sum_chips(squares, row_count // NORM_ROWS // 2)
+        squares, told, _ = sum_chips(squares, row_count // NORM_ROWS // 2)
         key_shared = share(key_far, told)
         squares = after(squares, key_far[1][1], key_shared[0][1])
     else:
@@ -376,7 +376,7 @@
     parts_sent = parts
     value_far = send_first(value_weight[0], after(value_partner, parts))
     if split:
-        parts, _ = sum_chips(parts)
+        parts, _, parts_sent = sum_chips(parts)
         summed = jnp.where(own_request == 0, parts[0], parts[1])
     else:
         own_part = jnp.where(own_request == 0, parts[0], parts[1])
@@ -386,6 +386,7 @@
 
     key_total = project(places, rows, key_near)
     key_total = project(places, rows, key_far + key_shared, key_total)
+    key_mid = key_total
     key_total = project(places, rows, key_last + share(key_last), key_total)
 
     within = first_row[0, :1] + jnp.arange(row_count, dtype=jnp.int32)
@@ -401,12 +402,14 @@
     near_top = top
     top = butterfly(top, "ctx", bits_below(team)[1:], jnp.maximum)
 
-    value_shared = share(value_far, parts_sent)
+    value_shared = share(value_far[:1], parts_sent)
     value_last = send_last(value_weight[0], value_shared)
+    value_shared += share(value_far[1:], key_mid, *[block for _, block in value_shared])
     value_total = project(after(places, near_top), rows, value_near)
     value_total = project(after(places, top), rows, value_far + value_shared, value_total)
 
-    blocks = value_last + share(value_last, value_total)
+    blocks = share(value_last, value_total)
+    value_total = project(places, rows, value_last, value_total)
     packed = call(
         functools.partial(weigh_kernel, [d for d, _ in blocks], len(rows), team),
         "weighted_values",

time: 70.8 us -> 70.6 us (level)
  waiting for transfers between devices: 29.3 us -> 28.2 us
    ppermute x10, waiting for transfers between devices: 12.7 us -> 10.2 us  [by_core(): return lax.ppermute(value, 'ctx', pairs)]
    ppermute x19, waiting for transfers between devices: 16.5 us -> 18 us  [swap(): return lax.ppermute(value, axis, [(i, i ^ distance) for i in range(count)])]
    ppermute x10, starting transfers between devices: 10.4 us -> 11.7 us  [by_core(): return lax.ppermute(value, 'ctx', pairs)]
    pallas_call x5 -> x6, Pallas kernels: 5.66 us -> 6.17 us  [project(): call(functools.partial(project_kernel, [d for d, _ in blocks], len(rows),...]
  transfers between devices with their start and end apart: 29 -> 29, of which waited for: 16 -> 15; matrix products, arithmetic and copies ran while one was open for 1% -> 1% of each run, Pallas kernels for 21% -> 22%
where the time goes in v9:
time: 70.6 us; the launch traced here: 70.4 us
  waiting for transfers between devices  28.2 us (40%)
  starting transfers between devices  21.5 us (30%)
  Pallas kernels  17.4 us (25%)
  local copies, waits for them, and re-layouts  1.59 us (2%)
  other arithmetic  1.49 us (2%)
    ppermute x19, waiting for transfers between devices, swap(): return lax.ppermute(value, axis, [(i, i ^ distance) for i in range(count)])  18 us
    ppermute x10, starting transfers between devices, by_core(): return lax.ppermute(value, 'ctx', pairs)  11.7 us
    ppermute x10, waiting for transfers between devices, by_core(): return lax.ppermute(value, 'ctx', pairs)  10.2 us
    ppermute x19, starting transfers between devices, swap(): return lax.ppermute(value, axis, [(i, i ^ distance) for i in range(count)])  9.85 us
    pallas_call x2, Pallas kernels, normalise(): call(functools.partial(norm_kernel, first), 'normalise', [IN_HBM, IN_VMEM...  7.47 us
    pallas_call x6, Pallas kernels, project(): call(functools.partial(project_kernel, [d for d, _ in blocks], len(rows),...  6.17 us
    unnamed x18, local copies, waits for them, and re-layouts  1.59 us
  transfers between devices with their start and end apart: 29, of which 15 were waited for; matrix products, arithmetic and copies ran while one was open for 1% of the time, Pallas kernels for 22%

profile of v9, /device:TPU:0, one launch (start us, length us, event | category | flops | bytes accessed | tf_op | source)
XLA Modules:
  0.0 70.4 jit_solution(13171010161918554021)
XLA Ops:
  0.0 0.5 collective-permute-start.1
  0.5 0.1 collective-permute-start.2
  0.5 2.9 %collective-permute-start.8 = (bf16[2048,128]{1,0:T(8,128)(2,1)}, bf16[2048,128]{1,0:T(8,128)(2,1)S(1)}, u32[]{:S(2)}, u32[]{:S(2)}) collective-permute-start(bf16[2048,128]{1,0:T(8,128)(2,1)} %bitcast.24), channel_id=1, source_target_pairs={{0,8},{4,20},{8,0},{12,28},{16,24},{20,4},{24,16},{28,12},{1,9},{5... | collective-permute-start | bytes 1572872 | tf_op jit(solution)/shard_map/ppermute | solution.py:64
  3.5 0.7 %copy-done.5 = f32[2,2048]{1,0:T(2,128)S(1)} copy-done((f32[2,2048]{1,0:T(2,128)S(1)}, f32[2,2048]{1,0:T(2,128)}, u32[]{:S(2)}) %copy-start.5) | copy-done | bytes 16408
  4.2 0.1 squares.1
  4.3 0.0 collective-permute-start
  4.3 1.1 %collective-permute-done = f32[2,128]{1,0:T(2,128)S(1)} collective-permute-done((f32[2,128]{1,0:T(2,128)S(1)}, f32[2,128]{1,0:T(2,128)S(1)}, u32[]{:S(2)}, u32[]{:S(2)}) %collective-permute-start) | collective-permute-done | bytes 1056 | tf_op jit(solution)/shard_map/ppermute | solution.py:43
  5.4 1.6 %collective-permute-start.3 = (f32[2,128]{1,0:T(2,128)S(1)}, f32[2,128]{1,0:T(2,128)S(1)}, u32[]{:S(2)}, u32[]{:S(2)}) collective-permute-start(f32[2,128]{1,0:T(2,128)S(1)} %add.53), channel_id=1, source_target_pairs={{0,16},{4,12},{8,24},{12,4},{16,0},{20,28},{24,8},{28,20},{1,17},{... | collective-permute-start | bytes 3080 | tf_op jit(solution)/shard_map/ppermute | solution.py:64
  7.0 0.8 %copy-done.4 = f32[1,16384]{1,0:T(1,128)S(1)} copy-done((f32[1,16384]{1,0:T(1,128)S(1)}, f32[1,16384]{1,0:T(1,128)}, u32[]{:S(2)}) %copy-start.4) | copy-done | bytes 65560
  7.8 3.2 %normalise.2 = (bf16[8,64,2048]{2,1,0:T(8,128)(2,1)S(1)}, bf16[8,64,2048]{2,1,0:T(8,128)(2,1)S(1)}) custom-call(bf16[320,16384]{1,0:T(8,128)(2,1)} %bitcast.35, f32[8,1,2048]{2,1,0:T(1,128)S(1)} %bitcast.31), custom_call_target="tpu_custom_call" | custom-call | flops 1000 | bytes 1000 | tf_op jit(solution)/shard_map/normalise/pallas_call | solution.py:173
  11.0 0.0 collective-permute-done.3
  11.0 0.1 collective-permute-start.4
  11.1 0.6 collective-permute-start.7
  11.7 0.0 collective-permute-done.8.refs_5_
  11.7 0.5 collective-permute-done.4
  12.3 0.2 collective-permute-start.9
  12.4 0.9 %collective-permute-start.5 = (bf16[2048,128]{1,0:T(8,128)(2,1)S(1)}, bf16[2048,128]{1,0:T(8,128)(2,1)S(1)}, u32[]{:S(2)}, u32[]{:S(2)}) collective-permute-start(bf16[2048,128]{1,0:T(8,128)(2,1)S(1)} %bitcast.28), channel_id=1, source_target_pairs={{0,8},{4,20},{8,0},{12,28},{16,24},{20,4},{24,16},{28,12},{1,9},{5... | collective-permute-start | bytes 1572872 | tf_op jit(solution)/shard_map/ppermute | solution.py:64
  13.3 1.1 %collective-permute-start.6 = (f32[2,128]{1,0:T(2,128)S(1)}, f32[2,128]{1,0:T(2,128)S(1)}, u32[]{:S(2)}, u32[]{:S(2)}) collective-permute-start(f32[2,128]{1,0:T(2,128)S(1)} %collective-permute-done.4), channel_id=1, source_target_pairs={{0,16},{4,12},{8,24},{12,4},{16,0},{20,28},{24,8},{28,20},{1,17},{... | collective-permute-start | bytes 3080 | tf_op jit(solution)/shard_map/ppermute | solution.py:64
  14.5 4.3 %normalise.3 = (bf16[8,64,2048]{2,1,0:T(8,128)(2,1)S(1)}, bf16[8,64,2048]{2,1,0:T(8,128)(2,1)S(1)}, bf16[8,64,2048]{2,1,0:T(8,128)(2,1)S(1)}) custom-call(bf16[320,16384]{1,0:T(8,128)(2,1)} %bitcast.36, f32[8,1,2048]{2,1,0:T(1,128)S(1)} %bitcast.32), custom_call_target="tpu_custom_call" | custom-call | flops 1000 | bytes 1000 | tf_op jit(solution)/shard_map/normalise/pallas_call | solution.py:173
  18.8 1.6 %collective-permute-done.7.refs_6_ = bf16[2048,128]{1,0:T(8,128)(2,1)S(1)} collective-permute-done((bf16[2048,128]{1,0:T(8,128)(2,1)S(1)}, bf16[2048,128]{1,0:T(8,128)(2,1)S(1)}, u32[]{:S(2)}, u32[]{:S(2)}) %collective-permute-start.7) | collective-permute-done | bytes 524320 | tf_op jit(solution)/shard_map/ppermute | solution.py:64
  20.4 0.0 copy-start.8
  20.4 0.8 %query_products.1 = f32[2,10,128]{2,1,0:T(8,128)S(1)} custom-call(s32[1]{0:T(128)} %bitcast.place_ref, f32[2,128]{1,0:T(2,128)S(1)} %add_add_fusion.2.squares_ref, f32[2,2048]{1,0:T(2,128)S(1)} %copy-done.5, f32[8,1,2048]{2,1,0:T(1,128)S(1)} %bitcast.33, bf16[2048,1024]{1,0:T(8,128)(2,1)S(1)} %bitcast.21, bf16[2048,128]{1,0:T(8,128)(2,1)S(1)} %bitcast.25, ...), custom_call_target="tpu_custom_call" | custom-call | flops 1000 | bytes 1000 | tf_op jit(solution)/shard_map/query_products/pallas_call | solution.py:369
  21.2 0.1 collective-permute-start.10
  21.3 1.2 %collective-permute-done.10 = f32[2,10,128]{2,1,0:T(8,128)S(1)} collective-permute-done((f32[2,10,128]{2,1,0:T(8,128)S(1)}, f32[2,10,128]{2,1,0:T(8,128)S(1)}, u32[]{:S(2)}, u32[]{:S(2)}) %collective-permute-start.10) | collective-permute-done | bytes 10272 | tf_op jit(solution)/shard_map/ppermute | solution.py:43
  22.5 0.5 collective-permute-start.11
  23.1 0.1 collective-permute-start.16
  23.1 1.4 %collective-permute-start.14 = (bf16[2048,128]{1,0:T(8,128)(2,1)S(1)}, bf16[2048,128]{1,0:T(8,128)(2,1)S(1)}, u32[]{:S(2)}, u32[]{:S(2)}) collective-permute-start(bf16[2048,128]{1,0:T(8,128)(2,1)S(1)} %collective-permute-done.9.refs_7_), channel_id=1, source_target_pairs={{0,8},{4,20},{8,0},{12,28},{16,24},{20,4},{24,16},{28,12},{1,9},{5... | collective-permute-start | bytes 1572872 | tf_op jit(solution)/shard_map/ppermute | solution.py:64
  24.6 0.7 collective-permute-start.21
  25.2 0.9 %collective-permute-done.5.refs_5_ = bf16[2048,128]{1,0:T(8,128)(2,1)S(1)} collective-permute-done((bf16[2048,128]{1,0:T(8,128)(2,1)S(1)}, bf16[2048,128]{1,0:T(8,128)(2,1)S(1)}, u32[]{:S(2)}, u32[]{:S(2)}) %collective-permute-start.5) | collective-permute-done | bytes 524320 | tf_op jit(solution)/shard_map/ppermute | solution.py:64
  26.2 0.0 collective-permute-done.11
  26.2 0.6 multiply_sine_fusion
  26.9 0.6 collective-permute-start.17
  27.5 0.1 multiply_sine_fusion.1
  27.6 0.9 %project.6.refs_9_ = f32[320,128]{1,0:T(8,128)S(1)} custom-call(s32[1]{0:T(128)} %bitcast.place_ref, bf16[8,64,2048]{2,1,0:T(8,128)(2,1)S(1)} %get-tuple-element.34.refs_0_, bf16[8,64,2048]{2,1,0:T(8,128)(2,1)S(1)} %get-tuple-element.35.refs_1_, bf16[8,64,2048]{2,1,0:T(8,128)(2,1)S(1)} %get-tuple-element.38.refs_2_, ...), custom_call_target="tpu_custom_call" | custom-call | flops 1000 | bytes 1000 | tf_op jit(solution)/shard_map/project/pallas_call | solution.py:218
  28.4 0.6 collective-permute-start.18
  29.0 1.5 %project.7.refs_7_ = f32[320,128]{1,0:T(8,128)S(1)} custom-call(s32[1]{0:T(128)} %bitcast.place_ref, bf16[8,64,2048]{2,1,0:T(8,128)(2,1)S(1)} %get-tuple-element.34.refs_0_, bf16[8,64,2048]{2,1,0:T(8,128)(2,1)S(1)} %get-tuple-element.35.refs_1_, bf16[8,64,2048]{2,1,0:T(8,128)(2,1)S(1)} %get-tuple-element.38.refs_2_, ...), custom_call_target="tpu_custom_call" | custom-call | flops 1000 | bytes 1000 | tf_op jit(solution)/shard_map/project/pallas_call | solution.py:218
  30.6 2.0 %collective-permute-done.14.refs_5_ = bf16[2048,128]{1,0:T(8,128)(2,1)S(1)} collective-permute-done((bf16[2048,128]{1,0:T(8,128)(2,1)S(1)}, bf16[2048,128]{1,0:T(8,128)(2,1)S(1)}, u32[]{:S(2)}, u32[]{:S(2)}) %collective-permute-start.14) | collective-permute-done | bytes 524320 | tf_op jit(solution)/shard_map/ppermute | solution.py:64
  32.6 5.6 %collective-permute-done.21.refs_6_ = bf16[2048,128]{1,0:T(8,128)(2,1)S(1)} collective-permute-done((bf16[2048,128]{1,0:T(8,128)(2,1)S(1)}, bf16[2048,128]{1,0:T(8,128)(2,1)S(1)}, u32[]{:S(2)}, u32[]{:S(2)}) %collective-permute-start.21) | collective-permute-done | bytes 524320 | tf_op jit(solution)/shard_map/ppermute | solution.py:64
  38.2 1.4 %collective-permute-start.13 = (bf16[2048,128]{1,0:T(8,128)(2,1)S(1)}, bf16[2048,128]{1,0:T(8,128)(2,1)S(1)}, u32[]{:S(2)}, u32[]{:S(2)}) collective-permute-start(bf16[2048,128]{1,0:T(8,128)(2,1)S(1)} %collective-permute-done.12.refs_7_), channel_id=1, source_target_pairs={{0,8},{4,20},{8,0},{12,28},{16,24},{20,4},{24,16},{28,12},{1,9},{5... | collective-permute-start | bytes 1572872 | tf_op jit(solution)/shard_map/ppermute | solution.py:64
  39.6 0.0 copy-start.7
  39.6 0.9 %project.8.refs_0_ = f32[320,128]{1,0:T(8,128)S(1)} custom-call(s32[1]{0:T(128)} %bitcast.place_ref, bf16[8,64,2048]{2,1,0:T(8,128)(2,1)S(1)} %get-tuple-element.34.refs_0_, bf16[8,64,2048]{2,1,0:T(8,128)(2,1)S(1)} %get-tuple-element.35.refs_1_, bf16[8,64,2048]{2,1,0:T(8,128)(2,1)S(1)} %get-tuple-element.38.refs_2_, ...), custom_call_target="tpu_custom_call" | custom-call | flops 1000 | bytes 1000 | tf_op jit(solution)/shard_map/project/pallas_call | solution.py:218
  40.5 1.0 %scores.1 = (f32[8,320]{1,0:T(8,128)S(1)}, f32[8,128]{1,0:T(8,128)S(1)}, f32[8,128]{1,0:T(8,128)S(1)}) custom-call(s32[1]{0:T(128)} %bitcast.place_ref, s32[2]{0:T(128)S(1)} %copy-done.7, f32[320,128]{1,0:T(8,128)S(1)} %project.8.refs_0_, f32[320,64]{1,0:T(8,128)S(1)} %get-tuple-element.58.refs_1_, f32[320,64]{1,0:T(8,128)S(1)} %get-tuple-element.57.refs_2_, ...), custom_call_target="tpu_custom_call" | custom-call | flops 1000 | bytes 1000 | tf_op jit(solution)/shard_map/scores/pallas_call | solution.py:395
  41.5 0.4 collective-permute-start.19
  41.9 0.8 %collective-permute-done.19 = f32[8,128]{1,0:T(8,128)S(1)} collective-permute-done((f32[8,128]{1,0:T(8,128)S(1)}, f32[8,128]{1,0:T(8,128)S(1)}, u32[]{:S(2)}, u32[]{:S(2)}) %collective-permute-start.19) | collective-permute-done | bytes 4128 | tf_op jit(solution)/shard_map/ppermute | solution.py:43
  42.7 0.6 collective-permute-start.20
  43.3 0.9 %project.9.refs_9_ = f32[320,128]{1,0:T(8,128)S(1)} custom-call(s32[1]{0:T(128)} %bitcast.place_ref, bf16[8,64,2048]{2,1,0:T(8,128)(2,1)S(1)} %get-tuple-element.34.refs_0_, bf16[8,64,2048]{2,1,0:T(8,128)(2,1)S(1)} %get-tuple-element.35.refs_1_, bf16[8,64,2048]{2,1,0:T(8,128)(2,1)S(1)} %get-tuple-element.38.refs_2_, ...), custom_call_target="tpu_custom_call" | custom-call | flops 1000 | bytes 1000 | tf_op jit(solution)/shard_map/project/pallas_call | solution.py:218
  44.2 3.3 %collective-permute-done.20 = f32[8,128]{1,0:T(8,128)S(1)} collective-permute-done((f32[8,128]{1,0:T(8,128)S(1)}, f32[8,128]{1,0:T(8,128)S(1)}, u32[]{:S(2)}, u32[]{:S(2)}) %collective-permute-start.20) | collective-permute-done | bytes 4128 | tf_op jit(solution)/shard_map/ppermute | solution.py:43
  47.5 1.5 %project.10.refs_6_ = f32[320,128]{1,0:T(8,128)S(1)} custom-call(s32[1]{0:T(128)} %bitcast.place_ref, bf16[8,64,2048]{2,1,0:T(8,128)(2,1)S(1)} %get-tuple-element.34.refs_0_, bf16[8,64,2048]{2,1,0:T(8,128)(2,1)S(1)} %get-tuple-element.35.refs_1_, bf16[8,64,2048]{2,1,0:T(8,128)(2,1)S(1)} %get-tuple-element.38.refs_2_, ...), custom_call_target="tpu_custom_call" | custom-call | flops 1000 | bytes 1000 | tf_op jit(solution)/shard_map/project/pallas_call | solution.py:218
  49.0 0.1 collective-permute-start.23
  49.1 0.5 project.11.refs_6_
  49.6 1.4 %collective-permute-done.23.refs_5_ = bf16[2048,128]{1,0:T(8,128)(2,1)S(1)} collective-permute-done((bf16[2048,128]{1,0:T(8,128)(2,1)S(1)}, bf16[2048,128]{1,0:T(8,128)(2,1)S(1)}, u32[]{:S(2)}, u32[]{:S(2)}) %collective-permute-start.23) | collective-permute-done | bytes 524320 | tf_op jit(solution)/shard_map/ppermute | solution.py:43
  51.0 1.2 %weighted_values.1 = f32[8,256]{1,0:T(8,128)S(1)} custom-call(s32[1]{0:T(128)} %bitcast.place_ref, s32[2]{0:T(128)S(1)} %copy-done.7, bf16[8,64,2048]{2,1,0:T(8,128)(2,1)S(1)} %get-tuple-element.34.refs_0_, bf16[8,64,2048]{2,1,0:T(8,128)(2,1)S(1)} %get-tuple-element.35.refs_1_, bf16[8,64,2048]{2,1,0:T(8,128)(2,1)S(1)} %get-tuple-element.38.refs_2_, ...), custom_call_target="tpu_custom_call" | custom-call | flops 1000 | bytes 1000 | tf_op jit(solution)/shard_map/weighted_values/pallas_call | solution.py:413
  52.2 0.1 collective-permute-start.24
  52.3 1.0 %collective-permute-done.24 = f32[8,256]{1,0:T(8,128)S(1)} collective-permute-done((f32[8,256]{1,0:T(8,128)S(1)}, f32[8,256]{1,0:T(8,128)S(1)}, u32[]{:S(2)}, u32[]{:S(2)}) %collective-permute-start.24) | collective-permute-done | bytes 8224 | tf_op jit(solution)/shard_map/ppermute | solution.py:43
  53.3 1.4 %collective-permute-start.25 = (f32[8,256]{1,0:T(8,128)S(1)}, f32[8,256]{1,0:T(8,128)S(1)}, u32[]{:S(2)}, u32[]{:S(2)}) collective-permute-start(f32[8,256]{1,0:T(8,128)S(1)} %add.64), channel_id=1, source_target_pairs={{0,8},{4,12},{8,0},{12,4},{16,24},{20,28},{24,16},{28,20},{1,9},{5... | collective-permute-start | bytes 24584 | tf_op jit(solution)/shard_map/ppermute | solution.py:43
  54.7 2.3 %collective-permute-done.25 = f32[8,256]{1,0:T(8,128)S(1)} collective-permute-done((f32[8,256]{1,0:T(8,128)S(1)}, f32[8,256]{1,0:T(8,128)S(1)}, u32[]{:S(2)}, u32[]{:S(2)}) %collective-permute-start.25) | collective-permute-done | bytes 8224 | tf_op jit(solution)/shard_map/ppermute | solution.py:43
  57.0 1.5 %collective-permute-start.26 = (f32[8,256]{1,0:T(8,128)S(1)}, f32[8,256]{1,0:T(8,128)S(1)}, u32[]{:S(2)}, u32[]{:S(2)}) collective-permute-start(f32[8,256]{1,0:T(8,128)S(1)} %add.65.mine_ref), channel_id=1, source_target_pairs={{0,16},{4,20},{8,24},{12,28},{16,0},{20,4},{24,8},{28,12},{1,17},{... | collective-permute-start | bytes 24584 | tf_op jit(solution)/shard_map/ppermute | solution.py:43
  58.5 2.1 %collective-permute-done.26.other_ref = f32[8,256]{1,0:T(8,128)S(1)} collective-permute-done((f32[8,256]{1,0:T(8,128)S(1)}, f32[8,256]{1,0:T(8,128)S(1)}, u32[]{:S(2)}, u32[]{:S(2)}) %collective-permute-start.26) | collective-permute-done | bytes 8224 | tf_op jit(solution)/shard_map/ppermute | solution.py:43
  60.7 0.6 output_products.1
  61.3 1.6 %collective-permute-start.27 = (f32[2,2048]{1,0:T(2,128)S(1)}, f32[2,2048]{1,0:T(2,128)S(1)}, u32[]{:S(2)}, u32[]{:S(2)}) collective-permute-start(f32[2,2048]{1,0:T(2,128)S(1)} %output_products.1), channel_id=1, source_target_pairs={{0,1},{1,0},{2,3},{3,2},{4,5},{5,4},{6,7},{7,6},{8,9},{9,8},{10,11... | collective-permute-start | bytes 49160 | tf_op jit(solution)/shard_map/ppermute | solution.py:43
  62.9 2.2 %collective-permute-done.27 = f32[2,2048]{1,0:T(2,128)S(1)} collective-permute-done((f32[2,2048]{1,0:T(2,128)S(1)}, f32[2,2048]{1,0:T(2,128)S(1)}, u32[]{:S(2)}, u32[]{:S(2)}) %collective-permute-start.27) | collective-permute-done | bytes 16416 | tf_op jit(solution)/shard_map/ppermute | solution.py:43
  65.1 2.7 %collective-permute-start.28 = (f32[2,2048]{1,0:T(2,128)S(1)}, f32[2,2048]{1,0:T(2,128)S(1)}, u32[]{:S(2)}, u32[]{:S(2)}) collective-permute-start(f32[2,2048]{1,0:T(2,128)S(1)} %add.66), channel_id=1, source_target_pairs={{0,2},{1,3},{2,0},{3,1},{4,6},{5,7},{6,4},{7,5},{8,10},{9,11},{10,... | collective-permute-start | bytes 49160 | tf_op jit(solution)/shard_map/ppermute | solution.py:43
  67.7 2.0 %collective-permute-done.28 = f32[2,2048]{1,0:T(2,128)S(1)} collective-permute-done((f32[2,2048]{1,0:T(2,128)S(1)}, f32[2,2048]{1,0:T(2,128)S(1)}, u32[]{:S(2)}, u32[]{:S(2)}) %collective-permute-start.28) | collective-permute-done | bytes 16416 | tf_op jit(solution)/shard_map/ppermute | solution.py:43
  69.8 0.6 add_add_fusion
  (43 shorter events, 0.2 us)
Async XLA Ops:
  0.0 5.4 %collective-permute-start.1 = (bf16[2048,128]{1,0:T(8,128)(2,1)}, bf16[2048,128]{1,0:T(8,128)(2,1)S(1)}, u32[]{:S(2)}, u32[]{:S(2)}) collective-permute-start(bf16[2048,128]{1,0:T(8,128)(2,1)} %bitcast.23), channel_id=1, source_target_pairs={{0,4},{4,0},{8,12},{12,8},{16,20},{20,16},{24,28},{28,24},{1,5},{5... | collective-permute-start | bytes 1572872 | tf_op jit(solution)/shard_map/ppermute | solution.py:43
  0.5 5.0 %collective-permute-start.2 = (bf16[2048,128]{1,0:T(8,128)(2,1)}, bf16[2048,128]{1,0:T(8,128)(2,1)S(1)}, u32[]{:S(2)}, u32[]{:S(2)}) collective-permute-start(bf16[2048,128]{1,0:T(8,128)(2,1)} %bitcast.27), channel_id=1, source_target_pairs={{0,4},{4,0},{8,12},{12,8},{16,20},{20,16},{24,28},{28,24},{1,5},{5... | collective-permute-start | bytes 1572872 | tf_op jit(solution)/shard_map/ppermute | solution.py:43
  0.5 11.2 %collective-permute-start.8 = (bf16[2048,128]{1,0:T(8,128)(2,1)}, bf16[2048,128]{1,0:T(8,128)(2,1)S(1)}, u32[]{:S(2)}, u32[]{:S(2)}) collective-permute-start(bf16[2048,128]{1,0:T(8,128)(2,1)} %bitcast.24), channel_id=1, source_target_pairs={{0,8},{4,20},{8,0},{12,28},{16,24},{20,4},{24,16},{28,12},{1,9},{5... | collective-permute-start | bytes 1572872 | tf_op jit(solution)/shard_map/ppermute | solution.py:64
  3.5 0.7 %copy-start.5 = (f32[2,2048]{1,0:T(2,128)S(1)}, f32[2,2048]{1,0:T(2,128)}, u32[]{:S(2)}) copy-start(f32[2,2048]{1,0:T(2,128)} %tokens_ref.3) | copy-start | bytes 49156
  4.3 1.1 %collective-permute-start = (f32[2,128]{1,0:T(2,128)S(1)}, f32[2,128]{1,0:T(2,128)S(1)}, u32[]{:S(2)}, u32[]{:S(2)}) collective-permute-start(f32[2,128]{1,0:T(2,128)S(1)} %get-tuple-element.31), channel_id=1, source_target_pairs={{0,4},{4,0},{8,12},{12,8},{16,20},{20,16},{24,28},{28,24},{1,5},{5... | collective-permute-start | bytes 3080 | tf_op jit(solution)/shard_map/ppermute | solution.py:43
  5.4 5.6 %collective-permute-start.3 = (f32[2,128]{1,0:T(2,128)S(1)}, f32[2,128]{1,0:T(2,128)S(1)}, u32[]{:S(2)}, u32[]{:S(2)}) collective-permute-start(f32[2,128]{1,0:T(2,128)S(1)} %add.53), channel_id=1, source_target_pairs={{0,16},{4,12},{8,24},{12,4},{16,0},{20,28},{24,8},{28,20},{1,17},{... | collective-permute-start | bytes 3080 | tf_op jit(solution)/shard_map/ppermute | solution.py:64
  7.0 0.8 %copy-start.4 = (f32[1,16384]{1,0:T(1,128)S(1)}, f32[1,16384]{1,0:T(1,128)}, u32[]{:S(2)}) copy-start(f32[1,16384]{1,0:T(1,128)} %param.11) | copy-start | bytes 196612
  7.8 4.6 %copy-start.3 = (bf16[1,2048,128]{2,1,0:T(8,128)(2,1)S(1)}, bf16[1,2048,128]{2,1,0:T(8,128)(2,1)}, u32[]{:S(2)}) copy-start(bf16[1,2048,128]{2,1,0:T(8,128)(2,1)} %param.14) | copy-start | bytes 1572868
  11.0 1.2 %collective-permute-start.4 = (f32[2,128]{1,0:T(2,128)S(1)}, f32[2,128]{1,0:T(2,128)S(1)}, u32[]{:S(2)}, u32[]{:S(2)}) collective-permute-start(f32[2,128]{1,0:T(2,128)S(1)} %collective-permute-done.3), channel_id=1, source_target_pairs={{0,4},{4,0},{8,12},{12,8},{16,20},{20,16},{24,28},{28,24},{1,5},{5... | collective-permute-start | bytes 3080 | tf_op jit(solution)/shard_map/ppermute | solution.py:43
  11.1 9.3 %collective-permute-start.7 = (bf16[2048,128]{1,0:T(8,128)(2,1)S(1)}, bf16[2048,128]{1,0:T(8,128)(2,1)S(1)}, u32[]{:S(2)}, u32[]{:S(2)}) collective-permute-start(bf16[2048,128]{1,0:T(8,128)(2,1)S(1)} %collective-permute-done.1.refs_6_), channel_id=1, source_target_pairs={{0,8},{4,20},{8,0},{12,28},{16,24},{20,4},{24,16},{28,12},{1,9},{5... | collective-permute-start | bytes 1572872 | tf_op jit(solution)/shard_map/ppermute | solution.py:64
  12.3 8.1 %collective-permute-start.9 = (bf16[2048,128]{1,0:T(8,128)(2,1)S(1)}, bf16[2048,128]{1,0:T(8,128)(2,1)S(1)}, u32[]{:S(2)}, u32[]{:S(2)}) collective-permute-start(bf16[2048,128]{1,0:T(8,128)(2,1)S(1)} %collective-permute-done.8.refs_5_), channel_id=1, source_target_pairs={{0,4},{4,0},{8,12},{12,8},{16,20},{20,16},{24,28},{28,24},{1,5},{5... | collective-permute-start | bytes 1572872 | tf_op jit(solution)/shard_map/ppermute | solution.py:43
  12.4 13.7 %collective-permute-start.5 = (bf16[2048,128]{1,0:T(8,128)(2,1)S(1)}, bf16[2048,128]{1,0:T(8,128)(2,1)S(1)}, u32[]{:S(2)}, u32[]{:S(2)}) collective-permute-start(bf16[2048,128]{1,0:T(8,128)(2,1)S(1)} %bitcast.28), channel_id=1, source_target_pairs={{0,8},{4,20},{8,0},{12,28},{16,24},{20,4},{24,16},{28,12},{1,9},{5... | collective-permute-start | bytes 1572872 | tf_op jit(solution)/shard_map/ppermute | solution.py:64
  13.3 5.4 %collective-permute-start.6 = (f32[2,128]{1,0:T(2,128)S(1)}, f32[2,128]{1,0:T(2,128)S(1)}, u32[]{:S(2)}, u32[]{:S(2)}) collective-permute-start(f32[2,128]{1,0:T(2,128)S(1)} %collective-permute-done.4), channel_id=1, source_target_pairs={{0,16},{4,12},{8,24},{12,4},{16,0},{20,28},{24,8},{28,20},{1,17},{... | collective-permute-start | bytes 3080 | tf_op jit(solution)/shard_map/ppermute | solution.py:64
  14.5 5.9 %copy-start = (bf16[1,2048,1024]{2,1,0:T(8,128)(2,1)S(1)}, bf16[1,2048,1024]{2,1,0:T(8,128)(2,1)}, u32[]{:S(2)}) copy-start(bf16[1,2048,1024]{2,1,0:T(8,128)(2,1)} %param.12) | copy-start | bytes 12582916
  14.5 5.9 %copy-start.2 = (bf16[1,2048,128]{2,1,0:T(8,128)(2,1)S(1)}, bf16[1,2048,128]{2,1,0:T(8,128)(2,1)}, u32[]{:S(2)}) copy-start(bf16[1,2048,128]{2,1,0:T(8,128)(2,1)} %param.13) | copy-start | bytes 1572868
  20.4 2.6 %copy-start.8 = (s32[2]{0:T(128)S(1)}, s32[2]{0:T(128)}, u32[]{:S(2)}) copy-start(s32[2]{0:T(128)} %param.17) | copy-start | bytes 28
  21.2 1.2 %collective-permute-start.10 = (f32[2,10,128]{2,1,0:T(8,128)S(1)}, f32[2,10,128]{2,1,0:T(8,128)S(1)}, u32[]{:S(2)}, u32[]{:S(2)}) collective-permute-start(f32[2,10,128]{2,1,0:T(8,128)S(1)} %query_products.1), channel_id=1, source_target_pairs={{0,4},{4,0},{8,12},{12,8},{16,20},{20,16},{24,28},{28,24},{1,5},{5... | collective-permute-start | bytes 30728 | tf_op jit(solution)/shard_map/ppermute | solution.py:43
  22.5 3.7 %collective-permute-start.11 = (f32[2,10,128]{2,1,0:T(8,128)S(1)}, f32[2,10,128]{2,1,0:T(8,128)S(1)}, u32[]{:S(2)}, u32[]{:S(2)}) collective-permute-start(f32[2,10,128]{2,1,0:T(8,128)S(1)} %add.57), channel_id=1, source_target_pairs={{0,16},{4,12},{8,24},{12,4},{16,0},{20,28},{24,8},{28,20},{1,17},{... | collective-permute-start | bytes 30728 | tf_op jit(solution)/shard_map/ppermute | solution.py:64
  23.1 6.0 %collective-permute-start.16 = (bf16[2048,128]{1,0:T(8,128)(2,1)S(1)}, bf16[2048,128]{1,0:T(8,128)(2,1)S(1)}, u32[]{:S(2)}, u32[]{:S(2)}) collective-permute-start(bf16[2048,128]{1,0:T(8,128)(2,1)S(1)} %collective-permute-done.7.refs_6_), channel_id=1, source_target_pairs={{0,4},{4,0},{8,12},{12,8},{16,20},{20,16},{24,28},{28,24},{1,5},{5... | collective-permute-start | bytes 1572872 | tf_op jit(solution)/shard_map/ppermute | solution.py:43
  23.1 9.4 %collective-permute-start.14 = (bf16[2048,128]{1,0:T(8,128)(2,1)S(1)}, bf16[2048,128]{1,0:T(8,128)(2,1)S(1)}, u32[]{:S(2)}, u32[]{:S(2)}) collective-permute-start(bf16[2048,128]{1,0:T(8,128)(2,1)S(1)} %collective-permute-done.9.refs_7_), channel_id=1, source_target_pairs={{0,8},{4,20},{8,0},{12,28},{16,24},{20,4},{24,16},{28,12},{1,9},{5... | collective-permute-start | bytes 1572872 | tf_op jit(solution)/shard_map/ppermute | solution.py:64
  24.6 13.6 %collective-permute-start.21 = (bf16[2048,128]{1,0:T(8,128)(2,1)S(1)}, bf16[2048,128]{1,0:T(8,128)(2,1)S(1)}, u32[]{:S(2)}, u32[]{:S(2)}) collective-permute-start(bf16[2048,128]{1,0:T(8,128)(2,1)S(1)} %collective-permute-done.2.refs_6_), channel_id=1, source_target_pairs={{0,8},{4,20},{8,0},{12,28},{16,24},{20,4},{24,16},{28,12},{1,9},{5... | collective-permute-start | bytes 1572872 | tf_op jit(solution)/shard_map/ppermute | solution.py:64
  26.2 12.0 %collective-permute-start.12 = (bf16[2048,128]{1,0:T(8,128)(2,1)S(1)}, bf16[2048,128]{1,0:T(8,128)(2,1)S(1)}, u32[]{:S(2)}, u32[]{:S(2)}) collective-permute-start(bf16[2048,128]{1,0:T(8,128)(2,1)S(1)} %collective-permute-done.5.refs_5_), channel_id=1, source_target_pairs={{0,4},{4,0},{8,12},{12,8},{16,20},{20,16},{24,28},{28,24},{1,5},{5... | collective-permute-start | bytes 1572872 | tf_op jit(solution)/shard_map/ppermute | solution.py:43
  26.9 1.5 %collective-permute-start.17 = (f32[2,10,128]{2,1,0:T(8,128)S(1)}, f32[2,10,128]{2,1,0:T(8,128)S(1)}, u32[]{:S(2)}, u32[]{:S(2)}) collective-permute-start(f32[2,10,128]{2,1,0:T(8,128)S(1)} %collective-permute-done.11), channel_id=1, source_target_pairs={{0,4},{4,0},{8,12},{12,8},{16,20},{20,16},{24,28},{28,24},{1,5},{5... | collective-permute-start | bytes 30728 | tf_op jit(solution)/shard_map/ppermute | solution.py:43
  28.4 11.1 %collective-permute-start.18 = (f32[2,10,128]{2,1,0:T(8,128)S(1)}, f32[2,10,128]{2,1,0:T(8,128)S(1)}, u32[]{:S(2)}, u32[]{:S(2)}) collective-permute-start(f32[2,10,128]{2,1,0:T(8,128)S(1)} %collective-permute-done.17), channel_id=1, source_target_pairs={{0,16},{4,12},{8,24},{12,4},{16,0},{20,28},{24,8},{28,20},{1,17},{... | collective-permute-start | bytes 30728 | tf_op jit(solution)/shard_map/ppermute | solution.py:64
  32.6 7.0 %collective-permute-start.15 = (bf16[2048,128]{1,0:T(8,128)(2,1)S(1)}, bf16[2048,128]{1,0:T(8,128)(2,1)S(1)}, u32[]{:S(2)}, u32[]{:S(2)}) collective-permute-start(bf16[2048,128]{1,0:T(8,128)(2,1)S(1)} %collective-permute-done.14.refs_5_), channel_id=1, source_target_pairs={{0,4},{4,0},{8,12},{12,8},{16,20},{20,16},{24,28},{28,24},{1,5},{5... | collective-permute-start | bytes 1572872 | tf_op jit(solution)/shard_map/ppermute | solution.py:43
  38.2 9.3 %collective-permute-start.22 = (bf16[2048,128]{1,0:T(8,128)(2,1)S(1)}, bf16[2048,128]{1,0:T(8,128)(2,1)S(1)}, u32[]{:S(2)}, u32[]{:S(2)}) collective-permute-start(bf16[2048,128]{1,0:T(8,128)(2,1)S(1)} %collective-permute-done.21.refs_6_), channel_id=1, source_target_pairs={{0,4},{4,0},{8,12},{12,8},{16,20},{20,16},{24,28},{28,24},{1,5},{5... | collective-permute-start | bytes 1572872 | tf_op jit(solution)/shard_map/ppermute | solution.py:43
  38.2 10.8 %collective-permute-start.13 = (bf16[2048,128]{1,0:T(8,128)(2,1)S(1)}, bf16[2048,128]{1,0:T(8,128)(2,1)S(1)}, u32[]{:S(2)}, u32[]{:S(2)}) collective-permute-start(bf16[2048,128]{1,0:T(8,128)(2,1)S(1)} %collective-permute-done.12.refs_7_), channel_id=1, source_target_pairs={{0,8},{4,20},{8,0},{12,28},{16,24},{20,4},{24,16},{28,12},{1,9},{5... | collective-permute-start | bytes 1572872 | tf_op jit(solution)/shard_map/ppermute | solution.py:64
  39.6 0.9 %copy-start.7 = (s32[2]{0:T(128)S(1)}, s32[2]{0:T(128)}, u32[]{:S(2)}) copy-start(s32[2]{0:T(128)} %lengths_ref.3) | copy-start | bytes 28
  41.5 1.2 %collective-permute-start.19 = (f32[8,128]{1,0:T(8,128)S(1)}, f32[8,128]{1,0:T(8,128)S(1)}, u32[]{:S(2)}, u32[]{:S(2)}) collective-permute-start(f32[8,128]{1,0:T(8,128)S(1)} %get-tuple-element.49), channel_id=1, source_target_pairs={{0,4},{4,0},{8,12},{12,8},{16,20},{20,16},{24,28},{28,24},{1,5},{5... | collective-permute-start | bytes 12296 | tf_op jit(solution)/shard_map/ppermute | solution.py:43
  42.7 4.8 %collective-permute-start.20 = (f32[8,128]{1,0:T(8,128)S(1)}, f32[8,128]{1,0:T(8,128)S(1)}, u32[]{:S(2)}, u32[]{:S(2)}) collective-permute-start(f32[8,128]{1,0:T(8,128)S(1)} %max.6), channel_id=1, source_target_pairs={{0,8},{4,12},{8,0},{12,4},{16,24},{20,28},{24,16},{28,20},{1,9},{5... | collective-permute-start | bytes 12296 | tf_op jit(solution)/shard_map/ppermute | solution.py:43
  49.0 2.0 %collective-permute-start.23 = (bf16[2048,128]{1,0:T(8,128)(2,1)S(1)}, bf16[2048,128]{1,0:T(8,128)(2,1)S(1)}, u32[]{:S(2)}, u32[]{:S(2)}) collective-permute-start(bf16[2048,128]{1,0:T(8,128)(2,1)S(1)} %collective-permute-done.13.refs_5_), channel_id=1, source_target_pairs={{0,4},{4,0},{8,12},{12,8},{16,20},{20,16},{24,28},{28,24},{1,5},{5... | collective-permute-start | bytes 1572872 | tf_op jit(solution)/shard_map/ppermute | solution.py:43
  51.0 9.7 %copy-start.1 = (bf16[1,1024,2048]{2,1,0:T(8,128)(2,1)S(1)}, bf16[1,1024,2048]{2,1,0:T(8,128)(2,1)}, u32[]{:S(2)}) copy-start(bf16[1,1024,2048]{2,1,0:T(8,128)(2,1)} %param.15) | copy-start | bytes 12582916
  52.2 1.2 %collective-permute-start.24 = (f32[8,256]{1,0:T(8,128)S(1)}, f32[8,256]{1,0:T(8,128)S(1)}, u32[]{:S(2)}, u32[]{:S(2)}) collective-permute-start(f32[8,256]{1,0:T(8,128)S(1)} %weighted_values.1), channel_id=1, source_target_pairs={{0,4},{4,0},{8,12},{12,8},{16,20},{20,16},{24,28},{28,24},{1,5},{5... | collective-permute-start | bytes 24584 | tf_op jit(solution)/shard_map/ppermute | solution.py:43
  53.3 3.7 %collective-permute-start.25 = (f32[8,256]{1,0:T(8,128)S(1)}, f32[8,256]{1,0:T(8,128)S(1)}, u32[]{:S(2)}, u32[]{:S(2)}) collective-permute-start(f32[8,256]{1,0:T(8,128)S(1)} %add.64), channel_id=1, source_target_pairs={{0,8},{4,12},{8,0},{12,4},{16,24},{20,28},{24,16},{28,20},{1,9},{5... | collective-permute-start | bytes 24584 | tf_op jit(solution)/shard_map/ppermute | solution.py:43
  57.0 3.7 %collective-permute-start.26 = (f32[8,256]{1,0:T(8,128)S(1)}, f32[8,256]{1,0:T(8,128)S(1)}, u32[]{:S(2)}, u32[]{:S(2)}) collective-permute-start(f32[8,256]{1,0:T(8,128)S(1)} %add.65.mine_ref), channel_id=1, source_target_pairs={{0,16},{4,20},{8,24},{12,28},{16,0},{20,4},{24,8},{28,12},{1,17},{... | collective-permute-start | bytes 24584 | tf_op jit(solution)/shard_map/ppermute | solution.py:43
  60.7 9.1 %copy-start.6 = (f32[2,2048]{1,0:T(2,128)S(1)}, f32[2,2048]{1,0:T(2,128)}, u32[]{:S(2)}) copy-start(f32[2,2048]{1,0:T(2,128)} %tokens_ref.3) | copy-start | bytes 49156
  61.3 3.8 %collective-permute-start.27 = (f32[2,2048]{1,0:T(2,128)S(1)}, f32[2,2048]{1,0:T(2,128)S(1)}, u32[]{:S(2)}, u32[]{:S(2)}) collective-permute-start(f32[2,2048]{1,0:T(2,128)S(1)} %output_products.1), channel_id=1, source_target_pairs={{0,1},{1,0},{2,3},{3,2},{4,5},{5,4},{6,7},{7,6},{8,9},{9,8},{10,11... | collective-permute-start | bytes 49160 | tf_op jit(solution)/shard_map/ppermute | solution.py:43
  65.1 4.7 %collective-permute-start.28 = (f32[2,2048]{1,0:T(2,128)S(1)}, f32[2,2048]{1,0:T(2,128)S(1)}, u32[]{:S(2)}, u32[]{:S(2)}) collective-permute-start(f32[2,2048]{1,0:T(2,128)S(1)} %add.66), channel_id=1, source_target_pairs={{0,2},{1,3},{2,0},{3,1},{4,6},{5,7},{6,4},{7,5},{8,10},{9,11},{10,... | collective-permute-start | bytes 49160 | tf_op jit(solution)/shard_map/ppermute | solution.py:43

commit v10 on v9

--- a/solution.py
+++ b/solution.py
@@ -359,9 +359,11 @@
     if split:
         squares, told, _ = sum_chips(squares, row_count // NORM_ROWS // 2)
         key_shared = share(key_far, told)
+        own_values = after(value_weight[0], key_far[0][1])
         squares = after(squares, key_far[1][1], key_shared[0][1])
     else:
         key_shared = share(key_far)
+        own_values = value_weight[0]
         squares = beside(squares, squares, row_count // NORM_ROWS)
         squares = butterfly(squares, "ctx", chip_bits, jnp.add)
     key_last = send_last(key_weight[0], key_shared)
@@ -374,7 +376,7 @@
     )(places, squares, new_tokens, gains, query_weight[0], key_weight[0], value_weight[0])
     parts = parts + swap(parts, "ctx", 1)
     parts_sent = parts
-    value_far = send_first(value_weight[0], after(value_partner, parts))
+    value_far = send_first(own_values, after(value_partner, parts))
     if split:
         parts, _, parts_sent = sum_chips(parts)
         summed = jnp.where(own_request == 0, parts[0], parts[1])
@@ -398,18 +400,27 @@
         [IN_SMEM] * 2 + [IN_VMEM] * 6,
         (shape((heads, row_count)), shape((heads, LANES)), shape((heads, LANES))),
     )(places, lengths, key_total, cosine, sine_part, new_cosine, new_sine, summed)
+    value_mid = value_far[:1] + share(value_far[:1], parts_sent)
+    value_next = send_last(own_values, value_mid[1:])
     top = butterfly(top, "ctx", [1], jnp.maximum)
+    top = after(top, *[block for _, block in value_next])
     near_top = top
-    top = butterfly(top, "ctx", bits_below(team)[1:], jnp.maximum)
-
-    value_shared = share(value_far[:1], parts_sent)
-    value_last = send_last(value_weight[0], value_shared)
-    value_shared += share(value_far[1:], key_mid, *[block for _, block in value_shared])
+    if split:
+        received = jnp.maximum(top, after(by_core(top, 4, 2), value_far[1][1]))
+        top = jnp.where(core == 0, swap(received, "ctx", 1), received)
+    else:
+        top = butterfly(top, "ctx", bits_below(team)[1:], jnp.maximum)
+        received = top
+
+    value_mid += value_next + share(value_next, near_top)
     value_total = project(after(places, near_top), rows, value_near)
-    value_total = project(after(places, top), rows, value_far + value_shared, value_total)
-
-    blocks = share(value_last, value_total)
-    value_total = project(places, rows, value_last, value_total)
+    value_total = project(places, rows, value_mid, value_total)
+
+    blocks = share(value_far[1:], received)
+    if blocks:
+        value_total = project(places, rows, value_far[1:], value_total)
+    else:
+        blocks = value_far[1:]
     packed = call(
         functools.partial(weigh_kernel, [d for d, _ in blocks], len(rows), team),
         "weighted_values",

time: 70.6 us -> 70.5 us (level)
  waiting for transfers between devices: 28.2 us -> 27.2 us
  starting transfers between devices: 21.5 us -> 22.3 us
    ppermute x19, waiting for transfers between devices: 18 us -> 14.4 us  [swap(): return lax.ppermute(value, axis, [(i, i ^ distance) for i in range(count)])]
    ppermute x10 -> x11, waiting for transfers between devices: 10.2 us -> 12.8 us  [by_core(): return lax.ppermute(value, 'ctx', pairs)]
    ppermute x10 -> x11, starting transfers between devices: 11.7 us -> 13.1 us  [by_core(): return lax.ppermute(value, 'ctx', pairs)]
  transfers between devices with their start and end apart: 29 -> 30, of which waited for: 15 -> 16; matrix products, arithmetic and copies ran while one was open for 1% -> 1% of each run, Pallas kernels for 22% -> 22%
where the time goes in v10:
time: 70.5 us; the launch traced here: 70.2 us
  waiting for transfers between devices  27.2 us (39%)
  starting transfers between devices  22.3 us (32%)
  Pallas kernels  17.4 us (25%)
  local copies, waits for them, and re-layouts  1.59 us (2%)
  other arithmetic  1.49 us (2%)
    ppermute x19, waiting for transfers between devices, swap(): return lax.ppermute(value, axis, [(i, i ^ distance) for i in range(count)])  14.4 us
    ppermute x11, starting transfers between devices, by_core(): return lax.ppermute(value, 'ctx', pairs)  13.1 us
    ppermute x11, waiting for transfers between devices, by_core(): return lax.ppermute(value, 'ctx', pairs)  12.8 us
    ppermute x19, starting transfers between devices, swap(): return lax.ppermute(value, axis, [(i, i ^ distance) for i in range(count)])  9.21 us
    pallas_call x2, Pallas kernels, normalise(): call(functools.partial(norm_kernel, first), 'normalise', [IN_HBM, IN_VMEM...  7.47 us
    pallas_call x6, Pallas kernels, project(): call(functools.partial(project_kernel, [d for d, _ in blocks], len(rows),...  6.18 us
    unnamed x18, local copies, waits for them, and re-layouts  1.59 us
  transfers between devices with their start and end apart: 30, of which 16 were waited for; matrix products, arithmetic and copies ran while one was open for 1% of the time, Pallas kernels for 22%

profile of v10, /device:TPU:0, one launch (start us, length us, event | category | flops | bytes accessed | tf_op | source)
XLA Modules:
  0.0 70.2 jit_solution(12185006052233375108)
XLA Ops:
  0.0 0.5 collective-permute-start.1
  0.5 0.1 collective-permute-start.2
  0.5 2.9 %collective-permute-start.7 = (bf16[2048,128]{1,0:T(8,128)(2,1)}, bf16[2048,128]{1,0:T(8,128)(2,1)S(1)}, u32[]{:S(2)}, u32[]{:S(2)}) collective-permute-start(bf16[2048,128]{1,0:T(8,128)(2,1)} %bitcast.24), channel_id=1, source_target_pairs={{0,8},{4,20},{8,0},{12,28},{16,24},{20,4},{24,16},{28,12},{1,9},{5... | collective-permute-start | bytes 1572872 | tf_op jit(solution)/shard_map/ppermute | solution.py:64
  3.5 0.7 %copy-done.5 = f32[2,2048]{1,0:T(2,128)S(1)} copy-done((f32[2,2048]{1,0:T(2,128)S(1)}, f32[2,2048]{1,0:T(2,128)}, u32[]{:S(2)}) %copy-start.5) | copy-done | bytes 16408
  4.2 0.1 squares.1
  4.3 1.1 %collective-permute-done = f32[2,128]{1,0:T(2,128)S(1)} collective-permute-done((f32[2,128]{1,0:T(2,128)S(1)}, f32[2,128]{1,0:T(2,128)S(1)}, u32[]{:S(2)}, u32[]{:S(2)}) %collective-permute-start) | collective-permute-done | bytes 1056 | tf_op jit(solution)/shard_map/ppermute | solution.py:43
  5.4 1.6 %collective-permute-start.3 = (f32[2,128]{1,0:T(2,128)S(1)}, f32[2,128]{1,0:T(2,128)S(1)}, u32[]{:S(2)}, u32[]{:S(2)}) collective-permute-start(f32[2,128]{1,0:T(2,128)S(1)} %add.53), channel_id=1, source_target_pairs={{0,16},{4,12},{8,24},{12,4},{16,0},{20,28},{24,8},{28,20},{1,17},{... | collective-permute-start | bytes 3080 | tf_op jit(solution)/shard_map/ppermute | solution.py:64
  7.0 0.8 %copy-done.4 = f32[1,16384]{1,0:T(1,128)S(1)} copy-done((f32[1,16384]{1,0:T(1,128)S(1)}, f32[1,16384]{1,0:T(1,128)}, u32[]{:S(2)}) %copy-start.4) | copy-done | bytes 65560
  7.8 3.2 %normalise.2 = (bf16[8,64,2048]{2,1,0:T(8,128)(2,1)S(1)}, bf16[8,64,2048]{2,1,0:T(8,128)(2,1)S(1)}) custom-call(bf16[320,16384]{1,0:T(8,128)(2,1)} %bitcast.35, f32[8,1,2048]{2,1,0:T(1,128)S(1)} %bitcast.31), custom_call_target="tpu_custom_call" | custom-call | flops 1000 | bytes 1000 | tf_op jit(solution)/shard_map/normalise/pallas_call | solution.py:173
  11.0 0.1 collective-permute-start.4
  11.1 0.6 collective-permute-start.6
  11.7 0.5 collective-permute-done.4
  12.3 0.2 collective-permute-start.8
  12.4 0.9 %collective-permute-start.18 = (bf16[2048,128]{1,0:T(8,128)(2,1)S(1)}, bf16[2048,128]{1,0:T(8,128)(2,1)S(1)}, u32[]{:S(2)}, u32[]{:S(2)}) collective-permute-start(bf16[2048,128]{1,0:T(8,128)(2,1)S(1)} %bitcast.28), channel_id=1, source_target_pairs={{0,8},{4,20},{8,0},{12,28},{16,24},{20,4},{24,16},{28,12},{1,9},{5... | collective-permute-start | bytes 1572872 | tf_op jit(solution)/shard_map/ppermute | solution.py:64
  13.3 1.1 %collective-permute-start.5 = (f32[2,128]{1,0:T(2,128)S(1)}, f32[2,128]{1,0:T(2,128)S(1)}, u32[]{:S(2)}, u32[]{:S(2)}) collective-permute-start(f32[2,128]{1,0:T(2,128)S(1)} %collective-permute-done.4), channel_id=1, source_target_pairs={{0,16},{4,12},{8,24},{12,4},{16,0},{20,28},{24,8},{28,20},{1,17},{... | collective-permute-start | bytes 3080 | tf_op jit(solution)/shard_map/ppermute | solution.py:64
  14.5 4.3 %normalise.3 = (bf16[8,64,2048]{2,1,0:T(8,128)(2,1)S(1)}, bf16[8,64,2048]{2,1,0:T(8,128)(2,1)S(1)}, bf16[8,64,2048]{2,1,0:T(8,128)(2,1)S(1)}) custom-call(bf16[320,16384]{1,0:T(8,128)(2,1)} %bitcast.36, f32[8,1,2048]{2,1,0:T(1,128)S(1)} %bitcast.32), custom_call_target="tpu_custom_call" | custom-call | flops 1000 | bytes 1000 | tf_op jit(solution)/shard_map/normalise/pallas_call | solution.py:173
  18.8 1.6 %collective-permute-done.6.refs_6_ = bf16[2048,128]{1,0:T(8,128)(2,1)S(1)} collective-permute-done((bf16[2048,128]{1,0:T(8,128)(2,1)S(1)}, bf16[2048,128]{1,0:T(8,128)(2,1)S(1)}, u32[]{:S(2)}, u32[]{:S(2)}) %collective-permute-start.6) | collective-permute-done | bytes 524320 | tf_op jit(solution)/shard_map/ppermute | solution.py:64
  20.4 0.0 collective-permute-done.8.refs_7_
  20.4 0.0 copy-start.8
  20.4 0.8 %query_products.1 = f32[2,10,128]{2,1,0:T(8,128)S(1)} custom-call(s32[1]{0:T(128)} %bitcast.place_ref, f32[2,128]{1,0:T(2,128)S(1)} %add_add_fusion.2.squares_ref, f32[2,2048]{1,0:T(2,128)S(1)} %copy-done.5, f32[8,1,2048]{2,1,0:T(1,128)S(1)} %bitcast.33, bf16[2048,1024]{1,0:T(8,128)(2,1)S(1)} %bitcast.21, bf16[2048,128]{1,0:T(8,128)(2,1)S(1)} %bitcast.25, ...), custom_call_target="tpu_custom_call" | custom-call | flops 1000 | bytes 1000 | tf_op jit(solution)/shard_map/query_products/pallas_call | solution.py:371
  21.2 0.1 collective-permute-start.9
  21.3 1.2 %collective-permute-done.9 = f32[2,10,128]{2,1,0:T(8,128)S(1)} collective-permute-done((f32[2,10,128]{2,1,0:T(8,128)S(1)}, f32[2,10,128]{2,1,0:T(8,128)S(1)}, u32[]{:S(2)}, u32[]{:S(2)}) %collective-permute-start.9) | collective-permute-done | bytes 10272 | tf_op jit(solution)/shard_map/ppermute | solution.py:43
  22.5 0.5 collective-permute-start.14
  23.1 1.4 %collective-permute-start.11 = (bf16[2048,128]{1,0:T(8,128)(2,1)S(1)}, bf16[2048,128]{1,0:T(8,128)(2,1)S(1)}, u32[]{:S(2)}, u32[]{:S(2)}) collective-permute-start(bf16[2048,128]{1,0:T(8,128)(2,1)S(1)} %collective-permute-done.8.refs_7_), channel_id=1, source_target_pairs={{0,8},{4,20},{8,0},{12,28},{16,24},{20,4},{24,16},{28,12},{1,9},{5... | collective-permute-start | bytes 1572872 | tf_op jit(solution)/shard_map/ppermute | solution.py:64
  24.5 1.7 %collective-permute-done.18.refs_5_ = bf16[2048,128]{1,0:T(8,128)(2,1)S(1)} collective-permute-done((bf16[2048,128]{1,0:T(8,128)(2,1)S(1)}, bf16[2048,128]{1,0:T(8,128)(2,1)S(1)}, u32[]{:S(2)}, u32[]{:S(2)}) %collective-permute-start.18) | collective-permute-done | bytes 524320 | tf_op jit(solution)/shard_map/ppermute | solution.py:64
  26.2 0.1 collective-permute-done.14
  26.3 0.0 collective-permute-start.19
  26.3 0.6 multiply_sine_fusion
  27.0 0.6 collective-permute-start.15
  27.6 0.1 multiply_sine_fusion.1
  27.7 0.1 collective-permute-start.13
  27.7 0.7 collective-permute-done.15
  28.4 0.4 collective-permute-start.16
  28.8 3.7 %collective-permute-done.11.refs_5_ = bf16[2048,128]{1,0:T(8,128)(2,1)S(1)} collective-permute-done((bf16[2048,128]{1,0:T(8,128)(2,1)S(1)}, bf16[2048,128]{1,0:T(8,128)(2,1)S(1)}, u32[]{:S(2)}, u32[]{:S(2)}) %collective-permute-start.11) | collective-permute-done | bytes 524320 | tf_op jit(solution)/shard_map/ppermute | solution.py:64
  32.5 1.4 %collective-permute-start.20 = (bf16[2048,128]{1,0:T(8,128)(2,1)S(1)}, bf16[2048,128]{1,0:T(8,128)(2,1)S(1)}, u32[]{:S(2)}, u32[]{:S(2)}) collective-permute-start(bf16[2048,128]{1,0:T(8,128)(2,1)S(1)} %collective-permute-done.19.refs_6_), channel_id=1, source_target_pairs={{0,8},{4,20},{8,0},{12,28},{16,24},{20,4},{24,16},{28,12},{1,9},{5... | collective-permute-start | bytes 1572872 | tf_op jit(solution)/shard_map/ppermute | solution.py:64
  33.8 0.9 %project.6.refs_9_ = f32[320,128]{1,0:T(8,128)S(1)} custom-call(s32[1]{0:T(128)} %bitcast.place_ref, bf16[8,64,2048]{2,1,0:T(8,128)(2,1)S(1)} %get-tuple-element.36.refs_0_, bf16[8,64,2048]{2,1,0:T(8,128)(2,1)S(1)} %get-tuple-element.37.refs_1_, bf16[8,64,2048]{2,1,0:T(8,128)(2,1)S(1)} %get-tuple-element.40.refs_2_, ...), custom_call_target="tpu_custom_call" | custom-call | flops 1000 | bytes 1000 | tf_op jit(solution)/shard_map/project/pallas_call | solution.py:218
  34.7 0.7 %collective-permute-start.10 = (bf16[2048,128]{1,0:T(8,128)(2,1)S(1)}, bf16[2048,128]{1,0:T(8,128)(2,1)S(1)}, u32[]{:S(2)}, u32[]{:S(2)}) collective-permute-start(bf16[2048,128]{1,0:T(8,128)(2,1)S(1)} %collective-permute-done.2.refs_6_), channel_id=1, source_target_pairs={{0,8},{4,20},{8,0},{12,28},{16,24},{20,4},{24,16},{28,12},{1,9},{5... | collective-permute-start | bytes 1572872 | tf_op jit(solution)/shard_map/ppermute | solution.py:64
  35.4 0.0 collective-permute-done.16
  35.5 1.5 %project.7.refs_7_ = f32[320,128]{1,0:T(8,128)S(1)} custom-call(s32[1]{0:T(128)} %bitcast.place_ref, bf16[8,64,2048]{2,1,0:T(8,128)(2,1)S(1)} %get-tuple-element.36.refs_0_, bf16[8,64,2048]{2,1,0:T(8,128)(2,1)S(1)} %get-tuple-element.37.refs_1_, bf16[8,64,2048]{2,1,0:T(8,128)(2,1)S(1)} %get-tuple-element.40.refs_2_, ...), custom_call_target="tpu_custom_call" | custom-call | flops 1000 | bytes 1000 | tf_op jit(solution)/shard_map/project/pallas_call | solution.py:218
  37.0 0.0 copy-start.7
  37.1 0.9 %project.8.refs_0_ = f32[320,128]{1,0:T(8,128)S(1)} custom-call(s32[1]{0:T(128)} %bitcast.place_ref, bf16[8,64,2048]{2,1,0:T(8,128)(2,1)S(1)} %get-tuple-element.36.refs_0_, bf16[8,64,2048]{2,1,0:T(8,128)(2,1)S(1)} %get-tuple-element.37.refs_1_, bf16[8,64,2048]{2,1,0:T(8,128)(2,1)S(1)} %get-tuple-element.40.refs_2_, ...), custom_call_target="tpu_custom_call" | custom-call | flops 1000 | bytes 1000 | tf_op jit(solution)/shard_map/project/pallas_call | solution.py:218
  37.9 1.0 %scores.1 = (f32[8,320]{1,0:T(8,128)S(1)}, f32[8,128]{1,0:T(8,128)S(1)}, f32[8,128]{1,0:T(8,128)S(1)}) custom-call(s32[1]{0:T(128)} %bitcast.place_ref, s32[2]{0:T(128)S(1)} %copy-done.7, f32[320,128]{1,0:T(8,128)S(1)} %project.8.refs_0_, f32[320,64]{1,0:T(8,128)S(1)} %get-tuple-element.62.refs_1_, f32[320,64]{1,0:T(8,128)S(1)} %get-tuple-element.61.refs_2_, ...), custom_call_target="tpu_custom_call" | custom-call | flops 1000 | bytes 1000 | tf_op jit(solution)/shard_map/scores/pallas_call | solution.py:397
  38.9 1.2 %collective-permute-done.17 = f32[8,128]{1,0:T(8,128)S(1)} collective-permute-done((f32[8,128]{1,0:T(8,128)S(1)}, f32[8,128]{1,0:T(8,128)S(1)}, u32[]{:S(2)}, u32[]{:S(2)}) %collective-permute-start.17) | collective-permute-done | bytes 4128 | tf_op jit(solution)/shard_map/ppermute | solution.py:43
  40.1 1.6 %collective-permute-done.20.refs_7_ = bf16[2048,128]{1,0:T(8,128)(2,1)S(1)} collective-permute-done((bf16[2048,128]{1,0:T(8,128)(2,1)S(1)}, bf16[2048,128]{1,0:T(8,128)(2,1)S(1)}, u32[]{:S(2)}, u32[]{:S(2)}) %collective-permute-start.20) | collective-permute-done | bytes 524320 | tf_op jit(solution)/shard_map/ppermute | solution.py:64
  41.7 1.5 %collective-permute-start.21 = (f32[8,128]{1,0:T(8,128)S(1)}, f32[8,128]{1,0:T(8,128)S(1)}, u32[]{:S(2)}, u32[]{:S(2)}) collective-permute-start(f32[8,128]{1,0:T(8,128)S(1)} %max.6), channel_id=1, source_target_pairs={{0,16},{4,12},{8,24},{12,4},{16,0},{20,28},{24,8},{28,20},{1,17},{... | collective-permute-start | bytes 12296 | tf_op jit(solution)/shard_map/ppermute | solution.py:64
  43.2 4.1 %collective-permute-done.10.refs_5_ = bf16[2048,128]{1,0:T(8,128)(2,1)S(1)} collective-permute-done((bf16[2048,128]{1,0:T(8,128)(2,1)S(1)}, bf16[2048,128]{1,0:T(8,128)(2,1)S(1)}, u32[]{:S(2)}, u32[]{:S(2)}) %collective-permute-start.10) | collective-permute-done | bytes 524320 | tf_op jit(solution)/shard_map/ppermute | solution.py:64
  47.3 0.5 collective-permute-start.24
  47.9 0.9 %project.9.refs_9_ = f32[320,128]{1,0:T(8,128)S(1)} custom-call(s32[1]{0:T(128)} %bitcast.place_ref, bf16[8,64,2048]{2,1,0:T(8,128)(2,1)S(1)} %get-tuple-element.36.refs_0_, bf16[8,64,2048]{2,1,0:T(8,128)(2,1)S(1)} %get-tuple-element.37.refs_1_, bf16[8,64,2048]{2,1,0:T(8,128)(2,1)S(1)} %get-tuple-element.40.refs_2_, ...), custom_call_target="tpu_custom_call" | custom-call | flops 1000 | bytes 1000 | tf_op jit(solution)/shard_map/project/pallas_call | solution.py:218
  48.7 1.6 %project.10.refs_6_ = f32[320,128]{1,0:T(8,128)S(1)} custom-call(s32[1]{0:T(128)} %bitcast.place_ref, bf16[8,64,2048]{2,1,0:T(8,128)(2,1)S(1)} %get-tuple-element.36.refs_0_, bf16[8,64,2048]{2,1,0:T(8,128)(2,1)S(1)} %get-tuple-element.37.refs_1_, bf16[8,64,2048]{2,1,0:T(8,128)(2,1)S(1)} %get-tuple-element.40.refs_2_, ...), custom_call_target="tpu_custom_call" | custom-call | flops 1000 | bytes 1000 | tf_op jit(solution)/shard_map/project/pallas_call | solution.py:218
  50.3 0.5 project.11.refs_6_
  50.8 0.0 copy-start.1
  50.8 1.2 %weighted_values.1 = f32[8,256]{1,0:T(8,128)S(1)} custom-call(s32[1]{0:T(128)} %bitcast.place_ref, s32[2]{0:T(128)S(1)} %copy-done.7, bf16[8,64,2048]{2,1,0:T(8,128)(2,1)S(1)} %get-tuple-element.36.refs_0_, bf16[8,64,2048]{2,1,0:T(8,128)(2,1)S(1)} %get-tuple-element.37.refs_1_, bf16[8,64,2048]{2,1,0:T(8,128)(2,1)S(1)} %get-tuple-element.40.refs_2_, ...), custom_call_target="tpu_custom_call" | custom-call | flops 1000 | bytes 1000 | tf_op jit(solution)/shard_map/weighted_values/pallas_call | solution.py:424
  52.0 0.1 collective-permute-start.25
  52.1 1.1 %collective-permute-done.25 = f32[8,256]{1,0:T(8,128)S(1)} collective-permute-done((f32[8,256]{1,0:T(8,128)S(1)}, f32[8,256]{1,0:T(8,128)S(1)}, u32[]{:S(2)}, u32[]{:S(2)}) %collective-permute-start.25) | collective-permute-done | bytes 8224 | tf_op jit(solution)/shard_map/ppermute | solution.py:43
  53.2 1.4 %collective-permute-start.26 = (f32[8,256]{1,0:T(8,128)S(1)}, f32[8,256]{1,0:T(8,128)S(1)}, u32[]{:S(2)}, u32[]{:S(2)}) collective-permute-start(f32[8,256]{1,0:T(8,128)S(1)} %add.64), channel_id=1, source_target_pairs={{0,8},{4,12},{8,0},{12,4},{16,24},{20,28},{24,16},{28,20},{1,9},{5... | collective-permute-start | bytes 24584 | tf_op jit(solution)/shard_map/ppermute | solution.py:43
  54.5 2.3 %collective-permute-done.26 = f32[8,256]{1,0:T(8,128)S(1)} collective-permute-done((f32[8,256]{1,0:T(8,128)S(1)}, f32[8,256]{1,0:T(8,128)S(1)}, u32[]{:S(2)}, u32[]{:S(2)}) %collective-permute-start.26) | collective-permute-done | bytes 8224 | tf_op jit(solution)/shard_map/ppermute | solution.py:43
  56.8 1.5 %collective-permute-start.27 = (f32[8,256]{1,0:T(8,128)S(1)}, f32[8,256]{1,0:T(8,128)S(1)}, u32[]{:S(2)}, u32[]{:S(2)}) collective-permute-start(f32[8,256]{1,0:T(8,128)S(1)} %add.65.mine_ref), channel_id=1, source_target_pairs={{0,16},{4,20},{8,24},{12,28},{16,0},{20,4},{24,8},{28,12},{1,17},{... | collective-permute-start | bytes 24584 | tf_op jit(solution)/shard_map/ppermute | solution.py:43
  58.4 2.1 %collective-permute-done.27.other_ref = f32[8,256]{1,0:T(8,128)S(1)} collective-permute-done((f32[8,256]{1,0:T(8,128)S(1)}, f32[8,256]{1,0:T(8,128)S(1)}, u32[]{:S(2)}, u32[]{:S(2)}) %collective-permute-start.27) | collective-permute-done | bytes 8224 | tf_op jit(solution)/shard_map/ppermute | solution.py:43
  60.5 0.6 output_products.1
  61.2 1.6 %collective-permute-start.28 = (f32[2,2048]{1,0:T(2,128)S(1)}, f32[2,2048]{1,0:T(2,128)S(1)}, u32[]{:S(2)}, u32[]{:S(2)}) collective-permute-start(f32[2,2048]{1,0:T(2,128)S(1)} %output_products.1), channel_id=1, source_target_pairs={{0,1},{1,0},{2,3},{3,2},{4,5},{5,4},{6,7},{7,6},{8,9},{9,8},{10,11... | collective-permute-start | bytes 49160 | tf_op jit(solution)/shard_map/ppermute | solution.py:43
  62.7 2.2 %collective-permute-done.28 = f32[2,2048]{1,0:T(2,128)S(1)} collective-permute-done((f32[2,2048]{1,0:T(2,128)S(1)}, f32[2,2048]{1,0:T(2,128)S(1)}, u32[]{:S(2)}, u32[]{:S(2)}) %collective-permute-start.28) | collective-permute-done | bytes 16416 | tf_op jit(solution)/shard_map/ppermute | solution.py:43
  64.9 2.7 %collective-permute-start.29 = (f32[2,2048]{1,0:T(2,128)S(1)}, f32[2,2048]{1,0:T(2,128)S(1)}, u32[]{:S(2)}, u32[]{:S(2)}) collective-permute-start(f32[2,2048]{1,0:T(2,128)S(1)} %add.66), channel_id=1, source_target_pairs={{0,2},{1,3},{2,0},{3,1},{4,6},{5,7},{6,4},{7,5},{8,10},{9,11},{10,... | collective-permute-start | bytes 49160 | tf_op jit(solution)/shard_map/ppermute | solution.py:43
  67.6 2.0 %collective-permute-done.29 = f32[2,2048]{1,0:T(2,128)S(1)} collective-permute-done((f32[2,2048]{1,0:T(2,128)S(1)}, f32[2,2048]{1,0:T(2,128)S(1)}, u32[]{:S(2)}, u32[]{:S(2)}) %collective-permute-start.29) | collective-permute-done | bytes 16416 | tf_op jit(solution)/shard_map/ppermute | solution.py:43
  69.6 0.6 add_add_fusion
  (46 shorter events, 0.2 us)
Async XLA Ops:
  0.0 5.4 %collective-permute-start.1 = (bf16[2048,128]{1,0:T(8,128)(2,1)}, bf16[2048,128]{1,0:T(8,128)(2,1)S(1)}, u32[]{:S(2)}, u32[]{:S(2)}) collective-permute-start(bf16[2048,128]{1,0:T(8,128)(2,1)} %bitcast.23), channel_id=1, source_target_pairs={{0,4},{4,0},{8,12},{12,8},{16,20},{20,16},{24,28},{28,24},{1,5},{5... | collective-permute-start | bytes 1572872 | tf_op jit(solution)/shard_map/ppermute | solution.py:43
  0.5 5.0 %collective-permute-start.2 = (bf16[2048,128]{1,0:T(8,128)(2,1)}, bf16[2048,128]{1,0:T(8,128)(2,1)S(1)}, u32[]{:S(2)}, u32[]{:S(2)}) collective-permute-start(bf16[2048,128]{1,0:T(8,128)(2,1)} %bitcast.27), channel_id=1, source_target_pairs={{0,4},{4,0},{8,12},{12,8},{16,20},{20,16},{24,28},{28,24},{1,5},{5... | collective-permute-start | bytes 1572872 | tf_op jit(solution)/shard_map/ppermute | solution.py:43
  0.5 11.2 %collective-permute-start.7 = (bf16[2048,128]{1,0:T(8,128)(2,1)}, bf16[2048,128]{1,0:T(8,128)(2,1)S(1)}, u32[]{:S(2)}, u32[]{:S(2)}) collective-permute-start(bf16[2048,128]{1,0:T(8,128)(2,1)} %bitcast.24), channel_id=1, source_target_pairs={{0,8},{4,20},{8,0},{12,28},{16,24},{20,4},{24,16},{28,12},{1,9},{5... | collective-permute-start | bytes 1572872 | tf_op jit(solution)/shard_map/ppermute | solution.py:64
  3.5 0.7 %copy-start.5 = (f32[2,2048]{1,0:T(2,128)S(1)}, f32[2,2048]{1,0:T(2,128)}, u32[]{:S(2)}) copy-start(f32[2,2048]{1,0:T(2,128)} %tokens_ref.3) | copy-start | bytes 49156
  4.3 1.1 %collective-permute-start = (f32[2,128]{1,0:T(2,128)S(1)}, f32[2,128]{1,0:T(2,128)S(1)}, u32[]{:S(2)}, u32[]{:S(2)}) collective-permute-start(f32[2,128]{1,0:T(2,128)S(1)} %get-tuple-element.33), channel_id=1, source_target_pairs={{0,4},{4,0},{8,12},{12,8},{16,20},{20,16},{24,28},{28,24},{1,5},{5... | collective-permute-start | bytes 3080 | tf_op jit(solution)/shard_map/ppermute | solution.py:43
  5.4 5.6 %collective-permute-start.3 = (f32[2,128]{1,0:T(2,128)S(1)}, f32[2,128]{1,0:T(2,128)S(1)}, u32[]{:S(2)}, u32[]{:S(2)}) collective-permute-start(f32[2,128]{1,0:T(2,128)S(1)} %add.53), channel_id=1, source_target_pairs={{0,16},{4,12},{8,24},{12,4},{16,0},{20,28},{24,8},{28,20},{1,17},{... | collective-permute-start | bytes 3080 | tf_op jit(solution)/shard_map/ppermute | solution.py:64
  7.0 0.8 %copy-start.4 = (f32[1,16384]{1,0:T(1,128)S(1)}, f32[1,16384]{1,0:T(1,128)}, u32[]{:S(2)}) copy-start(f32[1,16384]{1,0:T(1,128)} %param.11) | copy-start | bytes 196612
  7.8 4.6 %copy-start.3 = (bf16[1,2048,128]{2,1,0:T(8,128)(2,1)S(1)}, bf16[1,2048,128]{2,1,0:T(8,128)(2,1)}, u32[]{:S(2)}) copy-start(bf16[1,2048,128]{2,1,0:T(8,128)(2,1)} %param.14) | copy-start | bytes 1572868
  11.0 1.2 %collective-permute-start.4 = (f32[2,128]{1,0:T(2,128)S(1)}, f32[2,128]{1,0:T(2,128)S(1)}, u32[]{:S(2)}, u32[]{:S(2)}) collective-permute-start(f32[2,128]{1,0:T(2,128)S(1)} %collective-permute-done.3), channel_id=1, source_target_pairs={{0,4},{4,0},{8,12},{12,8},{16,20},{20,16},{24,28},{28,24},{1,5},{5... | collective-permute-start | bytes 3080 | tf_op jit(solution)/shard_map/ppermute | solution.py:43
  11.1 9.3 %collective-permute-start.6 = (bf16[2048,128]{1,0:T(8,128)(2,1)S(1)}, bf16[2048,128]{1,0:T(8,128)(2,1)S(1)}, u32[]{:S(2)}, u32[]{:S(2)}) collective-permute-start(bf16[2048,128]{1,0:T(8,128)(2,1)S(1)} %collective-permute-done.1.refs_6_), channel_id=1, source_target_pairs={{0,8},{4,20},{8,0},{12,28},{16,24},{20,4},{24,16},{28,12},{1,9},{5... | collective-permute-start | bytes 1572872 | tf_op jit(solution)/shard_map/ppermute | solution.py:64
  12.3 8.1 %collective-permute-start.8 = (bf16[2048,128]{1,0:T(8,128)(2,1)S(1)}, bf16[2048,128]{1,0:T(8,128)(2,1)S(1)}, u32[]{:S(2)}, u32[]{:S(2)}) collective-permute-start(bf16[2048,128]{1,0:T(8,128)(2,1)S(1)} %collective-permute-done.7.refs_5_), channel_id=1, source_target_pairs={{0,4},{4,0},{8,12},{12,8},{16,20},{20,16},{24,28},{28,24},{1,5},{5... | collective-permute-start | bytes 1572872 | tf_op jit(solution)/shard_map/ppermute | solution.py:43
  12.4 13.7 %collective-permute-start.18 = (bf16[2048,128]{1,0:T(8,128)(2,1)S(1)}, bf16[2048,128]{1,0:T(8,128)(2,1)S(1)}, u32[]{:S(2)}, u32[]{:S(2)}) collective-permute-start(bf16[2048,128]{1,0:T(8,128)(2,1)S(1)} %bitcast.28), channel_id=1, source_target_pairs={{0,8},{4,20},{8,0},{12,28},{16,24},{20,4},{24,16},{28,12},{1,9},{5... | collective-permute-start | bytes 1572872 | tf_op jit(solution)/shard_map/ppermute | solution.py:64
  13.3 5.4 %collective-permute-start.5 = (f32[2,128]{1,0:T(2,128)S(1)}, f32[2,128]{1,0:T(2,128)S(1)}, u32[]{:S(2)}, u32[]{:S(2)}) collective-permute-start(f32[2,128]{1,0:T(2,128)S(1)} %collective-permute-done.4), channel_id=1, source_target_pairs={{0,16},{4,12},{8,24},{12,4},{16,0},{20,28},{24,8},{28,20},{1,17},{... | collective-permute-start | bytes 3080 | tf_op jit(solution)/shard_map/ppermute | solution.py:64
  14.5 5.9 %copy-start = (bf16[1,2048,1024]{2,1,0:T(8,128)(2,1)S(1)}, bf16[1,2048,1024]{2,1,0:T(8,128)(2,1)}, u32[]{:S(2)}) copy-start(bf16[1,2048,1024]{2,1,0:T(8,128)(2,1)} %param.12) | copy-start | bytes 12582916
  14.5 5.9 %copy-start.2 = (bf16[1,2048,128]{2,1,0:T(8,128)(2,1)S(1)}, bf16[1,2048,128]{2,1,0:T(8,128)(2,1)}, u32[]{:S(2)}) copy-start(bf16[1,2048,128]{2,1,0:T(8,128)(2,1)} %param.13) | copy-start | bytes 1572868
  20.4 2.6 %copy-start.8 = (s32[2]{0:T(128)S(1)}, s32[2]{0:T(128)}, u32[]{:S(2)}) copy-start(s32[2]{0:T(128)} %param.17) | copy-start | bytes 28
  21.2 1.2 %collective-permute-start.9 = (f32[2,10,128]{2,1,0:T(8,128)S(1)}, f32[2,10,128]{2,1,0:T(8,128)S(1)}, u32[]{:S(2)}, u32[]{:S(2)}) collective-permute-start(f32[2,10,128]{2,1,0:T(8,128)S(1)} %query_products.1), channel_id=1, source_target_pairs={{0,4},{4,0},{8,12},{12,8},{16,20},{20,16},{24,28},{28,24},{1,5},{5... | collective-permute-start | bytes 30728 | tf_op jit(solution)/shard_map/ppermute | solution.py:43
  22.5 3.8 %collective-permute-start.14 = (f32[2,10,128]{2,1,0:T(8,128)S(1)}, f32[2,10,128]{2,1,0:T(8,128)S(1)}, u32[]{:S(2)}, u32[]{:S(2)}) collective-permute-start(f32[2,10,128]{2,1,0:T(8,128)S(1)} %add.57), channel_id=1, source_target_pairs={{0,16},{4,12},{8,24},{12,4},{16,0},{20,28},{24,8},{28,20},{1,17},{... | collective-permute-start | bytes 30728 | tf_op jit(solution)/shard_map/ppermute | solution.py:64
  23.1 9.4 %collective-permute-start.11 = (bf16[2048,128]{1,0:T(8,128)(2,1)S(1)}, bf16[2048,128]{1,0:T(8,128)(2,1)S(1)}, u32[]{:S(2)}, u32[]{:S(2)}) collective-permute-start(bf16[2048,128]{1,0:T(8,128)(2,1)S(1)} %collective-permute-done.8.refs_7_), channel_id=1, source_target_pairs={{0,8},{4,20},{8,0},{12,28},{16,24},{20,4},{24,16},{28,12},{1,9},{5... | collective-permute-start | bytes 1572872 | tf_op jit(solution)/shard_map/ppermute | solution.py:64
  26.3 6.2 %collective-permute-start.19 = (bf16[2048,128]{1,0:T(8,128)(2,1)S(1)}, bf16[2048,128]{1,0:T(8,128)(2,1)S(1)}, u32[]{:S(2)}, u32[]{:S(2)}) collective-permute-start(bf16[2048,128]{1,0:T(8,128)(2,1)S(1)} %collective-permute-done.18.refs_5_), channel_id=1, source_target_pairs={{0,4},{4,0},{8,12},{12,8},{16,20},{20,16},{24,28},{28,24},{1,5},{5... | collective-permute-start | bytes 1572872 | tf_op jit(solution)/shard_map/ppermute | solution.py:43
  27.0 1.4 %collective-permute-start.15 = (f32[2,10,128]{2,1,0:T(8,128)S(1)}, f32[2,10,128]{2,1,0:T(8,128)S(1)}, u32[]{:S(2)}, u32[]{:S(2)}) collective-permute-start(f32[2,10,128]{2,1,0:T(8,128)S(1)} %collective-permute-done.14), channel_id=1, source_target_pairs={{0,4},{4,0},{8,12},{12,8},{16,20},{20,16},{24,28},{28,24},{1,5},{5... | collective-permute-start | bytes 30728 | tf_op jit(solution)/shard_map/ppermute | solution.py:43
  27.7 7.8 %collective-permute-start.13 = (bf16[2048,128]{1,0:T(8,128)(2,1)S(1)}, bf16[2048,128]{1,0:T(8,128)(2,1)S(1)}, u32[]{:S(2)}, u32[]{:S(2)}) collective-permute-start(bf16[2048,128]{1,0:T(8,128)(2,1)S(1)} %collective-permute-done.6.refs_6_), channel_id=1, source_target_pairs={{0,4},{4,0},{8,12},{12,8},{16,20},{20,16},{24,28},{28,24},{1,5},{5... | collective-permute-start | bytes 1572872 | tf_op jit(solution)/shard_map/ppermute | solution.py:43
  28.4 7.1 %collective-permute-start.16 = (f32[2,10,128]{2,1,0:T(8,128)S(1)}, f32[2,10,128]{2,1,0:T(8,128)S(1)}, u32[]{:S(2)}, u32[]{:S(2)}) collective-permute-start(f32[2,10,128]{2,1,0:T(8,128)S(1)} %collective-permute-done.15), channel_id=1, source_target_pairs={{0,16},{4,12},{8,24},{12,4},{16,0},{20,28},{24,8},{28,20},{1,17},{... | collective-permute-start | bytes 30728 | tf_op jit(solution)/shard_map/ppermute | solution.py:64
  32.5 4.6 %collective-permute-start.12 = (bf16[2048,128]{1,0:T(8,128)(2,1)S(1)}, bf16[2048,128]{1,0:T(8,128)(2,1)S(1)}, u32[]{:S(2)}, u32[]{:S(2)}) collective-permute-start(bf16[2048,128]{1,0:T(8,128)(2,1)S(1)} %collective-permute-done.11.refs_5_), channel_id=1, source_target_pairs={{0,4},{4,0},{8,12},{12,8},{16,20},{20,16},{24,28},{28,24},{1,5},{5... | collective-permute-start | bytes 1572872 | tf_op jit(solution)/shard_map/ppermute | solution.py:43
  32.5 9.2 %collective-permute-start.20 = (bf16[2048,128]{1,0:T(8,128)(2,1)S(1)}, bf16[2048,128]{1,0:T(8,128)(2,1)S(1)}, u32[]{:S(2)}, u32[]{:S(2)}) collective-permute-start(bf16[2048,128]{1,0:T(8,128)(2,1)S(1)} %collective-permute-done.19.refs_6_), channel_id=1, source_target_pairs={{0,8},{4,20},{8,0},{12,28},{16,24},{20,4},{24,16},{28,12},{1,9},{5... | collective-permute-start | bytes 1572872 | tf_op jit(solution)/shard_map/ppermute | solution.py:64
  34.7 12.6 %collective-permute-start.10 = (bf16[2048,128]{1,0:T(8,128)(2,1)S(1)}, bf16[2048,128]{1,0:T(8,128)(2,1)S(1)}, u32[]{:S(2)}, u32[]{:S(2)}) collective-permute-start(bf16[2048,128]{1,0:T(8,128)(2,1)S(1)} %collective-permute-done.2.refs_6_), channel_id=1, source_target_pairs={{0,8},{4,20},{8,0},{12,28},{16,24},{20,4},{24,16},{28,12},{1,9},{5... | collective-permute-start | bytes 1572872 | tf_op jit(solution)/shard_map/ppermute | solution.py:64
  37.0 0.9 %copy-start.7 = (s32[2]{0:T(128)S(1)}, s32[2]{0:T(128)}, u32[]{:S(2)}) copy-start(s32[2]{0:T(128)} %lengths_ref.3) | copy-start | bytes 28
  38.9 1.2 %collective-permute-start.17 = (f32[8,128]{1,0:T(8,128)S(1)}, f32[8,128]{1,0:T(8,128)S(1)}, u32[]{:S(2)}, u32[]{:S(2)}) collective-permute-start(f32[8,128]{1,0:T(8,128)S(1)} %get-tuple-element.51), channel_id=1, source_target_pairs={{0,4},{4,0},{8,12},{12,8},{16,20},{20,16},{24,28},{28,24},{1,5},{5... | collective-permute-start | bytes 12296 | tf_op jit(solution)/shard_map/ppermute | solution.py:43
  41.7 7.0 %collective-permute-start.23 = (bf16[2048,128]{1,0:T(8,128)(2,1)S(1)}, bf16[2048,128]{1,0:T(8,128)(2,1)S(1)}, u32[]{:S(2)}, u32[]{:S(2)}) collective-permute-start(bf16[2048,128]{1,0:T(8,128)(2,1)S(1)} %collective-permute-done.20.refs_7_), channel_id=1, source_target_pairs={{0,4},{4,0},{8,12},{12,8},{16,20},{20,16},{24,28},{28,24},{1,5},{5... | collective-permute-start | bytes 1572872 | tf_op jit(solution)/shard_map/ppermute | solution.py:43
  41.7 5.7 %collective-permute-start.21 = (f32[8,128]{1,0:T(8,128)S(1)}, f32[8,128]{1,0:T(8,128)S(1)}, u32[]{:S(2)}, u32[]{:S(2)}) collective-permute-start(f32[8,128]{1,0:T(8,128)S(1)} %max.6), channel_id=1, source_target_pairs={{0,16},{4,12},{8,24},{12,4},{16,0},{20,28},{24,8},{28,20},{1,17},{... | collective-permute-start | bytes 12296 | tf_op jit(solution)/shard_map/ppermute | solution.py:64
  47.3 3.5 %collective-permute-start.22 = (bf16[2048,128]{1,0:T(8,128)(2,1)S(1)}, bf16[2048,128]{1,0:T(8,128)(2,1)S(1)}, u32[]{:S(2)}, u32[]{:S(2)}) collective-permute-start(bf16[2048,128]{1,0:T(8,128)(2,1)S(1)} %collective-permute-done.10.refs_5_), channel_id=1, source_target_pairs={{0,4},{4,0},{8,12},{12,8},{16,20},{20,16},{24,28},{28,24},{1,5},{5... | collective-permute-start | bytes 1572872 | tf_op jit(solution)/shard_map/ppermute | solution.py:43
  47.3 2.9 %collective-permute-start.24 = (f32[8,128]{1,0:T(8,128)S(1)}, f32[8,128]{1,0:T(8,128)S(1)}, u32[]{:S(2)}, u32[]{:S(2)}) collective-permute-start(f32[8,128]{1,0:T(8,128)S(1)} %max.7), channel_id=1, source_target_pairs={{0,4},{4,0},{8,12},{12,8},{16,20},{20,16},{24,28},{28,24},{1,5},{5... | collective-permute-start | bytes 12296 | tf_op jit(solution)/shard_map/ppermute | solution.py:43
  50.8 9.7 %copy-start.1 = (bf16[1,1024,2048]{2,1,0:T(8,128)(2,1)S(1)}, bf16[1,1024,2048]{2,1,0:T(8,128)(2,1)}, u32[]{:S(2)}) copy-start(bf16[1,1024,2048]{2,1,0:T(8,128)(2,1)} %param.15) | copy-start | bytes 12582916
  52.0 1.2 %collective-permute-start.25 = (f32[8,256]{1,0:T(8,128)S(1)}, f32[8,256]{1,0:T(8,128)S(1)}, u32[]{:S(2)}, u32[]{:S(2)}) collective-permute-start(f32[8,256]{1,0:T(8,128)S(1)} %weighted_values.1), channel_id=1, source_target_pairs={{0,4},{4,0},{8,12},{12,8},{16,20},{20,16},{24,28},{28,24},{1,5},{5... | collective-permute-start | bytes 24584 | tf_op jit(solution)/shard_map/ppermute | solution.py:43
  53.2 3.7 %collective-permute-start.26 = (f32[8,256]{1,0:T(8,128)S(1)}, f32[8,256]{1,0:T(8,128)S(1)}, u32[]{:S(2)}, u32[]{:S(2)}) collective-permute-start(f32[8,256]{1,0:T(8,128)S(1)} %add.64), channel_id=1, source_target_pairs={{0,8},{4,12},{8,0},{12,4},{16,24},{20,28},{24,16},{28,20},{1,9},{5... | collective-permute-start | bytes 24584 | tf_op jit(solution)/shard_map/ppermute | solution.py:43
  56.8 3.7 %collective-permute-start.27 = (f32[8,256]{1,0:T(8,128)S(1)}, f32[8,256]{1,0:T(8,128)S(1)}, u32[]{:S(2)}, u32[]{:S(2)}) collective-permute-start(f32[8,256]{1,0:T(8,128)S(1)} %add.65.mine_ref), channel_id=1, source_target_pairs={{0,16},{4,20},{8,24},{12,28},{16,0},{20,4},{24,8},{28,12},{1,17},{... | collective-permute-start | bytes 24584 | tf_op jit(solution)/shard_map/ppermute | solution.py:43
  60.5 9.1 %copy-start.6 = (f32[2,2048]{1,0:T(2,128)S(1)}, f32[2,2048]{1,0:T(2,128)}, u32[]{:S(2)}) copy-start(f32[2,2048]{1,0:T(2,128)} %tokens_ref.3) | copy-start | bytes 49156
  61.2 3.8 %collective-permute-start.28 = (f32[2,2048]{1,0:T(2,128)S(1)}, f32[2,2048]{1,0:T(2,128)S(1)}, u32[]{:S(2)}, u32[]{:S(2)}) collective-permute-start(f32[2,2048]{1,0:T(2,128)S(1)} %output_products.1), channel_id=1, source_target_pairs={{0,1},{1,0},{2,3},{3,2},{4,5},{5,4},{6,7},{7,6},{8,9},{9,8},{10,11... | collective-permute-start | bytes 49160 | tf_op jit(solution)/shard_map/ppermute | solution.py:43
  64.9 4.7 %collective-permute-start.29 = (f32[2,2048]{1,0:T(2,128)S(1)}, f32[2,2048]{1,0:T(2,128)S(1)}, u32[]{:S(2)}, u32[]{:S(2)}) collective-permute-start(f32[2,2048]{1,0:T(2,128)S(1)} %add.66), channel_id=1, source_target_pairs={{0,2},{1,3},{2,0},{3,1},{4,6},{5,7},{6,4},{7,5},{8,10},{9,11},{10,... | collective-permute-start | bytes 49160 | tf_op jit(solution)/shard_map/ppermute | solution.py:43

commit v11 on v10

--- a/solution.py
+++ b/solution.py
@@ -400,27 +400,24 @@
         [IN_SMEM] * 2 + [IN_VMEM] * 6,
         (shape((heads, row_count)), shape((heads, LANES)), shape((heads, LANES))),
     )(places, lengths, key_total, cosine, sine_part, new_cosine, new_sine, summed)
-    value_mid = value_far[:1] + share(value_far[:1], parts_sent)
-    value_next = send_last(own_values, value_mid[1:])
+    value_mid = value_far + share(value_far[:1], parts_sent)
+    value_last = send_last(own_values, value_mid[-1:])
     top = butterfly(top, "ctx", [1], jnp.maximum)
-    top = after(top, *[block for _, block in value_next])
+    top = after(top, *[block for _, block in value_far[1:]])
     near_top = top
     if split:
-        received = jnp.maximum(top, after(by_core(top, 4, 2), value_far[1][1]))
+        received = jnp.maximum(top, after(by_core(top, 4, 2), value_last[0][1]))
         top = jnp.where(core == 0, swap(received, "ctx", 1), received)
     else:
         top = butterfly(top, "ctx", bits_below(team)[1:], jnp.maximum)
         received = top
 
-    value_mid += value_next + share(value_next, near_top)
+    value_mid += share(value_far[1:], near_top)
     value_total = project(after(places, near_top), rows, value_near)
     value_total = project(places, rows, value_mid, value_total)
 
-    blocks = share(value_far[1:], received)
-    if blocks:
-        value_total = project(places, rows, value_far[1:], value_total)
-    else:
-        blocks = value_far[1:]
+    blocks = share(value_last, received)
+    value_total = project(places, rows, value_last, value_total)
     packed = call(
         functools.partial(weigh_kernel, [d for d, _ in blocks], len(rows), team),
         "weighted_values",

time: 70.5 us -> 66.4 us (0.942)
  waiting for transfers between devices: 27.2 us -> 24.8 us
  starting transfers between devices: 22.3 us -> 20.6 us
    ppermute x11, waiting for transfers between devices: 12.8 us -> 10.3 us  [by_core(): return lax.ppermute(value, 'ctx', pairs)]
    ppermute x19, starting transfers between devices: 9.21 us -> 8 us  [swap(): return lax.ppermute(value, axis, [(i, i ^ distance) for i in range(count)])]
  transfers between devices with their start and end apart: 30 -> 30, of which waited for: 16 -> 15; matrix products, arithmetic and copies ran while one was open for 1% -> 1% of each run, Pallas kernels for 22% -> 24%
where the time goes in v11:
time: 66.4 us; the launch traced here: 66.2 us
  waiting for transfers between devices  24.8 us (37%)
  starting transfers between devices  20.6 us (31%)
  Pallas kernels  17.4 us (26%)
  local copies, waits for them, and re-layouts  1.59 us (2%)
  other arithmetic  1.49 us (2%)
    ppermute x19, waiting for transfers between devices, swap(): return lax.ppermute(value, axis, [(i, i ^ distance) for i in range(count)])  14.5 us
    ppermute x11, starting transfers between devices, by_core(): return lax.ppermute(value, 'ctx', pairs)  12.6 us
    ppermute x11, waiting for transfers between devices, by_core(): return lax.ppermute(value, 'ctx', pairs)  10.3 us
    ppermute x19, starting transfers between devices, swap(): return lax.ppermute(value, axis, [(i, i ^ distance) for i in range(count)])  8 us
    pallas_call x2, Pallas kernels, normalise(): call(functools.partial(norm_kernel, first), 'normalise', [IN_HBM, IN_VMEM...  7.47 us
    pallas_call x6, Pallas kernels, project(): call(functools.partial(project_kernel, [d for d, _ in blocks], len(rows),...  6.17 us
    unnamed x18, local copies, waits for them, and re-layouts  1.59 us
  transfers between devices with their start and end apart: 30, of which 15 were waited for; matrix products, arithmetic and copies ran while one was open for 1% of the time, Pallas kernels for 24%

profile of v11, /device:TPU:0, one launch (start us, length us, event | category | flops | bytes accessed | tf_op | source)
XLA Modules:
  0.0 66.2 jit_solution(4517593336416762851)
XLA Ops:
  0.0 0.5 collective-permute-start.1
  0.5 0.1 collective-permute-start.2
  0.5 2.9 %collective-permute-start.5 = (bf16[2048,128]{1,0:T(8,128)(2,1)}, bf16[2048,128]{1,0:T(8,128)(2,1)S(1)}, u32[]{:S(2)}, u32[]{:S(2)}) collective-permute-start(bf16[2048,128]{1,0:T(8,128)(2,1)} %bitcast.24), channel_id=1, source_target_pairs={{0,8},{4,20},{8,0},{12,28},{16,24},{20,4},{24,16},{28,12},{1,9},{5... | collective-permute-start | bytes 1572872 | tf_op jit(solution)/shard_map/ppermute | solution.py:64
  3.5 0.7 %copy-done.5 = f32[2,2048]{1,0:T(2,128)S(1)} copy-done((f32[2,2048]{1,0:T(2,128)S(1)}, f32[2,2048]{1,0:T(2,128)}, u32[]{:S(2)}) %copy-start.5) | copy-done | bytes 16408
  4.2 0.1 squares.1
  4.3 1.1 %collective-permute-done = f32[2,128]{1,0:T(2,128)S(1)} collective-permute-done((f32[2,128]{1,0:T(2,128)S(1)}, f32[2,128]{1,0:T(2,128)S(1)}, u32[]{:S(2)}, u32[]{:S(2)}) %collective-permute-start) | collective-permute-done | bytes 1056 | tf_op jit(solution)/shard_map/ppermute | solution.py:43
  5.4 0.0 collective-permute-done.1.refs_6_
  5.4 0.0 collective-permute-done.2.refs_6_
  5.4 1.6 %collective-permute-start.3 = (f32[2,128]{1,0:T(2,128)S(1)}, f32[2,128]{1,0:T(2,128)S(1)}, u32[]{:S(2)}, u32[]{:S(2)}) collective-permute-start(f32[2,128]{1,0:T(2,128)S(1)} %add.53), channel_id=1, source_target_pairs={{0,16},{4,12},{8,24},{12,4},{16,0},{20,28},{24,8},{28,20},{1,17},{... | collective-permute-start | bytes 3080 | tf_op jit(solution)/shard_map/ppermute | solution.py:64
  7.0 0.8 %copy-done.4 = f32[1,16384]{1,0:T(1,128)S(1)} copy-done((f32[1,16384]{1,0:T(1,128)S(1)}, f32[1,16384]{1,0:T(1,128)}, u32[]{:S(2)}) %copy-start.4) | copy-done | bytes 65560
  7.8 3.2 %normalise.2 = (bf16[8,64,2048]{2,1,0:T(8,128)(2,1)S(1)}, bf16[8,64,2048]{2,1,0:T(8,128)(2,1)S(1)}) custom-call(bf16[320,16384]{1,0:T(8,128)(2,1)} %bitcast.35, f32[8,1,2048]{2,1,0:T(1,128)S(1)} %bitcast.31), custom_call_target="tpu_custom_call" | custom-call | flops 1000 | bytes 1000 | tf_op jit(solution)/shard_map/normalise/pallas_call | solution.py:173
  11.0 0.1 collective-permute-start.4
  11.1 0.6 collective-permute-start.8
  11.7 0.5 collective-permute-done.4
  12.3 0.2 collective-permute-start.9
  12.4 0.9 %collective-permute-start.6 = (bf16[2048,128]{1,0:T(8,128)(2,1)S(1)}, bf16[2048,128]{1,0:T(8,128)(2,1)S(1)}, u32[]{:S(2)}, u32[]{:S(2)}) collective-permute-start(bf16[2048,128]{1,0:T(8,128)(2,1)S(1)} %bitcast.28), channel_id=1, source_target_pairs={{0,8},{4,20},{8,0},{12,28},{16,24},{20,4},{24,16},{28,12},{1,9},{5... | collective-permute-start | bytes 1572872 | tf_op jit(solution)/shard_map/ppermute | solution.py:64
  13.3 1.1 %collective-permute-start.7 = (f32[2,128]{1,0:T(2,128)S(1)}, f32[2,128]{1,0:T(2,128)S(1)}, u32[]{:S(2)}, u32[]{:S(2)}) collective-permute-start(f32[2,128]{1,0:T(2,128)S(1)} %collective-permute-done.4), channel_id=1, source_target_pairs={{0,16},{4,12},{8,24},{12,4},{16,0},{20,28},{24,8},{28,20},{1,17},{... | collective-permute-start | bytes 3080 | tf_op jit(solution)/shard_map/ppermute | solution.py:64
  14.5 4.3 %normalise.3 = (bf16[8,64,2048]{2,1,0:T(8,128)(2,1)S(1)}, bf16[8,64,2048]{2,1,0:T(8,128)(2,1)S(1)}, bf16[8,64,2048]{2,1,0:T(8,128)(2,1)S(1)}) custom-call(bf16[320,16384]{1,0:T(8,128)(2,1)} %bitcast.36, f32[8,1,2048]{2,1,0:T(1,128)S(1)} %bitcast.32), custom_call_target="tpu_custom_call" | custom-call | flops 1000 | bytes 1000 | tf_op jit(solution)/shard_map/normalise/pallas_call | solution.py:173
  18.8 1.6 %collective-permute-done.8.refs_6_ = bf16[2048,128]{1,0:T(8,128)(2,1)S(1)} collective-permute-done((bf16[2048,128]{1,0:T(8,128)(2,1)S(1)}, bf16[2048,128]{1,0:T(8,128)(2,1)S(1)}, u32[]{:S(2)}, u32[]{:S(2)}) %collective-permute-start.8) | collective-permute-done | bytes 524320 | tf_op jit(solution)/shard_map/ppermute | solution.py:64
  20.4 0.0 copy-start.8
  20.4 0.8 %query_products.1 = f32[2,10,128]{2,1,0:T(8,128)S(1)} custom-call(s32[1]{0:T(128)} %bitcast.place_ref, f32[2,128]{1,0:T(2,128)S(1)} %add_add_fusion.2.squares_ref, f32[2,2048]{1,0:T(2,128)S(1)} %copy-done.5, f32[8,1,2048]{2,1,0:T(1,128)S(1)} %bitcast.33, bf16[2048,1024]{1,0:T(8,128)(2,1)S(1)} %bitcast.21, bf16[2048,128]{1,0:T(8,128)(2,1)S(1)} %bitcast.25, ...), custom_call_target="tpu_custom_call" | custom-call | flops 1000 | bytes 1000 | tf_op jit(solution)/shard_map/query_products/pallas_call | solution.py:371
  21.2 0.1 collective-permute-start.10
  21.4 0.6 collective-permute-start.14
  22.0 0.5 collective-permute-done.10
  22.5 0.9 %collective-permute-start.11 = (f32[2,10,128]{2,1,0:T(8,128)S(1)}, f32[2,10,128]{2,1,0:T(8,128)S(1)}, u32[]{:S(2)}, u32[]{:S(2)}) collective-permute-start(f32[2,10,128]{2,1,0:T(8,128)S(1)} %add.57), channel_id=1, source_target_pairs={{0,16},{4,12},{8,24},{12,4},{16,0},{20,28},{24,8},{28,20},{1,17},{... | collective-permute-start | bytes 30728 | tf_op jit(solution)/shard_map/ppermute | solution.py:64
  23.4 2.8 %collective-permute-done.6.refs_5_ = bf16[2048,128]{1,0:T(8,128)(2,1)S(1)} collective-permute-done((bf16[2048,128]{1,0:T(8,128)(2,1)S(1)}, bf16[2048,128]{1,0:T(8,128)(2,1)S(1)}, u32[]{:S(2)}, u32[]{:S(2)}) %collective-permute-start.6) | collective-permute-done | bytes 524320 | tf_op jit(solution)/shard_map/ppermute | solution.py:64
  26.2 0.3 collective-permute-done.11
  26.5 0.6 multiply_sine_fusion
  27.1 0.6 collective-permute-start.17
  27.7 0.1 multiply_sine_fusion.1
  27.8 0.1 collective-permute-start.16
  27.9 1.1 %collective-permute-start.20 = (bf16[2048,128]{1,0:T(8,128)(2,1)S(1)}, bf16[2048,128]{1,0:T(8,128)(2,1)S(1)}, u32[]{:S(2)}, u32[]{:S(2)}) collective-permute-start(bf16[2048,128]{1,0:T(8,128)(2,1)S(1)} %collective-permute-done.2.refs_6_), channel_id=1, source_target_pairs={{0,8},{4,20},{8,0},{12,28},{16,24},{20,4},{24,16},{28,12},{1,9},{5... | collective-permute-start | bytes 1572872 | tf_op jit(solution)/shard_map/ppermute | solution.py:64
  29.0 0.8 %collective-permute-start.18 = (f32[2,10,128]{2,1,0:T(8,128)S(1)}, f32[2,10,128]{2,1,0:T(8,128)S(1)}, u32[]{:S(2)}, u32[]{:S(2)}) collective-permute-start(f32[2,10,128]{2,1,0:T(8,128)S(1)} %collective-permute-done.17), channel_id=1, source_target_pairs={{0,16},{4,12},{8,24},{12,4},{16,0},{20,28},{24,8},{28,20},{1,17},{... | collective-permute-start | bytes 30728 | tf_op jit(solution)/shard_map/ppermute | solution.py:64
  29.8 2.1 %collective-permute-done.14.refs_5_ = bf16[2048,128]{1,0:T(8,128)(2,1)S(1)} collective-permute-done((bf16[2048,128]{1,0:T(8,128)(2,1)S(1)}, bf16[2048,128]{1,0:T(8,128)(2,1)S(1)}, u32[]{:S(2)}, u32[]{:S(2)}) %collective-permute-start.14) | collective-permute-done | bytes 524320 | tf_op jit(solution)/shard_map/ppermute | solution.py:64
  32.0 0.9 %project.6.refs_9_ = f32[320,128]{1,0:T(8,128)S(1)} custom-call(s32[1]{0:T(128)} %bitcast.place_ref, bf16[8,64,2048]{2,1,0:T(8,128)(2,1)S(1)} %get-tuple-element.36.refs_0_, bf16[8,64,2048]{2,1,0:T(8,128)(2,1)S(1)} %get-tuple-element.37.refs_1_, bf16[8,64,2048]{2,1,0:T(8,128)(2,1)S(1)} %get-tuple-element.40.refs_2_, ...), custom_call_target="tpu_custom_call" | custom-call | flops 1000 | bytes 1000 | tf_op jit(solution)/shard_map/project/pallas_call | solution.py:218
  32.8 0.4 collective-permute-start.13
  33.3 1.5 %project.7.refs_7_ = f32[320,128]{1,0:T(8,128)S(1)} custom-call(s32[1]{0:T(128)} %bitcast.place_ref, bf16[8,64,2048]{2,1,0:T(8,128)(2,1)S(1)} %get-tuple-element.36.refs_0_, bf16[8,64,2048]{2,1,0:T(8,128)(2,1)S(1)} %get-tuple-element.37.refs_1_, bf16[8,64,2048]{2,1,0:T(8,128)(2,1)S(1)} %get-tuple-element.40.refs_2_, ...), custom_call_target="tpu_custom_call" | custom-call | flops 1000 | bytes 1000 | tf_op jit(solution)/shard_map/project/pallas_call | solution.py:218
  34.9 0.0 copy-start.7
  34.9 0.9 %project.8.refs_0_ = f32[320,128]{1,0:T(8,128)S(1)} custom-call(s32[1]{0:T(128)} %bitcast.place_ref, bf16[8,64,2048]{2,1,0:T(8,128)(2,1)S(1)} %get-tuple-element.36.refs_0_, bf16[8,64,2048]{2,1,0:T(8,128)(2,1)S(1)} %get-tuple-element.37.refs_1_, bf16[8,64,2048]{2,1,0:T(8,128)(2,1)S(1)} %get-tuple-element.40.refs_2_, ...), custom_call_target="tpu_custom_call" | custom-call | flops 1000 | bytes 1000 | tf_op jit(solution)/shard_map/project/pallas_call | solution.py:218
  35.8 1.0 %scores.1 = (f32[8,320]{1,0:T(8,128)S(1)}, f32[8,128]{1,0:T(8,128)S(1)}, f32[8,128]{1,0:T(8,128)S(1)}) custom-call(s32[1]{0:T(128)} %bitcast.place_ref, s32[2]{0:T(128)S(1)} %copy-done.7, f32[320,128]{1,0:T(8,128)S(1)} %project.8.refs_0_, f32[320,64]{1,0:T(8,128)S(1)} %get-tuple-element.62.refs_1_, f32[320,64]{1,0:T(8,128)S(1)} %get-tuple-element.61.refs_2_, ...), custom_call_target="tpu_custom_call" | custom-call | flops 1000 | bytes 1000 | tf_op jit(solution)/shard_map/scores/pallas_call | solution.py:397
  36.8 0.2 collective-permute-start.19
  37.0 1.0 %collective-permute-done.19 = f32[8,128]{1,0:T(8,128)S(1)} collective-permute-done((f32[8,128]{1,0:T(8,128)S(1)}, f32[8,128]{1,0:T(8,128)S(1)}, u32[]{:S(2)}, u32[]{:S(2)}) %collective-permute-start.19) | collective-permute-done | bytes 4128 | tf_op jit(solution)/shard_map/ppermute | solution.py:43
  37.9 0.2 collective-permute-start.23
  38.1 1.7 %collective-permute-start.21 = (f32[8,128]{1,0:T(8,128)S(1)}, f32[8,128]{1,0:T(8,128)S(1)}, u32[]{:S(2)}, u32[]{:S(2)}) collective-permute-start(f32[8,128]{1,0:T(8,128)S(1)} %max.6), channel_id=1, source_target_pairs={{0,16},{4,12},{8,24},{12,4},{16,0},{20,28},{24,8},{28,20},{1,17},{... | collective-permute-start | bytes 12296 | tf_op jit(solution)/shard_map/ppermute | solution.py:64
  39.8 2.0 %collective-permute-done.21 = f32[8,128]{1,0:T(8,128)S(1)} collective-permute-done((f32[8,128]{1,0:T(8,128)S(1)}, f32[8,128]{1,0:T(8,128)S(1)}, u32[]{:S(2)}, u32[]{:S(2)}) %collective-permute-start.21) | collective-permute-done | bytes 4128 | tf_op jit(solution)/shard_map/ppermute | solution.py:64
  41.9 1.4 %collective-permute-done.13.refs_5_ = bf16[2048,128]{1,0:T(8,128)(2,1)S(1)} collective-permute-done((bf16[2048,128]{1,0:T(8,128)(2,1)S(1)}, bf16[2048,128]{1,0:T(8,128)(2,1)S(1)}, u32[]{:S(2)}, u32[]{:S(2)}) %collective-permute-start.13) | collective-permute-done | bytes 524320 | tf_op jit(solution)/shard_map/ppermute | solution.py:64
  43.3 0.5 collective-permute-start.24
  43.8 0.9 %project.9.refs_9_ = f32[320,128]{1,0:T(8,128)S(1)} custom-call(s32[1]{0:T(128)} %bitcast.place_ref, bf16[8,64,2048]{2,1,0:T(8,128)(2,1)S(1)} %get-tuple-element.36.refs_0_, bf16[8,64,2048]{2,1,0:T(8,128)(2,1)S(1)} %get-tuple-element.37.refs_1_, bf16[8,64,2048]{2,1,0:T(8,128)(2,1)S(1)} %get-tuple-element.40.refs_2_, ...), custom_call_target="tpu_custom_call" | custom-call | flops 1000 | bytes 1000 | tf_op jit(solution)/shard_map/project/pallas_call | solution.py:218
  44.6 1.5 %project.10.refs_6_ = f32[320,128]{1,0:T(8,128)S(1)} custom-call(s32[1]{0:T(128)} %bitcast.place_ref, bf16[8,64,2048]{2,1,0:T(8,128)(2,1)S(1)} %get-tuple-element.36.refs_0_, bf16[8,64,2048]{2,1,0:T(8,128)(2,1)S(1)} %get-tuple-element.37.refs_1_, bf16[8,64,2048]{2,1,0:T(8,128)(2,1)S(1)} %get-tuple-element.40.refs_2_, ...), custom_call_target="tpu_custom_call" | custom-call | flops 1000 | bytes 1000 | tf_op jit(solution)/shard_map/project/pallas_call | solution.py:218
  46.2 0.5 project.11.refs_6_
  46.7 0.0 copy-start.1
  46.8 1.2 %weighted_values.1 = f32[8,256]{1,0:T(8,128)S(1)} custom-call(s32[1]{0:T(128)} %bitcast.place_ref, s32[2]{0:T(128)S(1)} %copy-done.7, bf16[8,64,2048]{2,1,0:T(8,128)(2,1)S(1)} %get-tuple-element.36.refs_0_, bf16[8,64,2048]{2,1,0:T(8,128)(2,1)S(1)} %get-tuple-element.37.refs_1_, bf16[8,64,2048]{2,1,0:T(8,128)(2,1)S(1)} %get-tuple-element.40.refs_2_, ...), custom_call_target="tpu_custom_call" | custom-call | flops 1000 | bytes 1000 | tf_op jit(solution)/shard_map/weighted_values/pallas_call | solution.py:421
  47.9 0.0 collective-permute-start.25
  47.9 1.2 %collective-permute-done.25 = f32[8,256]{1,0:T(8,128)S(1)} collective-permute-done((f32[8,256]{1,0:T(8,128)S(1)}, f32[8,256]{1,0:T(8,128)S(1)}, u32[]{:S(2)}, u32[]{:S(2)}) %collective-permute-start.25) | collective-permute-done | bytes 8224 | tf_op jit(solution)/shard_map/ppermute | solution.py:43
  49.1 0.8 %collective-permute-start.26 = (f32[8,256]{1,0:T(8,128)S(1)}, f32[8,256]{1,0:T(8,128)S(1)}, u32[]{:S(2)}, u32[]{:S(2)}) collective-permute-start(f32[8,256]{1,0:T(8,128)S(1)} %add.64), channel_id=1, source_target_pairs={{0,8},{4,12},{8,0},{12,4},{16,24},{20,28},{24,16},{28,20},{1,9},{5... | collective-permute-start | bytes 24584 | tf_op jit(solution)/shard_map/ppermute | solution.py:43
  49.9 2.9 %collective-permute-done.26 = f32[8,256]{1,0:T(8,128)S(1)} collective-permute-done((f32[8,256]{1,0:T(8,128)S(1)}, f32[8,256]{1,0:T(8,128)S(1)}, u32[]{:S(2)}, u32[]{:S(2)}) %collective-permute-start.26) | collective-permute-done | bytes 8224 | tf_op jit(solution)/shard_map/ppermute | solution.py:43
  52.8 0.6 collective-permute-start.27
  53.3 3.1 %collective-permute-done.27.other_ref = f32[8,256]{1,0:T(8,128)S(1)} collective-permute-done((f32[8,256]{1,0:T(8,128)S(1)}, f32[8,256]{1,0:T(8,128)S(1)}, u32[]{:S(2)}, u32[]{:S(2)}) %collective-permute-start.27) | collective-permute-done | bytes 8224 | tf_op jit(solution)/shard_map/ppermute | solution.py:43
  56.4 0.6 output_products.1
  57.1 1.6 %collective-permute-start.28 = (f32[2,2048]{1,0:T(2,128)S(1)}, f32[2,2048]{1,0:T(2,128)S(1)}, u32[]{:S(2)}, u32[]{:S(2)}) collective-permute-start(f32[2,2048]{1,0:T(2,128)S(1)} %output_products.1), channel_id=1, source_target_pairs={{0,1},{1,0},{2,3},{3,2},{4,5},{5,4},{6,7},{7,6},{8,9},{9,8},{10,11... | collective-permute-start | bytes 49160 | tf_op jit(solution)/shard_map/ppermute | solution.py:43
  58.7 2.2 %collective-permute-done.28 = f32[2,2048]{1,0:T(2,128)S(1)} collective-permute-done((f32[2,2048]{1,0:T(2,128)S(1)}, f32[2,2048]{1,0:T(2,128)S(1)}, u32[]{:S(2)}, u32[]{:S(2)}) %collective-permute-start.28) | collective-permute-done | bytes 16416 | tf_op jit(solution)/shard_map/ppermute | solution.py:43
  60.8 2.7 %collective-permute-start.29 = (f32[2,2048]{1,0:T(2,128)S(1)}, f32[2,2048]{1,0:T(2,128)S(1)}, u32[]{:S(2)}, u32[]{:S(2)}) collective-permute-start(f32[2,2048]{1,0:T(2,128)S(1)} %add.66), channel_id=1, source_target_pairs={{0,2},{1,3},{2,0},{3,1},{4,6},{5,7},{6,4},{7,5},{8,10},{9,11},{10,... | collective-permute-start | bytes 49160 | tf_op jit(solution)/shard_map/ppermute | solution.py:43
  63.5 2.0 %collective-permute-done.29 = f32[2,2048]{1,0:T(2,128)S(1)} collective-permute-done((f32[2,2048]{1,0:T(2,128)S(1)}, f32[2,2048]{1,0:T(2,128)S(1)}, u32[]{:S(2)}, u32[]{:S(2)}) %collective-permute-start.29) | collective-permute-done | bytes 16416 | tf_op jit(solution)/shard_map/ppermute | solution.py:43
  65.5 0.6 add_add_fusion
  (46 shorter events, 0.2 us)
Async XLA Ops:
  0.0 5.4 %collective-permute-start.1 = (bf16[2048,128]{1,0:T(8,128)(2,1)}, bf16[2048,128]{1,0:T(8,128)(2,1)S(1)}, u32[]{:S(2)}, u32[]{:S(2)}) collective-permute-start(bf16[2048,128]{1,0:T(8,128)(2,1)} %bitcast.23), channel_id=1, source_target_pairs={{0,4},{4,0},{8,12},{12,8},{16,20},{20,16},{24,28},{28,24},{1,5},{5... | collective-permute-start | bytes 1572872 | tf_op jit(solution)/shard_map/ppermute | solution.py:43
  0.5 5.0 %collective-permute-start.2 = (bf16[2048,128]{1,0:T(8,128)(2,1)}, bf16[2048,128]{1,0:T(8,128)(2,1)S(1)}, u32[]{:S(2)}, u32[]{:S(2)}) collective-permute-start(bf16[2048,128]{1,0:T(8,128)(2,1)} %bitcast.27), channel_id=1, source_target_pairs={{0,4},{4,0},{8,12},{12,8},{16,20},{20,16},{24,28},{28,24},{1,5},{5... | collective-permute-start | bytes 1572872 | tf_op jit(solution)/shard_map/ppermute | solution.py:43
  0.5 11.2 %collective-permute-start.5 = (bf16[2048,128]{1,0:T(8,128)(2,1)}, bf16[2048,128]{1,0:T(8,128)(2,1)S(1)}, u32[]{:S(2)}, u32[]{:S(2)}) collective-permute-start(bf16[2048,128]{1,0:T(8,128)(2,1)} %bitcast.24), channel_id=1, source_target_pairs={{0,8},{4,20},{8,0},{12,28},{16,24},{20,4},{24,16},{28,12},{1,9},{5... | collective-permute-start | bytes 1572872 | tf_op jit(solution)/shard_map/ppermute | solution.py:64
  3.5 0.7 %copy-start.5 = (f32[2,2048]{1,0:T(2,128)S(1)}, f32[2,2048]{1,0:T(2,128)}, u32[]{:S(2)}) copy-start(f32[2,2048]{1,0:T(2,128)} %tokens_ref.3) | copy-start | bytes 49156
  4.3 1.1 %collective-permute-start = (f32[2,128]{1,0:T(2,128)S(1)}, f32[2,128]{1,0:T(2,128)S(1)}, u32[]{:S(2)}, u32[]{:S(2)}) collective-permute-start(f32[2,128]{1,0:T(2,128)S(1)} %get-tuple-element.33), channel_id=1, source_target_pairs={{0,4},{4,0},{8,12},{12,8},{16,20},{20,16},{24,28},{28,24},{1,5},{5... | collective-permute-start | bytes 3080 | tf_op jit(solution)/shard_map/ppermute | solution.py:43
  5.4 5.6 %collective-permute-start.3 = (f32[2,128]{1,0:T(2,128)S(1)}, f32[2,128]{1,0:T(2,128)S(1)}, u32[]{:S(2)}, u32[]{:S(2)}) collective-permute-start(f32[2,128]{1,0:T(2,128)S(1)} %add.53), channel_id=1, source_target_pairs={{0,16},{4,12},{8,24},{12,4},{16,0},{20,28},{24,8},{28,20},{1,17},{... | collective-permute-start | bytes 3080 | tf_op jit(solution)/shard_map/ppermute | solution.py:64
  7.0 0.8 %copy-start.4 = (f32[1,16384]{1,0:T(1,128)S(1)}, f32[1,16384]{1,0:T(1,128)}, u32[]{:S(2)}) copy-start(f32[1,16384]{1,0:T(1,128)} %param.11) | copy-start | bytes 196612
  7.8 4.6 %copy-start.3 = (bf16[1,2048,128]{2,1,0:T(8,128)(2,1)S(1)}, bf16[1,2048,128]{2,1,0:T(8,128)(2,1)}, u32[]{:S(2)}) copy-start(bf16[1,2048,128]{2,1,0:T(8,128)(2,1)} %param.14) | copy-start | bytes 1572868
  11.0 1.2 %collective-permute-start.4 = (f32[2,128]{1,0:T(2,128)S(1)}, f32[2,128]{1,0:T(2,128)S(1)}, u32[]{:S(2)}, u32[]{:S(2)}) collective-permute-start(f32[2,128]{1,0:T(2,128)S(1)} %collective-permute-done.3), channel_id=1, source_target_pairs={{0,4},{4,0},{8,12},{12,8},{16,20},{20,16},{24,28},{28,24},{1,5},{5... | collective-permute-start | bytes 3080 | tf_op jit(solution)/shard_map/ppermute | solution.py:43
  11.1 9.3 %collective-permute-start.8 = (bf16[2048,128]{1,0:T(8,128)(2,1)S(1)}, bf16[2048,128]{1,0:T(8,128)(2,1)S(1)}, u32[]{:S(2)}, u32[]{:S(2)}) collective-permute-start(bf16[2048,128]{1,0:T(8,128)(2,1)S(1)} %collective-permute-done.1.refs_6_), channel_id=1, source_target_pairs={{0,8},{4,20},{8,0},{12,28},{16,24},{20,4},{24,16},{28,12},{1,9},{5... | collective-permute-start | bytes 1572872 | tf_op jit(solution)/shard_map/ppermute | solution.py:64
  12.3 8.1 %collective-permute-start.9 = (bf16[2048,128]{1,0:T(8,128)(2,1)S(1)}, bf16[2048,128]{1,0:T(8,128)(2,1)S(1)}, u32[]{:S(2)}, u32[]{:S(2)}) collective-permute-start(bf16[2048,128]{1,0:T(8,128)(2,1)S(1)} %collective-permute-done.5.refs_5_), channel_id=1, source_target_pairs={{0,4},{4,0},{8,12},{12,8},{16,20},{20,16},{24,28},{28,24},{1,5},{5... | collective-permute-start | bytes 1572872 | tf_op jit(solution)/shard_map/ppermute | solution.py:43
  12.4 13.7 %collective-permute-start.6 = (bf16[2048,128]{1,0:T(8,128)(2,1)S(1)}, bf16[2048,128]{1,0:T(8,128)(2,1)S(1)}, u32[]{:S(2)}, u32[]{:S(2)}) collective-permute-start(bf16[2048,128]{1,0:T(8,128)(2,1)S(1)} %bitcast.28), channel_id=1, source_target_pairs={{0,8},{4,20},{8,0},{12,28},{16,24},{20,4},{24,16},{28,12},{1,9},{5... | collective-permute-start | bytes 1572872 | tf_op jit(solution)/shard_map/ppermute | solution.py:64
  13.3 5.4 %collective-permute-start.7 = (f32[2,128]{1,0:T(2,128)S(1)}, f32[2,128]{1,0:T(2,128)S(1)}, u32[]{:S(2)}, u32[]{:S(2)}) collective-permute-start(f32[2,128]{1,0:T(2,128)S(1)} %collective-permute-done.4), channel_id=1, source_target_pairs={{0,16},{4,12},{8,24},{12,4},{16,0},{20,28},{24,8},{28,20},{1,17},{... | collective-permute-start | bytes 3080 | tf_op jit(solution)/shard_map/ppermute | solution.py:64
  14.5 5.9 %copy-start = (bf16[1,2048,1024]{2,1,0:T(8,128)(2,1)S(1)}, bf16[1,2048,1024]{2,1,0:T(8,128)(2,1)}, u32[]{:S(2)}) copy-start(bf16[1,2048,1024]{2,1,0:T(8,128)(2,1)} %param.12) | copy-start | bytes 12582916
  14.5 5.9 %copy-start.2 = (bf16[1,2048,128]{2,1,0:T(8,128)(2,1)S(1)}, bf16[1,2048,128]{2,1,0:T(8,128)(2,1)}, u32[]{:S(2)}) copy-start(bf16[1,2048,128]{2,1,0:T(8,128)(2,1)} %param.13) | copy-start | bytes 1572868
  20.4 6.7 %copy-start.8 = (s32[2]{0:T(128)S(1)}, s32[2]{0:T(128)}, u32[]{:S(2)}) copy-start(s32[2]{0:T(128)} %param.17) | copy-start | bytes 28
  21.2 1.2 %collective-permute-start.10 = (f32[2,10,128]{2,1,0:T(8,128)S(1)}, f32[2,10,128]{2,1,0:T(8,128)S(1)}, u32[]{:S(2)}, u32[]{:S(2)}) collective-permute-start(f32[2,10,128]{2,1,0:T(8,128)S(1)} %query_products.1), channel_id=1, source_target_pairs={{0,4},{4,0},{8,12},{12,8},{16,20},{20,16},{24,28},{28,24},{1,5},{5... | collective-permute-start | bytes 30728 | tf_op jit(solution)/shard_map/ppermute | solution.py:43
  21.4 10.6 %collective-permute-start.14 = (bf16[2048,128]{1,0:T(8,128)(2,1)S(1)}, bf16[2048,128]{1,0:T(8,128)(2,1)S(1)}, u32[]{:S(2)}, u32[]{:S(2)}) collective-permute-start(bf16[2048,128]{1,0:T(8,128)(2,1)S(1)} %collective-permute-done.9.refs_7_), channel_id=1, source_target_pairs={{0,8},{4,20},{8,0},{12,28},{16,24},{20,4},{24,16},{28,12},{1,9},{5... | collective-permute-start | bytes 1572872 | tf_op jit(solution)/shard_map/ppermute | solution.py:64
  22.5 4.0 %collective-permute-start.11 = (f32[2,10,128]{2,1,0:T(8,128)S(1)}, f32[2,10,128]{2,1,0:T(8,128)S(1)}, u32[]{:S(2)}, u32[]{:S(2)}) collective-permute-start(f32[2,10,128]{2,1,0:T(8,128)S(1)} %add.57), channel_id=1, source_target_pairs={{0,16},{4,12},{8,24},{12,4},{16,0},{20,28},{24,8},{28,20},{1,17},{... | collective-permute-start | bytes 30728 | tf_op jit(solution)/shard_map/ppermute | solution.py:64
  26.5 6.4 %collective-permute-start.12 = (bf16[2048,128]{1,0:T(8,128)(2,1)S(1)}, bf16[2048,128]{1,0:T(8,128)(2,1)S(1)}, u32[]{:S(2)}, u32[]{:S(2)}) collective-permute-start(bf16[2048,128]{1,0:T(8,128)(2,1)S(1)} %collective-permute-done.6.refs_5_), channel_id=1, source_target_pairs={{0,4},{4,0},{8,12},{12,8},{16,20},{20,16},{24,28},{28,24},{1,5},{5... | collective-permute-start | bytes 1572872 | tf_op jit(solution)/shard_map/ppermute | solution.py:43
  27.1 1.9 %collective-permute-start.17 = (f32[2,10,128]{2,1,0:T(8,128)S(1)}, f32[2,10,128]{2,1,0:T(8,128)S(1)}, u32[]{:S(2)}, u32[]{:S(2)}) collective-permute-start(f32[2,10,128]{2,1,0:T(8,128)S(1)} %collective-permute-done.11), channel_id=1, source_target_pairs={{0,4},{4,0},{8,12},{12,8},{16,20},{20,16},{24,28},{28,24},{1,5},{5... | collective-permute-start | bytes 30728 | tf_op jit(solution)/shard_map/ppermute | solution.py:43
  27.8 5.5 %collective-permute-start.16 = (bf16[2048,128]{1,0:T(8,128)(2,1)S(1)}, bf16[2048,128]{1,0:T(8,128)(2,1)S(1)}, u32[]{:S(2)}, u32[]{:S(2)}) collective-permute-start(bf16[2048,128]{1,0:T(8,128)(2,1)S(1)} %collective-permute-done.8.refs_6_), channel_id=1, source_target_pairs={{0,4},{4,0},{8,12},{12,8},{16,20},{20,16},{24,28},{28,24},{1,5},{5... | collective-permute-start | bytes 1572872 | tf_op jit(solution)/shard_map/ppermute | solution.py:43
  27.9 10.0 %collective-permute-start.20 = (bf16[2048,128]{1,0:T(8,128)(2,1)S(1)}, bf16[2048,128]{1,0:T(8,128)(2,1)S(1)}, u32[]{:S(2)}, u32[]{:S(2)}) collective-permute-start(bf16[2048,128]{1,0:T(8,128)(2,1)S(1)} %collective-permute-done.2.refs_6_), channel_id=1, source_target_pairs={{0,8},{4,20},{8,0},{12,28},{16,24},{20,4},{24,16},{28,12},{1,9},{5... | collective-permute-start | bytes 1572872 | tf_op jit(solution)/shard_map/ppermute | solution.py:64
  29.0 4.3 %collective-permute-start.18 = (f32[2,10,128]{2,1,0:T(8,128)S(1)}, f32[2,10,128]{2,1,0:T(8,128)S(1)}, u32[]{:S(2)}, u32[]{:S(2)}) collective-permute-start(f32[2,10,128]{2,1,0:T(8,128)S(1)} %collective-permute-done.17), channel_id=1, source_target_pairs={{0,16},{4,12},{8,24},{12,4},{16,0},{20,28},{24,8},{28,20},{1,17},{... | collective-permute-start | bytes 30728 | tf_op jit(solution)/shard_map/ppermute | solution.py:64
  32.0 2.9 %collective-permute-start.15 = (bf16[2048,128]{1,0:T(8,128)(2,1)S(1)}, bf16[2048,128]{1,0:T(8,128)(2,1)S(1)}, u32[]{:S(2)}, u32[]{:S(2)}) collective-permute-start(bf16[2048,128]{1,0:T(8,128)(2,1)S(1)} %collective-permute-done.14.refs_5_), channel_id=1, source_target_pairs={{0,4},{4,0},{8,12},{12,8},{16,20},{20,16},{24,28},{28,24},{1,5},{5... | collective-permute-start | bytes 1572872 | tf_op jit(solution)/shard_map/ppermute | solution.py:43
  32.8 10.4 %collective-permute-start.13 = (bf16[2048,128]{1,0:T(8,128)(2,1)S(1)}, bf16[2048,128]{1,0:T(8,128)(2,1)S(1)}, u32[]{:S(2)}, u32[]{:S(2)}) collective-permute-start(bf16[2048,128]{1,0:T(8,128)(2,1)S(1)} %collective-permute-done.12.refs_7_), channel_id=1, source_target_pairs={{0,8},{4,20},{8,0},{12,28},{16,24},{20,4},{24,16},{28,12},{1,9},{5... | collective-permute-start | bytes 1572872 | tf_op jit(solution)/shard_map/ppermute | solution.py:64
  34.9 0.9 %copy-start.7 = (s32[2]{0:T(128)S(1)}, s32[2]{0:T(128)}, u32[]{:S(2)}) copy-start(s32[2]{0:T(128)} %lengths_ref.3) | copy-start | bytes 28
  36.8 1.2 %collective-permute-start.19 = (f32[8,128]{1,0:T(8,128)S(1)}, f32[8,128]{1,0:T(8,128)S(1)}, u32[]{:S(2)}, u32[]{:S(2)}) collective-permute-start(f32[8,128]{1,0:T(8,128)S(1)} %get-tuple-element.52), channel_id=1, source_target_pairs={{0,4},{4,0},{8,12},{12,8},{16,20},{20,16},{24,28},{28,24},{1,5},{5... | collective-permute-start | bytes 12296 | tf_op jit(solution)/shard_map/ppermute | solution.py:43
  37.9 6.7 %collective-permute-start.23 = (bf16[2048,128]{1,0:T(8,128)(2,1)S(1)}, bf16[2048,128]{1,0:T(8,128)(2,1)S(1)}, u32[]{:S(2)}, u32[]{:S(2)}) collective-permute-start(bf16[2048,128]{1,0:T(8,128)(2,1)S(1)} %collective-permute-done.20.refs_6_), channel_id=1, source_target_pairs={{0,4},{4,0},{8,12},{12,8},{16,20},{20,16},{24,28},{28,24},{1,5},{5... | collective-permute-start | bytes 1572872 | tf_op jit(solution)/shard_map/ppermute | solution.py:43
  38.1 3.7 %collective-permute-start.21 = (f32[8,128]{1,0:T(8,128)S(1)}, f32[8,128]{1,0:T(8,128)S(1)}, u32[]{:S(2)}, u32[]{:S(2)}) collective-permute-start(f32[8,128]{1,0:T(8,128)S(1)} %max.6), channel_id=1, source_target_pairs={{0,16},{4,12},{8,24},{12,4},{16,0},{20,28},{24,8},{28,20},{1,17},{... | collective-permute-start | bytes 12296 | tf_op jit(solution)/shard_map/ppermute | solution.py:64
  43.3 3.5 %collective-permute-start.22 = (bf16[2048,128]{1,0:T(8,128)(2,1)S(1)}, bf16[2048,128]{1,0:T(8,128)(2,1)S(1)}, u32[]{:S(2)}, u32[]{:S(2)}) collective-permute-start(bf16[2048,128]{1,0:T(8,128)(2,1)S(1)} %collective-permute-done.13.refs_5_), channel_id=1, source_target_pairs={{0,4},{4,0},{8,12},{12,8},{16,20},{20,16},{24,28},{28,24},{1,5},{5... | collective-permute-start | bytes 1572872 | tf_op jit(solution)/shard_map/ppermute | solution.py:43
  43.3 2.9 %collective-permute-start.24 = (f32[8,128]{1,0:T(8,128)S(1)}, f32[8,128]{1,0:T(8,128)S(1)}, u32[]{:S(2)}, u32[]{:S(2)}) collective-permute-start(f32[8,128]{1,0:T(8,128)S(1)} %max.7), channel_id=1, source_target_pairs={{0,4},{4,0},{8,12},{12,8},{16,20},{20,16},{24,28},{28,24},{1,5},{5... | collective-permute-start | bytes 12296 | tf_op jit(solution)/shard_map/ppermute | solution.py:43
  46.7 9.7 %copy-start.1 = (bf16[1,1024,2048]{2,1,0:T(8,128)(2,1)S(1)}, bf16[1,1024,2048]{2,1,0:T(8,128)(2,1)}, u32[]{:S(2)}) copy-start(bf16[1,1024,2048]{2,1,0:T(8,128)(2,1)} %param.15) | copy-start | bytes 12582916
  47.9 1.2 %collective-permute-start.25 = (f32[8,256]{1,0:T(8,128)S(1)}, f32[8,256]{1,0:T(8,128)S(1)}, u32[]{:S(2)}, u32[]{:S(2)}) collective-permute-start(f32[8,256]{1,0:T(8,128)S(1)} %weighted_values.1), channel_id=1, source_target_pairs={{0,4},{4,0},{8,12},{12,8},{16,20},{20,16},{24,28},{28,24},{1,5},{5... | collective-permute-start | bytes 24584 | tf_op jit(solution)/shard_map/ppermute | solution.py:43
  49.1 3.7 %collective-permute-start.26 = (f32[8,256]{1,0:T(8,128)S(1)}, f32[8,256]{1,0:T(8,128)S(1)}, u32[]{:S(2)}, u32[]{:S(2)}) collective-permute-start(f32[8,256]{1,0:T(8,128)S(1)} %add.64), channel_id=1, source_target_pairs={{0,8},{4,12},{8,0},{12,4},{16,24},{20,28},{24,16},{28,20},{1,9},{5... | collective-permute-start | bytes 24584 | tf_op jit(solution)/shard_map/ppermute | solution.py:43
  52.8 3.7 %collective-permute-start.27 = (f32[8,256]{1,0:T(8,128)S(1)}, f32[8,256]{1,0:T(8,128)S(1)}, u32[]{:S(2)}, u32[]{:S(2)}) collective-permute-start(f32[8,256]{1,0:T(8,128)S(1)} %add.65.mine_ref), channel_id=1, source_target_pairs={{0,16},{4,20},{8,24},{12,28},{16,0},{20,4},{24,8},{28,12},{1,17},{... | collective-permute-start | bytes 24584 | tf_op jit(solution)/shard_map/ppermute | solution.py:43
  56.4 9.1 %copy-start.6 = (f32[2,2048]{1,0:T(2,128)S(1)}, f32[2,2048]{1,0:T(2,128)}, u32[]{:S(2)}) copy-start(f32[2,2048]{1,0:T(2,128)} %tokens_ref.3) | copy-start | bytes 49156
  57.1 3.8 %collective-permute-start.28 = (f32[2,2048]{1,0:T(2,128)S(1)}, f32[2,2048]{1,0:T(2,128)S(1)}, u32[]{:S(2)}, u32[]{:S(2)}) collective-permute-start(f32[2,2048]{1,0:T(2,128)S(1)} %output_products.1), channel_id=1, source_target_pairs={{0,1},{1,0},{2,3},{3,2},{4,5},{5,4},{6,7},{7,6},{8,9},{9,8},{10,11... | collective-permute-start | bytes 49160 | tf_op jit(solution)/shard_map/ppermute | solution.py:43
  60.8 4.7 %collective-permute-start.29 = (f32[2,2048]{1,0:T(2,128)S(1)}, f32[2,2048]{1,0:T(2,128)S(1)}, u32[]{:S(2)}, u32[]{:S(2)}) collective-permute-start(f32[2,2048]{1,0:T(2,128)S(1)} %add.66), channel_id=1, source_target_pairs={{0,2},{1,3},{2,0},{3,1},{4,6},{5,7},{6,4},{7,5},{8,10},{9,11},{10,... | collective-permute-start | bytes 49160 | tf_op jit(solution)/shard_map/ppermute | solution.py:43

commit v12 on v11

--- a/solution.py
+++ b/solution.py
@@ -400,9 +400,11 @@
         [IN_SMEM] * 2 + [IN_VMEM] * 6,
         (shape((heads, row_count)), shape((heads, LANES)), shape((heads, LANES))),
     )(places, lengths, key_total, cosine, sine_part, new_cosine, new_sine, summed)
-    value_mid = value_far + share(value_far[:1], parts_sent)
-    value_last = send_last(own_values, value_mid[-1:])
-    top = butterfly(top, "ctx", [1], jnp.maximum)
+    value_first = share(value_far[:1], parts_sent)
+    value_last = send_last(own_values, value_first)
+    value_first += value_far[:1]
+    value_total = project(after(places, masked), rows, value_near + value_first)
+    top = butterfly(after(top, value_total), "ctx", [1], jnp.maximum)
     top = after(top, *[block for _, block in value_far[1:]])
     near_top = top
     if split:
@@ -412,9 +414,8 @@
         top = butterfly(top, "ctx", bits_below(team)[1:], jnp.maximum)
         received = top
 
-    value_mid += share(value_far[1:], near_top)
-    value_total = project(after(places, near_top), rows, value_near)
-    value_total = project(places, rows, value_mid, value_total)
+    value_second = value_far[1:] + share(value_far[1:], near_top)
+    value_total = project(places, rows, value_second, value_total)
 
     blocks = share(value_last, received)
     value_total = project(places, rows, value_last, value_total)

time: 66.4 us -> 65.4 us (0.985)
  waiting for transfers between devices: 24.8 us -> 21.8 us
  starting transfers between devices: 20.6 us -> 22.8 us
    ppermute x19, starting transfers between devices: 8 us -> 10.1 us  [swap(): return lax.ppermute(value, axis, [(i, i ^ distance) for i in range(count)])]
    ppermute x19, waiting for transfers between devices: 14.5 us -> 13 us  [swap(): return lax.ppermute(value, axis, [(i, i ^ distance) for i in range(count)])]
    ppermute x11, waiting for transfers between devices: 10.3 us -> 8.79 us  [by_core(): return lax.ppermute(value, 'ctx', pairs)]
where the time goes in v12:
time: 65.4 us; the launch traced here: 65.2 us
  starting transfers between devices  22.8 us (35%)
  waiting for transfers between devices  21.8 us (33%)
  Pallas kernels  17.4 us (27%)
  local copies, waits for them, and re-layouts  1.59 us (2%)
  other arithmetic  1.49 us (2%)
    ppermute x19, waiting for transfers between devices, swap(): return lax.ppermute(value, axis, [(i, i ^ distance) for i in range(count)])  13 us
    ppermute x11, starting transfers between devices, by_core(): return lax.ppermute(value, 'ctx', pairs)  12.6 us
    ppermute x19, starting transfers between devices, swap(): return lax.ppermute(value, axis, [(i, i ^ distance) for i in range(count)])  10.1 us
    ppermute x11, waiting for transfers between devices, by_core(): return lax.ppermute(value, 'ctx', pairs)  8.79 us
    pallas_call x2, Pallas kernels, normalise(): call(functools.partial(norm_kernel, first), 'normalise', [IN_HBM, IN_VMEM...  7.47 us
    pallas_call x6, Pallas kernels, project(): call(functools.partial(project_kernel, [d for d, _ in blocks], len(rows),...  6.17 us
    unnamed x18, local copies, waits for them, and re-layouts  1.59 us
  transfers between devices with their start and end apart: 30, of which 15 were waited for; matrix products, arithmetic and copies ran while one was open for 1% of the time, Pallas kernels for 24%

profile of v12, /device:TPU:0, one launch (start us, length us, event | category | flops | bytes accessed | tf_op | source)
XLA Modules:
  0.0 65.2 jit_solution(8089841029146699739)
XLA Ops:
  0.0 0.5 collective-permute-start.1
  0.5 0.1 collective-permute-start.2
  0.5 2.9 %collective-permute-start.5 = (bf16[2048,128]{1,0:T(8,128)(2,1)}, bf16[2048,128]{1,0:T(8,128)(2,1)S(1)}, u32[]{:S(2)}, u32[]{:S(2)}) collective-permute-start(bf16[2048,128]{1,0:T(8,128)(2,1)} %bitcast.24), channel_id=1, source_target_pairs={{0,8},{4,20},{8,0},{12,28},{16,24},{20,4},{24,16},{28,12},{1,9},{5... | collective-permute-start | bytes 1572872 | tf_op jit(solution)/shard_map/ppermute | solution.py:64
  3.5 0.7 %copy-done.5 = f32[2,2048]{1,0:T(2,128)S(1)} copy-done((f32[2,2048]{1,0:T(2,128)S(1)}, f32[2,2048]{1,0:T(2,128)}, u32[]{:S(2)}) %copy-start.5) | copy-done | bytes 16408
  4.2 0.1 squares.1
  4.3 1.1 %collective-permute-done = f32[2,128]{1,0:T(2,128)S(1)} collective-permute-done((f32[2,128]{1,0:T(2,128)S(1)}, f32[2,128]{1,0:T(2,128)S(1)}, u32[]{:S(2)}, u32[]{:S(2)}) %collective-permute-start) | collective-permute-done | bytes 1056 | tf_op jit(solution)/shard_map/ppermute | solution.py:43
  5.4 1.6 %collective-permute-start.3 = (f32[2,128]{1,0:T(2,128)S(1)}, f32[2,128]{1,0:T(2,128)S(1)}, u32[]{:S(2)}, u32[]{:S(2)}) collective-permute-start(f32[2,128]{1,0:T(2,128)S(1)} %add.53), channel_id=1, source_target_pairs={{0,16},{4,12},{8,24},{12,4},{16,0},{20,28},{24,8},{28,20},{1,17},{... | collective-permute-start | bytes 3080 | tf_op jit(solution)/shard_map/ppermute | solution.py:64
  7.0 0.8 %copy-done.4 = f32[1,16384]{1,0:T(1,128)S(1)} copy-done((f32[1,16384]{1,0:T(1,128)S(1)}, f32[1,16384]{1,0:T(1,128)}, u32[]{:S(2)}) %copy-start.4) | copy-done | bytes 65560
  7.8 3.2 %normalise.2 = (bf16[8,64,2048]{2,1,0:T(8,128)(2,1)S(1)}, bf16[8,64,2048]{2,1,0:T(8,128)(2,1)S(1)}) custom-call(bf16[320,16384]{1,0:T(8,128)(2,1)} %bitcast.35, f32[8,1,2048]{2,1,0:T(1,128)S(1)} %bitcast.31), custom_call_target="tpu_custom_call" | custom-call | flops 1000 | bytes 1000 | tf_op jit(solution)/shard_map/normalise/pallas_call | solution.py:173
  11.0 0.1 collective-permute-start.4
  11.1 0.6 collective-permute-start.8
  11.7 0.5 collective-permute-done.4
  12.3 0.2 collective-permute-start.9
  12.4 0.9 %collective-permute-start.6 = (bf16[2048,128]{1,0:T(8,128)(2,1)S(1)}, bf16[2048,128]{1,0:T(8,128)(2,1)S(1)}, u32[]{:S(2)}, u32[]{:S(2)}) collective-permute-start(bf16[2048,128]{1,0:T(8,128)(2,1)S(1)} %bitcast.28), channel_id=1, source_target_pairs={{0,8},{4,20},{8,0},{12,28},{16,24},{20,4},{24,16},{28,12},{1,9},{5... | collective-permute-start | bytes 1572872 | tf_op jit(solution)/shard_map/ppermute | solution.py:64
  13.3 1.1 %collective-permute-start.7 = (f32[2,128]{1,0:T(2,128)S(1)}, f32[2,128]{1,0:T(2,128)S(1)}, u32[]{:S(2)}, u32[]{:S(2)}) collective-permute-start(f32[2,128]{1,0:T(2,128)S(1)} %collective-permute-done.4), channel_id=1, source_target_pairs={{0,16},{4,12},{8,24},{12,4},{16,0},{20,28},{24,8},{28,20},{1,17},{... | collective-permute-start | bytes 3080 | tf_op jit(solution)/shard_map/ppermute | solution.py:64
  14.5 4.3 %normalise.3 = (bf16[8,64,2048]{2,1,0:T(8,128)(2,1)S(1)}, bf16[8,64,2048]{2,1,0:T(8,128)(2,1)S(1)}, bf16[8,64,2048]{2,1,0:T(8,128)(2,1)S(1)}) custom-call(bf16[320,16384]{1,0:T(8,128)(2,1)} %bitcast.36, f32[8,1,2048]{2,1,0:T(1,128)S(1)} %bitcast.32), custom_call_target="tpu_custom_call" | custom-call | flops 1000 | bytes 1000 | tf_op jit(solution)/shard_map/normalise/pallas_call | solution.py:173
  18.8 1.6 %collective-permute-done.8.refs_6_ = bf16[2048,128]{1,0:T(8,128)(2,1)S(1)} collective-permute-done((bf16[2048,128]{1,0:T(8,128)(2,1)S(1)}, bf16[2048,128]{1,0:T(8,128)(2,1)S(1)}, u32[]{:S(2)}, u32[]{:S(2)}) %collective-permute-start.8) | collective-permute-done | bytes 524320 | tf_op jit(solution)/shard_map/ppermute | solution.py:64
  20.4 0.0 collective-permute-done.9.refs_7_
  20.4 0.0 copy-start.8
  20.4 0.8 %query_products.1 = f32[2,10,128]{2,1,0:T(8,128)S(1)} custom-call(s32[1]{0:T(128)} %bitcast.place_ref, f32[2,128]{1,0:T(2,128)S(1)} %add_add_fusion.2.squares_ref, f32[2,2048]{1,0:T(2,128)S(1)} %copy-done.5, f32[8,1,2048]{2,1,0:T(1,128)S(1)} %bitcast.33, bf16[2048,1024]{1,0:T(8,128)(2,1)S(1)} %bitcast.21, bf16[2048,128]{1,0:T(8,128)(2,1)S(1)} %bitcast.25, ...), custom_call_target="tpu_custom_call" | custom-call | flops 1000 | bytes 1000 | tf_op jit(solution)/shard_map/query_products/pallas_call | solution.py:371
  21.2 0.1 collective-permute-start.10
  21.4 0.6 collective-permute-start.14
  22.0 0.5 collective-permute-done.10
  22.5 0.9 %collective-permute-start.11 = (f32[2,10,128]{2,1,0:T(8,128)S(1)}, f32[2,10,128]{2,1,0:T(8,128)S(1)}, u32[]{:S(2)}, u32[]{:S(2)}) collective-permute-start(f32[2,10,128]{2,1,0:T(8,128)S(1)} %add.57), channel_id=1, source_target_pairs={{0,16},{4,12},{8,24},{12,4},{16,0},{20,28},{24,8},{28,20},{1,17},{... | collective-permute-start | bytes 30728 | tf_op jit(solution)/shard_map/ppermute | solution.py:64
  23.4 2.8 %collective-permute-done.6.refs_8_ = bf16[2048,128]{1,0:T(8,128)(2,1)S(1)} collective-permute-done((bf16[2048,128]{1,0:T(8,128)(2,1)S(1)}, bf16[2048,128]{1,0:T(8,128)(2,1)S(1)}, u32[]{:S(2)}, u32[]{:S(2)}) %collective-permute-start.6) | collective-permute-done | bytes 524320 | tf_op jit(solution)/shard_map/ppermute | solution.py:64
  26.2 0.3 collective-permute-done.11
  26.5 0.6 multiply_sine_fusion
  27.1 0.6 collective-permute-start.17
  27.7 0.1 multiply_sine_fusion.1
  27.8 0.1 collective-permute-start.16
  27.9 1.1 %collective-permute-start.20 = (bf16[2048,128]{1,0:T(8,128)(2,1)S(1)}, bf16[2048,128]{1,0:T(8,128)(2,1)S(1)}, u32[]{:S(2)}, u32[]{:S(2)}) collective-permute-start(bf16[2048,128]{1,0:T(8,128)(2,1)S(1)} %collective-permute-done.2.refs_6_), channel_id=1, source_target_pairs={{0,8},{4,20},{8,0},{12,28},{16,24},{20,4},{24,16},{28,12},{1,9},{5... | collective-permute-start | bytes 1572872 | tf_op jit(solution)/shard_map/ppermute | solution.py:64
  29.0 0.0 collective-permute-done.17
  29.0 0.8 %collective-permute-start.18 = (f32[2,10,128]{2,1,0:T(8,128)S(1)}, f32[2,10,128]{2,1,0:T(8,128)S(1)}, u32[]{:S(2)}, u32[]{:S(2)}) collective-permute-start(f32[2,10,128]{2,1,0:T(8,128)S(1)} %collective-permute-done.17), channel_id=1, source_target_pairs={{0,16},{4,12},{8,24},{12,4},{16,0},{20,28},{24,8},{28,20},{1,17},{... | collective-permute-start | bytes 30728 | tf_op jit(solution)/shard_map/ppermute | solution.py:64
  29.8 2.1 %collective-permute-done.14.refs_5_ = bf16[2048,128]{1,0:T(8,128)(2,1)S(1)} collective-permute-done((bf16[2048,128]{1,0:T(8,128)(2,1)S(1)}, bf16[2048,128]{1,0:T(8,128)(2,1)S(1)}, u32[]{:S(2)}, u32[]{:S(2)}) %collective-permute-start.14) | collective-permute-done | bytes 524320 | tf_op jit(solution)/shard_map/ppermute | solution.py:64
  32.0 0.9 %project.6.refs_9_ = f32[320,128]{1,0:T(8,128)S(1)} custom-call(s32[1]{0:T(128)} %bitcast.place_ref, bf16[8,64,2048]{2,1,0:T(8,128)(2,1)S(1)} %get-tuple-element.37.refs_0_, bf16[8,64,2048]{2,1,0:T(8,128)(2,1)S(1)} %get-tuple-element.38.refs_1_, bf16[8,64,2048]{2,1,0:T(8,128)(2,1)S(1)} %get-tuple-element.41.refs_2_, ...), custom_call_target="tpu_custom_call" | custom-call | flops 1000 | bytes 1000 | tf_op jit(solution)/shard_map/project/pallas_call | solution.py:218
  32.8 0.4 collective-permute-start.13
  33.3 1.5 %project.7.refs_7_ = f32[320,128]{1,0:T(8,128)S(1)} custom-call(s32[1]{0:T(128)} %bitcast.place_ref, bf16[8,64,2048]{2,1,0:T(8,128)(2,1)S(1)} %get-tuple-element.37.refs_0_, bf16[8,64,2048]{2,1,0:T(8,128)(2,1)S(1)} %get-tuple-element.38.refs_1_, bf16[8,64,2048]{2,1,0:T(8,128)(2,1)S(1)} %get-tuple-element.41.refs_2_, ...), custom_call_target="tpu_custom_call" | custom-call | flops 1000 | bytes 1000 | tf_op jit(solution)/shard_map/project/pallas_call | solution.py:218
  34.9 0.0 copy-start.7
  34.9 0.9 %project.8.refs_0_ = f32[320,128]{1,0:T(8,128)S(1)} custom-call(s32[1]{0:T(128)} %bitcast.place_ref, bf16[8,64,2048]{2,1,0:T(8,128)(2,1)S(1)} %get-tuple-element.37.refs_0_, bf16[8,64,2048]{2,1,0:T(8,128)(2,1)S(1)} %get-tuple-element.38.refs_1_, bf16[8,64,2048]{2,1,0:T(8,128)(2,1)S(1)} %get-tuple-element.41.refs_2_, ...), custom_call_target="tpu_custom_call" | custom-call | flops 1000 | bytes 1000 | tf_op jit(solution)/shard_map/project/pallas_call | solution.py:218
  35.8 1.0 %scores.1 = (f32[8,320]{1,0:T(8,128)S(1)}, f32[8,128]{1,0:T(8,128)S(1)}, f32[8,128]{1,0:T(8,128)S(1)}) custom-call(s32[1]{0:T(128)} %bitcast.place_ref, s32[2]{0:T(128)S(1)} %copy-done.7, f32[320,128]{1,0:T(8,128)S(1)} %project.8.refs_0_, f32[320,64]{1,0:T(8,128)S(1)} %get-tuple-element.64.refs_1_, f32[320,64]{1,0:T(8,128)S(1)} %get-tuple-element.63.refs_2_, ...), custom_call_target="tpu_custom_call" | custom-call | flops 1000 | bytes 1000 | tf_op jit(solution)/shard_map/scores/pallas_call | solution.py:397
  36.8 1.5 %project.9.refs_7_ = f32[320,128]{1,0:T(8,128)S(1)} custom-call(s32[1]{0:T(128)} %bitcast.place_ref, bf16[8,64,2048]{2,1,0:T(8,128)(2,1)S(1)} %get-tuple-element.37.refs_0_, bf16[8,64,2048]{2,1,0:T(8,128)(2,1)S(1)} %get-tuple-element.38.refs_1_, bf16[8,64,2048]{2,1,0:T(8,128)(2,1)S(1)} %get-tuple-element.41.refs_2_, ...), custom_call_target="tpu_custom_call" | custom-call | flops 1000 | bytes 1000 | tf_op jit(solution)/shard_map/project/pallas_call | solution.py:218
  38.3 0.3 collective-permute-start.19
  38.6 1.0 %collective-permute-done.19 = f32[8,128]{1,0:T(8,128)S(1)} collective-permute-done((f32[8,128]{1,0:T(8,128)S(1)}, f32[8,128]{1,0:T(8,128)S(1)}, u32[]{:S(2)}, u32[]{:S(2)}) %collective-permute-start.19) | collective-permute-done | bytes 4128 | tf_op jit(solution)/shard_map/ppermute | solution.py:43
  39.6 0.2 collective-permute-start.23
  39.8 1.7 %collective-permute-start.21 = (f32[8,128]{1,0:T(8,128)S(1)}, f32[8,128]{1,0:T(8,128)S(1)}, u32[]{:S(2)}, u32[]{:S(2)}) collective-permute-start(f32[8,128]{1,0:T(8,128)S(1)} %max.6), channel_id=1, source_target_pairs={{0,16},{4,12},{8,24},{12,4},{16,0},{20,28},{24,8},{28,20},{1,17},{... | collective-permute-start | bytes 12296 | tf_op jit(solution)/shard_map/ppermute | solution.py:64
  41.4 1.9 %collective-permute-done.21 = f32[8,128]{1,0:T(8,128)S(1)} collective-permute-done((f32[8,128]{1,0:T(8,128)S(1)}, f32[8,128]{1,0:T(8,128)S(1)}, u32[]{:S(2)}, u32[]{:S(2)}) %collective-permute-start.21) | collective-permute-done | bytes 4128 | tf_op jit(solution)/shard_map/ppermute | solution.py:64
  43.4 0.5 collective-permute-start.24
  43.9 0.9 %project.10.refs_6_ = f32[320,128]{1,0:T(8,128)S(1)} custom-call(s32[1]{0:T(128)} %bitcast.place_ref, bf16[8,64,2048]{2,1,0:T(8,128)(2,1)S(1)} %get-tuple-element.37.refs_0_, bf16[8,64,2048]{2,1,0:T(8,128)(2,1)S(1)} %get-tuple-element.38.refs_1_, bf16[8,64,2048]{2,1,0:T(8,128)(2,1)S(1)} %get-tuple-element.41.refs_2_, ...), custom_call_target="tpu_custom_call" | custom-call | flops 1000 | bytes 1000 | tf_op jit(solution)/shard_map/project/pallas_call | solution.py:218
  44.7 0.5 collective-permute-done.24
  45.3 0.5 project.11.refs_6_
  45.8 0.0 copy-start.1
  45.8 1.2 %weighted_values.1 = f32[8,256]{1,0:T(8,128)S(1)} custom-call(s32[1]{0:T(128)} %bitcast.place_ref, s32[2]{0:T(128)S(1)} %copy-done.7, bf16[8,64,2048]{2,1,0:T(8,128)(2,1)S(1)} %get-tuple-element.37.refs_0_, bf16[8,64,2048]{2,1,0:T(8,128)(2,1)S(1)} %get-tuple-element.38.refs_1_, bf16[8,64,2048]{2,1,0:T(8,128)(2,1)S(1)} %get-tuple-element.41.refs_2_, ...), custom_call_target="tpu_custom_call" | custom-call | flops 1000 | bytes 1000 | tf_op jit(solution)/shard_map/weighted_values/pallas_call | solution.py:422
  47.0 0.1 collective-permute-start.25
  47.1 1.0 %collective-permute-done.25 = f32[8,256]{1,0:T(8,128)S(1)} collective-permute-done((f32[8,256]{1,0:T(8,128)S(1)}, f32[8,256]{1,0:T(8,128)S(1)}, u32[]{:S(2)}, u32[]{:S(2)}) %collective-permute-start.25) | collective-permute-done | bytes 8224 | tf_op jit(solution)/shard_map/ppermute | solution.py:43
  48.2 1.6 %collective-permute-start.26 = (f32[8,256]{1,0:T(8,128)S(1)}, f32[8,256]{1,0:T(8,128)S(1)}, u32[]{:S(2)}, u32[]{:S(2)}) collective-permute-start(f32[8,256]{1,0:T(8,128)S(1)} %add.64), channel_id=1, source_target_pairs={{0,8},{4,12},{8,0},{12,4},{16,24},{20,28},{24,16},{28,20},{1,9},{5... | collective-permute-start | bytes 24584 | tf_op jit(solution)/shard_map/ppermute | solution.py:43
  49.8 2.0 %collective-permute-done.26 = f32[8,256]{1,0:T(8,128)S(1)} collective-permute-done((f32[8,256]{1,0:T(8,128)S(1)}, f32[8,256]{1,0:T(8,128)S(1)}, u32[]{:S(2)}, u32[]{:S(2)}) %collective-permute-start.26) | collective-permute-done | bytes 8224 | tf_op jit(solution)/shard_map/ppermute | solution.py:43
  51.8 1.7 %collective-permute-start.27 = (f32[8,256]{1,0:T(8,128)S(1)}, f32[8,256]{1,0:T(8,128)S(1)}, u32[]{:S(2)}, u32[]{:S(2)}) collective-permute-start(f32[8,256]{1,0:T(8,128)S(1)} %add.65.mine_ref), channel_id=1, source_target_pairs={{0,16},{4,20},{8,24},{12,28},{16,0},{20,4},{24,8},{28,12},{1,17},{... | collective-permute-start | bytes 24584 | tf_op jit(solution)/shard_map/ppermute | solution.py:43
  53.5 2.0 %collective-permute-done.27.other_ref = f32[8,256]{1,0:T(8,128)S(1)} collective-permute-done((f32[8,256]{1,0:T(8,128)S(1)}, f32[8,256]{1,0:T(8,128)S(1)}, u32[]{:S(2)}, u32[]{:S(2)}) %collective-permute-start.27) | collective-permute-done | bytes 8224 | tf_op jit(solution)/shard_map/ppermute | solution.py:43
  55.5 0.6 output_products.1
  56.1 1.6 %collective-permute-start.28 = (f32[2,2048]{1,0:T(2,128)S(1)}, f32[2,2048]{1,0:T(2,128)S(1)}, u32[]{:S(2)}, u32[]{:S(2)}) collective-permute-start(f32[2,2048]{1,0:T(2,128)S(1)} %output_products.1), channel_id=1, source_target_pairs={{0,1},{1,0},{2,3},{3,2},{4,5},{5,4},{6,7},{7,6},{8,9},{9,8},{10,11... | collective-permute-start | bytes 49160 | tf_op jit(solution)/shard_map/ppermute | solution.py:43
  57.7 2.2 %collective-permute-done.28 = f32[2,2048]{1,0:T(2,128)S(1)} collective-permute-done((f32[2,2048]{1,0:T(2,128)S(1)}, f32[2,2048]{1,0:T(2,128)S(1)}, u32[]{:S(2)}, u32[]{:S(2)}) %collective-permute-start.28) | collective-permute-done | bytes 16416 | tf_op jit(solution)/shard_map/ppermute | solution.py:43
  59.9 2.7 %collective-permute-start.29 = (f32[2,2048]{1,0:T(2,128)S(1)}, f32[2,2048]{1,0:T(2,128)S(1)}, u32[]{:S(2)}, u32[]{:S(2)}) collective-permute-start(f32[2,2048]{1,0:T(2,128)S(1)} %add.66), channel_id=1, source_target_pairs={{0,2},{1,3},{2,0},{3,1},{4,6},{5,7},{6,4},{7,5},{8,10},{9,11},{10,... | collective-permute-start | bytes 49160 | tf_op jit(solution)/shard_map/ppermute | solution.py:43
  62.6 2.0 %collective-permute-done.29 = f32[2,2048]{1,0:T(2,128)S(1)} collective-permute-done((f32[2,2048]{1,0:T(2,128)S(1)}, f32[2,2048]{1,0:T(2,128)S(1)}, u32[]{:S(2)}, u32[]{:S(2)}) %collective-permute-start.29) | collective-permute-done | bytes 16416 | tf_op jit(solution)/shard_map/ppermute | solution.py:43
  64.6 0.6 add_add_fusion
  (46 shorter events, 0.2 us)
Async XLA Ops:
  0.0 5.4 %collective-permute-start.1 = (bf16[2048,128]{1,0:T(8,128)(2,1)}, bf16[2048,128]{1,0:T(8,128)(2,1)S(1)}, u32[]{:S(2)}, u32[]{:S(2)}) collective-permute-start(bf16[2048,128]{1,0:T(8,128)(2,1)} %bitcast.23), channel_id=1, source_target_pairs={{0,4},{4,0},{8,12},{12,8},{16,20},{20,16},{24,28},{28,24},{1,5},{5... | collective-permute-start | bytes 1572872 | tf_op jit(solution)/shard_map/ppermute | solution.py:43
  0.5 5.0 %collective-permute-start.2 = (bf16[2048,128]{1,0:T(8,128)(2,1)}, bf16[2048,128]{1,0:T(8,128)(2,1)S(1)}, u32[]{:S(2)}, u32[]{:S(2)}) collective-permute-start(bf16[2048,128]{1,0:T(8,128)(2,1)} %bitcast.27), channel_id=1, source_target_pairs={{0,4},{4,0},{8,12},{12,8},{16,20},{20,16},{24,28},{28,24},{1,5},{5... | collective-permute-start | bytes 1572872 | tf_op jit(solution)/shard_map/ppermute | solution.py:43
  0.5 11.2 %collective-permute-start.5 = (bf16[2048,128]{1,0:T(8,128)(2,1)}, bf16[2048,128]{1,0:T(8,128)(2,1)S(1)}, u32[]{:S(2)}, u32[]{:S(2)}) collective-permute-start(bf16[2048,128]{1,0:T(8,128)(2,1)} %bitcast.24), channel_id=1, source_target_pairs={{0,8},{4,20},{8,0},{12,28},{16,24},{20,4},{24,16},{28,12},{1,9},{5... | collective-permute-start | bytes 1572872 | tf_op jit(solution)/shard_map/ppermute | solution.py:64
  3.5 0.7 %copy-start.5 = (f32[2,2048]{1,0:T(2,128)S(1)}, f32[2,2048]{1,0:T(2,128)}, u32[]{:S(2)}) copy-start(f32[2,2048]{1,0:T(2,128)} %tokens_ref.3) | copy-start | bytes 49156
  4.3 1.1 %collective-permute-start = (f32[2,128]{1,0:T(2,128)S(1)}, f32[2,128]{1,0:T(2,128)S(1)}, u32[]{:S(2)}, u32[]{:S(2)}) collective-permute-start(f32[2,128]{1,0:T(2,128)S(1)} %get-tuple-element.34), channel_id=1, source_target_pairs={{0,4},{4,0},{8,12},{12,8},{16,20},{20,16},{24,28},{28,24},{1,5},{5... | collective-permute-start | bytes 3080 | tf_op jit(solution)/shard_map/ppermute | solution.py:43
  5.4 5.6 %collective-permute-start.3 = (f32[2,128]{1,0:T(2,128)S(1)}, f32[2,128]{1,0:T(2,128)S(1)}, u32[]{:S(2)}, u32[]{:S(2)}) collective-permute-start(f32[2,128]{1,0:T(2,128)S(1)} %add.53), channel_id=1, source_target_pairs={{0,16},{4,12},{8,24},{12,4},{16,0},{20,28},{24,8},{28,20},{1,17},{... | collective-permute-start | bytes 3080 | tf_op jit(solution)/shard_map/ppermute | solution.py:64
  7.0 0.8 %copy-start.4 = (f32[1,16384]{1,0:T(1,128)S(1)}, f32[1,16384]{1,0:T(1,128)}, u32[]{:S(2)}) copy-start(f32[1,16384]{1,0:T(1,128)} %param.11) | copy-start | bytes 196612
  7.8 4.6 %copy-start.3 = (bf16[1,2048,128]{2,1,0:T(8,128)(2,1)S(1)}, bf16[1,2048,128]{2,1,0:T(8,128)(2,1)}, u32[]{:S(2)}) copy-start(bf16[1,2048,128]{2,1,0:T(8,128)(2,1)} %param.14) | copy-start | bytes 1572868
  11.0 1.2 %collective-permute-start.4 = (f32[2,128]{1,0:T(2,128)S(1)}, f32[2,128]{1,0:T(2,128)S(1)}, u32[]{:S(2)}, u32[]{:S(2)}) collective-permute-start(f32[2,128]{1,0:T(2,128)S(1)} %collective-permute-done.3), channel_id=1, source_target_pairs={{0,4},{4,0},{8,12},{12,8},{16,20},{20,16},{24,28},{28,24},{1,5},{5... | collective-permute-start | bytes 3080 | tf_op jit(solution)/shard_map/ppermute | solution.py:43
  11.1 9.3 %collective-permute-start.8 = (bf16[2048,128]{1,0:T(8,128)(2,1)S(1)}, bf16[2048,128]{1,0:T(8,128)(2,1)S(1)}, u32[]{:S(2)}, u32[]{:S(2)}) collective-permute-start(bf16[2048,128]{1,0:T(8,128)(2,1)S(1)} %collective-permute-done.1.refs_6_), channel_id=1, source_target_pairs={{0,8},{4,20},{8,0},{12,28},{16,24},{20,4},{24,16},{28,12},{1,9},{5... | collective-permute-start | bytes 1572872 | tf_op jit(solution)/shard_map/ppermute | solution.py:64
  12.3 8.1 %collective-permute-start.9 = (bf16[2048,128]{1,0:T(8,128)(2,1)S(1)}, bf16[2048,128]{1,0:T(8,128)(2,1)S(1)}, u32[]{:S(2)}, u32[]{:S(2)}) collective-permute-start(bf16[2048,128]{1,0:T(8,128)(2,1)S(1)} %collective-permute-done.5.refs_5_), channel_id=1, source_target_pairs={{0,4},{4,0},{8,12},{12,8},{16,20},{20,16},{24,28},{28,24},{1,5},{5... | collective-permute-start | bytes 1572872 | tf_op jit(solution)/shard_map/ppermute | solution.py:43
  12.4 13.7 %collective-permute-start.6 = (bf16[2048,128]{1,0:T(8,128)(2,1)S(1)}, bf16[2048,128]{1,0:T(8,128)(2,1)S(1)}, u32[]{:S(2)}, u32[]{:S(2)}) collective-permute-start(bf16[2048,128]{1,0:T(8,128)(2,1)S(1)} %bitcast.28), channel_id=1, source_target_pairs={{0,8},{4,20},{8,0},{12,28},{16,24},{20,4},{24,16},{28,12},{1,9},{5... | collective-permute-start | bytes 1572872 | tf_op jit(solution)/shard_map/ppermute | solution.py:64
  13.3 5.4 %collective-permute-start.7 = (f32[2,128]{1,0:T(2,128)S(1)}, f32[2,128]{1,0:T(2,128)S(1)}, u32[]{:S(2)}, u32[]{:S(2)}) collective-permute-start(f32[2,128]{1,0:T(2,128)S(1)} %collective-permute-done.4), channel_id=1, source_target_pairs={{0,16},{4,12},{8,24},{12,4},{16,0},{20,28},{24,8},{28,20},{1,17},{... | collective-permute-start | bytes 3080 | tf_op jit(solution)/shard_map/ppermute | solution.py:64
  14.5 5.9 %copy-start = (bf16[1,2048,1024]{2,1,0:T(8,128)(2,1)S(1)}, bf16[1,2048,1024]{2,1,0:T(8,128)(2,1)}, u32[]{:S(2)}) copy-start(bf16[1,2048,1024]{2,1,0:T(8,128)(2,1)} %param.12) | copy-start | bytes 12582916
  14.5 5.9 %copy-start.2 = (bf16[1,2048,128]{2,1,0:T(8,128)(2,1)S(1)}, bf16[1,2048,128]{2,1,0:T(8,128)(2,1)}, u32[]{:S(2)}) copy-start(bf16[1,2048,128]{2,1,0:T(8,128)(2,1)} %param.13) | copy-start | bytes 1572868
  20.4 6.7 %copy-start.8 = (s32[2]{0:T(128)S(1)}, s32[2]{0:T(128)}, u32[]{:S(2)}) copy-start(s32[2]{0:T(128)} %param.17) | copy-start | bytes 28
  21.2 1.2 %collective-permute-start.10 = (f32[2,10,128]{2,1,0:T(8,128)S(1)}, f32[2,10,128]{2,1,0:T(8,128)S(1)}, u32[]{:S(2)}, u32[]{:S(2)}) collective-permute-start(f32[2,10,128]{2,1,0:T(8,128)S(1)} %query_products.1), channel_id=1, source_target_pairs={{0,4},{4,0},{8,12},{12,8},{16,20},{20,16},{24,28},{28,24},{1,5},{5... | collective-permute-start | bytes 30728 | tf_op jit(solution)/shard_map/ppermute | solution.py:43
  21.4 10.6 %collective-permute-start.14 = (bf16[2048,128]{1,0:T(8,128)(2,1)S(1)}, bf16[2048,128]{1,0:T(8,128)(2,1)S(1)}, u32[]{:S(2)}, u32[]{:S(2)}) collective-permute-start(bf16[2048,128]{1,0:T(8,128)(2,1)S(1)} %collective-permute-done.9.refs_7_), channel_id=1, source_target_pairs={{0,8},{4,20},{8,0},{12,28},{16,24},{20,4},{24,16},{28,12},{1,9},{5... | collective-permute-start | bytes 1572872 | tf_op jit(solution)/shard_map/ppermute | solution.py:64
  22.5 4.0 %collective-permute-start.11 = (f32[2,10,128]{2,1,0:T(8,128)S(1)}, f32[2,10,128]{2,1,0:T(8,128)S(1)}, u32[]{:S(2)}, u32[]{:S(2)}) collective-permute-start(f32[2,10,128]{2,1,0:T(8,128)S(1)} %add.57), channel_id=1, source_target_pairs={{0,16},{4,12},{8,24},{12,4},{16,0},{20,28},{24,8},{28,20},{1,17},{... | collective-permute-start | bytes 30728 | tf_op jit(solution)/shard_map/ppermute | solution.py:64
  26.5 6.4 %collective-permute-start.12 = (bf16[2048,128]{1,0:T(8,128)(2,1)S(1)}, bf16[2048,128]{1,0:T(8,128)(2,1)S(1)}, u32[]{:S(2)}, u32[]{:S(2)}) collective-permute-start(bf16[2048,128]{1,0:T(8,128)(2,1)S(1)} %collective-permute-done.6.refs_8_), channel_id=1, source_target_pairs={{0,4},{4,0},{8,12},{12,8},{16,20},{20,16},{24,28},{28,24},{1,5},{5... | collective-permute-start | bytes 1572872 | tf_op jit(solution)/shard_map/ppermute | solution.py:43
  27.1 1.9 %collective-permute-start.17 = (f32[2,10,128]{2,1,0:T(8,128)S(1)}, f32[2,10,128]{2,1,0:T(8,128)S(1)}, u32[]{:S(2)}, u32[]{:S(2)}) collective-permute-start(f32[2,10,128]{2,1,0:T(8,128)S(1)} %collective-permute-done.11), channel_id=1, source_target_pairs={{0,4},{4,0},{8,12},{12,8},{16,20},{20,16},{24,28},{28,24},{1,5},{5... | collective-permute-start | bytes 30728 | tf_op jit(solution)/shard_map/ppermute | solution.py:43
  27.8 5.5 %collective-permute-start.16 = (bf16[2048,128]{1,0:T(8,128)(2,1)S(1)}, bf16[2048,128]{1,0:T(8,128)(2,1)S(1)}, u32[]{:S(2)}, u32[]{:S(2)}) collective-permute-start(bf16[2048,128]{1,0:T(8,128)(2,1)S(1)} %collective-permute-done.8.refs_6_), channel_id=1, source_target_pairs={{0,4},{4,0},{8,12},{12,8},{16,20},{20,16},{24,28},{28,24},{1,5},{5... | collective-permute-start | bytes 1572872 | tf_op jit(solution)/shard_map/ppermute | solution.py:43
  27.9 11.7 %collective-permute-start.20 = (bf16[2048,128]{1,0:T(8,128)(2,1)S(1)}, bf16[2048,128]{1,0:T(8,128)(2,1)S(1)}, u32[]{:S(2)}, u32[]{:S(2)}) collective-permute-start(bf16[2048,128]{1,0:T(8,128)(2,1)S(1)} %collective-permute-done.2.refs_6_), channel_id=1, source_target_pairs={{0,8},{4,20},{8,0},{12,28},{16,24},{20,4},{24,16},{28,12},{1,9},{5... | collective-permute-start | bytes 1572872 | tf_op jit(solution)/shard_map/ppermute | solution.py:64
  29.0 4.3 %collective-permute-start.18 = (f32[2,10,128]{2,1,0:T(8,128)S(1)}, f32[2,10,128]{2,1,0:T(8,128)S(1)}, u32[]{:S(2)}, u32[]{:S(2)}) collective-permute-start(f32[2,10,128]{2,1,0:T(8,128)S(1)} %collective-permute-done.17), channel_id=1, source_target_pairs={{0,16},{4,12},{8,24},{12,4},{16,0},{20,28},{24,8},{28,20},{1,17},{... | collective-permute-start | bytes 30728 | tf_op jit(solution)/shard_map/ppermute | solution.py:64
  32.0 2.9 %collective-permute-start.15 = (bf16[2048,128]{1,0:T(8,128)(2,1)S(1)}, bf16[2048,128]{1,0:T(8,128)(2,1)S(1)}, u32[]{:S(2)}, u32[]{:S(2)}) collective-permute-start(bf16[2048,128]{1,0:T(8,128)(2,1)S(1)} %collective-permute-done.14.refs_5_), channel_id=1, source_target_pairs={{0,4},{4,0},{8,12},{12,8},{16,20},{20,16},{24,28},{28,24},{1,5},{5... | collective-permute-start | bytes 1572872 | tf_op jit(solution)/shard_map/ppermute | solution.py:43
  32.8 10.5 %collective-permute-start.13 = (bf16[2048,128]{1,0:T(8,128)(2,1)S(1)}, bf16[2048,128]{1,0:T(8,128)(2,1)S(1)}, u32[]{:S(2)}, u32[]{:S(2)}) collective-permute-start(bf16[2048,128]{1,0:T(8,128)(2,1)S(1)} %collective-permute-done.12.refs_7_), channel_id=1, source_target_pairs={{0,8},{4,20},{8,0},{12,28},{16,24},{20,4},{24,16},{28,12},{1,9},{5... | collective-permute-start | bytes 1572872 | tf_op jit(solution)/shard_map/ppermute | solution.py:64
  34.9 0.9 %copy-start.7 = (s32[2]{0:T(128)S(1)}, s32[2]{0:T(128)}, u32[]{:S(2)}) copy-start(s32[2]{0:T(128)} %lengths_ref.3) | copy-start | bytes 28
  38.3 1.2 %collective-permute-start.19 = (f32[8,128]{1,0:T(8,128)S(1)}, f32[8,128]{1,0:T(8,128)S(1)}, u32[]{:S(2)}, u32[]{:S(2)}) collective-permute-start(f32[8,128]{1,0:T(8,128)S(1)} %get-tuple-element.56), channel_id=1, source_target_pairs={{0,4},{4,0},{8,12},{12,8},{16,20},{20,16},{24,28},{28,24},{1,5},{5... | collective-permute-start | bytes 12296 | tf_op jit(solution)/shard_map/ppermute | solution.py:43
  39.6 4.3 %collective-permute-start.23 = (bf16[2048,128]{1,0:T(8,128)(2,1)S(1)}, bf16[2048,128]{1,0:T(8,128)(2,1)S(1)}, u32[]{:S(2)}, u32[]{:S(2)}) collective-permute-start(bf16[2048,128]{1,0:T(8,128)(2,1)S(1)} %collective-permute-done.20.refs_5_), channel_id=1, source_target_pairs={{0,4},{4,0},{8,12},{12,8},{16,20},{20,16},{24,28},{28,24},{1,5},{5... | collective-permute-start | bytes 1572872 | tf_op jit(solution)/shard_map/ppermute | solution.py:43
  39.8 3.6 %collective-permute-start.21 = (f32[8,128]{1,0:T(8,128)S(1)}, f32[8,128]{1,0:T(8,128)S(1)}, u32[]{:S(2)}, u32[]{:S(2)}) collective-permute-start(f32[8,128]{1,0:T(8,128)S(1)} %max.6), channel_id=1, source_target_pairs={{0,16},{4,12},{8,24},{12,4},{16,0},{20,28},{24,8},{28,20},{1,17},{... | collective-permute-start | bytes 12296 | tf_op jit(solution)/shard_map/ppermute | solution.py:64
  43.4 2.4 %collective-permute-start.22 = (bf16[2048,128]{1,0:T(8,128)(2,1)S(1)}, bf16[2048,128]{1,0:T(8,128)(2,1)S(1)}, u32[]{:S(2)}, u32[]{:S(2)}) collective-permute-start(bf16[2048,128]{1,0:T(8,128)(2,1)S(1)} %collective-permute-done.13.refs_5_), channel_id=1, source_target_pairs={{0,4},{4,0},{8,12},{12,8},{16,20},{20,16},{24,28},{28,24},{1,5},{5... | collective-permute-start | bytes 1572872 | tf_op jit(solution)/shard_map/ppermute | solution.py:43
  43.4 1.9 %collective-permute-start.24 = (f32[8,128]{1,0:T(8,128)S(1)}, f32[8,128]{1,0:T(8,128)S(1)}, u32[]{:S(2)}, u32[]{:S(2)}) collective-permute-start(f32[8,128]{1,0:T(8,128)S(1)} %max.7), channel_id=1, source_target_pairs={{0,4},{4,0},{8,12},{12,8},{16,20},{20,16},{24,28},{28,24},{1,5},{5... | collective-permute-start | bytes 12296 | tf_op jit(solution)/shard_map/ppermute | solution.py:43
  45.8 9.7 %copy-start.1 = (bf16[1,1024,2048]{2,1,0:T(8,128)(2,1)S(1)}, bf16[1,1024,2048]{2,1,0:T(8,128)(2,1)}, u32[]{:S(2)}) copy-start(bf16[1,1024,2048]{2,1,0:T(8,128)(2,1)} %param.15) | copy-start | bytes 12582916
  47.0 1.2 %collective-permute-start.25 = (f32[8,256]{1,0:T(8,128)S(1)}, f32[8,256]{1,0:T(8,128)S(1)}, u32[]{:S(2)}, u32[]{:S(2)}) collective-permute-start(f32[8,256]{1,0:T(8,128)S(1)} %weighted_values.1), channel_id=1, source_target_pairs={{0,4},{4,0},{8,12},{12,8},{16,20},{20,16},{24,28},{28,24},{1,5},{5... | collective-permute-start | bytes 24584 | tf_op jit(solution)/shard_map/ppermute | solution.py:43
  48.2 3.7 %collective-permute-start.26 = (f32[8,256]{1,0:T(8,128)S(1)}, f32[8,256]{1,0:T(8,128)S(1)}, u32[]{:S(2)}, u32[]{:S(2)}) collective-permute-start(f32[8,256]{1,0:T(8,128)S(1)} %add.64), channel_id=1, source_target_pairs={{0,8},{4,12},{8,0},{12,4},{16,24},{20,28},{24,16},{28,20},{1,9},{5... | collective-permute-start | bytes 24584 | tf_op jit(solution)/shard_map/ppermute | solution.py:43
  51.8 3.7 %collective-permute-start.27 = (f32[8,256]{1,0:T(8,128)S(1)}, f32[8,256]{1,0:T(8,128)S(1)}, u32[]{:S(2)}, u32[]{:S(2)}) collective-permute-start(f32[8,256]{1,0:T(8,128)S(1)} %add.65.mine_ref), channel_id=1, source_target_pairs={{0,16},{4,20},{8,24},{12,28},{16,0},{20,4},{24,8},{28,12},{1,17},{... | collective-permute-start | bytes 24584 | tf_op jit(solution)/shard_map/ppermute | solution.py:43
  55.5 9.1 %copy-start.6 = (f32[2,2048]{1,0:T(2,128)S(1)}, f32[2,2048]{1,0:T(2,128)}, u32[]{:S(2)}) copy-start(f32[2,2048]{1,0:T(2,128)} %tokens_ref.3) | copy-start | bytes 49156
  56.1 3.8 %collective-permute-start.28 = (f32[2,2048]{1,0:T(2,128)S(1)}, f32[2,2048]{1,0:T(2,128)S(1)}, u32[]{:S(2)}, u32[]{:S(2)}) collective-permute-start(f32[2,2048]{1,0:T(2,128)S(1)} %output_products.1), channel_id=1, source_target_pairs={{0,1},{1,0},{2,3},{3,2},{4,5},{5,4},{6,7},{7,6},{8,9},{9,8},{10,11... | collective-permute-start | bytes 49160 | tf_op jit(solution)/shard_map/ppermute | solution.py:43
  59.9 4.7 %collective-permute-start.29 = (f32[2,2048]{1,0:T(2,128)S(1)}, f32[2,2048]{1,0:T(2,128)S(1)}, u32[]{:S(2)}, u32[]{:S(2)}) collective-permute-start(f32[2,2048]{1,0:T(2,128)S(1)} %add.66), channel_id=1, source_target_pairs={{0,2},{1,3},{2,0},{3,1},{4,6},{5,7},{6,4},{7,5},{8,10},{9,11},{10,... | collective-permute-start | bytes 49160 | tf_op jit(solution)/shard_map/ppermute | solution.py:43

commit v13 on v12

--- a/solution.py
+++ b/solution.py
@@ -359,8 +359,8 @@
     if split:
         squares, told, _ = sum_chips(squares, row_count // NORM_ROWS // 2)
         key_shared = share(key_far, told)
-        own_values = after(value_weight[0], key_far[0][1])
-        squares = after(squares, key_far[1][1], key_shared[0][1])
+        own_values = value_weight[0]
+        squares = after(squares, key_far[1][1])
     else:
         key_shared = share(key_far)
         own_values = value_weight[0]
@@ -376,7 +376,7 @@
     )(places, squares, new_tokens, gains, query_weight[0], key_weight[0], value_weight[0])
     parts = parts + swap(parts, "ctx", 1)
     parts_sent = parts
-    value_far = send_first(own_values, after(value_partner, parts))
+    value_far = send_first(own_values, value_partner)
     if split:
         parts, _, parts_sent = sum_chips(parts)
         summed = jnp.where(own_request == 0, parts[0], parts[1])
@@ -389,7 +389,7 @@
     key_total = project(places, rows, key_near)
     key_total = project(places, rows, key_far + key_shared, key_total)
     key_mid = key_total
-    key_total = project(places, rows, key_last + share(key_last), key_total)
+    key_total = project(places, rows, key_last + share(key_last, key_total), key_total)
 
     within = first_row[0, :1] + jnp.arange(row_count, dtype=jnp.int32)
     cosine, sine_part = tables(within.astype(jnp.float32), head_size)

time: 65.4 us -> 64.4 us (0.985)
  waiting for transfers between devices: 21.8 us -> 20.2 us
    ppermute x11, waiting for transfers between devices: 8.79 us -> 5.8 us  [by_core(): return lax.ppermute(value, 'ctx', pairs)]
    ppermute x19, waiting for transfers between devices: 13 us -> 14.4 us  [swap(): return lax.ppermute(value, axis, [(i, i ^ distance) for i in range(count)])]
    ppermute x11, starting transfers between devices: 12.6 us -> 13.9 us  [by_core(): return lax.ppermute(value, 'ctx', pairs)]
    ppermute x19, starting transfers between devices: 10.1 us -> 9.27 us  [swap(): return lax.ppermute(value, axis, [(i, i ^ distance) for i in range(count)])]
  transfers between devices with their start and end apart: 30 -> 30, of which waited for: 15 -> 13; matrix products, arithmetic and copies ran while one was open for 1% -> 1% of each run, Pallas kernels for 24% -> 24%
where the time goes in v13:
time: 64.4 us; the launch traced here: 64.2 us
  starting transfers between devices  23.2 us (36%)
  waiting for transfers between devices  20.2 us (31%)
  Pallas kernels  17.4 us (27%)
  local copies, waits for them, and re-layouts  1.59 us (2%)
  other arithmetic  1.49 us (2%)
    ppermute x19, waiting for transfers between devices, swap(): return lax.ppermute(value, axis, [(i, i ^ distance) for i in range(count)])  14.4 us
    ppermute x11, starting transfers between devices, by_core(): return lax.ppermute(value, 'ctx', pairs)  13.9 us
    ppermute x19, starting transfers between devices, swap(): return lax.ppermute(value, axis, [(i, i ^ distance) for i in range(count)])  9.27 us
    pallas_call x2, Pallas kernels, normalise(): call(functools.partial(norm_kernel, first), 'normalise', [IN_HBM, IN_VMEM...  7.47 us
    pallas_call x6, Pallas kernels, project(): call(functools.partial(project_kernel, [d for d, _ in blocks], len(rows),...  6.15 us
    ppermute x11, waiting for transfers between devices, by_core(): return lax.ppermute(value, 'ctx', pairs)  5.8 us
    unnamed x18, local copies, waits for them, and re-layouts  1.59 us
  transfers between devices with their start and end apart: 30, of which 13 were waited for; matrix products, arithmetic and copies ran while one was open for 1% of the time, Pallas kernels for 24%

profile of v13, /device:TPU:0, one launch (start us, length us, event | category | flops | bytes accessed | tf_op | source)
XLA Modules:
  0.0 64.2 jit_solution(3255443511876436538)
XLA Ops:
  0.0 0.5 collective-permute-start.1
  0.5 0.1 collective-permute-start.2
  0.5 2.9 %collective-permute-start.12 = (bf16[2048,128]{1,0:T(8,128)(2,1)}, bf16[2048,128]{1,0:T(8,128)(2,1)S(1)}, u32[]{:S(2)}, u32[]{:S(2)}) collective-permute-start(bf16[2048,128]{1,0:T(8,128)(2,1)} %bitcast.24), channel_id=1, source_target_pairs={{0,8},{4,20},{8,0},{12,28},{16,24},{20,4},{24,16},{28,12},{1,9},{5... | collective-permute-start | bytes 1572872 | tf_op jit(solution)/shard_map/ppermute | solution.py:64
  3.5 1.6 %collective-permute-start.7 = (bf16[2048,128]{1,0:T(8,128)(2,1)S(1)}, bf16[2048,128]{1,0:T(8,128)(2,1)S(1)}, u32[]{:S(2)}, u32[]{:S(2)}) collective-permute-start(bf16[2048,128]{1,0:T(8,128)(2,1)S(1)} %collective-permute-done.1.refs_6_), channel_id=1, source_target_pairs={{0,8},{4,20},{8,0},{12,28},{16,24},{20,4},{24,16},{28,12},{1,9},{5... | collective-permute-start | bytes 1572872 | tf_op jit(solution)/shard_map/ppermute | solution.py:64
  5.1 0.7 %copy-done.5 = f32[2,2048]{1,0:T(2,128)S(1)} copy-done((f32[2,2048]{1,0:T(2,128)S(1)}, f32[2,2048]{1,0:T(2,128)}, u32[]{:S(2)}) %copy-start.5) | copy-done | bytes 16408
  5.8 0.1 squares.1
  5.9 0.0 collective-permute-start
  5.9 1.1 %collective-permute-done = f32[2,128]{1,0:T(2,128)S(1)} collective-permute-done((f32[2,128]{1,0:T(2,128)S(1)}, f32[2,128]{1,0:T(2,128)S(1)}, u32[]{:S(2)}, u32[]{:S(2)}) %collective-permute-start) | collective-permute-done | bytes 1056 | tf_op jit(solution)/shard_map/ppermute | solution.py:43
  7.0 0.0 collective-permute-done.2.refs_6_
  7.0 1.5 %collective-permute-start.3 = (f32[2,128]{1,0:T(2,128)S(1)}, f32[2,128]{1,0:T(2,128)S(1)}, u32[]{:S(2)}, u32[]{:S(2)}) collective-permute-start(f32[2,128]{1,0:T(2,128)S(1)} %add.53), channel_id=1, source_target_pairs={{0,16},{4,12},{8,24},{12,4},{16,0},{20,28},{24,8},{28,20},{1,17},{... | collective-permute-start | bytes 3080 | tf_op jit(solution)/shard_map/ppermute | solution.py:64
  8.5 0.8 %copy-done.4 = f32[1,16384]{1,0:T(1,128)S(1)} copy-done((f32[1,16384]{1,0:T(1,128)S(1)}, f32[1,16384]{1,0:T(1,128)}, u32[]{:S(2)}) %copy-start.4) | copy-done | bytes 65560
  9.4 3.2 %normalise.2 = (bf16[8,64,2048]{2,1,0:T(8,128)(2,1)S(1)}, bf16[8,64,2048]{2,1,0:T(8,128)(2,1)S(1)}) custom-call(bf16[320,16384]{1,0:T(8,128)(2,1)} %bitcast.35, f32[8,1,2048]{2,1,0:T(1,128)S(1)} %bitcast.31), custom_call_target="tpu_custom_call" | custom-call | flops 1000 | bytes 1000 | tf_op jit(solution)/shard_map/normalise/pallas_call | solution.py:173
  12.6 0.0 collective-permute-done.3
  12.6 0.1 collective-permute-start.4
  12.7 0.6 collective-permute-start.5
  13.3 0.5 collective-permute-done.4
  13.8 0.2 collective-permute-start.13
  14.0 0.9 %collective-permute-start.6 = (f32[2,128]{1,0:T(2,128)S(1)}, f32[2,128]{1,0:T(2,128)S(1)}, u32[]{:S(2)}, u32[]{:S(2)}) collective-permute-start(f32[2,128]{1,0:T(2,128)S(1)} %collective-permute-done.4), channel_id=1, source_target_pairs={{0,16},{4,12},{8,24},{12,4},{16,0},{20,28},{24,8},{28,20},{1,17},{... | collective-permute-start | bytes 3080 | tf_op jit(solution)/shard_map/ppermute | solution.py:64
  14.9 4.3 %normalise.3 = (bf16[8,64,2048]{2,1,0:T(8,128)(2,1)S(1)}, bf16[8,64,2048]{2,1,0:T(8,128)(2,1)S(1)}, bf16[8,64,2048]{2,1,0:T(8,128)(2,1)S(1)}) custom-call(bf16[320,16384]{1,0:T(8,128)(2,1)} %bitcast.36, f32[8,1,2048]{2,1,0:T(1,128)S(1)} %bitcast.32), custom_call_target="tpu_custom_call" | custom-call | flops 1000 | bytes 1000 | tf_op jit(solution)/shard_map/normalise/pallas_call | solution.py:173
  19.3 0.0 copy-start.8
  19.3 0.8 %query_products.1 = f32[2,10,128]{2,1,0:T(8,128)S(1)} custom-call(s32[1]{0:T(128)} %bitcast.place_ref, f32[2,128]{1,0:T(2,128)S(1)} %add_add_fusion.2.squares_ref, f32[2,2048]{1,0:T(2,128)S(1)} %copy-done.5, f32[8,1,2048]{2,1,0:T(1,128)S(1)} %bitcast.33, bf16[2048,1024]{1,0:T(8,128)(2,1)S(1)} %bitcast.21, bf16[2048,128]{1,0:T(8,128)(2,1)S(1)} %bitcast.25, ...), custom_call_target="tpu_custom_call" | custom-call | flops 1000 | bytes 1000 | tf_op jit(solution)/shard_map/query_products/pallas_call | solution.py:371
  20.1 0.1 collective-permute-start.8
  20.3 0.5 collective-permute-start.15
  20.8 0.8 %collective-permute-start.14 = (bf16[2048,128]{1,0:T(8,128)(2,1)S(1)}, bf16[2048,128]{1,0:T(8,128)(2,1)S(1)}, u32[]{:S(2)}, u32[]{:S(2)}) collective-permute-start(bf16[2048,128]{1,0:T(8,128)(2,1)S(1)} %collective-permute-done.13.refs_7_), channel_id=1, source_target_pairs={{0,8},{4,20},{8,0},{12,28},{16,24},{20,4},{24,16},{28,12},{1,9},{5... | collective-permute-start | bytes 1572872 | tf_op jit(solution)/shard_map/ppermute | solution.py:64
  21.6 1.2 %collective-permute-start.9 = (f32[2,10,128]{2,1,0:T(8,128)S(1)}, f32[2,10,128]{2,1,0:T(8,128)S(1)}, u32[]{:S(2)}, u32[]{:S(2)}) collective-permute-start(f32[2,10,128]{2,1,0:T(8,128)S(1)} %add.57), channel_id=1, source_target_pairs={{0,16},{4,12},{8,24},{12,4},{16,0},{20,28},{24,8},{28,20},{1,17},{... | collective-permute-start | bytes 30728 | tf_op jit(solution)/shard_map/ppermute | solution.py:64
  22.8 2.8 %collective-permute-done.9 = f32[2,10,128]{2,1,0:T(8,128)S(1)} collective-permute-done((f32[2,10,128]{2,1,0:T(8,128)S(1)}, f32[2,10,128]{2,1,0:T(8,128)S(1)}, u32[]{:S(2)}, u32[]{:S(2)}) %collective-permute-start.9) | collective-permute-done | bytes 10272 | tf_op jit(solution)/shard_map/ppermute | solution.py:64
  25.7 0.6 multiply_sine_fusion
  26.3 0.6 collective-permute-start.17
  26.9 0.1 multiply_sine_fusion.1
  27.0 1.3 %collective-permute-start.20 = (bf16[2048,128]{1,0:T(8,128)(2,1)S(1)}, bf16[2048,128]{1,0:T(8,128)(2,1)S(1)}, u32[]{:S(2)}, u32[]{:S(2)}) collective-permute-start(bf16[2048,128]{1,0:T(8,128)(2,1)S(1)} %collective-permute-done.2.refs_6_), channel_id=1, source_target_pairs={{0,8},{4,20},{8,0},{12,28},{16,24},{20,4},{24,16},{28,12},{1,9},{5... | collective-permute-start | bytes 1572872 | tf_op jit(solution)/shard_map/ppermute | solution.py:64
  28.3 0.9 %project.6.refs_9_ = f32[320,128]{1,0:T(8,128)S(1)} custom-call(s32[1]{0:T(128)} %bitcast.place_ref, bf16[8,64,2048]{2,1,0:T(8,128)(2,1)S(1)} %get-tuple-element.36.refs_0_, bf16[8,64,2048]{2,1,0:T(8,128)(2,1)S(1)} %get-tuple-element.37.refs_1_, bf16[8,64,2048]{2,1,0:T(8,128)(2,1)S(1)} %get-tuple-element.40.refs_2_, ...), custom_call_target="tpu_custom_call" | custom-call | flops 1000 | bytes 1000 | tf_op jit(solution)/shard_map/project/pallas_call | solution.py:218
  29.2 1.2 %collective-permute-start.18 = (f32[2,10,128]{2,1,0:T(8,128)S(1)}, f32[2,10,128]{2,1,0:T(8,128)S(1)}, u32[]{:S(2)}, u32[]{:S(2)}) collective-permute-start(f32[2,10,128]{2,1,0:T(8,128)S(1)} %collective-permute-done.17), channel_id=1, source_target_pairs={{0,16},{4,12},{8,24},{12,4},{16,0},{20,28},{24,8},{28,20},{1,17},{... | collective-permute-start | bytes 30728 | tf_op jit(solution)/shard_map/ppermute | solution.py:64
  30.3 1.5 %project.7.refs_7_ = f32[320,128]{1,0:T(8,128)S(1)} custom-call(s32[1]{0:T(128)} %bitcast.place_ref, bf16[8,64,2048]{2,1,0:T(8,128)(2,1)S(1)} %get-tuple-element.36.refs_0_, bf16[8,64,2048]{2,1,0:T(8,128)(2,1)S(1)} %get-tuple-element.37.refs_1_, bf16[8,64,2048]{2,1,0:T(8,128)(2,1)S(1)} %get-tuple-element.40.refs_2_, ...), custom_call_target="tpu_custom_call" | custom-call | flops 1000 | bytes 1000 | tf_op jit(solution)/shard_map/project/pallas_call | solution.py:218
  31.9 0.1 collective-permute-start.16
  32.0 0.9 %collective-permute-start.11 = (bf16[2048,128]{1,0:T(8,128)(2,1)S(1)}, bf16[2048,128]{1,0:T(8,128)(2,1)S(1)}, u32[]{:S(2)}, u32[]{:S(2)}) collective-permute-start(bf16[2048,128]{1,0:T(8,128)(2,1)S(1)} %collective-permute-done.10.refs_7_), channel_id=1, source_target_pairs={{0,8},{4,20},{8,0},{12,28},{16,24},{20,4},{24,16},{28,12},{1,9},{5... | collective-permute-start | bytes 1572872 | tf_op jit(solution)/shard_map/ppermute | solution.py:64
  32.9 0.3 collective-permute-done.18
  33.2 0.0 copy-start.7
  33.2 0.6 collective-permute-done.16.refs_6_
  33.9 0.9 %project.8.refs_0_ = f32[320,128]{1,0:T(8,128)S(1)} custom-call(s32[1]{0:T(128)} %bitcast.place_ref, bf16[8,64,2048]{2,1,0:T(8,128)(2,1)S(1)} %get-tuple-element.36.refs_0_, bf16[8,64,2048]{2,1,0:T(8,128)(2,1)S(1)} %get-tuple-element.37.refs_1_, bf16[8,64,2048]{2,1,0:T(8,128)(2,1)S(1)} %get-tuple-element.40.refs_2_, ...), custom_call_target="tpu_custom_call" | custom-call | flops 1000 | bytes 1000 | tf_op jit(solution)/shard_map/project/pallas_call | solution.py:218
  34.7 1.0 %scores.1 = (f32[8,320]{1,0:T(8,128)S(1)}, f32[8,128]{1,0:T(8,128)S(1)}, f32[8,128]{1,0:T(8,128)S(1)}) custom-call(s32[1]{0:T(128)} %bitcast.place_ref, s32[2]{0:T(128)S(1)} %copy-done.7, f32[320,128]{1,0:T(8,128)S(1)} %project.8.refs_0_, f32[320,64]{1,0:T(8,128)S(1)} %get-tuple-element.62.refs_1_, f32[320,64]{1,0:T(8,128)S(1)} %get-tuple-element.61.refs_2_, ...), custom_call_target="tpu_custom_call" | custom-call | flops 1000 | bytes 1000 | tf_op jit(solution)/shard_map/scores/pallas_call | solution.py:397
  35.7 1.5 %project.9.refs_7_ = f32[320,128]{1,0:T(8,128)S(1)} custom-call(s32[1]{0:T(128)} %bitcast.place_ref, bf16[8,64,2048]{2,1,0:T(8,128)(2,1)S(1)} %get-tuple-element.36.refs_0_, bf16[8,64,2048]{2,1,0:T(8,128)(2,1)S(1)} %get-tuple-element.37.refs_1_, bf16[8,64,2048]{2,1,0:T(8,128)(2,1)S(1)} %get-tuple-element.40.refs_2_, ...), custom_call_target="tpu_custom_call" | custom-call | flops 1000 | bytes 1000 | tf_op jit(solution)/shard_map/project/pallas_call | solution.py:218
  37.3 0.2 collective-permute-start.19
  37.5 1.0 %collective-permute-done.19 = f32[8,128]{1,0:T(8,128)S(1)} collective-permute-done((f32[8,128]{1,0:T(8,128)S(1)}, f32[8,128]{1,0:T(8,128)S(1)}, u32[]{:S(2)}, u32[]{:S(2)}) %collective-permute-start.19) | collective-permute-done | bytes 4128 | tf_op jit(solution)/shard_map/ppermute | solution.py:43
  38.5 0.2 collective-permute-start.23
  38.7 0.9 %collective-permute-start.21 = (f32[8,128]{1,0:T(8,128)S(1)}, f32[8,128]{1,0:T(8,128)S(1)}, u32[]{:S(2)}, u32[]{:S(2)}) collective-permute-start(f32[8,128]{1,0:T(8,128)S(1)} %max.6), channel_id=1, source_target_pairs={{0,16},{4,12},{8,24},{12,4},{16,0},{20,28},{24,8},{28,20},{1,17},{... | collective-permute-start | bytes 12296 | tf_op jit(solution)/shard_map/ppermute | solution.py:64
  39.6 2.7 %collective-permute-done.21 = f32[8,128]{1,0:T(8,128)S(1)} collective-permute-done((f32[8,128]{1,0:T(8,128)S(1)}, f32[8,128]{1,0:T(8,128)S(1)}, u32[]{:S(2)}, u32[]{:S(2)}) %collective-permute-start.21) | collective-permute-done | bytes 4128 | tf_op jit(solution)/shard_map/ppermute | solution.py:64
  42.3 0.5 collective-permute-start.24
  42.8 0.9 %project.10.refs_6_ = f32[320,128]{1,0:T(8,128)S(1)} custom-call(s32[1]{0:T(128)} %bitcast.place_ref, bf16[8,64,2048]{2,1,0:T(8,128)(2,1)S(1)} %get-tuple-element.36.refs_0_, bf16[8,64,2048]{2,1,0:T(8,128)(2,1)S(1)} %get-tuple-element.37.refs_1_, bf16[8,64,2048]{2,1,0:T(8,128)(2,1)S(1)} %get-tuple-element.40.refs_2_, ...), custom_call_target="tpu_custom_call" | custom-call | flops 1000 | bytes 1000 | tf_op jit(solution)/shard_map/project/pallas_call | solution.py:218
  43.7 0.5 collective-permute-done.24
  44.2 0.5 project.11.refs_6_
  44.7 0.0 copy-start.1
  44.8 1.2 %weighted_values.1 = f32[8,256]{1,0:T(8,128)S(1)} custom-call(s32[1]{0:T(128)} %bitcast.place_ref, s32[2]{0:T(128)S(1)} %copy-done.7, bf16[8,64,2048]{2,1,0:T(8,128)(2,1)S(1)} %get-tuple-element.36.refs_0_, bf16[8,64,2048]{2,1,0:T(8,128)(2,1)S(1)} %get-tuple-element.37.refs_1_, bf16[8,64,2048]{2,1,0:T(8,128)(2,1)S(1)} %get-tuple-element.40.refs_2_, ...), custom_call_target="tpu_custom_call" | custom-call | flops 1000 | bytes 1000 | tf_op jit(solution)/shard_map/weighted_values/pallas_call | solution.py:422
  45.9 0.1 collective-permute-start.25
  46.1 1.0 %collective-permute-done.25 = f32[8,256]{1,0:T(8,128)S(1)} collective-permute-done((f32[8,256]{1,0:T(8,128)S(1)}, f32[8,256]{1,0:T(8,128)S(1)}, u32[]{:S(2)}, u32[]{:S(2)}) %collective-permute-start.25) | collective-permute-done | bytes 8224 | tf_op jit(solution)/shard_map/ppermute | solution.py:43
  47.1 1.0 %collective-permute-start.26 = (f32[8,256]{1,0:T(8,128)S(1)}, f32[8,256]{1,0:T(8,128)S(1)}, u32[]{:S(2)}, u32[]{:S(2)}) collective-permute-start(f32[8,256]{1,0:T(8,128)S(1)} %add.64), channel_id=1, source_target_pairs={{0,8},{4,12},{8,0},{12,4},{16,24},{20,28},{24,16},{28,20},{1,9},{5... | collective-permute-start | bytes 24584 | tf_op jit(solution)/shard_map/ppermute | solution.py:43
  48.1 2.6 %collective-permute-done.26 = f32[8,256]{1,0:T(8,128)S(1)} collective-permute-done((f32[8,256]{1,0:T(8,128)S(1)}, f32[8,256]{1,0:T(8,128)S(1)}, u32[]{:S(2)}, u32[]{:S(2)}) %collective-permute-start.26) | collective-permute-done | bytes 8224 | tf_op jit(solution)/shard_map/ppermute | solution.py:43
  50.8 0.9 %collective-permute-start.27 = (f32[8,256]{1,0:T(8,128)S(1)}, f32[8,256]{1,0:T(8,128)S(1)}, u32[]{:S(2)}, u32[]{:S(2)}) collective-permute-start(f32[8,256]{1,0:T(8,128)S(1)} %add.65.mine_ref), channel_id=1, source_target_pairs={{0,16},{4,20},{8,24},{12,28},{16,0},{20,4},{24,8},{28,12},{1,17},{... | collective-permute-start | bytes 24584 | tf_op jit(solution)/shard_map/ppermute | solution.py:43
  51.7 2.7 %collective-permute-done.27.other_ref = f32[8,256]{1,0:T(8,128)S(1)} collective-permute-done((f32[8,256]{1,0:T(8,128)S(1)}, f32[8,256]{1,0:T(8,128)S(1)}, u32[]{:S(2)}, u32[]{:S(2)}) %collective-permute-start.27) | collective-permute-done | bytes 8224 | tf_op jit(solution)/shard_map/ppermute | solution.py:43
  54.4 0.6 %output_products.1 = f32[2,2048]{1,0:T(2,128)S(1)} custom-call(s32[1]{0:T(128)} %bitcast.place_ref, f32[8,256]{1,0:T(8,128)S(1)} %add.65.mine_ref, f32[8,256]{1,0:T(8,128)S(1)} %collective-permute-done.27.other_ref, bf16[1024,2048]{1,0:T(8,128)(2,1)S(1)} %bitcast.22), custom_call_target="tpu_custom_call" | custom-call | flops 1000 | bytes 1000 | tf_op jit(solution)/shard_map/output_products/pallas_call | solution.py:440
  55.1 1.6 %collective-permute-start.28 = (f32[2,2048]{1,0:T(2,128)S(1)}, f32[2,2048]{1,0:T(2,128)S(1)}, u32[]{:S(2)}, u32[]{:S(2)}) collective-permute-start(f32[2,2048]{1,0:T(2,128)S(1)} %output_products.1), channel_id=1, source_target_pairs={{0,1},{1,0},{2,3},{3,2},{4,5},{5,4},{6,7},{7,6},{8,9},{9,8},{10,11... | collective-permute-start | bytes 49160 | tf_op jit(solution)/shard_map/ppermute | solution.py:43
  56.7 2.2 %collective-permute-done.28 = f32[2,2048]{1,0:T(2,128)S(1)} collective-permute-done((f32[2,2048]{1,0:T(2,128)S(1)}, f32[2,2048]{1,0:T(2,128)S(1)}, u32[]{:S(2)}, u32[]{:S(2)}) %collective-permute-start.28) | collective-permute-done | bytes 16416 | tf_op jit(solution)/shard_map/ppermute | solution.py:43
  58.8 2.7 %collective-permute-start.29 = (f32[2,2048]{1,0:T(2,128)S(1)}, f32[2,2048]{1,0:T(2,128)S(1)}, u32[]{:S(2)}, u32[]{:S(2)}) collective-permute-start(f32[2,2048]{1,0:T(2,128)S(1)} %add.66), channel_id=1, source_target_pairs={{0,2},{1,3},{2,0},{3,1},{4,6},{5,7},{6,4},{7,5},{8,10},{9,11},{10,... | collective-permute-start | bytes 49160 | tf_op jit(solution)/shard_map/ppermute | solution.py:43
  61.5 2.1 %collective-permute-done.29 = f32[2,2048]{1,0:T(2,128)S(1)} collective-permute-done((f32[2,2048]{1,0:T(2,128)S(1)}, f32[2,2048]{1,0:T(2,128)S(1)}, u32[]{:S(2)}, u32[]{:S(2)}) %collective-permute-start.29) | collective-permute-done | bytes 16416 | tf_op jit(solution)/shard_map/ppermute | solution.py:43
  63.5 0.6 add_add_fusion
  (46 shorter events, 0.2 us)
Async XLA Ops:
  0.0 3.5 %collective-permute-start.1 = (bf16[2048,128]{1,0:T(8,128)(2,1)}, bf16[2048,128]{1,0:T(8,128)(2,1)S(1)}, u32[]{:S(2)}, u32[]{:S(2)}) collective-permute-start(bf16[2048,128]{1,0:T(8,128)(2,1)} %bitcast.23), channel_id=1, source_target_pairs={{0,4},{4,0},{8,12},{12,8},{16,20},{20,16},{24,28},{28,24},{1,5},{5... | collective-permute-start | bytes 1572872 | tf_op jit(solution)/shard_map/ppermute | solution.py:43
  0.5 6.6 %collective-permute-start.2 = (bf16[2048,128]{1,0:T(8,128)(2,1)}, bf16[2048,128]{1,0:T(8,128)(2,1)S(1)}, u32[]{:S(2)}, u32[]{:S(2)}) collective-permute-start(bf16[2048,128]{1,0:T(8,128)(2,1)} %bitcast.27), channel_id=1, source_target_pairs={{0,4},{4,0},{8,12},{12,8},{16,20},{20,16},{24,28},{28,24},{1,5},{5... | collective-permute-start | bytes 1572872 | tf_op jit(solution)/shard_map/ppermute | solution.py:43
  0.5 12.8 %collective-permute-start.12 = (bf16[2048,128]{1,0:T(8,128)(2,1)}, bf16[2048,128]{1,0:T(8,128)(2,1)S(1)}, u32[]{:S(2)}, u32[]{:S(2)}) collective-permute-start(bf16[2048,128]{1,0:T(8,128)(2,1)} %bitcast.24), channel_id=1, source_target_pairs={{0,8},{4,20},{8,0},{12,28},{16,24},{20,4},{24,16},{28,12},{1,9},{5... | collective-permute-start | bytes 1572872 | tf_op jit(solution)/shard_map/ppermute | solution.py:64
  3.5 15.8 %collective-permute-start.7 = (bf16[2048,128]{1,0:T(8,128)(2,1)S(1)}, bf16[2048,128]{1,0:T(8,128)(2,1)S(1)}, u32[]{:S(2)}, u32[]{:S(2)}) collective-permute-start(bf16[2048,128]{1,0:T(8,128)(2,1)S(1)} %collective-permute-done.1.refs_6_), channel_id=1, source_target_pairs={{0,8},{4,20},{8,0},{12,28},{16,24},{20,4},{24,16},{28,12},{1,9},{5... | collective-permute-start | bytes 1572872 | tf_op jit(solution)/shard_map/ppermute | solution.py:64
  5.1 0.7 %copy-start.5 = (f32[2,2048]{1,0:T(2,128)S(1)}, f32[2,2048]{1,0:T(2,128)}, u32[]{:S(2)}) copy-start(f32[2,2048]{1,0:T(2,128)} %tokens_ref.3) | copy-start | bytes 49156
  5.9 1.1 %collective-permute-start = (f32[2,128]{1,0:T(2,128)S(1)}, f32[2,128]{1,0:T(2,128)S(1)}, u32[]{:S(2)}, u32[]{:S(2)}) collective-permute-start(f32[2,128]{1,0:T(2,128)S(1)} %get-tuple-element.33), channel_id=1, source_target_pairs={{0,4},{4,0},{8,12},{12,8},{16,20},{20,16},{24,28},{28,24},{1,5},{5... | collective-permute-start | bytes 3080 | tf_op jit(solution)/shard_map/ppermute | solution.py:43
  7.0 5.6 %collective-permute-start.3 = (f32[2,128]{1,0:T(2,128)S(1)}, f32[2,128]{1,0:T(2,128)S(1)}, u32[]{:S(2)}, u32[]{:S(2)}) collective-permute-start(f32[2,128]{1,0:T(2,128)S(1)} %add.53), channel_id=1, source_target_pairs={{0,16},{4,12},{8,24},{12,4},{16,0},{20,28},{24,8},{28,20},{1,17},{... | collective-permute-start | bytes 3080 | tf_op jit(solution)/shard_map/ppermute | solution.py:64
  8.5 0.8 %copy-start.4 = (f32[1,16384]{1,0:T(1,128)S(1)}, f32[1,16384]{1,0:T(1,128)}, u32[]{:S(2)}) copy-start(f32[1,16384]{1,0:T(1,128)} %param.11) | copy-start | bytes 196612
  9.4 3.3 %copy-start.3 = (bf16[1,2048,128]{2,1,0:T(8,128)(2,1)S(1)}, bf16[1,2048,128]{2,1,0:T(8,128)(2,1)}, u32[]{:S(2)}) copy-start(bf16[1,2048,128]{2,1,0:T(8,128)(2,1)} %param.14) | copy-start | bytes 1572868
  12.6 1.2 %collective-permute-start.4 = (f32[2,128]{1,0:T(2,128)S(1)}, f32[2,128]{1,0:T(2,128)S(1)}, u32[]{:S(2)}, u32[]{:S(2)}) collective-permute-start(f32[2,128]{1,0:T(2,128)S(1)} %collective-permute-done.3), channel_id=1, source_target_pairs={{0,4},{4,0},{8,12},{12,8},{16,20},{20,16},{24,28},{28,24},{1,5},{5... | collective-permute-start | bytes 3080 | tf_op jit(solution)/shard_map/ppermute | solution.py:43
  12.7 10.2 %collective-permute-start.5 = (bf16[2048,128]{1,0:T(8,128)(2,1)S(1)}, bf16[2048,128]{1,0:T(8,128)(2,1)S(1)}, u32[]{:S(2)}, u32[]{:S(2)}) collective-permute-start(bf16[2048,128]{1,0:T(8,128)(2,1)S(1)} %bitcast.28), channel_id=1, source_target_pairs={{0,8},{4,20},{8,0},{12,28},{16,24},{20,4},{24,16},{28,12},{1,9},{5... | collective-permute-start | bytes 1572872 | tf_op jit(solution)/shard_map/ppermute | solution.py:64
  13.8 7.0 %collective-permute-start.13 = (bf16[2048,128]{1,0:T(8,128)(2,1)S(1)}, bf16[2048,128]{1,0:T(8,128)(2,1)S(1)}, u32[]{:S(2)}, u32[]{:S(2)}) collective-permute-start(bf16[2048,128]{1,0:T(8,128)(2,1)S(1)} %collective-permute-done.12.refs_5_), channel_id=1, source_target_pairs={{0,4},{4,0},{8,12},{12,8},{16,20},{20,16},{24,28},{28,24},{1,5},{5... | collective-permute-start | bytes 1572872 | tf_op jit(solution)/shard_map/ppermute | solution.py:43
  14.0 5.2 %collective-permute-start.6 = (f32[2,128]{1,0:T(2,128)S(1)}, f32[2,128]{1,0:T(2,128)S(1)}, u32[]{:S(2)}, u32[]{:S(2)}) collective-permute-start(f32[2,128]{1,0:T(2,128)S(1)} %collective-permute-done.4), channel_id=1, source_target_pairs={{0,16},{4,12},{8,24},{12,4},{16,0},{20,28},{24,8},{28,20},{1,17},{... | collective-permute-start | bytes 3080 | tf_op jit(solution)/shard_map/ppermute | solution.py:64
  14.9 4.3 %copy-start = (bf16[1,2048,1024]{2,1,0:T(8,128)(2,1)S(1)}, bf16[1,2048,1024]{2,1,0:T(8,128)(2,1)}, u32[]{:S(2)}) copy-start(bf16[1,2048,1024]{2,1,0:T(8,128)(2,1)} %param.12) | copy-start | bytes 12582916
  14.9 4.3 %copy-start.2 = (bf16[1,2048,128]{2,1,0:T(8,128)(2,1)S(1)}, bf16[1,2048,128]{2,1,0:T(8,128)(2,1)}, u32[]{:S(2)}) copy-start(bf16[1,2048,128]{2,1,0:T(8,128)(2,1)} %param.13) | copy-start | bytes 1572868
  19.3 7.0 %copy-start.8 = (s32[2]{0:T(128)S(1)}, s32[2]{0:T(128)}, u32[]{:S(2)}) copy-start(s32[2]{0:T(128)} %param.17) | copy-start | bytes 28
  20.1 1.5 %collective-permute-start.8 = (f32[2,10,128]{2,1,0:T(8,128)S(1)}, f32[2,10,128]{2,1,0:T(8,128)S(1)}, u32[]{:S(2)}, u32[]{:S(2)}) collective-permute-start(f32[2,10,128]{2,1,0:T(8,128)S(1)} %query_products.1), channel_id=1, source_target_pairs={{0,4},{4,0},{8,12},{12,8},{16,20},{20,16},{24,28},{28,24},{1,5},{5... | collective-permute-start | bytes 30728 | tf_op jit(solution)/shard_map/ppermute | solution.py:43
  20.3 10.0 %collective-permute-start.15 = (bf16[2048,128]{1,0:T(8,128)(2,1)S(1)}, bf16[2048,128]{1,0:T(8,128)(2,1)S(1)}, u32[]{:S(2)}, u32[]{:S(2)}) collective-permute-start(bf16[2048,128]{1,0:T(8,128)(2,1)S(1)} %collective-permute-done.7.refs_6_), channel_id=1, source_target_pairs={{0,4},{4,0},{8,12},{12,8},{16,20},{20,16},{24,28},{28,24},{1,5},{5... | collective-permute-start | bytes 1572872 | tf_op jit(solution)/shard_map/ppermute | solution.py:43
  20.8 11.1 %collective-permute-start.14 = (bf16[2048,128]{1,0:T(8,128)(2,1)S(1)}, bf16[2048,128]{1,0:T(8,128)(2,1)S(1)}, u32[]{:S(2)}, u32[]{:S(2)}) collective-permute-start(bf16[2048,128]{1,0:T(8,128)(2,1)S(1)} %collective-permute-done.13.refs_7_), channel_id=1, source_target_pairs={{0,8},{4,20},{8,0},{12,28},{16,24},{20,4},{24,16},{28,12},{1,9},{5... | collective-permute-start | bytes 1572872 | tf_op jit(solution)/shard_map/ppermute | solution.py:64
  21.6 4.0 %collective-permute-start.9 = (f32[2,10,128]{2,1,0:T(8,128)S(1)}, f32[2,10,128]{2,1,0:T(8,128)S(1)}, u32[]{:S(2)}, u32[]{:S(2)}) collective-permute-start(f32[2,10,128]{2,1,0:T(8,128)S(1)} %add.57), channel_id=1, source_target_pairs={{0,16},{4,12},{8,24},{12,4},{16,0},{20,28},{24,8},{28,20},{1,17},{... | collective-permute-start | bytes 30728 | tf_op jit(solution)/shard_map/ppermute | solution.py:64
  25.7 6.3 %collective-permute-start.10 = (bf16[2048,128]{1,0:T(8,128)(2,1)S(1)}, bf16[2048,128]{1,0:T(8,128)(2,1)S(1)}, u32[]{:S(2)}, u32[]{:S(2)}) collective-permute-start(bf16[2048,128]{1,0:T(8,128)(2,1)S(1)} %collective-permute-done.5.refs_8_), channel_id=1, source_target_pairs={{0,4},{4,0},{8,12},{12,8},{16,20},{20,16},{24,28},{28,24},{1,5},{5... | collective-permute-start | bytes 1572872 | tf_op jit(solution)/shard_map/ppermute | solution.py:43
  26.3 2.8 %collective-permute-start.17 = (f32[2,10,128]{2,1,0:T(8,128)S(1)}, f32[2,10,128]{2,1,0:T(8,128)S(1)}, u32[]{:S(2)}, u32[]{:S(2)}) collective-permute-start(f32[2,10,128]{2,1,0:T(8,128)S(1)} %collective-permute-done.9), channel_id=1, source_target_pairs={{0,4},{4,0},{8,12},{12,8},{16,20},{20,16},{24,28},{28,24},{1,5},{5... | collective-permute-start | bytes 30728 | tf_op jit(solution)/shard_map/ppermute | solution.py:43
  27.0 11.5 %collective-permute-start.20 = (bf16[2048,128]{1,0:T(8,128)(2,1)S(1)}, bf16[2048,128]{1,0:T(8,128)(2,1)S(1)}, u32[]{:S(2)}, u32[]{:S(2)}) collective-permute-start(bf16[2048,128]{1,0:T(8,128)(2,1)S(1)} %collective-permute-done.2.refs_6_), channel_id=1, source_target_pairs={{0,8},{4,20},{8,0},{12,28},{16,24},{20,4},{24,16},{28,12},{1,9},{5... | collective-permute-start | bytes 1572872 | tf_op jit(solution)/shard_map/ppermute | solution.py:64
  29.2 4.0 %collective-permute-start.18 = (f32[2,10,128]{2,1,0:T(8,128)S(1)}, f32[2,10,128]{2,1,0:T(8,128)S(1)}, u32[]{:S(2)}, u32[]{:S(2)}) collective-permute-start(f32[2,10,128]{2,1,0:T(8,128)S(1)} %collective-permute-done.17), channel_id=1, source_target_pairs={{0,16},{4,12},{8,24},{12,4},{16,0},{20,28},{24,8},{28,20},{1,17},{... | collective-permute-start | bytes 30728 | tf_op jit(solution)/shard_map/ppermute | solution.py:64
  31.9 2.0 %collective-permute-start.16 = (bf16[2048,128]{1,0:T(8,128)(2,1)S(1)}, bf16[2048,128]{1,0:T(8,128)(2,1)S(1)}, u32[]{:S(2)}, u32[]{:S(2)}) collective-permute-start(bf16[2048,128]{1,0:T(8,128)(2,1)S(1)} %collective-permute-done.14.refs_5_), channel_id=1, source_target_pairs={{0,4},{4,0},{8,12},{12,8},{16,20},{20,16},{24,28},{28,24},{1,5},{5... | collective-permute-start | bytes 1572872 | tf_op jit(solution)/shard_map/ppermute | solution.py:43
  32.0 10.3 %collective-permute-start.11 = (bf16[2048,128]{1,0:T(8,128)(2,1)S(1)}, bf16[2048,128]{1,0:T(8,128)(2,1)S(1)}, u32[]{:S(2)}, u32[]{:S(2)}) collective-permute-start(bf16[2048,128]{1,0:T(8,128)(2,1)S(1)} %collective-permute-done.10.refs_7_), channel_id=1, source_target_pairs={{0,8},{4,20},{8,0},{12,28},{16,24},{20,4},{24,16},{28,12},{1,9},{5... | collective-permute-start | bytes 1572872 | tf_op jit(solution)/shard_map/ppermute | solution.py:64
  33.2 1.5 %copy-start.7 = (s32[2]{0:T(128)S(1)}, s32[2]{0:T(128)}, u32[]{:S(2)}) copy-start(s32[2]{0:T(128)} %lengths_ref.3) | copy-start | bytes 28
  37.3 1.2 %collective-permute-start.19 = (f32[8,128]{1,0:T(8,128)S(1)}, f32[8,128]{1,0:T(8,128)S(1)}, u32[]{:S(2)}, u32[]{:S(2)}) collective-permute-start(f32[8,128]{1,0:T(8,128)S(1)} %get-tuple-element.55), channel_id=1, source_target_pairs={{0,4},{4,0},{8,12},{12,8},{16,20},{20,16},{24,28},{28,24},{1,5},{5... | collective-permute-start | bytes 12296 | tf_op jit(solution)/shard_map/ppermute | solution.py:43
  38.5 4.3 %collective-permute-start.23 = (bf16[2048,128]{1,0:T(8,128)(2,1)S(1)}, bf16[2048,128]{1,0:T(8,128)(2,1)S(1)}, u32[]{:S(2)}, u32[]{:S(2)}) collective-permute-start(bf16[2048,128]{1,0:T(8,128)(2,1)S(1)} %collective-permute-done.20.refs_5_), channel_id=1, source_target_pairs={{0,4},{4,0},{8,12},{12,8},{16,20},{20,16},{24,28},{28,24},{1,5},{5... | collective-permute-start | bytes 1572872 | tf_op jit(solution)/shard_map/ppermute | solution.py:43
  38.7 3.6 %collective-permute-start.21 = (f32[8,128]{1,0:T(8,128)S(1)}, f32[8,128]{1,0:T(8,128)S(1)}, u32[]{:S(2)}, u32[]{:S(2)}) collective-permute-start(f32[8,128]{1,0:T(8,128)S(1)} %max.6), channel_id=1, source_target_pairs={{0,16},{4,12},{8,24},{12,4},{16,0},{20,28},{24,8},{28,20},{1,17},{... | collective-permute-start | bytes 12296 | tf_op jit(solution)/shard_map/ppermute | solution.py:64
  42.3 2.4 %collective-permute-start.22 = (bf16[2048,128]{1,0:T(8,128)(2,1)S(1)}, bf16[2048,128]{1,0:T(8,128)(2,1)S(1)}, u32[]{:S(2)}, u32[]{:S(2)}) collective-permute-start(bf16[2048,128]{1,0:T(8,128)(2,1)S(1)} %collective-permute-done.11.refs_5_), channel_id=1, source_target_pairs={{0,4},{4,0},{8,12},{12,8},{16,20},{20,16},{24,28},{28,24},{1,5},{5... | collective-permute-start | bytes 1572872 | tf_op jit(solution)/shard_map/ppermute | solution.py:43
  42.3 1.9 %collective-permute-start.24 = (f32[8,128]{1,0:T(8,128)S(1)}, f32[8,128]{1,0:T(8,128)S(1)}, u32[]{:S(2)}, u32[]{:S(2)}) collective-permute-start(f32[8,128]{1,0:T(8,128)S(1)} %max.7), channel_id=1, source_target_pairs={{0,4},{4,0},{8,12},{12,8},{16,20},{20,16},{24,28},{28,24},{1,5},{5... | collective-permute-start | bytes 12296 | tf_op jit(solution)/shard_map/ppermute | solution.py:43
  44.7 9.7 %copy-start.1 = (bf16[1,1024,2048]{2,1,0:T(8,128)(2,1)S(1)}, bf16[1,1024,2048]{2,1,0:T(8,128)(2,1)}, u32[]{:S(2)}) copy-start(bf16[1,1024,2048]{2,1,0:T(8,128)(2,1)} %param.15) | copy-start | bytes 12582916
  45.9 1.2 %collective-permute-start.25 = (f32[8,256]{1,0:T(8,128)S(1)}, f32[8,256]{1,0:T(8,128)S(1)}, u32[]{:S(2)}, u32[]{:S(2)}) collective-permute-start(f32[8,256]{1,0:T(8,128)S(1)} %weighted_values.1), channel_id=1, source_target_pairs={{0,4},{4,0},{8,12},{12,8},{16,20},{20,16},{24,28},{28,24},{1,5},{5... | collective-permute-start | bytes 24584 | tf_op jit(solution)/shard_map/ppermute | solution.py:43
  47.1 3.7 %collective-permute-start.26 = (f32[8,256]{1,0:T(8,128)S(1)}, f32[8,256]{1,0:T(8,128)S(1)}, u32[]{:S(2)}, u32[]{:S(2)}) collective-permute-start(f32[8,256]{1,0:T(8,128)S(1)} %add.64), channel_id=1, source_target_pairs={{0,8},{4,12},{8,0},{12,4},{16,24},{20,28},{24,16},{28,20},{1,9},{5... | collective-permute-start | bytes 24584 | tf_op jit(solution)/shard_map/ppermute | solution.py:43
  50.8 3.7 %collective-permute-start.27 = (f32[8,256]{1,0:T(8,128)S(1)}, f32[8,256]{1,0:T(8,128)S(1)}, u32[]{:S(2)}, u32[]{:S(2)}) collective-permute-start(f32[8,256]{1,0:T(8,128)S(1)} %add.65.mine_ref), channel_id=1, source_target_pairs={{0,16},{4,20},{8,24},{12,28},{16,0},{20,4},{24,8},{28,12},{1,17},{... | collective-permute-start | bytes 24584 | tf_op jit(solution)/shard_map/ppermute | solution.py:43
  54.4 9.1 %copy-start.6 = (f32[2,2048]{1,0:T(2,128)S(1)}, f32[2,2048]{1,0:T(2,128)}, u32[]{:S(2)}) copy-start(f32[2,2048]{1,0:T(2,128)} %tokens_ref.3) | copy-start | bytes 49156
  55.1 3.8 %collective-permute-start.28 = (f32[2,2048]{1,0:T(2,128)S(1)}, f32[2,2048]{1,0:T(2,128)S(1)}, u32[]{:S(2)}, u32[]{:S(2)}) collective-permute-start(f32[2,2048]{1,0:T(2,128)S(1)} %output_products.1), channel_id=1, source_target_pairs={{0,1},{1,0},{2,3},{3,2},{4,5},{5,4},{6,7},{7,6},{8,9},{9,8},{10,11... | collective-permute-start | bytes 49160 | tf_op jit(solution)/shard_map/ppermute | solution.py:43
  58.8 4.7 %collective-permute-start.29 = (f32[2,2048]{1,0:T(2,128)S(1)}, f32[2,2048]{1,0:T(2,128)S(1)}, u32[]{:S(2)}, u32[]{:S(2)}) collective-permute-start(f32[2,2048]{1,0:T(2,128)S(1)} %add.66), channel_id=1, source_target_pairs={{0,2},{1,3},{2,0},{3,1},{4,6},{5,7},{6,4},{7,5},{8,10},{9,11},{10,... | collective-permute-start | bytes 49160 | tf_op jit(solution)/shard_map/ppermute | solution.py:43

commit v14 on v13

--- a/solution.py
+++ b/solution.py
@@ -403,22 +403,21 @@
     value_first = share(value_far[:1], parts_sent)
     value_last = send_last(own_values, value_first)
     value_first += value_far[:1]
-    value_total = project(after(places, masked), rows, value_near + value_first)
-    top = butterfly(after(top, value_total), "ctx", [1], jnp.maximum)
+    top = butterfly(top, "ctx", [1], jnp.maximum)
     top = after(top, *[block for _, block in value_far[1:]])
     near_top = top
+    value_total = project(after(places, near_top), rows, value_near + value_first)
     if split:
-        received = jnp.maximum(top, after(by_core(top, 4, 2), value_last[0][1]))
+        received = jnp.maximum(top, after(by_core(top, 4, 2), value_last[0][1], value_total))
         top = jnp.where(core == 0, swap(received, "ctx", 1), received)
     else:
         top = butterfly(top, "ctx", bits_below(team)[1:], jnp.maximum)
         received = top
 
-    value_second = value_far[1:] + share(value_far[1:], near_top)
-    value_total = project(places, rows, value_second, value_total)
+    value_second = value_far[1:] + share(value_far[1:], masked)
 
     blocks = share(value_last, received)
-    value_total = project(places, rows, value_last, value_total)
+    value_total = project(places, rows, value_second + value_last, value_total)
     packed = call(
         functools.partial(weigh_kernel, [d for d, _ in blocks], len(rows), team),
         "weighted_values",

time: 64.4 us -> 66.1 us (1.026)
  waiting for transfers between devices: 20.2 us -> 23.4 us
  starting transfers between devices: 23.2 us -> 21.9 us
    ppermute x19, waiting for transfers between devices: 14.4 us -> 16.9 us  [swap(): return lax.ppermute(value, axis, [(i, i ^ distance) for i in range(count)])]
    ppermute x19, starting transfers between devices: 9.27 us -> 8.41 us  [swap(): return lax.ppermute(value, axis, [(i, i ^ distance) for i in range(count)])]
    ppermute x11, waiting for transfers between devices: 5.8 us -> 6.48 us  [by_core(): return lax.ppermute(value, 'ctx', pairs)]
    pallas_call x6 -> x5, Pallas kernels: 6.15 us -> 5.99 us  [project(): call(functools.partial(project_kernel, [d for d, _ in blocks], len(rows),...]
  transfers between devices with their start and end apart: 30 -> 30, of which waited for: 13 -> 16; matrix products, arithmetic and copies ran while one was open for 1% -> 1% of each run, Pallas kernels for 24% -> 23%
where the time goes in v14:
time: 66.1 us; the launch traced here: 65.9 us
  waiting for transfers between devices  23.4 us (35%)
  starting transfers between devices  21.9 us (33%)
  Pallas kernels  17.2 us (26%)
  local copies, waits for them, and re-layouts  1.59 us (2%)
  other arithmetic  1.49 us (2%)
    ppermute x19, waiting for transfers between devices, swap(): return lax.ppermute(value, axis, [(i, i ^ distance) for i in range(count)])  16.9 us
    ppermute x11, starting transfers between devices, by_core(): return lax.ppermute(value, 'ctx', pairs)  13.5 us
    ppermute x19, starting transfers between devices, swap(): return lax.ppermute(value, axis, [(i, i ^ distance) for i in range(count)])  8.41 us
    pallas_call x2, Pallas kernels, normalise(): call(functools.partial(norm_kernel, first), 'normalise', [IN_HBM, IN_VMEM...  7.47 us
    ppermute x11, waiting for transfers between devices, by_core(): return lax.ppermute(value, 'ctx', pairs)  6.48 us
    pallas_call x5, Pallas kernels, project(): call(functools.partial(project_kernel, [d for d, _ in blocks], len(rows),...  5.99 us
    unnamed x18, local copies, waits for them, and re-layouts  1.59 us
  transfers between devices with their start and end apart: 30, of which 16 were waited for; matrix products, arithmetic and copies ran while one was open for 1% of the time, Pallas kernels for 23%

profile of v14, /device:TPU:0, one launch (start us, length us, event | category | flops | bytes accessed | tf_op | source)
XLA Modules:
  0.0 65.9 jit_solution(14622507880712347692)
XLA Ops:
  0.0 0.5 collective-permute-start.1
  0.5 0.1 collective-permute-start.2
  0.5 2.9 %collective-permute-start.12 = (bf16[2048,128]{1,0:T(8,128)(2,1)}, bf16[2048,128]{1,0:T(8,128)(2,1)S(1)}, u32[]{:S(2)}, u32[]{:S(2)}) collective-permute-start(bf16[2048,128]{1,0:T(8,128)(2,1)} %bitcast.24), channel_id=1, source_target_pairs={{0,8},{4,20},{8,0},{12,28},{16,24},{20,4},{24,16},{28,12},{1,9},{5... | collective-permute-start | bytes 1572872 | tf_op jit(solution)/shard_map/ppermute | solution.py:64
  3.5 1.6 %collective-permute-start.7 = (bf16[2048,128]{1,0:T(8,128)(2,1)S(1)}, bf16[2048,128]{1,0:T(8,128)(2,1)S(1)}, u32[]{:S(2)}, u32[]{:S(2)}) collective-permute-start(bf16[2048,128]{1,0:T(8,128)(2,1)S(1)} %collective-permute-done.1.refs_6_), channel_id=1, source_target_pairs={{0,8},{4,20},{8,0},{12,28},{16,24},{20,4},{24,16},{28,12},{1,9},{5... | collective-permute-start | bytes 1572872 | tf_op jit(solution)/shard_map/ppermute | solution.py:64
  5.1 0.7 %copy-done.5 = f32[2,2048]{1,0:T(2,128)S(1)} copy-done((f32[2,2048]{1,0:T(2,128)S(1)}, f32[2,2048]{1,0:T(2,128)}, u32[]{:S(2)}) %copy-start.5) | copy-done | bytes 16408
  5.8 0.1 squares.1
  5.9 1.1 %collective-permute-done = f32[2,128]{1,0:T(2,128)S(1)} collective-permute-done((f32[2,128]{1,0:T(2,128)S(1)}, f32[2,128]{1,0:T(2,128)S(1)}, u32[]{:S(2)}, u32[]{:S(2)}) %collective-permute-start) | collective-permute-done | bytes 1056 | tf_op jit(solution)/shard_map/ppermute | solution.py:43
  7.0 0.0 collective-permute-done.2.refs_6_
  7.0 1.5 %collective-permute-start.3 = (f32[2,128]{1,0:T(2,128)S(1)}, f32[2,128]{1,0:T(2,128)S(1)}, u32[]{:S(2)}, u32[]{:S(2)}) collective-permute-start(f32[2,128]{1,0:T(2,128)S(1)} %add.53), channel_id=1, source_target_pairs={{0,16},{4,12},{8,24},{12,4},{16,0},{20,28},{24,8},{28,20},{1,17},{... | collective-permute-start | bytes 3080 | tf_op jit(solution)/shard_map/ppermute | solution.py:64
  8.5 0.8 %copy-done.4 = f32[1,16384]{1,0:T(1,128)S(1)} copy-done((f32[1,16384]{1,0:T(1,128)S(1)}, f32[1,16384]{1,0:T(1,128)}, u32[]{:S(2)}) %copy-start.4) | copy-done | bytes 65560
  9.4 3.2 %normalise.2 = (bf16[8,64,2048]{2,1,0:T(8,128)(2,1)S(1)}, bf16[8,64,2048]{2,1,0:T(8,128)(2,1)S(1)}) custom-call(bf16[320,16384]{1,0:T(8,128)(2,1)} %bitcast.35, f32[8,1,2048]{2,1,0:T(1,128)S(1)} %bitcast.31), custom_call_target="tpu_custom_call" | custom-call | flops 1000 | bytes 1000 | tf_op jit(solution)/shard_map/normalise/pallas_call | solution.py:173
  12.6 0.1 collective-permute-start.4
  12.7 0.6 collective-permute-start.5
  13.3 0.5 collective-permute-done.4
  13.8 0.2 collective-permute-start.13
  14.0 0.9 %collective-permute-start.6 = (f32[2,128]{1,0:T(2,128)S(1)}, f32[2,128]{1,0:T(2,128)S(1)}, u32[]{:S(2)}, u32[]{:S(2)}) collective-permute-start(f32[2,128]{1,0:T(2,128)S(1)} %collective-permute-done.4), channel_id=1, source_target_pairs={{0,16},{4,12},{8,24},{12,4},{16,0},{20,28},{24,8},{28,20},{1,17},{... | collective-permute-start | bytes 3080 | tf_op jit(solution)/shard_map/ppermute | solution.py:64
  14.9 4.3 %normalise.3 = (bf16[8,64,2048]{2,1,0:T(8,128)(2,1)S(1)}, bf16[8,64,2048]{2,1,0:T(8,128)(2,1)S(1)}, bf16[8,64,2048]{2,1,0:T(8,128)(2,1)S(1)}) custom-call(bf16[320,16384]{1,0:T(8,128)(2,1)} %bitcast.36, f32[8,1,2048]{2,1,0:T(1,128)S(1)} %bitcast.32), custom_call_target="tpu_custom_call" | custom-call | flops 1000 | bytes 1000 | tf_op jit(solution)/shard_map/normalise/pallas_call | solution.py:173
  19.3 0.0 collective-permute-done.7.refs_6_
  19.3 0.0 copy-start.8
  19.3 0.8 %query_products.1 = f32[2,10,128]{2,1,0:T(8,128)S(1)} custom-call(s32[1]{0:T(128)} %bitcast.place_ref, f32[2,128]{1,0:T(2,128)S(1)} %add_add_fusion.2.squares_ref, f32[2,2048]{1,0:T(2,128)S(1)} %copy-done.5, f32[8,1,2048]{2,1,0:T(1,128)S(1)} %bitcast.33, bf16[2048,1024]{1,0:T(8,128)(2,1)S(1)} %bitcast.21, bf16[2048,128]{1,0:T(8,128)(2,1)S(1)} %bitcast.25, ...), custom_call_target="tpu_custom_call" | custom-call | flops 1000 | bytes 1000 | tf_op jit(solution)/shard_map/query_products/pallas_call | solution.py:371
  20.1 0.1 collective-permute-start.8
  20.3 1.1 %collective-permute-done.8 = f32[2,10,128]{2,1,0:T(8,128)S(1)} collective-permute-done((f32[2,10,128]{2,1,0:T(8,128)S(1)}, f32[2,10,128]{2,1,0:T(8,128)S(1)}, u32[]{:S(2)}, u32[]{:S(2)}) %collective-permute-start.8) | collective-permute-done | bytes 10272 | tf_op jit(solution)/shard_map/ppermute | solution.py:43
  21.4 1.1 %collective-permute-start.9 = (f32[2,10,128]{2,1,0:T(8,128)S(1)}, f32[2,10,128]{2,1,0:T(8,128)S(1)}, u32[]{:S(2)}, u32[]{:S(2)}) collective-permute-start(f32[2,10,128]{2,1,0:T(8,128)S(1)} %add.57), channel_id=1, source_target_pairs={{0,16},{4,12},{8,24},{12,4},{16,0},{20,28},{24,8},{28,20},{1,17},{... | collective-permute-start | bytes 30728 | tf_op jit(solution)/shard_map/ppermute | solution.py:64
  22.5 0.1 collective-permute-start.15
  22.6 0.0 collective-permute-done.13.refs_7_
  22.6 0.9 %collective-permute-start.14 = (bf16[2048,128]{1,0:T(8,128)(2,1)S(1)}, bf16[2048,128]{1,0:T(8,128)(2,1)S(1)}, u32[]{:S(2)}, u32[]{:S(2)}) collective-permute-start(bf16[2048,128]{1,0:T(8,128)(2,1)S(1)} %collective-permute-done.13.refs_7_), channel_id=1, source_target_pairs={{0,8},{4,20},{8,0},{12,28},{16,24},{20,4},{24,16},{28,12},{1,9},{5... | collective-permute-start | bytes 1572872 | tf_op jit(solution)/shard_map/ppermute | solution.py:64
  23.5 1.6 %collective-permute-done.9 = f32[2,10,128]{2,1,0:T(8,128)S(1)} collective-permute-done((f32[2,10,128]{2,1,0:T(8,128)S(1)}, f32[2,10,128]{2,1,0:T(8,128)S(1)}, u32[]{:S(2)}, u32[]{:S(2)}) %collective-permute-start.9) | collective-permute-done | bytes 10272 | tf_op jit(solution)/shard_map/ppermute | solution.py:64
  25.1 0.6 multiply_sine_fusion
  25.8 0.6 collective-permute-start.17
  26.4 0.1 multiply_sine_fusion.1
  26.5 0.9 %collective-permute-start.20 = (bf16[2048,128]{1,0:T(8,128)(2,1)S(1)}, bf16[2048,128]{1,0:T(8,128)(2,1)S(1)}, u32[]{:S(2)}, u32[]{:S(2)}) collective-permute-start(bf16[2048,128]{1,0:T(8,128)(2,1)S(1)} %collective-permute-done.2.refs_6_), channel_id=1, source_target_pairs={{0,8},{4,20},{8,0},{12,28},{16,24},{20,4},{24,16},{28,12},{1,9},{5... | collective-permute-start | bytes 1572872 | tf_op jit(solution)/shard_map/ppermute | solution.py:64
  27.3 0.9 %project.5.refs_9_ = f32[320,128]{1,0:T(8,128)S(1)} custom-call(s32[1]{0:T(128)} %bitcast.place_ref, bf16[8,64,2048]{2,1,0:T(8,128)(2,1)S(1)} %get-tuple-element.35.refs_0_, bf16[8,64,2048]{2,1,0:T(8,128)(2,1)S(1)} %get-tuple-element.36.refs_1_, bf16[8,64,2048]{2,1,0:T(8,128)(2,1)S(1)} %get-tuple-element.39.refs_2_, ...), custom_call_target="tpu_custom_call" | custom-call | flops 1000 | bytes 1000 | tf_op jit(solution)/shard_map/project/pallas_call | solution.py:218
  28.2 1.2 %collective-permute-start.18 = (f32[2,10,128]{2,1,0:T(8,128)S(1)}, f32[2,10,128]{2,1,0:T(8,128)S(1)}, u32[]{:S(2)}, u32[]{:S(2)}) collective-permute-start(f32[2,10,128]{2,1,0:T(8,128)S(1)} %collective-permute-done.17), channel_id=1, source_target_pairs={{0,16},{4,12},{8,24},{12,4},{16,0},{20,28},{24,8},{28,20},{1,17},{... | collective-permute-start | bytes 30728 | tf_op jit(solution)/shard_map/ppermute | solution.py:64
  29.4 1.5 %project.6.refs_7_ = f32[320,128]{1,0:T(8,128)S(1)} custom-call(s32[1]{0:T(128)} %bitcast.place_ref, bf16[8,64,2048]{2,1,0:T(8,128)(2,1)S(1)} %get-tuple-element.35.refs_0_, bf16[8,64,2048]{2,1,0:T(8,128)(2,1)S(1)} %get-tuple-element.36.refs_1_, bf16[8,64,2048]{2,1,0:T(8,128)(2,1)S(1)} %get-tuple-element.39.refs_2_, ...), custom_call_target="tpu_custom_call" | custom-call | flops 1000 | bytes 1000 | tf_op jit(solution)/shard_map/project/pallas_call | solution.py:218
  31.0 1.1 %collective-permute-done.14.refs_5_ = bf16[2048,128]{1,0:T(8,128)(2,1)S(1)} collective-permute-done((bf16[2048,128]{1,0:T(8,128)(2,1)S(1)}, bf16[2048,128]{1,0:T(8,128)(2,1)S(1)}, u32[]{:S(2)}, u32[]{:S(2)}) %collective-permute-start.14) | collective-permute-done | bytes 524320 | tf_op jit(solution)/shard_map/ppermute | solution.py:64
  32.0 0.9 %collective-permute-start.11 = (bf16[2048,128]{1,0:T(8,128)(2,1)S(1)}, bf16[2048,128]{1,0:T(8,128)(2,1)S(1)}, u32[]{:S(2)}, u32[]{:S(2)}) collective-permute-start(bf16[2048,128]{1,0:T(8,128)(2,1)S(1)} %collective-permute-done.10.refs_7_), channel_id=1, source_target_pairs={{0,8},{4,20},{8,0},{12,28},{16,24},{20,4},{24,16},{28,12},{1,9},{5... | collective-permute-start | bytes 1572872 | tf_op jit(solution)/shard_map/ppermute | solution.py:64
  32.9 0.0 copy-start.7
  33.0 1.0 %collective-permute-done.16.refs_6_ = bf16[2048,128]{1,0:T(8,128)(2,1)S(1)} collective-permute-done((bf16[2048,128]{1,0:T(8,128)(2,1)S(1)}, bf16[2048,128]{1,0:T(8,128)(2,1)S(1)}, u32[]{:S(2)}, u32[]{:S(2)}) %collective-permute-start.16) | collective-permute-done | bytes 524320 | tf_op jit(solution)/shard_map/ppermute | solution.py:43
  33.9 0.9 %project.7.refs_0_ = f32[320,128]{1,0:T(8,128)S(1)} custom-call(s32[1]{0:T(128)} %bitcast.place_ref, bf16[8,64,2048]{2,1,0:T(8,128)(2,1)S(1)} %get-tuple-element.35.refs_0_, bf16[8,64,2048]{2,1,0:T(8,128)(2,1)S(1)} %get-tuple-element.36.refs_1_, bf16[8,64,2048]{2,1,0:T(8,128)(2,1)S(1)} %get-tuple-element.39.refs_2_, ...), custom_call_target="tpu_custom_call" | custom-call | flops 1000 | bytes 1000 | tf_op jit(solution)/shard_map/project/pallas_call | solution.py:218
  34.8 1.0 %scores.1 = (f32[8,320]{1,0:T(8,128)S(1)}, f32[8,128]{1,0:T(8,128)S(1)}, f32[8,128]{1,0:T(8,128)S(1)}) custom-call(s32[1]{0:T(128)} %bitcast.place_ref, s32[2]{0:T(128)S(1)} %copy-done.7, f32[320,128]{1,0:T(8,128)S(1)} %project.7.refs_0_, f32[320,64]{1,0:T(8,128)S(1)} %get-tuple-element.60.refs_1_, f32[320,64]{1,0:T(8,128)S(1)} %get-tuple-element.59.refs_2_, ...), custom_call_target="tpu_custom_call" | custom-call | flops 1000 | bytes 1000 | tf_op jit(solution)/shard_map/scores/pallas_call | solution.py:397
  35.8 0.1 collective-permute-start.19
  35.9 1.0 %collective-permute-done.19 = f32[8,128]{1,0:T(8,128)S(1)} collective-permute-done((f32[8,128]{1,0:T(8,128)S(1)}, f32[8,128]{1,0:T(8,128)S(1)}, u32[]{:S(2)}, u32[]{:S(2)}) %collective-permute-start.19) | collective-permute-done | bytes 4128 | tf_op jit(solution)/shard_map/ppermute | solution.py:43
  37.0 0.7 %collective-permute-done.20.refs_5_ = bf16[2048,128]{1,0:T(8,128)(2,1)S(1)} collective-permute-done((bf16[2048,128]{1,0:T(8,128)(2,1)S(1)}, bf16[2048,128]{1,0:T(8,128)(2,1)S(1)}, u32[]{:S(2)}, u32[]{:S(2)}) %collective-permute-start.20) | collective-permute-done | bytes 524320 | tf_op jit(solution)/shard_map/ppermute | solution.py:64
  37.7 0.9 %collective-permute-start.21 = (f32[8,128]{1,0:T(8,128)S(1)}, f32[8,128]{1,0:T(8,128)S(1)}, u32[]{:S(2)}, u32[]{:S(2)}) collective-permute-start(f32[8,128]{1,0:T(8,128)S(1)} %max.6), channel_id=1, source_target_pairs={{0,16},{4,12},{8,24},{12,4},{16,0},{20,28},{24,8},{28,20},{1,17},{... | collective-permute-start | bytes 12296 | tf_op jit(solution)/shard_map/ppermute | solution.py:64
  38.6 1.5 %project.8.refs_8_ = f32[320,128]{1,0:T(8,128)S(1)} custom-call(s32[1]{0:T(128)} %bitcast.place_ref, bf16[8,64,2048]{2,1,0:T(8,128)(2,1)S(1)} %get-tuple-element.35.refs_0_, bf16[8,64,2048]{2,1,0:T(8,128)(2,1)S(1)} %get-tuple-element.36.refs_1_, bf16[8,64,2048]{2,1,0:T(8,128)(2,1)S(1)} %get-tuple-element.39.refs_2_, ...), custom_call_target="tpu_custom_call" | custom-call | flops 1000 | bytes 1000 | tf_op jit(solution)/shard_map/project/pallas_call | solution.py:218
  40.1 1.2 %collective-permute-done.21 = f32[8,128]{1,0:T(8,128)S(1)} collective-permute-done((f32[8,128]{1,0:T(8,128)S(1)}, f32[8,128]{1,0:T(8,128)S(1)}, u32[]{:S(2)}, u32[]{:S(2)}) %collective-permute-start.21) | collective-permute-done | bytes 4128 | tf_op jit(solution)/shard_map/ppermute | solution.py:64
  41.4 1.9 %collective-permute-done.11.refs_7_ = bf16[2048,128]{1,0:T(8,128)(2,1)S(1)} collective-permute-done((bf16[2048,128]{1,0:T(8,128)(2,1)S(1)}, bf16[2048,128]{1,0:T(8,128)(2,1)S(1)}, u32[]{:S(2)}, u32[]{:S(2)}) %collective-permute-start.11) | collective-permute-done | bytes 524320 | tf_op jit(solution)/shard_map/ppermute | solution.py:64
  43.3 0.5 collective-permute-start.24
  43.8 1.4 %collective-permute-done.24 = f32[8,128]{1,0:T(8,128)S(1)} collective-permute-done((f32[8,128]{1,0:T(8,128)S(1)}, f32[8,128]{1,0:T(8,128)S(1)}, u32[]{:S(2)}, u32[]{:S(2)}) %collective-permute-start.24) | collective-permute-done | bytes 4128 | tf_op jit(solution)/shard_map/ppermute | solution.py:43
  45.2 1.2 %project.9.refs_6_ = f32[320,128]{1,0:T(8,128)S(1)} custom-call(s32[1]{0:T(128)} %bitcast.place_ref, bf16[8,64,2048]{2,1,0:T(8,128)(2,1)S(1)} %get-tuple-element.35.refs_0_, bf16[8,64,2048]{2,1,0:T(8,128)(2,1)S(1)} %get-tuple-element.36.refs_1_, bf16[8,64,2048]{2,1,0:T(8,128)(2,1)S(1)} %get-tuple-element.39.refs_2_, ...), custom_call_target="tpu_custom_call" | custom-call | flops 1000 | bytes 1000 | tf_op jit(solution)/shard_map/project/pallas_call | solution.py:218
  46.5 0.0 copy-start.1
  46.5 1.2 %weighted_values.1 = f32[8,256]{1,0:T(8,128)S(1)} custom-call(s32[1]{0:T(128)} %bitcast.place_ref, s32[2]{0:T(128)S(1)} %copy-done.7, bf16[8,64,2048]{2,1,0:T(8,128)(2,1)S(1)} %get-tuple-element.35.refs_0_, bf16[8,64,2048]{2,1,0:T(8,128)(2,1)S(1)} %get-tuple-element.36.refs_1_, bf16[8,64,2048]{2,1,0:T(8,128)(2,1)S(1)} %get-tuple-element.39.refs_2_, ...), custom_call_target="tpu_custom_call" | custom-call | flops 1000 | bytes 1000 | tf_op jit(solution)/shard_map/weighted_values/pallas_call | solution.py:421
  47.6 0.1 collective-permute-start.25
  47.8 1.0 %collective-permute-done.25 = f32[8,256]{1,0:T(8,128)S(1)} collective-permute-done((f32[8,256]{1,0:T(8,128)S(1)}, f32[8,256]{1,0:T(8,128)S(1)}, u32[]{:S(2)}, u32[]{:S(2)}) %collective-permute-start.25) | collective-permute-done | bytes 8224 | tf_op jit(solution)/shard_map/ppermute | solution.py:43
  48.8 0.9 %collective-permute-start.26 = (f32[8,256]{1,0:T(8,128)S(1)}, f32[8,256]{1,0:T(8,128)S(1)}, u32[]{:S(2)}, u32[]{:S(2)}) collective-permute-start(f32[8,256]{1,0:T(8,128)S(1)} %add.64), channel_id=1, source_target_pairs={{0,8},{4,12},{8,0},{12,4},{16,24},{20,28},{24,16},{28,20},{1,9},{5... | collective-permute-start | bytes 24584 | tf_op jit(solution)/shard_map/ppermute | solution.py:43
  49.7 2.8 %collective-permute-done.26 = f32[8,256]{1,0:T(8,128)S(1)} collective-permute-done((f32[8,256]{1,0:T(8,128)S(1)}, f32[8,256]{1,0:T(8,128)S(1)}, u32[]{:S(2)}, u32[]{:S(2)}) %collective-permute-start.26) | collective-permute-done | bytes 8224 | tf_op jit(solution)/shard_map/ppermute | solution.py:43
  52.5 0.9 %collective-permute-start.27 = (f32[8,256]{1,0:T(8,128)S(1)}, f32[8,256]{1,0:T(8,128)S(1)}, u32[]{:S(2)}, u32[]{:S(2)}) collective-permute-start(f32[8,256]{1,0:T(8,128)S(1)} %add.65.mine_ref), channel_id=1, source_target_pairs={{0,16},{4,20},{8,24},{12,28},{16,0},{20,4},{24,8},{28,12},{1,17},{... | collective-permute-start | bytes 24584 | tf_op jit(solution)/shard_map/ppermute | solution.py:43
  53.4 2.7 %collective-permute-done.27.other_ref = f32[8,256]{1,0:T(8,128)S(1)} collective-permute-done((f32[8,256]{1,0:T(8,128)S(1)}, f32[8,256]{1,0:T(8,128)S(1)}, u32[]{:S(2)}, u32[]{:S(2)}) %collective-permute-start.27) | collective-permute-done | bytes 8224 | tf_op jit(solution)/shard_map/ppermute | solution.py:43
  56.1 0.6 output_products.1
  56.8 1.6 %collective-permute-start.28 = (f32[2,2048]{1,0:T(2,128)S(1)}, f32[2,2048]{1,0:T(2,128)S(1)}, u32[]{:S(2)}, u32[]{:S(2)}) collective-permute-start(f32[2,2048]{1,0:T(2,128)S(1)} %output_products.1), channel_id=1, source_target_pairs={{0,1},{1,0},{2,3},{3,2},{4,5},{5,4},{6,7},{7,6},{8,9},{9,8},{10,11... | collective-permute-start | bytes 49160 | tf_op jit(solution)/shard_map/ppermute | solution.py:43
  58.4 2.2 %collective-permute-done.28 = f32[2,2048]{1,0:T(2,128)S(1)} collective-permute-done((f32[2,2048]{1,0:T(2,128)S(1)}, f32[2,2048]{1,0:T(2,128)S(1)}, u32[]{:S(2)}, u32[]{:S(2)}) %collective-permute-start.28) | collective-permute-done | bytes 16416 | tf_op jit(solution)/shard_map/ppermute | solution.py:43
  60.6 2.7 %collective-permute-start.29 = (f32[2,2048]{1,0:T(2,128)S(1)}, f32[2,2048]{1,0:T(2,128)S(1)}, u32[]{:S(2)}, u32[]{:S(2)}) collective-permute-start(f32[2,2048]{1,0:T(2,128)S(1)} %add.66), channel_id=1, source_target_pairs={{0,2},{1,3},{2,0},{3,1},{4,6},{5,7},{6,4},{7,5},{8,10},{9,11},{10,... | collective-permute-start | bytes 49160 | tf_op jit(solution)/shard_map/ppermute | solution.py:43
  63.2 2.0 %collective-permute-done.29 = f32[2,2048]{1,0:T(2,128)S(1)} collective-permute-done((f32[2,2048]{1,0:T(2,128)S(1)}, f32[2,2048]{1,0:T(2,128)S(1)}, u32[]{:S(2)}, u32[]{:S(2)}) %collective-permute-start.29) | collective-permute-done | bytes 16416 | tf_op jit(solution)/shard_map/ppermute | solution.py:43
  65.3 0.6 add_add_fusion
  (45 shorter events, 0.2 us)
Async XLA Ops:
  0.0 3.5 %collective-permute-start.1 = (bf16[2048,128]{1,0:T(8,128)(2,1)}, bf16[2048,128]{1,0:T(8,128)(2,1)S(1)}, u32[]{:S(2)}, u32[]{:S(2)}) collective-permute-start(bf16[2048,128]{1,0:T(8,128)(2,1)} %bitcast.23), channel_id=1, source_target_pairs={{0,4},{4,0},{8,12},{12,8},{16,20},{20,16},{24,28},{28,24},{1,5},{5... | collective-permute-start | bytes 1572872 | tf_op jit(solution)/shard_map/ppermute | solution.py:43
  0.5 6.6 %collective-permute-start.2 = (bf16[2048,128]{1,0:T(8,128)(2,1)}, bf16[2048,128]{1,0:T(8,128)(2,1)S(1)}, u32[]{:S(2)}, u32[]{:S(2)}) collective-permute-start(bf16[2048,128]{1,0:T(8,128)(2,1)} %bitcast.27), channel_id=1, source_target_pairs={{0,4},{4,0},{8,12},{12,8},{16,20},{20,16},{24,28},{28,24},{1,5},{5... | collective-permute-start | bytes 1572872 | tf_op jit(solution)/shard_map/ppermute | solution.py:43
  0.5 12.8 %collective-permute-start.12 = (bf16[2048,128]{1,0:T(8,128)(2,1)}, bf16[2048,128]{1,0:T(8,128)(2,1)S(1)}, u32[]{:S(2)}, u32[]{:S(2)}) collective-permute-start(bf16[2048,128]{1,0:T(8,128)(2,1)} %bitcast.24), channel_id=1, source_target_pairs={{0,8},{4,20},{8,0},{12,28},{16,24},{20,4},{24,16},{28,12},{1,9},{5... | collective-permute-start | bytes 1572872 | tf_op jit(solution)/shard_map/ppermute | solution.py:64
  3.5 15.8 %collective-permute-start.7 = (bf16[2048,128]{1,0:T(8,128)(2,1)S(1)}, bf16[2048,128]{1,0:T(8,128)(2,1)S(1)}, u32[]{:S(2)}, u32[]{:S(2)}) collective-permute-start(bf16[2048,128]{1,0:T(8,128)(2,1)S(1)} %collective-permute-done.1.refs_6_), channel_id=1, source_target_pairs={{0,8},{4,20},{8,0},{12,28},{16,24},{20,4},{24,16},{28,12},{1,9},{5... | collective-permute-start | bytes 1572872 | tf_op jit(solution)/shard_map/ppermute | solution.py:64
  5.1 0.7 %copy-start.5 = (f32[2,2048]{1,0:T(2,128)S(1)}, f32[2,2048]{1,0:T(2,128)}, u32[]{:S(2)}) copy-start(f32[2,2048]{1,0:T(2,128)} %tokens_ref.3) | copy-start | bytes 49156
  5.9 1.1 %collective-permute-start = (f32[2,128]{1,0:T(2,128)S(1)}, f32[2,128]{1,0:T(2,128)S(1)}, u32[]{:S(2)}, u32[]{:S(2)}) collective-permute-start(f32[2,128]{1,0:T(2,128)S(1)} %get-tuple-element.32), channel_id=1, source_target_pairs={{0,4},{4,0},{8,12},{12,8},{16,20},{20,16},{24,28},{28,24},{1,5},{5... | collective-permute-start | bytes 3080 | tf_op jit(solution)/shard_map/ppermute | solution.py:43
  7.0 5.6 %collective-permute-start.3 = (f32[2,128]{1,0:T(2,128)S(1)}, f32[2,128]{1,0:T(2,128)S(1)}, u32[]{:S(2)}, u32[]{:S(2)}) collective-permute-start(f32[2,128]{1,0:T(2,128)S(1)} %add.53), channel_id=1, source_target_pairs={{0,16},{4,12},{8,24},{12,4},{16,0},{20,28},{24,8},{28,20},{1,17},{... | collective-permute-start | bytes 3080 | tf_op jit(solution)/shard_map/ppermute | solution.py:64
  8.5 0.8 %copy-start.4 = (f32[1,16384]{1,0:T(1,128)S(1)}, f32[1,16384]{1,0:T(1,128)}, u32[]{:S(2)}) copy-start(f32[1,16384]{1,0:T(1,128)} %param.11) | copy-start | bytes 196612
  9.4 3.3 %copy-start.3 = (bf16[1,2048,128]{2,1,0:T(8,128)(2,1)S(1)}, bf16[1,2048,128]{2,1,0:T(8,128)(2,1)}, u32[]{:S(2)}) copy-start(bf16[1,2048,128]{2,1,0:T(8,128)(2,1)} %param.14) | copy-start | bytes 1572868
  12.6 1.2 %collective-permute-start.4 = (f32[2,128]{1,0:T(2,128)S(1)}, f32[2,128]{1,0:T(2,128)S(1)}, u32[]{:S(2)}, u32[]{:S(2)}) collective-permute-start(f32[2,128]{1,0:T(2,128)S(1)} %collective-permute-done.3), channel_id=1, source_target_pairs={{0,4},{4,0},{8,12},{12,8},{16,20},{20,16},{24,28},{28,24},{1,5},{5... | collective-permute-start | bytes 3080 | tf_op jit(solution)/shard_map/ppermute | solution.py:43
  12.7 10.9 %collective-permute-start.5 = (bf16[2048,128]{1,0:T(8,128)(2,1)S(1)}, bf16[2048,128]{1,0:T(8,128)(2,1)S(1)}, u32[]{:S(2)}, u32[]{:S(2)}) collective-permute-start(bf16[2048,128]{1,0:T(8,128)(2,1)S(1)} %bitcast.28), channel_id=1, source_target_pairs={{0,8},{4,20},{8,0},{12,28},{16,24},{20,4},{24,16},{28,12},{1,9},{5... | collective-permute-start | bytes 1572872 | tf_op jit(solution)/shard_map/ppermute | solution.py:64
  13.8 8.8 %collective-permute-start.13 = (bf16[2048,128]{1,0:T(8,128)(2,1)S(1)}, bf16[2048,128]{1,0:T(8,128)(2,1)S(1)}, u32[]{:S(2)}, u32[]{:S(2)}) collective-permute-start(bf16[2048,128]{1,0:T(8,128)(2,1)S(1)} %collective-permute-done.12.refs_5_), channel_id=1, source_target_pairs={{0,4},{4,0},{8,12},{12,8},{16,20},{20,16},{24,28},{28,24},{1,5},{5... | collective-permute-start | bytes 1572872 | tf_op jit(solution)/shard_map/ppermute | solution.py:43
  14.0 5.2 %collective-permute-start.6 = (f32[2,128]{1,0:T(2,128)S(1)}, f32[2,128]{1,0:T(2,128)S(1)}, u32[]{:S(2)}, u32[]{:S(2)}) collective-permute-start(f32[2,128]{1,0:T(2,128)S(1)} %collective-permute-done.4), channel_id=1, source_target_pairs={{0,16},{4,12},{8,24},{12,4},{16,0},{20,28},{24,8},{28,20},{1,17},{... | collective-permute-start | bytes 3080 | tf_op jit(solution)/shard_map/ppermute | solution.py:64
  14.9 4.3 %copy-start = (bf16[1,2048,1024]{2,1,0:T(8,128)(2,1)S(1)}, bf16[1,2048,1024]{2,1,0:T(8,128)(2,1)}, u32[]{:S(2)}) copy-start(bf16[1,2048,1024]{2,1,0:T(8,128)(2,1)} %param.12) | copy-start | bytes 12582916
  14.9 4.3 %copy-start.2 = (bf16[1,2048,128]{2,1,0:T(8,128)(2,1)S(1)}, bf16[1,2048,128]{2,1,0:T(8,128)(2,1)}, u32[]{:S(2)}) copy-start(bf16[1,2048,128]{2,1,0:T(8,128)(2,1)} %param.13) | copy-start | bytes 1572868
  19.3 3.2 %copy-start.8 = (s32[2]{0:T(128)S(1)}, s32[2]{0:T(128)}, u32[]{:S(2)}) copy-start(s32[2]{0:T(128)} %param.17) | copy-start | bytes 28
  20.1 1.2 %collective-permute-start.8 = (f32[2,10,128]{2,1,0:T(8,128)S(1)}, f32[2,10,128]{2,1,0:T(8,128)S(1)}, u32[]{:S(2)}, u32[]{:S(2)}) collective-permute-start(f32[2,10,128]{2,1,0:T(8,128)S(1)} %query_products.1), channel_id=1, source_target_pairs={{0,4},{4,0},{8,12},{12,8},{16,20},{20,16},{24,28},{28,24},{1,5},{5... | collective-permute-start | bytes 30728 | tf_op jit(solution)/shard_map/ppermute | solution.py:43
  21.4 3.7 %collective-permute-start.9 = (f32[2,10,128]{2,1,0:T(8,128)S(1)}, f32[2,10,128]{2,1,0:T(8,128)S(1)}, u32[]{:S(2)}, u32[]{:S(2)}) collective-permute-start(f32[2,10,128]{2,1,0:T(8,128)S(1)} %add.57), channel_id=1, source_target_pairs={{0,16},{4,12},{8,24},{12,4},{16,0},{20,28},{24,8},{28,20},{1,17},{... | collective-permute-start | bytes 30728 | tf_op jit(solution)/shard_map/ppermute | solution.py:64
  22.5 6.9 %collective-permute-start.15 = (bf16[2048,128]{1,0:T(8,128)(2,1)S(1)}, bf16[2048,128]{1,0:T(8,128)(2,1)S(1)}, u32[]{:S(2)}, u32[]{:S(2)}) collective-permute-start(bf16[2048,128]{1,0:T(8,128)(2,1)S(1)} %collective-permute-done.7.refs_6_), channel_id=1, source_target_pairs={{0,4},{4,0},{8,12},{12,8},{16,20},{20,16},{24,28},{28,24},{1,5},{5... | collective-permute-start | bytes 1572872 | tf_op jit(solution)/shard_map/ppermute | solution.py:43
  22.6 9.4 %collective-permute-start.14 = (bf16[2048,128]{1,0:T(8,128)(2,1)S(1)}, bf16[2048,128]{1,0:T(8,128)(2,1)S(1)}, u32[]{:S(2)}, u32[]{:S(2)}) collective-permute-start(bf16[2048,128]{1,0:T(8,128)(2,1)S(1)} %collective-permute-done.13.refs_7_), channel_id=1, source_target_pairs={{0,8},{4,20},{8,0},{12,28},{16,24},{20,4},{24,16},{28,12},{1,9},{5... | collective-permute-start | bytes 1572872 | tf_op jit(solution)/shard_map/ppermute | solution.py:64
  25.1 6.9 %collective-permute-start.10 = (bf16[2048,128]{1,0:T(8,128)(2,1)S(1)}, bf16[2048,128]{1,0:T(8,128)(2,1)S(1)}, u32[]{:S(2)}, u32[]{:S(2)}) collective-permute-start(bf16[2048,128]{1,0:T(8,128)(2,1)S(1)} %collective-permute-done.5.refs_8_), channel_id=1, source_target_pairs={{0,4},{4,0},{8,12},{12,8},{16,20},{20,16},{24,28},{28,24},{1,5},{5... | collective-permute-start | bytes 1572872 | tf_op jit(solution)/shard_map/ppermute | solution.py:43
  25.8 2.4 %collective-permute-start.17 = (f32[2,10,128]{2,1,0:T(8,128)S(1)}, f32[2,10,128]{2,1,0:T(8,128)S(1)}, u32[]{:S(2)}, u32[]{:S(2)}) collective-permute-start(f32[2,10,128]{2,1,0:T(8,128)S(1)} %collective-permute-done.9), channel_id=1, source_target_pairs={{0,4},{4,0},{8,12},{12,8},{16,20},{20,16},{24,28},{28,24},{1,5},{5... | collective-permute-start | bytes 30728 | tf_op jit(solution)/shard_map/ppermute | solution.py:43
  26.5 11.2 %collective-permute-start.20 = (bf16[2048,128]{1,0:T(8,128)(2,1)S(1)}, bf16[2048,128]{1,0:T(8,128)(2,1)S(1)}, u32[]{:S(2)}, u32[]{:S(2)}) collective-permute-start(bf16[2048,128]{1,0:T(8,128)(2,1)S(1)} %collective-permute-done.2.refs_6_), channel_id=1, source_target_pairs={{0,8},{4,20},{8,0},{12,28},{16,24},{20,4},{24,16},{28,12},{1,9},{5... | collective-permute-start | bytes 1572872 | tf_op jit(solution)/shard_map/ppermute | solution.py:64
  28.2 4.7 %collective-permute-start.18 = (f32[2,10,128]{2,1,0:T(8,128)S(1)}, f32[2,10,128]{2,1,0:T(8,128)S(1)}, u32[]{:S(2)}, u32[]{:S(2)}) collective-permute-start(f32[2,10,128]{2,1,0:T(8,128)S(1)} %collective-permute-done.17), channel_id=1, source_target_pairs={{0,16},{4,12},{8,24},{12,4},{16,0},{20,28},{24,8},{28,20},{1,17},{... | collective-permute-start | bytes 30728 | tf_op jit(solution)/shard_map/ppermute | solution.py:64
  32.0 1.9 %collective-permute-start.16 = (bf16[2048,128]{1,0:T(8,128)(2,1)S(1)}, bf16[2048,128]{1,0:T(8,128)(2,1)S(1)}, u32[]{:S(2)}, u32[]{:S(2)}) collective-permute-start(bf16[2048,128]{1,0:T(8,128)(2,1)S(1)} %collective-permute-done.14.refs_5_), channel_id=1, source_target_pairs={{0,4},{4,0},{8,12},{12,8},{16,20},{20,16},{24,28},{28,24},{1,5},{5... | collective-permute-start | bytes 1572872 | tf_op jit(solution)/shard_map/ppermute | solution.py:43
  32.0 11.3 %collective-permute-start.11 = (bf16[2048,128]{1,0:T(8,128)(2,1)S(1)}, bf16[2048,128]{1,0:T(8,128)(2,1)S(1)}, u32[]{:S(2)}, u32[]{:S(2)}) collective-permute-start(bf16[2048,128]{1,0:T(8,128)(2,1)S(1)} %collective-permute-done.10.refs_7_), channel_id=1, source_target_pairs={{0,8},{4,20},{8,0},{12,28},{16,24},{20,4},{24,16},{28,12},{1,9},{5... | collective-permute-start | bytes 1572872 | tf_op jit(solution)/shard_map/ppermute | solution.py:64
  32.9 1.9 %copy-start.7 = (s32[2]{0:T(128)S(1)}, s32[2]{0:T(128)}, u32[]{:S(2)}) copy-start(s32[2]{0:T(128)} %lengths_ref.3) | copy-start | bytes 28
  35.8 1.2 %collective-permute-start.19 = (f32[8,128]{1,0:T(8,128)S(1)}, f32[8,128]{1,0:T(8,128)S(1)}, u32[]{:S(2)}, u32[]{:S(2)}) collective-permute-start(f32[8,128]{1,0:T(8,128)S(1)} %get-tuple-element.51), channel_id=1, source_target_pairs={{0,4},{4,0},{8,12},{12,8},{16,20},{20,16},{24,28},{28,24},{1,5},{5... | collective-permute-start | bytes 12296 | tf_op jit(solution)/shard_map/ppermute | solution.py:43
  37.7 3.7 %collective-permute-start.21 = (f32[8,128]{1,0:T(8,128)S(1)}, f32[8,128]{1,0:T(8,128)S(1)}, u32[]{:S(2)}, u32[]{:S(2)}) collective-permute-start(f32[8,128]{1,0:T(8,128)S(1)} %max.6), channel_id=1, source_target_pairs={{0,16},{4,12},{8,24},{12,4},{16,0},{20,28},{24,8},{28,20},{1,17},{... | collective-permute-start | bytes 12296 | tf_op jit(solution)/shard_map/ppermute | solution.py:64
  38.6 6.7 %collective-permute-start.23 = (bf16[2048,128]{1,0:T(8,128)(2,1)S(1)}, bf16[2048,128]{1,0:T(8,128)(2,1)S(1)}, u32[]{:S(2)}, u32[]{:S(2)}) collective-permute-start(bf16[2048,128]{1,0:T(8,128)(2,1)S(1)} %collective-permute-done.20.refs_5_), channel_id=1, source_target_pairs={{0,4},{4,0},{8,12},{12,8},{16,20},{20,16},{24,28},{28,24},{1,5},{5... | collective-permute-start | bytes 1572872 | tf_op jit(solution)/shard_map/ppermute | solution.py:43
  43.3 3.1 %collective-permute-start.22 = (bf16[2048,128]{1,0:T(8,128)(2,1)S(1)}, bf16[2048,128]{1,0:T(8,128)(2,1)S(1)}, u32[]{:S(2)}, u32[]{:S(2)}) collective-permute-start(bf16[2048,128]{1,0:T(8,128)(2,1)S(1)} %collective-permute-done.11.refs_7_), channel_id=1, source_target_pairs={{0,4},{4,0},{8,12},{12,8},{16,20},{20,16},{24,28},{28,24},{1,5},{5... | collective-permute-start | bytes 1572872 | tf_op jit(solution)/shard_map/ppermute | solution.py:43
  43.3 1.9 %collective-permute-start.24 = (f32[8,128]{1,0:T(8,128)S(1)}, f32[8,128]{1,0:T(8,128)S(1)}, u32[]{:S(2)}, u32[]{:S(2)}) collective-permute-start(f32[8,128]{1,0:T(8,128)S(1)} %max.7), channel_id=1, source_target_pairs={{0,4},{4,0},{8,12},{12,8},{16,20},{20,16},{24,28},{28,24},{1,5},{5... | collective-permute-start | bytes 12296 | tf_op jit(solution)/shard_map/ppermute | solution.py:43
  46.5 9.7 %copy-start.1 = (bf16[1,1024,2048]{2,1,0:T(8,128)(2,1)S(1)}, bf16[1,1024,2048]{2,1,0:T(8,128)(2,1)}, u32[]{:S(2)}) copy-start(bf16[1,1024,2048]{2,1,0:T(8,128)(2,1)} %param.15) | copy-start | bytes 12582916
  47.6 1.2 %collective-permute-start.25 = (f32[8,256]{1,0:T(8,128)S(1)}, f32[8,256]{1,0:T(8,128)S(1)}, u32[]{:S(2)}, u32[]{:S(2)}) collective-permute-start(f32[8,256]{1,0:T(8,128)S(1)} %weighted_values.1), channel_id=1, source_target_pairs={{0,4},{4,0},{8,12},{12,8},{16,20},{20,16},{24,28},{28,24},{1,5},{5... | collective-permute-start | bytes 24584 | tf_op jit(solution)/shard_map/ppermute | solution.py:43
  48.8 3.7 %collective-permute-start.26 = (f32[8,256]{1,0:T(8,128)S(1)}, f32[8,256]{1,0:T(8,128)S(1)}, u32[]{:S(2)}, u32[]{:S(2)}) collective-permute-start(f32[8,256]{1,0:T(8,128)S(1)} %add.64), channel_id=1, source_target_pairs={{0,8},{4,12},{8,0},{12,4},{16,24},{20,28},{24,16},{28,20},{1,9},{5... | collective-permute-start | bytes 24584 | tf_op jit(solution)/shard_map/ppermute | solution.py:43
  52.5 3.7 %collective-permute-start.27 = (f32[8,256]{1,0:T(8,128)S(1)}, f32[8,256]{1,0:T(8,128)S(1)}, u32[]{:S(2)}, u32[]{:S(2)}) collective-permute-start(f32[8,256]{1,0:T(8,128)S(1)} %add.65.mine_ref), channel_id=1, source_target_pairs={{0,16},{4,20},{8,24},{12,28},{16,0},{20,4},{24,8},{28,12},{1,17},{... | collective-permute-start | bytes 24584 | tf_op jit(solution)/shard_map/ppermute | solution.py:43
  56.1 9.1 %copy-start.6 = (f32[2,2048]{1,0:T(2,128)S(1)}, f32[2,2048]{1,0:T(2,128)}, u32[]{:S(2)}) copy-start(f32[2,2048]{1,0:T(2,128)} %tokens_ref.3) | copy-start | bytes 49156
  56.8 3.8 %collective-permute-start.28 = (f32[2,2048]{1,0:T(2,128)S(1)}, f32[2,2048]{1,0:T(2,128)S(1)}, u32[]{:S(2)}, u32[]{:S(2)}) collective-permute-start(f32[2,2048]{1,0:T(2,128)S(1)} %output_products.1), channel_id=1, source_target_pairs={{0,1},{1,0},{2,3},{3,2},{4,5},{5,4},{6,7},{7,6},{8,9},{9,8},{10,11... | collective-permute-start | bytes 49160 | tf_op jit(solution)/shard_map/ppermute | solution.py:43
  60.6 4.7 %collective-permute-start.29 = (f32[2,2048]{1,0:T(2,128)S(1)}, f32[2,2048]{1,0:T(2,128)S(1)}, u32[]{:S(2)}, u32[]{:S(2)}) collective-permute-start(f32[2,2048]{1,0:T(2,128)S(1)} %add.66), channel_id=1, source_target_pairs={{0,2},{1,3},{2,0},{3,1},{4,6},{5,7},{6,4},{7,5},{8,10},{9,11},{10,... | collective-permute-start | bytes 49160 | tf_op jit(solution)/shard_map/ppermute | solution.py:43

commit v15 on v14

--- a/solution.py
+++ b/solution.py
@@ -415,9 +415,10 @@
         received = top
 
     value_second = value_far[1:] + share(value_far[1:], masked)
+    value_total = project(places, rows, value_second, value_total)
 
     blocks = share(value_last, received)
-    value_total = project(places, rows, value_second + value_last, value_total)
+    value_total = project(places, rows, value_last, value_total)
     packed = call(
         functools.partial(weigh_kernel, [d for d, _ in blocks], len(rows), team),
         "weighted_values",

time: 66.1 us -> 64.2 us (0.971)
  waiting for transfers between devices: 23.4 us -> 19.3 us
  starting transfers between devices: 21.9 us -> 23.9 us
    ppermute x19, waiting for transfers between devices: 16.9 us -> 14.4 us  [swap(): return lax.ppermute(value, axis, [(i, i ^ distance) for i in range(count)])]
    ppermute x11, waiting for transfers between devices: 6.48 us -> 4.88 us  [by_core(): return lax.ppermute(value, 'ctx', pairs)]
    ppermute x19, starting transfers between devices: 8.41 us -> 9.81 us  [swap(): return lax.ppermute(value, axis, [(i, i ^ distance) for i in range(count)])]
    pallas_call x5 -> x6, Pallas kernels: 5.99 us -> 6.15 us  [project(): call(functools.partial(project_kernel, [d for d, _ in blocks], len(rows),...]
  transfers between devices with their start and end apart: 30 -> 30, of which waited for: 16 -> 15; matrix products, arithmetic and copies ran while one was open for 1% -> 1% of each run, Pallas kernels for 23% -> 24%
where the time goes in v15:
time: 64.2 us; the launch traced here: 64 us
  starting transfers between devices  23.9 us (37%)
  waiting for transfers between devices  19.3 us (30%)
  Pallas kernels  17.4 us (27%)
  local copies, waits for them, and re-layouts  1.59 us (2%)
  other arithmetic  1.49 us (2%)
    ppermute x19, waiting for transfers between devices, swap(): return lax.ppermute(value, axis, [(i, i ^ distance) for i in range(count)])  14.4 us
    ppermute x11, starting transfers between devices, by_core(): return lax.ppermute(value, 'ctx', pairs)  14.1 us
    ppermute x19, starting transfers between devices, swap(): return lax.ppermute(value, axis, [(i, i ^ distance) for i in range(count)])  9.81 us
    pallas_call x2, Pallas kernels, normalise(): call(functools.partial(norm_kernel, first), 'normalise', [IN_HBM, IN_VMEM...  7.47 us
    pallas_call x6, Pallas kernels, project(): call(functools.partial(project_kernel, [d for d, _ in blocks], len(rows),...  6.15 us
    ppermute x11, waiting for transfers between devices, by_core(): return lax.ppermute(value, 'ctx', pairs)  4.88 us
    unnamed x18, local copies, waits for them, and re-layouts  1.59 us
  transfers between devices with their start and end apart: 30, of which 15 were waited for; matrix products, arithmetic and copies ran while one was open for 1% of the time, Pallas kernels for 24%

profile of v15, /device:TPU:0, one launch (start us, length us, event | category | flops | bytes accessed | tf_op | source)
XLA Modules:
  0.0 64.0 jit_solution(7453695602203234245)
XLA Ops:
  0.0 0.5 collective-permute-start.1
  0.5 0.1 collective-permute-start.2
  0.5 2.9 %collective-permute-start.12 = (bf16[2048,128]{1,0:T(8,128)(2,1)}, bf16[2048,128]{1,0:T(8,128)(2,1)S(1)}, u32[]{:S(2)}, u32[]{:S(2)}) collective-permute-start(bf16[2048,128]{1,0:T(8,128)(2,1)} %bitcast.24), channel_id=1, source_target_pairs={{0,8},{4,20},{8,0},{12,28},{16,24},{20,4},{24,16},{28,12},{1,9},{5... | collective-permute-start | bytes 1572872 | tf_op jit(solution)/shard_map/ppermute | solution.py:64
  3.5 1.6 %collective-permute-start.7 = (bf16[2048,128]{1,0:T(8,128)(2,1)S(1)}, bf16[2048,128]{1,0:T(8,128)(2,1)S(1)}, u32[]{:S(2)}, u32[]{:S(2)}) collective-permute-start(bf16[2048,128]{1,0:T(8,128)(2,1)S(1)} %collective-permute-done.1.refs_6_), channel_id=1, source_target_pairs={{0,8},{4,20},{8,0},{12,28},{16,24},{20,4},{24,16},{28,12},{1,9},{5... | collective-permute-start | bytes 1572872 | tf_op jit(solution)/shard_map/ppermute | solution.py:64
  5.1 0.7 %copy-done.5 = f32[2,2048]{1,0:T(2,128)S(1)} copy-done((f32[2,2048]{1,0:T(2,128)S(1)}, f32[2,2048]{1,0:T(2,128)}, u32[]{:S(2)}) %copy-start.5) | copy-done | bytes 16408
  5.8 0.1 squares.1
  5.9 1.1 %collective-permute-done = f32[2,128]{1,0:T(2,128)S(1)} collective-permute-done((f32[2,128]{1,0:T(2,128)S(1)}, f32[2,128]{1,0:T(2,128)S(1)}, u32[]{:S(2)}, u32[]{:S(2)}) %collective-permute-start) | collective-permute-done | bytes 1056 | tf_op jit(solution)/shard_map/ppermute | solution.py:43
  7.0 0.0 collective-permute-done.2.refs_6_
  7.0 1.5 %collective-permute-start.3 = (f32[2,128]{1,0:T(2,128)S(1)}, f32[2,128]{1,0:T(2,128)S(1)}, u32[]{:S(2)}, u32[]{:S(2)}) collective-permute-start(f32[2,128]{1,0:T(2,128)S(1)} %add.53), channel_id=1, source_target_pairs={{0,16},{4,12},{8,24},{12,4},{16,0},{20,28},{24,8},{28,20},{1,17},{... | collective-permute-start | bytes 3080 | tf_op jit(solution)/shard_map/ppermute | solution.py:64
  8.5 0.8 %copy-done.4 = f32[1,16384]{1,0:T(1,128)S(1)} copy-done((f32[1,16384]{1,0:T(1,128)S(1)}, f32[1,16384]{1,0:T(1,128)}, u32[]{:S(2)}) %copy-start.4) | copy-done | bytes 65560
  9.4 3.2 %normalise.2 = (bf16[8,64,2048]{2,1,0:T(8,128)(2,1)S(1)}, bf16[8,64,2048]{2,1,0:T(8,128)(2,1)S(1)}) custom-call(bf16[320,16384]{1,0:T(8,128)(2,1)} %bitcast.35, f32[8,1,2048]{2,1,0:T(1,128)S(1)} %bitcast.31), custom_call_target="tpu_custom_call" | custom-call | flops 1000 | bytes 1000 | tf_op jit(solution)/shard_map/normalise/pallas_call | solution.py:173
  12.6 0.1 collective-permute-start.4
  12.7 0.6 collective-permute-start.5
  13.3 0.5 collective-permute-done.4
  13.8 0.2 collective-permute-start.13
  14.0 0.9 %collective-permute-start.6 = (f32[2,128]{1,0:T(2,128)S(1)}, f32[2,128]{1,0:T(2,128)S(1)}, u32[]{:S(2)}, u32[]{:S(2)}) collective-permute-start(f32[2,128]{1,0:T(2,128)S(1)} %collective-permute-done.4), channel_id=1, source_target_pairs={{0,16},{4,12},{8,24},{12,4},{16,0},{20,28},{24,8},{28,20},{1,17},{... | collective-permute-start | bytes 3080 | tf_op jit(solution)/shard_map/ppermute | solution.py:64
  14.9 4.3 %normalise.3 = (bf16[8,64,2048]{2,1,0:T(8,128)(2,1)S(1)}, bf16[8,64,2048]{2,1,0:T(8,128)(2,1)S(1)}, bf16[8,64,2048]{2,1,0:T(8,128)(2,1)S(1)}) custom-call(bf16[320,16384]{1,0:T(8,128)(2,1)} %bitcast.36, f32[8,1,2048]{2,1,0:T(1,128)S(1)} %bitcast.32), custom_call_target="tpu_custom_call" | custom-call | flops 1000 | bytes 1000 | tf_op jit(solution)/shard_map/normalise/pallas_call | solution.py:173
  19.3 0.0 copy-start.8
  19.3 0.8 %query_products.1 = f32[2,10,128]{2,1,0:T(8,128)S(1)} custom-call(s32[1]{0:T(128)} %bitcast.place_ref, f32[2,128]{1,0:T(2,128)S(1)} %add_add_fusion.2.squares_ref, f32[2,2048]{1,0:T(2,128)S(1)} %copy-done.5, f32[8,1,2048]{2,1,0:T(1,128)S(1)} %bitcast.33, bf16[2048,1024]{1,0:T(8,128)(2,1)S(1)} %bitcast.21, bf16[2048,128]{1,0:T(8,128)(2,1)S(1)} %bitcast.25, ...), custom_call_target="tpu_custom_call" | custom-call | flops 1000 | bytes 1000 | tf_op jit(solution)/shard_map/query_products/pallas_call | solution.py:371
  20.1 0.1 collective-permute-start.8
  20.3 0.5 collective-permute-start.15
  20.8 0.0 collective-permute-done.13.refs_7_
  20.8 0.8 %collective-permute-start.14 = (bf16[2048,128]{1,0:T(8,128)(2,1)S(1)}, bf16[2048,128]{1,0:T(8,128)(2,1)S(1)}, u32[]{:S(2)}, u32[]{:S(2)}) collective-permute-start(bf16[2048,128]{1,0:T(8,128)(2,1)S(1)} %collective-permute-done.13.refs_7_), channel_id=1, source_target_pairs={{0,8},{4,20},{8,0},{12,28},{16,24},{20,4},{24,16},{28,12},{1,9},{5... | collective-permute-start | bytes 1572872 | tf_op jit(solution)/shard_map/ppermute | solution.py:64
  21.6 1.2 %collective-permute-start.9 = (f32[2,10,128]{2,1,0:T(8,128)S(1)}, f32[2,10,128]{2,1,0:T(8,128)S(1)}, u32[]{:S(2)}, u32[]{:S(2)}) collective-permute-start(f32[2,10,128]{2,1,0:T(8,128)S(1)} %add.57), channel_id=1, source_target_pairs={{0,16},{4,12},{8,24},{12,4},{16,0},{20,28},{24,8},{28,20},{1,17},{... | collective-permute-start | bytes 30728 | tf_op jit(solution)/shard_map/ppermute | solution.py:64
  22.8 2.8 %collective-permute-done.9 = f32[2,10,128]{2,1,0:T(8,128)S(1)} collective-permute-done((f32[2,10,128]{2,1,0:T(8,128)S(1)}, f32[2,10,128]{2,1,0:T(8,128)S(1)}, u32[]{:S(2)}, u32[]{:S(2)}) %collective-permute-start.9) | collective-permute-done | bytes 10272 | tf_op jit(solution)/shard_map/ppermute | solution.py:64
  25.7 0.6 %multiply_sine_fusion = (f32[320,64]{1,0:T(8,128)S(1)}, f32[320,64]{1,0:T(8,128)S(1)}) fusion(f32[64]{0:T(128)S(1)} %multiply_exponential_fusion, f32[320]{0:T(512)S(1)} %add_convert_fusion), kind=kLoop, calls=%fused_computation | loop fusion | flops 20480 | bytes 165376 | tf_op jit(solution)/shard_map/sin | solution.py:97
  26.3 0.6 collective-permute-start.17
  26.9 0.1 multiply_sine_fusion.1
  27.0 1.3 %collective-permute-start.20 = (bf16[2048,128]{1,0:T(8,128)(2,1)S(1)}, bf16[2048,128]{1,0:T(8,128)(2,1)S(1)}, u32[]{:S(2)}, u32[]{:S(2)}) collective-permute-start(bf16[2048,128]{1,0:T(8,128)(2,1)S(1)} %collective-permute-done.2.refs_6_), channel_id=1, source_target_pairs={{0,8},{4,20},{8,0},{12,28},{16,24},{20,4},{24,16},{28,12},{1,9},{5... | collective-permute-start | bytes 1572872 | tf_op jit(solution)/shard_map/ppermute | solution.py:64
  28.3 0.9 %project.6.refs_9_ = f32[320,128]{1,0:T(8,128)S(1)} custom-call(s32[1]{0:T(128)} %bitcast.place_ref, bf16[8,64,2048]{2,1,0:T(8,128)(2,1)S(1)} %get-tuple-element.35.refs_0_, bf16[8,64,2048]{2,1,0:T(8,128)(2,1)S(1)} %get-tuple-element.36.refs_1_, bf16[8,64,2048]{2,1,0:T(8,128)(2,1)S(1)} %get-tuple-element.39.refs_2_, ...), custom_call_target="tpu_custom_call" | custom-call | flops 1000 | bytes 1000 | tf_op jit(solution)/shard_map/project/pallas_call | solution.py:218
  29.2 1.2 %collective-permute-start.18 = (f32[2,10,128]{2,1,0:T(8,128)S(1)}, f32[2,10,128]{2,1,0:T(8,128)S(1)}, u32[]{:S(2)}, u32[]{:S(2)}) collective-permute-start(f32[2,10,128]{2,1,0:T(8,128)S(1)} %collective-permute-done.17), channel_id=1, source_target_pairs={{0,16},{4,12},{8,24},{12,4},{16,0},{20,28},{24,8},{28,20},{1,17},{... | collective-permute-start | bytes 30728 | tf_op jit(solution)/shard_map/ppermute | solution.py:64
  30.3 1.5 %project.7.refs_7_ = f32[320,128]{1,0:T(8,128)S(1)} custom-call(s32[1]{0:T(128)} %bitcast.place_ref, bf16[8,64,2048]{2,1,0:T(8,128)(2,1)S(1)} %get-tuple-element.35.refs_0_, bf16[8,64,2048]{2,1,0:T(8,128)(2,1)S(1)} %get-tuple-element.36.refs_1_, bf16[8,64,2048]{2,1,0:T(8,128)(2,1)S(1)} %get-tuple-element.39.refs_2_, ...), custom_call_target="tpu_custom_call" | custom-call | flops 1000 | bytes 1000 | tf_op jit(solution)/shard_map/project/pallas_call | solution.py:218
  31.9 0.1 collective-permute-start.16
  32.0 0.9 %collective-permute-start.11 = (bf16[2048,128]{1,0:T(8,128)(2,1)S(1)}, bf16[2048,128]{1,0:T(8,128)(2,1)S(1)}, u32[]{:S(2)}, u32[]{:S(2)}) collective-permute-start(bf16[2048,128]{1,0:T(8,128)(2,1)S(1)} %collective-permute-done.10.refs_7_), channel_id=1, source_target_pairs={{0,8},{4,20},{8,0},{12,28},{16,24},{20,4},{24,16},{28,12},{1,9},{5... | collective-permute-start | bytes 1572872 | tf_op jit(solution)/shard_map/ppermute | solution.py:64
  32.9 0.3 collective-permute-done.18
  33.2 0.0 copy-start.7
  33.2 0.6 collective-permute-done.16.refs_6_
  33.9 0.9 %project.8.refs_0_ = f32[320,128]{1,0:T(8,128)S(1)} custom-call(s32[1]{0:T(128)} %bitcast.place_ref, bf16[8,64,2048]{2,1,0:T(8,128)(2,1)S(1)} %get-tuple-element.35.refs_0_, bf16[8,64,2048]{2,1,0:T(8,128)(2,1)S(1)} %get-tuple-element.36.refs_1_, bf16[8,64,2048]{2,1,0:T(8,128)(2,1)S(1)} %get-tuple-element.39.refs_2_, ...), custom_call_target="tpu_custom_call" | custom-call | flops 1000 | bytes 1000 | tf_op jit(solution)/shard_map/project/pallas_call | solution.py:218
  34.7 1.0 %scores.1 = (f32[8,320]{1,0:T(8,128)S(1)}, f32[8,128]{1,0:T(8,128)S(1)}, f32[8,128]{1,0:T(8,128)S(1)}) custom-call(s32[1]{0:T(128)} %bitcast.place_ref, s32[2]{0:T(128)S(1)} %copy-done.7, f32[320,128]{1,0:T(8,128)S(1)} %project.8.refs_0_, f32[320,64]{1,0:T(8,128)S(1)} %get-tuple-element.60.refs_1_, f32[320,64]{1,0:T(8,128)S(1)} %get-tuple-element.59.refs_2_, ...), custom_call_target="tpu_custom_call" | custom-call | flops 1000 | bytes 1000 | tf_op jit(solution)/shard_map/scores/pallas_call | solution.py:397
  35.7 0.7 %collective-permute-done.20.refs_5_ = bf16[2048,128]{1,0:T(8,128)(2,1)S(1)} collective-permute-done((bf16[2048,128]{1,0:T(8,128)(2,1)S(1)}, bf16[2048,128]{1,0:T(8,128)(2,1)S(1)}, u32[]{:S(2)}, u32[]{:S(2)}) %collective-permute-start.20) | collective-permute-done | bytes 524320 | tf_op jit(solution)/shard_map/ppermute | solution.py:64
  36.4 0.5 collective-permute-start.19
  36.9 1.4 %collective-permute-done.19 = f32[8,128]{1,0:T(8,128)S(1)} collective-permute-done((f32[8,128]{1,0:T(8,128)S(1)}, f32[8,128]{1,0:T(8,128)S(1)}, u32[]{:S(2)}, u32[]{:S(2)}) %collective-permute-start.19) | collective-permute-done | bytes 4128 | tf_op jit(solution)/shard_map/ppermute | solution.py:43
  38.4 1.1 %collective-permute-start.21 = (f32[8,128]{1,0:T(8,128)S(1)}, f32[8,128]{1,0:T(8,128)S(1)}, u32[]{:S(2)}, u32[]{:S(2)}) collective-permute-start(f32[8,128]{1,0:T(8,128)S(1)} %max.6), channel_id=1, source_target_pairs={{0,16},{4,12},{8,24},{12,4},{16,0},{20,28},{24,8},{28,20},{1,17},{... | collective-permute-start | bytes 12296 | tf_op jit(solution)/shard_map/ppermute | solution.py:64
  39.5 1.5 %project.9.refs_7_ = f32[320,128]{1,0:T(8,128)S(1)} custom-call(s32[1]{0:T(128)} %bitcast.place_ref, bf16[8,64,2048]{2,1,0:T(8,128)(2,1)S(1)} %get-tuple-element.35.refs_0_, bf16[8,64,2048]{2,1,0:T(8,128)(2,1)S(1)} %get-tuple-element.36.refs_1_, bf16[8,64,2048]{2,1,0:T(8,128)(2,1)S(1)} %get-tuple-element.39.refs_2_, ...), custom_call_target="tpu_custom_call" | custom-call | flops 1000 | bytes 1000 | tf_op jit(solution)/shard_map/project/pallas_call | solution.py:218
  41.1 0.9 %collective-permute-done.21 = f32[8,128]{1,0:T(8,128)S(1)} collective-permute-done((f32[8,128]{1,0:T(8,128)S(1)}, f32[8,128]{1,0:T(8,128)S(1)}, u32[]{:S(2)}, u32[]{:S(2)}) %collective-permute-start.21) | collective-permute-done | bytes 4128 | tf_op jit(solution)/shard_map/ppermute | solution.py:64
  42.0 0.1 collective-permute-done.11.refs_5_
  42.1 0.5 collective-permute-start.24
  42.6 0.9 %project.10.refs_6_ = f32[320,128]{1,0:T(8,128)S(1)} custom-call(s32[1]{0:T(128)} %bitcast.place_ref, bf16[8,64,2048]{2,1,0:T(8,128)(2,1)S(1)} %get-tuple-element.35.refs_0_, bf16[8,64,2048]{2,1,0:T(8,128)(2,1)S(1)} %get-tuple-element.36.refs_1_, bf16[8,64,2048]{2,1,0:T(8,128)(2,1)S(1)} %get-tuple-element.39.refs_2_, ...), custom_call_target="tpu_custom_call" | custom-call | flops 1000 | bytes 1000 | tf_op jit(solution)/shard_map/project/pallas_call | solution.py:218
  43.5 0.5 collective-permute-done.24
  44.0 0.5 project.11.refs_6_
  44.5 0.0 copy-start.1
  44.6 1.2 %weighted_values.1 = f32[8,256]{1,0:T(8,128)S(1)} custom-call(s32[1]{0:T(128)} %bitcast.place_ref, s32[2]{0:T(128)S(1)} %copy-done.7, bf16[8,64,2048]{2,1,0:T(8,128)(2,1)S(1)} %get-tuple-element.35.refs_0_, bf16[8,64,2048]{2,1,0:T(8,128)(2,1)S(1)} %get-tuple-element.36.refs_1_, bf16[8,64,2048]{2,1,0:T(8,128)(2,1)S(1)} %get-tuple-element.39.refs_2_, ...), custom_call_target="tpu_custom_call" | custom-call | flops 1000 | bytes 1000 | tf_op jit(solution)/shard_map/weighted_values/pallas_call | solution.py:422
  45.7 0.1 collective-permute-start.25
  45.9 1.0 %collective-permute-done.25 = f32[8,256]{1,0:T(8,128)S(1)} collective-permute-done((f32[8,256]{1,0:T(8,128)S(1)}, f32[8,256]{1,0:T(8,128)S(1)}, u32[]{:S(2)}, u32[]{:S(2)}) %collective-permute-start.25) | collective-permute-done | bytes 8224 | tf_op jit(solution)/shard_map/ppermute | solution.py:43
  46.9 1.2 %collective-permute-start.26 = (f32[8,256]{1,0:T(8,128)S(1)}, f32[8,256]{1,0:T(8,128)S(1)}, u32[]{:S(2)}, u32[]{:S(2)}) collective-permute-start(f32[8,256]{1,0:T(8,128)S(1)} %add.64), channel_id=1, source_target_pairs={{0,8},{4,12},{8,0},{12,4},{16,24},{20,28},{24,16},{28,20},{1,9},{5... | collective-permute-start | bytes 24584 | tf_op jit(solution)/shard_map/ppermute | solution.py:43
  48.1 2.4 %collective-permute-done.26 = f32[8,256]{1,0:T(8,128)S(1)} collective-permute-done((f32[8,256]{1,0:T(8,128)S(1)}, f32[8,256]{1,0:T(8,128)S(1)}, u32[]{:S(2)}, u32[]{:S(2)}) %collective-permute-start.26) | collective-permute-done | bytes 8224 | tf_op jit(solution)/shard_map/ppermute | solution.py:43
  50.6 1.1 %collective-permute-start.27 = (f32[8,256]{1,0:T(8,128)S(1)}, f32[8,256]{1,0:T(8,128)S(1)}, u32[]{:S(2)}, u32[]{:S(2)}) collective-permute-start(f32[8,256]{1,0:T(8,128)S(1)} %add.65.mine_ref), channel_id=1, source_target_pairs={{0,16},{4,20},{8,24},{12,28},{16,0},{20,4},{24,8},{28,12},{1,17},{... | collective-permute-start | bytes 24584 | tf_op jit(solution)/shard_map/ppermute | solution.py:43
  51.7 2.5 %collective-permute-done.27.other_ref = f32[8,256]{1,0:T(8,128)S(1)} collective-permute-done((f32[8,256]{1,0:T(8,128)S(1)}, f32[8,256]{1,0:T(8,128)S(1)}, u32[]{:S(2)}, u32[]{:S(2)}) %collective-permute-start.27) | collective-permute-done | bytes 8224 | tf_op jit(solution)/shard_map/ppermute | solution.py:43
  54.2 0.6 %output_products.1 = f32[2,2048]{1,0:T(2,128)S(1)} custom-call(s32[1]{0:T(128)} %bitcast.place_ref, f32[8,256]{1,0:T(8,128)S(1)} %add.65.mine_ref, f32[8,256]{1,0:T(8,128)S(1)} %collective-permute-done.27.other_ref, bf16[1024,2048]{1,0:T(8,128)(2,1)S(1)} %bitcast.22), custom_call_target="tpu_custom_call" | custom-call | flops 1000 | bytes 1000 | tf_op jit(solution)/shard_map/output_products/pallas_call | solution.py:440
  54.9 1.6 %collective-permute-start.28 = (f32[2,2048]{1,0:T(2,128)S(1)}, f32[2,2048]{1,0:T(2,128)S(1)}, u32[]{:S(2)}, u32[]{:S(2)}) collective-permute-start(f32[2,2048]{1,0:T(2,128)S(1)} %output_products.1), channel_id=1, source_target_pairs={{0,1},{1,0},{2,3},{3,2},{4,5},{5,4},{6,7},{7,6},{8,9},{9,8},{10,11... | collective-permute-start | bytes 49160 | tf_op jit(solution)/shard_map/ppermute | solution.py:43
  56.5 2.2 %collective-permute-done.28 = f32[2,2048]{1,0:T(2,128)S(1)} collective-permute-done((f32[2,2048]{1,0:T(2,128)S(1)}, f32[2,2048]{1,0:T(2,128)S(1)}, u32[]{:S(2)}, u32[]{:S(2)}) %collective-permute-start.28) | collective-permute-done | bytes 16416 | tf_op jit(solution)/shard_map/ppermute | solution.py:43
  58.6 2.7 %collective-permute-start.29 = (f32[2,2048]{1,0:T(2,128)S(1)}, f32[2,2048]{1,0:T(2,128)S(1)}, u32[]{:S(2)}, u32[]{:S(2)}) collective-permute-start(f32[2,2048]{1,0:T(2,128)S(1)} %add.66), channel_id=1, source_target_pairs={{0,2},{1,3},{2,0},{3,1},{4,6},{5,7},{6,4},{7,5},{8,10},{9,11},{10,... | collective-permute-start | bytes 49160 | tf_op jit(solution)/shard_map/ppermute | solution.py:43
  61.3 2.1 %collective-permute-done.29 = f32[2,2048]{1,0:T(2,128)S(1)} collective-permute-done((f32[2,2048]{1,0:T(2,128)S(1)}, f32[2,2048]{1,0:T(2,128)S(1)}, u32[]{:S(2)}, u32[]{:S(2)}) %collective-permute-start.29) | collective-permute-done | bytes 16416 | tf_op jit(solution)/shard_map/ppermute | solution.py:43
  63.3 0.6 add_add_fusion
  (46 shorter events, 0.2 us)
Async XLA Ops:
  0.0 3.5 %collective-permute-start.1 = (bf16[2048,128]{1,0:T(8,128)(2,1)}, bf16[2048,128]{1,0:T(8,128)(2,1)S(1)}, u32[]{:S(2)}, u32[]{:S(2)}) collective-permute-start(bf16[2048,128]{1,0:T(8,128)(2,1)} %bitcast.23), channel_id=1, source_target_pairs={{0,4},{4,0},{8,12},{12,8},{16,20},{20,16},{24,28},{28,24},{1,5},{5... | collective-permute-start | bytes 1572872 | tf_op jit(solution)/shard_map/ppermute | solution.py:43
  0.5 6.6 %collective-permute-start.2 = (bf16[2048,128]{1,0:T(8,128)(2,1)}, bf16[2048,128]{1,0:T(8,128)(2,1)S(1)}, u32[]{:S(2)}, u32[]{:S(2)}) collective-permute-start(bf16[2048,128]{1,0:T(8,128)(2,1)} %bitcast.27), channel_id=1, source_target_pairs={{0,4},{4,0},{8,12},{12,8},{16,20},{20,16},{24,28},{28,24},{1,5},{5... | collective-permute-start | bytes 1572872 | tf_op jit(solution)/shard_map/ppermute | solution.py:43
  0.5 12.8 %collective-permute-start.12 = (bf16[2048,128]{1,0:T(8,128)(2,1)}, bf16[2048,128]{1,0:T(8,128)(2,1)S(1)}, u32[]{:S(2)}, u32[]{:S(2)}) collective-permute-start(bf16[2048,128]{1,0:T(8,128)(2,1)} %bitcast.24), channel_id=1, source_target_pairs={{0,8},{4,20},{8,0},{12,28},{16,24},{20,4},{24,16},{28,12},{1,9},{5... | collective-permute-start | bytes 1572872 | tf_op jit(solution)/shard_map/ppermute | solution.py:64
  3.5 15.8 %collective-permute-start.7 = (bf16[2048,128]{1,0:T(8,128)(2,1)S(1)}, bf16[2048,128]{1,0:T(8,128)(2,1)S(1)}, u32[]{:S(2)}, u32[]{:S(2)}) collective-permute-start(bf16[2048,128]{1,0:T(8,128)(2,1)S(1)} %collective-permute-done.1.refs_6_), channel_id=1, source_target_pairs={{0,8},{4,20},{8,0},{12,28},{16,24},{20,4},{24,16},{28,12},{1,9},{5... | collective-permute-start | bytes 1572872 | tf_op jit(solution)/shard_map/ppermute | solution.py:64
  5.1 0.7 %copy-start.5 = (f32[2,2048]{1,0:T(2,128)S(1)}, f32[2,2048]{1,0:T(2,128)}, u32[]{:S(2)}) copy-start(f32[2,2048]{1,0:T(2,128)} %tokens_ref.3) | copy-start | bytes 49156
  5.9 1.1 %collective-permute-start = (f32[2,128]{1,0:T(2,128)S(1)}, f32[2,128]{1,0:T(2,128)S(1)}, u32[]{:S(2)}, u32[]{:S(2)}) collective-permute-start(f32[2,128]{1,0:T(2,128)S(1)} %get-tuple-element.32), channel_id=1, source_target_pairs={{0,4},{4,0},{8,12},{12,8},{16,20},{20,16},{24,28},{28,24},{1,5},{5... | collective-permute-start | bytes 3080 | tf_op jit(solution)/shard_map/ppermute | solution.py:43
  7.0 5.6 %collective-permute-start.3 = (f32[2,128]{1,0:T(2,128)S(1)}, f32[2,128]{1,0:T(2,128)S(1)}, u32[]{:S(2)}, u32[]{:S(2)}) collective-permute-start(f32[2,128]{1,0:T(2,128)S(1)} %add.53), channel_id=1, source_target_pairs={{0,16},{4,12},{8,24},{12,4},{16,0},{20,28},{24,8},{28,20},{1,17},{... | collective-permute-start | bytes 3080 | tf_op jit(solution)/shard_map/ppermute | solution.py:64
  8.5 0.8 %copy-start.4 = (f32[1,16384]{1,0:T(1,128)S(1)}, f32[1,16384]{1,0:T(1,128)}, u32[]{:S(2)}) copy-start(f32[1,16384]{1,0:T(1,128)} %param.11) | copy-start | bytes 196612
  9.4 3.3 %copy-start.3 = (bf16[1,2048,128]{2,1,0:T(8,128)(2,1)S(1)}, bf16[1,2048,128]{2,1,0:T(8,128)(2,1)}, u32[]{:S(2)}) copy-start(bf16[1,2048,128]{2,1,0:T(8,128)(2,1)} %param.14) | copy-start | bytes 1572868
  12.6 1.2 %collective-permute-start.4 = (f32[2,128]{1,0:T(2,128)S(1)}, f32[2,128]{1,0:T(2,128)S(1)}, u32[]{:S(2)}, u32[]{:S(2)}) collective-permute-start(f32[2,128]{1,0:T(2,128)S(1)} %collective-permute-done.3), channel_id=1, source_target_pairs={{0,4},{4,0},{8,12},{12,8},{16,20},{20,16},{24,28},{28,24},{1,5},{5... | collective-permute-start | bytes 3080 | tf_op jit(solution)/shard_map/ppermute | solution.py:43
  12.7 10.2 %collective-permute-start.5 = (bf16[2048,128]{1,0:T(8,128)(2,1)S(1)}, bf16[2048,128]{1,0:T(8,128)(2,1)S(1)}, u32[]{:S(2)}, u32[]{:S(2)}) collective-permute-start(bf16[2048,128]{1,0:T(8,128)(2,1)S(1)} %bitcast.28), channel_id=1, source_target_pairs={{0,8},{4,20},{8,0},{12,28},{16,24},{20,4},{24,16},{28,12},{1,9},{5... | collective-permute-start | bytes 1572872 | tf_op jit(solution)/shard_map/ppermute | solution.py:64
  13.8 7.0 %collective-permute-start.13 = (bf16[2048,128]{1,0:T(8,128)(2,1)S(1)}, bf16[2048,128]{1,0:T(8,128)(2,1)S(1)}, u32[]{:S(2)}, u32[]{:S(2)}) collective-permute-start(bf16[2048,128]{1,0:T(8,128)(2,1)S(1)} %collective-permute-done.12.refs_5_), channel_id=1, source_target_pairs={{0,4},{4,0},{8,12},{12,8},{16,20},{20,16},{24,28},{28,24},{1,5},{5... | collective-permute-start | bytes 1572872 | tf_op jit(solution)/shard_map/ppermute | solution.py:43
  14.0 5.2 %collective-permute-start.6 = (f32[2,128]{1,0:T(2,128)S(1)}, f32[2,128]{1,0:T(2,128)S(1)}, u32[]{:S(2)}, u32[]{:S(2)}) collective-permute-start(f32[2,128]{1,0:T(2,128)S(1)} %collective-permute-done.4), channel_id=1, source_target_pairs={{0,16},{4,12},{8,24},{12,4},{16,0},{20,28},{24,8},{28,20},{1,17},{... | collective-permute-start | bytes 3080 | tf_op jit(solution)/shard_map/ppermute | solution.py:64
  14.9 4.3 %copy-start = (bf16[1,2048,1024]{2,1,0:T(8,128)(2,1)S(1)}, bf16[1,2048,1024]{2,1,0:T(8,128)(2,1)}, u32[]{:S(2)}) copy-start(bf16[1,2048,1024]{2,1,0:T(8,128)(2,1)} %param.12) | copy-start | bytes 12582916
  14.9 4.3 %copy-start.2 = (bf16[1,2048,128]{2,1,0:T(8,128)(2,1)S(1)}, bf16[1,2048,128]{2,1,0:T(8,128)(2,1)}, u32[]{:S(2)}) copy-start(bf16[1,2048,128]{2,1,0:T(8,128)(2,1)} %param.13) | copy-start | bytes 1572868
  19.3 7.0 %copy-start.8 = (s32[2]{0:T(128)S(1)}, s32[2]{0:T(128)}, u32[]{:S(2)}) copy-start(s32[2]{0:T(128)} %param.17) | copy-start | bytes 28
  20.1 1.5 %collective-permute-start.8 = (f32[2,10,128]{2,1,0:T(8,128)S(1)}, f32[2,10,128]{2,1,0:T(8,128)S(1)}, u32[]{:S(2)}, u32[]{:S(2)}) collective-permute-start(f32[2,10,128]{2,1,0:T(8,128)S(1)} %query_products.1), channel_id=1, source_target_pairs={{0,4},{4,0},{8,12},{12,8},{16,20},{20,16},{24,28},{28,24},{1,5},{5... | collective-permute-start | bytes 30728 | tf_op jit(solution)/shard_map/ppermute | solution.py:43
  20.3 10.0 %collective-permute-start.15 = (bf16[2048,128]{1,0:T(8,128)(2,1)S(1)}, bf16[2048,128]{1,0:T(8,128)(2,1)S(1)}, u32[]{:S(2)}, u32[]{:S(2)}) collective-permute-start(bf16[2048,128]{1,0:T(8,128)(2,1)S(1)} %collective-permute-done.7.refs_6_), channel_id=1, source_target_pairs={{0,4},{4,0},{8,12},{12,8},{16,20},{20,16},{24,28},{28,24},{1,5},{5... | collective-permute-start | bytes 1572872 | tf_op jit(solution)/shard_map/ppermute | solution.py:43
  20.8 11.1 %collective-permute-start.14 = (bf16[2048,128]{1,0:T(8,128)(2,1)S(1)}, bf16[2048,128]{1,0:T(8,128)(2,1)S(1)}, u32[]{:S(2)}, u32[]{:S(2)}) collective-permute-start(bf16[2048,128]{1,0:T(8,128)(2,1)S(1)} %collective-permute-done.13.refs_7_), channel_id=1, source_target_pairs={{0,8},{4,20},{8,0},{12,28},{16,24},{20,4},{24,16},{28,12},{1,9},{5... | collective-permute-start | bytes 1572872 | tf_op jit(solution)/shard_map/ppermute | solution.py:64
  21.6 4.0 %collective-permute-start.9 = (f32[2,10,128]{2,1,0:T(8,128)S(1)}, f32[2,10,128]{2,1,0:T(8,128)S(1)}, u32[]{:S(2)}, u32[]{:S(2)}) collective-permute-start(f32[2,10,128]{2,1,0:T(8,128)S(1)} %add.57), channel_id=1, source_target_pairs={{0,16},{4,12},{8,24},{12,4},{16,0},{20,28},{24,8},{28,20},{1,17},{... | collective-permute-start | bytes 30728 | tf_op jit(solution)/shard_map/ppermute | solution.py:64
  25.7 6.3 %collective-permute-start.10 = (bf16[2048,128]{1,0:T(8,128)(2,1)S(1)}, bf16[2048,128]{1,0:T(8,128)(2,1)S(1)}, u32[]{:S(2)}, u32[]{:S(2)}) collective-permute-start(bf16[2048,128]{1,0:T(8,128)(2,1)S(1)} %collective-permute-done.5.refs_8_), channel_id=1, source_target_pairs={{0,4},{4,0},{8,12},{12,8},{16,20},{20,16},{24,28},{28,24},{1,5},{5... | collective-permute-start | bytes 1572872 | tf_op jit(solution)/shard_map/ppermute | solution.py:43
  26.3 2.8 %collective-permute-start.17 = (f32[2,10,128]{2,1,0:T(8,128)S(1)}, f32[2,10,128]{2,1,0:T(8,128)S(1)}, u32[]{:S(2)}, u32[]{:S(2)}) collective-permute-start(f32[2,10,128]{2,1,0:T(8,128)S(1)} %collective-permute-done.9), channel_id=1, source_target_pairs={{0,4},{4,0},{8,12},{12,8},{16,20},{20,16},{24,28},{28,24},{1,5},{5... | collective-permute-start | bytes 30728 | tf_op jit(solution)/shard_map/ppermute | solution.py:43
  27.0 9.4 %collective-permute-start.20 = (bf16[2048,128]{1,0:T(8,128)(2,1)S(1)}, bf16[2048,128]{1,0:T(8,128)(2,1)S(1)}, u32[]{:S(2)}, u32[]{:S(2)}) collective-permute-start(bf16[2048,128]{1,0:T(8,128)(2,1)S(1)} %collective-permute-done.2.refs_6_), channel_id=1, source_target_pairs={{0,8},{4,20},{8,0},{12,28},{16,24},{20,4},{24,16},{28,12},{1,9},{5... | collective-permute-start | bytes 1572872 | tf_op jit(solution)/shard_map/ppermute | solution.py:64
  29.2 4.0 %collective-permute-start.18 = (f32[2,10,128]{2,1,0:T(8,128)S(1)}, f32[2,10,128]{2,1,0:T(8,128)S(1)}, u32[]{:S(2)}, u32[]{:S(2)}) collective-permute-start(f32[2,10,128]{2,1,0:T(8,128)S(1)} %collective-permute-done.17), channel_id=1, source_target_pairs={{0,16},{4,12},{8,24},{12,4},{16,0},{20,28},{24,8},{28,20},{1,17},{... | collective-permute-start | bytes 30728 | tf_op jit(solution)/shard_map/ppermute | solution.py:64
  31.9 2.0 %collective-permute-start.16 = (bf16[2048,128]{1,0:T(8,128)(2,1)S(1)}, bf16[2048,128]{1,0:T(8,128)(2,1)S(1)}, u32[]{:S(2)}, u32[]{:S(2)}) collective-permute-start(bf16[2048,128]{1,0:T(8,128)(2,1)S(1)} %collective-permute-done.14.refs_5_), channel_id=1, source_target_pairs={{0,4},{4,0},{8,12},{12,8},{16,20},{20,16},{24,28},{28,24},{1,5},{5... | collective-permute-start | bytes 1572872 | tf_op jit(solution)/shard_map/ppermute | solution.py:43
  32.0 10.1 %collective-permute-start.11 = (bf16[2048,128]{1,0:T(8,128)(2,1)S(1)}, bf16[2048,128]{1,0:T(8,128)(2,1)S(1)}, u32[]{:S(2)}, u32[]{:S(2)}) collective-permute-start(bf16[2048,128]{1,0:T(8,128)(2,1)S(1)} %collective-permute-done.10.refs_7_), channel_id=1, source_target_pairs={{0,8},{4,20},{8,0},{12,28},{16,24},{20,4},{24,16},{28,12},{1,9},{5... | collective-permute-start | bytes 1572872 | tf_op jit(solution)/shard_map/ppermute | solution.py:64
  33.2 1.5 %copy-start.7 = (s32[2]{0:T(128)S(1)}, s32[2]{0:T(128)}, u32[]{:S(2)}) copy-start(s32[2]{0:T(128)} %lengths_ref.3) | copy-start | bytes 28
  36.4 6.2 %collective-permute-start.23 = (bf16[2048,128]{1,0:T(8,128)(2,1)S(1)}, bf16[2048,128]{1,0:T(8,128)(2,1)S(1)}, u32[]{:S(2)}, u32[]{:S(2)}) collective-permute-start(bf16[2048,128]{1,0:T(8,128)(2,1)S(1)} %collective-permute-done.20.refs_5_), channel_id=1, source_target_pairs={{0,4},{4,0},{8,12},{12,8},{16,20},{20,16},{24,28},{28,24},{1,5},{5... | collective-permute-start | bytes 1572872 | tf_op jit(solution)/shard_map/ppermute | solution.py:43
  36.4 1.9 %collective-permute-start.19 = (f32[8,128]{1,0:T(8,128)S(1)}, f32[8,128]{1,0:T(8,128)S(1)}, u32[]{:S(2)}, u32[]{:S(2)}) collective-permute-start(f32[8,128]{1,0:T(8,128)S(1)} %get-tuple-element.51), channel_id=1, source_target_pairs={{0,4},{4,0},{8,12},{12,8},{16,20},{20,16},{24,28},{28,24},{1,5},{5... | collective-permute-start | bytes 12296 | tf_op jit(solution)/shard_map/ppermute | solution.py:43
  38.4 3.6 %collective-permute-start.21 = (f32[8,128]{1,0:T(8,128)S(1)}, f32[8,128]{1,0:T(8,128)S(1)}, u32[]{:S(2)}, u32[]{:S(2)}) collective-permute-start(f32[8,128]{1,0:T(8,128)S(1)} %max.6), channel_id=1, source_target_pairs={{0,16},{4,12},{8,24},{12,4},{16,0},{20,28},{24,8},{28,20},{1,17},{... | collective-permute-start | bytes 12296 | tf_op jit(solution)/shard_map/ppermute | solution.py:64
  42.1 2.4 %collective-permute-start.22 = (bf16[2048,128]{1,0:T(8,128)(2,1)S(1)}, bf16[2048,128]{1,0:T(8,128)(2,1)S(1)}, u32[]{:S(2)}, u32[]{:S(2)}) collective-permute-start(bf16[2048,128]{1,0:T(8,128)(2,1)S(1)} %collective-permute-done.11.refs_5_), channel_id=1, source_target_pairs={{0,4},{4,0},{8,12},{12,8},{16,20},{20,16},{24,28},{28,24},{1,5},{5... | collective-permute-start | bytes 1572872 | tf_op jit(solution)/shard_map/ppermute | solution.py:43
  42.1 1.9 %collective-permute-start.24 = (f32[8,128]{1,0:T(8,128)S(1)}, f32[8,128]{1,0:T(8,128)S(1)}, u32[]{:S(2)}, u32[]{:S(2)}) collective-permute-start(f32[8,128]{1,0:T(8,128)S(1)} %max.7), channel_id=1, source_target_pairs={{0,4},{4,0},{8,12},{12,8},{16,20},{20,16},{24,28},{28,24},{1,5},{5... | collective-permute-start | bytes 12296 | tf_op jit(solution)/shard_map/ppermute | solution.py:43
  44.5 9.7 %copy-start.1 = (bf16[1,1024,2048]{2,1,0:T(8,128)(2,1)S(1)}, bf16[1,1024,2048]{2,1,0:T(8,128)(2,1)}, u32[]{:S(2)}) copy-start(bf16[1,1024,2048]{2,1,0:T(8,128)(2,1)} %param.15) | copy-start | bytes 12582916
  45.7 1.2 %collective-permute-start.25 = (f32[8,256]{1,0:T(8,128)S(1)}, f32[8,256]{1,0:T(8,128)S(1)}, u32[]{:S(2)}, u32[]{:S(2)}) collective-permute-start(f32[8,256]{1,0:T(8,128)S(1)} %weighted_values.1), channel_id=1, source_target_pairs={{0,4},{4,0},{8,12},{12,8},{16,20},{20,16},{24,28},{28,24},{1,5},{5... | collective-permute-start | bytes 24584 | tf_op jit(solution)/shard_map/ppermute | solution.py:43
  46.9 3.7 %collective-permute-start.26 = (f32[8,256]{1,0:T(8,128)S(1)}, f32[8,256]{1,0:T(8,128)S(1)}, u32[]{:S(2)}, u32[]{:S(2)}) collective-permute-start(f32[8,256]{1,0:T(8,128)S(1)} %add.64), channel_id=1, source_target_pairs={{0,8},{4,12},{8,0},{12,4},{16,24},{20,28},{24,16},{28,20},{1,9},{5... | collective-permute-start | bytes 24584 | tf_op jit(solution)/shard_map/ppermute | solution.py:43
  50.6 3.7 %collective-permute-start.27 = (f32[8,256]{1,0:T(8,128)S(1)}, f32[8,256]{1,0:T(8,128)S(1)}, u32[]{:S(2)}, u32[]{:S(2)}) collective-permute-start(f32[8,256]{1,0:T(8,128)S(1)} %add.65.mine_ref), channel_id=1, source_target_pairs={{0,16},{4,20},{8,24},{12,28},{16,0},{20,4},{24,8},{28,12},{1,17},{... | collective-permute-start | bytes 24584 | tf_op jit(solution)/shard_map/ppermute | solution.py:43
  54.2 9.1 %copy-start.6 = (f32[2,2048]{1,0:T(2,128)S(1)}, f32[2,2048]{1,0:T(2,128)}, u32[]{:S(2)}) copy-start(f32[2,2048]{1,0:T(2,128)} %tokens_ref.3) | copy-start | bytes 49156
  54.9 3.8 %collective-permute-start.28 = (f32[2,2048]{1,0:T(2,128)S(1)}, f32[2,2048]{1,0:T(2,128)S(1)}, u32[]{:S(2)}, u32[]{:S(2)}) collective-permute-start(f32[2,2048]{1,0:T(2,128)S(1)} %output_products.1), channel_id=1, source_target_pairs={{0,1},{1,0},{2,3},{3,2},{4,5},{5,4},{6,7},{7,6},{8,9},{9,8},{10,11... | collective-permute-start | bytes 49160 | tf_op jit(solution)/shard_map/ppermute | solution.py:43
  58.6 4.7 %collective-permute-start.29 = (f32[2,2048]{1,0:T(2,128)S(1)}, f32[2,2048]{1,0:T(2,128)S(1)}, u32[]{:S(2)}, u32[]{:S(2)}) collective-permute-start(f32[2,2048]{1,0:T(2,128)S(1)} %add.66), channel_id=1, source_target_pairs={{0,2},{1,3},{2,0},{3,1},{4,6},{5,7},{6,4},{7,5},{8,10},{9,11},{10,... | collective-permute-start | bytes 49160 | tf_op jit(solution)/shard_map/ppermute | solution.py:43

commit v16 on v15

--- a/solution.py
+++ b/solution.py
@@ -116,8 +116,8 @@
     row_ref[...] = jnp.full(row_ref.shape, lax.rem(place, team) * row_count)
 
 
-def norm_kernel(first, x_ref, gain_ref, *refs):
-    out_refs, (held_ref, sems) = refs[:-2], refs[-2:]
+def norm_kernel(first, x_ref, gain_hbm_ref, *refs):
+    out_refs, (held_ref, gain_ref, sems, gain_sem) = refs[:-4], refs[-4:]
     blocks, rows, width = out_refs[0].shape
     features = blocks * width
     groups = len(out_refs) * rows // GROUP_ROWS
@@ -148,11 +148,15 @@
                     jnp.bfloat16
                 )
 
+    gain_copy = pltpu.make_async_copy(gain_hbm_ref, gain_ref, gain_sem)
     for g in range(groups):
         copy(g).start()
+        if g == 0:
+            gain_copy.start()
     copy(0).wait()
 
     factor = factor_of(0)
+    gain_copy.wait()
     for i, out_ref in enumerate(out_refs):
         start = i * rows // GROUP_ROWS
         stop = min(start + rows // GROUP_ROWS, groups - 1)
@@ -173,13 +177,18 @@
     return call(
         functools.partial(norm_kernel, first),
         "normalise",
-        [IN_HBM, IN_VMEM],
+        [IN_HBM, IN_HBM],
         (shape((blocks, NORM_ROWS, width), jnp.bfloat16),) * parts,
         [
             pltpu.VMEM((groups, GROUP_ROWS, blocks * width), jnp.bfloat16),
+            pltpu.VMEM(gains.shape, jnp.float32),
             pltpu.SemaphoreType.DMA((groups,)),
+            pltpu.SemaphoreType.DMA(()),
         ],
-    )(pltpu.with_memory_space_constraint(hidden, pltpu.HBM), gains)
+    )(
+        pltpu.with_memory_space_constraint(hidden, pltpu.HBM),
+        pltpu.with_memory_space_constraint(gains, pltpu.HBM),
+    )
 
 
 def query_kernel(
@@ -414,7 +423,7 @@
         top = butterfly(top, "ctx", bits_below(team)[1:], jnp.maximum)
         received = top
 
-    value_second = value_far[1:] + share(value_far[1:], masked)
+    value_second = value_far[1:] + share(value_far[1:], near_top)
     value_total = project(places, rows, value_second, value_total)
 
     blocks = share(value_last, received)

time: 64.2 us -> 65.4 us (1.019)
  Pallas kernels: 17.4 us -> 19.4 us
  local copies, waits for them, and re-layouts: 1.59 us -> 0.76 us
    pallas_call x2, Pallas kernels: 7.47 us -> 9.53 us  [normalise(): call(functools.partial(norm_kernel, first), 'normalise', [IN_HBM, IN_HBM]...]
    unnamed x18, local copies, waits for them, and re-layouts: 1.59 us -> 0.76 us
    ppermute x11, waiting for transfers between devices: 4.88 us -> 5.68 us  [by_core(): return lax.ppermute(value, 'ctx', pairs)]
  transfers between devices with their start and end apart: 30 -> 30, of which waited for: 15 -> 14; matrix products, arithmetic and copies ran while one was open for 1% -> 1% of each run, Pallas kernels for 24% -> 27%
where the time goes in v16:
time: 65.4 us; the launch traced here: 65.2 us
  starting transfers between devices  23.5 us (36%)
  waiting for transfers between devices  19.7 us (30%)
  Pallas kernels  19.4 us (30%)
  other arithmetic  1.48 us (2%)
  local copies, waits for them, and re-layouts  0.76 us (1%)
    ppermute x19, waiting for transfers between devices, swap(): return lax.ppermute(value, axis, [(i, i ^ distance) for i in range(count)])  14.1 us
    ppermute x11, starting transfers between devices, by_core(): return lax.ppermute(value, 'ctx', pairs)  13.9 us
    ppermute x19, starting transfers between devices, swap(): return lax.ppermute(value, axis, [(i, i ^ distance) for i in range(count)])  9.62 us
    pallas_call x2, Pallas kernels, normalise(): call(functools.partial(norm_kernel, first), 'normalise', [IN_HBM, IN_HBM]...  9.53 us
    pallas_call x6, Pallas kernels, project(): call(functools.partial(project_kernel, [d for d, _ in blocks], len(rows),...  6.15 us
    ppermute x11, waiting for transfers between devices, by_core(): return lax.ppermute(value, 'ctx', pairs)  5.68 us
  transfers between devices with their start and end apart: 30, of which 14 were waited for; matrix products, arithmetic and copies ran while one was open for 1% of the time, Pallas kernels for 27%

profile of v16, /device:TPU:0, one launch (start us, length us, event | category | flops | bytes accessed | tf_op | source)
XLA Modules:
  0.0 65.2 jit_solution(11330145869317305280)
XLA Ops:
  0.0 0.5 collective-permute-start.1
  0.5 0.1 collective-permute-start.2
  0.5 2.9 %collective-permute-start.12 = (bf16[2048,128]{1,0:T(8,128)(2,1)}, bf16[2048,128]{1,0:T(8,128)(2,1)S(1)}, u32[]{:S(2)}, u32[]{:S(2)}) collective-permute-start(bf16[2048,128]{1,0:T(8,128)(2,1)} %bitcast.24), channel_id=1, source_target_pairs={{0,8},{4,20},{8,0},{12,28},{16,24},{20,4},{24,16},{28,12},{1,9},{5... | collective-permute-start | bytes 1572872 | tf_op jit(solution)/shard_map/ppermute | solution.py:64
  3.5 0.0 collective-permute-done.1.refs_6_
  3.5 1.6 %collective-permute-start.7 = (bf16[2048,128]{1,0:T(8,128)(2,1)S(1)}, bf16[2048,128]{1,0:T(8,128)(2,1)S(1)}, u32[]{:S(2)}, u32[]{:S(2)}) collective-permute-start(bf16[2048,128]{1,0:T(8,128)(2,1)S(1)} %collective-permute-done.1.refs_6_), channel_id=1, source_target_pairs={{0,8},{4,20},{8,0},{12,28},{16,24},{20,4},{24,16},{28,12},{1,9},{5... | collective-permute-start | bytes 1572872 | tf_op jit(solution)/shard_map/ppermute | solution.py:64
  5.1 0.7 %copy-done.5 = f32[2,2048]{1,0:T(2,128)S(1)} copy-done((f32[2,2048]{1,0:T(2,128)S(1)}, f32[2,2048]{1,0:T(2,128)}, u32[]{:S(2)}) %copy-start.5) | copy-done | bytes 16408
  5.8 0.1 squares.1
  5.9 1.1 %collective-permute-done = f32[2,128]{1,0:T(2,128)S(1)} collective-permute-done((f32[2,128]{1,0:T(2,128)S(1)}, f32[2,128]{1,0:T(2,128)S(1)}, u32[]{:S(2)}, u32[]{:S(2)}) %collective-permute-start) | collective-permute-done | bytes 1056 | tf_op jit(solution)/shard_map/ppermute | solution.py:43
  7.0 1.5 %collective-permute-start.3 = (f32[2,128]{1,0:T(2,128)S(1)}, f32[2,128]{1,0:T(2,128)S(1)}, u32[]{:S(2)}, u32[]{:S(2)}) collective-permute-start(f32[2,128]{1,0:T(2,128)S(1)} %add.53), channel_id=1, source_target_pairs={{0,16},{4,12},{8,24},{12,4},{16,0},{20,28},{24,8},{28,20},{1,17},{... | collective-permute-start | bytes 3080 | tf_op jit(solution)/shard_map/ppermute | solution.py:64
  8.5 3.9 %normalise.2 = (bf16[8,64,2048]{2,1,0:T(8,128)(2,1)S(1)}, bf16[8,64,2048]{2,1,0:T(8,128)(2,1)S(1)}) custom-call(bf16[320,16384]{1,0:T(8,128)(2,1)} %bitcast.35, f32[8,1,2048]{2,1,0:T(1,128)} %bitcast.31), custom_call_target="tpu_custom_call" | custom-call | flops 1000 | bytes 1000 | tf_op jit(solution)/shard_map/normalise/pallas_call | solution.py:177
  12.5 0.1 collective-permute-start.4
  12.6 0.6 collective-permute-start.5
  13.2 0.5 collective-permute-done.4
  13.7 0.2 collective-permute-start.13
  13.9 0.9 %collective-permute-start.6 = (f32[2,128]{1,0:T(2,128)S(1)}, f32[2,128]{1,0:T(2,128)S(1)}, u32[]{:S(2)}, u32[]{:S(2)}) collective-permute-start(f32[2,128]{1,0:T(2,128)S(1)} %collective-permute-done.4), channel_id=1, source_target_pairs={{0,16},{4,12},{8,24},{12,4},{16,0},{20,28},{24,8},{28,20},{1,17},{... | collective-permute-start | bytes 3080 | tf_op jit(solution)/shard_map/ppermute | solution.py:64
  14.8 0.0 copy-start.4
  14.8 0.0 copy-start.6
  14.8 5.6 %normalise.3 = (bf16[8,64,2048]{2,1,0:T(8,128)(2,1)S(1)}, bf16[8,64,2048]{2,1,0:T(8,128)(2,1)S(1)}, bf16[8,64,2048]{2,1,0:T(8,128)(2,1)S(1)}) custom-call(bf16[320,16384]{1,0:T(8,128)(2,1)} %bitcast.36, f32[8,1,2048]{2,1,0:T(1,128)} %bitcast.32), custom_call_target="tpu_custom_call" | custom-call | flops 1000 | bytes 1000 | tf_op jit(solution)/shard_map/normalise/pallas_call | solution.py:177
  20.5 0.0 copy-start.8
  20.6 0.8 %query_products.1 = f32[2,10,128]{2,1,0:T(8,128)S(1)} custom-call(s32[1]{0:T(128)} %bitcast.place_ref, f32[2,128]{1,0:T(2,128)S(1)} %add_add_fusion.2.squares_ref, f32[2,2048]{1,0:T(2,128)S(1)} %copy-done.6, f32[8,1,2048]{2,1,0:T(1,128)S(1)} %bitcast.33, bf16[2048,1024]{1,0:T(8,128)(2,1)S(1)} %bitcast.21, bf16[2048,128]{1,0:T(8,128)(2,1)S(1)} %bitcast.25, ...), custom_call_target="tpu_custom_call" | custom-call | flops 1000 | bytes 1000 | tf_op jit(solution)/shard_map/query_products/pallas_call | solution.py:380
  21.4 0.1 collective-permute-start.8
  21.6 0.5 collective-permute-start.15
  22.1 0.8 %collective-permute-start.14 = (bf16[2048,128]{1,0:T(8,128)(2,1)S(1)}, bf16[2048,128]{1,0:T(8,128)(2,1)S(1)}, u32[]{:S(2)}, u32[]{:S(2)}) collective-permute-start(bf16[2048,128]{1,0:T(8,128)(2,1)S(1)} %collective-permute-done.13.refs_7_), channel_id=1, source_target_pairs={{0,8},{4,20},{8,0},{12,28},{16,24},{20,4},{24,16},{28,12},{1,9},{5... | collective-permute-start | bytes 1572872 | tf_op jit(solution)/shard_map/ppermute | solution.py:64
  22.9 1.2 %collective-permute-start.9 = (f32[2,10,128]{2,1,0:T(8,128)S(1)}, f32[2,10,128]{2,1,0:T(8,128)S(1)}, u32[]{:S(2)}, u32[]{:S(2)}) collective-permute-start(f32[2,10,128]{2,1,0:T(8,128)S(1)} %add.57), channel_id=1, source_target_pairs={{0,16},{4,12},{8,24},{12,4},{16,0},{20,28},{24,8},{28,20},{1,17},{... | collective-permute-start | bytes 30728 | tf_op jit(solution)/shard_map/ppermute | solution.py:64
  24.1 2.8 %collective-permute-done.9 = f32[2,10,128]{2,1,0:T(8,128)S(1)} collective-permute-done((f32[2,10,128]{2,1,0:T(8,128)S(1)}, f32[2,10,128]{2,1,0:T(8,128)S(1)}, u32[]{:S(2)}, u32[]{:S(2)}) %collective-permute-start.9) | collective-permute-done | bytes 10272 | tf_op jit(solution)/shard_map/ppermute | solution.py:64
  26.9 0.6 multiply_sine_fusion
  27.6 0.6 collective-permute-start.17
  28.2 0.1 multiply_sine_fusion.1
  28.3 1.3 %collective-permute-start.20 = (bf16[2048,128]{1,0:T(8,128)(2,1)S(1)}, bf16[2048,128]{1,0:T(8,128)(2,1)S(1)}, u32[]{:S(2)}, u32[]{:S(2)}) collective-permute-start(bf16[2048,128]{1,0:T(8,128)(2,1)S(1)} %collective-permute-done.2.refs_6_), channel_id=1, source_target_pairs={{0,8},{4,20},{8,0},{12,28},{16,24},{20,4},{24,16},{28,12},{1,9},{5... | collective-permute-start | bytes 1572872 | tf_op jit(solution)/shard_map/ppermute | solution.py:64
  29.6 0.9 %project.6.refs_9_ = f32[320,128]{1,0:T(8,128)S(1)} custom-call(s32[1]{0:T(128)} %bitcast.place_ref, bf16[8,64,2048]{2,1,0:T(8,128)(2,1)S(1)} %get-tuple-element.35.refs_0_, bf16[8,64,2048]{2,1,0:T(8,128)(2,1)S(1)} %get-tuple-element.36.refs_1_, bf16[8,64,2048]{2,1,0:T(8,128)(2,1)S(1)} %get-tuple-element.39.refs_2_, ...), custom_call_target="tpu_custom_call" | custom-call | flops 1000 | bytes 1000 | tf_op jit(solution)/shard_map/project/pallas_call | solution.py:227
  30.4 1.2 %collective-permute-start.18 = (f32[2,10,128]{2,1,0:T(8,128)S(1)}, f32[2,10,128]{2,1,0:T(8,128)S(1)}, u32[]{:S(2)}, u32[]{:S(2)}) collective-permute-start(f32[2,10,128]{2,1,0:T(8,128)S(1)} %collective-permute-done.17), channel_id=1, source_target_pairs={{0,16},{4,12},{8,24},{12,4},{16,0},{20,28},{24,8},{28,20},{1,17},{... | collective-permute-start | bytes 30728 | tf_op jit(solution)/shard_map/ppermute | solution.py:64
  31.6 1.5 %project.7.refs_7_ = f32[320,128]{1,0:T(8,128)S(1)} custom-call(s32[1]{0:T(128)} %bitcast.place_ref, bf16[8,64,2048]{2,1,0:T(8,128)(2,1)S(1)} %get-tuple-element.35.refs_0_, bf16[8,64,2048]{2,1,0:T(8,128)(2,1)S(1)} %get-tuple-element.36.refs_1_, bf16[8,64,2048]{2,1,0:T(8,128)(2,1)S(1)} %get-tuple-element.39.refs_2_, ...), custom_call_target="tpu_custom_call" | custom-call | flops 1000 | bytes 1000 | tf_op jit(solution)/shard_map/project/pallas_call | solution.py:227
  33.1 0.1 collective-permute-start.16
  33.3 0.9 %collective-permute-start.11 = (bf16[2048,128]{1,0:T(8,128)(2,1)S(1)}, bf16[2048,128]{1,0:T(8,128)(2,1)S(1)}, u32[]{:S(2)}, u32[]{:S(2)}) collective-permute-start(bf16[2048,128]{1,0:T(8,128)(2,1)S(1)} %collective-permute-done.10.refs_7_), channel_id=1, source_target_pairs={{0,8},{4,20},{8,0},{12,28},{16,24},{20,4},{24,16},{28,12},{1,9},{5... | collective-permute-start | bytes 1572872 | tf_op jit(solution)/shard_map/ppermute | solution.py:64
  34.2 0.3 collective-permute-done.18
  34.5 0.0 copy-start.7
  34.5 0.6 collective-permute-done.16.refs_6_
  35.1 0.9 %project.8.refs_0_ = f32[320,128]{1,0:T(8,128)S(1)} custom-call(s32[1]{0:T(128)} %bitcast.place_ref, bf16[8,64,2048]{2,1,0:T(8,128)(2,1)S(1)} %get-tuple-element.35.refs_0_, bf16[8,64,2048]{2,1,0:T(8,128)(2,1)S(1)} %get-tuple-element.36.refs_1_, bf16[8,64,2048]{2,1,0:T(8,128)(2,1)S(1)} %get-tuple-element.39.refs_2_, ...), custom_call_target="tpu_custom_call" | custom-call | flops 1000 | bytes 1000 | tf_op jit(solution)/shard_map/project/pallas_call | solution.py:227
  36.0 1.0 %scores.1 = (f32[8,320]{1,0:T(8,128)S(1)}, f32[8,128]{1,0:T(8,128)S(1)}, f32[8,128]{1,0:T(8,128)S(1)}) custom-call(s32[1]{0:T(128)} %bitcast.place_ref, s32[2]{0:T(128)S(1)} %copy-done.7, f32[320,128]{1,0:T(8,128)S(1)} %project.8.refs_0_, f32[320,64]{1,0:T(8,128)S(1)} %get-tuple-element.60.refs_1_, f32[320,64]{1,0:T(8,128)S(1)} %get-tuple-element.59.refs_2_, ...), custom_call_target="tpu_custom_call" | custom-call | flops 1000 | bytes 1000 | tf_op jit(solution)/shard_map/scores/pallas_call | solution.py:406
  37.0 0.1 collective-permute-start.19
  37.1 1.0 %collective-permute-done.19 = f32[8,128]{1,0:T(8,128)S(1)} collective-permute-done((f32[8,128]{1,0:T(8,128)S(1)}, f32[8,128]{1,0:T(8,128)S(1)}, u32[]{:S(2)}, u32[]{:S(2)}) %collective-permute-start.19) | collective-permute-done | bytes 4128 | tf_op jit(solution)/shard_map/ppermute | solution.py:43
  38.2 0.2 collective-permute-start.23
  38.3 0.9 %collective-permute-start.21 = (f32[8,128]{1,0:T(8,128)S(1)}, f32[8,128]{1,0:T(8,128)S(1)}, u32[]{:S(2)}, u32[]{:S(2)}) collective-permute-start(f32[8,128]{1,0:T(8,128)S(1)} %max.6), channel_id=1, source_target_pairs={{0,16},{4,12},{8,24},{12,4},{16,0},{20,28},{24,8},{28,20},{1,17},{... | collective-permute-start | bytes 12296 | tf_op jit(solution)/shard_map/ppermute | solution.py:64
  39.3 1.5 %project.9.refs_7_ = f32[320,128]{1,0:T(8,128)S(1)} custom-call(s32[1]{0:T(128)} %bitcast.place_ref, bf16[8,64,2048]{2,1,0:T(8,128)(2,1)S(1)} %get-tuple-element.35.refs_0_, bf16[8,64,2048]{2,1,0:T(8,128)(2,1)S(1)} %get-tuple-element.36.refs_1_, bf16[8,64,2048]{2,1,0:T(8,128)(2,1)S(1)} %get-tuple-element.39.refs_2_, ...), custom_call_target="tpu_custom_call" | custom-call | flops 1000 | bytes 1000 | tf_op jit(solution)/shard_map/project/pallas_call | solution.py:227
  40.8 1.2 %collective-permute-done.21 = f32[8,128]{1,0:T(8,128)S(1)} collective-permute-done((f32[8,128]{1,0:T(8,128)S(1)}, f32[8,128]{1,0:T(8,128)S(1)}, u32[]{:S(2)}, u32[]{:S(2)}) %collective-permute-start.21) | collective-permute-done | bytes 4128 | tf_op jit(solution)/shard_map/ppermute | solution.py:64
  42.0 1.3 %collective-permute-done.11.refs_5_ = bf16[2048,128]{1,0:T(8,128)(2,1)S(1)} collective-permute-done((bf16[2048,128]{1,0:T(8,128)(2,1)S(1)}, bf16[2048,128]{1,0:T(8,128)(2,1)S(1)}, u32[]{:S(2)}, u32[]{:S(2)}) %collective-permute-start.11) | collective-permute-done | bytes 524320 | tf_op jit(solution)/shard_map/ppermute | solution.py:64
  43.4 0.5 collective-permute-start.24
  43.9 0.9 %project.10.refs_6_ = f32[320,128]{1,0:T(8,128)S(1)} custom-call(s32[1]{0:T(128)} %bitcast.place_ref, bf16[8,64,2048]{2,1,0:T(8,128)(2,1)S(1)} %get-tuple-element.35.refs_0_, bf16[8,64,2048]{2,1,0:T(8,128)(2,1)S(1)} %get-tuple-element.36.refs_1_, bf16[8,64,2048]{2,1,0:T(8,128)(2,1)S(1)} %get-tuple-element.39.refs_2_, ...), custom_call_target="tpu_custom_call" | custom-call | flops 1000 | bytes 1000 | tf_op jit(solution)/shard_map/project/pallas_call | solution.py:227
  44.7 0.5 collective-permute-done.24
  45.3 0.5 project.11.refs_6_
  45.8 0.0 copy-start.1
  45.8 1.2 %weighted_values.1 = f32[8,256]{1,0:T(8,128)S(1)} custom-call(s32[1]{0:T(128)} %bitcast.place_ref, s32[2]{0:T(128)S(1)} %copy-done.7, bf16[8,64,2048]{2,1,0:T(8,128)(2,1)S(1)} %get-tuple-element.35.refs_0_, bf16[8,64,2048]{2,1,0:T(8,128)(2,1)S(1)} %get-tuple-element.36.refs_1_, bf16[8,64,2048]{2,1,0:T(8,128)(2,1)S(1)} %get-tuple-element.39.refs_2_, ...), custom_call_target="tpu_custom_call" | custom-call | flops 1000 | bytes 1000 | tf_op jit(solution)/shard_map/weighted_values/pallas_call | solution.py:431
  47.0 0.1 collective-permute-start.25
  47.1 1.0 %collective-permute-done.25 = f32[8,256]{1,0:T(8,128)S(1)} collective-permute-done((f32[8,256]{1,0:T(8,128)S(1)}, f32[8,256]{1,0:T(8,128)S(1)}, u32[]{:S(2)}, u32[]{:S(2)}) %collective-permute-start.25) | collective-permute-done | bytes 8224 | tf_op jit(solution)/shard_map/ppermute | solution.py:43
  48.2 1.2 %collective-permute-start.26 = (f32[8,256]{1,0:T(8,128)S(1)}, f32[8,256]{1,0:T(8,128)S(1)}, u32[]{:S(2)}, u32[]{:S(2)}) collective-permute-start(f32[8,256]{1,0:T(8,128)S(1)} %add.64), channel_id=1, source_target_pairs={{0,8},{4,12},{8,0},{12,4},{16,24},{20,28},{24,16},{28,20},{1,9},{5... | collective-permute-start | bytes 24584 | tf_op jit(solution)/shard_map/ppermute | solution.py:43
  49.4 2.4 %collective-permute-done.26 = f32[8,256]{1,0:T(8,128)S(1)} collective-permute-done((f32[8,256]{1,0:T(8,128)S(1)}, f32[8,256]{1,0:T(8,128)S(1)}, u32[]{:S(2)}, u32[]{:S(2)}) %collective-permute-start.26) | collective-permute-done | bytes 8224 | tf_op jit(solution)/shard_map/ppermute | solution.py:43
  51.8 1.1 %collective-permute-start.27 = (f32[8,256]{1,0:T(8,128)S(1)}, f32[8,256]{1,0:T(8,128)S(1)}, u32[]{:S(2)}, u32[]{:S(2)}) collective-permute-start(f32[8,256]{1,0:T(8,128)S(1)} %add.65.mine_ref), channel_id=1, source_target_pairs={{0,16},{4,20},{8,24},{12,28},{16,0},{20,4},{24,8},{28,12},{1,17},{... | collective-permute-start | bytes 24584 | tf_op jit(solution)/shard_map/ppermute | solution.py:43
  53.0 2.5 %collective-permute-done.27.other_ref = f32[8,256]{1,0:T(8,128)S(1)} collective-permute-done((f32[8,256]{1,0:T(8,128)S(1)}, f32[8,256]{1,0:T(8,128)S(1)}, u32[]{:S(2)}, u32[]{:S(2)}) %collective-permute-start.27) | collective-permute-done | bytes 8224 | tf_op jit(solution)/shard_map/ppermute | solution.py:43
  55.5 0.6 output_products.1
  56.1 1.6 %collective-permute-start.28 = (f32[2,2048]{1,0:T(2,128)S(1)}, f32[2,2048]{1,0:T(2,128)S(1)}, u32[]{:S(2)}, u32[]{:S(2)}) collective-permute-start(f32[2,2048]{1,0:T(2,128)S(1)} %output_products.1), channel_id=1, source_target_pairs={{0,1},{1,0},{2,3},{3,2},{4,5},{5,4},{6,7},{7,6},{8,9},{9,8},{10,11... | collective-permute-start | bytes 49160 | tf_op jit(solution)/shard_map/ppermute | solution.py:43
  57.7 2.2 %collective-permute-done.28 = f32[2,2048]{1,0:T(2,128)S(1)} collective-permute-done((f32[2,2048]{1,0:T(2,128)S(1)}, f32[2,2048]{1,0:T(2,128)S(1)}, u32[]{:S(2)}, u32[]{:S(2)}) %collective-permute-start.28) | collective-permute-done | bytes 16416 | tf_op jit(solution)/shard_map/ppermute | solution.py:43
  59.9 2.7 %collective-permute-start.29 = (f32[2,2048]{1,0:T(2,128)S(1)}, f32[2,2048]{1,0:T(2,128)S(1)}, u32[]{:S(2)}, u32[]{:S(2)}) collective-permute-start(f32[2,2048]{1,0:T(2,128)S(1)} %add.66), channel_id=1, source_target_pairs={{0,2},{1,3},{2,0},{3,1},{4,6},{5,7},{6,4},{7,5},{8,10},{9,11},{10,... | collective-permute-start | bytes 49160 | tf_op jit(solution)/shard_map/ppermute | solution.py:43
  62.6 2.0 %collective-permute-done.29 = f32[2,2048]{1,0:T(2,128)S(1)} collective-permute-done((f32[2,2048]{1,0:T(2,128)S(1)}, f32[2,2048]{1,0:T(2,128)S(1)}, u32[]{:S(2)}, u32[]{:S(2)}) %collective-permute-start.29) | collective-permute-done | bytes 16416 | tf_op jit(solution)/shard_map/ppermute | solution.py:43
  64.6 0.6 add_add_fusion
  (46 shorter events, 0.2 us)
Async XLA Ops:
  0.0 3.5 %collective-permute-start.1 = (bf16[2048,128]{1,0:T(8,128)(2,1)}, bf16[2048,128]{1,0:T(8,128)(2,1)S(1)}, u32[]{:S(2)}, u32[]{:S(2)}) collective-permute-start(bf16[2048,128]{1,0:T(8,128)(2,1)} %bitcast.23), channel_id=1, source_target_pairs={{0,4},{4,0},{8,12},{12,8},{16,20},{20,16},{24,28},{28,24},{1,5},{5... | collective-permute-start | bytes 1572872 | tf_op jit(solution)/shard_map/ppermute | solution.py:43
  0.5 6.6 %collective-permute-start.2 = (bf16[2048,128]{1,0:T(8,128)(2,1)}, bf16[2048,128]{1,0:T(8,128)(2,1)S(1)}, u32[]{:S(2)}, u32[]{:S(2)}) collective-permute-start(bf16[2048,128]{1,0:T(8,128)(2,1)} %bitcast.27), channel_id=1, source_target_pairs={{0,4},{4,0},{8,12},{12,8},{16,20},{20,16},{24,28},{28,24},{1,5},{5... | collective-permute-start | bytes 1572872 | tf_op jit(solution)/shard_map/ppermute | solution.py:43
  0.5 12.6 %collective-permute-start.12 = (bf16[2048,128]{1,0:T(8,128)(2,1)}, bf16[2048,128]{1,0:T(8,128)(2,1)S(1)}, u32[]{:S(2)}, u32[]{:S(2)}) collective-permute-start(bf16[2048,128]{1,0:T(8,128)(2,1)} %bitcast.24), channel_id=1, source_target_pairs={{0,8},{4,20},{8,0},{12,28},{16,24},{20,4},{24,16},{28,12},{1,9},{5... | collective-permute-start | bytes 1572872 | tf_op jit(solution)/shard_map/ppermute | solution.py:64
  3.5 17.0 %collective-permute-start.7 = (bf16[2048,128]{1,0:T(8,128)(2,1)S(1)}, bf16[2048,128]{1,0:T(8,128)(2,1)S(1)}, u32[]{:S(2)}, u32[]{:S(2)}) collective-permute-start(bf16[2048,128]{1,0:T(8,128)(2,1)S(1)} %collective-permute-done.1.refs_6_), channel_id=1, source_target_pairs={{0,8},{4,20},{8,0},{12,28},{16,24},{20,4},{24,16},{28,12},{1,9},{5... | collective-permute-start | bytes 1572872 | tf_op jit(solution)/shard_map/ppermute | solution.py:64
  5.1 0.7 %copy-start.5 = (f32[2,2048]{1,0:T(2,128)S(1)}, f32[2,2048]{1,0:T(2,128)}, u32[]{:S(2)}) copy-start(f32[2,2048]{1,0:T(2,128)} %tokens_ref.3) | copy-start | bytes 49156
  5.9 1.1 %collective-permute-start = (f32[2,128]{1,0:T(2,128)S(1)}, f32[2,128]{1,0:T(2,128)S(1)}, u32[]{:S(2)}, u32[]{:S(2)}) collective-permute-start(f32[2,128]{1,0:T(2,128)S(1)} %get-tuple-element.32), channel_id=1, source_target_pairs={{0,4},{4,0},{8,12},{12,8},{16,20},{20,16},{24,28},{28,24},{1,5},{5... | collective-permute-start | bytes 3080 | tf_op jit(solution)/shard_map/ppermute | solution.py:43
  7.0 5.4 %collective-permute-start.3 = (f32[2,128]{1,0:T(2,128)S(1)}, f32[2,128]{1,0:T(2,128)S(1)}, u32[]{:S(2)}, u32[]{:S(2)}) collective-permute-start(f32[2,128]{1,0:T(2,128)S(1)} %add.53), channel_id=1, source_target_pairs={{0,16},{4,12},{8,24},{12,4},{16,0},{20,28},{24,8},{28,20},{1,17},{... | collective-permute-start | bytes 3080 | tf_op jit(solution)/shard_map/ppermute | solution.py:64
  8.5 4.0 %copy-start.3 = (bf16[1,2048,128]{2,1,0:T(8,128)(2,1)S(1)}, bf16[1,2048,128]{2,1,0:T(8,128)(2,1)}, u32[]{:S(2)}) copy-start(bf16[1,2048,128]{2,1,0:T(8,128)(2,1)} %param.14) | copy-start | bytes 1572868
  12.5 1.2 %collective-permute-start.4 = (f32[2,128]{1,0:T(2,128)S(1)}, f32[2,128]{1,0:T(2,128)S(1)}, u32[]{:S(2)}, u32[]{:S(2)}) collective-permute-start(f32[2,128]{1,0:T(2,128)S(1)} %collective-permute-done.3), channel_id=1, source_target_pairs={{0,4},{4,0},{8,12},{12,8},{16,20},{20,16},{24,28},{28,24},{1,5},{5... | collective-permute-start | bytes 3080 | tf_op jit(solution)/shard_map/ppermute | solution.py:43
  12.6 11.5 %collective-permute-start.5 = (bf16[2048,128]{1,0:T(8,128)(2,1)S(1)}, bf16[2048,128]{1,0:T(8,128)(2,1)S(1)}, u32[]{:S(2)}, u32[]{:S(2)}) collective-permute-start(bf16[2048,128]{1,0:T(8,128)(2,1)S(1)} %bitcast.28), channel_id=1, source_target_pairs={{0,8},{4,20},{8,0},{12,28},{16,24},{20,4},{24,16},{28,12},{1,9},{5... | collective-permute-start | bytes 1572872 | tf_op jit(solution)/shard_map/ppermute | solution.py:64
  13.7 8.4 %collective-permute-start.13 = (bf16[2048,128]{1,0:T(8,128)(2,1)S(1)}, bf16[2048,128]{1,0:T(8,128)(2,1)S(1)}, u32[]{:S(2)}, u32[]{:S(2)}) collective-permute-start(bf16[2048,128]{1,0:T(8,128)(2,1)S(1)} %collective-permute-done.12.refs_5_), channel_id=1, source_target_pairs={{0,4},{4,0},{8,12},{12,8},{16,20},{20,16},{24,28},{28,24},{1,5},{5... | collective-permute-start | bytes 1572872 | tf_op jit(solution)/shard_map/ppermute | solution.py:43
  13.9 6.6 %collective-permute-start.6 = (f32[2,128]{1,0:T(2,128)S(1)}, f32[2,128]{1,0:T(2,128)S(1)}, u32[]{:S(2)}, u32[]{:S(2)}) collective-permute-start(f32[2,128]{1,0:T(2,128)S(1)} %collective-permute-done.4), channel_id=1, source_target_pairs={{0,16},{4,12},{8,24},{12,4},{16,0},{20,28},{24,8},{28,20},{1,17},{... | collective-permute-start | bytes 3080 | tf_op jit(solution)/shard_map/ppermute | solution.py:64
  14.8 5.7 %copy-start = (bf16[1,2048,1024]{2,1,0:T(8,128)(2,1)S(1)}, bf16[1,2048,1024]{2,1,0:T(8,128)(2,1)}, u32[]{:S(2)}) copy-start(bf16[1,2048,1024]{2,1,0:T(8,128)(2,1)} %param.12) | copy-start | bytes 12582916
  14.8 5.7 %copy-start.2 = (bf16[1,2048,128]{2,1,0:T(8,128)(2,1)S(1)}, bf16[1,2048,128]{2,1,0:T(8,128)(2,1)}, u32[]{:S(2)}) copy-start(bf16[1,2048,128]{2,1,0:T(8,128)(2,1)} %param.13) | copy-start | bytes 1572868
  14.8 5.7 %copy-start.4 = (f32[1,16384]{1,0:T(1,128)S(1)}, f32[1,16384]{1,0:T(1,128)}, u32[]{:S(2)}) copy-start(f32[1,16384]{1,0:T(1,128)} %param.11) | copy-start | bytes 196612
  14.8 5.7 %copy-start.6 = (f32[2,2048]{1,0:T(2,128)S(1)}, f32[2,2048]{1,0:T(2,128)}, u32[]{:S(2)}) copy-start(f32[2,2048]{1,0:T(2,128)} %tokens_ref.3) | copy-start | bytes 49156
  20.5 7.0 %copy-start.8 = (s32[2]{0:T(128)S(1)}, s32[2]{0:T(128)}, u32[]{:S(2)}) copy-start(s32[2]{0:T(128)} %param.17) | copy-start | bytes 28
  21.4 1.5 %collective-permute-start.8 = (f32[2,10,128]{2,1,0:T(8,128)S(1)}, f32[2,10,128]{2,1,0:T(8,128)S(1)}, u32[]{:S(2)}, u32[]{:S(2)}) collective-permute-start(f32[2,10,128]{2,1,0:T(8,128)S(1)} %query_products.1), channel_id=1, source_target_pairs={{0,4},{4,0},{8,12},{12,8},{16,20},{20,16},{24,28},{28,24},{1,5},{5... | collective-permute-start | bytes 30728 | tf_op jit(solution)/shard_map/ppermute | solution.py:43
  21.6 10.0 %collective-permute-start.15 = (bf16[2048,128]{1,0:T(8,128)(2,1)S(1)}, bf16[2048,128]{1,0:T(8,128)(2,1)S(1)}, u32[]{:S(2)}, u32[]{:S(2)}) collective-permute-start(bf16[2048,128]{1,0:T(8,128)(2,1)S(1)} %collective-permute-done.7.refs_6_), channel_id=1, source_target_pairs={{0,4},{4,0},{8,12},{12,8},{16,20},{20,16},{24,28},{28,24},{1,5},{5... | collective-permute-start | bytes 1572872 | tf_op jit(solution)/shard_map/ppermute | solution.py:43
  22.1 11.1 %collective-permute-start.14 = (bf16[2048,128]{1,0:T(8,128)(2,1)S(1)}, bf16[2048,128]{1,0:T(8,128)(2,1)S(1)}, u32[]{:S(2)}, u32[]{:S(2)}) collective-permute-start(bf16[2048,128]{1,0:T(8,128)(2,1)S(1)} %collective-permute-done.13.refs_7_), channel_id=1, source_target_pairs={{0,8},{4,20},{8,0},{12,28},{16,24},{20,4},{24,16},{28,12},{1,9},{5... | collective-permute-start | bytes 1572872 | tf_op jit(solution)/shard_map/ppermute | solution.py:64
  22.9 4.0 %collective-permute-start.9 = (f32[2,10,128]{2,1,0:T(8,128)S(1)}, f32[2,10,128]{2,1,0:T(8,128)S(1)}, u32[]{:S(2)}, u32[]{:S(2)}) collective-permute-start(f32[2,10,128]{2,1,0:T(8,128)S(1)} %add.57), channel_id=1, source_target_pairs={{0,16},{4,12},{8,24},{12,4},{16,0},{20,28},{24,8},{28,20},{1,17},{... | collective-permute-start | bytes 30728 | tf_op jit(solution)/shard_map/ppermute | solution.py:64
  26.9 6.3 %collective-permute-start.10 = (bf16[2048,128]{1,0:T(8,128)(2,1)S(1)}, bf16[2048,128]{1,0:T(8,128)(2,1)S(1)}, u32[]{:S(2)}, u32[]{:S(2)}) collective-permute-start(bf16[2048,128]{1,0:T(8,128)(2,1)S(1)} %collective-permute-done.5.refs_8_), channel_id=1, source_target_pairs={{0,4},{4,0},{8,12},{12,8},{16,20},{20,16},{24,28},{28,24},{1,5},{5... | collective-permute-start | bytes 1572872 | tf_op jit(solution)/shard_map/ppermute | solution.py:43
  27.6 2.8 %collective-permute-start.17 = (f32[2,10,128]{2,1,0:T(8,128)S(1)}, f32[2,10,128]{2,1,0:T(8,128)S(1)}, u32[]{:S(2)}, u32[]{:S(2)}) collective-permute-start(f32[2,10,128]{2,1,0:T(8,128)S(1)} %collective-permute-done.9), channel_id=1, source_target_pairs={{0,4},{4,0},{8,12},{12,8},{16,20},{20,16},{24,28},{28,24},{1,5},{5... | collective-permute-start | bytes 30728 | tf_op jit(solution)/shard_map/ppermute | solution.py:43
  28.3 9.9 %collective-permute-start.20 = (bf16[2048,128]{1,0:T(8,128)(2,1)S(1)}, bf16[2048,128]{1,0:T(8,128)(2,1)S(1)}, u32[]{:S(2)}, u32[]{:S(2)}) collective-permute-start(bf16[2048,128]{1,0:T(8,128)(2,1)S(1)} %collective-permute-done.2.refs_6_), channel_id=1, source_target_pairs={{0,8},{4,20},{8,0},{12,28},{16,24},{20,4},{24,16},{28,12},{1,9},{5... | collective-permute-start | bytes 1572872 | tf_op jit(solution)/shard_map/ppermute | solution.py:64
  30.4 4.0 %collective-permute-start.18 = (f32[2,10,128]{2,1,0:T(8,128)S(1)}, f32[2,10,128]{2,1,0:T(8,128)S(1)}, u32[]{:S(2)}, u32[]{:S(2)}) collective-permute-start(f32[2,10,128]{2,1,0:T(8,128)S(1)} %collective-permute-done.17), channel_id=1, source_target_pairs={{0,16},{4,12},{8,24},{12,4},{16,0},{20,28},{24,8},{28,20},{1,17},{... | collective-permute-start | bytes 30728 | tf_op jit(solution)/shard_map/ppermute | solution.py:64
  33.1 2.0 %collective-permute-start.16 = (bf16[2048,128]{1,0:T(8,128)(2,1)S(1)}, bf16[2048,128]{1,0:T(8,128)(2,1)S(1)}, u32[]{:S(2)}, u32[]{:S(2)}) collective-permute-start(bf16[2048,128]{1,0:T(8,128)(2,1)S(1)} %collective-permute-done.14.refs_5_), channel_id=1, source_target_pairs={{0,4},{4,0},{8,12},{12,8},{16,20},{20,16},{24,28},{28,24},{1,5},{5... | collective-permute-start | bytes 1572872 | tf_op jit(solution)/shard_map/ppermute | solution.py:43
  33.3 10.1 %collective-permute-start.11 = (bf16[2048,128]{1,0:T(8,128)(2,1)S(1)}, bf16[2048,128]{1,0:T(8,128)(2,1)S(1)}, u32[]{:S(2)}, u32[]{:S(2)}) collective-permute-start(bf16[2048,128]{1,0:T(8,128)(2,1)S(1)} %collective-permute-done.10.refs_7_), channel_id=1, source_target_pairs={{0,8},{4,20},{8,0},{12,28},{16,24},{20,4},{24,16},{28,12},{1,9},{5... | collective-permute-start | bytes 1572872 | tf_op jit(solution)/shard_map/ppermute | solution.py:64
  34.5 1.5 %copy-start.7 = (s32[2]{0:T(128)S(1)}, s32[2]{0:T(128)}, u32[]{:S(2)}) copy-start(s32[2]{0:T(128)} %lengths_ref.3) | copy-start | bytes 28
  37.0 1.2 %collective-permute-start.19 = (f32[8,128]{1,0:T(8,128)S(1)}, f32[8,128]{1,0:T(8,128)S(1)}, u32[]{:S(2)}, u32[]{:S(2)}) collective-permute-start(f32[8,128]{1,0:T(8,128)S(1)} %get-tuple-element.51), channel_id=1, source_target_pairs={{0,4},{4,0},{8,12},{12,8},{16,20},{20,16},{24,28},{28,24},{1,5},{5... | collective-permute-start | bytes 12296 | tf_op jit(solution)/shard_map/ppermute | solution.py:43
  38.2 5.7 %collective-permute-start.23 = (bf16[2048,128]{1,0:T(8,128)(2,1)S(1)}, bf16[2048,128]{1,0:T(8,128)(2,1)S(1)}, u32[]{:S(2)}, u32[]{:S(2)}) collective-permute-start(bf16[2048,128]{1,0:T(8,128)(2,1)S(1)} %collective-permute-done.20.refs_5_), channel_id=1, source_target_pairs={{0,4},{4,0},{8,12},{12,8},{16,20},{20,16},{24,28},{28,24},{1,5},{5... | collective-permute-start | bytes 1572872 | tf_op jit(solution)/shard_map/ppermute | solution.py:43
  38.3 3.7 %collective-permute-start.21 = (f32[8,128]{1,0:T(8,128)S(1)}, f32[8,128]{1,0:T(8,128)S(1)}, u32[]{:S(2)}, u32[]{:S(2)}) collective-permute-start(f32[8,128]{1,0:T(8,128)S(1)} %max.6), channel_id=1, source_target_pairs={{0,16},{4,12},{8,24},{12,4},{16,0},{20,28},{24,8},{28,20},{1,17},{... | collective-permute-start | bytes 12296 | tf_op jit(solution)/shard_map/ppermute | solution.py:64
  43.4 2.4 %collective-permute-start.22 = (bf16[2048,128]{1,0:T(8,128)(2,1)S(1)}, bf16[2048,128]{1,0:T(8,128)(2,1)S(1)}, u32[]{:S(2)}, u32[]{:S(2)}) collective-permute-start(bf16[2048,128]{1,0:T(8,128)(2,1)S(1)} %collective-permute-done.11.refs_5_), channel_id=1, source_target_pairs={{0,4},{4,0},{8,12},{12,8},{16,20},{20,16},{24,28},{28,24},{1,5},{5... | collective-permute-start | bytes 1572872 | tf_op jit(solution)/shard_map/ppermute | solution.py:43
  43.4 1.9 %collective-permute-start.24 = (f32[8,128]{1,0:T(8,128)S(1)}, f32[8,128]{1,0:T(8,128)S(1)}, u32[]{:S(2)}, u32[]{:S(2)}) collective-permute-start(f32[8,128]{1,0:T(8,128)S(1)} %max.7), channel_id=1, source_target_pairs={{0,4},{4,0},{8,12},{12,8},{16,20},{20,16},{24,28},{28,24},{1,5},{5... | collective-permute-start | bytes 12296 | tf_op jit(solution)/shard_map/ppermute | solution.py:43
  45.8 9.7 %copy-start.1 = (bf16[1,1024,2048]{2,1,0:T(8,128)(2,1)S(1)}, bf16[1,1024,2048]{2,1,0:T(8,128)(2,1)}, u32[]{:S(2)}) copy-start(bf16[1,1024,2048]{2,1,0:T(8,128)(2,1)} %param.15) | copy-start | bytes 12582916
  47.0 1.2 %collective-permute-start.25 = (f32[8,256]{1,0:T(8,128)S(1)}, f32[8,256]{1,0:T(8,128)S(1)}, u32[]{:S(2)}, u32[]{:S(2)}) collective-permute-start(f32[8,256]{1,0:T(8,128)S(1)} %weighted_values.1), channel_id=1, source_target_pairs={{0,4},{4,0},{8,12},{12,8},{16,20},{20,16},{24,28},{28,24},{1,5},{5... | collective-permute-start | bytes 24584 | tf_op jit(solution)/shard_map/ppermute | solution.py:43
  48.2 3.7 %collective-permute-start.26 = (f32[8,256]{1,0:T(8,128)S(1)}, f32[8,256]{1,0:T(8,128)S(1)}, u32[]{:S(2)}, u32[]{:S(2)}) collective-permute-start(f32[8,256]{1,0:T(8,128)S(1)} %add.64), channel_id=1, source_target_pairs={{0,8},{4,12},{8,0},{12,4},{16,24},{20,28},{24,16},{28,20},{1,9},{5... | collective-permute-start | bytes 24584 | tf_op jit(solution)/shard_map/ppermute | solution.py:43
  51.8 3.7 %collective-permute-start.27 = (f32[8,256]{1,0:T(8,128)S(1)}, f32[8,256]{1,0:T(8,128)S(1)}, u32[]{:S(2)}, u32[]{:S(2)}) collective-permute-start(f32[8,256]{1,0:T(8,128)S(1)} %add.65.mine_ref), channel_id=1, source_target_pairs={{0,16},{4,20},{8,24},{12,28},{16,0},{20,4},{24,8},{28,12},{1,17},{... | collective-permute-start | bytes 24584 | tf_op jit(solution)/shard_map/ppermute | solution.py:43
  56.1 3.8 %collective-permute-start.28 = (f32[2,2048]{1,0:T(2,128)S(1)}, f32[2,2048]{1,0:T(2,128)S(1)}, u32[]{:S(2)}, u32[]{:S(2)}) collective-permute-start(f32[2,2048]{1,0:T(2,128)S(1)} %output_products.1), channel_id=1, source_target_pairs={{0,1},{1,0},{2,3},{3,2},{4,5},{5,4},{6,7},{7,6},{8,9},{9,8},{10,11... | collective-permute-start | bytes 49160 | tf_op jit(solution)/shard_map/ppermute | solution.py:43
  59.9 4.7 %collective-permute-start.29 = (f32[2,2048]{1,0:T(2,128)S(1)}, f32[2,2048]{1,0:T(2,128)S(1)}, u32[]{:S(2)}, u32[]{:S(2)}) collective-permute-start(f32[2,2048]{1,0:T(2,128)S(1)} %add.66), channel_id=1, source_target_pairs={{0,2},{1,3},{2,0},{3,1},{4,6},{5,7},{6,4},{7,5},{8,10},{9,11},{10,... | collective-permute-start | bytes 49160 | tf_op jit(solution)/shard_map/ppermute | solution.py:43

commit v17 on v15

--- a/solution.py
+++ b/solution.py
@@ -336,14 +336,14 @@
         rows.extend(normalise(after(ctx_hidden[0], sent), gains, first, parts))
         return after(received, rows[-1])
 
-    def sum_chips(value, norm_parts=0):
+    def sum_chips(value, first_parts=0, second_parts=0):
         received = by_core(value, 4, 2)
-        if norm_parts:
-            received = beside(received, value, norm_parts)
+        if first_parts:
+            received = beside(received, value, first_parts)
         told = swap(received, "ctx", 1)
         opposite = by_core(told, 4, 2)
-        if norm_parts:
-            opposite = beside(opposite, told, row_count // NORM_ROWS - norm_parts)
+        if second_parts:
+            opposite = beside(opposite, told, second_parts)
         over_x = jnp.where(core == 0, told, received)
         over_y = jnp.where(core == 0, received, told)
         return (value + over_x) + (over_y + opposite), told, received
@@ -357,7 +357,7 @@
     squares = squares + swap(squares, "ctx", 1)
     squares = after(squares, key_partner, value_partner)
     if split:
-        squares, told, _ = sum_chips(squares, row_count // NORM_ROWS // 2)
+        squares, told, _ = sum_chips(squares, 2, row_count // NORM_ROWS - 3)
         key_shared = share(key_far, told)
         own_values = value_weight[0]
         squares = after(squares, key_far[1][1])
@@ -378,7 +378,7 @@
     parts_sent = parts
     value_far = send_first(own_values, value_partner)
     if split:
-        parts, _, parts_sent = sum_chips(parts)
+        parts, _, parts_sent = sum_chips(parts, 1)
         summed = jnp.where(own_request == 0, parts[0], parts[1])
     else:
         own_part = jnp.where(own_request == 0, parts[0], parts[1])
@@ -414,7 +414,7 @@
         top = butterfly(top, "ctx", bits_below(team)[1:], jnp.maximum)
         received = top
 
-    value_second = value_far[1:] + share(value_far[1:], masked)
+    value_second = value_far[1:] + share(value_far[1:], near_top)
     value_total = project(places, rows, value_second, value_total)
 
     blocks = share(value_last, received)

time: 64.2 us -> 63.4 us (0.988)
  waiting for transfers between devices: 19.3 us -> 17.6 us
  Pallas kernels: 17.4 us -> 18.5 us
    ppermute x11, waiting for transfers between devices: 4.88 us -> 3.51 us  [by_core(): return lax.ppermute(value, 'ctx', pairs)]
    pallas_call x2 -> x3, Pallas kernels: 7.47 us -> 8.6 us  [normalise(): call(functools.partial(norm_kernel, first), 'normalise', [IN_HBM, IN_VMEM...]
  transfers between devices with their start and end apart: 30 -> 30, of which waited for: 15 -> 14; matrix products, arithmetic and copies ran while one was open for 1% -> 1% of each run, Pallas kernels for 24% -> 26%
where the time goes in v17:
time: 63.4 us; the launch traced here: 63.2 us
  starting transfers between devices  23.5 us (37%)
  Pallas kernels  18.5 us (29%)
  waiting for transfers between devices  17.6 us (28%)
  local copies, waits for them, and re-layouts  1.81 us (3%)
  other arithmetic  1.49 us (2%)
    ppermute x19, waiting for transfers between devices, swap(): return lax.ppermute(value, axis, [(i, i ^ distance) for i in range(count)])  14.1 us
    ppermute x11, starting transfers between devices, by_core(): return lax.ppermute(value, 'ctx', pairs)  13.9 us
    ppermute x19, starting transfers between devices, swap(): return lax.ppermute(value, axis, [(i, i ^ distance) for i in range(count)])  9.62 us
    pallas_call x3, Pallas kernels, normalise(): call(functools.partial(norm_kernel, first), 'normalise', [IN_HBM, IN_VMEM...  8.6 us
    pallas_call x6, Pallas kernels, project(): call(functools.partial(project_kernel, [d for d, _ in blocks], len(rows),...  6.17 us
    ppermute x11, waiting for transfers between devices, by_core(): return lax.ppermute(value, 'ctx', pairs)  3.51 us
    unnamed x18, local copies, waits for them, and re-layouts  1.81 us
  transfers between devices with their start and end apart: 30, of which 14 were waited for; matrix products, arithmetic and copies ran while one was open for 1% of the time, Pallas kernels for 26%

profile of v17, /device:TPU:0, one launch (start us, length us, event | category | flops | bytes accessed | tf_op | source)
XLA Modules:
  0.0 63.2 jit_solution(11848050987799756484)
XLA Ops:
  0.0 0.5 collective-permute-start.1
  0.5 0.1 collective-permute-start.2
  0.5 2.9 %collective-permute-start.12 = (bf16[2048,128]{1,0:T(8,128)(2,1)}, bf16[2048,128]{1,0:T(8,128)(2,1)S(1)}, u32[]{:S(2)}, u32[]{:S(2)}) collective-permute-start(bf16[2048,128]{1,0:T(8,128)(2,1)} %bitcast.24), channel_id=1, source_target_pairs={{0,8},{4,20},{8,0},{12,28},{16,24},{20,4},{24,16},{28,12},{1,9},{5... | collective-permute-start | bytes 1572872 | tf_op jit(solution)/shard_map/ppermute | solution.py:64
  3.5 1.6 %collective-permute-start.6 = (bf16[2048,128]{1,0:T(8,128)(2,1)S(1)}, bf16[2048,128]{1,0:T(8,128)(2,1)S(1)}, u32[]{:S(2)}, u32[]{:S(2)}) collective-permute-start(bf16[2048,128]{1,0:T(8,128)(2,1)S(1)} %collective-permute-done.1.refs_6_), channel_id=1, source_target_pairs={{0,8},{4,20},{8,0},{12,28},{16,24},{20,4},{24,16},{28,12},{1,9},{5... | collective-permute-start | bytes 1572872 | tf_op jit(solution)/shard_map/ppermute | solution.py:64
  5.1 0.7 %copy-done.5 = f32[2,2048]{1,0:T(2,128)S(1)} copy-done((f32[2,2048]{1,0:T(2,128)S(1)}, f32[2,2048]{1,0:T(2,128)}, u32[]{:S(2)}) %copy-start.5) | copy-done | bytes 16408
  5.8 0.1 squares.1
  5.9 1.1 %collective-permute-done = f32[2,128]{1,0:T(2,128)S(1)} collective-permute-done((f32[2,128]{1,0:T(2,128)S(1)}, f32[2,128]{1,0:T(2,128)S(1)}, u32[]{:S(2)}, u32[]{:S(2)}) %collective-permute-start) | collective-permute-done | bytes 1056 | tf_op jit(solution)/shard_map/ppermute | solution.py:43
  7.0 1.5 %collective-permute-start.3 = (f32[2,128]{1,0:T(2,128)S(1)}, f32[2,128]{1,0:T(2,128)S(1)}, u32[]{:S(2)}, u32[]{:S(2)}) collective-permute-start(f32[2,128]{1,0:T(2,128)S(1)} %add.53), channel_id=1, source_target_pairs={{0,16},{4,12},{8,24},{12,4},{16,0},{20,28},{24,8},{28,20},{1,17},{... | collective-permute-start | bytes 3080 | tf_op jit(solution)/shard_map/ppermute | solution.py:64
  8.5 0.8 %copy-done.4 = f32[1,16384]{1,0:T(1,128)S(1)} copy-done((f32[1,16384]{1,0:T(1,128)S(1)}, f32[1,16384]{1,0:T(1,128)}, u32[]{:S(2)}) %copy-start.4) | copy-done | bytes 65560
  9.4 3.2 %normalise.3 = (bf16[8,64,2048]{2,1,0:T(8,128)(2,1)S(1)}, bf16[8,64,2048]{2,1,0:T(8,128)(2,1)S(1)}) custom-call(bf16[320,16384]{1,0:T(8,128)(2,1)} %bitcast.36, f32[8,1,2048]{2,1,0:T(1,128)S(1)} %bitcast.31), custom_call_target="tpu_custom_call" | custom-call | flops 1000 | bytes 1000 | tf_op jit(solution)/shard_map/normalise/pallas_call | solution.py:173
  12.6 0.1 collective-permute-start.4
  12.7 0.6 collective-permute-start.8
  13.3 0.5 collective-permute-done.4
  13.8 0.2 collective-permute-start.13
  14.0 0.9 %collective-permute-start.5 = (f32[2,128]{1,0:T(2,128)S(1)}, f32[2,128]{1,0:T(2,128)S(1)}, u32[]{:S(2)}, u32[]{:S(2)}) collective-permute-start(f32[2,128]{1,0:T(2,128)S(1)} %collective-permute-done.4), channel_id=1, source_target_pairs={{0,16},{4,12},{8,24},{12,4},{16,0},{20,28},{24,8},{28,20},{1,17},{... | collective-permute-start | bytes 3080 | tf_op jit(solution)/shard_map/ppermute | solution.py:64
  14.9 3.3 %normalise.4 = (bf16[8,64,2048]{2,1,0:T(8,128)(2,1)S(1)}, bf16[8,64,2048]{2,1,0:T(8,128)(2,1)S(1)}) custom-call(bf16[320,16384]{1,0:T(8,128)(2,1)} %bitcast.37, f32[8,1,2048]{2,1,0:T(1,128)S(1)} %bitcast.32), custom_call_target="tpu_custom_call" | custom-call | flops 1000 | bytes 1000 | tf_op jit(solution)/shard_map/normalise/pallas_call | solution.py:173
  18.3 0.1 copy-done
  18.4 0.1 copy-done.2
  18.5 0.8 %query_products.1 = f32[2,10,128]{2,1,0:T(8,128)S(1)} custom-call(s32[1]{0:T(128)} %bitcast.place_ref, f32[2,128]{1,0:T(2,128)S(1)} %add_add_fusion.2.squares_ref, f32[2,2048]{1,0:T(2,128)S(1)} %copy-done.5, f32[8,1,2048]{2,1,0:T(1,128)S(1)} %bitcast.33, bf16[2048,1024]{1,0:T(8,128)(2,1)S(1)} %bitcast.21, bf16[2048,128]{1,0:T(8,128)(2,1)S(1)} %bitcast.25, ...), custom_call_target="tpu_custom_call" | custom-call | flops 1000 | bytes 1000 | tf_op jit(solution)/shard_map/query_products/pallas_call | solution.py:371
  19.3 0.1 collective-permute-start.7
  19.5 0.5 collective-permute-start.15
  20.0 0.8 %collective-permute-start.14 = (bf16[2048,128]{1,0:T(8,128)(2,1)S(1)}, bf16[2048,128]{1,0:T(8,128)(2,1)S(1)}, u32[]{:S(2)}, u32[]{:S(2)}) collective-permute-start(bf16[2048,128]{1,0:T(8,128)(2,1)S(1)} %collective-permute-done.13.refs_7_), channel_id=1, source_target_pairs={{0,8},{4,20},{8,0},{12,28},{16,24},{20,4},{24,16},{28,12},{1,9},{5... | collective-permute-start | bytes 1572872 | tf_op jit(solution)/shard_map/ppermute | solution.py:64
  20.8 1.2 %collective-permute-start.9 = (f32[2,10,128]{2,1,0:T(8,128)S(1)}, f32[2,10,128]{2,1,0:T(8,128)S(1)}, u32[]{:S(2)}, u32[]{:S(2)}) collective-permute-start(f32[2,10,128]{2,1,0:T(8,128)S(1)} %add.57), channel_id=1, source_target_pairs={{0,16},{4,12},{8,24},{12,4},{16,0},{20,28},{24,8},{28,20},{1,17},{... | collective-permute-start | bytes 30728 | tf_op jit(solution)/shard_map/ppermute | solution.py:64
  22.0 2.1 %normalise.5.refs_4_ = bf16[8,64,2048]{2,1,0:T(8,128)(2,1)S(1)} custom-call(bf16[320,16384]{1,0:T(8,128)(2,1)} %bitcast.38, f32[8,1,2048]{2,1,0:T(1,128)S(1)} %bitcast.34), custom_call_target="tpu_custom_call" | custom-call | flops 1000 | bytes 1000 | tf_op jit(solution)/shard_map/normalise/pallas_call | solution.py:173
  24.2 0.7 %collective-permute-done.9 = f32[2,10,128]{2,1,0:T(8,128)S(1)} collective-permute-done((f32[2,10,128]{2,1,0:T(8,128)S(1)}, f32[2,10,128]{2,1,0:T(8,128)S(1)}, u32[]{:S(2)}, u32[]{:S(2)}) %collective-permute-start.9) | collective-permute-done | bytes 10272 | tf_op jit(solution)/shard_map/ppermute | solution.py:64
  24.9 0.6 %multiply_sine_fusion = (f32[320,64]{1,0:T(8,128)S(1)}, f32[320,64]{1,0:T(8,128)S(1)}) fusion(f32[64]{0:T(128)S(1)} %multiply_exponential_fusion, f32[320]{0:T(512)S(1)} %add_convert_fusion), kind=kLoop, calls=%fused_computation | loop fusion | flops 20480 | bytes 165376 | tf_op jit(solution)/shard_map/sin | solution.py:97
  25.5 0.6 collective-permute-start.17
  26.1 0.1 multiply_sine_fusion.1
  26.2 1.3 %collective-permute-start.20 = (bf16[2048,128]{1,0:T(8,128)(2,1)S(1)}, bf16[2048,128]{1,0:T(8,128)(2,1)S(1)}, u32[]{:S(2)}, u32[]{:S(2)}) collective-permute-start(bf16[2048,128]{1,0:T(8,128)(2,1)S(1)} %collective-permute-done.2.refs_6_), channel_id=1, source_target_pairs={{0,8},{4,20},{8,0},{12,28},{16,24},{20,4},{24,16},{28,12},{1,9},{5... | collective-permute-start | bytes 1572872 | tf_op jit(solution)/shard_map/ppermute | solution.py:64
  27.5 0.9 %project.6.refs_9_ = f32[320,128]{1,0:T(8,128)S(1)} custom-call(s32[1]{0:T(128)} %bitcast.place_ref, bf16[8,64,2048]{2,1,0:T(8,128)(2,1)S(1)} %get-tuple-element.36.refs_0_, bf16[8,64,2048]{2,1,0:T(8,128)(2,1)S(1)} %get-tuple-element.37.refs_1_, bf16[8,64,2048]{2,1,0:T(8,128)(2,1)S(1)} %get-tuple-element.40.refs_2_, ...), custom_call_target="tpu_custom_call" | custom-call | flops 1000 | bytes 1000 | tf_op jit(solution)/shard_map/project/pallas_call | solution.py:218
  28.4 1.2 %collective-permute-start.18 = (f32[2,10,128]{2,1,0:T(8,128)S(1)}, f32[2,10,128]{2,1,0:T(8,128)S(1)}, u32[]{:S(2)}, u32[]{:S(2)}) collective-permute-start(f32[2,10,128]{2,1,0:T(8,128)S(1)} %collective-permute-done.17), channel_id=1, source_target_pairs={{0,16},{4,12},{8,24},{12,4},{16,0},{20,28},{24,8},{28,20},{1,17},{... | collective-permute-start | bytes 30728 | tf_op jit(solution)/shard_map/ppermute | solution.py:64
  29.5 1.5 %project.7.refs_7_ = f32[320,128]{1,0:T(8,128)S(1)} custom-call(s32[1]{0:T(128)} %bitcast.place_ref, bf16[8,64,2048]{2,1,0:T(8,128)(2,1)S(1)} %get-tuple-element.36.refs_0_, bf16[8,64,2048]{2,1,0:T(8,128)(2,1)S(1)} %get-tuple-element.37.refs_1_, bf16[8,64,2048]{2,1,0:T(8,128)(2,1)S(1)} %get-tuple-element.40.refs_2_, ...), custom_call_target="tpu_custom_call" | custom-call | flops 1000 | bytes 1000 | tf_op jit(solution)/shard_map/project/pallas_call | solution.py:218
  31.1 0.1 collective-permute-start.16
  31.2 0.9 %collective-permute-start.11 = (bf16[2048,128]{1,0:T(8,128)(2,1)S(1)}, bf16[2048,128]{1,0:T(8,128)(2,1)S(1)}, u32[]{:S(2)}, u32[]{:S(2)}) collective-permute-start(bf16[2048,128]{1,0:T(8,128)(2,1)S(1)} %collective-permute-done.10.refs_7_), channel_id=1, source_target_pairs={{0,8},{4,20},{8,0},{12,28},{16,24},{20,4},{24,16},{28,12},{1,9},{5... | collective-permute-start | bytes 1572872 | tf_op jit(solution)/shard_map/ppermute | solution.py:64
  32.1 0.3 collective-permute-done.18
  32.4 0.0 copy-start.7
  32.4 0.6 collective-permute-done.16.refs_6_
  33.1 0.9 %project.8.refs_0_ = f32[320,128]{1,0:T(8,128)S(1)} custom-call(s32[1]{0:T(128)} %bitcast.place_ref, bf16[8,64,2048]{2,1,0:T(8,128)(2,1)S(1)} %get-tuple-element.36.refs_0_, bf16[8,64,2048]{2,1,0:T(8,128)(2,1)S(1)} %get-tuple-element.37.refs_1_, bf16[8,64,2048]{2,1,0:T(8,128)(2,1)S(1)} %get-tuple-element.40.refs_2_, ...), custom_call_target="tpu_custom_call" | custom-call | flops 1000 | bytes 1000 | tf_op jit(solution)/shard_map/project/pallas_call | solution.py:218
  33.9 1.0 %scores.1 = (f32[8,320]{1,0:T(8,128)S(1)}, f32[8,128]{1,0:T(8,128)S(1)}, f32[8,128]{1,0:T(8,128)S(1)}) custom-call(s32[1]{0:T(128)} %bitcast.place_ref, s32[2]{0:T(128)S(1)} %copy-done.7, f32[320,128]{1,0:T(8,128)S(1)} %project.8.refs_0_, f32[320,64]{1,0:T(8,128)S(1)} %get-tuple-element.62.refs_1_, f32[320,64]{1,0:T(8,128)S(1)} %get-tuple-element.61.refs_2_, ...), custom_call_target="tpu_custom_call" | custom-call | flops 1000 | bytes 1000 | tf_op jit(solution)/shard_map/scores/pallas_call | solution.py:397
  34.9 0.1 collective-permute-start.19
  35.1 1.0 %collective-permute-done.19 = f32[8,128]{1,0:T(8,128)S(1)} collective-permute-done((f32[8,128]{1,0:T(8,128)S(1)}, f32[8,128]{1,0:T(8,128)S(1)}, u32[]{:S(2)}, u32[]{:S(2)}) %collective-permute-start.19) | collective-permute-done | bytes 4128 | tf_op jit(solution)/shard_map/ppermute | solution.py:43
  36.1 0.2 collective-permute-start.23
  36.3 0.9 %collective-permute-start.21 = (f32[8,128]{1,0:T(8,128)S(1)}, f32[8,128]{1,0:T(8,128)S(1)}, u32[]{:S(2)}, u32[]{:S(2)}) collective-permute-start(f32[8,128]{1,0:T(8,128)S(1)} %max.6), channel_id=1, source_target_pairs={{0,16},{4,12},{8,24},{12,4},{16,0},{20,28},{24,8},{28,20},{1,17},{... | collective-permute-start | bytes 12296 | tf_op jit(solution)/shard_map/ppermute | solution.py:64
  37.2 1.5 %project.9.refs_7_ = f32[320,128]{1,0:T(8,128)S(1)} custom-call(s32[1]{0:T(128)} %bitcast.place_ref, bf16[8,64,2048]{2,1,0:T(8,128)(2,1)S(1)} %get-tuple-element.36.refs_0_, bf16[8,64,2048]{2,1,0:T(8,128)(2,1)S(1)} %get-tuple-element.37.refs_1_, bf16[8,64,2048]{2,1,0:T(8,128)(2,1)S(1)} %get-tuple-element.40.refs_2_, ...), custom_call_target="tpu_custom_call" | custom-call | flops 1000 | bytes 1000 | tf_op jit(solution)/shard_map/project/pallas_call | solution.py:218
  38.8 1.2 %collective-permute-done.21 = f32[8,128]{1,0:T(8,128)S(1)} collective-permute-done((f32[8,128]{1,0:T(8,128)S(1)}, f32[8,128]{1,0:T(8,128)S(1)}, u32[]{:S(2)}, u32[]{:S(2)}) %collective-permute-start.21) | collective-permute-done | bytes 4128 | tf_op jit(solution)/shard_map/ppermute | solution.py:64
  40.0 1.3 %collective-permute-done.11.refs_5_ = bf16[2048,128]{1,0:T(8,128)(2,1)S(1)} collective-permute-done((bf16[2048,128]{1,0:T(8,128)(2,1)S(1)}, bf16[2048,128]{1,0:T(8,128)(2,1)S(1)}, u32[]{:S(2)}, u32[]{:S(2)}) %collective-permute-start.11) | collective-permute-done | bytes 524320 | tf_op jit(solution)/shard_map/ppermute | solution.py:64
  41.3 0.5 collective-permute-start.24
  41.8 0.9 %project.10.refs_6_ = f32[320,128]{1,0:T(8,128)S(1)} custom-call(s32[1]{0:T(128)} %bitcast.place_ref, bf16[8,64,2048]{2,1,0:T(8,128)(2,1)S(1)} %get-tuple-element.36.refs_0_, bf16[8,64,2048]{2,1,0:T(8,128)(2,1)S(1)} %get-tuple-element.37.refs_1_, bf16[8,64,2048]{2,1,0:T(8,128)(2,1)S(1)} %get-tuple-element.40.refs_2_, ...), custom_call_target="tpu_custom_call" | custom-call | flops 1000 | bytes 1000 | tf_op jit(solution)/shard_map/project/pallas_call | solution.py:218
  42.7 0.5 collective-permute-done.24
  43.2 0.5 project.11.refs_6_
  43.7 0.0 copy-start.1
  43.8 1.2 %weighted_values.1 = f32[8,256]{1,0:T(8,128)S(1)} custom-call(s32[1]{0:T(128)} %bitcast.place_ref, s32[2]{0:T(128)S(1)} %copy-done.7, bf16[8,64,2048]{2,1,0:T(8,128)(2,1)S(1)} %get-tuple-element.36.refs_0_, bf16[8,64,2048]{2,1,0:T(8,128)(2,1)S(1)} %get-tuple-element.37.refs_1_, bf16[8,64,2048]{2,1,0:T(8,128)(2,1)S(1)} %get-tuple-element.40.refs_2_, ...), custom_call_target="tpu_custom_call" | custom-call | flops 1000 | bytes 1000 | tf_op jit(solution)/shard_map/weighted_values/pallas_call | solution.py:422
  44.9 0.1 collective-permute-start.25
  45.1 1.0 %collective-permute-done.25 = f32[8,256]{1,0:T(8,128)S(1)} collective-permute-done((f32[8,256]{1,0:T(8,128)S(1)}, f32[8,256]{1,0:T(8,128)S(1)}, u32[]{:S(2)}, u32[]{:S(2)}) %collective-permute-start.25) | collective-permute-done | bytes 8224 | tf_op jit(solution)/shard_map/ppermute | solution.py:43
  46.1 1.2 %collective-permute-start.26 = (f32[8,256]{1,0:T(8,128)S(1)}, f32[8,256]{1,0:T(8,128)S(1)}, u32[]{:S(2)}, u32[]{:S(2)}) collective-permute-start(f32[8,256]{1,0:T(8,128)S(1)} %add.64), channel_id=1, source_target_pairs={{0,8},{4,12},{8,0},{12,4},{16,24},{20,28},{24,16},{28,20},{1,9},{5... | collective-permute-start | bytes 24584 | tf_op jit(solution)/shard_map/ppermute | solution.py:43
  47.3 2.4 %collective-permute-done.26 = f32[8,256]{1,0:T(8,128)S(1)} collective-permute-done((f32[8,256]{1,0:T(8,128)S(1)}, f32[8,256]{1,0:T(8,128)S(1)}, u32[]{:S(2)}, u32[]{:S(2)}) %collective-permute-start.26) | collective-permute-done | bytes 8224 | tf_op jit(solution)/shard_map/ppermute | solution.py:43
  49.8 1.1 %collective-permute-start.27 = (f32[8,256]{1,0:T(8,128)S(1)}, f32[8,256]{1,0:T(8,128)S(1)}, u32[]{:S(2)}, u32[]{:S(2)}) collective-permute-start(f32[8,256]{1,0:T(8,128)S(1)} %add.65.mine_ref), channel_id=1, source_target_pairs={{0,16},{4,20},{8,24},{12,28},{16,0},{20,4},{24,8},{28,12},{1,17},{... | collective-permute-start | bytes 24584 | tf_op jit(solution)/shard_map/ppermute | solution.py:43
  50.9 2.5 %collective-permute-done.27.other_ref = f32[8,256]{1,0:T(8,128)S(1)} collective-permute-done((f32[8,256]{1,0:T(8,128)S(1)}, f32[8,256]{1,0:T(8,128)S(1)}, u32[]{:S(2)}, u32[]{:S(2)}) %collective-permute-start.27) | collective-permute-done | bytes 8224 | tf_op jit(solution)/shard_map/ppermute | solution.py:43
  53.4 0.6 %output_products.1 = f32[2,2048]{1,0:T(2,128)S(1)} custom-call(s32[1]{0:T(128)} %bitcast.place_ref, f32[8,256]{1,0:T(8,128)S(1)} %add.65.mine_ref, f32[8,256]{1,0:T(8,128)S(1)} %collective-permute-done.27.other_ref, bf16[1024,2048]{1,0:T(8,128)(2,1)S(1)} %bitcast.22), custom_call_target="tpu_custom_call" | custom-call | flops 1000 | bytes 1000 | tf_op jit(solution)/shard_map/output_products/pallas_call | solution.py:440
  54.1 1.6 %collective-permute-start.28 = (f32[2,2048]{1,0:T(2,128)S(1)}, f32[2,2048]{1,0:T(2,128)S(1)}, u32[]{:S(2)}, u32[]{:S(2)}) collective-permute-start(f32[2,2048]{1,0:T(2,128)S(1)} %output_products.1), channel_id=1, source_target_pairs={{0,1},{1,0},{2,3},{3,2},{4,5},{5,4},{6,7},{7,6},{8,9},{9,8},{10,11... | collective-permute-start | bytes 49160 | tf_op jit(solution)/shard_map/ppermute | solution.py:43
  55.7 2.2 %collective-permute-done.28 = f32[2,2048]{1,0:T(2,128)S(1)} collective-permute-done((f32[2,2048]{1,0:T(2,128)S(1)}, f32[2,2048]{1,0:T(2,128)S(1)}, u32[]{:S(2)}, u32[]{:S(2)}) %collective-permute-start.28) | collective-permute-done | bytes 16416 | tf_op jit(solution)/shard_map/ppermute | solution.py:43
  57.8 2.7 %collective-permute-start.29 = (f32[2,2048]{1,0:T(2,128)S(1)}, f32[2,2048]{1,0:T(2,128)S(1)}, u32[]{:S(2)}, u32[]{:S(2)}) collective-permute-start(f32[2,2048]{1,0:T(2,128)S(1)} %add.66), channel_id=1, source_target_pairs={{0,2},{1,3},{2,0},{3,1},{4,6},{5,7},{6,4},{7,5},{8,10},{9,11},{10,... | collective-permute-start | bytes 49160 | tf_op jit(solution)/shard_map/ppermute | solution.py:43
  60.5 2.0 %collective-permute-done.29 = f32[2,2048]{1,0:T(2,128)S(1)} collective-permute-done((f32[2,2048]{1,0:T(2,128)S(1)}, f32[2,2048]{1,0:T(2,128)S(1)}, u32[]{:S(2)}, u32[]{:S(2)}) %collective-permute-start.29) | collective-permute-done | bytes 16416 | tf_op jit(solution)/shard_map/ppermute | solution.py:43
  62.5 0.6 add_add_fusion
  (47 shorter events, 0.2 us)
Async XLA Ops:
  0.0 3.5 %collective-permute-start.1 = (bf16[2048,128]{1,0:T(8,128)(2,1)}, bf16[2048,128]{1,0:T(8,128)(2,1)S(1)}, u32[]{:S(2)}, u32[]{:S(2)}) collective-permute-start(bf16[2048,128]{1,0:T(8,128)(2,1)} %bitcast.23), channel_id=1, source_target_pairs={{0,4},{4,0},{8,12},{12,8},{16,20},{20,16},{24,28},{28,24},{1,5},{5... | collective-permute-start | bytes 1572872 | tf_op jit(solution)/shard_map/ppermute | solution.py:43
  0.5 6.6 %collective-permute-start.2 = (bf16[2048,128]{1,0:T(8,128)(2,1)}, bf16[2048,128]{1,0:T(8,128)(2,1)S(1)}, u32[]{:S(2)}, u32[]{:S(2)}) collective-permute-start(bf16[2048,128]{1,0:T(8,128)(2,1)} %bitcast.27), channel_id=1, source_target_pairs={{0,4},{4,0},{8,12},{12,8},{16,20},{20,16},{24,28},{28,24},{1,5},{5... | collective-permute-start | bytes 1572872 | tf_op jit(solution)/shard_map/ppermute | solution.py:43
  0.5 12.8 %collective-permute-start.12 = (bf16[2048,128]{1,0:T(8,128)(2,1)}, bf16[2048,128]{1,0:T(8,128)(2,1)S(1)}, u32[]{:S(2)}, u32[]{:S(2)}) collective-permute-start(bf16[2048,128]{1,0:T(8,128)(2,1)} %bitcast.24), channel_id=1, source_target_pairs={{0,8},{4,20},{8,0},{12,28},{16,24},{20,4},{24,16},{28,12},{1,9},{5... | collective-permute-start | bytes 1572872 | tf_op jit(solution)/shard_map/ppermute | solution.py:64
  3.5 14.8 %collective-permute-start.6 = (bf16[2048,128]{1,0:T(8,128)(2,1)S(1)}, bf16[2048,128]{1,0:T(8,128)(2,1)S(1)}, u32[]{:S(2)}, u32[]{:S(2)}) collective-permute-start(bf16[2048,128]{1,0:T(8,128)(2,1)S(1)} %collective-permute-done.1.refs_6_), channel_id=1, source_target_pairs={{0,8},{4,20},{8,0},{12,28},{16,24},{20,4},{24,16},{28,12},{1,9},{5... | collective-permute-start | bytes 1572872 | tf_op jit(solution)/shard_map/ppermute | solution.py:64
  5.1 0.7 %copy-start.5 = (f32[2,2048]{1,0:T(2,128)S(1)}, f32[2,2048]{1,0:T(2,128)}, u32[]{:S(2)}) copy-start(f32[2,2048]{1,0:T(2,128)} %tokens_ref.3) | copy-start | bytes 49156
  5.9 1.1 %collective-permute-start = (f32[2,128]{1,0:T(2,128)S(1)}, f32[2,128]{1,0:T(2,128)S(1)}, u32[]{:S(2)}, u32[]{:S(2)}) collective-permute-start(f32[2,128]{1,0:T(2,128)S(1)} %get-tuple-element.33), channel_id=1, source_target_pairs={{0,4},{4,0},{8,12},{12,8},{16,20},{20,16},{24,28},{28,24},{1,5},{5... | collective-permute-start | bytes 3080 | tf_op jit(solution)/shard_map/ppermute | solution.py:43
  7.0 5.6 %collective-permute-start.3 = (f32[2,128]{1,0:T(2,128)S(1)}, f32[2,128]{1,0:T(2,128)S(1)}, u32[]{:S(2)}, u32[]{:S(2)}) collective-permute-start(f32[2,128]{1,0:T(2,128)S(1)} %add.53), channel_id=1, source_target_pairs={{0,16},{4,12},{8,24},{12,4},{16,0},{20,28},{24,8},{28,20},{1,17},{... | collective-permute-start | bytes 3080 | tf_op jit(solution)/shard_map/ppermute | solution.py:64
  8.5 0.8 %copy-start.4 = (f32[1,16384]{1,0:T(1,128)S(1)}, f32[1,16384]{1,0:T(1,128)}, u32[]{:S(2)}) copy-start(f32[1,16384]{1,0:T(1,128)} %param.11) | copy-start | bytes 196612
  9.4 3.3 %copy-start.3 = (bf16[1,2048,128]{2,1,0:T(8,128)(2,1)S(1)}, bf16[1,2048,128]{2,1,0:T(8,128)(2,1)}, u32[]{:S(2)}) copy-start(bf16[1,2048,128]{2,1,0:T(8,128)(2,1)} %param.14) | copy-start | bytes 1572868
  12.6 1.2 %collective-permute-start.4 = (f32[2,128]{1,0:T(2,128)S(1)}, f32[2,128]{1,0:T(2,128)S(1)}, u32[]{:S(2)}, u32[]{:S(2)}) collective-permute-start(f32[2,128]{1,0:T(2,128)S(1)} %collective-permute-done.3), channel_id=1, source_target_pairs={{0,4},{4,0},{8,12},{12,8},{16,20},{20,16},{24,28},{28,24},{1,5},{5... | collective-permute-start | bytes 3080 | tf_op jit(solution)/shard_map/ppermute | solution.py:43
  12.7 12.2 %collective-permute-start.8 = (bf16[2048,128]{1,0:T(8,128)(2,1)S(1)}, bf16[2048,128]{1,0:T(8,128)(2,1)S(1)}, u32[]{:S(2)}, u32[]{:S(2)}) collective-permute-start(bf16[2048,128]{1,0:T(8,128)(2,1)S(1)} %bitcast.28), channel_id=1, source_target_pairs={{0,8},{4,20},{8,0},{12,28},{16,24},{20,4},{24,16},{28,12},{1,9},{5... | collective-permute-start | bytes 1572872 | tf_op jit(solution)/shard_map/ppermute | solution.py:64
  13.8 6.2 %collective-permute-start.13 = (bf16[2048,128]{1,0:T(8,128)(2,1)S(1)}, bf16[2048,128]{1,0:T(8,128)(2,1)S(1)}, u32[]{:S(2)}, u32[]{:S(2)}) collective-permute-start(bf16[2048,128]{1,0:T(8,128)(2,1)S(1)} %collective-permute-done.12.refs_5_), channel_id=1, source_target_pairs={{0,4},{4,0},{8,12},{12,8},{16,20},{20,16},{24,28},{28,24},{1,5},{5... | collective-permute-start | bytes 1572872 | tf_op jit(solution)/shard_map/ppermute | solution.py:43
  14.0 4.2 %collective-permute-start.5 = (f32[2,128]{1,0:T(2,128)S(1)}, f32[2,128]{1,0:T(2,128)S(1)}, u32[]{:S(2)}, u32[]{:S(2)}) collective-permute-start(f32[2,128]{1,0:T(2,128)S(1)} %collective-permute-done.4), channel_id=1, source_target_pairs={{0,16},{4,12},{8,24},{12,4},{16,0},{20,28},{24,8},{28,20},{1,17},{... | collective-permute-start | bytes 3080 | tf_op jit(solution)/shard_map/ppermute | solution.py:64
  14.9 3.4 %copy-start = (bf16[1,2048,1024]{2,1,0:T(8,128)(2,1)S(1)}, bf16[1,2048,1024]{2,1,0:T(8,128)(2,1)}, u32[]{:S(2)}) copy-start(bf16[1,2048,1024]{2,1,0:T(8,128)(2,1)} %param.12) | copy-start | bytes 12582916
  14.9 3.6 %copy-start.2 = (bf16[1,2048,128]{2,1,0:T(8,128)(2,1)S(1)}, bf16[1,2048,128]{2,1,0:T(8,128)(2,1)}, u32[]{:S(2)}) copy-start(bf16[1,2048,128]{2,1,0:T(8,128)(2,1)} %param.13) | copy-start | bytes 1572868
  19.3 1.5 %collective-permute-start.7 = (f32[2,10,128]{2,1,0:T(8,128)S(1)}, f32[2,10,128]{2,1,0:T(8,128)S(1)}, u32[]{:S(2)}, u32[]{:S(2)}) collective-permute-start(f32[2,10,128]{2,1,0:T(8,128)S(1)} %query_products.1), channel_id=1, source_target_pairs={{0,4},{4,0},{8,12},{12,8},{16,20},{20,16},{24,28},{28,24},{1,5},{5... | collective-permute-start | bytes 30728 | tf_op jit(solution)/shard_map/ppermute | solution.py:43
  19.5 10.0 %collective-permute-start.15 = (bf16[2048,128]{1,0:T(8,128)(2,1)S(1)}, bf16[2048,128]{1,0:T(8,128)(2,1)S(1)}, u32[]{:S(2)}, u32[]{:S(2)}) collective-permute-start(bf16[2048,128]{1,0:T(8,128)(2,1)S(1)} %collective-permute-done.6.refs_6_), channel_id=1, source_target_pairs={{0,4},{4,0},{8,12},{12,8},{16,20},{20,16},{24,28},{28,24},{1,5},{5... | collective-permute-start | bytes 1572872 | tf_op jit(solution)/shard_map/ppermute | solution.py:43
  20.0 11.1 %collective-permute-start.14 = (bf16[2048,128]{1,0:T(8,128)(2,1)S(1)}, bf16[2048,128]{1,0:T(8,128)(2,1)S(1)}, u32[]{:S(2)}, u32[]{:S(2)}) collective-permute-start(bf16[2048,128]{1,0:T(8,128)(2,1)S(1)} %collective-permute-done.13.refs_7_), channel_id=1, source_target_pairs={{0,8},{4,20},{8,0},{12,28},{16,24},{20,4},{24,16},{28,12},{1,9},{5... | collective-permute-start | bytes 1572872 | tf_op jit(solution)/shard_map/ppermute | solution.py:64
  20.8 4.0 %collective-permute-start.9 = (f32[2,10,128]{2,1,0:T(8,128)S(1)}, f32[2,10,128]{2,1,0:T(8,128)S(1)}, u32[]{:S(2)}, u32[]{:S(2)}) collective-permute-start(f32[2,10,128]{2,1,0:T(8,128)S(1)} %add.57), channel_id=1, source_target_pairs={{0,16},{4,12},{8,24},{12,4},{16,0},{20,28},{24,8},{28,20},{1,17},{... | collective-permute-start | bytes 30728 | tf_op jit(solution)/shard_map/ppermute | solution.py:64
  22.0 3.5 %copy-start.8 = (s32[2]{0:T(128)S(1)}, s32[2]{0:T(128)}, u32[]{:S(2)}) copy-start(s32[2]{0:T(128)} %param.17) | copy-start | bytes 28
  24.9 6.3 %collective-permute-start.10 = (bf16[2048,128]{1,0:T(8,128)(2,1)S(1)}, bf16[2048,128]{1,0:T(8,128)(2,1)S(1)}, u32[]{:S(2)}, u32[]{:S(2)}) collective-permute-start(bf16[2048,128]{1,0:T(8,128)(2,1)S(1)} %collective-permute-done.8.refs_8_), channel_id=1, source_target_pairs={{0,4},{4,0},{8,12},{12,8},{16,20},{20,16},{24,28},{28,24},{1,5},{5... | collective-permute-start | bytes 1572872 | tf_op jit(solution)/shard_map/ppermute | solution.py:43
  25.5 2.8 %collective-permute-start.17 = (f32[2,10,128]{2,1,0:T(8,128)S(1)}, f32[2,10,128]{2,1,0:T(8,128)S(1)}, u32[]{:S(2)}, u32[]{:S(2)}) collective-permute-start(f32[2,10,128]{2,1,0:T(8,128)S(1)} %collective-permute-done.9), channel_id=1, source_target_pairs={{0,4},{4,0},{8,12},{12,8},{16,20},{20,16},{24,28},{28,24},{1,5},{5... | collective-permute-start | bytes 30728 | tf_op jit(solution)/shard_map/ppermute | solution.py:43
  26.2 9.9 %collective-permute-start.20 = (bf16[2048,128]{1,0:T(8,128)(2,1)S(1)}, bf16[2048,128]{1,0:T(8,128)(2,1)S(1)}, u32[]{:S(2)}, u32[]{:S(2)}) collective-permute-start(bf16[2048,128]{1,0:T(8,128)(2,1)S(1)} %collective-permute-done.2.refs_6_), channel_id=1, source_target_pairs={{0,8},{4,20},{8,0},{12,28},{16,24},{20,4},{24,16},{28,12},{1,9},{5... | collective-permute-start | bytes 1572872 | tf_op jit(solution)/shard_map/ppermute | solution.py:64
  28.4 4.0 %collective-permute-start.18 = (f32[2,10,128]{2,1,0:T(8,128)S(1)}, f32[2,10,128]{2,1,0:T(8,128)S(1)}, u32[]{:S(2)}, u32[]{:S(2)}) collective-permute-start(f32[2,10,128]{2,1,0:T(8,128)S(1)} %collective-permute-done.17), channel_id=1, source_target_pairs={{0,16},{4,12},{8,24},{12,4},{16,0},{20,28},{24,8},{28,20},{1,17},{... | collective-permute-start | bytes 30728 | tf_op jit(solution)/shard_map/ppermute | solution.py:64
  31.1 2.0 %collective-permute-start.16 = (bf16[2048,128]{1,0:T(8,128)(2,1)S(1)}, bf16[2048,128]{1,0:T(8,128)(2,1)S(1)}, u32[]{:S(2)}, u32[]{:S(2)}) collective-permute-start(bf16[2048,128]{1,0:T(8,128)(2,1)S(1)} %collective-permute-done.14.refs_5_), channel_id=1, source_target_pairs={{0,4},{4,0},{8,12},{12,8},{16,20},{20,16},{24,28},{28,24},{1,5},{5... | collective-permute-start | bytes 1572872 | tf_op jit(solution)/shard_map/ppermute | solution.py:43
  31.2 10.1 %collective-permute-start.11 = (bf16[2048,128]{1,0:T(8,128)(2,1)S(1)}, bf16[2048,128]{1,0:T(8,128)(2,1)S(1)}, u32[]{:S(2)}, u32[]{:S(2)}) collective-permute-start(bf16[2048,128]{1,0:T(8,128)(2,1)S(1)} %collective-permute-done.10.refs_7_), channel_id=1, source_target_pairs={{0,8},{4,20},{8,0},{12,28},{16,24},{20,4},{24,16},{28,12},{1,9},{5... | collective-permute-start | bytes 1572872 | tf_op jit(solution)/shard_map/ppermute | solution.py:64
  32.4 1.5 %copy-start.7 = (s32[2]{0:T(128)S(1)}, s32[2]{0:T(128)}, u32[]{:S(2)}) copy-start(s32[2]{0:T(128)} %lengths_ref.3) | copy-start | bytes 28
  34.9 1.2 %collective-permute-start.19 = (f32[8,128]{1,0:T(8,128)S(1)}, f32[8,128]{1,0:T(8,128)S(1)}, u32[]{:S(2)}, u32[]{:S(2)}) collective-permute-start(f32[8,128]{1,0:T(8,128)S(1)} %get-tuple-element.53), channel_id=1, source_target_pairs={{0,4},{4,0},{8,12},{12,8},{16,20},{20,16},{24,28},{28,24},{1,5},{5... | collective-permute-start | bytes 12296 | tf_op jit(solution)/shard_map/ppermute | solution.py:43
  36.1 5.7 %collective-permute-start.23 = (bf16[2048,128]{1,0:T(8,128)(2,1)S(1)}, bf16[2048,128]{1,0:T(8,128)(2,1)S(1)}, u32[]{:S(2)}, u32[]{:S(2)}) collective-permute-start(bf16[2048,128]{1,0:T(8,128)(2,1)S(1)} %collective-permute-done.20.refs_5_), channel_id=1, source_target_pairs={{0,4},{4,0},{8,12},{12,8},{16,20},{20,16},{24,28},{28,24},{1,5},{5... | collective-permute-start | bytes 1572872 | tf_op jit(solution)/shard_map/ppermute | solution.py:43
  36.3 3.7 %collective-permute-start.21 = (f32[8,128]{1,0:T(8,128)S(1)}, f32[8,128]{1,0:T(8,128)S(1)}, u32[]{:S(2)}, u32[]{:S(2)}) collective-permute-start(f32[8,128]{1,0:T(8,128)S(1)} %max.6), channel_id=1, source_target_pairs={{0,16},{4,12},{8,24},{12,4},{16,0},{20,28},{24,8},{28,20},{1,17},{... | collective-permute-start | bytes 12296 | tf_op jit(solution)/shard_map/ppermute | solution.py:64
  41.3 2.4 %collective-permute-start.22 = (bf16[2048,128]{1,0:T(8,128)(2,1)S(1)}, bf16[2048,128]{1,0:T(8,128)(2,1)S(1)}, u32[]{:S(2)}, u32[]{:S(2)}) collective-permute-start(bf16[2048,128]{1,0:T(8,128)(2,1)S(1)} %collective-permute-done.11.refs_5_), channel_id=1, source_target_pairs={{0,4},{4,0},{8,12},{12,8},{16,20},{20,16},{24,28},{28,24},{1,5},{5... | collective-permute-start | bytes 1572872 | tf_op jit(solution)/shard_map/ppermute | solution.py:43
  41.3 1.9 %collective-permute-start.24 = (f32[8,128]{1,0:T(8,128)S(1)}, f32[8,128]{1,0:T(8,128)S(1)}, u32[]{:S(2)}, u32[]{:S(2)}) collective-permute-start(f32[8,128]{1,0:T(8,128)S(1)} %max.7), channel_id=1, source_target_pairs={{0,4},{4,0},{8,12},{12,8},{16,20},{20,16},{24,28},{28,24},{1,5},{5... | collective-permute-start | bytes 12296 | tf_op jit(solution)/shard_map/ppermute | solution.py:43
  43.7 9.7 %copy-start.1 = (bf16[1,1024,2048]{2,1,0:T(8,128)(2,1)S(1)}, bf16[1,1024,2048]{2,1,0:T(8,128)(2,1)}, u32[]{:S(2)}) copy-start(bf16[1,1024,2048]{2,1,0:T(8,128)(2,1)} %param.15) | copy-start | bytes 12582916
  44.9 1.2 %collective-permute-start.25 = (f32[8,256]{1,0:T(8,128)S(1)}, f32[8,256]{1,0:T(8,128)S(1)}, u32[]{:S(2)}, u32[]{:S(2)}) collective-permute-start(f32[8,256]{1,0:T(8,128)S(1)} %weighted_values.1), channel_id=1, source_target_pairs={{0,4},{4,0},{8,12},{12,8},{16,20},{20,16},{24,28},{28,24},{1,5},{5... | collective-permute-start | bytes 24584 | tf_op jit(solution)/shard_map/ppermute | solution.py:43
  46.1 3.7 %collective-permute-start.26 = (f32[8,256]{1,0:T(8,128)S(1)}, f32[8,256]{1,0:T(8,128)S(1)}, u32[]{:S(2)}, u32[]{:S(2)}) collective-permute-start(f32[8,256]{1,0:T(8,128)S(1)} %add.64), channel_id=1, source_target_pairs={{0,8},{4,12},{8,0},{12,4},{16,24},{20,28},{24,16},{28,20},{1,9},{5... | collective-permute-start | bytes 24584 | tf_op jit(solution)/shard_map/ppermute | solution.py:43
  49.8 3.7 %collective-permute-start.27 = (f32[8,256]{1,0:T(8,128)S(1)}, f32[8,256]{1,0:T(8,128)S(1)}, u32[]{:S(2)}, u32[]{:S(2)}) collective-permute-start(f32[8,256]{1,0:T(8,128)S(1)} %add.65.mine_ref), channel_id=1, source_target_pairs={{0,16},{4,20},{8,24},{12,28},{16,0},{20,4},{24,8},{28,12},{1,17},{... | collective-permute-start | bytes 24584 | tf_op jit(solution)/shard_map/ppermute | solution.py:43
  53.4 9.1 %copy-start.6 = (f32[2,2048]{1,0:T(2,128)S(1)}, f32[2,2048]{1,0:T(2,128)}, u32[]{:S(2)}) copy-start(f32[2,2048]{1,0:T(2,128)} %tokens_ref.3) | copy-start | bytes 49156
  54.1 3.8 %collective-permute-start.28 = (f32[2,2048]{1,0:T(2,128)S(1)}, f32[2,2048]{1,0:T(2,128)S(1)}, u32[]{:S(2)}, u32[]{:S(2)}) collective-permute-start(f32[2,2048]{1,0:T(2,128)S(1)} %output_products.1), channel_id=1, source_target_pairs={{0,1},{1,0},{2,3},{3,2},{4,5},{5,4},{6,7},{7,6},{8,9},{9,8},{10,11... | collective-permute-start | bytes 49160 | tf_op jit(solution)/shard_map/ppermute | solution.py:43
  57.8 4.7 %collective-permute-start.29 = (f32[2,2048]{1,0:T(2,128)S(1)}, f32[2,2048]{1,0:T(2,128)S(1)}, u32[]{:S(2)}, u32[]{:S(2)}) collective-permute-start(f32[2,2048]{1,0:T(2,128)S(1)} %add.66), channel_id=1, source_target_pairs={{0,2},{1,3},{2,0},{3,1},{4,6},{5,7},{6,4},{7,5},{8,10},{9,11},{10,... | collective-permute-start | bytes 49160 | tf_op jit(solution)/shard_map/ppermute | solution.py:43

commit v18 on v17

--- a/solution.py
+++ b/solution.py
@@ -391,9 +391,10 @@
     key_mid = key_total
     key_total = project(places, rows, key_last + share(key_last, key_total), key_total)
 
-    within = first_row[0, :1] + jnp.arange(row_count, dtype=jnp.int32)
+    late_row, late_places = lax.optimization_barrier((first_row, positions, key_mid))[:2]
+    within = late_row[0, :1] + jnp.arange(row_count, dtype=jnp.int32)
     cosine, sine_part = tables(within.astype(jnp.float32), head_size)
-    new_cosine, new_sine = tables(positions.astype(jnp.float32), head_size)
+    new_cosine, new_sine = tables(late_places.astype(jnp.float32), head_size)
     masked, top, self_scores = call(
         functools.partial(score_kernel, team),
         "scores",

time: 63.4 us -> 67.5 us (1.065)
  waiting for transfers between devices: 17.6 us -> 22.9 us
  starting transfers between devices: 23.5 us -> 22.3 us
    ppermute x11, waiting for transfers between devices: 3.51 us -> 7.82 us  [by_core(): return lax.ppermute(value, 'ctx', pairs)]
    ppermute x19, starting transfers between devices: 9.62 us -> 8.54 us  [swap(): return lax.ppermute(value, axis, [(i, i ^ distance) for i in range(count)])]
    ppermute x19, waiting for transfers between devices: 14.1 us -> 15 us  [swap(): return lax.ppermute(value, axis, [(i, i ^ distance) for i in range(count)])]
  transfers between devices with their start and end apart: 30 -> 30, of which waited for: 14 -> 17; matrix products, arithmetic and copies ran while one was open for 1% -> 1% of each run, Pallas kernels for 26% -> 25%
where the time goes in v18:
time: 67.5 us; the launch traced here: 67.3 us
  waiting for transfers between devices  22.9 us (34%)
  starting transfers between devices  22.3 us (33%)
  Pallas kernels  18.5 us (27%)
  local copies, waits for them, and re-layouts  1.82 us (3%)
  other arithmetic  1.48 us (2%)
    ppermute x19, waiting for transfers between devices, swap(): return lax.ppermute(value, axis, [(i, i ^ distance) for i in range(count)])  15 us
    ppermute x11, starting transfers between devices, by_core(): return lax.ppermute(value, 'ctx', pairs)  13.8 us
    pallas_call x3, Pallas kernels, normalise(): call(functools.partial(norm_kernel, first), 'normalise', [IN_HBM, IN_VMEM...  8.58 us
    ppermute x19, starting transfers between devices, swap(): return lax.ppermute(value, axis, [(i, i ^ distance) for i in range(count)])  8.54 us
    ppermute x11, waiting for transfers between devices, by_core(): return lax.ppermute(value, 'ctx', pairs)  7.82 us
    pallas_call x6, Pallas kernels, project(): call(functools.partial(project_kernel, [d for d, _ in blocks], len(rows),...  6.18 us
    unnamed x18, local copies, waits for them, and re-layouts  1.82 us
  transfers between devices with their start and end apart: 30, of which 17 were waited for; matrix products, arithmetic and copies ran while one was open for 1% of the time, Pallas kernels for 25%

profile of v18, /device:TPU:0, one launch (start us, length us, event | category | flops | bytes accessed | tf_op | source)
XLA Modules:
  0.0 67.3 jit_solution(9345949694380683603)
XLA Ops:
  0.0 0.5 collective-permute-start.1
  0.5 0.1 collective-permute-start.2
  0.5 2.9 %collective-permute-start.12 = (bf16[2048,128]{1,0:T(8,128)(2,1)}, bf16[2048,128]{1,0:T(8,128)(2,1)S(1)}, u32[]{:S(2)}, u32[]{:S(2)}) collective-permute-start(bf16[2048,128]{1,0:T(8,128)(2,1)} %bitcast.24), channel_id=1, source_target_pairs={{0,8},{4,20},{8,0},{12,28},{16,24},{20,4},{24,16},{28,12},{1,9},{5... | collective-permute-start | bytes 1572872 | tf_op jit(solution)/shard_map/ppermute | solution.py:64
  3.5 1.6 %collective-permute-start.6 = (bf16[2048,128]{1,0:T(8,128)(2,1)S(1)}, bf16[2048,128]{1,0:T(8,128)(2,1)S(1)}, u32[]{:S(2)}, u32[]{:S(2)}) collective-permute-start(bf16[2048,128]{1,0:T(8,128)(2,1)S(1)} %collective-permute-done.1.refs_6_), channel_id=1, source_target_pairs={{0,8},{4,20},{8,0},{12,28},{16,24},{20,4},{24,16},{28,12},{1,9},{5... | collective-permute-start | bytes 1572872 | tf_op jit(solution)/shard_map/ppermute | solution.py:64
  5.1 0.7 %copy-done.5 = f32[2,2048]{1,0:T(2,128)S(1)} copy-done((f32[2,2048]{1,0:T(2,128)S(1)}, f32[2,2048]{1,0:T(2,128)}, u32[]{:S(2)}) %copy-start.5) | copy-done | bytes 16408
  5.8 0.1 squares.1
  5.9 1.1 %collective-permute-done = f32[2,128]{1,0:T(2,128)S(1)} collective-permute-done((f32[2,128]{1,0:T(2,128)S(1)}, f32[2,128]{1,0:T(2,128)S(1)}, u32[]{:S(2)}, u32[]{:S(2)}) %collective-permute-start) | collective-permute-done | bytes 1056 | tf_op jit(solution)/shard_map/ppermute | solution.py:43
  7.0 1.5 %collective-permute-start.3 = (f32[2,128]{1,0:T(2,128)S(1)}, f32[2,128]{1,0:T(2,128)S(1)}, u32[]{:S(2)}, u32[]{:S(2)}) collective-permute-start(f32[2,128]{1,0:T(2,128)S(1)} %add.53), channel_id=1, source_target_pairs={{0,16},{4,12},{8,24},{12,4},{16,0},{20,28},{24,8},{28,20},{1,17},{... | collective-permute-start | bytes 3080 | tf_op jit(solution)/shard_map/ppermute | solution.py:64
  8.5 0.8 %copy-done.4 = f32[1,16384]{1,0:T(1,128)S(1)} copy-done((f32[1,16384]{1,0:T(1,128)S(1)}, f32[1,16384]{1,0:T(1,128)}, u32[]{:S(2)}) %copy-start.4) | copy-done | bytes 65560
  9.4 3.2 %normalise.3 = (bf16[8,64,2048]{2,1,0:T(8,128)(2,1)S(1)}, bf16[8,64,2048]{2,1,0:T(8,128)(2,1)S(1)}) custom-call(bf16[320,16384]{1,0:T(8,128)(2,1)} %bitcast.36, f32[8,1,2048]{2,1,0:T(1,128)S(1)} %bitcast.31), custom_call_target="tpu_custom_call" | custom-call | flops 1000 | bytes 1000 | tf_op jit(solution)/shard_map/normalise/pallas_call | solution.py:173
  12.6 0.1 collective-permute-start.4
  12.7 0.6 collective-permute-start.8
  13.3 0.5 collective-permute-done.4
  13.8 0.2 collective-permute-start.13
  14.0 0.9 %collective-permute-start.5 = (f32[2,128]{1,0:T(2,128)S(1)}, f32[2,128]{1,0:T(2,128)S(1)}, u32[]{:S(2)}, u32[]{:S(2)}) collective-permute-start(f32[2,128]{1,0:T(2,128)S(1)} %collective-permute-done.4), channel_id=1, source_target_pairs={{0,16},{4,12},{8,24},{12,4},{16,0},{20,28},{24,8},{28,20},{1,17},{... | collective-permute-start | bytes 3080 | tf_op jit(solution)/shard_map/ppermute | solution.py:64
  14.9 3.3 %normalise.4 = (bf16[8,64,2048]{2,1,0:T(8,128)(2,1)S(1)}, bf16[8,64,2048]{2,1,0:T(8,128)(2,1)S(1)}) custom-call(bf16[320,16384]{1,0:T(8,128)(2,1)} %bitcast.37, f32[8,1,2048]{2,1,0:T(1,128)S(1)} %bitcast.32), custom_call_target="tpu_custom_call" | custom-call | flops 1000 | bytes 1000 | tf_op jit(solution)/shard_map/normalise/pallas_call | solution.py:173
  18.3 0.1 copy-done
  18.4 0.1 copy-done.2
  18.5 0.8 %query_products.1 = f32[2,10,128]{2,1,0:T(8,128)S(1)} custom-call(s32[1]{0:T(128)} %bitcast.place_ref, f32[2,128]{1,0:T(2,128)S(1)} %add_add_fusion.2.squares_ref, f32[2,2048]{1,0:T(2,128)S(1)} %copy-done.5, f32[8,1,2048]{2,1,0:T(1,128)S(1)} %bitcast.33, bf16[2048,1024]{1,0:T(8,128)(2,1)S(1)} %bitcast.21, bf16[2048,128]{1,0:T(8,128)(2,1)S(1)} %bitcast.25, ...), custom_call_target="tpu_custom_call" | custom-call | flops 1000 | bytes 1000 | tf_op jit(solution)/shard_map/query_products/pallas_call | solution.py:371
  19.3 0.1 collective-permute-start.7
  19.5 1.1 %collective-permute-done.7 = f32[2,10,128]{2,1,0:T(8,128)S(1)} collective-permute-done((f32[2,10,128]{2,1,0:T(8,128)S(1)}, f32[2,10,128]{2,1,0:T(8,128)S(1)}, u32[]{:S(2)}, u32[]{:S(2)}) %collective-permute-start.7) | collective-permute-done | bytes 10272 | tf_op jit(solution)/shard_map/ppermute | solution.py:43
  20.6 1.1 %collective-permute-start.9 = (f32[2,10,128]{2,1,0:T(8,128)S(1)}, f32[2,10,128]{2,1,0:T(8,128)S(1)}, u32[]{:S(2)}, u32[]{:S(2)}) collective-permute-start(f32[2,10,128]{2,1,0:T(8,128)S(1)} %add.57), channel_id=1, source_target_pairs={{0,16},{4,12},{8,24},{12,4},{16,0},{20,28},{24,8},{28,20},{1,17},{... | collective-permute-start | bytes 30728 | tf_op jit(solution)/shard_map/ppermute | solution.py:64
  21.7 2.1 %normalise.5.refs_4_ = bf16[8,64,2048]{2,1,0:T(8,128)(2,1)S(1)} custom-call(bf16[320,16384]{1,0:T(8,128)(2,1)} %bitcast.38, f32[8,1,2048]{2,1,0:T(1,128)S(1)} %bitcast.34), custom_call_target="tpu_custom_call" | custom-call | flops 1000 | bytes 1000 | tf_op jit(solution)/shard_map/normalise/pallas_call | solution.py:173
  23.8 0.5 collective-permute-done.9
  24.3 0.5 collective-permute-start.15
  24.8 0.8 %collective-permute-start.14 = (bf16[2048,128]{1,0:T(8,128)(2,1)S(1)}, bf16[2048,128]{1,0:T(8,128)(2,1)S(1)}, u32[]{:S(2)}, u32[]{:S(2)}) collective-permute-start(bf16[2048,128]{1,0:T(8,128)(2,1)S(1)} %collective-permute-done.13.refs_7_), channel_id=1, source_target_pairs={{0,8},{4,20},{8,0},{12,28},{16,24},{20,4},{24,16},{28,12},{1,9},{5... | collective-permute-start | bytes 1572872 | tf_op jit(solution)/shard_map/ppermute | solution.py:64
  25.6 1.1 %collective-permute-start.18 = (f32[2,10,128]{2,1,0:T(8,128)S(1)}, f32[2,10,128]{2,1,0:T(8,128)S(1)}, u32[]{:S(2)}, u32[]{:S(2)}) collective-permute-start(f32[2,10,128]{2,1,0:T(8,128)S(1)} %collective-permute-done.17), channel_id=1, source_target_pairs={{0,16},{4,12},{8,24},{12,4},{16,0},{20,28},{24,8},{28,20},{1,17},{... | collective-permute-start | bytes 30728 | tf_op jit(solution)/shard_map/ppermute | solution.py:64
  26.8 1.2 %collective-permute-start.20 = (bf16[2048,128]{1,0:T(8,128)(2,1)S(1)}, bf16[2048,128]{1,0:T(8,128)(2,1)S(1)}, u32[]{:S(2)}, u32[]{:S(2)}) collective-permute-start(bf16[2048,128]{1,0:T(8,128)(2,1)S(1)} %collective-permute-done.2.refs_6_), channel_id=1, source_target_pairs={{0,8},{4,20},{8,0},{12,28},{16,24},{20,4},{24,16},{28,12},{1,9},{5... | collective-permute-start | bytes 1572872 | tf_op jit(solution)/shard_map/ppermute | solution.py:64
  28.0 0.9 %project.6.refs_9_ = f32[320,128]{1,0:T(8,128)S(1)} custom-call(s32[1]{0:T(128)} %bitcast.place_ref, bf16[8,64,2048]{2,1,0:T(8,128)(2,1)S(1)} %get-tuple-element.38.refs_0_, bf16[8,64,2048]{2,1,0:T(8,128)(2,1)S(1)} %get-tuple-element.39.refs_1_, bf16[8,64,2048]{2,1,0:T(8,128)(2,1)S(1)} %get-tuple-element.42.refs_2_, ...), custom_call_target="tpu_custom_call" | custom-call | flops 1000 | bytes 1000 | tf_op jit(solution)/shard_map/project/pallas_call | solution.py:218
  28.8 0.1 collective-permute-start.10
  28.9 0.7 %collective-permute-done.18 = f32[2,10,128]{2,1,0:T(8,128)S(1)} collective-permute-done((f32[2,10,128]{2,1,0:T(8,128)S(1)}, f32[2,10,128]{2,1,0:T(8,128)S(1)}, u32[]{:S(2)}, u32[]{:S(2)}) %collective-permute-start.18) | collective-permute-done | bytes 10272 | tf_op jit(solution)/shard_map/ppermute | solution.py:64
  29.6 0.0 copy-start.8
  29.7 1.6 %project.7.refs_7_ = f32[320,128]{1,0:T(8,128)S(1)} custom-call(s32[1]{0:T(128)} %bitcast.place_ref, bf16[8,64,2048]{2,1,0:T(8,128)(2,1)S(1)} %get-tuple-element.38.refs_0_, bf16[8,64,2048]{2,1,0:T(8,128)(2,1)S(1)} %get-tuple-element.39.refs_1_, bf16[8,64,2048]{2,1,0:T(8,128)(2,1)S(1)} %get-tuple-element.42.refs_2_, ...), custom_call_target="tpu_custom_call" | custom-call | flops 1000 | bytes 1000 | tf_op jit(solution)/shard_map/project/pallas_call | solution.py:218
  31.2 2.8 %collective-permute-done.14.refs_5_ = bf16[2048,128]{1,0:T(8,128)(2,1)S(1)} collective-permute-done((bf16[2048,128]{1,0:T(8,128)(2,1)S(1)}, bf16[2048,128]{1,0:T(8,128)(2,1)S(1)}, u32[]{:S(2)}, u32[]{:S(2)}) %collective-permute-start.14) | collective-permute-done | bytes 524320 | tf_op jit(solution)/shard_map/ppermute | solution.py:64
  34.1 0.1 multiply_sine_fusion.1
  34.2 0.9 %collective-permute-start.11 = (bf16[2048,128]{1,0:T(8,128)(2,1)S(1)}, bf16[2048,128]{1,0:T(8,128)(2,1)S(1)}, u32[]{:S(2)}, u32[]{:S(2)}) collective-permute-start(bf16[2048,128]{1,0:T(8,128)(2,1)S(1)} %collective-permute-done.10.refs_7_), channel_id=1, source_target_pairs={{0,8},{4,20},{8,0},{12,28},{16,24},{20,4},{24,16},{28,12},{1,9},{5... | collective-permute-start | bytes 1572872 | tf_op jit(solution)/shard_map/ppermute | solution.py:64
  35.2 0.6 multiply_sine_fusion
  35.8 0.2 collective-permute-done.16.refs_6_
  36.0 0.9 %project.8.refs_0_ = f32[320,128]{1,0:T(8,128)S(1)} custom-call(s32[1]{0:T(128)} %bitcast.place_ref, bf16[8,64,2048]{2,1,0:T(8,128)(2,1)S(1)} %get-tuple-element.38.refs_0_, bf16[8,64,2048]{2,1,0:T(8,128)(2,1)S(1)} %get-tuple-element.39.refs_1_, bf16[8,64,2048]{2,1,0:T(8,128)(2,1)S(1)} %get-tuple-element.42.refs_2_, ...), custom_call_target="tpu_custom_call" | custom-call | flops 1000 | bytes 1000 | tf_op jit(solution)/shard_map/project/pallas_call | solution.py:218
  36.9 1.0 %scores.1 = (f32[8,320]{1,0:T(8,128)S(1)}, f32[8,128]{1,0:T(8,128)S(1)}, f32[8,128]{1,0:T(8,128)S(1)}) custom-call(s32[1]{0:T(128)} %bitcast.place_ref, s32[2]{0:T(128)S(1)} %copy-done.7, f32[320,128]{1,0:T(8,128)S(1)} %project.8.refs_0_, f32[320,64]{1,0:T(8,128)S(1)} %get-tuple-element.66.refs_1_, f32[320,64]{1,0:T(8,128)S(1)} %get-tuple-element.65.refs_2_, ...), custom_call_target="tpu_custom_call" | custom-call | flops 1000 | bytes 1000 | tf_op jit(solution)/shard_map/scores/pallas_call | solution.py:398
  37.9 0.3 collective-permute-start.19
  38.1 0.9 %collective-permute-done.19 = f32[8,128]{1,0:T(8,128)S(1)} collective-permute-done((f32[8,128]{1,0:T(8,128)S(1)}, f32[8,128]{1,0:T(8,128)S(1)}, u32[]{:S(2)}, u32[]{:S(2)}) %collective-permute-start.19) | collective-permute-done | bytes 4128 | tf_op jit(solution)/shard_map/ppermute | solution.py:43
  39.0 0.7 collective-permute-done.20.refs_5_
  39.7 1.0 %collective-permute-start.21 = (f32[8,128]{1,0:T(8,128)S(1)}, f32[8,128]{1,0:T(8,128)S(1)}, u32[]{:S(2)}, u32[]{:S(2)}) collective-permute-start(f32[8,128]{1,0:T(8,128)S(1)} %max.6), channel_id=1, source_target_pairs={{0,16},{4,12},{8,24},{12,4},{16,0},{20,28},{24,8},{28,20},{1,17},{... | collective-permute-start | bytes 12296 | tf_op jit(solution)/shard_map/ppermute | solution.py:64
  40.7 1.6 %project.9.refs_7_ = f32[320,128]{1,0:T(8,128)S(1)} custom-call(s32[1]{0:T(128)} %bitcast.place_ref, bf16[8,64,2048]{2,1,0:T(8,128)(2,1)S(1)} %get-tuple-element.38.refs_0_, bf16[8,64,2048]{2,1,0:T(8,128)(2,1)S(1)} %get-tuple-element.39.refs_1_, bf16[8,64,2048]{2,1,0:T(8,128)(2,1)S(1)} %get-tuple-element.42.refs_2_, ...), custom_call_target="tpu_custom_call" | custom-call | flops 1000 | bytes 1000 | tf_op jit(solution)/shard_map/project/pallas_call | solution.py:218
  42.3 1.1 %collective-permute-done.21 = f32[8,128]{1,0:T(8,128)S(1)} collective-permute-done((f32[8,128]{1,0:T(8,128)S(1)}, f32[8,128]{1,0:T(8,128)S(1)}, u32[]{:S(2)}, u32[]{:S(2)}) %collective-permute-start.21) | collective-permute-done | bytes 4128 | tf_op jit(solution)/shard_map/ppermute | solution.py:64
  43.4 1.9 %collective-permute-done.11.refs_5_ = bf16[2048,128]{1,0:T(8,128)(2,1)S(1)} collective-permute-done((bf16[2048,128]{1,0:T(8,128)(2,1)S(1)}, bf16[2048,128]{1,0:T(8,128)(2,1)S(1)}, u32[]{:S(2)}, u32[]{:S(2)}) %collective-permute-start.11) | collective-permute-done | bytes 524320 | tf_op jit(solution)/shard_map/ppermute | solution.py:64
  45.4 0.5 collective-permute-start.24
  45.9 0.9 %project.10.refs_6_ = f32[320,128]{1,0:T(8,128)S(1)} custom-call(s32[1]{0:T(128)} %bitcast.place_ref, bf16[8,64,2048]{2,1,0:T(8,128)(2,1)S(1)} %get-tuple-element.38.refs_0_, bf16[8,64,2048]{2,1,0:T(8,128)(2,1)S(1)} %get-tuple-element.39.refs_1_, bf16[8,64,2048]{2,1,0:T(8,128)(2,1)S(1)} %get-tuple-element.42.refs_2_, ...), custom_call_target="tpu_custom_call" | custom-call | flops 1000 | bytes 1000 | tf_op jit(solution)/shard_map/project/pallas_call | solution.py:218
  46.8 0.5 collective-permute-done.24
  47.3 0.5 project.11.refs_6_
  47.8 1.2 %weighted_values.1 = f32[8,256]{1,0:T(8,128)S(1)} custom-call(s32[1]{0:T(128)} %bitcast.place_ref, s32[2]{0:T(128)S(1)} %copy-done.7, bf16[8,64,2048]{2,1,0:T(8,128)(2,1)S(1)} %get-tuple-element.38.refs_0_, bf16[8,64,2048]{2,1,0:T(8,128)(2,1)S(1)} %get-tuple-element.39.refs_1_, bf16[8,64,2048]{2,1,0:T(8,128)(2,1)S(1)} %get-tuple-element.42.refs_2_, ...), custom_call_target="tpu_custom_call" | custom-call | flops 1000 | bytes 1000 | tf_op jit(solution)/shard_map/weighted_values/pallas_call | solution.py:423
  49.0 0.1 collective-permute-start.25
  49.2 1.0 %collective-permute-done.25 = f32[8,256]{1,0:T(8,128)S(1)} collective-permute-done((f32[8,256]{1,0:T(8,128)S(1)}, f32[8,256]{1,0:T(8,128)S(1)}, u32[]{:S(2)}, u32[]{:S(2)}) %collective-permute-start.25) | collective-permute-done | bytes 8224 | tf_op jit(solution)/shard_map/ppermute | solution.py:43
  50.2 0.9 %collective-permute-start.26 = (f32[8,256]{1,0:T(8,128)S(1)}, f32[8,256]{1,0:T(8,128)S(1)}, u32[]{:S(2)}, u32[]{:S(2)}) collective-permute-start(f32[8,256]{1,0:T(8,128)S(1)} %add.64), channel_id=1, source_target_pairs={{0,8},{4,12},{8,0},{12,4},{16,24},{20,28},{24,16},{28,20},{1,9},{5... | collective-permute-start | bytes 24584 | tf_op jit(solution)/shard_map/ppermute | solution.py:43
  51.1 2.8 %collective-permute-done.26 = f32[8,256]{1,0:T(8,128)S(1)} collective-permute-done((f32[8,256]{1,0:T(8,128)S(1)}, f32[8,256]{1,0:T(8,128)S(1)}, u32[]{:S(2)}, u32[]{:S(2)}) %collective-permute-start.26) | collective-permute-done | bytes 8224 | tf_op jit(solution)/shard_map/ppermute | solution.py:43
  53.9 1.0 %collective-permute-start.27 = (f32[8,256]{1,0:T(8,128)S(1)}, f32[8,256]{1,0:T(8,128)S(1)}, u32[]{:S(2)}, u32[]{:S(2)}) collective-permute-start(f32[8,256]{1,0:T(8,128)S(1)} %add.65.mine_ref), channel_id=1, source_target_pairs={{0,16},{4,20},{8,24},{12,28},{16,0},{20,4},{24,8},{28,12},{1,17},{... | collective-permute-start | bytes 24584 | tf_op jit(solution)/shard_map/ppermute | solution.py:43
  54.9 2.6 %collective-permute-done.27.other_ref = f32[8,256]{1,0:T(8,128)S(1)} collective-permute-done((f32[8,256]{1,0:T(8,128)S(1)}, f32[8,256]{1,0:T(8,128)S(1)}, u32[]{:S(2)}, u32[]{:S(2)}) %collective-permute-start.27) | collective-permute-done | bytes 8224 | tf_op jit(solution)/shard_map/ppermute | solution.py:43
  57.5 0.6 output_products.1
  58.2 1.6 %collective-permute-start.28 = (f32[2,2048]{1,0:T(2,128)S(1)}, f32[2,2048]{1,0:T(2,128)S(1)}, u32[]{:S(2)}, u32[]{:S(2)}) collective-permute-start(f32[2,2048]{1,0:T(2,128)S(1)} %output_products.1), channel_id=1, source_target_pairs={{0,1},{1,0},{2,3},{3,2},{4,5},{5,4},{6,7},{7,6},{8,9},{9,8},{10,11... | collective-permute-start | bytes 49160 | tf_op jit(solution)/shard_map/ppermute | solution.py:43
  59.7 2.2 %collective-permute-done.28 = f32[2,2048]{1,0:T(2,128)S(1)} collective-permute-done((f32[2,2048]{1,0:T(2,128)S(1)}, f32[2,2048]{1,0:T(2,128)S(1)}, u32[]{:S(2)}, u32[]{:S(2)}) %collective-permute-start.28) | collective-permute-done | bytes 16416 | tf_op jit(solution)/shard_map/ppermute | solution.py:43
  61.9 2.6 %collective-permute-start.29 = (f32[2,2048]{1,0:T(2,128)S(1)}, f32[2,2048]{1,0:T(2,128)S(1)}, u32[]{:S(2)}, u32[]{:S(2)}) collective-permute-start(f32[2,2048]{1,0:T(2,128)S(1)} %add.66), channel_id=1, source_target_pairs={{0,2},{1,3},{2,0},{3,1},{4,6},{5,7},{6,4},{7,5},{8,10},{9,11},{10,... | collective-permute-start | bytes 49160 | tf_op jit(solution)/shard_map/ppermute | solution.py:43
  64.6 2.1 %collective-permute-done.29 = f32[2,2048]{1,0:T(2,128)S(1)} collective-permute-done((f32[2,2048]{1,0:T(2,128)S(1)}, f32[2,2048]{1,0:T(2,128)S(1)}, u32[]{:S(2)}, u32[]{:S(2)}) %collective-permute-start.29) | collective-permute-done | bytes 16416 | tf_op jit(solution)/shard_map/ppermute | solution.py:43
  66.6 0.6 add_add_fusion
  (47 shorter events, 0.2 us)
Async XLA Ops:
  0.0 3.5 %collective-permute-start.1 = (bf16[2048,128]{1,0:T(8,128)(2,1)}, bf16[2048,128]{1,0:T(8,128)(2,1)S(1)}, u32[]{:S(2)}, u32[]{:S(2)}) collective-permute-start(bf16[2048,128]{1,0:T(8,128)(2,1)} %bitcast.23), channel_id=1, source_target_pairs={{0,4},{4,0},{8,12},{12,8},{16,20},{20,16},{24,28},{28,24},{1,5},{5... | collective-permute-start | bytes 1572872 | tf_op jit(solution)/shard_map/ppermute | solution.py:43
  0.5 6.6 %collective-permute-start.2 = (bf16[2048,128]{1,0:T(8,128)(2,1)}, bf16[2048,128]{1,0:T(8,128)(2,1)S(1)}, u32[]{:S(2)}, u32[]{:S(2)}) collective-permute-start(bf16[2048,128]{1,0:T(8,128)(2,1)} %bitcast.27), channel_id=1, source_target_pairs={{0,4},{4,0},{8,12},{12,8},{16,20},{20,16},{24,28},{28,24},{1,5},{5... | collective-permute-start | bytes 1572872 | tf_op jit(solution)/shard_map/ppermute | solution.py:43
  0.5 12.8 %collective-permute-start.12 = (bf16[2048,128]{1,0:T(8,128)(2,1)}, bf16[2048,128]{1,0:T(8,128)(2,1)S(1)}, u32[]{:S(2)}, u32[]{:S(2)}) collective-permute-start(bf16[2048,128]{1,0:T(8,128)(2,1)} %bitcast.24), channel_id=1, source_target_pairs={{0,8},{4,20},{8,0},{12,28},{16,24},{20,4},{24,16},{28,12},{1,9},{5... | collective-permute-start | bytes 1572872 | tf_op jit(solution)/shard_map/ppermute | solution.py:64
  3.5 14.8 %collective-permute-start.6 = (bf16[2048,128]{1,0:T(8,128)(2,1)S(1)}, bf16[2048,128]{1,0:T(8,128)(2,1)S(1)}, u32[]{:S(2)}, u32[]{:S(2)}) collective-permute-start(bf16[2048,128]{1,0:T(8,128)(2,1)S(1)} %collective-permute-done.1.refs_6_), channel_id=1, source_target_pairs={{0,8},{4,20},{8,0},{12,28},{16,24},{20,4},{24,16},{28,12},{1,9},{5... | collective-permute-start | bytes 1572872 | tf_op jit(solution)/shard_map/ppermute | solution.py:64
  5.1 0.7 %copy-start.5 = (f32[2,2048]{1,0:T(2,128)S(1)}, f32[2,2048]{1,0:T(2,128)}, u32[]{:S(2)}) copy-start(f32[2,2048]{1,0:T(2,128)} %tokens_ref.3) | copy-start | bytes 49156
  5.9 1.1 %collective-permute-start = (f32[2,128]{1,0:T(2,128)S(1)}, f32[2,128]{1,0:T(2,128)S(1)}, u32[]{:S(2)}, u32[]{:S(2)}) collective-permute-start(f32[2,128]{1,0:T(2,128)S(1)} %get-tuple-element.35), channel_id=1, source_target_pairs={{0,4},{4,0},{8,12},{12,8},{16,20},{20,16},{24,28},{28,24},{1,5},{5... | collective-permute-start | bytes 3080 | tf_op jit(solution)/shard_map/ppermute | solution.py:43
  7.0 5.6 %collective-permute-start.3 = (f32[2,128]{1,0:T(2,128)S(1)}, f32[2,128]{1,0:T(2,128)S(1)}, u32[]{:S(2)}, u32[]{:S(2)}) collective-permute-start(f32[2,128]{1,0:T(2,128)S(1)} %add.53), channel_id=1, source_target_pairs={{0,16},{4,12},{8,24},{12,4},{16,0},{20,28},{24,8},{28,20},{1,17},{... | collective-permute-start | bytes 3080 | tf_op jit(solution)/shard_map/ppermute | solution.py:64
  8.5 0.8 %copy-start.4 = (f32[1,16384]{1,0:T(1,128)S(1)}, f32[1,16384]{1,0:T(1,128)}, u32[]{:S(2)}) copy-start(f32[1,16384]{1,0:T(1,128)} %param.11) | copy-start | bytes 196612
  9.4 3.3 %copy-start.3 = (bf16[1,2048,128]{2,1,0:T(8,128)(2,1)S(1)}, bf16[1,2048,128]{2,1,0:T(8,128)(2,1)}, u32[]{:S(2)}) copy-start(bf16[1,2048,128]{2,1,0:T(8,128)(2,1)} %param.14) | copy-start | bytes 1572868
  12.6 1.2 %collective-permute-start.4 = (f32[2,128]{1,0:T(2,128)S(1)}, f32[2,128]{1,0:T(2,128)S(1)}, u32[]{:S(2)}, u32[]{:S(2)}) collective-permute-start(f32[2,128]{1,0:T(2,128)S(1)} %collective-permute-done.3), channel_id=1, source_target_pairs={{0,4},{4,0},{8,12},{12,8},{16,20},{20,16},{24,28},{28,24},{1,5},{5... | collective-permute-start | bytes 3080 | tf_op jit(solution)/shard_map/ppermute | solution.py:43
  12.7 16.1 %collective-permute-start.8 = (bf16[2048,128]{1,0:T(8,128)(2,1)S(1)}, bf16[2048,128]{1,0:T(8,128)(2,1)S(1)}, u32[]{:S(2)}, u32[]{:S(2)}) collective-permute-start(bf16[2048,128]{1,0:T(8,128)(2,1)S(1)} %bitcast.28), channel_id=1, source_target_pairs={{0,8},{4,20},{8,0},{12,28},{16,24},{20,4},{24,16},{28,12},{1,9},{5... | collective-permute-start | bytes 1572872 | tf_op jit(solution)/shard_map/ppermute | solution.py:64
  13.8 11.0 %collective-permute-start.13 = (bf16[2048,128]{1,0:T(8,128)(2,1)S(1)}, bf16[2048,128]{1,0:T(8,128)(2,1)S(1)}, u32[]{:S(2)}, u32[]{:S(2)}) collective-permute-start(bf16[2048,128]{1,0:T(8,128)(2,1)S(1)} %collective-permute-done.12.refs_5_), channel_id=1, source_target_pairs={{0,4},{4,0},{8,12},{12,8},{16,20},{20,16},{24,28},{28,24},{1,5},{5... | collective-permute-start | bytes 1572872 | tf_op jit(solution)/shard_map/ppermute | solution.py:43
  14.0 4.2 %collective-permute-start.5 = (f32[2,128]{1,0:T(2,128)S(1)}, f32[2,128]{1,0:T(2,128)S(1)}, u32[]{:S(2)}, u32[]{:S(2)}) collective-permute-start(f32[2,128]{1,0:T(2,128)S(1)} %collective-permute-done.4), channel_id=1, source_target_pairs={{0,16},{4,12},{8,24},{12,4},{16,0},{20,28},{24,8},{28,20},{1,17},{... | collective-permute-start | bytes 3080 | tf_op jit(solution)/shard_map/ppermute | solution.py:64
  14.9 3.4 %copy-start = (bf16[1,2048,1024]{2,1,0:T(8,128)(2,1)S(1)}, bf16[1,2048,1024]{2,1,0:T(8,128)(2,1)}, u32[]{:S(2)}) copy-start(bf16[1,2048,1024]{2,1,0:T(8,128)(2,1)} %param.12) | copy-start | bytes 12582916
  14.9 3.6 %copy-start.2 = (bf16[1,2048,128]{2,1,0:T(8,128)(2,1)S(1)}, bf16[1,2048,128]{2,1,0:T(8,128)(2,1)}, u32[]{:S(2)}) copy-start(bf16[1,2048,128]{2,1,0:T(8,128)(2,1)} %param.13) | copy-start | bytes 1572868
  19.3 1.2 %collective-permute-start.7 = (f32[2,10,128]{2,1,0:T(8,128)S(1)}, f32[2,10,128]{2,1,0:T(8,128)S(1)}, u32[]{:S(2)}, u32[]{:S(2)}) collective-permute-start(f32[2,10,128]{2,1,0:T(8,128)S(1)} %query_products.1), channel_id=1, source_target_pairs={{0,4},{4,0},{8,12},{12,8},{16,20},{20,16},{24,28},{28,24},{1,5},{5... | collective-permute-start | bytes 30728 | tf_op jit(solution)/shard_map/ppermute | solution.py:43
  20.6 3.7 %collective-permute-start.9 = (f32[2,10,128]{2,1,0:T(8,128)S(1)}, f32[2,10,128]{2,1,0:T(8,128)S(1)}, u32[]{:S(2)}, u32[]{:S(2)}) collective-permute-start(f32[2,10,128]{2,1,0:T(8,128)S(1)} %add.57), channel_id=1, source_target_pairs={{0,16},{4,12},{8,24},{12,4},{16,0},{20,28},{24,8},{28,20},{1,17},{... | collective-permute-start | bytes 30728 | tf_op jit(solution)/shard_map/ppermute | solution.py:64
  24.3 1.3 %collective-permute-start.17 = (f32[2,10,128]{2,1,0:T(8,128)S(1)}, f32[2,10,128]{2,1,0:T(8,128)S(1)}, u32[]{:S(2)}, u32[]{:S(2)}) collective-permute-start(f32[2,10,128]{2,1,0:T(8,128)S(1)} %collective-permute-done.9), channel_id=1, source_target_pairs={{0,4},{4,0},{8,12},{12,8},{16,20},{20,16},{24,28},{28,24},{1,5},{5... | collective-permute-start | bytes 30728 | tf_op jit(solution)/shard_map/ppermute | solution.py:43
  24.3 5.3 %collective-permute-start.15 = (bf16[2048,128]{1,0:T(8,128)(2,1)S(1)}, bf16[2048,128]{1,0:T(8,128)(2,1)S(1)}, u32[]{:S(2)}, u32[]{:S(2)}) collective-permute-start(bf16[2048,128]{1,0:T(8,128)(2,1)S(1)} %collective-permute-done.6.refs_6_), channel_id=1, source_target_pairs={{0,4},{4,0},{8,12},{12,8},{16,20},{20,16},{24,28},{28,24},{1,5},{5... | collective-permute-start | bytes 1572872 | tf_op jit(solution)/shard_map/ppermute | solution.py:43
  24.8 9.3 %collective-permute-start.14 = (bf16[2048,128]{1,0:T(8,128)(2,1)S(1)}, bf16[2048,128]{1,0:T(8,128)(2,1)S(1)}, u32[]{:S(2)}, u32[]{:S(2)}) collective-permute-start(bf16[2048,128]{1,0:T(8,128)(2,1)S(1)} %collective-permute-done.13.refs_7_), channel_id=1, source_target_pairs={{0,8},{4,20},{8,0},{12,28},{16,24},{20,4},{24,16},{28,12},{1,9},{5... | collective-permute-start | bytes 1572872 | tf_op jit(solution)/shard_map/ppermute | solution.py:64
  25.6 4.0 %collective-permute-start.18 = (f32[2,10,128]{2,1,0:T(8,128)S(1)}, f32[2,10,128]{2,1,0:T(8,128)S(1)}, u32[]{:S(2)}, u32[]{:S(2)}) collective-permute-start(f32[2,10,128]{2,1,0:T(8,128)S(1)} %collective-permute-done.17), channel_id=1, source_target_pairs={{0,16},{4,12},{8,24},{12,4},{16,0},{20,28},{24,8},{28,20},{1,17},{... | collective-permute-start | bytes 30728 | tf_op jit(solution)/shard_map/ppermute | solution.py:64
  26.8 12.9 %collective-permute-start.20 = (bf16[2048,128]{1,0:T(8,128)(2,1)S(1)}, bf16[2048,128]{1,0:T(8,128)(2,1)S(1)}, u32[]{:S(2)}, u32[]{:S(2)}) collective-permute-start(bf16[2048,128]{1,0:T(8,128)(2,1)S(1)} %collective-permute-done.2.refs_6_), channel_id=1, source_target_pairs={{0,8},{4,20},{8,0},{12,28},{16,24},{20,4},{24,16},{28,12},{1,9},{5... | collective-permute-start | bytes 1572872 | tf_op jit(solution)/shard_map/ppermute | solution.py:64
  28.8 5.4 %collective-permute-start.10 = (bf16[2048,128]{1,0:T(8,128)(2,1)S(1)}, bf16[2048,128]{1,0:T(8,128)(2,1)S(1)}, u32[]{:S(2)}, u32[]{:S(2)}) collective-permute-start(bf16[2048,128]{1,0:T(8,128)(2,1)S(1)} %collective-permute-done.8.refs_8_), channel_id=1, source_target_pairs={{0,4},{4,0},{8,12},{12,8},{16,20},{20,16},{24,28},{28,24},{1,5},{5... | collective-permute-start | bytes 1572872 | tf_op jit(solution)/shard_map/ppermute | solution.py:43
  29.6 1.6 %copy-start.8 = (s32[2]{0:T(128)S(1)}, s32[2]{0:T(128)}, u32[]{:S(2)}) copy-start(s32[2]{0:T(128)} %param.17) | copy-start | bytes 28
  34.1 1.9 %collective-permute-start.16 = (bf16[2048,128]{1,0:T(8,128)(2,1)S(1)}, bf16[2048,128]{1,0:T(8,128)(2,1)S(1)}, u32[]{:S(2)}, u32[]{:S(2)}) collective-permute-start(bf16[2048,128]{1,0:T(8,128)(2,1)S(1)} %collective-permute-done.14.refs_5_), channel_id=1, source_target_pairs={{0,4},{4,0},{8,12},{12,8},{16,20},{20,16},{24,28},{28,24},{1,5},{5... | collective-permute-start | bytes 1572872 | tf_op jit(solution)/shard_map/ppermute | solution.py:43
  34.2 11.2 %collective-permute-start.11 = (bf16[2048,128]{1,0:T(8,128)(2,1)S(1)}, bf16[2048,128]{1,0:T(8,128)(2,1)S(1)}, u32[]{:S(2)}, u32[]{:S(2)}) collective-permute-start(bf16[2048,128]{1,0:T(8,128)(2,1)S(1)} %collective-permute-done.10.refs_7_), channel_id=1, source_target_pairs={{0,8},{4,20},{8,0},{12,28},{16,24},{20,4},{24,16},{28,12},{1,9},{5... | collective-permute-start | bytes 1572872 | tf_op jit(solution)/shard_map/ppermute | solution.py:64
  35.8 1.0 %copy-start.7 = (s32[2]{0:T(128)S(1)}, s32[2]{0:T(128)}, u32[]{:S(2)}) copy-start(s32[2]{0:T(128)} %lengths_ref.3) | copy-start | bytes 28
  37.9 1.2 %collective-permute-start.19 = (f32[8,128]{1,0:T(8,128)S(1)}, f32[8,128]{1,0:T(8,128)S(1)}, u32[]{:S(2)}, u32[]{:S(2)}) collective-permute-start(f32[8,128]{1,0:T(8,128)S(1)} %get-tuple-element.57), channel_id=1, source_target_pairs={{0,4},{4,0},{8,12},{12,8},{16,20},{20,16},{24,28},{28,24},{1,5},{5... | collective-permute-start | bytes 12296 | tf_op jit(solution)/shard_map/ppermute | solution.py:43
  39.7 6.2 %collective-permute-start.23 = (bf16[2048,128]{1,0:T(8,128)(2,1)S(1)}, bf16[2048,128]{1,0:T(8,128)(2,1)S(1)}, u32[]{:S(2)}, u32[]{:S(2)}) collective-permute-start(bf16[2048,128]{1,0:T(8,128)(2,1)S(1)} %collective-permute-done.20.refs_5_), channel_id=1, source_target_pairs={{0,4},{4,0},{8,12},{12,8},{16,20},{20,16},{24,28},{28,24},{1,5},{5... | collective-permute-start | bytes 1572872 | tf_op jit(solution)/shard_map/ppermute | solution.py:43
  39.7 3.7 %collective-permute-start.21 = (f32[8,128]{1,0:T(8,128)S(1)}, f32[8,128]{1,0:T(8,128)S(1)}, u32[]{:S(2)}, u32[]{:S(2)}) collective-permute-start(f32[8,128]{1,0:T(8,128)S(1)} %max.6), channel_id=1, source_target_pairs={{0,16},{4,12},{8,24},{12,4},{16,0},{20,28},{24,8},{28,20},{1,17},{... | collective-permute-start | bytes 12296 | tf_op jit(solution)/shard_map/ppermute | solution.py:64
  45.4 2.4 %collective-permute-start.22 = (bf16[2048,128]{1,0:T(8,128)(2,1)S(1)}, bf16[2048,128]{1,0:T(8,128)(2,1)S(1)}, u32[]{:S(2)}, u32[]{:S(2)}) collective-permute-start(bf16[2048,128]{1,0:T(8,128)(2,1)S(1)} %collective-permute-done.11.refs_5_), channel_id=1, source_target_pairs={{0,4},{4,0},{8,12},{12,8},{16,20},{20,16},{24,28},{28,24},{1,5},{5... | collective-permute-start | bytes 1572872 | tf_op jit(solution)/shard_map/ppermute | solution.py:43
  45.4 1.9 %collective-permute-start.24 = (f32[8,128]{1,0:T(8,128)S(1)}, f32[8,128]{1,0:T(8,128)S(1)}, u32[]{:S(2)}, u32[]{:S(2)}) collective-permute-start(f32[8,128]{1,0:T(8,128)S(1)} %max.7), channel_id=1, source_target_pairs={{0,4},{4,0},{8,12},{12,8},{16,20},{20,16},{24,28},{28,24},{1,5},{5... | collective-permute-start | bytes 12296 | tf_op jit(solution)/shard_map/ppermute | solution.py:43
  47.8 9.7 %copy-start.1 = (bf16[1,1024,2048]{2,1,0:T(8,128)(2,1)S(1)}, bf16[1,1024,2048]{2,1,0:T(8,128)(2,1)}, u32[]{:S(2)}) copy-start(bf16[1,1024,2048]{2,1,0:T(8,128)(2,1)} %param.15) | copy-start | bytes 12582916
  49.0 1.2 %collective-permute-start.25 = (f32[8,256]{1,0:T(8,128)S(1)}, f32[8,256]{1,0:T(8,128)S(1)}, u32[]{:S(2)}, u32[]{:S(2)}) collective-permute-start(f32[8,256]{1,0:T(8,128)S(1)} %weighted_values.1), channel_id=1, source_target_pairs={{0,4},{4,0},{8,12},{12,8},{16,20},{20,16},{24,28},{28,24},{1,5},{5... | collective-permute-start | bytes 24584 | tf_op jit(solution)/shard_map/ppermute | solution.py:43
  50.2 3.7 %collective-permute-start.26 = (f32[8,256]{1,0:T(8,128)S(1)}, f32[8,256]{1,0:T(8,128)S(1)}, u32[]{:S(2)}, u32[]{:S(2)}) collective-permute-start(f32[8,256]{1,0:T(8,128)S(1)} %add.64), channel_id=1, source_target_pairs={{0,8},{4,12},{8,0},{12,4},{16,24},{20,28},{24,16},{28,20},{1,9},{5... | collective-permute-start | bytes 24584 | tf_op jit(solution)/shard_map/ppermute | solution.py:43
  53.9 3.7 %collective-permute-start.27 = (f32[8,256]{1,0:T(8,128)S(1)}, f32[8,256]{1,0:T(8,128)S(1)}, u32[]{:S(2)}, u32[]{:S(2)}) collective-permute-start(f32[8,256]{1,0:T(8,128)S(1)} %add.65.mine_ref), channel_id=1, source_target_pairs={{0,16},{4,20},{8,24},{12,28},{16,0},{20,4},{24,8},{28,12},{1,17},{... | collective-permute-start | bytes 24584 | tf_op jit(solution)/shard_map/ppermute | solution.py:43
  57.5 9.1 %copy-start.6 = (f32[2,2048]{1,0:T(2,128)S(1)}, f32[2,2048]{1,0:T(2,128)}, u32[]{:S(2)}) copy-start(f32[2,2048]{1,0:T(2,128)} %tokens_ref.3) | copy-start | bytes 49156
  58.2 3.8 %collective-permute-start.28 = (f32[2,2048]{1,0:T(2,128)S(1)}, f32[2,2048]{1,0:T(2,128)S(1)}, u32[]{:S(2)}, u32[]{:S(2)}) collective-permute-start(f32[2,2048]{1,0:T(2,128)S(1)} %output_products.1), channel_id=1, source_target_pairs={{0,1},{1,0},{2,3},{3,2},{4,5},{5,4},{6,7},{7,6},{8,9},{9,8},{10,11... | collective-permute-start | bytes 49160 | tf_op jit(solution)/shard_map/ppermute | solution.py:43
  61.9 4.7 %collective-permute-start.29 = (f32[2,2048]{1,0:T(2,128)S(1)}, f32[2,2048]{1,0:T(2,128)S(1)}, u32[]{:S(2)}, u32[]{:S(2)}) collective-permute-start(f32[2,2048]{1,0:T(2,128)S(1)} %add.66), channel_id=1, source_target_pairs={{0,2},{1,3},{2,0},{3,1},{4,6},{5,7},{6,4},{7,5},{8,10},{9,11},{10,... | collective-permute-start | bytes 49160 | tf_op jit(solution)/shard_map/ppermute | solution.py:43

commit v19 on v18

--- a/solution.py
+++ b/solution.py
@@ -387,14 +387,14 @@
         summed = butterfly(summed, "ctx", chip_bits[:-1], jnp.add)
 
     key_total = project(places, rows, key_near)
+    key_mid = key_total
     key_total = project(places, rows, key_far + key_shared, key_total)
-    key_mid = key_total
     key_total = project(places, rows, key_last + share(key_last, key_total), key_total)
 
     late_row, late_places = lax.optimization_barrier((first_row, positions, key_mid))[:2]
     within = late_row[0, :1] + jnp.arange(row_count, dtype=jnp.int32)
     cosine, sine_part = tables(within.astype(jnp.float32), head_size)
-    new_cosine, new_sine = tables(late_places.astype(jnp.float32), head_size)
+    new_cosine, new_sine = tables(positions.astype(jnp.float32), head_size)
     masked, top, self_scores = call(
         functools.partial(score_kernel, team),
         "scores",

time: 67.5 us -> 63 us (0.933)
  waiting for transfers between devices: 22.9 us -> 18.2 us
    ppermute x11, waiting for transfers between devices: 7.82 us -> 2.94 us  [by_core(): return lax.ppermute(value, 'ctx', pairs)]
  transfers between devices with their start and end apart: 30 -> 30, of which waited for: 17 -> 14; matrix products, arithmetic and copies ran while one was open for 1% -> 1% of each run, Pallas kernels for 25% -> 27%
where the time goes in v19:
time: 63 us; the launch traced here: 62.8 us
  starting transfers between devices  22.5 us (36%)
  Pallas kernels  18.5 us (29%)
  waiting for transfers between devices  18.2 us (29%)
  local copies, waits for them, and re-layouts  1.81 us (3%)
  other arithmetic  1.49 us (2%)
    ppermute x19, waiting for transfers between devices, swap(): return lax.ppermute(value, axis, [(i, i ^ distance) for i in range(count)])  15.3 us
    ppermute x11, starting transfers between devices, by_core(): return lax.ppermute(value, 'ctx', pairs)  13.9 us
    ppermute x19, starting transfers between devices, swap(): return lax.ppermute(value, axis, [(i, i ^ distance) for i in range(count)])  8.65 us
    pallas_call x3, Pallas kernels, normalise(): call(functools.partial(norm_kernel, first), 'normalise', [IN_HBM, IN_VMEM...  8.59 us
    pallas_call x6, Pallas kernels, project(): call(functools.partial(project_kernel, [d for d, _ in blocks], len(rows),...  6.17 us
    ppermute x11, waiting for transfers between devices, by_core(): return lax.ppermute(value, 'ctx', pairs)  2.94 us
    unnamed x18, local copies, waits for them, and re-layouts  1.81 us
  transfers between devices with their start and end apart: 30, of which 14 were waited for; matrix products, arithmetic and copies ran while one was open for 1% of the time, Pallas kernels for 27%

profile of v19, /device:TPU:0, one launch (start us, length us, event | category | flops | bytes accessed | tf_op | source)
XLA Modules:
  0.0 62.8 jit_solution(8692937209425556977)
XLA Ops:
  0.0 0.5 collective-permute-start.1
  0.5 0.1 collective-permute-start.2
  0.5 2.9 %collective-permute-start.12 = (bf16[2048,128]{1,0:T(8,128)(2,1)}, bf16[2048,128]{1,0:T(8,128)(2,1)S(1)}, u32[]{:S(2)}, u32[]{:S(2)}) collective-permute-start(bf16[2048,128]{1,0:T(8,128)(2,1)} %bitcast.24), channel_id=1, source_target_pairs={{0,8},{4,20},{8,0},{12,28},{16,24},{20,4},{24,16},{28,12},{1,9},{5... | collective-permute-start | bytes 1572872 | tf_op jit(solution)/shard_map/ppermute | solution.py:64
  3.5 1.6 %collective-permute-start.6 = (bf16[2048,128]{1,0:T(8,128)(2,1)S(1)}, bf16[2048,128]{1,0:T(8,128)(2,1)S(1)}, u32[]{:S(2)}, u32[]{:S(2)}) collective-permute-start(bf16[2048,128]{1,0:T(8,128)(2,1)S(1)} %collective-permute-done.1.refs_6_), channel_id=1, source_target_pairs={{0,8},{4,20},{8,0},{12,28},{16,24},{20,4},{24,16},{28,12},{1,9},{5... | collective-permute-start | bytes 1572872 | tf_op jit(solution)/shard_map/ppermute | solution.py:64
  5.1 0.7 %copy-done.5 = f32[2,2048]{1,0:T(2,128)S(1)} copy-done((f32[2,2048]{1,0:T(2,128)S(1)}, f32[2,2048]{1,0:T(2,128)}, u32[]{:S(2)}) %copy-start.5) | copy-done | bytes 16408
  5.8 0.1 squares.1
  5.9 1.1 %collective-permute-done = f32[2,128]{1,0:T(2,128)S(1)} collective-permute-done((f32[2,128]{1,0:T(2,128)S(1)}, f32[2,128]{1,0:T(2,128)S(1)}, u32[]{:S(2)}, u32[]{:S(2)}) %collective-permute-start) | collective-permute-done | bytes 1056 | tf_op jit(solution)/shard_map/ppermute | solution.py:43
  7.0 1.5 %collective-permute-start.3 = (f32[2,128]{1,0:T(2,128)S(1)}, f32[2,128]{1,0:T(2,128)S(1)}, u32[]{:S(2)}, u32[]{:S(2)}) collective-permute-start(f32[2,128]{1,0:T(2,128)S(1)} %add.53), channel_id=1, source_target_pairs={{0,16},{4,12},{8,24},{12,4},{16,0},{20,28},{24,8},{28,20},{1,17},{... | collective-permute-start | bytes 3080 | tf_op jit(solution)/shard_map/ppermute | solution.py:64
  8.5 0.8 %copy-done.4 = f32[1,16384]{1,0:T(1,128)S(1)} copy-done((f32[1,16384]{1,0:T(1,128)S(1)}, f32[1,16384]{1,0:T(1,128)}, u32[]{:S(2)}) %copy-start.4) | copy-done | bytes 65560
  9.4 3.2 %normalise.3 = (bf16[8,64,2048]{2,1,0:T(8,128)(2,1)S(1)}, bf16[8,64,2048]{2,1,0:T(8,128)(2,1)S(1)}) custom-call(bf16[320,16384]{1,0:T(8,128)(2,1)} %bitcast.36, f32[8,1,2048]{2,1,0:T(1,128)S(1)} %bitcast.31), custom_call_target="tpu_custom_call" | custom-call | flops 1000 | bytes 1000 | tf_op jit(solution)/shard_map/normalise/pallas_call | solution.py:173
  12.6 0.1 collective-permute-start.4
  12.7 0.6 collective-permute-start.8
  13.3 0.5 collective-permute-done.4
  13.8 0.2 collective-permute-start.13
  14.0 0.9 %collective-permute-start.5 = (f32[2,128]{1,0:T(2,128)S(1)}, f32[2,128]{1,0:T(2,128)S(1)}, u32[]{:S(2)}, u32[]{:S(2)}) collective-permute-start(f32[2,128]{1,0:T(2,128)S(1)} %collective-permute-done.4), channel_id=1, source_target_pairs={{0,16},{4,12},{8,24},{12,4},{16,0},{20,28},{24,8},{28,20},{1,17},{... | collective-permute-start | bytes 3080 | tf_op jit(solution)/shard_map/ppermute | solution.py:64
  14.9 3.3 %normalise.4 = (bf16[8,64,2048]{2,1,0:T(8,128)(2,1)S(1)}, bf16[8,64,2048]{2,1,0:T(8,128)(2,1)S(1)}) custom-call(bf16[320,16384]{1,0:T(8,128)(2,1)} %bitcast.37, f32[8,1,2048]{2,1,0:T(1,128)S(1)} %bitcast.32), custom_call_target="tpu_custom_call" | custom-call | flops 1000 | bytes 1000 | tf_op jit(solution)/shard_map/normalise/pallas_call | solution.py:173
  18.3 0.1 copy-done
  18.4 0.1 copy-done.2
  18.5 0.8 %query_products.1 = f32[2,10,128]{2,1,0:T(8,128)S(1)} custom-call(s32[1]{0:T(128)} %bitcast.place_ref, f32[2,128]{1,0:T(2,128)S(1)} %add_add_fusion.2.squares_ref, f32[2,2048]{1,0:T(2,128)S(1)} %copy-done.5, f32[8,1,2048]{2,1,0:T(1,128)S(1)} %bitcast.33, bf16[2048,1024]{1,0:T(8,128)(2,1)S(1)} %bitcast.21, bf16[2048,128]{1,0:T(8,128)(2,1)S(1)} %bitcast.25, ...), custom_call_target="tpu_custom_call" | custom-call | flops 1000 | bytes 1000 | tf_op jit(solution)/shard_map/query_products/pallas_call | solution.py:371
  19.3 0.1 collective-permute-start.7
  19.5 0.5 collective-permute-start.15
  20.0 0.8 %collective-permute-start.14 = (bf16[2048,128]{1,0:T(8,128)(2,1)S(1)}, bf16[2048,128]{1,0:T(8,128)(2,1)S(1)}, u32[]{:S(2)}, u32[]{:S(2)}) collective-permute-start(bf16[2048,128]{1,0:T(8,128)(2,1)S(1)} %collective-permute-done.13.refs_7_), channel_id=1, source_target_pairs={{0,8},{4,20},{8,0},{12,28},{16,24},{20,4},{24,16},{28,12},{1,9},{5... | collective-permute-start | bytes 1572872 | tf_op jit(solution)/shard_map/ppermute | solution.py:64
  20.8 1.2 %collective-permute-start.9 = (f32[2,10,128]{2,1,0:T(8,128)S(1)}, f32[2,10,128]{2,1,0:T(8,128)S(1)}, u32[]{:S(2)}, u32[]{:S(2)}) collective-permute-start(f32[2,10,128]{2,1,0:T(8,128)S(1)} %add.57), channel_id=1, source_target_pairs={{0,16},{4,12},{8,24},{12,4},{16,0},{20,28},{24,8},{28,20},{1,17},{... | collective-permute-start | bytes 30728 | tf_op jit(solution)/shard_map/ppermute | solution.py:64
  22.0 0.1 multiply_sine_fusion.1
  22.1 2.1 %normalise.5.refs_4_ = bf16[8,64,2048]{2,1,0:T(8,128)(2,1)S(1)} custom-call(bf16[320,16384]{1,0:T(8,128)(2,1)} %bitcast.38, f32[8,1,2048]{2,1,0:T(1,128)S(1)} %bitcast.34), custom_call_target="tpu_custom_call" | custom-call | flops 1000 | bytes 1000 | tf_op jit(solution)/shard_map/normalise/pallas_call | solution.py:173
  24.2 0.6 collective-permute-done.9
  24.8 1.3 %collective-permute-start.20 = (bf16[2048,128]{1,0:T(8,128)(2,1)S(1)}, bf16[2048,128]{1,0:T(8,128)(2,1)S(1)}, u32[]{:S(2)}, u32[]{:S(2)}) collective-permute-start(bf16[2048,128]{1,0:T(8,128)(2,1)S(1)} %collective-permute-done.2.refs_6_), channel_id=1, source_target_pairs={{0,8},{4,20},{8,0},{12,28},{16,24},{20,4},{24,16},{28,12},{1,9},{5... | collective-permute-start | bytes 1572872 | tf_op jit(solution)/shard_map/ppermute | solution.py:64
  26.1 0.9 %project.6.refs_9_ = f32[320,128]{1,0:T(8,128)S(1)} custom-call(s32[1]{0:T(128)} %bitcast.place_ref, bf16[8,64,2048]{2,1,0:T(8,128)(2,1)S(1)} %get-tuple-element.37.refs_0_, bf16[8,64,2048]{2,1,0:T(8,128)(2,1)S(1)} %get-tuple-element.38.refs_1_, bf16[8,64,2048]{2,1,0:T(8,128)(2,1)S(1)} %get-tuple-element.41.refs_2_, ...), custom_call_target="tpu_custom_call" | custom-call | flops 1000 | bytes 1000 | tf_op jit(solution)/shard_map/project/pallas_call | solution.py:218
  27.0 0.2 collective-permute-start.17
  27.2 1.0 %collective-permute-done.17 = f32[2,10,128]{2,1,0:T(8,128)S(1)} collective-permute-done((f32[2,10,128]{2,1,0:T(8,128)S(1)}, f32[2,10,128]{2,1,0:T(8,128)S(1)}, u32[]{:S(2)}, u32[]{:S(2)}) %collective-permute-start.17) | collective-permute-done | bytes 10272 | tf_op jit(solution)/shard_map/ppermute | solution.py:43
  28.2 1.1 %collective-permute-start.18 = (f32[2,10,128]{2,1,0:T(8,128)S(1)}, f32[2,10,128]{2,1,0:T(8,128)S(1)}, u32[]{:S(2)}, u32[]{:S(2)}) collective-permute-start(f32[2,10,128]{2,1,0:T(8,128)S(1)} %collective-permute-done.17), channel_id=1, source_target_pairs={{0,16},{4,12},{8,24},{12,4},{16,0},{20,28},{24,8},{28,20},{1,17},{... | collective-permute-start | bytes 30728 | tf_op jit(solution)/shard_map/ppermute | solution.py:64
  29.3 1.5 %project.7.refs_7_ = f32[320,128]{1,0:T(8,128)S(1)} custom-call(s32[1]{0:T(128)} %bitcast.place_ref, bf16[8,64,2048]{2,1,0:T(8,128)(2,1)S(1)} %get-tuple-element.37.refs_0_, bf16[8,64,2048]{2,1,0:T(8,128)(2,1)S(1)} %get-tuple-element.38.refs_1_, bf16[8,64,2048]{2,1,0:T(8,128)(2,1)S(1)} %get-tuple-element.41.refs_2_, ...), custom_call_target="tpu_custom_call" | custom-call | flops 1000 | bytes 1000 | tf_op jit(solution)/shard_map/project/pallas_call | solution.py:218
  30.9 0.1 collective-permute-start.16
  31.0 0.6 %multiply_sine_fusion = (f32[320,64]{1,0:T(8,128)S(1)}, f32[320,64]{1,0:T(8,128)S(1)}) fusion(f32[64]{0:T(128)S(1)} %multiply_exponential_fusion, f32[320]{0:T(512)S(1)} %add_convert_fusion), kind=kLoop, calls=%fused_computation | loop fusion | flops 20480 | bytes 165376 | tf_op jit(solution)/shard_map/sin | solution.py:97
  31.6 0.9 %collective-permute-start.11 = (bf16[2048,128]{1,0:T(8,128)(2,1)S(1)}, bf16[2048,128]{1,0:T(8,128)(2,1)S(1)}, u32[]{:S(2)}, u32[]{:S(2)}) collective-permute-start(bf16[2048,128]{1,0:T(8,128)(2,1)S(1)} %collective-permute-done.10.refs_7_), channel_id=1, source_target_pairs={{0,8},{4,20},{8,0},{12,28},{16,24},{20,4},{24,16},{28,12},{1,9},{5... | collective-permute-start | bytes 1572872 | tf_op jit(solution)/shard_map/ppermute | solution.py:64
  32.6 0.0 copy-start.7
  32.6 0.3 collective-permute-done.16.refs_6_
  32.9 0.9 %project.8.refs_0_ = f32[320,128]{1,0:T(8,128)S(1)} custom-call(s32[1]{0:T(128)} %bitcast.place_ref, bf16[8,64,2048]{2,1,0:T(8,128)(2,1)S(1)} %get-tuple-element.37.refs_0_, bf16[8,64,2048]{2,1,0:T(8,128)(2,1)S(1)} %get-tuple-element.38.refs_1_, bf16[8,64,2048]{2,1,0:T(8,128)(2,1)S(1)} %get-tuple-element.41.refs_2_, ...), custom_call_target="tpu_custom_call" | custom-call | flops 1000 | bytes 1000 | tf_op jit(solution)/shard_map/project/pallas_call | solution.py:218
  33.7 1.0 %scores.1 = (f32[8,320]{1,0:T(8,128)S(1)}, f32[8,128]{1,0:T(8,128)S(1)}, f32[8,128]{1,0:T(8,128)S(1)}) custom-call(s32[1]{0:T(128)} %bitcast.place_ref, s32[2]{0:T(128)S(1)} %copy-done.7, f32[320,128]{1,0:T(8,128)S(1)} %project.8.refs_0_, f32[320,64]{1,0:T(8,128)S(1)} %get-tuple-element.64.refs_1_, f32[320,64]{1,0:T(8,128)S(1)} %get-tuple-element.63.refs_2_, ...), custom_call_target="tpu_custom_call" | custom-call | flops 1000 | bytes 1000 | tf_op jit(solution)/shard_map/scores/pallas_call | solution.py:398
  34.7 0.1 collective-permute-start.19
  34.9 1.0 %collective-permute-done.19 = f32[8,128]{1,0:T(8,128)S(1)} collective-permute-done((f32[8,128]{1,0:T(8,128)S(1)}, f32[8,128]{1,0:T(8,128)S(1)}, u32[]{:S(2)}, u32[]{:S(2)}) %collective-permute-start.19) | collective-permute-done | bytes 4128 | tf_op jit(solution)/shard_map/ppermute | solution.py:43
  35.9 0.2 collective-permute-start.23
  36.1 1.0 %collective-permute-start.21 = (f32[8,128]{1,0:T(8,128)S(1)}, f32[8,128]{1,0:T(8,128)S(1)}, u32[]{:S(2)}, u32[]{:S(2)}) collective-permute-start(f32[8,128]{1,0:T(8,128)S(1)} %max.6), channel_id=1, source_target_pairs={{0,16},{4,12},{8,24},{12,4},{16,0},{20,28},{24,8},{28,20},{1,17},{... | collective-permute-start | bytes 12296 | tf_op jit(solution)/shard_map/ppermute | solution.py:64
  37.0 1.5 %project.9.refs_7_ = f32[320,128]{1,0:T(8,128)S(1)} custom-call(s32[1]{0:T(128)} %bitcast.place_ref, bf16[8,64,2048]{2,1,0:T(8,128)(2,1)S(1)} %get-tuple-element.37.refs_0_, bf16[8,64,2048]{2,1,0:T(8,128)(2,1)S(1)} %get-tuple-element.38.refs_1_, bf16[8,64,2048]{2,1,0:T(8,128)(2,1)S(1)} %get-tuple-element.41.refs_2_, ...), custom_call_target="tpu_custom_call" | custom-call | flops 1000 | bytes 1000 | tf_op jit(solution)/shard_map/project/pallas_call | solution.py:218
  38.6 1.2 %collective-permute-done.21 = f32[8,128]{1,0:T(8,128)S(1)} collective-permute-done((f32[8,128]{1,0:T(8,128)S(1)}, f32[8,128]{1,0:T(8,128)S(1)}, u32[]{:S(2)}, u32[]{:S(2)}) %collective-permute-start.21) | collective-permute-done | bytes 4128 | tf_op jit(solution)/shard_map/ppermute | solution.py:64
  39.8 1.1 %collective-permute-done.11.refs_5_ = bf16[2048,128]{1,0:T(8,128)(2,1)S(1)} collective-permute-done((bf16[2048,128]{1,0:T(8,128)(2,1)S(1)}, bf16[2048,128]{1,0:T(8,128)(2,1)S(1)}, u32[]{:S(2)}, u32[]{:S(2)}) %collective-permute-start.11) | collective-permute-done | bytes 524320 | tf_op jit(solution)/shard_map/ppermute | solution.py:64
  40.9 0.5 collective-permute-start.24
  41.4 0.9 %project.10.refs_6_ = f32[320,128]{1,0:T(8,128)S(1)} custom-call(s32[1]{0:T(128)} %bitcast.place_ref, bf16[8,64,2048]{2,1,0:T(8,128)(2,1)S(1)} %get-tuple-element.37.refs_0_, bf16[8,64,2048]{2,1,0:T(8,128)(2,1)S(1)} %get-tuple-element.38.refs_1_, bf16[8,64,2048]{2,1,0:T(8,128)(2,1)S(1)} %get-tuple-element.41.refs_2_, ...), custom_call_target="tpu_custom_call" | custom-call | flops 1000 | bytes 1000 | tf_op jit(solution)/shard_map/project/pallas_call | solution.py:218
  42.3 0.5 collective-permute-done.24
  42.9 0.5 project.11.refs_6_
  43.4 0.0 copy-start.1
  43.4 1.2 %weighted_values.1 = f32[8,256]{1,0:T(8,128)S(1)} custom-call(s32[1]{0:T(128)} %bitcast.place_ref, s32[2]{0:T(128)S(1)} %copy-done.7, bf16[8,64,2048]{2,1,0:T(8,128)(2,1)S(1)} %get-tuple-element.37.refs_0_, bf16[8,64,2048]{2,1,0:T(8,128)(2,1)S(1)} %get-tuple-element.38.refs_1_, bf16[8,64,2048]{2,1,0:T(8,128)(2,1)S(1)} %get-tuple-element.41.refs_2_, ...), custom_call_target="tpu_custom_call" | custom-call | flops 1000 | bytes 1000 | tf_op jit(solution)/shard_map/weighted_values/pallas_call | solution.py:423
  44.6 0.1 collective-permute-start.25
  44.7 1.0 %collective-permute-done.25 = f32[8,256]{1,0:T(8,128)S(1)} collective-permute-done((f32[8,256]{1,0:T(8,128)S(1)}, f32[8,256]{1,0:T(8,128)S(1)}, u32[]{:S(2)}, u32[]{:S(2)}) %collective-permute-start.25) | collective-permute-done | bytes 8224 | tf_op jit(solution)/shard_map/ppermute | solution.py:43
  45.7 0.9 %collective-permute-start.26 = (f32[8,256]{1,0:T(8,128)S(1)}, f32[8,256]{1,0:T(8,128)S(1)}, u32[]{:S(2)}, u32[]{:S(2)}) collective-permute-start(f32[8,256]{1,0:T(8,128)S(1)} %add.64), channel_id=1, source_target_pairs={{0,8},{4,12},{8,0},{12,4},{16,24},{20,28},{24,16},{28,20},{1,9},{5... | collective-permute-start | bytes 24584 | tf_op jit(solution)/shard_map/ppermute | solution.py:43
  46.6 2.8 %collective-permute-done.26 = f32[8,256]{1,0:T(8,128)S(1)} collective-permute-done((f32[8,256]{1,0:T(8,128)S(1)}, f32[8,256]{1,0:T(8,128)S(1)}, u32[]{:S(2)}, u32[]{:S(2)}) %collective-permute-start.26) | collective-permute-done | bytes 8224 | tf_op jit(solution)/shard_map/ppermute | solution.py:43
  49.4 0.9 %collective-permute-start.27 = (f32[8,256]{1,0:T(8,128)S(1)}, f32[8,256]{1,0:T(8,128)S(1)}, u32[]{:S(2)}, u32[]{:S(2)}) collective-permute-start(f32[8,256]{1,0:T(8,128)S(1)} %add.65.mine_ref), channel_id=1, source_target_pairs={{0,16},{4,20},{8,24},{12,28},{16,0},{20,4},{24,8},{28,12},{1,17},{... | collective-permute-start | bytes 24584 | tf_op jit(solution)/shard_map/ppermute | solution.py:43
  50.3 2.7 %collective-permute-done.27.other_ref = f32[8,256]{1,0:T(8,128)S(1)} collective-permute-done((f32[8,256]{1,0:T(8,128)S(1)}, f32[8,256]{1,0:T(8,128)S(1)}, u32[]{:S(2)}, u32[]{:S(2)}) %collective-permute-start.27) | collective-permute-done | bytes 8224 | tf_op jit(solution)/shard_map/ppermute | solution.py:43
  53.1 0.6 %output_products.1 = f32[2,2048]{1,0:T(2,128)S(1)} custom-call(s32[1]{0:T(128)} %bitcast.place_ref, f32[8,256]{1,0:T(8,128)S(1)} %add.65.mine_ref, f32[8,256]{1,0:T(8,128)S(1)} %collective-permute-done.27.other_ref, bf16[1024,2048]{1,0:T(8,128)(2,1)S(1)} %bitcast.22), custom_call_target="tpu_custom_call" | custom-call | flops 1000 | bytes 1000 | tf_op jit(solution)/shard_map/output_products/pallas_call | solution.py:441
  53.7 1.6 %collective-permute-start.28 = (f32[2,2048]{1,0:T(2,128)S(1)}, f32[2,2048]{1,0:T(2,128)S(1)}, u32[]{:S(2)}, u32[]{:S(2)}) collective-permute-start(f32[2,2048]{1,0:T(2,128)S(1)} %output_products.1), channel_id=1, source_target_pairs={{0,1},{1,0},{2,3},{3,2},{4,5},{5,4},{6,7},{7,6},{8,9},{9,8},{10,11... | collective-permute-start | bytes 49160 | tf_op jit(solution)/shard_map/ppermute | solution.py:43
  55.3 2.2 %collective-permute-done.28 = f32[2,2048]{1,0:T(2,128)S(1)} collective-permute-done((f32[2,2048]{1,0:T(2,128)S(1)}, f32[2,2048]{1,0:T(2,128)S(1)}, u32[]{:S(2)}, u32[]{:S(2)}) %collective-permute-start.28) | collective-permute-done | bytes 16416 | tf_op jit(solution)/shard_map/ppermute | solution.py:43
  57.5 2.7 %collective-permute-start.29 = (f32[2,2048]{1,0:T(2,128)S(1)}, f32[2,2048]{1,0:T(2,128)S(1)}, u32[]{:S(2)}, u32[]{:S(2)}) collective-permute-start(f32[2,2048]{1,0:T(2,128)S(1)} %add.66), channel_id=1, source_target_pairs={{0,2},{1,3},{2,0},{3,1},{4,6},{5,7},{6,4},{7,5},{8,10},{9,11},{10,... | collective-permute-start | bytes 49160 | tf_op jit(solution)/shard_map/ppermute | solution.py:43
  60.1 2.0 %collective-permute-done.29 = f32[2,2048]{1,0:T(2,128)S(1)} collective-permute-done((f32[2,2048]{1,0:T(2,128)S(1)}, f32[2,2048]{1,0:T(2,128)S(1)}, u32[]{:S(2)}, u32[]{:S(2)}) %collective-permute-start.29) | collective-permute-done | bytes 16416 | tf_op jit(solution)/shard_map/ppermute | solution.py:43
  62.2 0.6 add_add_fusion
  (47 shorter events, 0.2 us)
Async XLA Ops:
  0.0 3.5 %collective-permute-start.1 = (bf16[2048,128]{1,0:T(8,128)(2,1)}, bf16[2048,128]{1,0:T(8,128)(2,1)S(1)}, u32[]{:S(2)}, u32[]{:S(2)}) collective-permute-start(bf16[2048,128]{1,0:T(8,128)(2,1)} %bitcast.23), channel_id=1, source_target_pairs={{0,4},{4,0},{8,12},{12,8},{16,20},{20,16},{24,28},{28,24},{1,5},{5... | collective-permute-start | bytes 1572872 | tf_op jit(solution)/shard_map/ppermute | solution.py:43
  0.5 6.6 %collective-permute-start.2 = (bf16[2048,128]{1,0:T(8,128)(2,1)}, bf16[2048,128]{1,0:T(8,128)(2,1)S(1)}, u32[]{:S(2)}, u32[]{:S(2)}) collective-permute-start(bf16[2048,128]{1,0:T(8,128)(2,1)} %bitcast.27), channel_id=1, source_target_pairs={{0,4},{4,0},{8,12},{12,8},{16,20},{20,16},{24,28},{28,24},{1,5},{5... | collective-permute-start | bytes 1572872 | tf_op jit(solution)/shard_map/ppermute | solution.py:43
  0.5 12.8 %collective-permute-start.12 = (bf16[2048,128]{1,0:T(8,128)(2,1)}, bf16[2048,128]{1,0:T(8,128)(2,1)S(1)}, u32[]{:S(2)}, u32[]{:S(2)}) collective-permute-start(bf16[2048,128]{1,0:T(8,128)(2,1)} %bitcast.24), channel_id=1, source_target_pairs={{0,8},{4,20},{8,0},{12,28},{16,24},{20,4},{24,16},{28,12},{1,9},{5... | collective-permute-start | bytes 1572872 | tf_op jit(solution)/shard_map/ppermute | solution.py:64
  3.5 14.8 %collective-permute-start.6 = (bf16[2048,128]{1,0:T(8,128)(2,1)S(1)}, bf16[2048,128]{1,0:T(8,128)(2,1)S(1)}, u32[]{:S(2)}, u32[]{:S(2)}) collective-permute-start(bf16[2048,128]{1,0:T(8,128)(2,1)S(1)} %collective-permute-done.1.refs_6_), channel_id=1, source_target_pairs={{0,8},{4,20},{8,0},{12,28},{16,24},{20,4},{24,16},{28,12},{1,9},{5... | collective-permute-start | bytes 1572872 | tf_op jit(solution)/shard_map/ppermute | solution.py:64
  5.1 0.7 %copy-start.5 = (f32[2,2048]{1,0:T(2,128)S(1)}, f32[2,2048]{1,0:T(2,128)}, u32[]{:S(2)}) copy-start(f32[2,2048]{1,0:T(2,128)} %tokens_ref.3) | copy-start | bytes 49156
  5.9 1.1 %collective-permute-start = (f32[2,128]{1,0:T(2,128)S(1)}, f32[2,128]{1,0:T(2,128)S(1)}, u32[]{:S(2)}, u32[]{:S(2)}) collective-permute-start(f32[2,128]{1,0:T(2,128)S(1)} %get-tuple-element.34), channel_id=1, source_target_pairs={{0,4},{4,0},{8,12},{12,8},{16,20},{20,16},{24,28},{28,24},{1,5},{5... | collective-permute-start | bytes 3080 | tf_op jit(solution)/shard_map/ppermute | solution.py:43
  7.0 5.6 %collective-permute-start.3 = (f32[2,128]{1,0:T(2,128)S(1)}, f32[2,128]{1,0:T(2,128)S(1)}, u32[]{:S(2)}, u32[]{:S(2)}) collective-permute-start(f32[2,128]{1,0:T(2,128)S(1)} %add.53), channel_id=1, source_target_pairs={{0,16},{4,12},{8,24},{12,4},{16,0},{20,28},{24,8},{28,20},{1,17},{... | collective-permute-start | bytes 3080 | tf_op jit(solution)/shard_map/ppermute | solution.py:64
  8.5 0.8 %copy-start.4 = (f32[1,16384]{1,0:T(1,128)S(1)}, f32[1,16384]{1,0:T(1,128)}, u32[]{:S(2)}) copy-start(f32[1,16384]{1,0:T(1,128)} %param.11) | copy-start | bytes 196612
  9.4 3.3 %copy-start.3 = (bf16[1,2048,128]{2,1,0:T(8,128)(2,1)S(1)}, bf16[1,2048,128]{2,1,0:T(8,128)(2,1)}, u32[]{:S(2)}) copy-start(bf16[1,2048,128]{2,1,0:T(8,128)(2,1)} %param.14) | copy-start | bytes 1572868
  12.6 1.2 %collective-permute-start.4 = (f32[2,128]{1,0:T(2,128)S(1)}, f32[2,128]{1,0:T(2,128)S(1)}, u32[]{:S(2)}, u32[]{:S(2)}) collective-permute-start(f32[2,128]{1,0:T(2,128)S(1)} %collective-permute-done.3), channel_id=1, source_target_pairs={{0,4},{4,0},{8,12},{12,8},{16,20},{20,16},{24,28},{28,24},{1,5},{5... | collective-permute-start | bytes 3080 | tf_op jit(solution)/shard_map/ppermute | solution.py:43
  12.7 12.2 %collective-permute-start.8 = (bf16[2048,128]{1,0:T(8,128)(2,1)S(1)}, bf16[2048,128]{1,0:T(8,128)(2,1)S(1)}, u32[]{:S(2)}, u32[]{:S(2)}) collective-permute-start(bf16[2048,128]{1,0:T(8,128)(2,1)S(1)} %bitcast.28), channel_id=1, source_target_pairs={{0,8},{4,20},{8,0},{12,28},{16,24},{20,4},{24,16},{28,12},{1,9},{5... | collective-permute-start | bytes 1572872 | tf_op jit(solution)/shard_map/ppermute | solution.py:64
  13.8 6.2 %collective-permute-start.13 = (bf16[2048,128]{1,0:T(8,128)(2,1)S(1)}, bf16[2048,128]{1,0:T(8,128)(2,1)S(1)}, u32[]{:S(2)}, u32[]{:S(2)}) collective-permute-start(bf16[2048,128]{1,0:T(8,128)(2,1)S(1)} %collective-permute-done.12.refs_5_), channel_id=1, source_target_pairs={{0,4},{4,0},{8,12},{12,8},{16,20},{20,16},{24,28},{28,24},{1,5},{5... | collective-permute-start | bytes 1572872 | tf_op jit(solution)/shard_map/ppermute | solution.py:43
  14.0 4.2 %collective-permute-start.5 = (f32[2,128]{1,0:T(2,128)S(1)}, f32[2,128]{1,0:T(2,128)S(1)}, u32[]{:S(2)}, u32[]{:S(2)}) collective-permute-start(f32[2,128]{1,0:T(2,128)S(1)} %collective-permute-done.4), channel_id=1, source_target_pairs={{0,16},{4,12},{8,24},{12,4},{16,0},{20,28},{24,8},{28,20},{1,17},{... | collective-permute-start | bytes 3080 | tf_op jit(solution)/shard_map/ppermute | solution.py:64
  14.9 3.4 %copy-start = (bf16[1,2048,1024]{2,1,0:T(8,128)(2,1)S(1)}, bf16[1,2048,1024]{2,1,0:T(8,128)(2,1)}, u32[]{:S(2)}) copy-start(bf16[1,2048,1024]{2,1,0:T(8,128)(2,1)} %param.12) | copy-start | bytes 12582916
  14.9 3.6 %copy-start.2 = (bf16[1,2048,128]{2,1,0:T(8,128)(2,1)S(1)}, bf16[1,2048,128]{2,1,0:T(8,128)(2,1)}, u32[]{:S(2)}) copy-start(bf16[1,2048,128]{2,1,0:T(8,128)(2,1)} %param.13) | copy-start | bytes 1572868
  18.5 1.0 %copy-start.8 = (s32[2]{0:T(128)S(1)}, s32[2]{0:T(128)}, u32[]{:S(2)}) copy-start(s32[2]{0:T(128)} %param.17) | copy-start | bytes 28
  19.3 1.5 %collective-permute-start.7 = (f32[2,10,128]{2,1,0:T(8,128)S(1)}, f32[2,10,128]{2,1,0:T(8,128)S(1)}, u32[]{:S(2)}, u32[]{:S(2)}) collective-permute-start(f32[2,10,128]{2,1,0:T(8,128)S(1)} %query_products.1), channel_id=1, source_target_pairs={{0,4},{4,0},{8,12},{12,8},{16,20},{20,16},{24,28},{28,24},{1,5},{5... | collective-permute-start | bytes 30728 | tf_op jit(solution)/shard_map/ppermute | solution.py:43
  19.5 9.8 %collective-permute-start.15 = (bf16[2048,128]{1,0:T(8,128)(2,1)S(1)}, bf16[2048,128]{1,0:T(8,128)(2,1)S(1)}, u32[]{:S(2)}, u32[]{:S(2)}) collective-permute-start(bf16[2048,128]{1,0:T(8,128)(2,1)S(1)} %collective-permute-done.6.refs_6_), channel_id=1, source_target_pairs={{0,4},{4,0},{8,12},{12,8},{16,20},{20,16},{24,28},{28,24},{1,5},{5... | collective-permute-start | bytes 1572872 | tf_op jit(solution)/shard_map/ppermute | solution.py:43
  20.0 10.9 %collective-permute-start.14 = (bf16[2048,128]{1,0:T(8,128)(2,1)S(1)}, bf16[2048,128]{1,0:T(8,128)(2,1)S(1)}, u32[]{:S(2)}, u32[]{:S(2)}) collective-permute-start(bf16[2048,128]{1,0:T(8,128)(2,1)S(1)} %collective-permute-done.13.refs_7_), channel_id=1, source_target_pairs={{0,8},{4,20},{8,0},{12,28},{16,24},{20,4},{24,16},{28,12},{1,9},{5... | collective-permute-start | bytes 1572872 | tf_op jit(solution)/shard_map/ppermute | solution.py:64
  20.8 4.0 %collective-permute-start.9 = (f32[2,10,128]{2,1,0:T(8,128)S(1)}, f32[2,10,128]{2,1,0:T(8,128)S(1)}, u32[]{:S(2)}, u32[]{:S(2)}) collective-permute-start(f32[2,10,128]{2,1,0:T(8,128)S(1)} %add.57), channel_id=1, source_target_pairs={{0,16},{4,12},{8,24},{12,4},{16,0},{20,28},{24,8},{28,20},{1,17},{... | collective-permute-start | bytes 30728 | tf_op jit(solution)/shard_map/ppermute | solution.py:64
  24.8 6.8 %collective-permute-start.10 = (bf16[2048,128]{1,0:T(8,128)(2,1)S(1)}, bf16[2048,128]{1,0:T(8,128)(2,1)S(1)}, u32[]{:S(2)}, u32[]{:S(2)}) collective-permute-start(bf16[2048,128]{1,0:T(8,128)(2,1)S(1)} %collective-permute-done.8.refs_8_), channel_id=1, source_target_pairs={{0,4},{4,0},{8,12},{12,8},{16,20},{20,16},{24,28},{28,24},{1,5},{5... | collective-permute-start | bytes 1572872 | tf_op jit(solution)/shard_map/ppermute | solution.py:43
  24.8 11.1 %collective-permute-start.20 = (bf16[2048,128]{1,0:T(8,128)(2,1)S(1)}, bf16[2048,128]{1,0:T(8,128)(2,1)S(1)}, u32[]{:S(2)}, u32[]{:S(2)}) collective-permute-start(bf16[2048,128]{1,0:T(8,128)(2,1)S(1)} %collective-permute-done.2.refs_6_), channel_id=1, source_target_pairs={{0,8},{4,20},{8,0},{12,28},{16,24},{20,4},{24,16},{28,12},{1,9},{5... | collective-permute-start | bytes 1572872 | tf_op jit(solution)/shard_map/ppermute | solution.py:64
  27.0 1.2 %collective-permute-start.17 = (f32[2,10,128]{2,1,0:T(8,128)S(1)}, f32[2,10,128]{2,1,0:T(8,128)S(1)}, u32[]{:S(2)}, u32[]{:S(2)}) collective-permute-start(f32[2,10,128]{2,1,0:T(8,128)S(1)} %collective-permute-done.9), channel_id=1, source_target_pairs={{0,4},{4,0},{8,12},{12,8},{16,20},{20,16},{24,28},{28,24},{1,5},{5... | collective-permute-start | bytes 30728 | tf_op jit(solution)/shard_map/ppermute | solution.py:43
  28.2 4.3 %collective-permute-start.18 = (f32[2,10,128]{2,1,0:T(8,128)S(1)}, f32[2,10,128]{2,1,0:T(8,128)S(1)}, u32[]{:S(2)}, u32[]{:S(2)}) collective-permute-start(f32[2,10,128]{2,1,0:T(8,128)S(1)} %collective-permute-done.17), channel_id=1, source_target_pairs={{0,16},{4,12},{8,24},{12,4},{16,0},{20,28},{24,8},{28,20},{1,17},{... | collective-permute-start | bytes 30728 | tf_op jit(solution)/shard_map/ppermute | solution.py:64
  30.9 2.0 %collective-permute-start.16 = (bf16[2048,128]{1,0:T(8,128)(2,1)S(1)}, bf16[2048,128]{1,0:T(8,128)(2,1)S(1)}, u32[]{:S(2)}, u32[]{:S(2)}) collective-permute-start(bf16[2048,128]{1,0:T(8,128)(2,1)S(1)} %collective-permute-done.14.refs_5_), channel_id=1, source_target_pairs={{0,4},{4,0},{8,12},{12,8},{16,20},{20,16},{24,28},{28,24},{1,5},{5... | collective-permute-start | bytes 1572872 | tf_op jit(solution)/shard_map/ppermute | solution.py:43
  31.6 9.3 %collective-permute-start.11 = (bf16[2048,128]{1,0:T(8,128)(2,1)S(1)}, bf16[2048,128]{1,0:T(8,128)(2,1)S(1)}, u32[]{:S(2)}, u32[]{:S(2)}) collective-permute-start(bf16[2048,128]{1,0:T(8,128)(2,1)S(1)} %collective-permute-done.10.refs_7_), channel_id=1, source_target_pairs={{0,8},{4,20},{8,0},{12,28},{16,24},{20,4},{24,16},{28,12},{1,9},{5... | collective-permute-start | bytes 1572872 | tf_op jit(solution)/shard_map/ppermute | solution.py:64
  32.6 1.1 %copy-start.7 = (s32[2]{0:T(128)S(1)}, s32[2]{0:T(128)}, u32[]{:S(2)}) copy-start(s32[2]{0:T(128)} %lengths_ref.3) | copy-start | bytes 28
  34.7 1.2 %collective-permute-start.19 = (f32[8,128]{1,0:T(8,128)S(1)}, f32[8,128]{1,0:T(8,128)S(1)}, u32[]{:S(2)}, u32[]{:S(2)}) collective-permute-start(f32[8,128]{1,0:T(8,128)S(1)} %get-tuple-element.55), channel_id=1, source_target_pairs={{0,4},{4,0},{8,12},{12,8},{16,20},{20,16},{24,28},{28,24},{1,5},{5... | collective-permute-start | bytes 12296 | tf_op jit(solution)/shard_map/ppermute | solution.py:43
  35.9 5.5 %collective-permute-start.23 = (bf16[2048,128]{1,0:T(8,128)(2,1)S(1)}, bf16[2048,128]{1,0:T(8,128)(2,1)S(1)}, u32[]{:S(2)}, u32[]{:S(2)}) collective-permute-start(bf16[2048,128]{1,0:T(8,128)(2,1)S(1)} %collective-permute-done.20.refs_5_), channel_id=1, source_target_pairs={{0,4},{4,0},{8,12},{12,8},{16,20},{20,16},{24,28},{28,24},{1,5},{5... | collective-permute-start | bytes 1572872 | tf_op jit(solution)/shard_map/ppermute | solution.py:43
  36.1 3.7 %collective-permute-start.21 = (f32[8,128]{1,0:T(8,128)S(1)}, f32[8,128]{1,0:T(8,128)S(1)}, u32[]{:S(2)}, u32[]{:S(2)}) collective-permute-start(f32[8,128]{1,0:T(8,128)S(1)} %max.6), channel_id=1, source_target_pairs={{0,16},{4,12},{8,24},{12,4},{16,0},{20,28},{24,8},{28,20},{1,17},{... | collective-permute-start | bytes 12296 | tf_op jit(solution)/shard_map/ppermute | solution.py:64
  40.9 2.4 %collective-permute-start.22 = (bf16[2048,128]{1,0:T(8,128)(2,1)S(1)}, bf16[2048,128]{1,0:T(8,128)(2,1)S(1)}, u32[]{:S(2)}, u32[]{:S(2)}) collective-permute-start(bf16[2048,128]{1,0:T(8,128)(2,1)S(1)} %collective-permute-done.11.refs_5_), channel_id=1, source_target_pairs={{0,4},{4,0},{8,12},{12,8},{16,20},{20,16},{24,28},{28,24},{1,5},{5... | collective-permute-start | bytes 1572872 | tf_op jit(solution)/shard_map/ppermute | solution.py:43
  40.9 1.9 %collective-permute-start.24 = (f32[8,128]{1,0:T(8,128)S(1)}, f32[8,128]{1,0:T(8,128)S(1)}, u32[]{:S(2)}, u32[]{:S(2)}) collective-permute-start(f32[8,128]{1,0:T(8,128)S(1)} %max.7), channel_id=1, source_target_pairs={{0,4},{4,0},{8,12},{12,8},{16,20},{20,16},{24,28},{28,24},{1,5},{5... | collective-permute-start | bytes 12296 | tf_op jit(solution)/shard_map/ppermute | solution.py:43
  43.4 9.7 %copy-start.1 = (bf16[1,1024,2048]{2,1,0:T(8,128)(2,1)S(1)}, bf16[1,1024,2048]{2,1,0:T(8,128)(2,1)}, u32[]{:S(2)}) copy-start(bf16[1,1024,2048]{2,1,0:T(8,128)(2,1)} %param.15) | copy-start | bytes 12582916
  44.6 1.2 %collective-permute-start.25 = (f32[8,256]{1,0:T(8,128)S(1)}, f32[8,256]{1,0:T(8,128)S(1)}, u32[]{:S(2)}, u32[]{:S(2)}) collective-permute-start(f32[8,256]{1,0:T(8,128)S(1)} %weighted_values.1), channel_id=1, source_target_pairs={{0,4},{4,0},{8,12},{12,8},{16,20},{20,16},{24,28},{28,24},{1,5},{5... | collective-permute-start | bytes 24584 | tf_op jit(solution)/shard_map/ppermute | solution.py:43
  45.7 3.7 %collective-permute-start.26 = (f32[8,256]{1,0:T(8,128)S(1)}, f32[8,256]{1,0:T(8,128)S(1)}, u32[]{:S(2)}, u32[]{:S(2)}) collective-permute-start(f32[8,256]{1,0:T(8,128)S(1)} %add.64), channel_id=1, source_target_pairs={{0,8},{4,12},{8,0},{12,4},{16,24},{20,28},{24,16},{28,20},{1,9},{5... | collective-permute-start | bytes 24584 | tf_op jit(solution)/shard_map/ppermute | solution.py:43
  49.4 3.7 %collective-permute-start.27 = (f32[8,256]{1,0:T(8,128)S(1)}, f32[8,256]{1,0:T(8,128)S(1)}, u32[]{:S(2)}, u32[]{:S(2)}) collective-permute-start(f32[8,256]{1,0:T(8,128)S(1)} %add.65.mine_ref), channel_id=1, source_target_pairs={{0,16},{4,20},{8,24},{12,28},{16,0},{20,4},{24,8},{28,12},{1,17},{... | collective-permute-start | bytes 24584 | tf_op jit(solution)/shard_map/ppermute | solution.py:43
  53.1 9.1 %copy-start.6 = (f32[2,2048]{1,0:T(2,128)S(1)}, f32[2,2048]{1,0:T(2,128)}, u32[]{:S(2)}) copy-start(f32[2,2048]{1,0:T(2,128)} %tokens_ref.3) | copy-start | bytes 49156
  53.7 3.8 %collective-permute-start.28 = (f32[2,2048]{1,0:T(2,128)S(1)}, f32[2,2048]{1,0:T(2,128)S(1)}, u32[]{:S(2)}, u32[]{:S(2)}) collective-permute-start(f32[2,2048]{1,0:T(2,128)S(1)} %output_products.1), channel_id=1, source_target_pairs={{0,1},{1,0},{2,3},{3,2},{4,5},{5,4},{6,7},{7,6},{8,9},{9,8},{10,11... | collective-permute-start | bytes 49160 | tf_op jit(solution)/shard_map/ppermute | solution.py:43
  57.5 4.7 %collective-permute-start.29 = (f32[2,2048]{1,0:T(2,128)S(1)}, f32[2,2048]{1,0:T(2,128)S(1)}, u32[]{:S(2)}, u32[]{:S(2)}) collective-permute-start(f32[2,2048]{1,0:T(2,128)S(1)} %add.66), channel_id=1, source_target_pairs={{0,2},{1,3},{2,0},{3,1},{4,6},{5,7},{6,4},{7,5},{8,10},{9,11},{10,... | collective-permute-start | bytes 49160 | tf_op jit(solution)/shard_map/ppermute | solution.py:43

commit v20 on v19

--- a/solution.py
+++ b/solution.py
@@ -410,7 +410,7 @@
     value_total = project(after(places, near_top), rows, value_near + value_first)
     if split:
         received = jnp.maximum(top, after(by_core(top, 4, 2), value_last[0][1], value_total))
-        top = jnp.where(core == 0, swap(received, "ctx", 1), received)
+        told = swap(received, "ctx", 1)
     else:
         top = butterfly(top, "ctx", bits_below(team)[1:], jnp.maximum)
         received = top
@@ -420,6 +420,8 @@
 
     blocks = share(value_last, received)
     value_total = project(places, rows, value_last, value_total)
+    if split:
+        top = jnp.where(core == 0, after(told, value_total), received)
     packed = call(
         functools.partial(weigh_kernel, [d for d, _ in blocks], len(rows), team),
         "weighted_values",

time: 63 us -> 62.5 us (level)
  transfers between devices with their start and end apart: 30 -> 30, of which waited for: 14 -> 13; matrix products, arithmetic and copies ran while one was open for 1% -> 1% of each run, Pallas kernels for 27% -> 27%
where the time goes in v20:
time: 62.5 us; the launch traced here: 62.3 us
  starting transfers between devices  22.5 us (36%)
  Pallas kernels  18.5 us (30%)
  waiting for transfers between devices  17.7 us (28%)
  local copies, waits for them, and re-layouts  1.81 us (3%)
  other arithmetic  1.49 us (2%)
    ppermute x19, waiting for transfers between devices, swap(): return lax.ppermute(value, axis, [(i, i ^ distance) for i in range(count)])  14.8 us
    ppermute x11, starting transfers between devices, by_core(): return lax.ppermute(value, 'ctx', pairs)  13.9 us
    ppermute x19, starting transfers between devices, swap(): return lax.ppermute(value, axis, [(i, i ^ distance) for i in range(count)])  8.64 us
    pallas_call x3, Pallas kernels, normalise(): call(functools.partial(norm_kernel, first), 'normalise', [IN_HBM, IN_VMEM...  8.59 us
    pallas_call x6, Pallas kernels, project(): call(functools.partial(project_kernel, [d for d, _ in blocks], len(rows),...  6.17 us
    ppermute x11, waiting for transfers between devices, by_core(): return lax.ppermute(value, 'ctx', pairs)  2.94 us
    unnamed x18, local copies, waits for them, and re-layouts  1.81 us
  transfers between devices with their start and end apart: 30, of which 13 were waited for; matrix products, arithmetic and copies ran while one was open for 1% of the time, Pallas kernels for 27%

profile of v20, /device:TPU:0, one launch (start us, length us, event | category | flops | bytes accessed | tf_op | source)
XLA Modules:
  0.0 62.3 jit_solution(2132836583132051042)
XLA Ops:
  0.0 0.5 collective-permute-start.1
  0.5 0.1 collective-permute-start.2
  0.5 2.9 %collective-permute-start.12 = (bf16[2048,128]{1,0:T(8,128)(2,1)}, bf16[2048,128]{1,0:T(8,128)(2,1)S(1)}, u32[]{:S(2)}, u32[]{:S(2)}) collective-permute-start(bf16[2048,128]{1,0:T(8,128)(2,1)} %bitcast.24), channel_id=1, source_target_pairs={{0,8},{4,20},{8,0},{12,28},{16,24},{20,4},{24,16},{28,12},{1,9},{5... | collective-permute-start | bytes 1572872 | tf_op jit(solution)/shard_map/ppermute | solution.py:64
  3.5 1.6 %collective-permute-start.6 = (bf16[2048,128]{1,0:T(8,128)(2,1)S(1)}, bf16[2048,128]{1,0:T(8,128)(2,1)S(1)}, u32[]{:S(2)}, u32[]{:S(2)}) collective-permute-start(bf16[2048,128]{1,0:T(8,128)(2,1)S(1)} %collective-permute-done.1.refs_6_), channel_id=1, source_target_pairs={{0,8},{4,20},{8,0},{12,28},{16,24},{20,4},{24,16},{28,12},{1,9},{5... | collective-permute-start | bytes 1572872 | tf_op jit(solution)/shard_map/ppermute | solution.py:64
  5.1 0.7 %copy-done.5 = f32[2,2048]{1,0:T(2,128)S(1)} copy-done((f32[2,2048]{1,0:T(2,128)S(1)}, f32[2,2048]{1,0:T(2,128)}, u32[]{:S(2)}) %copy-start.5) | copy-done | bytes 16408
  5.8 0.1 squares.1
  5.9 1.1 %collective-permute-done = f32[2,128]{1,0:T(2,128)S(1)} collective-permute-done((f32[2,128]{1,0:T(2,128)S(1)}, f32[2,128]{1,0:T(2,128)S(1)}, u32[]{:S(2)}, u32[]{:S(2)}) %collective-permute-start) | collective-permute-done | bytes 1056 | tf_op jit(solution)/shard_map/ppermute | solution.py:43
  7.0 1.5 %collective-permute-start.3 = (f32[2,128]{1,0:T(2,128)S(1)}, f32[2,128]{1,0:T(2,128)S(1)}, u32[]{:S(2)}, u32[]{:S(2)}) collective-permute-start(f32[2,128]{1,0:T(2,128)S(1)} %add.53), channel_id=1, source_target_pairs={{0,16},{4,12},{8,24},{12,4},{16,0},{20,28},{24,8},{28,20},{1,17},{... | collective-permute-start | bytes 3080 | tf_op jit(solution)/shard_map/ppermute | solution.py:64
  8.5 0.8 %copy-done.4 = f32[1,16384]{1,0:T(1,128)S(1)} copy-done((f32[1,16384]{1,0:T(1,128)S(1)}, f32[1,16384]{1,0:T(1,128)}, u32[]{:S(2)}) %copy-start.4) | copy-done | bytes 65560
  9.4 3.2 %normalise.3 = (bf16[8,64,2048]{2,1,0:T(8,128)(2,1)S(1)}, bf16[8,64,2048]{2,1,0:T(8,128)(2,1)S(1)}) custom-call(bf16[320,16384]{1,0:T(8,128)(2,1)} %bitcast.36, f32[8,1,2048]{2,1,0:T(1,128)S(1)} %bitcast.31), custom_call_target="tpu_custom_call" | custom-call | flops 1000 | bytes 1000 | tf_op jit(solution)/shard_map/normalise/pallas_call | solution.py:173
  12.6 0.1 collective-permute-start.4
  12.7 0.6 collective-permute-start.8
  13.3 0.5 collective-permute-done.4
  13.8 0.2 collective-permute-start.13
  14.0 0.9 %collective-permute-start.5 = (f32[2,128]{1,0:T(2,128)S(1)}, f32[2,128]{1,0:T(2,128)S(1)}, u32[]{:S(2)}, u32[]{:S(2)}) collective-permute-start(f32[2,128]{1,0:T(2,128)S(1)} %collective-permute-done.4), channel_id=1, source_target_pairs={{0,16},{4,12},{8,24},{12,4},{16,0},{20,28},{24,8},{28,20},{1,17},{... | collective-permute-start | bytes 3080 | tf_op jit(solution)/shard_map/ppermute | solution.py:64
  14.9 3.3 %normalise.4 = (bf16[8,64,2048]{2,1,0:T(8,128)(2,1)S(1)}, bf16[8,64,2048]{2,1,0:T(8,128)(2,1)S(1)}) custom-call(bf16[320,16384]{1,0:T(8,128)(2,1)} %bitcast.37, f32[8,1,2048]{2,1,0:T(1,128)S(1)} %bitcast.32), custom_call_target="tpu_custom_call" | custom-call | flops 1000 | bytes 1000 | tf_op jit(solution)/shard_map/normalise/pallas_call | solution.py:173
  18.3 0.1 copy-done
  18.4 0.1 copy-done.2
  18.5 0.8 %query_products.1 = f32[2,10,128]{2,1,0:T(8,128)S(1)} custom-call(s32[1]{0:T(128)} %bitcast.place_ref, f32[2,128]{1,0:T(2,128)S(1)} %add_add_fusion.2.squares_ref, f32[2,2048]{1,0:T(2,128)S(1)} %copy-done.5, f32[8,1,2048]{2,1,0:T(1,128)S(1)} %bitcast.33, bf16[2048,1024]{1,0:T(8,128)(2,1)S(1)} %bitcast.21, bf16[2048,128]{1,0:T(8,128)(2,1)S(1)} %bitcast.25, ...), custom_call_target="tpu_custom_call" | custom-call | flops 1000 | bytes 1000 | tf_op jit(solution)/shard_map/query_products/pallas_call | solution.py:371
  19.3 0.1 collective-permute-start.7
  19.5 0.5 collective-permute-start.15
  20.0 0.8 %collective-permute-start.14 = (bf16[2048,128]{1,0:T(8,128)(2,1)S(1)}, bf16[2048,128]{1,0:T(8,128)(2,1)S(1)}, u32[]{:S(2)}, u32[]{:S(2)}) collective-permute-start(bf16[2048,128]{1,0:T(8,128)(2,1)S(1)} %collective-permute-done.13.refs_7_), channel_id=1, source_target_pairs={{0,8},{4,20},{8,0},{12,28},{16,24},{20,4},{24,16},{28,12},{1,9},{5... | collective-permute-start | bytes 1572872 | tf_op jit(solution)/shard_map/ppermute | solution.py:64
  20.8 1.2 %collective-permute-start.9 = (f32[2,10,128]{2,1,0:T(8,128)S(1)}, f32[2,10,128]{2,1,0:T(8,128)S(1)}, u32[]{:S(2)}, u32[]{:S(2)}) collective-permute-start(f32[2,10,128]{2,1,0:T(8,128)S(1)} %add.57), channel_id=1, source_target_pairs={{0,16},{4,12},{8,24},{12,4},{16,0},{20,28},{24,8},{28,20},{1,17},{... | collective-permute-start | bytes 30728 | tf_op jit(solution)/shard_map/ppermute | solution.py:64
  22.0 0.1 multiply_sine_fusion.1
  22.1 2.1 %normalise.5.refs_4_ = bf16[8,64,2048]{2,1,0:T(8,128)(2,1)S(1)} custom-call(bf16[320,16384]{1,0:T(8,128)(2,1)} %bitcast.38, f32[8,1,2048]{2,1,0:T(1,128)S(1)} %bitcast.34), custom_call_target="tpu_custom_call" | custom-call | flops 1000 | bytes 1000 | tf_op jit(solution)/shard_map/normalise/pallas_call | solution.py:173
  24.2 0.6 collective-permute-done.9
  24.8 1.3 %collective-permute-start.20 = (bf16[2048,128]{1,0:T(8,128)(2,1)S(1)}, bf16[2048,128]{1,0:T(8,128)(2,1)S(1)}, u32[]{:S(2)}, u32[]{:S(2)}) collective-permute-start(bf16[2048,128]{1,0:T(8,128)(2,1)S(1)} %collective-permute-done.2.refs_6_), channel_id=1, source_target_pairs={{0,8},{4,20},{8,0},{12,28},{16,24},{20,4},{24,16},{28,12},{1,9},{5... | collective-permute-start | bytes 1572872 | tf_op jit(solution)/shard_map/ppermute | solution.py:64
  26.1 0.9 %project.6.refs_9_ = f32[320,128]{1,0:T(8,128)S(1)} custom-call(s32[1]{0:T(128)} %bitcast.place_ref, bf16[8,64,2048]{2,1,0:T(8,128)(2,1)S(1)} %get-tuple-element.38.refs_0_, bf16[8,64,2048]{2,1,0:T(8,128)(2,1)S(1)} %get-tuple-element.39.refs_1_, bf16[8,64,2048]{2,1,0:T(8,128)(2,1)S(1)} %get-tuple-element.42.refs_2_, ...), custom_call_target="tpu_custom_call" | custom-call | flops 1000 | bytes 1000 | tf_op jit(solution)/shard_map/project/pallas_call | solution.py:218
  27.0 0.2 collective-permute-start.17
  27.2 1.0 %collective-permute-done.17 = f32[2,10,128]{2,1,0:T(8,128)S(1)} collective-permute-done((f32[2,10,128]{2,1,0:T(8,128)S(1)}, f32[2,10,128]{2,1,0:T(8,128)S(1)}, u32[]{:S(2)}, u32[]{:S(2)}) %collective-permute-start.17) | collective-permute-done | bytes 10272 | tf_op jit(solution)/shard_map/ppermute | solution.py:43
  28.2 1.1 %collective-permute-start.18 = (f32[2,10,128]{2,1,0:T(8,128)S(1)}, f32[2,10,128]{2,1,0:T(8,128)S(1)}, u32[]{:S(2)}, u32[]{:S(2)}) collective-permute-start(f32[2,10,128]{2,1,0:T(8,128)S(1)} %collective-permute-done.17), channel_id=1, source_target_pairs={{0,16},{4,12},{8,24},{12,4},{16,0},{20,28},{24,8},{28,20},{1,17},{... | collective-permute-start | bytes 30728 | tf_op jit(solution)/shard_map/ppermute | solution.py:64
  29.3 1.5 %project.7.refs_7_ = f32[320,128]{1,0:T(8,128)S(1)} custom-call(s32[1]{0:T(128)} %bitcast.place_ref, bf16[8,64,2048]{2,1,0:T(8,128)(2,1)S(1)} %get-tuple-element.38.refs_0_, bf16[8,64,2048]{2,1,0:T(8,128)(2,1)S(1)} %get-tuple-element.39.refs_1_, bf16[8,64,2048]{2,1,0:T(8,128)(2,1)S(1)} %get-tuple-element.42.refs_2_, ...), custom_call_target="tpu_custom_call" | custom-call | flops 1000 | bytes 1000 | tf_op jit(solution)/shard_map/project/pallas_call | solution.py:218
  30.9 0.1 collective-permute-start.16
  31.0 0.6 %multiply_sine_fusion = (f32[320,64]{1,0:T(8,128)S(1)}, f32[320,64]{1,0:T(8,128)S(1)}) fusion(f32[64]{0:T(128)S(1)} %multiply_exponential_fusion, f32[320]{0:T(512)S(1)} %add_convert_fusion), kind=kLoop, calls=%fused_computation | loop fusion | flops 20480 | bytes 165376 | tf_op jit(solution)/shard_map/sin | solution.py:97
  31.6 0.9 %collective-permute-start.11 = (bf16[2048,128]{1,0:T(8,128)(2,1)S(1)}, bf16[2048,128]{1,0:T(8,128)(2,1)S(1)}, u32[]{:S(2)}, u32[]{:S(2)}) collective-permute-start(bf16[2048,128]{1,0:T(8,128)(2,1)S(1)} %collective-permute-done.10.refs_7_), channel_id=1, source_target_pairs={{0,8},{4,20},{8,0},{12,28},{16,24},{20,4},{24,16},{28,12},{1,9},{5... | collective-permute-start | bytes 1572872 | tf_op jit(solution)/shard_map/ppermute | solution.py:64
  32.6 0.0 copy-start.7
  32.6 0.3 collective-permute-done.16.refs_6_
  32.9 0.9 %project.8.refs_0_ = f32[320,128]{1,0:T(8,128)S(1)} custom-call(s32[1]{0:T(128)} %bitcast.place_ref, bf16[8,64,2048]{2,1,0:T(8,128)(2,1)S(1)} %get-tuple-element.38.refs_0_, bf16[8,64,2048]{2,1,0:T(8,128)(2,1)S(1)} %get-tuple-element.39.refs_1_, bf16[8,64,2048]{2,1,0:T(8,128)(2,1)S(1)} %get-tuple-element.42.refs_2_, ...), custom_call_target="tpu_custom_call" | custom-call | flops 1000 | bytes 1000 | tf_op jit(solution)/shard_map/project/pallas_call | solution.py:218
  33.7 1.0 %scores.1 = (f32[8,320]{1,0:T(8,128)S(1)}, f32[8,128]{1,0:T(8,128)S(1)}, f32[8,128]{1,0:T(8,128)S(1)}) custom-call(s32[1]{0:T(128)} %bitcast.place_ref, s32[2]{0:T(128)S(1)} %copy-done.7, f32[320,128]{1,0:T(8,128)S(1)} %project.8.refs_0_, f32[320,64]{1,0:T(8,128)S(1)} %get-tuple-element.66.refs_1_, f32[320,64]{1,0:T(8,128)S(1)} %get-tuple-element.65.refs_2_, ...), custom_call_target="tpu_custom_call" | custom-call | flops 1000 | bytes 1000 | tf_op jit(solution)/shard_map/scores/pallas_call | solution.py:398
  34.7 0.1 collective-permute-start.19
  34.9 1.0 %collective-permute-done.19 = f32[8,128]{1,0:T(8,128)S(1)} collective-permute-done((f32[8,128]{1,0:T(8,128)S(1)}, f32[8,128]{1,0:T(8,128)S(1)}, u32[]{:S(2)}, u32[]{:S(2)}) %collective-permute-start.19) | collective-permute-done | bytes 4128 | tf_op jit(solution)/shard_map/ppermute | solution.py:43
  35.9 0.2 collective-permute-start.23
  36.1 1.0 %collective-permute-start.21 = (f32[8,128]{1,0:T(8,128)S(1)}, f32[8,128]{1,0:T(8,128)S(1)}, u32[]{:S(2)}, u32[]{:S(2)}) collective-permute-start(f32[8,128]{1,0:T(8,128)S(1)} %max.6), channel_id=1, source_target_pairs={{0,16},{4,12},{8,24},{12,4},{16,0},{20,28},{24,8},{28,20},{1,17},{... | collective-permute-start | bytes 12296 | tf_op jit(solution)/shard_map/ppermute | solution.py:64
  37.0 1.5 %project.9.refs_7_ = f32[320,128]{1,0:T(8,128)S(1)} custom-call(s32[1]{0:T(128)} %bitcast.place_ref, bf16[8,64,2048]{2,1,0:T(8,128)(2,1)S(1)} %get-tuple-element.38.refs_0_, bf16[8,64,2048]{2,1,0:T(8,128)(2,1)S(1)} %get-tuple-element.39.refs_1_, bf16[8,64,2048]{2,1,0:T(8,128)(2,1)S(1)} %get-tuple-element.42.refs_2_, ...), custom_call_target="tpu_custom_call" | custom-call | flops 1000 | bytes 1000 | tf_op jit(solution)/shard_map/project/pallas_call | solution.py:218
  38.6 1.2 %collective-permute-done.21 = f32[8,128]{1,0:T(8,128)S(1)} collective-permute-done((f32[8,128]{1,0:T(8,128)S(1)}, f32[8,128]{1,0:T(8,128)S(1)}, u32[]{:S(2)}, u32[]{:S(2)}) %collective-permute-start.21) | collective-permute-done | bytes 4128 | tf_op jit(solution)/shard_map/ppermute | solution.py:64
  39.8 1.1 %collective-permute-done.11.refs_5_ = bf16[2048,128]{1,0:T(8,128)(2,1)S(1)} collective-permute-done((bf16[2048,128]{1,0:T(8,128)(2,1)S(1)}, bf16[2048,128]{1,0:T(8,128)(2,1)S(1)}, u32[]{:S(2)}, u32[]{:S(2)}) %collective-permute-start.11) | collective-permute-done | bytes 524320 | tf_op jit(solution)/shard_map/ppermute | solution.py:64
  40.9 0.5 collective-permute-start.24
  41.4 0.9 %project.10.refs_6_ = f32[320,128]{1,0:T(8,128)S(1)} custom-call(s32[1]{0:T(128)} %bitcast.place_ref, bf16[8,64,2048]{2,1,0:T(8,128)(2,1)S(1)} %get-tuple-element.38.refs_0_, bf16[8,64,2048]{2,1,0:T(8,128)(2,1)S(1)} %get-tuple-element.39.refs_1_, bf16[8,64,2048]{2,1,0:T(8,128)(2,1)S(1)} %get-tuple-element.42.refs_2_, ...), custom_call_target="tpu_custom_call" | custom-call | flops 1000 | bytes 1000 | tf_op jit(solution)/shard_map/project/pallas_call | solution.py:218
  42.3 0.5 project.11.refs_6_
  42.8 0.0 collective-permute-done.24
  42.9 0.0 copy-start.1
  42.9 1.2 %weighted_values.1 = f32[8,256]{1,0:T(8,128)S(1)} custom-call(s32[1]{0:T(128)} %bitcast.place_ref, s32[2]{0:T(128)S(1)} %copy-done.7, bf16[8,64,2048]{2,1,0:T(8,128)(2,1)S(1)} %get-tuple-element.38.refs_0_, bf16[8,64,2048]{2,1,0:T(8,128)(2,1)S(1)} %get-tuple-element.39.refs_1_, bf16[8,64,2048]{2,1,0:T(8,128)(2,1)S(1)} %get-tuple-element.42.refs_2_, ...), custom_call_target="tpu_custom_call" | custom-call | flops 1000 | bytes 1000 | tf_op jit(solution)/shard_map/weighted_values/pallas_call | solution.py:425
  44.0 0.1 collective-permute-start.25
  44.2 1.0 %collective-permute-done.25 = f32[8,256]{1,0:T(8,128)S(1)} collective-permute-done((f32[8,256]{1,0:T(8,128)S(1)}, f32[8,256]{1,0:T(8,128)S(1)}, u32[]{:S(2)}, u32[]{:S(2)}) %collective-permute-start.25) | collective-permute-done | bytes 8224 | tf_op jit(solution)/shard_map/ppermute | solution.py:43
  45.2 0.9 %collective-permute-start.26 = (f32[8,256]{1,0:T(8,128)S(1)}, f32[8,256]{1,0:T(8,128)S(1)}, u32[]{:S(2)}, u32[]{:S(2)}) collective-permute-start(f32[8,256]{1,0:T(8,128)S(1)} %add.64), channel_id=1, source_target_pairs={{0,8},{4,12},{8,0},{12,4},{16,24},{20,28},{24,16},{28,20},{1,9},{5... | collective-permute-start | bytes 24584 | tf_op jit(solution)/shard_map/ppermute | solution.py:43
  46.1 2.8 %collective-permute-done.26 = f32[8,256]{1,0:T(8,128)S(1)} collective-permute-done((f32[8,256]{1,0:T(8,128)S(1)}, f32[8,256]{1,0:T(8,128)S(1)}, u32[]{:S(2)}, u32[]{:S(2)}) %collective-permute-start.26) | collective-permute-done | bytes 8224 | tf_op jit(solution)/shard_map/ppermute | solution.py:43
  48.9 0.9 %collective-permute-start.27 = (f32[8,256]{1,0:T(8,128)S(1)}, f32[8,256]{1,0:T(8,128)S(1)}, u32[]{:S(2)}, u32[]{:S(2)}) collective-permute-start(f32[8,256]{1,0:T(8,128)S(1)} %add.65.mine_ref), channel_id=1, source_target_pairs={{0,16},{4,20},{8,24},{12,28},{16,0},{20,4},{24,8},{28,12},{1,17},{... | collective-permute-start | bytes 24584 | tf_op jit(solution)/shard_map/ppermute | solution.py:43
  49.8 2.7 %collective-permute-done.27.other_ref = f32[8,256]{1,0:T(8,128)S(1)} collective-permute-done((f32[8,256]{1,0:T(8,128)S(1)}, f32[8,256]{1,0:T(8,128)S(1)}, u32[]{:S(2)}, u32[]{:S(2)}) %collective-permute-start.27) | collective-permute-done | bytes 8224 | tf_op jit(solution)/shard_map/ppermute | solution.py:43
  52.5 0.6 %output_products.1 = f32[2,2048]{1,0:T(2,128)S(1)} custom-call(s32[1]{0:T(128)} %bitcast.place_ref, f32[8,256]{1,0:T(8,128)S(1)} %add.65.mine_ref, f32[8,256]{1,0:T(8,128)S(1)} %collective-permute-done.27.other_ref, bf16[1024,2048]{1,0:T(8,128)(2,1)S(1)} %bitcast.22), custom_call_target="tpu_custom_call" | custom-call | flops 1000 | bytes 1000 | tf_op jit(solution)/shard_map/output_products/pallas_call | solution.py:443
  53.2 1.6 %collective-permute-start.28 = (f32[2,2048]{1,0:T(2,128)S(1)}, f32[2,2048]{1,0:T(2,128)S(1)}, u32[]{:S(2)}, u32[]{:S(2)}) collective-permute-start(f32[2,2048]{1,0:T(2,128)S(1)} %output_products.1), channel_id=1, source_target_pairs={{0,1},{1,0},{2,3},{3,2},{4,5},{5,4},{6,7},{7,6},{8,9},{9,8},{10,11... | collective-permute-start | bytes 49160 | tf_op jit(solution)/shard_map/ppermute | solution.py:43
  54.8 2.2 %collective-permute-done.28 = f32[2,2048]{1,0:T(2,128)S(1)} collective-permute-done((f32[2,2048]{1,0:T(2,128)S(1)}, f32[2,2048]{1,0:T(2,128)S(1)}, u32[]{:S(2)}, u32[]{:S(2)}) %collective-permute-start.28) | collective-permute-done | bytes 16416 | tf_op jit(solution)/shard_map/ppermute | solution.py:43
  57.0 2.7 %collective-permute-start.29 = (f32[2,2048]{1,0:T(2,128)S(1)}, f32[2,2048]{1,0:T(2,128)S(1)}, u32[]{:S(2)}, u32[]{:S(2)}) collective-permute-start(f32[2,2048]{1,0:T(2,128)S(1)} %add.66), channel_id=1, source_target_pairs={{0,2},{1,3},{2,0},{3,1},{4,6},{5,7},{6,4},{7,5},{8,10},{9,11},{10,... | collective-permute-start | bytes 49160 | tf_op jit(solution)/shard_map/ppermute | solution.py:43
  59.6 2.0 %collective-permute-done.29 = f32[2,2048]{1,0:T(2,128)S(1)} collective-permute-done((f32[2,2048]{1,0:T(2,128)S(1)}, f32[2,2048]{1,0:T(2,128)S(1)}, u32[]{:S(2)}, u32[]{:S(2)}) %collective-permute-start.29) | collective-permute-done | bytes 16416 | tf_op jit(solution)/shard_map/ppermute | solution.py:43
  61.7 0.6 add_add_fusion
  (47 shorter events, 0.2 us)
Async XLA Ops:
  0.0 3.5 %collective-permute-start.1 = (bf16[2048,128]{1,0:T(8,128)(2,1)}, bf16[2048,128]{1,0:T(8,128)(2,1)S(1)}, u32[]{:S(2)}, u32[]{:S(2)}) collective-permute-start(bf16[2048,128]{1,0:T(8,128)(2,1)} %bitcast.23), channel_id=1, source_target_pairs={{0,4},{4,0},{8,12},{12,8},{16,20},{20,16},{24,28},{28,24},{1,5},{5... | collective-permute-start | bytes 1572872 | tf_op jit(solution)/shard_map/ppermute | solution.py:43
  0.5 6.6 %collective-permute-start.2 = (bf16[2048,128]{1,0:T(8,128)(2,1)}, bf16[2048,128]{1,0:T(8,128)(2,1)S(1)}, u32[]{:S(2)}, u32[]{:S(2)}) collective-permute-start(bf16[2048,128]{1,0:T(8,128)(2,1)} %bitcast.27), channel_id=1, source_target_pairs={{0,4},{4,0},{8,12},{12,8},{16,20},{20,16},{24,28},{28,24},{1,5},{5... | collective-permute-start | bytes 1572872 | tf_op jit(solution)/shard_map/ppermute | solution.py:43
  0.5 12.8 %collective-permute-start.12 = (bf16[2048,128]{1,0:T(8,128)(2,1)}, bf16[2048,128]{1,0:T(8,128)(2,1)S(1)}, u32[]{:S(2)}, u32[]{:S(2)}) collective-permute-start(bf16[2048,128]{1,0:T(8,128)(2,1)} %bitcast.24), channel_id=1, source_target_pairs={{0,8},{4,20},{8,0},{12,28},{16,24},{20,4},{24,16},{28,12},{1,9},{5... | collective-permute-start | bytes 1572872 | tf_op jit(solution)/shard_map/ppermute | solution.py:64
  3.5 14.8 %collective-permute-start.6 = (bf16[2048,128]{1,0:T(8,128)(2,1)S(1)}, bf16[2048,128]{1,0:T(8,128)(2,1)S(1)}, u32[]{:S(2)}, u32[]{:S(2)}) collective-permute-start(bf16[2048,128]{1,0:T(8,128)(2,1)S(1)} %collective-permute-done.1.refs_6_), channel_id=1, source_target_pairs={{0,8},{4,20},{8,0},{12,28},{16,24},{20,4},{24,16},{28,12},{1,9},{5... | collective-permute-start | bytes 1572872 | tf_op jit(solution)/shard_map/ppermute | solution.py:64
  5.1 0.7 %copy-start.5 = (f32[2,2048]{1,0:T(2,128)S(1)}, f32[2,2048]{1,0:T(2,128)}, u32[]{:S(2)}) copy-start(f32[2,2048]{1,0:T(2,128)} %tokens_ref.3) | copy-start | bytes 49156
  5.9 1.1 %collective-permute-start = (f32[2,128]{1,0:T(2,128)S(1)}, f32[2,128]{1,0:T(2,128)S(1)}, u32[]{:S(2)}, u32[]{:S(2)}) collective-permute-start(f32[2,128]{1,0:T(2,128)S(1)} %get-tuple-element.35), channel_id=1, source_target_pairs={{0,4},{4,0},{8,12},{12,8},{16,20},{20,16},{24,28},{28,24},{1,5},{5... | collective-permute-start | bytes 3080 | tf_op jit(solution)/shard_map/ppermute | solution.py:43
  7.0 5.6 %collective-permute-start.3 = (f32[2,128]{1,0:T(2,128)S(1)}, f32[2,128]{1,0:T(2,128)S(1)}, u32[]{:S(2)}, u32[]{:S(2)}) collective-permute-start(f32[2,128]{1,0:T(2,128)S(1)} %add.53), channel_id=1, source_target_pairs={{0,16},{4,12},{8,24},{12,4},{16,0},{20,28},{24,8},{28,20},{1,17},{... | collective-permute-start | bytes 3080 | tf_op jit(solution)/shard_map/ppermute | solution.py:64
  8.5 0.8 %copy-start.4 = (f32[1,16384]{1,0:T(1,128)S(1)}, f32[1,16384]{1,0:T(1,128)}, u32[]{:S(2)}) copy-start(f32[1,16384]{1,0:T(1,128)} %param.11) | copy-start | bytes 196612
  9.4 3.3 %copy-start.3 = (bf16[1,2048,128]{2,1,0:T(8,128)(2,1)S(1)}, bf16[1,2048,128]{2,1,0:T(8,128)(2,1)}, u32[]{:S(2)}) copy-start(bf16[1,2048,128]{2,1,0:T(8,128)(2,1)} %param.14) | copy-start | bytes 1572868
  12.6 1.2 %collective-permute-start.4 = (f32[2,128]{1,0:T(2,128)S(1)}, f32[2,128]{1,0:T(2,128)S(1)}, u32[]{:S(2)}, u32[]{:S(2)}) collective-permute-start(f32[2,128]{1,0:T(2,128)S(1)} %collective-permute-done.3), channel_id=1, source_target_pairs={{0,4},{4,0},{8,12},{12,8},{16,20},{20,16},{24,28},{28,24},{1,5},{5... | collective-permute-start | bytes 3080 | tf_op jit(solution)/shard_map/ppermute | solution.py:43
  12.7 12.2 %collective-permute-start.8 = (bf16[2048,128]{1,0:T(8,128)(2,1)S(1)}, bf16[2048,128]{1,0:T(8,128)(2,1)S(1)}, u32[]{:S(2)}, u32[]{:S(2)}) collective-permute-start(bf16[2048,128]{1,0:T(8,128)(2,1)S(1)} %bitcast.28), channel_id=1, source_target_pairs={{0,8},{4,20},{8,0},{12,28},{16,24},{20,4},{24,16},{28,12},{1,9},{5... | collective-permute-start | bytes 1572872 | tf_op jit(solution)/shard_map/ppermute | solution.py:64
  13.8 6.2 %collective-permute-start.13 = (bf16[2048,128]{1,0:T(8,128)(2,1)S(1)}, bf16[2048,128]{1,0:T(8,128)(2,1)S(1)}, u32[]{:S(2)}, u32[]{:S(2)}) collective-permute-start(bf16[2048,128]{1,0:T(8,128)(2,1)S(1)} %collective-permute-done.12.refs_5_), channel_id=1, source_target_pairs={{0,4},{4,0},{8,12},{12,8},{16,20},{20,16},{24,28},{28,24},{1,5},{5... | collective-permute-start | bytes 1572872 | tf_op jit(solution)/shard_map/ppermute | solution.py:43
  14.0 4.2 %collective-permute-start.5 = (f32[2,128]{1,0:T(2,128)S(1)}, f32[2,128]{1,0:T(2,128)S(1)}, u32[]{:S(2)}, u32[]{:S(2)}) collective-permute-start(f32[2,128]{1,0:T(2,128)S(1)} %collective-permute-done.4), channel_id=1, source_target_pairs={{0,16},{4,12},{8,24},{12,4},{16,0},{20,28},{24,8},{28,20},{1,17},{... | collective-permute-start | bytes 3080 | tf_op jit(solution)/shard_map/ppermute | solution.py:64
  14.9 3.4 %copy-start = (bf16[1,2048,1024]{2,1,0:T(8,128)(2,1)S(1)}, bf16[1,2048,1024]{2,1,0:T(8,128)(2,1)}, u32[]{:S(2)}) copy-start(bf16[1,2048,1024]{2,1,0:T(8,128)(2,1)} %param.12) | copy-start | bytes 12582916
  14.9 3.6 %copy-start.2 = (bf16[1,2048,128]{2,1,0:T(8,128)(2,1)S(1)}, bf16[1,2048,128]{2,1,0:T(8,128)(2,1)}, u32[]{:S(2)}) copy-start(bf16[1,2048,128]{2,1,0:T(8,128)(2,1)} %param.13) | copy-start | bytes 1572868
  18.5 1.0 %copy-start.8 = (s32[2]{0:T(128)S(1)}, s32[2]{0:T(128)}, u32[]{:S(2)}) copy-start(s32[2]{0:T(128)} %param.17) | copy-start | bytes 28
  19.3 1.5 %collective-permute-start.7 = (f32[2,10,128]{2,1,0:T(8,128)S(1)}, f32[2,10,128]{2,1,0:T(8,128)S(1)}, u32[]{:S(2)}, u32[]{:S(2)}) collective-permute-start(f32[2,10,128]{2,1,0:T(8,128)S(1)} %query_products.1), channel_id=1, source_target_pairs={{0,4},{4,0},{8,12},{12,8},{16,20},{20,16},{24,28},{28,24},{1,5},{5... | collective-permute-start | bytes 30728 | tf_op jit(solution)/shard_map/ppermute | solution.py:43
  19.5 9.8 %collective-permute-start.15 = (bf16[2048,128]{1,0:T(8,128)(2,1)S(1)}, bf16[2048,128]{1,0:T(8,128)(2,1)S(1)}, u32[]{:S(2)}, u32[]{:S(2)}) collective-permute-start(bf16[2048,128]{1,0:T(8,128)(2,1)S(1)} %collective-permute-done.6.refs_6_), channel_id=1, source_target_pairs={{0,4},{4,0},{8,12},{12,8},{16,20},{20,16},{24,28},{28,24},{1,5},{5... | collective-permute-start | bytes 1572872 | tf_op jit(solution)/shard_map/ppermute | solution.py:43
  20.0 10.9 %collective-permute-start.14 = (bf16[2048,128]{1,0:T(8,128)(2,1)S(1)}, bf16[2048,128]{1,0:T(8,128)(2,1)S(1)}, u32[]{:S(2)}, u32[]{:S(2)}) collective-permute-start(bf16[2048,128]{1,0:T(8,128)(2,1)S(1)} %collective-permute-done.13.refs_7_), channel_id=1, source_target_pairs={{0,8},{4,20},{8,0},{12,28},{16,24},{20,4},{24,16},{28,12},{1,9},{5... | collective-permute-start | bytes 1572872 | tf_op jit(solution)/shard_map/ppermute | solution.py:64
  20.8 4.0 %collective-permute-start.9 = (f32[2,10,128]{2,1,0:T(8,128)S(1)}, f32[2,10,128]{2,1,0:T(8,128)S(1)}, u32[]{:S(2)}, u32[]{:S(2)}) collective-permute-start(f32[2,10,128]{2,1,0:T(8,128)S(1)} %add.57), channel_id=1, source_target_pairs={{0,16},{4,12},{8,24},{12,4},{16,0},{20,28},{24,8},{28,20},{1,17},{... | collective-permute-start | bytes 30728 | tf_op jit(solution)/shard_map/ppermute | solution.py:64
  24.8 6.8 %collective-permute-start.10 = (bf16[2048,128]{1,0:T(8,128)(2,1)S(1)}, bf16[2048,128]{1,0:T(8,128)(2,1)S(1)}, u32[]{:S(2)}, u32[]{:S(2)}) collective-permute-start(bf16[2048,128]{1,0:T(8,128)(2,1)S(1)} %collective-permute-done.8.refs_8_), channel_id=1, source_target_pairs={{0,4},{4,0},{8,12},{12,8},{16,20},{20,16},{24,28},{28,24},{1,5},{5... | collective-permute-start | bytes 1572872 | tf_op jit(solution)/shard_map/ppermute | solution.py:43
  24.8 11.1 %collective-permute-start.20 = (bf16[2048,128]{1,0:T(8,128)(2,1)S(1)}, bf16[2048,128]{1,0:T(8,128)(2,1)S(1)}, u32[]{:S(2)}, u32[]{:S(2)}) collective-permute-start(bf16[2048,128]{1,0:T(8,128)(2,1)S(1)} %collective-permute-done.2.refs_6_), channel_id=1, source_target_pairs={{0,8},{4,20},{8,0},{12,28},{16,24},{20,4},{24,16},{28,12},{1,9},{5... | collective-permute-start | bytes 1572872 | tf_op jit(solution)/shard_map/ppermute | solution.py:64
  27.0 1.2 %collective-permute-start.17 = (f32[2,10,128]{2,1,0:T(8,128)S(1)}, f32[2,10,128]{2,1,0:T(8,128)S(1)}, u32[]{:S(2)}, u32[]{:S(2)}) collective-permute-start(f32[2,10,128]{2,1,0:T(8,128)S(1)} %collective-permute-done.9), channel_id=1, source_target_pairs={{0,4},{4,0},{8,12},{12,8},{16,20},{20,16},{24,28},{28,24},{1,5},{5... | collective-permute-start | bytes 30728 | tf_op jit(solution)/shard_map/ppermute | solution.py:43
  28.2 4.3 %collective-permute-start.18 = (f32[2,10,128]{2,1,0:T(8,128)S(1)}, f32[2,10,128]{2,1,0:T(8,128)S(1)}, u32[]{:S(2)}, u32[]{:S(2)}) collective-permute-start(f32[2,10,128]{2,1,0:T(8,128)S(1)} %collective-permute-done.17), channel_id=1, source_target_pairs={{0,16},{4,12},{8,24},{12,4},{16,0},{20,28},{24,8},{28,20},{1,17},{... | collective-permute-start | bytes 30728 | tf_op jit(solution)/shard_map/ppermute | solution.py:64
  30.9 2.0 %collective-permute-start.16 = (bf16[2048,128]{1,0:T(8,128)(2,1)S(1)}, bf16[2048,128]{1,0:T(8,128)(2,1)S(1)}, u32[]{:S(2)}, u32[]{:S(2)}) collective-permute-start(bf16[2048,128]{1,0:T(8,128)(2,1)S(1)} %collective-permute-done.14.refs_5_), channel_id=1, source_target_pairs={{0,4},{4,0},{8,12},{12,8},{16,20},{20,16},{24,28},{28,24},{1,5},{5... | collective-permute-start | bytes 1572872 | tf_op jit(solution)/shard_map/ppermute | solution.py:43
  31.6 9.3 %collective-permute-start.11 = (bf16[2048,128]{1,0:T(8,128)(2,1)S(1)}, bf16[2048,128]{1,0:T(8,128)(2,1)S(1)}, u32[]{:S(2)}, u32[]{:S(2)}) collective-permute-start(bf16[2048,128]{1,0:T(8,128)(2,1)S(1)} %collective-permute-done.10.refs_7_), channel_id=1, source_target_pairs={{0,8},{4,20},{8,0},{12,28},{16,24},{20,4},{24,16},{28,12},{1,9},{5... | collective-permute-start | bytes 1572872 | tf_op jit(solution)/shard_map/ppermute | solution.py:64
  32.6 1.1 %copy-start.7 = (s32[2]{0:T(128)S(1)}, s32[2]{0:T(128)}, u32[]{:S(2)}) copy-start(s32[2]{0:T(128)} %lengths_ref.3) | copy-start | bytes 28
  34.7 1.2 %collective-permute-start.19 = (f32[8,128]{1,0:T(8,128)S(1)}, f32[8,128]{1,0:T(8,128)S(1)}, u32[]{:S(2)}, u32[]{:S(2)}) collective-permute-start(f32[8,128]{1,0:T(8,128)S(1)} %get-tuple-element.56), channel_id=1, source_target_pairs={{0,4},{4,0},{8,12},{12,8},{16,20},{20,16},{24,28},{28,24},{1,5},{5... | collective-permute-start | bytes 12296 | tf_op jit(solution)/shard_map/ppermute | solution.py:43
  35.9 5.5 %collective-permute-start.23 = (bf16[2048,128]{1,0:T(8,128)(2,1)S(1)}, bf16[2048,128]{1,0:T(8,128)(2,1)S(1)}, u32[]{:S(2)}, u32[]{:S(2)}) collective-permute-start(bf16[2048,128]{1,0:T(8,128)(2,1)S(1)} %collective-permute-done.20.refs_5_), channel_id=1, source_target_pairs={{0,4},{4,0},{8,12},{12,8},{16,20},{20,16},{24,28},{28,24},{1,5},{5... | collective-permute-start | bytes 1572872 | tf_op jit(solution)/shard_map/ppermute | solution.py:43
  36.1 3.7 %collective-permute-start.21 = (f32[8,128]{1,0:T(8,128)S(1)}, f32[8,128]{1,0:T(8,128)S(1)}, u32[]{:S(2)}, u32[]{:S(2)}) collective-permute-start(f32[8,128]{1,0:T(8,128)S(1)} %max.6), channel_id=1, source_target_pairs={{0,16},{4,12},{8,24},{12,4},{16,0},{20,28},{24,8},{28,20},{1,17},{... | collective-permute-start | bytes 12296 | tf_op jit(solution)/shard_map/ppermute | solution.py:64
  40.9 1.9 %collective-permute-start.22 = (bf16[2048,128]{1,0:T(8,128)(2,1)S(1)}, bf16[2048,128]{1,0:T(8,128)(2,1)S(1)}, u32[]{:S(2)}, u32[]{:S(2)}) collective-permute-start(bf16[2048,128]{1,0:T(8,128)(2,1)S(1)} %collective-permute-done.11.refs_5_), channel_id=1, source_target_pairs={{0,4},{4,0},{8,12},{12,8},{16,20},{20,16},{24,28},{28,24},{1,5},{5... | collective-permute-start | bytes 1572872 | tf_op jit(solution)/shard_map/ppermute | solution.py:43
  40.9 1.9 %collective-permute-start.24 = (f32[8,128]{1,0:T(8,128)S(1)}, f32[8,128]{1,0:T(8,128)S(1)}, u32[]{:S(2)}, u32[]{:S(2)}) collective-permute-start(f32[8,128]{1,0:T(8,128)S(1)} %max.7), channel_id=1, source_target_pairs={{0,4},{4,0},{8,12},{12,8},{16,20},{20,16},{24,28},{28,24},{1,5},{5... | collective-permute-start | bytes 12296 | tf_op jit(solution)/shard_map/ppermute | solution.py:43
  42.9 9.7 %copy-start.1 = (bf16[1,1024,2048]{2,1,0:T(8,128)(2,1)S(1)}, bf16[1,1024,2048]{2,1,0:T(8,128)(2,1)}, u32[]{:S(2)}) copy-start(bf16[1,1024,2048]{2,1,0:T(8,128)(2,1)} %param.15) | copy-start | bytes 12582916
  44.0 1.2 %collective-permute-start.25 = (f32[8,256]{1,0:T(8,128)S(1)}, f32[8,256]{1,0:T(8,128)S(1)}, u32[]{:S(2)}, u32[]{:S(2)}) collective-permute-start(f32[8,256]{1,0:T(8,128)S(1)} %weighted_values.1), channel_id=1, source_target_pairs={{0,4},{4,0},{8,12},{12,8},{16,20},{20,16},{24,28},{28,24},{1,5},{5... | collective-permute-start | bytes 24584 | tf_op jit(solution)/shard_map/ppermute | solution.py:43
  45.2 3.7 %collective-permute-start.26 = (f32[8,256]{1,0:T(8,128)S(1)}, f32[8,256]{1,0:T(8,128)S(1)}, u32[]{:S(2)}, u32[]{:S(2)}) collective-permute-start(f32[8,256]{1,0:T(8,128)S(1)} %add.64), channel_id=1, source_target_pairs={{0,8},{4,12},{8,0},{12,4},{16,24},{20,28},{24,16},{28,20},{1,9},{5... | collective-permute-start | bytes 24584 | tf_op jit(solution)/shard_map/ppermute | solution.py:43
  48.9 3.7 %collective-permute-start.27 = (f32[8,256]{1,0:T(8,128)S(1)}, f32[8,256]{1,0:T(8,128)S(1)}, u32[]{:S(2)}, u32[]{:S(2)}) collective-permute-start(f32[8,256]{1,0:T(8,128)S(1)} %add.65.mine_ref), channel_id=1, source_target_pairs={{0,16},{4,20},{8,24},{12,28},{16,0},{20,4},{24,8},{28,12},{1,17},{... | collective-permute-start | bytes 24584 | tf_op jit(solution)/shard_map/ppermute | solution.py:43
  52.5 9.1 %copy-start.6 = (f32[2,2048]{1,0:T(2,128)S(1)}, f32[2,2048]{1,0:T(2,128)}, u32[]{:S(2)}) copy-start(f32[2,2048]{1,0:T(2,128)} %tokens_ref.3) | copy-start | bytes 49156
  53.2 3.8 %collective-permute-start.28 = (f32[2,2048]{1,0:T(2,128)S(1)}, f32[2,2048]{1,0:T(2,128)S(1)}, u32[]{:S(2)}, u32[]{:S(2)}) collective-permute-start(f32[2,2048]{1,0:T(2,128)S(1)} %output_products.1), channel_id=1, source_target_pairs={{0,1},{1,0},{2,3},{3,2},{4,5},{5,4},{6,7},{7,6},{8,9},{9,8},{10,11... | collective-permute-start | bytes 49160 | tf_op jit(solution)/shard_map/ppermute | solution.py:43
  57.0 4.7 %collective-permute-start.29 = (f32[2,2048]{1,0:T(2,128)S(1)}, f32[2,2048]{1,0:T(2,128)S(1)}, u32[]{:S(2)}, u32[]{:S(2)}) collective-permute-start(f32[2,2048]{1,0:T(2,128)S(1)} %add.66), channel_id=1, source_target_pairs={{0,2},{1,3},{2,0},{3,1},{4,6},{5,7},{6,4},{7,5},{8,10},{9,11},{10,... | collective-permute-start | bytes 49160 | tf_op jit(solution)/shard_map/ppermute | solution.py:43
